TPU v7x, 32 devices: a whole 2x2x4 slice. The times are simulated.
32 devices in a mesh: row: 4 (over z), col: 8 (over y, x, core).
Axes of the slice: x: 2, y: 2, z: 4, core: 2. Of those that a mesh axis runs over, the one named last changes fastest.
Arguments:
- inputs: bfloat16 [4096, 2048], P('row', 'col'), may hold values from -6 to 6
- query_weight: bfloat16 [2048, 2048], P('row', 'col'), may hold values from -0.125 to 0.125
- key_weight: bfloat16 [2048, 2048], P('row', 'col'), may hold values from -0.125 to 0.125
- value_weight: bfloat16 [2048, 2048], P('row', 'col'), may hold values from -0.125 to 0.125
- out_weight: bfloat16 [2048, 2048], P('row', 'col'), may hold values from -2 to 2
- gate_weight: bfloat16 [2048, 8192], P('row', 'col'), may hold values from -0.125 to 0.125
- up_weight: bfloat16 [2048, 8192], P('row', 'col'), may hold values from -0.125 to 0.125
- down_weight: bfloat16 [2048, 8192], P('row', 'col'), may hold values from -0.0625 to 0.0625
- first_gain: bfloat16 [2048], P('row'), may hold values from 0.5 to 1.5
- second_gain: bfloat16 [2048], P('row'), may hold values from 0.5 to 1.5
- segment_ids: int32 [4096], P('row'), may hold values from 0 to 7, as said below
- positions: int32 [4096], P('row'), may hold values from 0 to 767, as said below
- out_grad: bfloat16 [4096, 2048], P('row', 'col'), may hold values from -6 to 6
Outputs:
- block_out: bfloat16 [4096, 2048], P('row', 'col')
- input_grad: bfloat16 [4096, 2048], P('row', 'col')
- query_weight_grad: float32 [2048, 2048], P('row', 'col')
- key_weight_grad: float32 [2048, 2048], P('row', 'col')
- value_weight_grad: float32 [2048, 2048], P('row', 'col')
- out_weight_grad: float32 [2048, 2048], P('row', 'col')
- gate_weight_grad: float32 [2048, 8192], P('row', 'col')
- up_weight_grad: float32 [2048, 8192], P('row', 'col')
- down_weight_grad: float32 [2048, 8192], P('row', 'col')
- first_gain_grad: float32 [2048], P('row')
- second_gain_grad: float32 [2048], P('row')
Inputs may be any that keep to these rules, and one draw needn't show every extreme that they name: `segment_ids`: ids never fall along the rows. Each aligned block of 1024 rows holds two documents, numbered 2 b and 2 b + 1 in block b; the second starts at a row from 256 to 768 of its block. `positions`: each row's offset from the first row of its document.
All inputs are finite; a program needn't handle non-finite values.
Results may differ from a plain program's by a relative error of at most 0.019.
Values may be sent and summed in bfloat16 or wider, within the bound.
No kernel may reach another device: no remote copies, remote signals or barrier semaphores. Data moves between devices by JAX's collectives and lax.ppermute only.
A program may use at most 192 MiB of HBM per device.

v0:
```python
import math

import jax
import jax.numpy as jnp
from jax import lax
from jax.sharding import PartitionSpec as P

HEAD_DIM = 64
SEQ = 1024


eps = 1e-05
rope_base = 130000.0


def rope_tables(positions, head_size):
    half_size = head_size // 2
    freqs = jnp.exp(
        jnp.arange(half_size, dtype=jnp.float32) * (-2.0 * math.log(rope_base) / head_size)
    )
    angles = positions.astype(jnp.float32)[:, None] * freqs[None, :]
    return (jnp.cos(angles), jnp.sin(angles))


def rotate(values, cosine, sine):
    half_size = values.shape[-1] // 2
    front_half = values[..., :half_size]
    back_half = values[..., half_size:]
    cosine_wide = cosine[:, None, :]
    sine_wide = sine[:, None, :]
    return jnp.concatenate(
        [
            front_half * cosine_wide - back_half * sine_wide,
            back_half * cosine_wide + front_half * sine_wide,
        ],
        axis=-1,
    )


def unrotate(values, cosine, sine):
    half_size = values.shape[-1] // 2
    front_half = values[..., :half_size]
    back_half = values[..., half_size:]
    cosine_wide = cosine[:, None, :]
    sine_wide = sine[:, None, :]
    return jnp.concatenate(
        [
            front_half * cosine_wide + back_half * sine_wide,
            back_half * cosine_wide - front_half * sine_wide,
        ],
        axis=-1,
    )


def contract_last(left, right):
    return lax.dot_general(
        left, right, (((1,), (1,)), ((), ())), preferred_element_type=jnp.float32
    )


def contract_first(left, right):
    return lax.dot_general(
        left, right, (((0,), (0,)), ((), ())), preferred_element_type=jnp.float32
    )


def block_mask(segment_ids, row_start, seq_start, block_rows):
    query_ids = lax.dynamic_slice_in_dim(segment_ids, row_start, block_rows, 0)
    query_index = row_start + jnp.arange(block_rows)
    key_index = seq_start + jnp.arange(SEQ)
    return (query_ids[:, None] == segment_ids[None, :]) & (
        query_index[:, None] >= key_index[None, :]
    )


def block_scores(query_piece, key_piece, allowed):
    scores = jnp.einsum(
        "qhd,khd->hqk", query_piece, key_piece, preferred_element_type=jnp.float32
    ) * HEAD_DIM ** (-0.5)
    return jnp.where(allowed[None], scores, -1e30)


def attend_forward(query_rows, key_rows, value_rows, segment_ids):
    token_count, heads_here, head_size = query_rows.shape
    block_rows = min(512, SEQ)
    block_count = token_count // block_rows

    def one_block(index_block):
        row_start = index_block * block_rows
        seq_start = row_start // SEQ * SEQ
        query_piece = lax.dynamic_slice_in_dim(query_rows, row_start, block_rows, 0)
        scores = block_scores(
            query_piece, key_rows, block_mask(segment_ids, row_start, seq_start, block_rows)
        )
        peak = jnp.max(scores, axis=-1, keepdims=True)
        raised = jnp.exp(scores - peak)
        denominator = jnp.sum(raised, axis=-1, keepdims=True)
        weights = (raised / denominator).astype(jnp.bfloat16)
        attended = jnp.einsum(
            "hqk,khd->qhd", weights, value_rows, preferred_element_type=jnp.float32
        )
        return (attended.astype(jnp.bfloat16), (peak + jnp.log(denominator))[..., 0])

    attended, logsum = lax.map(one_block, jnp.arange(block_count))
    return (attended.reshape(token_count, heads_here * head_size), logsum)


def attend_backward(query_rows, key_rows, value_rows, mixed_grad, logsum, segment_ids):
    token_count, heads_here, head_size = query_rows.shape
    block_rows = min(512, SEQ)
    block_count = token_count // block_rows
    score_scale = HEAD_DIM ** (-0.5)

    def one_block(carry, pieces):
        key_grad, value_grad = carry
        index_block, logsum_piece = pieces
        row_start = index_block * block_rows
        seq_start = row_start // SEQ * SEQ
        query_piece = lax.dynamic_slice_in_dim(query_rows, row_start, block_rows, 0)
        grad_piece = lax.dynamic_slice_in_dim(mixed_grad, row_start, block_rows, 0)
        scores = block_scores(
            query_piece, key_rows, block_mask(segment_ids, row_start, seq_start, block_rows)
        )
        weights = jnp.exp(scores - logsum_piece[..., None])
        weight_grad = jnp.einsum(
            "qhd,khd->hqk", grad_piece, value_rows, preferred_element_type=jnp.float32
        )
        row_dots = jnp.sum(weights * weight_grad, axis=-1, keepdims=True)
        score_grad = (weights * (weight_grad - row_dots)).astype(jnp.bfloat16)
        query_grad = (
            jnp.einsum("hqk,khd->qhd", score_grad, key_rows, preferred_element_type=jnp.float32)
            * score_scale
        )
        key_add = (
            jnp.einsum("hqk,qhd->khd", score_grad, query_piece, preferred_element_type=jnp.float32)
            * score_scale
        )
        value_add = jnp.einsum(
            "hqk,qhd->khd",
            weights.astype(jnp.bfloat16),
            grad_piece,
            preferred_element_type=jnp.float32,
        )
        key_grad = key_grad + key_add
        value_grad = value_grad + value_add
        return ((key_grad, value_grad), query_grad)

    zeros_grad = jnp.zeros((token_count, heads_here, head_size), jnp.float32)
    (key_grad, value_grad), query_grad = lax.scan(
        one_block, (zeros_grad, zeros_grad), (jnp.arange(block_count), logsum)
    )
    return (query_grad.reshape(token_count, heads_here, head_size), key_grad, value_grad)


def local(
    inputs,
    query_weight,
    key_weight,
    value_weight,
    out_weight,
    gate_weight,
    up_weight,
    down_weight,
    first_gain,
    second_gain,
    segment_ids,
    positions,
    out_grad,
):
    col_index = lax.axis_index("col")
    feat_here = inputs.shape[1]
    width = feat_here * lax.axis_size("col")
    token_count = inputs.shape[0]
    heads_here = query_weight.shape[1] // HEAD_DIM
    gathered = (
        lax.all_gather(query_weight, "row", axis=0, tiled=True),
        lax.all_gather(key_weight, "row", axis=0, tiled=True),
        lax.all_gather(value_weight, "row", axis=0, tiled=True),
        lax.all_gather(out_weight, "row", axis=0, tiled=True),
        lax.all_gather(gate_weight, "row", axis=0, tiled=True),
        lax.all_gather(up_weight, "row", axis=0, tiled=True),
        lax.all_gather(down_weight, "row", axis=0, tiled=True),
        lax.all_gather(first_gain, "row", axis=0, tiled=True),
        lax.all_gather(second_gain, "row", axis=0, tiled=True),
    )
    (
        query_full,
        key_full,
        value_full,
        out_full,
        gate_full,
        up_full,
        down_full,
        gain_one,
        gain_two,
    ) = gathered
    gain_one = gain_one.astype(jnp.float32)
    gain_two = gain_two.astype(jnp.float32)
    gain_one_block = lax.dynamic_slice_in_dim(gain_one, col_index * feat_here, feat_here, 0)
    gain_two_block = lax.dynamic_slice_in_dim(gain_two, col_index * feat_here, feat_here, 0)
    input_rows = lax.all_gather(inputs, "col", axis=1, tiled=True).astype(jnp.float32)
    scale_one = lax.rsqrt(jnp.mean(input_rows * input_rows, axis=1, keepdims=True) + eps)
    unit_one = input_rows * scale_one
    normed_one = (unit_one * gain_one).astype(jnp.bfloat16)
    cosine, sine = rope_tables(positions, HEAD_DIM)
    query_pre = jnp.dot(normed_one, query_full, preferred_element_type=jnp.float32).reshape(
        token_count, heads_here, HEAD_DIM
    )
    key_pre = jnp.dot(normed_one, key_full, preferred_element_type=jnp.float32).reshape(
        token_count, heads_here, HEAD_DIM
    )
    query_rows = rotate(query_pre, cosine, sine).astype(jnp.bfloat16)
    key_rows = rotate(key_pre, cosine, sine).astype(jnp.bfloat16)
    value_rows = (
        jnp.dot(normed_one, value_full, preferred_element_type=jnp.float32)
        .astype(jnp.bfloat16)
        .reshape(token_count, heads_here, HEAD_DIM)
    )
    mixed, logsum = attend_forward(query_rows, key_rows, value_rows, segment_ids)
    input_block = inputs.astype(jnp.float32)
    attention_part = contract_last(mixed, out_full)
    attention_block = lax.psum_scatter(attention_part, "col", scatter_dimension=1, tiled=True)
    middle_block = input_block + attention_block
    middle_rows = lax.all_gather(middle_block, "col", axis=1, tiled=True)
    scale_two = lax.rsqrt(jnp.mean(middle_rows * middle_rows, axis=1, keepdims=True) + eps)
    unit_two = middle_rows * scale_two
    normed_two = (unit_two * gain_two).astype(jnp.bfloat16)
    gate_rows = jnp.dot(normed_two, gate_full, preferred_element_type=jnp.float32)
    up_rows = jnp.dot(normed_two, up_full, preferred_element_type=jnp.float32)
    sigmoid_gate = jax.nn.sigmoid(gate_rows)
    silu_gate = gate_rows * sigmoid_gate
    hidden = (silu_gate * up_rows).astype(jnp.bfloat16)
    feed_part = contract_last(hidden, down_full)
    feed_block = lax.psum_scatter(
        feed_part.astype(jnp.bfloat16), "col", scatter_dimension=1, tiled=True
    ).astype(jnp.float32)
    block_out = (middle_block + feed_block).astype(jnp.bfloat16)
    grad_rows = lax.all_gather(out_grad, "col", axis=1, tiled=True)
    hidden_grad = jnp.dot(grad_rows, down_full, preferred_element_type=jnp.float32)
    down_weight_grad = contract_first(grad_rows, hidden)
    gate_grad = (
        hidden_grad * up_rows * sigmoid_gate * (1.0 + gate_rows * (1.0 - sigmoid_gate))
    ).astype(jnp.bfloat16)
    up_grad = (hidden_grad * silu_gate).astype(jnp.bfloat16)
    gate_weight_grad = contract_first(normed_two, gate_grad)
    up_weight_grad = contract_first(normed_two, up_grad)
    normed_two_grad = contract_last(gate_grad, gate_full) + contract_last(up_grad, up_full)
    gain_two_part = jnp.sum(normed_two_grad * unit_two, axis=0)
    token_two_part = jnp.sum(normed_two_grad * gain_two * unit_two, axis=1)
    token_two, gain_two_grad = lax.psum((token_two_part, gain_two_part), "col")
    normed_two_block = lax.psum_scatter(
        normed_two_grad.astype(jnp.bfloat16), "col", scatter_dimension=1, tiled=True
    ).astype(jnp.float32)
    unit_two_block = lax.dynamic_slice_in_dim(unit_two, col_index * feat_here, feat_here, 1)
    middle_grad = out_grad.astype(jnp.float32) + scale_two * (
        normed_two_block * gain_two_block - unit_two_block * (token_two[:, None] / width)
    )
    middle_rows_grad = lax.all_gather(middle_grad.astype(jnp.bfloat16), "col", axis=1, tiled=True)
    mixed_grad = jnp.dot(middle_rows_grad, out_full, preferred_element_type=jnp.float32).astype(
        jnp.bfloat16
    )
    out_weight_grad = contract_first(middle_rows_grad, mixed)
    query_grad, key_grad, value_grad = attend_backward(
        query_rows,
        key_rows,
        value_rows,
        mixed_grad.reshape(token_count, heads_here, HEAD_DIM),
        logsum,
        segment_ids,
    )
    query_grad = (
        unrotate(query_grad, cosine, sine)
        .astype(jnp.bfloat16)
        .reshape(token_count, heads_here * HEAD_DIM)
    )
    key_grad = (
        unrotate(key_grad, cosine, sine)
        .astype(jnp.bfloat16)
        .reshape(token_count, heads_here * HEAD_DIM)
    )
    value_grad = value_grad.astype(jnp.bfloat16).reshape(token_count, heads_here * HEAD_DIM)
    query_weight_grad = contract_first(normed_one, query_grad)
    key_weight_grad = contract_first(normed_one, key_grad)
    value_weight_grad = contract_first(normed_one, value_grad)
    normed_one_grad = (
        contract_last(query_grad, query_full)
        + contract_last(key_grad, key_full)
        + contract_last(value_grad, value_full)
    )
    gain_one_part = jnp.sum(normed_one_grad * unit_one, axis=0)
    token_one_part = jnp.sum(normed_one_grad * gain_one * unit_one, axis=1)
    token_one, gain_one_grad = lax.psum((token_one_part, gain_one_part), "col")
    normed_one_block = lax.psum_scatter(
        normed_one_grad.astype(jnp.bfloat16), "col", scatter_dimension=1, tiled=True
    ).astype(jnp.float32)
    unit_one_block = lax.dynamic_slice_in_dim(unit_one, col_index * feat_here, feat_here, 1)
    input_grad = (
        middle_grad
        + scale_one
        * (normed_one_block * gain_one_block - unit_one_block * (token_one[:, None] / width))
    ).astype(jnp.bfloat16)
    summed = (
        lax.psum_scatter(
            query_weight_grad.astype(jnp.bfloat16), "row", scatter_dimension=0, tiled=True
        ).astype(jnp.float32),
        lax.psum_scatter(
            key_weight_grad.astype(jnp.bfloat16), "row", scatter_dimension=0, tiled=True
        ).astype(jnp.float32),
        lax.psum_scatter(
            value_weight_grad.astype(jnp.bfloat16), "row", scatter_dimension=0, tiled=True
        ).astype(jnp.float32),
        lax.psum_scatter(
            out_weight_grad.astype(jnp.bfloat16), "row", scatter_dimension=0, tiled=True
        ).astype(jnp.float32),
        lax.psum_scatter(
            gate_weight_grad.astype(jnp.bfloat16), "row", scatter_dimension=0, tiled=True
        ).astype(jnp.float32),
        lax.psum_scatter(
            up_weight_grad.astype(jnp.bfloat16), "row", scatter_dimension=0, tiled=True
        ).astype(jnp.float32),
        lax.psum_scatter(
            down_weight_grad.astype(jnp.bfloat16), "row", scatter_dimension=0, tiled=True
        ).astype(jnp.float32),
        lax.psum_scatter(
            gain_one_grad.astype(jnp.bfloat16), "row", scatter_dimension=0, tiled=True
        ).astype(jnp.float32),
        lax.psum_scatter(
            gain_two_grad.astype(jnp.bfloat16), "row", scatter_dimension=0, tiled=True
        ).astype(jnp.float32),
    )
    return (block_out, input_grad) + tuple(summed)


def solution(mesh):
    return jax.shard_map(
        local,
        mesh=mesh,
        in_specs=(
            P("row", "col"),
            P("row", "col"),
            P("row", "col"),
            P("row", "col"),
            P("row", "col"),
            P("row", "col"),
            P("row", "col"),
            P("row", "col"),
            P("row"),
            P("row"),
            P("row"),
            P("row"),
            P("row", "col"),
        ),
        out_specs=(
            P("row", "col"),
            P("row", "col"),
            P("row", "col"),
            P("row", "col"),
            P("row", "col"),
            P("row", "col"),
            P("row", "col"),
            P("row", "col"),
            P("row", "col"),
            P("row"),
            P("row"),
        ),
        check_vma=False,
    )
```

profile of v0, /device:TPU:0, one launch (start us, length us, event | category | flops | bytes accessed | tf_op | source)
XLA Modules:
  0.0 1178.6 jit_solution(17229201245399395030)
XLA Ops:
  12.0 13.5 %all-gather = bf16[4,1,512]{2,1,0:T(2,128)(2,1)S(1)} all-gather(bf16[1,1,512]{2,1,0:T(2,128)(2,1)S(1)} %reshape.296), channel_id=1, replica_groups=mesh['row'=4,'col'=8] {'row'}, dimensions={0}, use_global_device_ids=true | all-gather | bytes 5120 | tf_op jit(solution)/shard_map/all_gather | solution.py:183
  26.1 23.9 %all-gather.14.cloned.1.call-done = bf16[1024,2048]{1,0:T(8,128)(2,1)} async-done(((bf16[1024,256]{1,0:T(8,128)(2,1)}), bf16[1024,2048]{1,0:T(8,128)(2,1)}) %all-gather.14.cloned.1.call-update) | async-done | bytes 4194320 | tf_op jit(solution)/shard_map/all_gather | solution.py:201
  50.1 3.2 fusion.36
  53.5 3.1 multiply_convert_fusion.2
  56.6 23.0 %all-gather.18.cloned.1.call-done = bf16[2048,256]{1,0:T(8,128)(2,1)} async-done(((bf16[512,256]{1,0:T(8,128)(2,1)}), bf16[2048,256]{1,0:T(8,128)(2,1)}) %all-gather.18.cloned.1.call-update) | async-done | bytes 1048592 | tf_op jit(solution)/shard_map/all_gather | solution.py:177
  79.6 3.8 fusion.40
  83.4 25.3 %all-gather.16.cloned.1.call-done = bf16[2048,256]{1,0:T(8,128)(2,1)} async-done(((bf16[512,256]{1,0:T(8,128)(2,1)}), bf16[2048,256]{1,0:T(8,128)(2,1)}) %all-gather.16.cloned.1.call-update) | async-done | bytes 1048592 | tf_op jit(solution)/shard_map/all_gather | solution.py:176
  108.6 3.8 fusion.39
  112.8 24.7 %all-gather.20.cloned.1.call-done = bf16[2048,256]{1,0:T(8,128)(2,1)} async-done(((bf16[512,256]{1,0:T(8,128)(2,1)}), bf16[2048,256]{1,0:T(8,128)(2,1)}) %all-gather.20.cloned.1.call-update) | async-done | bytes 1048592 | tf_op jit(solution)/shard_map/all_gather | solution.py:178
  137.5 3.8 convolution_convert_fusion.8
  141.3 18.1 %while.31 = (s32[]{:T(128)}, bf16[2,512,4,64]{1,3,2,0:T(8,128)(2,1)S(1)}, f32[2,4,512]{2,1,0:T(4,128)S(1)}, s32[2]{0:T(128)S(1)}, s32[1024]{0:T(1024)S(1)}, /*in...) while((s32[]{:T(128)}, ...), condition=%wide.region_4.5_spmd, body=%wide.region_1.4_spmd.sunk | while | flops 563740160 | bytes 28924288 | solution.py:104
  147.4 3.0 fusion.118
  156.3 3.0 fusion.118
  160.0 6.4 all-gather.22.cloned.1.call-done
  166.4 5.8 fusion.41
  172.3 70.8 %reduce-scatter.12.cloned.1.call-done = f32[1024,256]{1,0:T(8,128)} async-done(((f32[1024,2048]{1,0:T(8,128)}), f32[1024,256]{1,0:T(8,128)}) %reduce-scatter.12.cloned.1.call-update) | async-done | bytes 1048592 | tf_op jit(solution)/shard_map/reduce_scatter | solution.py:222
  248.4 12.1 %all-gather.1 = bf16[4,1,512]{2,1,0:T(2,128)(2,1)S(1)} all-gather(bf16[1,1,512]{2,1,0:T(2,128)(2,1)S(1)} %reshape.298), channel_id=1, replica_groups=mesh['row'=4,'col'=8] {'row'}, dimensions={0}, use_global_device_ids=true | all-gather | bytes 5120 | tf_op jit(solution)/shard_map/all_gather | solution.py:184
  260.5 41.1 %all-gather.24.cloned.1.call-done = f32[1024,2048]{1,0:T(8,128)} async-done(((f32[1024,256]{1,0:T(8,128)}), f32[1024,2048]{1,0:T(8,128)}) %all-gather.24.cloned.1.call-update) | async-done | bytes 8388624 | tf_op jit(solution)/shard_map/all_gather | solution.py:224
  301.6 4.1 multiply_reduce_fusion.5
  307.4 6.1 multiply_convert_fusion.1
  313.4 70.6 %all-gather.28.cloned.1.call-done = bf16[2048,1024]{1,0:T(8,128)(2,1)} async-done(((bf16[512,1024]{1,0:T(8,128)(2,1)}), bf16[2048,1024]{1,0:T(8,128)(2,1)}) %all-gather.28.cloned.1.call-update) | async-done | bytes 4194320 | tf_op jit(solution)/shard_map/all_gather | solution.py:181
  384.0 9.9 fusion.43
  393.9 71.1 %all-gather.26.cloned.1.call-done = bf16[2048,1024]{1,0:T(8,128)(2,1)} async-done(((bf16[512,1024]{1,0:T(8,128)(2,1)}), bf16[2048,1024]{1,0:T(8,128)(2,1)}) %all-gather.26.cloned.1.call-update) | async-done | bytes 4194320 | tf_op jit(solution)/shard_map/all_gather | solution.py:180
  465.0 10.0 fusion.42
  475.0 70.8 %all-gather.30.cloned.1.call-done = bf16[2048,1024]{1,0:T(8,128)(2,1)} async-done(((bf16[512,1024]{1,0:T(8,128)(2,1)}), bf16[2048,1024]{1,0:T(8,128)(2,1)}) %all-gather.30.cloned.1.call-update) | async-done | bytes 4194320 | tf_op jit(solution)/shard_map/all_gather | solution.py:182
  545.8 38.0 %all-gather.32.cloned.1.call-done = bf16[1024,2048]{1,0:T(8,128)(2,1)} async-done(((bf16[1024,256]{1,0:T(8,128)(2,1)}), bf16[1024,2048]{1,0:T(8,128)(2,1)}) %all-gather.32.cloned.1.call-update) | async-done | bytes 4194320 | tf_op jit(solution)/shard_map/all_gather | solution.py:238
  583.9 14.0 %multiply_convert_fusion.3 = (bf16[1024,1024]{1,0:T(8,128)(2,1)}, bf16[1024,1024]{1,0:T(8,128)(2,1)S(1)}, bf16[1024,1024]{1,0:T(8,128)(2,1)}) fusion(f32[1024,1024]{1,0:T(8,128)} %fusion.42, f32[1024,1024]{1,0:T(8,128)} %fusion.43, bf16[1024,2048]{1,0:T(8,128)(2,1)} %all-gather.32.cloned.1.call-done, bf16[2048,1024]{1,0:T(8,128)(2,1)} %all-gather.30.cloned.1.call-done), kind=kOutput, calls=%fused_computation.59 | convolution fusion | flops 4310695936 | bytes 23068672 | tf_op jit(solution)/shard_map/dot_general | solution.py:239
  597.8 7.2 fusion.44
  605.1 11.7 multiply_reduce_fusion.1
  617.0 13.1 %psum.28 = f32[1024]{0:T(1024)S(1)} all-reduce(f32[1024]{0:T(1024)S(1)} %get-tuple-element.329), channel_id=1, replica_groups=mesh['row'=4,'col'=8] {'col'}, use_global_device_ids=true, to_apply=%region_10.11 | all-reduce | flops 1024 | bytes 8192 | tf_op jit(solution)/shard_map/psum | solution.py:250
  630.1 38.3 %reduce-scatter.16.cloned.1.call-done = bf16[1024,256]{1,0:T(8,128)(2,1)} async-done(((bf16[1024,2048]{1,0:T(8,128)(2,1)}), bf16[1024,256]{1,0:T(8,128)(2,1)}) %reduce-scatter.16.cloned.1.call-update) | async-done | bytes 524304 | tf_op jit(solution)/shard_map/reduce_scatter | solution.py:251
  668.4 2.5 fusion.38
  670.9 9.4 convolution_convert_fusion.2
  680.6 9.4 convert_bitcast_fusion
  690.0 9.5 convolution_convert_fusion
  699.6 9.6 convolution_convert_fusion.1
  709.4 4.5 convolution_convert_fusion.3
  714.3 4.6 convolution_convert_fusion.7
  718.9 54.1 %while.32 = (s32[]{:T(128)}, f32[1024,4,64]{0,2,1:T(8,128)S(1)}, f32[1024,4,64]{0,2,1:T(8,128)}, f32[2,512,4,64]{1,0,3,2:T(2,128)}, s32[2]{0:T(128)S(1)}, /*inde...) while((s32[]{:T(128)}, f32[1024,4,64]{0,2,1:T(8,128)S(1)}, ...), condition=%wide.region_13.14_spmd.clone, body=%wide.region_11.13_spmd.clone.sunk | while | flops 1376648704 | bytes 82917864 | solution.py:149
  722.1 3.6 fusion.130
  725.7 4.5 multiply_reduce_fusion.7
  730.3 2.4 multiply_convert_fusion.7
  735.6 10.4 dynamic_update_slice.29
  749.1 3.6 fusion.130
  752.7 4.5 multiply_reduce_fusion.7
  757.3 2.4 multiply_convert_fusion.7
  762.6 10.4 dynamic_update_slice.29
  774.3 4.6 convolution_convert_fusion.4
  783.5 2.4 convolution_convert_fusion.6
  786.0 4.6 convolution_convert_fusion.5
  793.4 8.5 multiply_reduce_fusion.2
  805.8 36.4 %reduce-scatter.32.cloned.1.call-done = bf16[512,1024]{0,1:T(8,128)(2,1)} async-done(((bf16[2048,1024]{0,1:T(8,128)(2,1)}), bf16[512,1024]{0,1:T(8,128)(2,1)}) %reduce-scatter.32.cloned.1.call-update) | async-done | bytes 1048592 | tf_op jit(solution)/shard_map/reduce_scatter | solution.py:321
  842.1 2.6 copy.30
  844.7 76.8 %reduce-scatter.30.cloned.1.call-done = bf16[512,1024]{1,0:T(8,128)(2,1)} async-done(((bf16[2048,1024]{1,0:T(8,128)(2,1)}), bf16[512,1024]{1,0:T(8,128)(2,1)}) %reduce-scatter.30.cloned.1.call-update) | async-done | bytes 1048592 | tf_op jit(solution)/shard_map/reduce_scatter | solution.py:318
  921.6 2.8 convert_element_type.201
  924.3 76.8 %reduce-scatter.28.cloned.1.call-done = bf16[512,1024]{1,0:T(8,128)(2,1)} async-done(((bf16[2048,1024]{1,0:T(8,128)(2,1)}), bf16[512,1024]{1,0:T(8,128)(2,1)}) %reduce-scatter.28.cloned.1.call-update) | async-done | bytes 1048592 | tf_op jit(solution)/shard_map/reduce_scatter | solution.py:315
  1001.1 2.8 convert_element_type.199
  1003.9 25.2 %all-reduce.2 = (f32[1024]{0:T(1024)S(1)}, bf16[2048]{0:T(1024)(128)(2,1)S(1)}, bf16[2048]{0:T(1024)(128)(2,1)S(1)}) all-reduce(f32[1024]{0:T(1024)S(1)} %get-tuple-element.331, f32[2048]{0:T(1024)S(1)} %get-tuple-element.330, f32[2048]{0:T(1024)S(1)} %copy-done.28), channel_id=1, replica_groups=mesh['row'=4,'col'=8] {'col'}, use_global_device_ids=true, to_apply=%region_16.17 | all-reduce | flops 5120 | bytes 32768 | tf_op jit(solution)/shard_map/psum | solution.py:292
  1029.1 11.4 all-reduce.3
  1043.7 15.5 %reduce-scatter.24.cloned.1.call-done = bf16[512,256]{1,0:T(8,128)(2,1)} async-done(((bf16[2048,256]{1,0:T(8,128)(2,1)}), bf16[512,256]{1,0:T(8,128)(2,1)}) %reduce-scatter.24.cloned.1.call-update) | async-done | bytes 262160 | tf_op jit(solution)/shard_map/reduce_scatter | solution.py:309
  1061.0 26.2 %reduce-scatter.20.cloned.1.call-done = bf16[512,256]{1,0:T(8,128)(2,1)} async-done(((bf16[2048,256]{1,0:T(8,128)(2,1)}), bf16[512,256]{1,0:T(8,128)(2,1)}) %reduce-scatter.20.cloned.1.call-update) | async-done | bytes 262160 | tf_op jit(solution)/shard_map/reduce_scatter | solution.py:303
  1088.9 26.5 %reduce-scatter.22.cloned.1.call-done = bf16[512,256]{1,0:T(8,128)(2,1)} async-done(((bf16[2048,256]{1,0:T(8,128)(2,1)}), bf16[512,256]{1,0:T(8,128)(2,1)}) %reduce-scatter.22.cloned.1.call-update) | async-done | bytes 262160 | tf_op jit(solution)/shard_map/reduce_scatter | solution.py:306
  1117.2 51.6 %reduce-scatter.18.cloned.1.call-done = bf16[1024,256]{1,0:T(8,128)(2,1)} async-done(((bf16[1024,2048]{1,0:T(8,128)(2,1)}), bf16[1024,256]{1,0:T(8,128)(2,1)}) %reduce-scatter.18.cloned.1.call-update) | async-done | bytes 524304 | tf_op jit(solution)/shard_map/reduce_scatter | solution.py:293
  1168.7 2.9 add_convert_fusion
  (195 shorter events, 55.9 us)
Async XLA Ops:
  7.2 42.9 %all-gather.14.cloned.1.call-start = ((), (), s32[]{:S(2)}) async-start(), calls=%async_computation.11 | async-start | bytes 4718592 | tf_op jit(solution)/shard_map/all_gather | solution.py:201
  7.9 71.7 %all-gather.18.cloned.1.call-start = ((), (), s32[]{:S(2)}) async-start(), calls=%async_computation.13 | async-start | bytes 1310720 | tf_op jit(solution)/shard_map/all_gather | solution.py:177
  8.7 100.0 %all-gather.16.cloned.1.call-start = ((), (), s32[]{:S(2)}) async-start(), calls=%async_computation.12 | async-start | bytes 1310720 | tf_op jit(solution)/shard_map/all_gather | solution.py:176
  9.4 128.1 %all-gather.20.cloned.1.call-start = ((), (), s32[]{:S(2)}) async-start(), calls=%async_computation.14 | async-start | bytes 1310720 | tf_op jit(solution)/shard_map/all_gather | solution.py:178
  10.0 156.4 %all-gather.22.cloned.1.call-start = ((), (), s32[]{:S(2)}) async-start(), calls=%async_computation.15 | async-start | bytes 1310720 | tf_op jit(solution)/shard_map/all_gather | solution.py:179
  10.6 232.6 %reduce-scatter.12.cloned.1.call-start = ((), (), s32[]{:S(2)}) async-start(), calls=%async_computation.16 | async-start | bytes 9437184 | tf_op jit(solution)/shard_map/reduce_scatter | solution.py:222
  25.6 31.0 %copy-start.18 = (f32[4,1,512]{2,1,0:T(1,128)}, f32[4,1,512]{2,1,0:T(1,128)S(1)}, u32[]{:S(2)}) copy-start(f32[4,1,512]{2,1,0:T(1,128)S(1)} %convert_element_type.209) | copy-start | bytes 24580
  26.1 86.3 %copy-start.8 = (f32[1024,32]{0,1:T(8,128)}, f32[1024,32]{0,1:T(8,128)S(1)}, u32[]{:S(2)}) copy-start(f32[1024,32]{0,1:T(8,128)S(1)} %get-tuple-element.399) | copy-start | bytes 393220
  26.1 86.3 %copy-start.10 = (f32[1024,32]{0,1:T(8,128)}, f32[1024,32]{0,1:T(8,128)S(1)}, u32[]{:S(2)}) copy-start(f32[1024,32]{0,1:T(8,128)S(1)} %get-tuple-element.400) | copy-start | bytes 393220
  50.1 3.4 copy-start
  53.3 3.3 copy-start.20
  112.8 28.5 %copy-start.17 = (s32[1024]{0:T(1024)S(1)}, s32[1024]{0:T(1024)}, u32[]{:S(2)}) copy-start(s32[1024]{0:T(1024)} %param.27) | copy-start | bytes 12292
  172.2 70.9 %copy-start.6 = (bf16[1024,256]{1,0:T(8,128)(2,1)S(1)}, bf16[1024,256]{1,0:T(8,128)(2,1)}, u32[]{:S(2)}) copy-start(bf16[1024,256]{1,0:T(8,128)(2,1)} %param.17) | copy-start | bytes 1572868
  172.3 76.1 %copy-start.29 = (bf16[512]{0:T(512)(128)(2,1)S(1)}, bf16[512]{0:T(512)(128)(2,1)}, u32[]{:S(2)}) copy-start(bf16[512]{0:T(512)(128)(2,1)} %param.26) | copy-start | bytes 3076
  172.3 129.3 %all-gather.24.cloned.1.call-start = ((), (), s32[]{:S(2)}) async-start(), calls=%async_computation.17 | async-start | bytes 9437184 | tf_op jit(solution)/shard_map/all_gather | solution.py:224
  245.5 138.5 %all-gather.28.cloned.1.call-start = ((), (), s32[]{:S(2)}) async-start(), calls=%async_computation.19 | async-start | bytes 5242880 | tf_op jit(solution)/shard_map/all_gather | solution.py:181
  246.2 218.8 %all-gather.26.cloned.1.call-start = ((), (), s32[]{:S(2)}) async-start(), calls=%async_computation.18 | async-start | bytes 5242880 | tf_op jit(solution)/shard_map/all_gather | solution.py:180
  247.0 298.9 %all-gather.30.cloned.1.call-start = ((), (), s32[]{:S(2)}) async-start(), calls=%async_computation.20 | async-start | bytes 5242880 | tf_op jit(solution)/shard_map/all_gather | solution.py:182
  247.6 336.3 %all-gather.32.cloned.1.call-start = ((), (), s32[]{:S(2)}) async-start(), calls=%async_computation.22 | async-start | bytes 4718592 | tf_op jit(solution)/shard_map/all_gather | solution.py:238
  248.3 420.1 %reduce-scatter.16.cloned.1.call-start = ((), (), s32[]{:S(2)}) async-start(), calls=%async_computation.23 | async-start | bytes 4718592 | tf_op jit(solution)/shard_map/reduce_scatter | solution.py:251
  301.6 5.8 copy-start.1
  305.8 362.6 %copy-start.22 = (f32[1024]{0:T(1024)}, f32[1024]{0:T(1024)S(1)}, u32[]{:S(2)}) copy-start(f32[1024]{0:T(1024)S(1)} %add_rsqrt_fusion) | copy-start | bytes 12292
  583.9 14.0 %copy-start.31 = (bf16[2048,1024]{1,0:T(8,128)(2,1)S(1)}, bf16[2048,1024]{1,0:T(8,128)(2,1)}, u32[]{:S(2)}) copy-start(bf16[2048,1024]{1,0:T(8,128)(2,1)} %all-gather.26.cloned.1.call-done) | copy-start | bytes 12582916
  597.8 7.2 copy-start.33
  597.8 7.2 copy-start.30
  616.8 51.5 %copy-start.3 = (bf16[1024,256]{1,0:T(8,128)(2,1)S(1)}, bf16[1024,256]{1,0:T(8,128)(2,1)}, u32[]{:S(2)}) copy-start(bf16[1024,256]{1,0:T(8,128)(2,1)} %param.29) | copy-start | bytes 1572868
  616.9 92.5 %all-gather.34.cloned.1.call-start = ((), (), s32[]{:S(2)}) async-start(), calls=%async_computation.24 | async-start | bytes 4718592 | tf_op jit(solution)/shard_map/all_gather | solution.py:258
  617.0 63.4 %copy-start.26 = (f32[256]{0:T(256)}, f32[256]{0:T(256)S(1)}, u32[]{:S(2)}) copy-start(f32[256]{0:T(256)S(1)} %dynamic_slice.62) | copy-start | bytes 3076
  630.1 50.3 %copy-start.24 = (f32[1024]{0:T(1024)}, f32[1024]{0:T(1024)S(1)}, u32[]{:S(2)}) copy-start(f32[1024]{0:T(1024)S(1)} %broadcast_multiply_fusion.2) | copy-start | bytes 12292
  670.9 132.9 %reduce-scatter.14.cloned.1.call-start = ((), (), s32[]{:S(2)}) async-start(), calls=%async_computation.21 | async-start | bytes 4718592 | tf_op jit(solution)/shard_map/reduce_scatter | solution.py:234
  680.4 161.8 %reduce-scatter.32.cloned.1.call-start = ((), (), s32[]{:S(2)}) async-start(), calls=%async_computation.32 | async-start | bytes 5242880 | tf_op jit(solution)/shard_map/reduce_scatter | solution.py:321
  690.0 231.6 %reduce-scatter.30.cloned.1.call-start = ((), (), s32[]{:S(2)}) async-start(), calls=%async_computation.31 | async-start | bytes 5242880 | tf_op jit(solution)/shard_map/reduce_scatter | solution.py:318
  699.6 301.5 %reduce-scatter.28.cloned.1.call-start = ((), (), s32[]{:S(2)}) async-start(), calls=%async_computation.30 | async-start | bytes 5242880 | tf_op jit(solution)/shard_map/reduce_scatter | solution.py:315
  709.3 332.6 %reduce-scatter.26.cloned.1.call-start = ((), (), s32[]{:S(2)}) async-start(), calls=%async_computation.29 | async-start | bytes 1310720 | tf_op jit(solution)/shard_map/reduce_scatter | solution.py:312
  713.9 345.3 %reduce-scatter.24.cloned.1.call-start = ((), (), s32[]{:S(2)}) async-start(), calls=%async_computation.28 | async-start | bytes 1310720 | tf_op jit(solution)/shard_map/reduce_scatter | solution.py:309
  720.8 1.3 copy-start.15
  725.7 4.6 copy-start.16
  747.8 1.3 copy-start.15
  752.7 4.6 copy-start.16
  774.3 7.0 copy-start.9
  774.3 7.0 copy-start.11
  778.9 308.2 %reduce-scatter.20.cloned.1.call-start = ((), (), s32[]{:S(2)}) async-start(), calls=%async_computation.26 | async-start | bytes 1310720 | tf_op jit(solution)/shard_map/reduce_scatter | solution.py:303
  781.3 2.2 copy-start.5
  785.9 329.5 %reduce-scatter.22.cloned.1.call-start = ((), (), s32[]{:S(2)}) async-start(), calls=%async_computation.27 | async-start | bytes 1310720 | tf_op jit(solution)/shard_map/reduce_scatter | solution.py:306
  786.0 4.7 copy-start.12
  790.6 378.1 %reduce-scatter.18.cloned.1.call-start = ((), (), s32[]{:S(2)}) async-start(), calls=%async_computation.25 | async-start | bytes 4718592 | tf_op jit(solution)/shard_map/reduce_scatter | solution.py:293
  790.7 1.3 copy-start.13
  792.0 1.4 copy-start.14
  792.0 1.4 copy-start.19
  792.0 1.4 copy-start.21
  801.9 0.7 copy-start.32
  801.9 1.9 copy-start.2
  805.8 198.2 %copy-start.28 = (f32[2048]{0:T(1024)S(1)}, f32[2048]{0:T(1024)}, u32[]{:S(2)}) copy-start(f32[2048]{0:T(1024)} %get-tuple-element.328) | copy-start | bytes 24580
  844.7 324.0 %copy-start.4 = (bf16[1024,256]{1,0:T(8,128)(2,1)S(1)}, bf16[1024,256]{1,0:T(8,128)(2,1)}, u32[]{:S(2)}) copy-start(bf16[1024,256]{1,0:T(8,128)(2,1)} %param.29) | copy-start | bytes 1572868
  844.7 324.0 %copy-start.7 = (bf16[1024,256]{1,0:T(8,128)(2,1)S(1)}, bf16[1024,256]{1,0:T(8,128)(2,1)}, u32[]{:S(2)}) copy-start(bf16[1024,256]{1,0:T(8,128)(2,1)} %reduce-scatter.16.cloned.1.call-done) | copy-start | bytes 1572868
  844.7 324.0 %copy-start.23 = (f32[1024]{0:T(1024)S(1)}, f32[1024]{0:T(1024)}, u32[]{:S(2)}) copy-start(f32[1024]{0:T(1024)} %copy-done.22) | copy-start | bytes 12292
  844.7 324.0 %copy-start.25 = (f32[1024]{0:T(1024)S(1)}, f32[1024]{0:T(1024)}, u32[]{:S(2)}) copy-start(f32[1024]{0:T(1024)} %copy-done.24) | copy-start | bytes 12292
  844.7 324.0 %copy-start.27 = (f32[256]{0:T(256)S(1)}, f32[256]{0:T(256)}, u32[]{:S(2)}) copy-start(f32[256]{0:T(256)} %copy-done.26) | copy-start | bytes 3076
Sparse Core Ops, SparseCore 0:
  9.9 40.1 all-gather.13
  51.6 27.9 all-gather.17
  81.2 27.4 all-gather.15
  110.0 27.4 all-gather.19
  138.9 27.4 all-gather.21
  172.4 70.7 reduce-scatter.11
  245.6 55.9 all-gather.23
  303.2 80.7 all-gather.27
  385.7 79.2 all-gather.25
  466.5 79.2 all-gather.29
  547.9 35.9 all-gather.31
  617.0 51.3 reduce-scatter.15
  671.0 37.4 all-gather.33
  711.7 51.3 reduce-scatter.13
  765.3 76.7 reduce-scatter.31
  844.3 77.2 reduce-scatter.29
  923.8 77.2 reduce-scatter.27
  1003.3 27.6 reduce-scatter.25
  1033.4 25.7 reduce-scatter.23
  1061.3 25.7 reduce-scatter.19
  1089.5 25.8 reduce-scatter.21
  1118.7 49.9 reduce-scatter.17
where the time goes:
time: 1190 us; the launch traced here: 1180 us
  waiting for transfers between devices  820 us (69%)
  matrix products  173 us (15%)
  blocking collectives  75.4 us (6%)
  other arithmetic  54.9 us (5%)
  local copies, waits for them, and re-layouts  35.6 us (3%)
  between operations  15.7 us (1%)
    reduce_scatter x1, waiting for transfers between devices, local(): lax.psum_scatter(up_weight_grad.astype(jnp.bfloat16), 'row', scatter_dime...  76.8 us
    reduce_scatter x1, waiting for transfers between devices, local(): lax.psum_scatter(gate_weight_grad.astype(jnp.bfloat16), 'row', scatter_di...  76.8 us
    all_gather x1, waiting for transfers between devices, local(): lax.all_gather(gate_weight, 'row', axis=0, tiled=True)  71.1 us
    reduce_scatter x1, waiting for transfers between devices, local(): lax.psum_scatter(attention_part, 'col', scatter_dimension=1, tiled=True)  70.8 us
    all_gather x1, waiting for transfers between devices, local(): lax.all_gather(down_weight, 'row', axis=0, tiled=True)  70.8 us
    all_gather x1, waiting for transfers between devices, local(): lax.all_gather(up_weight, 'row', axis=0, tiled=True)  70.6 us
    reduce_scatter x1, waiting for transfers between devices, local(): lax.psum_scatter(normed_one_grad.astype(jnp.bfloat16), 'col', scatter_dim...  51.6 us
    dot_general x7, matrix products, contract_last(): lax.dot_general(left, right, (((1,), (1,)), ((), ())), preferred_element_...  45.3 us
  transfers between devices with their start and end apart: 22, of which 19 were waited for; matrix products, arithmetic and copies ran while one was open for 18% of the time, Pallas kernels for 0%

commit v1 on v0

v1 whole, which is shorter than its diff:
```python
import functools
import math

import jax
import jax.numpy as jnp
from jax import lax
from jax.experimental import pallas as pl
from jax.experimental.pallas import tpu as pltpu
from jax.sharding import PartitionSpec as P

HEAD_DIM = 64
LANES = 128
EPS = 1e-05
ROPE_BASE = 130000.0
LOG2E = math.log2(math.e)
SCORE_SCALE = HEAD_DIM**-0.5
BF16 = jnp.bfloat16
F32 = jnp.float32
VMEM_BYTES = 56 * 1024 * 1024


def nn(left, right):
    return lax.dot_general(left, right, (((1,), (0,)), ((), ())), preferred_element_type=F32)


def nt(left, right):
    return lax.dot_general(left, right, (((1,), (1,)), ((), ())), preferred_element_type=F32)


def tn(left, right):
    return lax.dot_general(left, right, (((0,), (0,)), ((), ())), preferred_element_type=F32)


def spin(values, cosine, sine_front, sine_back):
    half = HEAD_DIM // 2
    lanes = values.shape[-1]
    return (
        values * cosine
        + pltpu.roll(values, lanes - half, 1) * sine_front
        + pltpu.roll(values, half, 1) * sine_back
    )


def weave(own, other, feat):
    pieces = []
    for at in range(0, own.shape[1], feat):
        pieces += [own[:, at : at + feat], other[:, at : at + feat]]
    return jnp.concatenate(pieces, axis=1)


def norm_scale(values):
    wide = values.astype(F32)
    return lax.rsqrt(jnp.sum(wide * wide, axis=1, keepdims=True) / values.shape[1] + EPS)


def whole_spec(a):
    return pl.BlockSpec(a.shape, lambda i: (0,) * a.ndim, pipeline_mode=pl.Buffered(1))


def row_spec(block, a):
    return pl.BlockSpec((block, a.shape[1]), lambda i: (i, 0))


def project_kernel(feat, own_ref, other_ref, weight_ref, cos_ref, front_ref, back_ref, q_ref, k_ref, v_ref, scale_ref):
    values = weave(own_ref[...], other_ref[...], feat)
    scale = norm_scale(values)
    scale_ref[...] = scale
    heads = q_ref.shape[1]
    cosine, front, back = cos_ref[...], front_ref[...], back_ref[...]
    for at, ref in enumerate((q_ref, k_ref, v_ref)):
        result = nn(values, weight_ref[:, at * heads : (at + 1) * heads]) * scale
        if at < 2:
            result = spin(result, cosine, front, back)
        ref[...] = result.astype(BF16)


def project(feat, own, other, weight, cosine, front, back):
    tokens = own.shape[0]
    heads = weight.shape[1] // 3
    block = 256
    result = jax.ShapeDtypeStruct((tokens, heads), BF16)
    scale = jax.ShapeDtypeStruct((tokens, 1), F32)
    return pl.pallas_call(
        functools.partial(project_kernel, feat),
        grid=(tokens // block,),
        in_specs=[row_spec(block, own), row_spec(block, other), whole_spec(weight)]
        + [row_spec(block, cosine)] * 3,
        out_specs=[row_spec(block, result)] * 3 + [row_spec(block, scale)],
        out_shape=[result] * 3 + [scale],
        compiler_params=pltpu.CompilerParams(vmem_limit_bytes=VMEM_BYTES),
        name="project",
    )(own, other, weight, cosine, front, back)


def unfold_kernel(feat, groups, *refs):
    count = sum(groups)
    lefts, weights = refs[: len(groups)], refs[len(groups) : len(groups) + count]
    own_ref, other_ref = refs[-2:]
    for at in range(0, own_ref.shape[1], feat):
        rows = slice(2 * at, 2 * (at + feat))
        total = None
        ids = iter(weights)
        for left, number in zip(lefts, groups):
            part = left.shape[1] // number
            for i in range(number):
                term = nt(left[:, i * part : (i + 1) * part], next(ids)[rows, :])
                total = term if total is None else total + term
        own_ref[:, at : at + feat] = total[:, :feat].astype(own_ref.dtype)
        other_ref[:, at : at + feat] = total[:, feat:].astype(BF16)


def unfold(feat, name, *pairs):
    lefts = [left for left, _ in pairs]
    weights = [w for _, ws in pairs for w in ws]
    tokens, half = lefts[0].shape[0], weights[0].shape[0] // 2
    block = 256
    own = jax.ShapeDtypeStruct((tokens, half), F32)
    other = jax.ShapeDtypeStruct((tokens, half), BF16)
    return pl.pallas_call(
        functools.partial(unfold_kernel, feat, tuple(len(ws) for _, ws in pairs)),
        grid=(tokens // block,),
        in_specs=[row_spec(block, a) for a in lefts] + [whole_spec(w) for w in weights],
        out_specs=[row_spec(block, own), row_spec(block, other)],
        out_shape=[own, other],
        compiler_params=pltpu.CompilerParams(vmem_limit_bytes=VMEM_BYTES),
        name=name,
    )(*lefts, *weights)


def hidden_kernel(feat, count, *refs):
    m_own, m_other, g_own, g_other = refs[:4]
    gates, ups, downs = (refs[4 + i * count : 4 + (i + 1) * count] for i in range(3))
    hidden_ref, gate_ref, up_ref, gate_scaled_ref, up_scaled_ref = refs[4 + 3 * count :]
    middle = weave(m_own[...], m_other[...], feat)
    grad = weave(g_own[...], g_other[...], feat)
    scale = norm_scale(middle)
    part = hidden_ref.shape[1] // count
    for i in range(count):
        columns = slice(i * part, (i + 1) * part)
        gate = nn(middle, gates[i][...]) * scale
        up = nn(middle, ups[i][...]) * scale
        hidden_grad = nn(grad, downs[i][...])
        sigmoid = 1.0 / (1.0 + jnp.exp(-gate))
        silu = gate * sigmoid
        hidden_ref[:, columns] = (silu * up).astype(BF16)
        gate_grad = hidden_grad * up * (sigmoid + silu * (1.0 - sigmoid))
        up_grad = hidden_grad * silu
        gate_ref[:, columns] = gate_grad.astype(BF16)
        up_ref[:, columns] = up_grad.astype(BF16)
        gate_scaled_ref[:, columns] = (gate_grad * scale).astype(BF16)
        up_scaled_ref[:, columns] = (up_grad * scale).astype(BF16)


def hidden_units(feat, halves, gates, ups, downs):
    tokens = halves[0].shape[0]
    count, part = len(gates), gates[0].shape[1]
    block = 256
    result = jax.ShapeDtypeStruct((tokens, count * part), BF16)
    weights = gates + ups + downs
    return pl.pallas_call(
        functools.partial(hidden_kernel, feat, count),
        grid=(tokens // block,),
        in_specs=[row_spec(block, a) for a in halves] + [whole_spec(w) for w in weights],
        out_specs=[row_spec(block, result)] * 5,
        out_shape=[result] * 5,
        compiler_params=pltpu.CompilerParams(vmem_limit_bytes=VMEM_BYTES),
        name="hidden_units",
    )(*halves, *weights)


def allowed_block(start_row, key_base, query_base, keys, queries):
    key_index = key_base + lax.broadcasted_iota(jnp.int32, (keys, queries), 0)
    query_index = query_base + lax.broadcasted_iota(jnp.int32, (keys, queries), 1)
    return (key_index >= start_row) & (key_index <= query_index)


def attend_kernel(q_ref, k_ref, v_ref, start_ref, out_ref, log_ref):
    tokens = q_ref.shape[0]
    block = 256
    keys_all = k_ref[...]
    values_turned = v_ref[...].T
    lane = lax.broadcasted_iota(jnp.int32, (1, LANES), 1)
    sub = lax.broadcasted_iota(jnp.int32, (LANES, 1), 0)
    for place in range(tokens // block):
        rows = slice(place * block, (place + 1) * block)
        reach = (place + 1) * block
        query = q_ref[rows, :]
        start_row = start_ref[:, rows]
        allowed = allowed_block(start_row, 0, place * block, reach, block)
        parts = []
        for head in range(LANES // HEAD_DIM):
            mine = lane // HEAD_DIM == head
            query_head = query * mine.astype(BF16)
            scores = nt(keys_all[:reach], query_head) * (SCORE_SCALE * LOG2E)
            scores = jnp.where(allowed, scores, -1e30)
            peak = jnp.max(scores, axis=0, keepdims=True)
            raised = jnp.exp2(scores - peak)
            total = jnp.sum(raised, axis=0, keepdims=True)
            mixed = nn(values_turned[:, :reach], raised.astype(BF16)) / total
            parts.append(mixed)
            log_ref[0, head : head + 1, rows] = peak + jnp.log2(total)
        joined = jnp.where(sub // HEAD_DIM == 0, parts[0], parts[1])
        out_ref[rows, :] = joined.T.astype(BF16)


def attend(query, key, value, start_row):
    tokens, width = query.shape
    pairs = width // LANES
    column = pl.BlockSpec((tokens, LANES), lambda i: (0, i))
    return pl.pallas_call(
        attend_kernel,
        grid=(pairs,),
        in_specs=[column, column, column, pl.BlockSpec((1, tokens), lambda i: (0, 0))],
        out_specs=[column, pl.BlockSpec((1, 2, tokens), lambda i: (i, 0, 0))],
        out_shape=[
            jax.ShapeDtypeStruct((tokens, width), BF16),
            jax.ShapeDtypeStruct((pairs, 2, tokens), F32),
        ],
        compiler_params=pltpu.CompilerParams(vmem_limit_bytes=VMEM_BYTES),
        name="attend",
    )(query, key, value, start_row)


def attend_back_kernel(
    q_ref, k_ref, v_ref, o_ref, do_ref, start_ref, log_ref, cos_ref, front_ref, back_ref,
    dq_ref, dk_ref, dv_ref, dq_acc,
):
    tokens = q_ref.shape[0]
    block = 256
    lane = lax.broadcasted_iota(jnp.int32, (1, LANES), 1)
    sub = lax.broadcasted_iota(jnp.int32, (LANES, 1), 0)
    query_all = q_ref[...]
    grad_all = do_ref[...]
    product = (o_ref[...].astype(F32) * grad_all.astype(F32)).T
    dots = [
        jnp.sum(product[head * HEAD_DIM : (head + 1) * HEAD_DIM], axis=0, keepdims=True)
        for head in range(LANES // HEAD_DIM)
    ]
    dq_acc[...] = jnp.zeros_like(dq_acc)
    for place in range(tokens // block):
        rows = slice(place * block, (place + 1) * block)
        tail = slice(place * block, tokens)
        keys = k_ref[rows, :]
        values = v_ref[rows, :]
        keys_turned = keys.T
        query = query_all[place * block :]
        grad = grad_all[place * block :]
        start_row = start_ref[:, tail]
        allowed = allowed_block(
            start_row, place * block, place * block, block, tokens - place * block
        )
        key_grad = jnp.zeros((block, LANES), F32)
        value_grad = jnp.zeros((block, LANES), F32)
        for head in range(LANES // HEAD_DIM):
            mine = lane // HEAD_DIM == head
            scores = nt(keys * mine.astype(BF16), query) * (SCORE_SCALE * LOG2E)
            weights = jnp.where(allowed, jnp.exp2(scores - log_ref[0, head : head + 1, tail]), 0.0)
            weight_grad = nt(values * mine.astype(BF16), grad)
            score_grad = (weights * (weight_grad - dots[head][:, place * block :])).astype(BF16)
            value_grad = jnp.where(mine, nn(weights.astype(BF16), grad), value_grad)
            key_grad = jnp.where(mine, nn(score_grad, query), key_grad)
            dq_acc[:, tail] += nn(
                keys_turned * (sub // HEAD_DIM == head).astype(BF16), score_grad
            )
        dv_ref[rows, :] = value_grad.astype(BF16)
        dk_ref[rows, :] = spin(
            key_grad * SCORE_SCALE, cos_ref[rows, :], -front_ref[rows, :], -back_ref[rows, :]
        ).astype(BF16)
    dq_ref[...] = spin(
        dq_acc[...].T * SCORE_SCALE, cos_ref[...], -front_ref[...], -back_ref[...]
    ).astype(BF16)


def attend_back(query, key, value, mixed, mixed_grad, start_row, logs, cosine, front, back):
    tokens, width = query.shape
    pairs = width // LANES
    column = pl.BlockSpec((tokens, LANES), lambda i: (0, i))
    table = pl.BlockSpec((tokens, LANES), lambda i: (0, 0))
    return pl.pallas_call(
        attend_back_kernel,
        grid=(pairs,),
        in_specs=[
            column, column, column, column, column,
            pl.BlockSpec((1, tokens), lambda i: (0, 0)),
            pl.BlockSpec((1, 2, tokens), lambda i: (i, 0, 0)),
            table, table, table,
        ],
        out_specs=[column, column, column],
        out_shape=[jax.ShapeDtypeStruct((tokens, width), BF16)] * 3,
        scratch_shapes=[pltpu.VMEM((LANES, tokens), F32)],
        compiler_params=pltpu.CompilerParams(vmem_limit_bytes=VMEM_BYTES),
        name="attend_back",
    )(query, key, value, mixed, mixed_grad, start_row, logs, cosine, front, back)


def rope_tables(positions, width):
    half = HEAD_DIM // 2
    freqs = jnp.exp(jnp.arange(half, dtype=F32) * (-2.0 * math.log(ROPE_BASE) / HEAD_DIM))
    angles = positions.astype(F32)[:, None] * freqs[None, :]
    cosine, sine = jnp.cos(angles), jnp.sin(angles)
    zero = jnp.zeros_like(sine)
    heads = width // HEAD_DIM
    return (
        jnp.tile(cosine, (1, 2 * heads)),
        jnp.tile(jnp.concatenate([-sine, zero], axis=1), (1, heads)),
        jnp.tile(jnp.concatenate([zero, sine], axis=1), (1, heads)),
    )


def local(
    inputs,
    query_weight,
    key_weight,
    value_weight,
    out_weight,
    gate_weight,
    up_weight,
    down_weight,
    first_gain,
    second_gain,
    segment_ids,
    positions,
    out_grad,
):
    rows = lax.axis_size("row")
    cols = lax.axis_size("col")
    places = cols // 2
    row = lax.axis_index("row")
    col = lax.axis_index("col")
    core = col % 2
    place = col // 2
    tokens, feat = inputs.shape
    width = feat * cols
    half = width // 2
    quarter = tokens // places

    def core_swap(a):
        return lax.ppermute(a, "col", [(i, i ^ 1) for i in range(cols)])

    def plane_swap(a, step):
        return lax.ppermute(a, "col", [(i, i ^ (2 * step)) for i in range(cols)])

    def token_part(a, step):
        return lax.dynamic_slice_in_dim(a, (place ^ step) * quarter, quarter, 0)

    def feat_part(a, step):
        return lax.dynamic_slice_in_dim(a, (place ^ step) * feat, feat, 1)

    def own_first(w):
        return jnp.concatenate(
            [jnp.where(core == 0, w[:feat], w[feat:]), jnp.where(core == 0, w[feat:], w[:feat])], axis=0
        )

    def shift(a, step):
        return lax.ppermute(a, "row", [(i, (i + step) % rows) for i in range(rows)])

    def put_rows(pieces):
        whole = jnp.zeros((tokens,) + pieces[0].shape[1:], pieces[0].dtype)
        for step, piece in enumerate(pieces):
            whole = lax.dynamic_update_slice_in_dim(whole, piece, (place ^ step) * quarter, 0)
        return whole

    def put_feats(pieces):
        whole = jnp.zeros((pieces[0].shape[0], half), pieces[0].dtype)
        for step, piece in enumerate(pieces):
            whole = lax.dynamic_update_slice_in_dim(whole, piece, (place ^ step) * feat, 1)
        return whole

    def spread(a):
        return [a] + [plane_swap(a, step) for step in range(1, places)]

    def to_parts(a):
        return put_feats(
            [token_part(a, 0)] + [plane_swap(token_part(a, s), s) for s in range(1, places)]
        )

    def to_home(a):
        return put_rows([feat_part(a, 0)] + [plane_swap(feat_part(a, s), s) for s in range(1, places)])

    def sum_cols(a):
        step = 1
        while step < cols:
            a = a + lax.ppermute(a, "col", [(i, i ^ step) for i in range(cols)])
            step *= 2
        return a

    gain_one = first_gain.astype(F32)[:, None]
    gain_two = second_gain.astype(F32)[:, None]

    def scaled(w, gain):
        return own_first((w.astype(F32) * gain).astype(BF16))

    def exchange(w):
        part = w.shape[1] // rows
        whole = jnp.zeros((width, part), BF16)
        for s in range(rows):
            piece = lax.dynamic_slice_in_dim(w, (row + s) % rows * part, part, 1)
            piece = shift(piece, s) if s else piece
            whole = lax.dynamic_update_slice_in_dim(whole, piece, (row - s) % rows * 2 * feat, 0)
        if places != 4:
            return spread(whole)
        first, second = plane_swap(whole, 1), plane_swap(whole, 2)
        return [
            whole,
            first,
            second,
            jnp.concatenate([plane_swap(second[:half], 1), plane_swap(first[half:], 2)], axis=0),
        ]

    def give_back(pieces):
        if places != 4:
            total = pieces[0].astype(F32)
            for s in range(1, places):
                total = total + plane_swap(pieces[s], s).astype(F32)
        else:
            to_second = pieces[2].astype(F32) + jnp.concatenate(
                [plane_swap(pieces[3][:half], 1), jnp.zeros_like(pieces[3][half:])], axis=0
            ).astype(F32)
            to_first = pieces[1].astype(F32) + jnp.concatenate(
                [jnp.zeros_like(pieces[3][:half]), plane_swap(pieces[3][half:], 2)], axis=0
            ).astype(F32)
            total = (
                pieces[0].astype(F32)
                + plane_swap(to_first.astype(BF16), 1).astype(F32)
                + plane_swap(to_second.astype(BF16), 2).astype(F32)
            )
        total = total.astype(BF16)
        part = total.shape[1]
        whole = jnp.zeros((2 * feat, rows * part), F32)
        for s in range(rows):
            piece = lax.dynamic_slice_in_dim(total, (row + s) % rows * 2 * feat, 2 * feat, 0)
            piece = own_first(shift(piece, s) if s else piece).astype(F32)
            whole = lax.dynamic_update_slice_in_dim(whole, piece, (row - s) % rows * part, 1)
        return whole

    def give_rows(w):
        return own_first(lax.psum_scatter(w, "row", scatter_dimension=0, tiled=True)).astype(F32)

    def outer(own, other, right):
        return tn(weave(own, other, feat), right).astype(BF16)

    qkv = jnp.concatenate(
        [scaled(w, gain_one) for w in (query_weight, key_weight, value_weight)], axis=1
    )
    qkv_full = lax.all_gather(qkv, "row", axis=0, tiled=True)
    out_full = lax.all_gather(own_first(out_weight), "row", axis=0, tiled=True)
    gates = exchange(scaled(gate_weight, gain_two))
    ups = exchange(scaled(up_weight, gain_two))
    downs = exchange(own_first(down_weight))

    x_own = put_feats(spread(inputs))
    x_other = core_swap(x_own)
    heads_width = query_weight.shape[1]
    cosine, front, back = rope_tables(positions, heads_width)
    start_row = jnp.sum(
        (segment_ids[None, :] < segment_ids[:, None]).astype(jnp.int32), axis=1
    )[None, :]
    query, key, value, scale_one = project(feat, x_own, x_other, qkv_full, cosine, front, back)
    mixed, logs = attend(query, key, value, start_row)

    def scatter_parts(own, other):
        own = own + core_swap(other).astype(F32)
        low = own.astype(BF16)
        total = token_part(own, 0)
        for s in range(1, places):
            total = total + plane_swap(token_part(low, s), s).astype(F32)
        return total

    middle = token_part(x_own, 0).astype(F32) + scatter_parts(*unfold(feat, "mix", (mixed, [out_full])))
    square = jnp.sum(middle * middle, axis=1, keepdims=True)
    square = square + core_swap(square)
    scale_mid = lax.rsqrt(square / width + EPS)

    m_own = lax.all_gather(middle.astype(BF16), "row", axis=0, tiled=True)
    m_other = core_swap(m_own)
    g_part = to_parts(out_grad)
    g_own = lax.all_gather(g_part, "row", axis=0, tiled=True)
    g_other = core_swap(g_own)
    hidden, gate_low, up_low, gate_scaled, up_scaled = hidden_units(
        feat, (m_own, m_other, g_own, g_other), gates, ups, downs
    )

    def gather_sum(own, other):
        own = own + core_swap(other).astype(F32)
        return lax.psum_scatter(own.astype(BF16), "row", scatter_dimension=0, tiled=True).astype(F32)

    unit_grad = gather_sum(*unfold(feat, "unit_grad", (gate_low, gates), (up_low, ups)))
    feed = gather_sum(*unfold(feat, "feed", (hidden, downs)))
    block_out = to_home((middle + feed).astype(BF16))

    unit_mid = middle * scale_mid
    dot_two = jnp.sum(unit_grad * unit_mid, axis=1, keepdims=True)
    dot_two = dot_two + core_swap(dot_two)
    middle_grad = g_part.astype(F32) + scale_mid * (unit_grad - unit_mid * (dot_two / width))

    d_own = put_rows(spread(middle_grad.astype(BF16)))
    d_other = core_swap(d_own)
    d_all = weave(d_own, d_other, feat)
    mixed_grad = nn(d_all, out_full).astype(BF16)
    query_grad, key_grad, value_grad = attend_back(
        query, key, value, mixed, mixed_grad, start_row, logs, cosine, front, back
    )
    grads = jnp.concatenate([query_grad, key_grad, value_grad], axis=1)
    grads_scaled = (grads.astype(F32) * scale_one).astype(BF16)
    qkv_part = tn(weave(x_own, x_other, feat), grads_scaled)
    qkv_grad = give_rows(qkv_part.astype(BF16))
    gain_dots = jnp.sum(qkv_part * qkv_full.astype(F32), axis=1).reshape(rows, 2, feat)
    gain_dots = sum_cols(jnp.where(core == 0, gain_dots, gain_dots[:, ::-1]).reshape(width))
    gain_row = sum(
        shift(lax.dynamic_slice_in_dim(gain_dots, (row + s) % rows * 2 * feat, 2 * feat, 0), s)
        for s in range(1, rows)
    ) + lax.dynamic_slice_in_dim(gain_dots, row * 2 * feat, 2 * feat, 0)
    first_gain_grad = gain_row / gain_one[:, 0]
    first_unit_grad = scatter_parts(*unfold(feat, "first_grad", (grads, [qkv_full])))
    scale_first = token_part(scale_one, 0)
    unit_first = token_part(x_own, 0).astype(F32) * scale_first
    dot_one = jnp.sum(first_unit_grad * unit_first, axis=1, keepdims=True)
    dot_one = dot_one + core_swap(dot_one)
    input_grad = to_home(
        (middle_grad + scale_first * (first_unit_grad - unit_first * (dot_one / width))).astype(BF16)
    )

    out_weight_grad = give_rows(tn(d_all, mixed).astype(BF16))

    def by_place(w):
        part = w.shape[1] // places
        return [w[:, s * part : (s + 1) * part] for s in range(places)]

    down_weight_grad = give_back(by_place(outer(g_own, g_other, hidden)))
    gate_unit = give_back(by_place(outer(m_own, m_other, gate_scaled)))
    up_unit = give_back(by_place(outer(m_own, m_other, up_scaled)))
    q_unit = qkv_grad[:, :heads_width]
    k_unit = qkv_grad[:, heads_width : 2 * heads_width]
    v_unit = qkv_grad[:, 2 * heads_width :]

    def row_dots(*pairs):
        return sum(jnp.sum(w.astype(F32) * d, axis=1) for w, d in pairs)

    second_gain_grad = sum_cols(row_dots((gate_weight, gate_unit), (up_weight, up_unit)))
    return (
        block_out,
        input_grad,
        q_unit * gain_one,
        k_unit * gain_one,
        v_unit * gain_one,
        out_weight_grad,
        gate_unit * gain_two,
        up_unit * gain_two,
        down_weight_grad,
        first_gain_grad,
        second_gain_grad,
    )


def solution(mesh):
    grid, line = P("row", "col"), P("row")
    return jax.shard_map(
        local,
        mesh=mesh,
        in_specs=(grid,) * 8 + (line,) * 4 + (grid,),
        out_specs=(grid,) * 9 + (line,) * 2,
        check_vma=False,
    )
```

time: 1190 us -> 808 us (0.68)
  waiting for transfers between devices: 820 us -> 329 us
  matrix products: 173 us -> 30.6 us
  starting transfers between devices: 1.64 us -> 141 us
  Pallas kernels: 0 us -> 87.3 us
  blocking collectives: 75.4 us -> 0 us
  local copies, waits for them, and re-layouts: 35.6 us -> 103 us
  other arithmetic: 54.9 us -> 88.9 us
    reduce_scatter x11 -> x4, waiting for transfers between devices: 419 us -> 31.8 us  [the longest x2 31.8 us: gather_sum(): lax.psum_scatter(own.astype(BF16), 'row', scatter_dimension=0, tiled=True)]
    all_gather x11 -> x4, waiting for transfers between devices: 395 us -> 31.9 us  [the longest x1 21.6 us: local(): qkv_full = lax.all_gather(qkv, 'row', axis=0, tiled=True)]
    ppermute x0 -> x83, waiting for transfers between devices: none -> 266 us  [the longest x45 207 us: plane_swap(): return lax.ppermute(a, 'col', [(i, i ^ 2 * step) for i in range(cols)])]
    dot_general x35 -> x6, matrix products: 173 us -> 30.6 us  [the longest x5 28.5 us: tn(): lax.dot_general(left, right, (((0,), (0,)), ((), ())), preferred_element_...]
    ppermute x0 -> x83, starting transfers between devices: none -> 141 us  [the longest x21 75.7 us: shift(): return lax.ppermute(a, 'row', [(i, (i + step) % rows) for i in range(rows)])]
    pallas_call x0 -> x8, Pallas kernels: none -> 87.3 us  [the longest x4 36.5 us: unfold(): pl.pallas_call(functools.partial(unfold_kernel, feat, tuple((len(ws) for...]
    psum x2 -> x0, blocking collectives: 38.3 us -> none  [the longest x1 25.2 us: local(): token_one, gain_one_grad = lax.psum((token_one_part, gain_one_part), 'col')]
    unnamed x69 -> x152, local copies, waits for them, and re-layouts: 8.18 us -> 44.4 us
  transfers between devices with their start and end apart: 22 -> 91, of which waited for: 19 -> 37; matrix products, arithmetic and copies ran while one was open for 18% -> 25% of each run, Pallas kernels for 0% -> 6%
where the time goes in v1:
time: 808 us; the launch traced here: 797 us
  waiting for transfers between devices  329 us (41%)
  starting transfers between devices  141 us (17%)
  local copies, waits for them, and re-layouts  103 us (13%)
  other arithmetic  88.9 us (11%)
  Pallas kernels  87.3 us (11%)
  matrix products  30.6 us (4%)
  between operations  15.8 us (2%)
    ppermute x45, waiting for transfers between devices, plane_swap(): return lax.ppermute(a, 'col', [(i, i ^ 2 * step) for i in range(cols)])  207 us
    ppermute x21, starting transfers between devices, shift(): return lax.ppermute(a, 'row', [(i, (i + step) % rows) for i in range(rows)])  75.7 us
    ppermute x45, starting transfers between devices, plane_swap(): return lax.ppermute(a, 'col', [(i, i ^ 2 * step) for i in range(cols)])  58.6 us
    ppermute x21, waiting for transfers between devices, shift(): return lax.ppermute(a, 'row', [(i, (i + step) % rows) for i in range(rows)])  57.4 us
    unnamed x152, local copies, waits for them, and re-layouts  44.4 us
    pallas_call x4, Pallas kernels, unfold(): pl.pallas_call(functools.partial(unfold_kernel, feat, tuple((len(ws) for...  36.5 us
    reduce_scatter x2, waiting for transfers between devices, gather_sum(): lax.psum_scatter(own.astype(BF16), 'row', scatter_dimension=0, tiled=True)  31.8 us
    dot_general x5, matrix products, tn(): lax.dot_general(left, right, (((0,), (0,)), ((), ())), preferred_element_...  28.5 us
  transfers between devices with their start and end apart: 91, of which 37 were waited for; matrix products, arithmetic and copies ran while one was open for 25% of the time, Pallas kernels for 6%

profile of v1, /device:TPU:0, one launch (start us, length us, event | category | flops | bytes accessed | tf_op | source)
XLA Modules:
  0.0 796.5 jit_solution(7304504399720044611)
XLA Ops:
  10.4 3.0 collective-permute-start
  15.3 10.9 %collective-permute-done = bf16[1024,256]{1,0:T(8,128)(2,1)S(1)} collective-permute-done((bf16[1024,256]{1,0:T(8,128)(2,1)S(1)}, bf16[1024,256]{1,0:T(8,128)(2,1)S(1)}, u32[]{:S(2)}, u32[]{:S(2)}) %collective-permute-start) | collective-permute-done | bytes 524320 | tf_op jit(solution)/shard_map/ppermute | solution.py:341
  26.2 11.9 %collective-permute-done.1 = bf16[1024,256]{1,0:T(8,128)(2,1)} collective-permute-done((bf16[1024,256]{1,0:T(8,128)(2,1)S(1)}, bf16[1024,256]{1,0:T(8,128)(2,1)}, u32[]{:S(2)}, u32[]{:S(2)}) %collective-permute-start.1) | collective-permute-done | bytes 524320 | tf_op jit(solution)/shard_map/ppermute | solution.py:341
  45.2 2.6 copy.35.front_ref
  48.9 2.5 copy.36.back_ref
  52.5 2.5 copy.34.cos_ref
  55.1 21.6 %all-gather.5.cloned.1.call-done.weight_ref.refs_1_ = bf16[2048,768]{1,0:T(8,128)(2,1)} async-done(((bf16[512,768]{1,0:T(8,128)(2,1)}), bf16[2048,768]{1,0:T(8,128)(2,1)}) %all-gather.5.cloned.1.call-update) | async-done | bytes 3145744 | tf_op jit(solution)/shard_map/all_gather | solution.py:445
  76.7 8.5 %project.1 = (bf16[1024,256]{1,0:T(8,128)(2,1)}, bf16[1024,256]{1,0:T(8,128)(2,1)}, bf16[1024,256]{1,0:T(8,128)(2,1)}, f32[1024,1]{1,0:T(8,128)}) custom-call(bf16[1024,1024]{1,0:T(8,128)(2,1)} %copy-done, bf16[1024,1024]{1,0:T(8,128)(2,1)} %collective-permute-done.3.other_ref, bf16[2048,768]{1,0:T(8,128)(2,1)} %all-gather.5.cloned.1.call-done.weight_ref.refs_1_, ...), custom_call_target="tpu_custom_call" | custom-call | tf_op jit(solution)/shard_map/project/pallas_call | solution.py:83
  85.1 10.0 %attend.1 = (bf16[1024,256]{1,0:T(8,128)(2,1)}, f32[2,2,1024]{2,1,0:T(2,128)}) custom-call(bf16[1024,256]{1,0:T(8,128)(2,1)} %get-tuple-element.33.q_ref, bf16[1024,256]{1,0:T(8,128)(2,1)} %get-tuple-element.34.k_ref, bf16[1024,256]{1,0:T(8,128)(2,1)} %get-tuple-element.35.v_ref, s32[1,1024]{1,0:T(1,128)} %bitcast.27), custom_call_target="tpu_custom_call" | custom-call | tf_op jit(solution)/shard_map/attend/pallas_call | solution.py:210
  95.2 10.3 %all-gather.7.cloned.1.call-done.refs_1_ = bf16[2048,256]{1,0:T(8,128)(2,1)} async-done(((bf16[512,256]{1,0:T(8,128)(2,1)}), bf16[2048,256]{1,0:T(8,128)(2,1)}) %all-gather.7.cloned.1.call-update) | async-done | bytes 1048592 | tf_op jit(solution)/shard_map/all_gather | solution.py:446
  105.4 5.4 mix.1
  113.8 5.8 collective-permute-done.10
  121.8 6.0 fusion.35
  132.5 3.1 fusion.2
  135.6 8.5 %collective-permute-done.5 = bf16[256,1024]{1,0:T(8,128)(2,1)} collective-permute-done((bf16[256,1024]{1,0:T(8,128)(2,1)}, bf16[256,1024]{1,0:T(8,128)(2,1)}, u32[]{:S(2)}, u32[]{:S(2)}) %collective-permute-start.5) | collective-permute-done | bytes 524320 | tf_op jit(solution)/shard_map/ppermute | solution.py:341
  144.1 11.2 %collective-permute-done.6 = bf16[256,1024]{1,0:T(8,128)(2,1)} collective-permute-done((bf16[256,1024]{1,0:T(8,128)(2,1)}, bf16[256,1024]{1,0:T(8,128)(2,1)}, u32[]{:S(2)}, u32[]{:S(2)}) %collective-permute-start.6) | collective-permute-done | bytes 524320 | tf_op jit(solution)/shard_map/ppermute | solution.py:341
  163.2 2.5 collective-permute-start.22
  174.7 8.9 %collective-permute-done.21 = bf16[512,256]{1,0:T(8,128)(2,1)} collective-permute-done((bf16[512,256]{1,0:T(8,128)(2,1)}, bf16[512,256]{1,0:T(8,128)(2,1)}, u32[]{:S(2)}, u32[]{:S(2)}) %collective-permute-start.21) | collective-permute-done | bytes 262176 | tf_op jit(solution)/shard_map/ppermute | solution.py:355
  190.7 27.7 %collective-permute-start.27 = (bf16[512,256]{1,0:T(8,128)(2,1)S(1)}, bf16[512,256]{1,0:T(8,128)(2,1)S(1)}, u32[]{:S(2)}, u32[]{:S(2)}) collective-permute-start(bf16[512,256]{1,0:T(8,128)(2,1)S(1)} %get-tuple-element.109), channel_id=1, source_target_pairs={{0,8},{8,16},{16,24},{24,0},{1,9},{9,17},{17,25},{25,1},{2,10},{10... | collective-permute-start | bytes 786440 | tf_op jit(solution)/shard_map/ppermute | solution.py:355
  218.4 4.7 collective-permute-start.28
  224.8 18.4 %collective-permute-done.14 = bf16[512,256]{1,0:T(8,128)(2,1)S(1)} collective-permute-done((bf16[512,256]{1,0:T(8,128)(2,1)}, bf16[512,256]{1,0:T(8,128)(2,1)S(1)}, u32[]{:S(2)}, u32[]{:S(2)}) %collective-permute-start.14) | collective-permute-done | bytes 262176 | tf_op jit(solution)/shard_map/ppermute | solution.py:355
  250.0 11.6 %collective-permute-done.28 = bf16[512,256]{1,0:T(8,128)(2,1)S(1)} collective-permute-done((bf16[512,256]{1,0:T(8,128)(2,1)S(1)}, bf16[512,256]{1,0:T(8,128)(2,1)S(1)}, u32[]{:S(2)}, u32[]{:S(2)}) %collective-permute-start.28) | collective-permute-done | bytes 262176 | tf_op jit(solution)/shard_map/ppermute | solution.py:355
  266.4 5.0 collective-permute-done.23.refs_9_.refs_7_
  271.4 3.2 collective-permute-done.17.refs_6_.refs_4_
  278.3 15.6 %collective-permute-done.16.refs_5_.refs_3_ = bf16[2048,256]{1,0:T(8,128)(2,1)} collective-permute-done((bf16[2048,256]{1,0:T(8,128)(2,1)}, bf16[2048,256]{1,0:T(8,128)(2,1)}, u32[]{:S(2)}, u32[]{:S(2)}) %collective-permute-start.16) | collective-permute-done | bytes 1048608 | tf_op jit(solution)/shard_map/ppermute | solution.py:341
  297.8 18.6 %collective-permute-done.30.refs_13_.refs_2_ = bf16[2048,256]{1,0:T(8,128)(2,1)} collective-permute-done((bf16[2048,256]{1,0:T(8,128)(2,1)}, bf16[2048,256]{1,0:T(8,128)(2,1)}, u32[]{:S(2)}, u32[]{:S(2)}) %collective-permute-start.30) | collective-permute-done | bytes 1048608 | tf_op jit(solution)/shard_map/ppermute | solution.py:341
  320.1 7.5 collective-permute-done.25
  327.6 2.4 collective-permute-start.26
  330.0 8.8 %collective-permute-done.18 = bf16[1024,256]{1,0:T(8,128)(2,1)} collective-permute-done((bf16[1024,256]{1,0:T(8,128)(2,1)}, bf16[1024,256]{1,0:T(8,128)(2,1)}, u32[]{:S(2)}, u32[]{:S(2)}) %collective-permute-start.18) | collective-permute-done | bytes 524320 | tf_op jit(solution)/shard_map/ppermute | solution.py:341
  343.3 3.1 collective-permute-done.32
  346.3 2.5 collective-permute-start.33
  352.2 7.5 collective-permute-done.33
  363.0 21.3 %hidden_units.1 = (bf16[1024,1024]{1,0:T(8,128)(2,1)}, bf16[1024,1024]{1,0:T(8,128)(2,1)}, bf16[1024,1024]{1,0:T(8,128)(2,1)}, bf16[1024,1024]{1,0:T(8,128)(2,1)}, bf16[1024,1024]{1,0:T(8,128)(2,1)}) custom-call(bf16[1024,1024]{1,0:T(8,128)(2,1)} %all-gather.9.cloned.1.call-done.refs_0_, bf16[1024,1024]{1,0:T(8,128)(2,1)} %collective-permute-done.8.refs_1_, ...), custom_call_target="tpu_custom_call" | custom-call | tf_op jit(solution)/shard_map/hidden_units/pallas_call | solution.py:160
  384.3 14.5 %unit_grad.1 = (f32[1024,1024]{1,0:T(8,128)}, bf16[1024,1024]{1,0:T(8,128)(2,1)}) custom-call(bf16[1024,1024]{1,0:T(8,128)(2,1)} %get-tuple-element.42.refs_0_, bf16[1024,1024]{1,0:T(8,128)(2,1)} %get-tuple-element.43.refs_1_, bf16[2048,256]{1,0:T(8,128)(2,1)} %constant_dynamic-update-slice_fusion.25.refs_4_.refs_2_, ...), custom_call_target="tpu_custom_call" | custom-call | tf_op jit(solution)/shard_map/unit_grad/pallas_call | solution.py:119
  417.0 5.0 add_convert_fusion
  437.4 6.6 convolution_convert_fusion.1
  444.1 31.8 %reduce-scatter.7.cloned.1.call-done = bf16[256,1024]{1,0:T(8,128)(2,1)} async-done(((bf16[1024,1024]{1,0:T(8,128)(2,1)}), bf16[256,1024]{1,0:T(8,128)(2,1)}) %reduce-scatter.7.cloned.1.call-update) | async-done | bytes 524304 | tf_op jit(solution)/shard_map/reduce_scatter | solution.py:485
  486.9 4.9 convolution_convert_fusion.2
  491.8 15.6 %collective-permute-done.41 = bf16[256,1024]{1,0:T(8,128)(2,1)S(1)} collective-permute-done((bf16[256,1024]{1,0:T(8,128)(2,1)S(1)}, bf16[256,1024]{1,0:T(8,128)(2,1)S(1)}, u32[]{:S(2)}, u32[]{:S(2)}) %collective-permute-start.41) | collective-permute-done | bytes 524320 | tf_op jit(solution)/shard_map/ppermute | solution.py:341
  507.5 10.4 %collective-permute-done.43 = bf16[256,1024]{1,0:T(8,128)(2,1)S(1)} collective-permute-done((bf16[256,1024]{1,0:T(8,128)(2,1)S(1)}, bf16[256,1024]{1,0:T(8,128)(2,1)S(1)}, u32[]{:S(2)}, u32[]{:S(2)}) %collective-permute-start.43) | collective-permute-done | bytes 524320 | tf_op jit(solution)/shard_map/ppermute | solution.py:341
  522.1 6.2 convolution_convert_fusion
  528.3 8.8 %feed.1 = (f32[1024,1024]{1,0:T(8,128)}, bf16[1024,1024]{1,0:T(8,128)(2,1)}) custom-call(bf16[1024,1024]{1,0:T(8,128)(2,1)} %get-tuple-element.39.refs_0_, bf16[2048,256]{1,0:T(8,128)(2,1)} %constant_dynamic-update-slice_fusion.19.refs_12_.refs_1_, bf16[2048,256]{1,0:T(8,128)(2,1)} %collective-permute-done.30.refs_13_.refs_2_, ...), custom_call_target="tpu_custom_call" | custom-call | tf_op jit(solution)/shard_map/feed/pallas_call | solution.py:119
  540.6 3.3 add_convert_fusion.7
  556.5 3.5 add_convert_fusion.10
  561.4 3.0 add_convert_fusion.4
  564.4 15.4 %collective-permute-done.61 = bf16[2048,256]{1,0:T(8,128)(2,1)S(1)} collective-permute-done((bf16[2048,256]{1,0:T(8,128)(2,1)}, bf16[2048,256]{1,0:T(8,128)(2,1)S(1)}, u32[]{:S(2)}, u32[]{:S(2)}) %collective-permute-start.61) | collective-permute-done | bytes 1048608 | tf_op jit(solution)/shard_map/ppermute | solution.py:341
  586.4 3.8 add_convert_fusion.1
  590.2 12.1 %collective-permute-done.54 = bf16[2048,256]{1,0:T(8,128)(2,1)} collective-permute-done((bf16[2048,256]{1,0:T(8,128)(2,1)}, bf16[2048,256]{1,0:T(8,128)(2,1)}, u32[]{:S(2)}, u32[]{:S(2)}) %collective-permute-start.54) | collective-permute-done | bytes 1048608 | tf_op jit(solution)/shard_map/ppermute | solution.py:341
  608.5 15.9 %collective-permute-done.68 = bf16[2048,256]{1,0:T(8,128)(2,1)} collective-permute-done((bf16[2048,256]{1,0:T(8,128)(2,1)}, bf16[2048,256]{1,0:T(8,128)(2,1)}, u32[]{:S(2)}, u32[]{:S(2)}) %collective-permute-start.68) | collective-permute-done | bytes 1048608 | tf_op jit(solution)/shard_map/ppermute | solution.py:341
  633.3 7.8 collective-permute-done.57
  641.1 22.5 %collective-permute-start.71 = (bf16[512,256]{1,0:T(8,128)(2,1)}, bf16[512,256]{1,0:T(8,128)(2,1)}, u32[]{:S(2)}, u32[]{:S(2)}) collective-permute-start(bf16[512,256]{1,0:T(8,128)(2,1)} %get-tuple-element.92), channel_id=1, source_target_pairs={{0,8},{8,16},{16,24},{24,0},{1,9},{9,17},{17,25},{25,1},{2,10},{10... | collective-permute-start | bytes 786440 | tf_op jit(solution)/shard_map/ppermute | solution.py:355
  672.3 2.5 collective-permute-start.73
  677.6 11.0 %attend_back.1 = (bf16[1024,256]{1,0:T(8,128)(2,1)}, bf16[1024,256]{1,0:T(8,128)(2,1)}, bf16[1024,256]{1,0:T(8,128)(2,1)}) custom-call(bf16[1024,256]{1,0:T(8,128)(2,1)} %get-tuple-element.33.q_ref, bf16[1024,256]{1,0:T(8,128)(2,1)} %get-tuple-element.34.k_ref, bf16[1024,256]{1,0:T(8,128)(2,1)} %get-tuple-element.35.v_ref, ...), custom_call_target="tpu_custom_call" | custom-call | tf_op jit(solution)/shard_map/attend_back/pallas_call | solution.py:279
  692.0 8.4 %multiply_reduce_fusion = (f32[2048]{0:T(1024)S(1)}, bf16[2048,768]{1,0:T(8,128)(2,1)}) fusion(bf16[2048,768]{1,0:T(8,128)(2,1)S(1)} %copy-done.2, bf16[1024,2048]{1,0:T(8,128)(2,1)} %slice_dynamic-update-slice_fusion.16, bf16[1024,768]{1,0:T(8,128)(2,1)S(1)} %constant_dynamic-update-slice_fusion.6.refs_0_, f32[1024]{0:T(1024)S(1)} %reduce.1), kind=kOutput, calls=%fused_computation | convolution fusion | flops 3229874176 | bytes 12070912 | tf_op jit(solution)/shard_map/dot_general | solution.py:31
  706.9 7.7 first_grad.1
  716.3 3.3 fusion.3
  719.6 3.2 fusion.1
  737.4 2.7 fusion.33
  745.0 4.5 collective-permute-done.77
  750.2 3.7 collective-permute-done.79
  755.2 9.8 %collective-permute-done.47 = bf16[256,1024]{1,0:T(8,128)(2,1)S(1)} collective-permute-done((bf16[256,1024]{1,0:T(8,128)(2,1)S(1)}, bf16[256,1024]{1,0:T(8,128)(2,1)S(1)}, u32[]{:S(2)}, u32[]{:S(2)}) %collective-permute-start.47) | collective-permute-done | bytes 524320 | tf_op jit(solution)/shard_map/ppermute | solution.py:341
  767.2 2.9 fusion.12
  778.3 3.4 collective-permute-done.51
  783.2 3.3 collective-permute-done.36
  (442 shorter events, 230.3 us)
Async XLA Ops:
  7.2 69.5 %all-gather.5.cloned.1.call-start = ((), (), s32[]{:S(2)}) async-start(), calls=%async_computation.4 | async-start | bytes 3932160 | tf_op jit(solution)/shard_map/all_gather | solution.py:445
  10.3 95.1 %all-gather.7.cloned.1.call-start = ((), (), s32[]{:S(2)}) async-start(), calls=%async_computation.5 | async-start | bytes 1310720 | tf_op jit(solution)/shard_map/all_gather | solution.py:446
  10.4 15.8 %collective-permute-start = (bf16[1024,256]{1,0:T(8,128)(2,1)S(1)}, bf16[1024,256]{1,0:T(8,128)(2,1)S(1)}, u32[]{:S(2)}, u32[]{:S(2)}) collective-permute-start(bf16[1024,256]{1,0:T(8,128)(2,1)S(1)} %copy-done.39), channel_id=1, source_target_pairs={{0,2},{1,3},{2,0},{3,1},{4,6},{5,7},{6,4},{7,5},{8,10},{9,11},{10,... | collective-permute-start | bytes 1572872 | tf_op jit(solution)/shard_map/ppermute | solution.py:341
  13.4 24.7 %collective-permute-start.1 = (bf16[1024,256]{1,0:T(8,128)(2,1)S(1)}, bf16[1024,256]{1,0:T(8,128)(2,1)}, u32[]{:S(2)}, u32[]{:S(2)}) collective-permute-start(bf16[1024,256]{1,0:T(8,128)(2,1)S(1)} %copy-done.39), channel_id=1, source_target_pairs={{0,4},{1,5},{2,6},{3,7},{4,0},{5,1},{6,2},{7,3},{8,12},{9,13},{10,... | collective-permute-start | bytes 1572872 | tf_op jit(solution)/shard_map/ppermute | solution.py:341
  14.9 24.3 %collective-permute-start.2 = (bf16[1024,256]{1,0:T(8,128)(2,1)S(1)}, bf16[1024,256]{1,0:T(8,128)(2,1)}, u32[]{:S(2)}, u32[]{:S(2)}) collective-permute-start(bf16[1024,256]{1,0:T(8,128)(2,1)S(1)} %copy-done.39), channel_id=1, source_target_pairs={{0,6},{1,7},{2,4},{3,5},{4,2},{5,3},{6,0},{7,1},{8,14},{9,15},{10,... | collective-permute-start | bytes 1572872 | tf_op jit(solution)/shard_map/ppermute | solution.py:341
  41.4 230.0 %all-gather.11.cloned.1.call-start = ((), (), s32[]{:S(2)}) async-start(), calls=%async_computation.7 | async-start | bytes 2621440 | tf_op jit(solution)/shard_map/all_gather | solution.py:477
  42.2 71.5 %collective-permute-start.9 = (bf16[256,256]{1,0:T(8,128)(2,1)}, bf16[256,256]{1,0:T(8,128)(2,1)S(1)}, u32[]{:S(2)}, u32[]{:S(2)}) collective-permute-start(bf16[256,256]{1,0:T(8,128)(2,1)} %get-tuple-element.136), channel_id=1, source_target_pairs={{0,2},{1,3},{2,0},{3,1},{4,6},{5,7},{6,4},{7,5},{8,10},{9,11},{10,... | collective-permute-start | bytes 393224 | tf_op jit(solution)/shard_map/ppermute | solution.py:341
  120.4 154.2 %all-gather.9.cloned.1.call-start = ((), (), s32[]{:S(2)}) async-start(), calls=%async_computation.6 | async-start | bytes 2621440 | tf_op jit(solution)/shard_map/all_gather | solution.py:474
  130.5 24.8 %collective-permute-start.6 = (bf16[256,1024]{1,0:T(8,128)(2,1)}, bf16[256,1024]{1,0:T(8,128)(2,1)}, u32[]{:S(2)}, u32[]{:S(2)}) collective-permute-start(bf16[256,1024]{1,0:T(8,128)(2,1)} %get-tuple-element.86), channel_id=1, source_target_pairs={{0,4},{1,5},{2,6},{3,7},{4,0},{5,1},{6,2},{7,3},{8,12},{9,13},{10,... | collective-permute-start | bytes 1572872 | tf_op jit(solution)/shard_map/ppermute | solution.py:341
  132.0 23.4 %collective-permute-start.7 = (bf16[256,1024]{1,0:T(8,128)(2,1)}, bf16[256,1024]{1,0:T(8,128)(2,1)}, u32[]{:S(2)}, u32[]{:S(2)}) collective-permute-start(bf16[256,1024]{1,0:T(8,128)(2,1)} %get-tuple-element.85), channel_id=1, source_target_pairs={{0,6},{1,7},{2,4},{3,5},{4,2},{5,3},{6,0},{7,1},{8,14},{9,15},{10,... | collective-permute-start | bytes 1572872 | tf_op jit(solution)/shard_map/ppermute | solution.py:341
  158.3 317.5 %reduce-scatter.7.cloned.1.call-start = ((), (), s32[]{:S(2)}) async-start(), calls=%async_computation.9 | async-start | bytes 2621440 | tf_op jit(solution)/shard_map/reduce_scatter | solution.py:485
  162.2 21.5 %collective-permute-start.21 = (bf16[512,256]{1,0:T(8,128)(2,1)}, bf16[512,256]{1,0:T(8,128)(2,1)}, u32[]{:S(2)}, u32[]{:S(2)}) collective-permute-start(bf16[512,256]{1,0:T(8,128)(2,1)} %get-tuple-element.116), channel_id=1, source_target_pairs={{0,16},{8,24},{16,0},{24,8},{1,17},{9,25},{17,1},{25,9},{2,18},{10... | collective-permute-start | bytes 786440 | tf_op jit(solution)/shard_map/ppermute | solution.py:355
  163.2 22.1 %collective-permute-start.22 = (bf16[512,256]{1,0:T(8,128)(2,1)}, bf16[512,256]{1,0:T(8,128)(2,1)}, u32[]{:S(2)}, u32[]{:S(2)}) collective-permute-start(bf16[512,256]{1,0:T(8,128)(2,1)} %get-tuple-element.113), channel_id=1, source_target_pairs={{0,24},{8,0},{16,8},{24,16},{1,25},{9,1},{17,9},{25,17},{2,26},{10... | collective-permute-start | bytes 786440 | tf_op jit(solution)/shard_map/ppermute | solution.py:355
  167.9 50.6 %collective-permute-start.13 = (bf16[512,256]{1,0:T(8,128)(2,1)}, bf16[512,256]{1,0:T(8,128)(2,1)}, u32[]{:S(2)}, u32[]{:S(2)}) collective-permute-start(bf16[512,256]{1,0:T(8,128)(2,1)} %get-tuple-element.121), channel_id=1, source_target_pairs={{0,8},{8,16},{16,24},{24,0},{1,9},{9,17},{17,25},{25,1},{2,10},{10... | collective-permute-start | bytes 786440 | tf_op jit(solution)/shard_map/ppermute | solution.py:355
  167.9 75.3 %collective-permute-start.14 = (bf16[512,256]{1,0:T(8,128)(2,1)}, bf16[512,256]{1,0:T(8,128)(2,1)S(1)}, u32[]{:S(2)}, u32[]{:S(2)}) collective-permute-start(bf16[512,256]{1,0:T(8,128)(2,1)} %get-tuple-element.122), channel_id=1, source_target_pairs={{0,16},{8,24},{16,0},{24,8},{1,17},{9,25},{17,1},{25,9},{2,18},{10... | collective-permute-start | bytes 786440 | tf_op jit(solution)/shard_map/ppermute | solution.py:355
  172.6 73.1 %collective-permute-start.15 = (bf16[512,256]{1,0:T(8,128)(2,1)}, bf16[512,256]{1,0:T(8,128)(2,1)S(1)}, u32[]{:S(2)}, u32[]{:S(2)}) collective-permute-start(bf16[512,256]{1,0:T(8,128)(2,1)} %get-tuple-element.119), channel_id=1, source_target_pairs={{0,24},{8,0},{16,8},{24,16},{1,25},{9,1},{17,9},{25,17},{2,26},{10... | collective-permute-start | bytes 786440 | tf_op jit(solution)/shard_map/ppermute | solution.py:355
  187.0 78.7 %collective-permute-start.24 = (bf16[2048,256]{1,0:T(8,128)(2,1)}, bf16[2048,256]{1,0:T(8,128)(2,1)}, u32[]{:S(2)}, u32[]{:S(2)}) collective-permute-start(bf16[2048,256]{1,0:T(8,128)(2,1)} %constant_dynamic-update-slice_fusion.22.refs_8_.refs_6_), channel_id=1, source_target_pairs={{0,4},{1,5},{2,6},{3,7},{4,0},{5,1},{6,2},{7,3},{8,12},{9,13},{10,... | collective-permute-start | bytes 3145736 | tf_op jit(solution)/shard_map/ppermute | solution.py:341
  190.7 57.5 %collective-permute-start.27 = (bf16[512,256]{1,0:T(8,128)(2,1)S(1)}, bf16[512,256]{1,0:T(8,128)(2,1)S(1)}, u32[]{:S(2)}, u32[]{:S(2)}) collective-permute-start(bf16[512,256]{1,0:T(8,128)(2,1)S(1)} %get-tuple-element.109), channel_id=1, source_target_pairs={{0,8},{8,16},{16,24},{24,0},{1,9},{9,17},{17,25},{25,1},{2,10},{10... | collective-permute-start | bytes 786440 | tf_op jit(solution)/shard_map/ppermute | solution.py:355
  218.4 43.1 %collective-permute-start.28 = (bf16[512,256]{1,0:T(8,128)(2,1)S(1)}, bf16[512,256]{1,0:T(8,128)(2,1)S(1)}, u32[]{:S(2)}, u32[]{:S(2)}) collective-permute-start(bf16[512,256]{1,0:T(8,128)(2,1)S(1)} %get-tuple-element.110), channel_id=1, source_target_pairs={{0,16},{8,24},{16,0},{24,8},{1,17},{9,25},{17,1},{25,9},{2,18},{10... | collective-permute-start | bytes 786440 | tf_op jit(solution)/shard_map/ppermute | solution.py:355
  243.2 20.4 %collective-permute-start.29 = (bf16[512,256]{1,0:T(8,128)(2,1)S(1)}, bf16[512,256]{1,0:T(8,128)(2,1)S(1)}, u32[]{:S(2)}, u32[]{:S(2)}) collective-permute-start(bf16[512,256]{1,0:T(8,128)(2,1)S(1)} %get-tuple-element.107), channel_id=1, source_target_pairs={{0,24},{8,0},{16,8},{24,16},{1,25},{9,1},{17,9},{25,17},{2,26},{10... | collective-permute-start | bytes 786440 | tf_op jit(solution)/shard_map/ppermute | solution.py:355
  245.7 25.7 %collective-permute-start.23 = (bf16[2048,256]{1,0:T(8,128)(2,1)S(1)}, bf16[2048,256]{1,0:T(8,128)(2,1)}, u32[]{:S(2)}, u32[]{:S(2)}) collective-permute-start(bf16[2048,256]{1,0:T(8,128)(2,1)S(1)} %copy-done.5), channel_id=1, source_target_pairs={{0,2},{1,3},{2,0},{3,1},{4,6},{5,7},{6,4},{7,5},{8,10},{9,11},{10,... | collective-permute-start | bytes 3145736 | tf_op jit(solution)/shard_map/ppermute | solution.py:341
  248.2 26.4 %collective-permute-start.17 = (bf16[2048,256]{1,0:T(8,128)(2,1)}, bf16[2048,256]{1,0:T(8,128)(2,1)}, u32[]{:S(2)}, u32[]{:S(2)}) collective-permute-start(bf16[2048,256]{1,0:T(8,128)(2,1)} %constant_dynamic-update-slice_fusion.25.refs_4_.refs_2_), channel_id=1, source_target_pairs={{0,4},{1,5},{2,6},{3,7},{4,0},{5,1},{6,2},{7,3},{8,12},{9,13},{10,... | collective-permute-start | bytes 3145736 | tf_op jit(solution)/shard_map/ppermute | solution.py:341
  261.5 32.4 %collective-permute-start.16 = (bf16[2048,256]{1,0:T(8,128)(2,1)}, bf16[2048,256]{1,0:T(8,128)(2,1)}, u32[]{:S(2)}, u32[]{:S(2)}) collective-permute-start(bf16[2048,256]{1,0:T(8,128)(2,1)} %constant_dynamic-update-slice_fusion.25.refs_4_.refs_2_), channel_id=1, source_target_pairs={{0,2},{1,3},{2,0},{3,1},{4,6},{5,7},{6,4},{7,5},{8,10},{9,11},{10,... | collective-permute-start | bytes 3145736 | tf_op jit(solution)/shard_map/ppermute | solution.py:341
  264.3 31.2 %collective-permute-start.31 = (bf16[2048,256]{1,0:T(8,128)(2,1)}, bf16[2048,256]{1,0:T(8,128)(2,1)}, u32[]{:S(2)}, u32[]{:S(2)}) collective-permute-start(bf16[2048,256]{1,0:T(8,128)(2,1)} %constant_dynamic-update-slice_fusion.19.refs_12_.refs_1_), channel_id=1, source_target_pairs={{0,4},{1,5},{2,6},{3,7},{4,0},{5,1},{6,2},{7,3},{8,12},{9,13},{10,... | collective-permute-start | bytes 3145736 | tf_op jit(solution)/shard_map/ppermute | solution.py:341
  265.7 50.7 %collective-permute-start.30 = (bf16[2048,256]{1,0:T(8,128)(2,1)}, bf16[2048,256]{1,0:T(8,128)(2,1)}, u32[]{:S(2)}, u32[]{:S(2)}) collective-permute-start(bf16[2048,256]{1,0:T(8,128)(2,1)} %constant_dynamic-update-slice_fusion.19.refs_12_.refs_1_), channel_id=1, source_target_pairs={{0,2},{1,3},{2,0},{3,1},{4,6},{5,7},{6,4},{7,5},{8,10},{9,11},{10,... | collective-permute-start | bytes 3145736 | tf_op jit(solution)/shard_map/ppermute | solution.py:341
  271.4 91.5 %collective-permute-start.12 = (bf16[1024,1024]{1,0:T(8,128)(2,1)}, bf16[1024,1024]{1,0:T(8,128)(2,1)}, u32[]{:S(2)}, u32[]{:S(2)}) collective-permute-start(bf16[1024,1024]{1,0:T(8,128)(2,1)} %all-gather.11.cloned.1.call-done.refs_2_), channel_id=1, source_target_pairs={{0,1},{1,0},{2,3},{3,2},{4,5},{5,4},{6,7},{7,6},{8,9},{9,8},{10,11... | collective-permute-start | bytes 6291464 | tf_op jit(solution)/shard_map/ppermute | solution.py:338
  274.6 88.4 %collective-permute-start.8 = (bf16[1024,1024]{1,0:T(8,128)(2,1)}, bf16[1024,1024]{1,0:T(8,128)(2,1)}, u32[]{:S(2)}, u32[]{:S(2)}) collective-permute-start(bf16[1024,1024]{1,0:T(8,128)(2,1)} %all-gather.9.cloned.1.call-done.refs_0_), channel_id=1, source_target_pairs={{0,1},{1,0},{2,3},{3,2},{4,5},{5,4},{6,7},{7,6},{8,9},{9,8},{10,11... | collective-permute-start | bytes 6291464 | tf_op jit(solution)/shard_map/ppermute | solution.py:338
  293.9 33.7 %collective-permute-start.25 = (bf16[1024,256]{1,0:T(8,128)(2,1)}, bf16[1024,256]{1,0:T(8,128)(2,1)}, u32[]{:S(2)}, u32[]{:S(2)}) collective-permute-start(bf16[1024,256]{1,0:T(8,128)(2,1)} %slice.463), channel_id=1, source_target_pairs={{0,2},{1,3},{2,0},{3,1},{4,6},{5,7},{6,4},{7,5},{8,10},{9,11},{10,... | collective-permute-start | bytes 1572872 | tf_op jit(solution)/shard_map/ppermute | solution.py:341
  295.5 43.3 %collective-permute-start.18 = (bf16[1024,256]{1,0:T(8,128)(2,1)}, bf16[1024,256]{1,0:T(8,128)(2,1)}, u32[]{:S(2)}, u32[]{:S(2)}) collective-permute-start(bf16[1024,256]{1,0:T(8,128)(2,1)} %slice.459), channel_id=1, source_target_pairs={{0,2},{1,3},{2,0},{3,1},{4,6},{5,7},{6,4},{7,5},{8,10},{9,11},{10,... | collective-permute-start | bytes 1572872 | tf_op jit(solution)/shard_map/ppermute | solution.py:341
  316.3 30.0 %collective-permute-start.32 = (bf16[1024,256]{1,0:T(8,128)(2,1)}, bf16[1024,256]{1,0:T(8,128)(2,1)}, u32[]{:S(2)}, u32[]{:S(2)}) collective-permute-start(bf16[1024,256]{1,0:T(8,128)(2,1)} %slice.465), channel_id=1, source_target_pairs={{0,2},{1,3},{2,0},{3,1},{4,6},{5,7},{6,4},{7,5},{8,10},{9,11},{10,... | collective-permute-start | bytes 1572872 | tf_op jit(solution)/shard_map/ppermute | solution.py:341
  327.6 24.5 %collective-permute-start.26 = (bf16[1024,256]{1,0:T(8,128)(2,1)S(1)}, bf16[1024,256]{1,0:T(8,128)(2,1)S(1)}, u32[]{:S(2)}, u32[]{:S(2)}) collective-permute-start(bf16[1024,256]{1,0:T(8,128)(2,1)S(1)} %slice.464), channel_id=1, source_target_pairs={{0,4},{1,5},{2,6},{3,7},{4,0},{5,1},{6,2},{7,3},{8,12},{9,13},{10,... | collective-permute-start | bytes 1572872 | tf_op jit(solution)/shard_map/ppermute | solution.py:341
  398.9 18.1 %collective-permute-start.39 = (bf16[1024,1024]{1,0:T(8,128)(2,1)}, bf16[1024,1024]{1,0:T(8,128)(2,1)}, u32[]{:S(2)}, u32[]{:S(2)}) collective-permute-start(bf16[1024,1024]{1,0:T(8,128)(2,1)} %get-tuple-element.45), channel_id=1, source_target_pairs={{0,1},{1,0},{2,3},{3,2},{4,5},{5,4},{6,7},{7,6},{8,9},{9,8},{10,11... | collective-permute-start | bytes 6291464 | tf_op jit(solution)/shard_map/ppermute | solution.py:338
  422.0 344.0 %reduce-scatter.11.cloned.1.call-start = ((), (), s32[]{:S(2)}) async-start(), calls=%async_computation.11 | async-start | bytes 1310720 | tf_op jit(solution)/shard_map/reduce_scatter | solution.py:437
  479.7 59.7 %collective-permute-start.60 = (bf16[1024,256]{1,0:T(8,128)(2,1)}, bf16[1024,256]{1,0:T(8,128)(2,1)S(1)}, u32[]{:S(2)}, u32[]{:S(2)}) collective-permute-start(bf16[1024,256]{1,0:T(8,128)(2,1)} %get-tuple-element.71), channel_id=1, source_target_pairs={{0,4},{1,5},{2,6},{3,7},{4,0},{5,1},{6,2},{7,3},{8,12},{9,13},{10,... | collective-permute-start | bytes 1572872 | tf_op jit(solution)/shard_map/ppermute | solution.py:341
  481.2 58.8 %collective-permute-start.62 = (bf16[1024,256]{1,0:T(8,128)(2,1)}, bf16[1024,256]{1,0:T(8,128)(2,1)}, u32[]{:S(2)}, u32[]{:S(2)}) collective-permute-start(bf16[1024,256]{1,0:T(8,128)(2,1)} %get-tuple-element.72), channel_id=1, source_target_pairs={{0,2},{1,3},{2,0},{3,1},{4,6},{5,7},{6,4},{7,5},{8,10},{9,11},{10,... | collective-permute-start | bytes 1572872 | tf_op jit(solution)/shard_map/ppermute | solution.py:341
  483.3 24.1 %collective-permute-start.41 = (bf16[256,1024]{1,0:T(8,128)(2,1)S(1)}, bf16[256,1024]{1,0:T(8,128)(2,1)S(1)}, u32[]{:S(2)}, u32[]{:S(2)}) collective-permute-start(bf16[256,1024]{1,0:T(8,128)(2,1)S(1)} %get-tuple-element.58), channel_id=1, source_target_pairs={{0,2},{1,3},{2,0},{3,1},{4,6},{5,7},{6,4},{7,5},{8,10},{9,11},{10,... | collective-permute-start | bytes 1572872 | tf_op jit(solution)/shard_map/ppermute | solution.py:341
  483.9 23.5 %collective-permute-start.42 = (bf16[256,1024]{1,0:T(8,128)(2,1)S(1)}, bf16[256,1024]{1,0:T(8,128)(2,1)S(1)}, u32[]{:S(2)}, u32[]{:S(2)}) collective-permute-start(bf16[256,1024]{1,0:T(8,128)(2,1)S(1)} %get-tuple-element.58), channel_id=1, source_target_pairs={{0,4},{1,5},{2,6},{3,7},{4,0},{5,1},{6,2},{7,3},{8,12},{9,13},{10,... | collective-permute-start | bytes 1572872 | tf_op jit(solution)/shard_map/ppermute | solution.py:341
  484.5 33.4 %collective-permute-start.43 = (bf16[256,1024]{1,0:T(8,128)(2,1)S(1)}, bf16[256,1024]{1,0:T(8,128)(2,1)S(1)}, u32[]{:S(2)}, u32[]{:S(2)}) collective-permute-start(bf16[256,1024]{1,0:T(8,128)(2,1)S(1)} %get-tuple-element.58), channel_id=1, source_target_pairs={{0,6},{1,7},{2,4},{3,5},{4,2},{5,3},{6,0},{7,1},{8,14},{9,15},{10,... | collective-permute-start | bytes 1572872 | tf_op jit(solution)/shard_map/ppermute | solution.py:341
  517.9 26.0 %collective-permute-start.44 = (bf16[1024,1024]{1,0:T(8,128)(2,1)S(1)}, bf16[1024,1024]{1,0:T(8,128)(2,1)}, u32[]{:S(2)}, u32[]{:S(2)}) collective-permute-start(bf16[1024,1024]{1,0:T(8,128)(2,1)S(1)} %constant_dynamic-update-slice_fusion.12), channel_id=1, source_target_pairs={{0,1},{1,0},{2,3},{3,2},{4,5},{5,4},{6,7},{7,6},{8,9},{9,8},{10,11... | collective-permute-start | bytes 6291464 | tf_op jit(solution)/shard_map/ppermute | solution.py:338
  519.1 34.4 %collective-permute-start.53 = (bf16[1024,256]{1,0:T(8,128)(2,1)}, bf16[1024,256]{1,0:T(8,128)(2,1)}, u32[]{:S(2)}, u32[]{:S(2)}) collective-permute-start(bf16[1024,256]{1,0:T(8,128)(2,1)} %get-tuple-element.75), channel_id=1, source_target_pairs={{0,4},{1,5},{2,6},{3,7},{4,0},{5,1},{6,2},{7,3},{8,12},{9,13},{10,... | collective-permute-start | bytes 1572872 | tf_op jit(solution)/shard_map/ppermute | solution.py:341
  520.6 34.4 %collective-permute-start.55 = (bf16[1024,256]{1,0:T(8,128)(2,1)}, bf16[1024,256]{1,0:T(8,128)(2,1)}, u32[]{:S(2)}, u32[]{:S(2)}) collective-permute-start(bf16[1024,256]{1,0:T(8,128)(2,1)} %get-tuple-element.76), channel_id=1, source_target_pairs={{0,2},{1,3},{2,0},{3,1},{4,6},{5,7},{6,4},{7,5},{8,10},{9,11},{10,... | collective-permute-start | bytes 1572872 | tf_op jit(solution)/shard_map/ppermute | solution.py:341
  539.4 20.6 %collective-permute-start.67 = (bf16[1024,256]{1,0:T(8,128)(2,1)}, bf16[1024,256]{1,0:T(8,128)(2,1)}, u32[]{:S(2)}, u32[]{:S(2)}) collective-permute-start(bf16[1024,256]{1,0:T(8,128)(2,1)} %get-tuple-element.67), channel_id=1, source_target_pairs={{0,4},{1,5},{2,6},{3,7},{4,0},{5,1},{6,2},{7,3},{8,12},{9,13},{10,... | collective-permute-start | bytes 1572872 | tf_op jit(solution)/shard_map/ppermute | solution.py:341
  540.0 20.6 %collective-permute-start.69 = (bf16[1024,256]{1,0:T(8,128)(2,1)}, bf16[1024,256]{1,0:T(8,128)(2,1)}, u32[]{:S(2)}, u32[]{:S(2)}) collective-permute-start(bf16[1024,256]{1,0:T(8,128)(2,1)} %get-tuple-element.68), channel_id=1, source_target_pairs={{0,2},{1,3},{2,0},{3,1},{4,6},{5,7},{6,4},{7,5},{8,10},{9,11},{10,... | collective-permute-start | bytes 1572872 | tf_op jit(solution)/shard_map/ppermute | solution.py:341
  544.0 42.4 %collective-permute-start.34 = (bf16[1024,1024]{1,0:T(8,128)(2,1)}, bf16[1024,1024]{1,0:T(8,128)(2,1)}, u32[]{:S(2)}, u32[]{:S(2)}) collective-permute-start(bf16[1024,1024]{1,0:T(8,128)(2,1)} %get-tuple-element.41), channel_id=1, source_target_pairs={{0,1},{1,0},{2,3},{3,2},{4,5},{5,4},{6,7},{7,6},{8,9},{9,8},{10,11... | collective-permute-start | bytes 6291464 | tf_op jit(solution)/shard_map/ppermute | solution.py:338
  553.3 213.9 %reduce-scatter.5.cloned.1.call-start = ((), (), s32[]{:S(2)}) async-start(), calls=%async_computation.8 | async-start | bytes 2621440 | tf_op jit(solution)/shard_map/reduce_scatter | solution.py:485
  553.5 26.2 %collective-permute-start.61 = (bf16[2048,256]{1,0:T(8,128)(2,1)}, bf16[2048,256]{1,0:T(8,128)(2,1)S(1)}, u32[]{:S(2)}, u32[]{:S(2)}) collective-permute-start(bf16[2048,256]{1,0:T(8,128)(2,1)} %get-tuple-element.69), channel_id=1, source_target_pairs={{0,2},{1,3},{2,0},{3,1},{4,6},{5,7},{6,4},{7,5},{8,10},{9,11},{10,... | collective-permute-start | bytes 3145736 | tf_op jit(solution)/shard_map/ppermute | solution.py:341
  555.0 26.2 %collective-permute-start.63 = (bf16[2048,256]{1,0:T(8,128)(2,1)}, bf16[2048,256]{1,0:T(8,128)(2,1)S(1)}, u32[]{:S(2)}, u32[]{:S(2)}) collective-permute-start(bf16[2048,256]{1,0:T(8,128)(2,1)} %get-tuple-element.70), channel_id=1, source_target_pairs={{0,4},{1,5},{2,6},{3,7},{4,0},{5,1},{6,2},{7,3},{8,12},{9,13},{10,... | collective-permute-start | bytes 3145736 | tf_op jit(solution)/shard_map/ppermute | solution.py:341
  560.0 42.3 %collective-permute-start.54 = (bf16[2048,256]{1,0:T(8,128)(2,1)}, bf16[2048,256]{1,0:T(8,128)(2,1)}, u32[]{:S(2)}, u32[]{:S(2)}) collective-permute-start(bf16[2048,256]{1,0:T(8,128)(2,1)} %get-tuple-element.73), channel_id=1, source_target_pairs={{0,2},{1,3},{2,0},{3,1},{4,6},{5,7},{6,4},{7,5},{8,10},{9,11},{10,... | collective-permute-start | bytes 3145736 | tf_op jit(solution)/shard_map/ppermute | solution.py:341
  560.6 43.5 %collective-permute-start.56 = (bf16[2048,256]{1,0:T(8,128)(2,1)}, bf16[2048,256]{1,0:T(8,128)(2,1)}, u32[]{:S(2)}, u32[]{:S(2)}) collective-permute-start(bf16[2048,256]{1,0:T(8,128)(2,1)} %get-tuple-element.74), channel_id=1, source_target_pairs={{0,4},{1,5},{2,6},{3,7},{4,0},{5,1},{6,2},{7,3},{8,12},{9,13},{10,... | collective-permute-start | bytes 3145736 | tf_op jit(solution)/shard_map/ppermute | solution.py:341
  579.7 44.6 %collective-permute-start.68 = (bf16[2048,256]{1,0:T(8,128)(2,1)}, bf16[2048,256]{1,0:T(8,128)(2,1)}, u32[]{:S(2)}, u32[]{:S(2)}) collective-permute-start(bf16[2048,256]{1,0:T(8,128)(2,1)} %get-tuple-element.65), channel_id=1, source_target_pairs={{0,2},{1,3},{2,0},{3,1},{4,6},{5,7},{6,4},{7,5},{8,10},{9,11},{10,... | collective-permute-start | bytes 3145736 | tf_op jit(solution)/shard_map/ppermute | solution.py:341
  581.2 44.3 %collective-permute-start.70 = (bf16[2048,256]{1,0:T(8,128)(2,1)}, bf16[2048,256]{1,0:T(8,128)(2,1)}, u32[]{:S(2)}, u32[]{:S(2)}) collective-permute-start(bf16[2048,256]{1,0:T(8,128)(2,1)} %get-tuple-element.66), channel_id=1, source_target_pairs={{0,4},{1,5},{2,6},{3,7},{4,0},{5,1},{6,2},{7,3},{8,12},{9,13},{10,... | collective-permute-start | bytes 3145736 | tf_op jit(solution)/shard_map/ppermute | solution.py:341
  586.4 44.2 %collective-permute-start.64 = (bf16[512,256]{1,0:T(8,128)(2,1)}, bf16[512,256]{1,0:T(8,128)(2,1)S(1)}, u32[]{:S(2)}, u32[]{:S(2)}) collective-permute-start(bf16[512,256]{1,0:T(8,128)(2,1)} %get-tuple-element.97), channel_id=1, source_target_pairs={{0,8},{8,16},{16,24},{24,0},{1,9},{9,17},{17,25},{25,1},{2,10},{10... | collective-permute-start | bytes 786440 | tf_op jit(solution)/shard_map/ppermute | solution.py:355
  590.2 196.5 %reduce-scatter.9.cloned.1.call-start = ((), (), s32[]{:S(2)}) async-start(), calls=%async_computation.10 | async-start | bytes 3932160 | tf_op jit(solution)/shard_map/reduce_scatter | solution.py:437
  602.3 67.0 %collective-permute-start.65 = (bf16[512,256]{1,0:T(8,128)(2,1)}, bf16[512,256]{1,0:T(8,128)(2,1)S(1)}, u32[]{:S(2)}, u32[]{:S(2)}) collective-permute-start(bf16[512,256]{1,0:T(8,128)(2,1)} %get-tuple-element.96), channel_id=1, source_target_pairs={{0,16},{8,24},{16,0},{24,8},{1,17},{9,25},{17,1},{25,9},{2,18},{10... | collective-permute-start | bytes 786440 | tf_op jit(solution)/shard_map/ppermute | solution.py:355
  604.1 100.7 %collective-permute-start.66 = (bf16[512,256]{1,0:T(8,128)(2,1)}, bf16[512,256]{1,0:T(8,128)(2,1)}, u32[]{:S(2)}, u32[]{:S(2)}) collective-permute-start(bf16[512,256]{1,0:T(8,128)(2,1)} %get-tuple-element.95), channel_id=1, source_target_pairs={{0,24},{8,0},{16,8},{24,16},{1,25},{9,1},{17,9},{25,17},{2,26},{10... | collective-permute-start | bytes 786440 | tf_op jit(solution)/shard_map/ppermute | solution.py:355
  624.4 16.7 %collective-permute-start.57 = (bf16[512,256]{1,0:T(8,128)(2,1)S(1)}, bf16[512,256]{1,0:T(8,128)(2,1)S(1)}, u32[]{:S(2)}, u32[]{:S(2)}) collective-permute-start(bf16[512,256]{1,0:T(8,128)(2,1)S(1)} %get-tuple-element.102), channel_id=1, source_target_pairs={{0,8},{8,16},{16,24},{24,0},{1,9},{9,17},{17,25},{25,1},{2,10},{10... | collective-permute-start | bytes 786440 | tf_op jit(solution)/shard_map/ppermute | solution.py:355
  625.6 46.8 %collective-permute-start.58 = (bf16[512,256]{1,0:T(8,128)(2,1)S(1)}, bf16[512,256]{1,0:T(8,128)(2,1)S(1)}, u32[]{:S(2)}, u32[]{:S(2)}) collective-permute-start(bf16[512,256]{1,0:T(8,128)(2,1)S(1)} %get-tuple-element.101), channel_id=1, source_target_pairs={{0,16},{8,24},{16,0},{24,8},{1,17},{9,25},{17,1},{25,9},{2,18},{10... | collective-permute-start | bytes 786440 | tf_op jit(solution)/shard_map/ppermute | solution.py:355
  630.6 75.3 %collective-permute-start.59 = (bf16[512,256]{1,0:T(8,128)(2,1)}, bf16[512,256]{1,0:T(8,128)(2,1)}, u32[]{:S(2)}, u32[]{:S(2)}) collective-permute-start(bf16[512,256]{1,0:T(8,128)(2,1)} %get-tuple-element.100), channel_id=1, source_target_pairs={{0,24},{8,0},{16,8},{24,16},{1,25},{9,1},{17,9},{25,17},{2,26},{10... | collective-permute-start | bytes 786440 | tf_op jit(solution)/shard_map/ppermute | solution.py:355
  641.1 82.8 %collective-permute-start.71 = (bf16[512,256]{1,0:T(8,128)(2,1)}, bf16[512,256]{1,0:T(8,128)(2,1)}, u32[]{:S(2)}, u32[]{:S(2)}) collective-permute-start(bf16[512,256]{1,0:T(8,128)(2,1)} %get-tuple-element.92), channel_id=1, source_target_pairs={{0,8},{8,16},{16,24},{24,0},{1,9},{9,17},{17,25},{25,1},{2,10},{10... | collective-permute-start | bytes 786440 | tf_op jit(solution)/shard_map/ppermute | solution.py:355
  669.3 56.6 %collective-permute-start.72 = (bf16[512,256]{1,0:T(8,128)(2,1)}, bf16[512,256]{1,0:T(8,128)(2,1)}, u32[]{:S(2)}, u32[]{:S(2)}) collective-permute-start(bf16[512,256]{1,0:T(8,128)(2,1)} %get-tuple-element.91), channel_id=1, source_target_pairs={{0,16},{8,24},{16,0},{24,8},{1,17},{9,25},{17,1},{25,9},{2,18},{10... | collective-permute-start | bytes 786440 | tf_op jit(solution)/shard_map/ppermute | solution.py:355
  672.3 55.0 %collective-permute-start.73 = (bf16[512,256]{1,0:T(8,128)(2,1)}, bf16[512,256]{1,0:T(8,128)(2,1)}, u32[]{:S(2)}, u32[]{:S(2)}) collective-permute-start(bf16[512,256]{1,0:T(8,128)(2,1)} %get-tuple-element.90), channel_id=1, source_target_pairs={{0,24},{8,0},{16,8},{24,16},{1,25},{9,1},{17,9},{25,17},{2,26},{10... | collective-permute-start | bytes 786440 | tf_op jit(solution)/shard_map/ppermute | solution.py:355
  714.6 22.7 %collective-permute-start.45 = (bf16[1024,1024]{1,0:T(8,128)(2,1)}, bf16[1024,1024]{1,0:T(8,128)(2,1)}, u32[]{:S(2)}, u32[]{:S(2)}) collective-permute-start(bf16[1024,1024]{1,0:T(8,128)(2,1)} %get-tuple-element.52), channel_id=1, source_target_pairs={{0,1},{1,0},{2,3},{3,2},{4,5},{5,4},{6,7},{7,6},{8,9},{9,8},{10,11... | collective-permute-start | bytes 6291464 | tf_op jit(solution)/shard_map/ppermute | solution.py:338
  741.0 24.1 %collective-permute-start.47 = (bf16[256,1024]{1,0:T(8,128)(2,1)S(1)}, bf16[256,1024]{1,0:T(8,128)(2,1)S(1)}, u32[]{:S(2)}, u32[]{:S(2)}) collective-permute-start(bf16[256,1024]{1,0:T(8,128)(2,1)S(1)} %get-tuple-element.83), channel_id=1, source_target_pairs={{0,4},{1,5},{2,6},{3,7},{4,0},{5,1},{6,2},{7,3},{8,12},{9,13},{10,... | collective-permute-start | bytes 1572872 | tf_op jit(solution)/shard_map/ppermute | solution.py:341
  742.4 22.6 %collective-permute-start.48 = (bf16[256,1024]{1,0:T(8,128)(2,1)S(1)}, bf16[256,1024]{1,0:T(8,128)(2,1)S(1)}, u32[]{:S(2)}, u32[]{:S(2)}) collective-permute-start(bf16[256,1024]{1,0:T(8,128)(2,1)S(1)} %get-tuple-element.82), channel_id=1, source_target_pairs={{0,6},{1,7},{2,4},{3,5},{4,2},{5,3},{6,0},{7,1},{8,14},{9,15},{10,... | collective-permute-start | bytes 1572872 | tf_op jit(solution)/shard_map/ppermute | solution.py:341
  (86 other events, 867.6 us)
Sparse Core Ops, SparseCore 0:
  10.4 66.1 all-gather.4
  78.8 26.5 all-gather.6
  120.5 56.9 all-gather.10
  179.5 77.0 all-gather.8
  422.1 53.7 reduce-scatter.6
  553.4 26.5 reduce-scatter.10
  590.3 69.4 reduce-scatter.4
  700.5 58.6 reduce-scatter.8

commit v2 on v1

--- a/solution.py
+++ b/solution.py
@@ -127,45 +127,112 @@
     )(*lefts, *weights)
 
 
-def hidden_kernel(feat, count, *refs):
-    m_own, m_other, g_own, g_other = refs[:4]
-    gates, ups, downs = (refs[4 + i * count : 4 + (i + 1) * count] for i in range(3))
-    hidden_ref, gate_ref, up_ref, gate_scaled_ref, up_scaled_ref = refs[4 + 3 * count :]
+def units_kernel(feat, count, m_own, m_other, g_own, g_other, *refs):
+    sources = refs[: 3 * count]
+    hidden_ref, gate_ref, up_ref, own_ref, other_ref, held, arrived = refs[3 * count :]
+    copies = [
+        pltpu.make_async_copy(source, held.at[at], arrived.at[at]) for at, source in enumerate(sources)
+    ]
+    for copy in copies:
+        copy.start()
     middle = weave(m_own[...], m_other[...], feat)
     grad = weave(g_own[...], g_other[...], feat)
     scale = norm_scale(middle)
     part = hidden_ref.shape[1] // count
+    pairs = []
     for i in range(count):
         columns = slice(i * part, (i + 1) * part)
-        gate = nn(middle, gates[i][...]) * scale
-        up = nn(middle, ups[i][...]) * scale
-        hidden_grad = nn(grad, downs[i][...])
+        for copy in copies[3 * i : 3 * i + 3]:
+            copy.wait()
+        gate = nn(middle, held[3 * i]) * scale
+        up = nn(middle, held[3 * i + 1]) * scale
+        hidden_grad = nn(grad, held[3 * i + 2])
         sigmoid = 1.0 / (1.0 + jnp.exp(-gate))
         silu = gate * sigmoid
         hidden_ref[:, columns] = (silu * up).astype(BF16)
         gate_grad = hidden_grad * up * (sigmoid + silu * (1.0 - sigmoid))
         up_grad = hidden_grad * silu
-        gate_ref[:, columns] = gate_grad.astype(BF16)
-        up_ref[:, columns] = up_grad.astype(BF16)
-        gate_scaled_ref[:, columns] = (gate_grad * scale).astype(BF16)
-        up_scaled_ref[:, columns] = (up_grad * scale).astype(BF16)
-
-
-def hidden_units(feat, halves, gates, ups, downs):
-    tokens = halves[0].shape[0]
+        pairs.append((gate_grad.astype(BF16), held.at[3 * i]))
+        pairs.append((up_grad.astype(BF16), held.at[3 * i + 1]))
+        gate_ref[:, columns] = (gate_grad * scale).astype(BF16)
+        up_ref[:, columns] = (up_grad * scale).astype(BF16)
+    for at in range(0, own_ref.shape[1], feat):
+        rows = slice(2 * at, 2 * (at + feat))
+        total = None
+        for left, weight in pairs:
+            term = nt(left, weight[rows, :])
+            total = term if total is None else total + term
+        own_ref[:, at : at + feat] = total[:, :feat]
+        other_ref[:, at : at + feat] = total[:, feat:].astype(BF16)
+
+
+def units(feat, m_own, m_other, g_own, g_other, gates, ups, downs):
+    tokens, half = m_own.shape
     count, part = len(gates), gates[0].shape[1]
+    hidden = jax.ShapeDtypeStruct((tokens, count * part), BF16)
+    weights = [w for three in zip(gates, ups, downs) for w in three]
+    return pl.pallas_call(
+        functools.partial(units_kernel, feat, count),
+        in_specs=[pl.BlockSpec(memory_space=pltpu.VMEM)] * 4
+        + [pl.BlockSpec(memory_space=pl.ANY)] * len(weights),
+        out_specs=[pl.BlockSpec(memory_space=pltpu.VMEM)] * 5,
+        out_shape=[hidden] * 3
+        + [jax.ShapeDtypeStruct((tokens, half), F32), jax.ShapeDtypeStruct((tokens, half), BF16)],
+        scratch_shapes=[
+            pltpu.VMEM((len(weights),) + weights[0].shape, BF16),
+            pltpu.SemaphoreType.DMA((len(weights),)),
+        ],
+        compiler_params=pltpu.CompilerParams(vmem_limit_bytes=40 * 1024 * 1024),
+        name="units",
+    )(m_own, m_other, g_own, g_other, *weights)
+
+
+def outer_kernel(groups, count, *refs):
+    owns, others, rights = refs[:groups], refs[groups : 2 * groups], refs[2 * groups : 3 * groups]
+    outs = refs[3 * groups : 3 * groups + count]
+    left = jnp.concatenate(
+        [jnp.concatenate([own[...], other[...]], axis=1) for own, other in zip(owns, others)], axis=0
+    )
+    part = outs[0].shape[1]
+    for i, out in enumerate(outs):
+        columns = slice(i * part, (i + 1) * part)
+        right = jnp.concatenate([ref[:, columns] for ref in rights], axis=0)
+        result = tn(left, right)
+        out[...] = result.astype(BF16)
+
+
+def outer(feat, name, owns, others, rights, count=1):
+    half, columns = owns[0].shape[1], rights[0].shape[1]
+    part = columns // count
+    side = pl.BlockSpec((owns[0].shape[0], feat), lambda i: (0, i))
+    return pl.pallas_call(
+        functools.partial(outer_kernel, len(owns), count),
+        grid=(half // feat,),
+        in_specs=[side] * (2 * len(owns)) + [whole_spec(a) for a in rights],
+        out_specs=[pl.BlockSpec((2 * feat, part), lambda i: (i, 0))] * count,
+        out_shape=[jax.ShapeDtypeStruct((2 * half, part), BF16)] * count,
+        compiler_params=pltpu.CompilerParams(vmem_limit_bytes=40 * 1024 * 1024),
+        name=name,
+    )(*owns, *others, *rights)
+
+
+def fold_kernel(feat, own_ref, other_ref, weight_ref, out_ref):
+    out_ref[...] = nn(weave(own_ref[...], other_ref[...], feat), weight_ref[...]).astype(BF16)
+
+
+def fold(feat, own, other, weight):
+    tokens = own.shape[0]
     block = 256
-    result = jax.ShapeDtypeStruct((tokens, count * part), BF16)
-    weights = gates + ups + downs
+    result = jax.ShapeDtypeStruct((tokens, weight.shape[1]), BF16)
     return pl.pallas_call(
-        functools.partial(hidden_kernel, feat, count),
+        functools.partial(fold_kernel, feat),
         grid=(tokens // block,),
-        in_specs=[row_spec(block, a) for a in halves] + [whole_spec(w) for w in weights],
-        out_specs=[row_spec(block, result)] * 5,
-        out_shape=[result] * 5,
-        compiler_params=pltpu.CompilerParams(vmem_limit_bytes=VMEM_BYTES),
-        name="hidden_units",
-    )(*halves, *weights)
+        in_specs=[row_spec(block, own), row_spec(block, other), whole_spec(weight)],
+        out_specs=row_spec(block, result),
+        out_shape=result,
+        compiler_params=pltpu.CompilerParams(vmem_limit_bytes=40 * 1024 * 1024),
+        name="fold",
+    )(own, other, weight)
 
 
 def allowed_block(start_row, key_base, query_base, keys, queries):
@@ -351,8 +418,41 @@
             [jnp.where(core == 0, w[:feat], w[feat:]), jnp.where(core == 0, w[feat:], w[:feat])], axis=0
         )
 
-    def shift(a, step):
-        return lax.ppermute(a, "row", [(i, (i + step) % rows) for i in range(rows)])
+    def row_swap(a, step):
+        return lax.ppermute(a, "row", [(i, i ^ step) for i in range(rows)])
+
+    def gather_row(a):
+        got, bit = {0: a}, rows // 2
+        while bit:
+            for step in list(got):
+                got[step ^ bit] = row_swap(got[step], bit)
+            bit //= 2
+        return [got[step] for step in range(rows)]
+
+    def reduce_row(parts):
+        parts, bit = list(parts), 1
+        while bit < rows:
+            for at in range(0, rows, 2 * bit):
+                sent = row_swap(parts[at + bit].astype(BF16), bit)
+                parts[at] = parts[at].astype(F32) + sent.astype(F32)
+            bit *= 2
+        return parts[0]
+
+    def row_part(a, step):
+        size = a.shape[0] // rows
+        return lax.dynamic_slice_in_dim(a, (row ^ step) * size, size, 0)
+
+    def join_rows(pieces, axis=0, dtype=BF16):
+        size = pieces[0].shape[axis]
+        shape = list(pieces[0].shape)
+        shape[axis] *= rows
+        whole = jnp.zeros(shape, dtype)
+        for step, piece in enumerate(pieces):
+            whole = lax.dynamic_update_slice_in_dim(whole, piece, (row ^ step) * size, axis)
+        return whole
+
+    def after(value, *others):
+        return lax.optimization_barrier((value,) + others)[0]
 
     def put_rows(pieces):
         whole = jnp.zeros((tokens,) + pieces[0].shape[1:], pieces[0].dtype)
@@ -392,11 +492,10 @@
 
     def exchange(w):
         part = w.shape[1] // rows
-        whole = jnp.zeros((width, part), BF16)
-        for s in range(rows):
-            piece = lax.dynamic_slice_in_dim(w, (row + s) % rows * part, part, 1)
-            piece = shift(piece, s) if s else piece
-            whole = lax.dynamic_update_slice_in_dim(whole, piece, (row - s) % rows * 2 * feat, 0)
+        pieces = [lax.dynamic_slice_in_dim(w, (row ^ s) * part, part, 1) for s in range(rows)]
+        return join_rows([row_swap(piece, s) if s else piece for s, piece in enumerate(pieces)])
+
+    def spread_weights(whole):
         if places != 4:
             return spread(whole)
         first, second = plane_swap(whole, 1), plane_swap(whole, 2)
@@ -425,28 +524,27 @@
                 + plane_swap(to_second.astype(BF16), 2).astype(F32)
             )
         total = total.astype(BF16)
-        part = total.shape[1]
-        whole = jnp.zeros((2 * feat, rows * part), F32)
-        for s in range(rows):
-            piece = lax.dynamic_slice_in_dim(total, (row + s) % rows * 2 * feat, 2 * feat, 0)
-            piece = own_first(shift(piece, s) if s else piece).astype(F32)
-            whole = lax.dynamic_update_slice_in_dim(whole, piece, (row - s) % rows * part, 1)
-        return whole
+        pieces = [row_part(total, s) for s in range(rows)]
+        pieces = [own_first(row_swap(piece, s) if s else piece).astype(F32) for s, piece in enumerate(pieces)]
+        return join_rows(pieces, 1, F32)
 
     def give_rows(w):
-        return own_first(lax.psum_scatter(w, "row", scatter_dimension=0, tiled=True)).astype(F32)
-
-    def outer(own, other, right):
-        return tn(weave(own, other, feat), right).astype(BF16)
-
-    qkv = jnp.concatenate(
-        [scaled(w, gain_one) for w in (query_weight, key_weight, value_weight)], axis=1
-    )
-    qkv_full = lax.all_gather(qkv, "row", axis=0, tiled=True)
-    out_full = lax.all_gather(own_first(out_weight), "row", axis=0, tiled=True)
-    gates = exchange(scaled(gate_weight, gain_two))
-    ups = exchange(scaled(up_weight, gain_two))
-    downs = exchange(own_first(down_weight))
+        return own_first(reduce_row([row_part(w, s) for s in range(rows)]))
+
+    qkv_list = gather_row(
+        jnp.concatenate(
+            [scaled(w, gain_one) for w in (query_weight, key_weight, value_weight)], axis=1
+        )
+    )
+    gate_whole = exchange(scaled(gate_weight, gain_two))
+    up_whole = exchange(after(scaled(up_weight, gain_two), gate_whole, *qkv_list[1:3]))
+    out_list = gather_row(after(own_first(out_weight), *qkv_list))
+    down_whole = exchange(after(own_first(down_weight), up_whole, *qkv_list))
+    g_part = to_parts(out_grad)
+    g_list = gather_row(after(g_part, down_whole))
+    gates, ups, downs = (spread_weights(w) for w in (gate_whole, up_whole, down_whole))
+    qkv_full = join_rows(qkv_list)
+    out_full = join_rows(out_list)
 
     x_own = put_feats(spread(inputs))
     x_other = core_swap(x_own)
@@ -455,8 +553,10 @@
     start_row = jnp.sum(
         (segment_ids[None, :] < segment_ids[:, None]).astype(jnp.int32), axis=1
     )[None, :]
-    query, key, value, scale_one = project(feat, x_own, x_other, qkv_full, cosine, front, back)
+    x_ready = after(x_own, gates[1], gates[2], g_part)
+    query, key, value, scale_one = project(feat, x_ready, x_other, qkv_full, cosine, front, back)
     mixed, logs = attend(query, key, value, start_row)
+    mixed = after(mixed, up_whole, gates[3])
 
     def scatter_parts(own, other):
         own = own + core_swap(other).astype(F32)
@@ -471,21 +571,18 @@
     square = square + core_swap(square)
     scale_mid = lax.rsqrt(square / width + EPS)
 
-    m_own = lax.all_gather(middle.astype(BF16), "row", axis=0, tiled=True)
-    m_other = core_swap(m_own)
-    g_part = to_parts(out_grad)
-    g_own = lax.all_gather(g_part, "row", axis=0, tiled=True)
-    g_other = core_swap(g_own)
-    hidden, gate_low, up_low, gate_scaled, up_scaled = hidden_units(
-        feat, (m_own, m_other, g_own, g_other), gates, ups, downs
-    )
-
-    def gather_sum(own, other):
-        own = own + core_swap(other).astype(F32)
-        return lax.psum_scatter(own.astype(BF16), "row", scatter_dimension=0, tiled=True).astype(F32)
-
-    unit_grad = gather_sum(*unfold(feat, "unit_grad", (gate_low, gates), (up_low, ups)))
-    feed = gather_sum(*unfold(feat, "feed", (hidden, downs)))
+    m_list = gather_row(middle.astype(BF16))
+    m_others = [core_swap(m) for m in m_list]
+    g_others = [core_swap(g) for g in g_list]
+    found = [
+        units(feat, m, m_other, g, g_other, gates, ups, downs)
+        for m, m_other, g, g_other in zip(m_list, m_others, g_list, g_others)
+    ]
+    hidden = jnp.concatenate([f[0] for f in found], axis=0)
+    unit_grad = reduce_row([f[3] + core_swap(f[4]).astype(F32) for f in found])
+    feed_own, feed_other = unfold(feat, "feed", (after(hidden, found[-1][4]), downs))
+    feed_own = feed_own + core_swap(feed_other).astype(F32)
+    feed = reduce_row([feed_own[s * quarter : (s + 1) * quarter] for s in range(rows)])
     block_out = to_home((middle + feed).astype(BF16))
 
     unit_mid = middle * scale_mid
@@ -495,21 +592,17 @@
 
     d_own = put_rows(spread(middle_grad.astype(BF16)))
     d_other = core_swap(d_own)
-    d_all = weave(d_own, d_other, feat)
-    mixed_grad = nn(d_all, out_full).astype(BF16)
+    mixed_grad = fold(feat, d_own, d_other, out_full)
     query_grad, key_grad, value_grad = attend_back(
         query, key, value, mixed, mixed_grad, start_row, logs, cosine, front, back
     )
     grads = jnp.concatenate([query_grad, key_grad, value_grad], axis=1)
     grads_scaled = (grads.astype(F32) * scale_one).astype(BF16)
-    qkv_part = tn(weave(x_own, x_other, feat), grads_scaled)
-    qkv_grad = give_rows(qkv_part.astype(BF16))
-    gain_dots = jnp.sum(qkv_part * qkv_full.astype(F32), axis=1).reshape(rows, 2, feat)
+    qkv_part = outer(feat, "qkv_outer", [x_own], [x_other], [grads_scaled])[0]
+    qkv_grad = give_rows(qkv_part)
+    gain_dots = jnp.sum(qkv_part.astype(F32) * qkv_full.astype(F32), axis=1).reshape(rows, 2, feat)
     gain_dots = sum_cols(jnp.where(core == 0, gain_dots, gain_dots[:, ::-1]).reshape(width))
-    gain_row = sum(
-        shift(lax.dynamic_slice_in_dim(gain_dots, (row + s) % rows * 2 * feat, 2 * feat, 0), s)
-        for s in range(1, rows)
-    ) + lax.dynamic_slice_in_dim(gain_dots, row * 2 * feat, 2 * feat, 0)
+    gain_row = row_part(gain_dots, 0) + sum(row_swap(row_part(gain_dots, s), s) for s in range(1, rows))
     first_gain_grad = gain_row / gain_one[:, 0]
     first_unit_grad = scatter_parts(*unfold(feat, "first_grad", (grads, [qkv_full])))
     scale_first = token_part(scale_one, 0)
@@ -520,15 +613,12 @@
         (middle_grad + scale_first * (first_unit_grad - unit_first * (dot_one / width))).astype(BF16)
     )
 
-    out_weight_grad = give_rows(tn(d_all, mixed).astype(BF16))
-
-    def by_place(w):
-        part = w.shape[1] // places
-        return [w[:, s * part : (s + 1) * part] for s in range(places)]
-
-    down_weight_grad = give_back(by_place(outer(g_own, g_other, hidden)))
-    gate_unit = give_back(by_place(outer(m_own, m_other, gate_scaled)))
-    up_unit = give_back(by_place(outer(m_own, m_other, up_scaled)))
+    out_weight_grad = give_rows(outer(feat, "out_outer", [d_own], [d_other], [mixed])[0])
+    down_weight_grad = give_back(
+        outer(feat, "down_outer", g_list, g_others, [f[0] for f in found], places)
+    )
+    gate_unit = give_back(outer(feat, "gate_outer", m_list, m_others, [f[1] for f in found], places))
+    up_unit = give_back(outer(feat, "up_outer", m_list, m_others, [f[2] for f in found], places))
     q_unit = qkv_grad[:, :heads_width]
     k_unit = qkv_grad[:, heads_width : 2 * heads_width]
     v_unit = qkv_grad[:, 2 * heads_width :]

time: 808 us -> 782 us (0.968)
  waiting for transfers between devices: 329 us -> 412 us
  other arithmetic: 88.9 us -> 45.4 us
  Pallas kernels: 87.3 us -> 125 us
  starting transfers between devices: 141 us -> 110 us
  matrix products: 30.6 us -> 0 us
  local copies, waits for them, and re-layouts: 103 us -> 79.3 us
  between operations: 15.8 us -> 2.83 us
    ppermute x21 -> x45, waiting for transfers between devices: 57.4 us -> 243 us  [row_swap(): return lax.ppermute(a, 'row', [(i, i ^ step) for i in range(rows)])]
    pallas_call x1 -> x10, Pallas kernels: 21.3 us -> 72.2 us  [the longest x4 42.5 us: units(): pl.pallas_call(functools.partial(units_kernel, feat, count), in_specs=[pl...]
    ppermute x45, waiting for transfers between devices: 207 us -> 159 us  [plane_swap(): return lax.ppermute(a, 'col', [(i, i ^ 2 * step) for i in range(cols)])]
    all_gather x4 -> x0, waiting for transfers between devices: 31.9 us -> none  [the longest x1 21.6 us: local(): qkv_full = lax.all_gather(qkv, 'row', axis=0, tiled=True)]
    reduce_scatter x4 -> x0, waiting for transfers between devices: 31.8 us -> none  [the longest x2 31.8 us: gather_sum(): lax.psum_scatter(own.astype(BF16), 'row', scatter_dimension=0, tiled=True)]
    dot_general x6 -> x0, matrix products: 30.6 us -> none  [the longest x5 28.5 us: tn(): lax.dot_general(left, right, (((0,), (0,)), ((), ())), preferred_element_...]
    ppermute x21 -> x45, starting transfers between devices: 75.7 us -> 49.8 us  [row_swap(): return lax.ppermute(a, 'row', [(i, i ^ step) for i in range(rows)])]
    unnamed x152 -> x184, local copies, waits for them, and re-layouts: 44.4 us -> 26.7 us
  transfers between devices with their start and end apart: 91 -> 116, of which waited for: 37 -> 51; matrix products, arithmetic and copies ran while one was open for 25% -> 13% of each run, Pallas kernels for 6% -> 13%
where the time goes in v2:
time: 782 us; the launch traced here: 774 us
  waiting for transfers between devices  412 us (53%)
  Pallas kernels  125 us (16%)
  starting transfers between devices  110 us (14%)
  local copies, waits for them, and re-layouts  79.3 us (10%)
  other arithmetic  45.4 us (6%)
    ppermute x45, waiting for transfers between devices, row_swap(): return lax.ppermute(a, 'row', [(i, i ^ step) for i in range(rows)])  243 us
    ppermute x45, waiting for transfers between devices, plane_swap(): return lax.ppermute(a, 'col', [(i, i ^ 2 * step) for i in range(cols)])  159 us
    ppermute x45, starting transfers between devices, plane_swap(): return lax.ppermute(a, 'col', [(i, i ^ 2 * step) for i in range(cols)])  52.3 us
    ppermute x45, starting transfers between devices, row_swap(): return lax.ppermute(a, 'row', [(i, i ^ step) for i in range(rows)])  49.8 us
    pallas_call x4, Pallas kernels, units(): pl.pallas_call(functools.partial(units_kernel, feat, count), in_specs=[pl...  42.5 us
    pallas_call x5, Pallas kernels, outer(): pl.pallas_call(functools.partial(outer_kernel, len(owns), count), grid=(h...  27.9 us
    unnamed x184, local copies, waits for them, and re-layouts  26.7 us
    pallas_call x3, Pallas kernels, unfold(): pl.pallas_call(functools.partial(unfold_kernel, feat, tuple((len(ws) for...  22 us
  transfers between devices with their start and end apart: 116, of which 51 were waited for; matrix products, arithmetic and copies ran while one was open for 13% of the time, Pallas kernels for 13%

profile of v2, /device:TPU:0, one launch (start us, length us, event | category | flops | bytes accessed | tf_op | source)
XLA Modules:
  0.0 773.8 jit_solution(275762459300697161)
XLA Ops:
  0.6 3.0 collective-permute-start
  10.5 2.6 collective-permute-start.4
  23.2 9.0 %collective-permute-done.4 = bf16[512,256]{1,0:T(8,128)(2,1)} collective-permute-done((bf16[512,256]{1,0:T(8,128)(2,1)}, bf16[512,256]{1,0:T(8,128)(2,1)}, u32[]{:S(2)}, u32[]{:S(2)}) %collective-permute-start.4) | collective-permute-done | bytes 262176 | tf_op jit(solution)/shard_map/ppermute | solution.py:422
  43.8 3.0 collective-permute-done.2
  47.4 10.6 %collective-permute-done.12 = bf16[512,768]{1,0:T(8,128)(2,1)} collective-permute-done((bf16[512,768]{1,0:T(8,128)(2,1)}, bf16[512,768]{1,0:T(8,128)(2,1)}, u32[]{:S(2)}, u32[]{:S(2)}) %collective-permute-start.12) | collective-permute-done | bytes 786464 | tf_op jit(solution)/shard_map/ppermute | solution.py:422
  58.5 11.1 %collective-permute-done.13 = bf16[512,768]{1,0:T(8,128)(2,1)} collective-permute-done((bf16[512,768]{1,0:T(8,128)(2,1)}, bf16[512,768]{1,0:T(8,128)(2,1)}, u32[]{:S(2)}, u32[]{:S(2)}) %collective-permute-start.13) | collective-permute-done | bytes 786464 | tf_op jit(solution)/shard_map/ppermute | solution.py:422
  74.0 2.5 copy.30.cos_ref
  78.6 2.5 copy.31.front_ref
  82.3 2.6 copy.32.back_ref
  95.4 15.0 %collective-permute-done.16 = bf16[512,256]{1,0:T(8,128)(2,1)S(1)} collective-permute-done((bf16[512,256]{1,0:T(8,128)(2,1)}, bf16[512,256]{1,0:T(8,128)(2,1)S(1)}, u32[]{:S(2)}, u32[]{:S(2)}) %collective-permute-start.16) | collective-permute-done | bytes 262176 | tf_op jit(solution)/shard_map/ppermute | solution.py:422
  110.3 2.5 collective-permute-start.17
  121.3 5.2 collective-permute-start.21
  128.9 9.6 %collective-permute-done.21 = bf16[512,256]{1,0:T(8,128)(2,1)S(1)} collective-permute-done((bf16[512,256]{1,0:T(8,128)(2,1)S(1)}, bf16[512,256]{1,0:T(8,128)(2,1)S(1)}, u32[]{:S(2)}, u32[]{:S(2)}) %collective-permute-start.21) | collective-permute-done | bytes 262176 | tf_op jit(solution)/shard_map/ppermute | solution.py:422
  140.9 5.2 collective-permute-done.22
  146.2 8.8 %project.1 = (bf16[1024,256]{1,0:T(8,128)(2,1)}, bf16[1024,256]{1,0:T(8,128)(2,1)}, bf16[1024,256]{1,0:T(8,128)(2,1)}, f32[1024,1]{1,0:T(8,128)}) custom-call(bf16[1024,1024]{1,0:T(8,128)(2,1)} %copy-done.2, bf16[1024,1024]{1,0:T(8,128)(2,1)} %collective-permute-done.11.other_ref.refs_1_, ...), custom_call_target="tpu_custom_call" | custom-call | tf_op jit(solution)/shard_map/project/pallas_call | solution.py:83
  155.0 10.1 %attend.1 = (bf16[1024,256]{1,0:T(8,128)(2,1)}, f32[2,2,1024]{2,1,0:T(2,128)}) custom-call(bf16[1024,256]{1,0:T(8,128)(2,1)} %get-tuple-element.66.q_ref, bf16[1024,256]{1,0:T(8,128)(2,1)} %get-tuple-element.67.k_ref, bf16[1024,256]{1,0:T(8,128)(2,1)} %get-tuple-element.68.v_ref, s32[1,1024]{1,0:T(1,128)} %bitcast.16), custom_call_target="tpu_custom_call" | custom-call | tf_op jit(solution)/shard_map/attend/pallas_call | solution.py:277
  165.1 5.4 mix.1
  176.8 7.4 collective-permute-done.28
  184.8 7.7 collective-permute-done.29
  192.6 5.8 collective-permute-start.46
  203.2 18.6 %collective-permute-done.34.refs_7_ = bf16[2048,256]{1,0:T(8,128)(2,1)S(1)} collective-permute-done((bf16[2048,256]{1,0:T(8,128)(2,1)}, bf16[2048,256]{1,0:T(8,128)(2,1)S(1)}, u32[]{:S(2)}, u32[]{:S(2)}) %collective-permute-start.34) | collective-permute-done | bytes 1048608 | tf_op jit(solution)/shard_map/ppermute | solution.py:408
  223.8 9.2 %collective-permute-done.25 = bf16[256,1024]{1,0:T(8,128)(2,1)S(1)} collective-permute-done((bf16[256,1024]{1,0:T(8,128)(2,1)S(1)}, bf16[256,1024]{1,0:T(8,128)(2,1)S(1)}, u32[]{:S(2)}, u32[]{:S(2)}) %collective-permute-start.25) | collective-permute-done | bytes 524320 | tf_op jit(solution)/shard_map/ppermute | solution.py:408
  237.6 20.1 %collective-permute-done.36 = bf16[1024,256]{1,0:T(8,128)(2,1)S(1)} collective-permute-done((bf16[1024,256]{1,0:T(8,128)(2,1)S(1)}, bf16[1024,256]{1,0:T(8,128)(2,1)S(1)}, u32[]{:S(2)}, u32[]{:S(2)}) %collective-permute-start.36) | collective-permute-done | bytes 524320 | tf_op jit(solution)/shard_map/ppermute | solution.py:408
  261.4 4.1 collective-permute-done.37
  266.9 17.3 %collective-permute-done.44.m_own.refs_2_ = bf16[256,1024]{1,0:T(8,128)(2,1)} collective-permute-done((bf16[256,1024]{1,0:T(8,128)(2,1)}, bf16[256,1024]{1,0:T(8,128)(2,1)}, u32[]{:S(2)}, u32[]{:S(2)}) %collective-permute-start.44) | collective-permute-done | bytes 524320 | tf_op jit(solution)/shard_map/ppermute | solution.py:422
  286.8 5.4 collective-permute-done.40.m_own.refs_1_
  292.8 8.3 %collective-permute-done.48.m_own.refs_3_ = bf16[256,1024]{1,0:T(8,128)(2,1)} collective-permute-done((bf16[256,1024]{1,0:T(8,128)(2,1)}, bf16[256,1024]{1,0:T(8,128)(2,1)}, u32[]{:S(2)}, u32[]{:S(2)}) %collective-permute-start.48) | collective-permute-done | bytes 524320 | tf_op jit(solution)/shard_map/ppermute | solution.py:422
  311.5 10.1 %units.4 = (bf16[256,1024]{1,0:T(8,128)(2,1)S(1)}, bf16[256,1024]{1,0:T(8,128)(2,1)S(1)}, bf16[256,1024]{1,0:T(8,128)(2,1)S(1)}, f32[256,1024]{1,0:T(8,128)S(1)}, bf16[256,1024]{1,0:T(8,128)(2,1)S(1)}) custom-call(bf16[256,1024]{1,0:T(8,128)(2,1)} %convert_element_type.334.m_own.refs_0_, bf16[256,1024]{1,0:T(8,128)(2,1)} %collective-permute-done.27.m_other.refs_4_, ...), custom_call_target="tpu_custom_call" | custom-call | tf_op jit(solution)/shard_map/units/pallas_call | solution.py:174
  322.4 10.7 %units.6 = (bf16[256,1024]{1,0:T(8,128)(2,1)S(1)}, bf16[256,1024]{1,0:T(8,128)(2,1)S(1)}, bf16[256,1024]{1,0:T(8,128)(2,1)S(1)}, f32[256,1024]{1,0:T(8,128)S(1)}, bf16[256,1024]{1,0:T(8,128)(2,1)}) custom-call(bf16[256,1024]{1,0:T(8,128)(2,1)} %collective-permute-done.44.m_own.refs_2_, bf16[256,1024]{1,0:T(8,128)(2,1)} %collective-permute-done.45.m_other.refs_6_, ...), custom_call_target="tpu_custom_call" | custom-call | tf_op jit(solution)/shard_map/units/pallas_call | solution.py:174
  334.6 10.9 %units.5 = (bf16[256,1024]{1,0:T(8,128)(2,1)S(1)}, bf16[256,1024]{1,0:T(8,128)(2,1)S(1)}, bf16[256,1024]{1,0:T(8,128)(2,1)S(1)}, f32[256,1024]{1,0:T(8,128)S(1)}, bf16[256,1024]{1,0:T(8,128)(2,1)}) custom-call(bf16[256,1024]{1,0:T(8,128)(2,1)} %collective-permute-done.40.m_own.refs_1_, bf16[256,1024]{1,0:T(8,128)(2,1)} %collective-permute-done.41.m_other.refs_5_, ...), custom_call_target="tpu_custom_call" | custom-call | tf_op jit(solution)/shard_map/units/pallas_call | solution.py:174
  346.6 10.8 %units.7 = (bf16[256,1024]{1,0:T(8,128)(2,1)S(1)}, bf16[256,1024]{1,0:T(8,128)(2,1)S(1)}, bf16[256,1024]{1,0:T(8,128)(2,1)S(1)}, f32[256,1024]{1,0:T(8,128)S(1)}, bf16[256,1024]{1,0:T(8,128)(2,1)}) custom-call(bf16[256,1024]{1,0:T(8,128)(2,1)} %collective-permute-done.48.m_own.refs_3_, bf16[256,1024]{1,0:T(8,128)(2,1)} %collective-permute-done.49.m_other.refs_7_, ...), custom_call_target="tpu_custom_call" | custom-call | tf_op jit(solution)/shard_map/units/pallas_call | solution.py:174
  360.6 6.7 up_outer.1
  371.5 6.6 gate_outer.1
  379.1 6.4 down_outer.1
  391.7 8.9 %feed.1 = (f32[1024,1024]{1,0:T(8,128)}, bf16[1024,1024]{1,0:T(8,128)(2,1)}) custom-call(bf16[1024,1024]{1,0:T(8,128)(2,1)} %pad_maximum_fusion.refs_0_, bf16[2048,256]{1,0:T(8,128)(2,1)} %copy-done, bf16[2048,256]{1,0:T(8,128)(2,1)} %copy-done.1, bf16[2048,256]{1,0:T(8,128)(2,1)} %copy-done.54, bf16[2048,256]{1,0:T(8,128)(2,1)} %copy-done.55), custom_call_target="tpu_custom_call" | custom-call | tf_op jit(solution)/shard_map/feed/pallas_call | solution.py:119
  408.4 7.4 collective-permute-done.86
  419.8 7.2 collective-permute-done.100
  430.3 19.2 %collective-permute-done.96 = bf16[2048,256]{1,0:T(8,128)(2,1)S(1)} collective-permute-done((bf16[2048,256]{1,0:T(8,128)(2,1)S(1)}, bf16[2048,256]{1,0:T(8,128)(2,1)S(1)}, u32[]{:S(2)}, u32[]{:S(2)}) %collective-permute-start.96) | collective-permute-done | bytes 1048608 | tf_op jit(solution)/shard_map/ppermute | solution.py:408
  450.1 20.2 %collective-permute-done.89 = bf16[2048,256]{1,0:T(8,128)(2,1)S(1)} collective-permute-done((bf16[2048,256]{1,0:T(8,128)(2,1)S(1)}, bf16[2048,256]{1,0:T(8,128)(2,1)S(1)}, u32[]{:S(2)}, u32[]{:S(2)}) %collective-permute-start.89) | collective-permute-done | bytes 1048608 | tf_op jit(solution)/shard_map/ppermute | solution.py:408
  473.2 20.7 %collective-permute-done.103 = bf16[2048,256]{1,0:T(8,128)(2,1)S(1)} collective-permute-done((bf16[2048,256]{1,0:T(8,128)(2,1)S(1)}, bf16[2048,256]{1,0:T(8,128)(2,1)S(1)}, u32[]{:S(2)}, u32[]{:S(2)}) %collective-permute-start.103) | collective-permute-done | bytes 1048608 | tf_op jit(solution)/shard_map/ppermute | solution.py:408
  501.8 4.1 collective-permute-done.97
  509.8 18.4 %collective-permute-done.54 = bf16[256,1024]{1,0:T(8,128)(2,1)S(1)} collective-permute-done((bf16[256,1024]{1,0:T(8,128)(2,1)S(1)}, bf16[256,1024]{1,0:T(8,128)(2,1)S(1)}, u32[]{:S(2)}, u32[]{:S(2)}) %collective-permute-start.54) | collective-permute-done | bytes 524320 | tf_op jit(solution)/shard_map/ppermute | solution.py:422
  528.4 3.0 collective-permute-start.66
  531.4 2.3 collective-permute-done.90
  533.7 17.2 %collective-permute-done.91 = bf16[512,256]{1,0:T(8,128)(2,1)S(1)} collective-permute-done((bf16[512,256]{1,0:T(8,128)(2,1)S(1)}, bf16[512,256]{1,0:T(8,128)(2,1)S(1)}, u32[]{:S(2)}, u32[]{:S(2)}) %collective-permute-start.91) | collective-permute-done | bytes 262176 | tf_op jit(solution)/shard_map/ppermute | solution.py:422
  554.5 27.2 %collective-permute-done.66 = bf16[256,1024]{1,0:T(8,128)(2,1)S(1)} collective-permute-done((bf16[256,1024]{1,0:T(8,128)(2,1)S(1)}, bf16[256,1024]{1,0:T(8,128)(2,1)S(1)}, u32[]{:S(2)}, u32[]{:S(2)}) %collective-permute-start.66) | collective-permute-done | bytes 524320 | tf_op jit(solution)/shard_map/ppermute | solution.py:422
  581.7 13.8 %collective-permute-done.55 = bf16[256,1024]{1,0:T(8,128)(2,1)S(1)} collective-permute-done((bf16[256,1024]{1,0:T(8,128)(2,1)S(1)}, bf16[256,1024]{1,0:T(8,128)(2,1)S(1)}, u32[]{:S(2)}, u32[]{:S(2)}) %collective-permute-start.55) | collective-permute-done | bytes 524320 | tf_op jit(solution)/shard_map/ppermute | solution.py:422
  597.6 2.5 constant_dynamic-update-slice_fusion.6
  604.4 10.5 %collective-permute-done.68 = bf16[256,1024]{1,0:T(8,128)(2,1)S(1)} collective-permute-done((bf16[256,1024]{1,0:T(8,128)(2,1)S(1)}, bf16[256,1024]{1,0:T(8,128)(2,1)S(1)}, u32[]{:S(2)}, u32[]{:S(2)}) %collective-permute-start.68) | collective-permute-done | bytes 524320 | tf_op jit(solution)/shard_map/ppermute | solution.py:408
  616.9 8.5 %collective-permute-done.69 = bf16[256,1024]{1,0:T(8,128)(2,1)S(1)} collective-permute-done((bf16[256,1024]{1,0:T(8,128)(2,1)S(1)}, bf16[256,1024]{1,0:T(8,128)(2,1)S(1)}, u32[]{:S(2)}, u32[]{:S(2)}) %collective-permute-start.69) | collective-permute-done | bytes 524320 | tf_op jit(solution)/shard_map/ppermute | solution.py:408
  636.5 2.8 collective-permute-done.115
  644.7 11.4 %attend_back.1 = (bf16[1024,256]{1,0:T(8,128)(2,1)}, bf16[1024,256]{1,0:T(8,128)(2,1)}, bf16[1024,256]{1,0:T(8,128)(2,1)}) custom-call(bf16[1024,256]{1,0:T(8,128)(2,1)} %get-tuple-element.66.q_ref, bf16[1024,256]{1,0:T(8,128)(2,1)} %get-tuple-element.67.k_ref, bf16[1024,256]{1,0:T(8,128)(2,1)} %get-tuple-element.68.v_ref, ...), custom_call_target="tpu_custom_call" | custom-call | tf_op jit(solution)/shard_map/attend_back/pallas_call | solution.py:346
  659.6 7.7 first_grad.1
  669.4 5.4 qkv_outer.1
  676.6 2.8 multiply_reduce_fusion
  683.1 2.7 out_outer.1
  687.3 2.3 collective-permute-done.108
  698.6 14.4 %collective-permute-done.112 = f32[512]{0:T(512)S(1)} collective-permute-done((f32[512]{0:T(512)S(1)}, f32[512]{0:T(512)S(1)}, u32[]{:S(2)}, u32[]{:S(2)}) %collective-permute-start.112) | collective-permute-done | bytes 2080 | tf_op jit(solution)/shard_map/ppermute | solution.py:422
  713.4 2.6 collective-permute-start.85
  722.0 4.5 collective-permute-done.85
  726.9 2.5 fusion.26
  733.2 21.6 %collective-permute-done.80 = bf16[512,768]{1,0:T(8,128)(2,1)S(1)} collective-permute-done((bf16[512,768]{1,0:T(8,128)(2,1)S(1)}, bf16[512,768]{1,0:T(8,128)(2,1)S(1)}, u32[]{:S(2)}, u32[]{:S(2)}) %collective-permute-start.80) | collective-permute-done | bytes 786464 | tf_op jit(solution)/shard_map/ppermute | solution.py:422
  754.8 5.4 collective-permute-done.82
  768.4 2.6 collective-permute-done.78
  (540 shorter events, 216.1 us)
Async XLA Ops:
  0.6 37.8 %collective-permute-start = (bf16[1024,256]{1,0:T(8,128)(2,1)}, bf16[1024,256]{1,0:T(8,128)(2,1)}, u32[]{:S(2)}, u32[]{:S(2)}) collective-permute-start(bf16[1024,256]{1,0:T(8,128)(2,1)} %param.13), channel_id=1, source_target_pairs={{0,2},{1,3},{2,0},{3,1},{4,6},{5,7},{6,4},{7,5},{8,10},{9,11},{10,... | collective-permute-start | bytes 1572872 | tf_op jit(solution)/shard_map/ppermute | solution.py:408
  3.6 37.5 %collective-permute-start.1 = (bf16[1024,256]{1,0:T(8,128)(2,1)}, bf16[1024,256]{1,0:T(8,128)(2,1)}, u32[]{:S(2)}, u32[]{:S(2)}) collective-permute-start(bf16[1024,256]{1,0:T(8,128)(2,1)} %param.13), channel_id=1, source_target_pairs={{0,4},{1,5},{2,6},{3,7},{4,0},{5,1},{6,2},{7,3},{8,12},{9,13},{10,... | collective-permute-start | bytes 1572872 | tf_op jit(solution)/shard_map/ppermute | solution.py:408
  22.4 35.5 %collective-permute-start.12 = (bf16[512,768]{1,0:T(8,128)(2,1)}, bf16[512,768]{1,0:T(8,128)(2,1)}, u32[]{:S(2)}, u32[]{:S(2)}) collective-permute-start(bf16[512,768]{1,0:T(8,128)(2,1)} %get-tuple-element.192), channel_id=1, source_target_pairs={{0,8},{8,0},{16,24},{24,16},{1,9},{9,1},{17,25},{25,17},{2,10},{10... | collective-permute-start | bytes 2359304 | tf_op jit(solution)/shard_map/ppermute | solution.py:422
  32.2 37.4 %collective-permute-start.13 = (bf16[512,768]{1,0:T(8,128)(2,1)}, bf16[512,768]{1,0:T(8,128)(2,1)}, u32[]{:S(2)}, u32[]{:S(2)}) collective-permute-start(bf16[512,768]{1,0:T(8,128)(2,1)} %get-tuple-element.192), channel_id=1, source_target_pairs={{0,16},{8,24},{16,0},{24,8},{1,17},{9,25},{17,1},{25,9},{2,18},{10... | collective-permute-start | bytes 2359304 | tf_op jit(solution)/shard_map/ppermute | solution.py:422
  38.5 33.2 %collective-permute-start.8 = (bf16[256,256]{1,0:T(8,128)(2,1)}, bf16[256,256]{1,0:T(8,128)(2,1)}, u32[]{:S(2)}, u32[]{:S(2)}) collective-permute-start(bf16[256,256]{1,0:T(8,128)(2,1)} %get-tuple-element.205), channel_id=1, source_target_pairs={{0,2},{1,3},{2,0},{3,1},{4,6},{5,7},{6,4},{7,5},{8,10},{9,11},{10,... | collective-permute-start | bytes 393224 | tf_op jit(solution)/shard_map/ppermute | solution.py:408
  41.1 43.7 %collective-permute-start.9 = (bf16[256,256]{1,0:T(8,128)(2,1)}, bf16[256,256]{1,0:T(8,128)(2,1)}, u32[]{:S(2)}, u32[]{:S(2)}) collective-permute-start(bf16[256,256]{1,0:T(8,128)(2,1)} %get-tuple-element.207), channel_id=1, source_target_pairs={{0,4},{1,5},{2,6},{3,7},{4,0},{5,1},{6,2},{7,3},{8,12},{9,13},{10,... | collective-permute-start | bytes 393224 | tf_op jit(solution)/shard_map/ppermute | solution.py:408
  46.8 38.6 %collective-permute-start.10 = (bf16[256,256]{1,0:T(8,128)(2,1)}, bf16[256,256]{1,0:T(8,128)(2,1)}, u32[]{:S(2)}, u32[]{:S(2)}) collective-permute-start(bf16[256,256]{1,0:T(8,128)(2,1)} %get-tuple-element.204), channel_id=1, source_target_pairs={{0,6},{1,7},{2,4},{3,5},{4,2},{5,3},{6,0},{7,1},{8,14},{9,15},{10,... | collective-permute-start | bytes 393224 | tf_op jit(solution)/shard_map/ppermute | solution.py:408
  58.0 59.4 %collective-permute-start.7 = (bf16[2048,256]{1,0:T(8,128)(2,1)S(1)}, bf16[2048,256]{1,0:T(8,128)(2,1)}, u32[]{:S(2)}, u32[]{:S(2)}) collective-permute-start(bf16[2048,256]{1,0:T(8,128)(2,1)S(1)} %constant_dynamic-update-slice_fusion.27.refs_0_), channel_id=1, source_target_pairs={{0,4},{1,5},{2,6},{3,7},{4,0},{5,1},{6,2},{7,3},{8,12},{9,13},{10,... | collective-permute-start | bytes 3145736 | tf_op jit(solution)/shard_map/ppermute | solution.py:408
  69.6 76.5 %collective-permute-start.11 = (bf16[1024,1024]{1,0:T(8,128)(2,1)S(1)}, bf16[1024,1024]{1,0:T(8,128)(2,1)}, u32[]{:S(2)}, u32[]{:S(2)}) collective-permute-start(bf16[1024,1024]{1,0:T(8,128)(2,1)S(1)} %constant_dynamic-update-slice_fusion.30.own_ref.refs_0_), channel_id=1, source_target_pairs={{0,1},{1,0},{2,3},{3,2},{4,5},{5,4},{6,7},{7,6},{8,9},{9,8},{10,11... | collective-permute-start | bytes 6291464 | tf_op jit(solution)/shard_map/ppermute | solution.py:405
  84.8 42.4 %collective-permute-start.6 = (bf16[2048,256]{1,0:T(8,128)(2,1)S(1)}, bf16[2048,256]{1,0:T(8,128)(2,1)S(1)}, u32[]{:S(2)}, u32[]{:S(2)}) collective-permute-start(bf16[2048,256]{1,0:T(8,128)(2,1)S(1)} %constant_dynamic-update-slice_fusion.27.refs_0_), channel_id=1, source_target_pairs={{0,2},{1,3},{2,0},{3,1},{4,6},{5,7},{6,4},{7,5},{8,10},{9,11},{10,... | collective-permute-start | bytes 3145736 | tf_op jit(solution)/shard_map/ppermute | solution.py:408
  85.4 34.6 %collective-permute-start.14 = (bf16[512,768]{1,0:T(8,128)(2,1)}, bf16[512,768]{1,0:T(8,128)(2,1)S(1)}, u32[]{:S(2)}, u32[]{:S(2)}) collective-permute-start(bf16[512,768]{1,0:T(8,128)(2,1)} %collective-permute-done.13), channel_id=1, source_target_pairs={{0,8},{8,0},{16,24},{24,16},{1,9},{9,1},{17,25},{25,17},{2,10},{10... | collective-permute-start | bytes 2359304 | tf_op jit(solution)/shard_map/ppermute | solution.py:422
  170.5 27.9 %collective-permute-start.23 = (bf16[1024,1024]{1,0:T(8,128)(2,1)}, bf16[1024,1024]{1,0:T(8,128)(2,1)S(1)}, u32[]{:S(2)}, u32[]{:S(2)}) collective-permute-start(bf16[1024,1024]{1,0:T(8,128)(2,1)} %get-tuple-element.74), channel_id=1, source_target_pairs={{0,1},{1,0},{2,3},{3,2},{4,5},{5,4},{6,7},{7,6},{8,9},{9,8},{10,11... | collective-permute-start | bytes 6291464 | tf_op jit(solution)/shard_map/ppermute | solution.py:405
  175.3 27.4 %collective-permute-start.32 = (bf16[2048,256]{1,0:T(8,128)(2,1)}, bf16[2048,256]{1,0:T(8,128)(2,1)S(1)}, u32[]{:S(2)}, u32[]{:S(2)}) collective-permute-start(bf16[2048,256]{1,0:T(8,128)(2,1)} %constant_dynamic-update-slice_fusion.17.refs_1_), channel_id=1, source_target_pairs={{0,2},{1,3},{2,0},{3,1},{4,6},{5,7},{6,4},{7,5},{8,10},{9,11},{10,... | collective-permute-start | bytes 3145736 | tf_op jit(solution)/shard_map/ppermute | solution.py:408
  184.3 37.5 %collective-permute-start.34 = (bf16[2048,256]{1,0:T(8,128)(2,1)}, bf16[2048,256]{1,0:T(8,128)(2,1)S(1)}, u32[]{:S(2)}, u32[]{:S(2)}) collective-permute-start(bf16[2048,256]{1,0:T(8,128)(2,1)} %constant_dynamic-update-slice_fusion.17.refs_1_), channel_id=1, source_target_pairs={{0,4},{1,5},{2,6},{3,7},{4,0},{5,1},{6,2},{7,3},{8,12},{9,13},{10,... | collective-permute-start | bytes 3145736 | tf_op jit(solution)/shard_map/ppermute | solution.py:408
  192.6 29.7 %collective-permute-start.46 = (bf16[256,1024]{1,0:T(8,128)(2,1)}, bf16[256,1024]{1,0:T(8,128)(2,1)S(1)}, u32[]{:S(2)}, u32[]{:S(2)}) collective-permute-start(bf16[256,1024]{1,0:T(8,128)(2,1)} %constant_dynamic-update-slice_fusion.24.g_own.refs_0_), channel_id=1, source_target_pairs={{0,16},{8,24},{16,0},{24,8},{1,17},{9,25},{17,1},{25,9},{2,18},{10... | collective-permute-start | bytes 1572872 | tf_op jit(solution)/shard_map/ppermute | solution.py:422
  199.7 24.1 %collective-permute-start.26 = (bf16[256,1024]{1,0:T(8,128)(2,1)S(1)}, bf16[256,1024]{1,0:T(8,128)(2,1)S(1)}, u32[]{:S(2)}, u32[]{:S(2)}) collective-permute-start(bf16[256,1024]{1,0:T(8,128)(2,1)S(1)} %get-tuple-element.142), channel_id=1, source_target_pairs={{0,6},{1,7},{2,4},{3,5},{4,2},{5,3},{6,0},{7,1},{8,14},{9,15},{10,... | collective-permute-start | bytes 1572872 | tf_op jit(solution)/shard_map/ppermute | solution.py:408
  201.2 31.9 %collective-permute-start.25 = (bf16[256,1024]{1,0:T(8,128)(2,1)S(1)}, bf16[256,1024]{1,0:T(8,128)(2,1)S(1)}, u32[]{:S(2)}, u32[]{:S(2)}) collective-permute-start(bf16[256,1024]{1,0:T(8,128)(2,1)S(1)} %get-tuple-element.143), channel_id=1, source_target_pairs={{0,4},{1,5},{2,6},{3,7},{4,0},{5,1},{6,2},{7,3},{8,12},{9,13},{10,... | collective-permute-start | bytes 1572872 | tf_op jit(solution)/shard_map/ppermute | solution.py:408
  202.7 30.3 %collective-permute-start.24 = (bf16[256,1024]{1,0:T(8,128)(2,1)S(1)}, bf16[256,1024]{1,0:T(8,128)(2,1)S(1)}, u32[]{:S(2)}, u32[]{:S(2)}) collective-permute-start(bf16[256,1024]{1,0:T(8,128)(2,1)S(1)} %get-tuple-element.141), channel_id=1, source_target_pairs={{0,2},{1,3},{2,0},{3,1},{4,6},{5,7},{6,4},{7,5},{8,10},{9,11},{10,... | collective-permute-start | bytes 1572872 | tf_op jit(solution)/shard_map/ppermute | solution.py:408
  221.8 35.9 %collective-permute-start.35 = (bf16[2048,256]{1,0:T(8,128)(2,1)S(1)}, bf16[2048,256]{1,0:T(8,128)(2,1)S(1)}, u32[]{:S(2)}, u32[]{:S(2)}) collective-permute-start(bf16[2048,256]{1,0:T(8,128)(2,1)S(1)} %constant_dynamic-update-slice_fusion.10.refs_2_.refs_1_), channel_id=1, source_target_pairs={{0,4},{1,5},{2,6},{3,7},{4,0},{5,1},{6,2},{7,3},{8,12},{9,13},{10,... | collective-permute-start | bytes 3145736 | tf_op jit(solution)/shard_map/ppermute | solution.py:408
  222.3 36.7 %collective-permute-start.33 = (bf16[2048,256]{1,0:T(8,128)(2,1)S(1)}, bf16[2048,256]{1,0:T(8,128)(2,1)S(1)}, u32[]{:S(2)}, u32[]{:S(2)}) collective-permute-start(bf16[2048,256]{1,0:T(8,128)(2,1)S(1)} %constant_dynamic-update-slice_fusion.10.refs_2_.refs_1_), channel_id=1, source_target_pairs={{0,2},{1,3},{2,0},{3,1},{4,6},{5,7},{6,4},{7,5},{8,10},{9,11},{10,... | collective-permute-start | bytes 3145736 | tf_op jit(solution)/shard_map/ppermute | solution.py:408
  233.0 24.7 %collective-permute-start.36 = (bf16[1024,256]{1,0:T(8,128)(2,1)S(1)}, bf16[1024,256]{1,0:T(8,128)(2,1)S(1)}, u32[]{:S(2)}, u32[]{:S(2)}) collective-permute-start(bf16[1024,256]{1,0:T(8,128)(2,1)S(1)} %slice.300), channel_id=1, source_target_pairs={{0,2},{1,3},{2,0},{3,1},{4,6},{5,7},{6,4},{7,5},{8,10},{9,11},{10,... | collective-permute-start | bytes 1572872 | tf_op jit(solution)/shard_map/ppermute | solution.py:408
  236.1 29.3 %collective-permute-start.37 = (bf16[1024,256]{1,0:T(8,128)(2,1)S(1)}, bf16[1024,256]{1,0:T(8,128)(2,1)S(1)}, u32[]{:S(2)}, u32[]{:S(2)}) collective-permute-start(bf16[1024,256]{1,0:T(8,128)(2,1)S(1)} %slice.301), channel_id=1, source_target_pairs={{0,4},{1,5},{2,6},{3,7},{4,0},{5,1},{6,2},{7,3},{8,12},{9,13},{10,... | collective-permute-start | bytes 1572872 | tf_op jit(solution)/shard_map/ppermute | solution.py:408
  237.6 28.4 %collective-permute-start.50 = (bf16[256,1024]{1,0:T(8,128)(2,1)S(1)}, bf16[256,1024]{1,0:T(8,128)(2,1)S(1)}, u32[]{:S(2)}, u32[]{:S(2)}) collective-permute-start(bf16[256,1024]{1,0:T(8,128)(2,1)S(1)} %collective-permute-done.46.g_own.refs_2_), channel_id=1, source_target_pairs={{0,8},{8,0},{16,24},{24,16},{1,9},{9,1},{17,25},{25,17},{2,10},{10... | collective-permute-start | bytes 1572872 | tf_op jit(solution)/shard_map/ppermute | solution.py:422
  257.7 26.4 %collective-permute-start.44 = (bf16[256,1024]{1,0:T(8,128)(2,1)}, bf16[256,1024]{1,0:T(8,128)(2,1)}, u32[]{:S(2)}, u32[]{:S(2)}) collective-permute-start(bf16[256,1024]{1,0:T(8,128)(2,1)} %convert_element_type.334.m_own.refs_0_), channel_id=1, source_target_pairs={{0,16},{8,24},{16,0},{24,8},{1,17},{9,25},{17,1},{25,9},{2,18},{10... | collective-permute-start | bytes 1572872 | tf_op jit(solution)/shard_map/ppermute | solution.py:422
  259.0 25.3 %collective-permute-start.38 = (bf16[1024,256]{1,0:T(8,128)(2,1)}, bf16[1024,256]{1,0:T(8,128)(2,1)}, u32[]{:S(2)}, u32[]{:S(2)}) collective-permute-start(bf16[1024,256]{1,0:T(8,128)(2,1)} %slice.302), channel_id=1, source_target_pairs={{0,2},{1,3},{2,0},{3,1},{4,6},{5,7},{6,4},{7,5},{8,10},{9,11},{10,... | collective-permute-start | bytes 1572872 | tf_op jit(solution)/shard_map/ppermute | solution.py:408
  266.0 26.3 %collective-permute-start.40 = (bf16[256,1024]{1,0:T(8,128)(2,1)}, bf16[256,1024]{1,0:T(8,128)(2,1)}, u32[]{:S(2)}, u32[]{:S(2)}) collective-permute-start(bf16[256,1024]{1,0:T(8,128)(2,1)} %convert_element_type.334.m_own.refs_0_), channel_id=1, source_target_pairs={{0,8},{8,0},{16,24},{24,16},{1,9},{9,1},{17,25},{25,17},{2,10},{10... | collective-permute-start | bytes 1572872 | tf_op jit(solution)/shard_map/ppermute | solution.py:422
  266.9 25.4 %collective-permute-start.27 = (bf16[256,1024]{1,0:T(8,128)(2,1)}, bf16[256,1024]{1,0:T(8,128)(2,1)}, u32[]{:S(2)}, u32[]{:S(2)}) collective-permute-start(bf16[256,1024]{1,0:T(8,128)(2,1)} %convert_element_type.334.m_own.refs_0_), channel_id=1, source_target_pairs={{0,1},{1,0},{2,3},{3,2},{4,5},{5,4},{6,7},{7,6},{8,9},{9,8},{10,11... | collective-permute-start | bytes 1572872 | tf_op jit(solution)/shard_map/ppermute | solution.py:405
  286.3 48.3 %collective-permute-start.43 = (bf16[256,1024]{1,0:T(8,128)(2,1)}, bf16[256,1024]{1,0:T(8,128)(2,1)}, u32[]{:S(2)}, u32[]{:S(2)}) collective-permute-start(bf16[256,1024]{1,0:T(8,128)(2,1)} %copy-done.22), channel_id=1, source_target_pairs={{0,1},{1,0},{2,3},{3,2},{4,5},{5,4},{6,7},{7,6},{8,9},{9,8},{10,11... | collective-permute-start | bytes 1572872 | tf_op jit(solution)/shard_map/ppermute | solution.py:405
  286.8 59.7 %collective-permute-start.51 = (bf16[256,1024]{1,0:T(8,128)(2,1)}, bf16[256,1024]{1,0:T(8,128)(2,1)}, u32[]{:S(2)}, u32[]{:S(2)}) collective-permute-start(bf16[256,1024]{1,0:T(8,128)(2,1)} %copy-done.27), channel_id=1, source_target_pairs={{0,1},{1,0},{2,3},{3,2},{4,5},{5,4},{6,7},{7,6},{8,9},{9,8},{10,11... | collective-permute-start | bytes 1572872 | tf_op jit(solution)/shard_map/ppermute | solution.py:405
  292.3 30.1 %collective-permute-start.45 = (bf16[256,1024]{1,0:T(8,128)(2,1)}, bf16[256,1024]{1,0:T(8,128)(2,1)}, u32[]{:S(2)}, u32[]{:S(2)}) collective-permute-start(bf16[256,1024]{1,0:T(8,128)(2,1)} %collective-permute-done.44.m_own.refs_2_), channel_id=1, source_target_pairs={{0,1},{1,0},{2,3},{3,2},{4,5},{5,4},{6,7},{7,6},{8,9},{9,8},{10,11... | collective-permute-start | bytes 1572872 | tf_op jit(solution)/shard_map/ppermute | solution.py:405
  292.3 42.3 %collective-permute-start.41 = (bf16[256,1024]{1,0:T(8,128)(2,1)}, bf16[256,1024]{1,0:T(8,128)(2,1)}, u32[]{:S(2)}, u32[]{:S(2)}) collective-permute-start(bf16[256,1024]{1,0:T(8,128)(2,1)} %collective-permute-done.40.m_own.refs_1_), channel_id=1, source_target_pairs={{0,1},{1,0},{2,3},{3,2},{4,5},{5,4},{6,7},{7,6},{8,9},{9,8},{10,11... | collective-permute-start | bytes 1572872 | tf_op jit(solution)/shard_map/ppermute | solution.py:405
  301.1 45.4 %collective-permute-start.49 = (bf16[256,1024]{1,0:T(8,128)(2,1)}, bf16[256,1024]{1,0:T(8,128)(2,1)}, u32[]{:S(2)}, u32[]{:S(2)}) collective-permute-start(bf16[256,1024]{1,0:T(8,128)(2,1)} %collective-permute-done.48.m_own.refs_3_), channel_id=1, source_target_pairs={{0,1},{1,0},{2,3},{3,2},{4,5},{5,4},{6,7},{7,6},{8,9},{9,8},{10,11... | collective-permute-start | bytes 1572872 | tf_op jit(solution)/shard_map/ppermute | solution.py:405
  334.1 84.1 %collective-permute-start.63 = (bf16[256,1024]{1,0:T(8,128)(2,1)}, bf16[256,1024]{1,0:T(8,128)(2,1)}, u32[]{:S(2)}, u32[]{:S(2)}) collective-permute-start(bf16[256,1024]{1,0:T(8,128)(2,1)} %get-tuple-element.90), channel_id=1, source_target_pairs={{0,1},{1,0},{2,3},{3,2},{4,5},{5,4},{6,7},{7,6},{8,9},{9,8},{10,11... | collective-permute-start | bytes 1572872 | tf_op jit(solution)/shard_map/ppermute | solution.py:405
  346.4 41.3 %collective-permute-start.61 = (bf16[256,1024]{1,0:T(8,128)(2,1)}, bf16[256,1024]{1,0:T(8,128)(2,1)}, u32[]{:S(2)}, u32[]{:S(2)}) collective-permute-start(bf16[256,1024]{1,0:T(8,128)(2,1)} %get-tuple-element.88), channel_id=1, source_target_pairs={{0,1},{1,0},{2,3},{3,2},{4,5},{5,4},{6,7},{7,6},{8,9},{9,8},{10,11... | collective-permute-start | bytes 1572872 | tf_op jit(solution)/shard_map/ppermute | solution.py:405
  359.2 45.1 %collective-permute-start.64 = (bf16[256,1024]{1,0:T(8,128)(2,1)}, bf16[256,1024]{1,0:T(8,128)(2,1)}, u32[]{:S(2)}, u32[]{:S(2)}) collective-permute-start(bf16[256,1024]{1,0:T(8,128)(2,1)} %get-tuple-element.81), channel_id=1, source_target_pairs={{0,1},{1,0},{2,3},{3,2},{4,5},{5,4},{6,7},{7,6},{8,9},{9,8},{10,11... | collective-permute-start | bytes 1572872 | tf_op jit(solution)/shard_map/ppermute | solution.py:405
  368.5 32.2 %collective-permute-start.95 = (bf16[1024,256]{1,0:T(8,128)(2,1)}, bf16[1024,256]{1,0:T(8,128)(2,1)}, u32[]{:S(2)}, u32[]{:S(2)}) collective-permute-start(bf16[1024,256]{1,0:T(8,128)(2,1)} %get-tuple-element.162), channel_id=1, source_target_pairs={{0,2},{1,3},{2,0},{3,1},{4,6},{5,7},{6,4},{7,5},{8,10},{9,11},{10,... | collective-permute-start | bytes 1572872 | tf_op jit(solution)/shard_map/ppermute | solution.py:408
  369.9 32.9 %collective-permute-start.93 = (bf16[1024,256]{1,0:T(8,128)(2,1)}, bf16[1024,256]{1,0:T(8,128)(2,1)S(1)}, u32[]{:S(2)}, u32[]{:S(2)}) collective-permute-start(bf16[1024,256]{1,0:T(8,128)(2,1)} %get-tuple-element.161), channel_id=1, source_target_pairs={{0,4},{1,5},{2,6},{3,7},{4,0},{5,1},{6,2},{7,3},{8,12},{9,13},{10,... | collective-permute-start | bytes 1572872 | tf_op jit(solution)/shard_map/ppermute | solution.py:408
  415.8 33.7 %collective-permute-start.96 = (bf16[2048,256]{1,0:T(8,128)(2,1)S(1)}, bf16[2048,256]{1,0:T(8,128)(2,1)S(1)}, u32[]{:S(2)}, u32[]{:S(2)}) collective-permute-start(bf16[2048,256]{1,0:T(8,128)(2,1)S(1)} %add_convert_fusion.4), channel_id=1, source_target_pairs={{0,4},{1,5},{2,6},{3,7},{4,0},{5,1},{6,2},{7,3},{8,12},{9,13},{10,... | collective-permute-start | bytes 3145736 | tf_op jit(solution)/shard_map/ppermute | solution.py:408
  416.7 32.8 %collective-permute-start.94 = (bf16[2048,256]{1,0:T(8,128)(2,1)S(1)}, bf16[2048,256]{1,0:T(8,128)(2,1)S(1)}, u32[]{:S(2)}, u32[]{:S(2)}) collective-permute-start(bf16[2048,256]{1,0:T(8,128)(2,1)S(1)} %add_convert_fusion.5), channel_id=1, source_target_pairs={{0,2},{1,3},{2,0},{3,1},{4,6},{5,7},{6,4},{7,5},{8,10},{9,11},{10,... | collective-permute-start | bytes 3145736 | tf_op jit(solution)/shard_map/ppermute | solution.py:408
  418.2 52.0 %collective-permute-start.89 = (bf16[2048,256]{1,0:T(8,128)(2,1)S(1)}, bf16[2048,256]{1,0:T(8,128)(2,1)S(1)}, u32[]{:S(2)}, u32[]{:S(2)}) collective-permute-start(bf16[2048,256]{1,0:T(8,128)(2,1)S(1)} %add_convert_fusion.7), channel_id=1, source_target_pairs={{0,4},{1,5},{2,6},{3,7},{4,0},{5,1},{6,2},{7,3},{8,12},{9,13},{10,... | collective-permute-start | bytes 3145736 | tf_op jit(solution)/shard_map/ppermute | solution.py:408
  427.0 44.6 %collective-permute-start.87 = (bf16[2048,256]{1,0:T(8,128)(2,1)S(1)}, bf16[2048,256]{1,0:T(8,128)(2,1)S(1)}, u32[]{:S(2)}, u32[]{:S(2)}) collective-permute-start(bf16[2048,256]{1,0:T(8,128)(2,1)S(1)} %add_convert_fusion.8), channel_id=1, source_target_pairs={{0,2},{1,3},{2,0},{3,1},{4,6},{5,7},{6,4},{7,5},{8,10},{9,11},{10,... | collective-permute-start | bytes 3145736 | tf_op jit(solution)/shard_map/ppermute | solution.py:408
  428.7 122.2 %collective-permute-start.60 = (bf16[256,1024]{1,0:T(8,128)(2,1)S(1)}, bf16[256,1024]{1,0:T(8,128)(2,1)S(1)}, u32[]{:S(2)}, u32[]{:S(2)}) collective-permute-start(bf16[256,1024]{1,0:T(8,128)(2,1)S(1)} %copy-done.53), channel_id=1, source_target_pairs={{0,1},{1,0},{2,3},{3,2},{4,5},{5,4},{6,7},{7,6},{8,9},{9,8},{10,11... | collective-permute-start | bytes 1572872 | tf_op jit(solution)/shard_map/ppermute | solution.py:405
  449.5 103.3 %collective-permute-start.62 = (bf16[256,1024]{1,0:T(8,128)(2,1)S(1)}, bf16[256,1024]{1,0:T(8,128)(2,1)S(1)}, u32[]{:S(2)}, u32[]{:S(2)}) collective-permute-start(bf16[256,1024]{1,0:T(8,128)(2,1)S(1)} %copy-done.75), channel_id=1, source_target_pairs={{0,8},{8,0},{16,24},{24,16},{1,9},{9,1},{17,25},{25,17},{2,10},{10... | collective-permute-start | bytes 1572872 | tf_op jit(solution)/shard_map/ppermute | solution.py:422
  449.5 47.5 %collective-permute-start.52 = (bf16[1024,1024]{1,0:T(8,128)(2,1)S(1)}, bf16[1024,1024]{1,0:T(8,128)(2,1)S(1)}, u32[]{:S(2)}, u32[]{:S(2)}) collective-permute-start(bf16[1024,1024]{1,0:T(8,128)(2,1)S(1)} %copy-done.88), channel_id=1, source_target_pairs={{0,1},{1,0},{2,3},{3,2},{4,5},{5,4},{6,7},{7,6},{8,9},{9,8},{10,11... | collective-permute-start | bytes 6291464 | tf_op jit(solution)/shard_map/ppermute | solution.py:405
  500.0 28.3 %collective-permute-start.54 = (bf16[256,1024]{1,0:T(8,128)(2,1)S(1)}, bf16[256,1024]{1,0:T(8,128)(2,1)S(1)}, u32[]{:S(2)}, u32[]{:S(2)}) collective-permute-start(bf16[256,1024]{1,0:T(8,128)(2,1)S(1)} %get-tuple-element.140), channel_id=1, source_target_pairs={{0,8},{8,0},{16,24},{24,16},{1,9},{9,1},{17,25},{25,17},{2,10},{10... | collective-permute-start | bytes 1572872 | tf_op jit(solution)/shard_map/ppermute | solution.py:422
  509.8 23.9 %collective-permute-start.90 = (bf16[512,256]{1,0:T(8,128)(2,1)S(1)}, bf16[512,256]{1,0:T(8,128)(2,1)S(1)}, u32[]{:S(2)}, u32[]{:S(2)}) collective-permute-start(bf16[512,256]{1,0:T(8,128)(2,1)S(1)} %get-tuple-element.165), channel_id=1, source_target_pairs={{0,8},{8,0},{16,24},{24,16},{1,9},{9,1},{17,25},{25,17},{2,10},{10... | collective-permute-start | bytes 786440 | tf_op jit(solution)/shard_map/ppermute | solution.py:422
  528.4 53.3 %collective-permute-start.66 = (bf16[256,1024]{1,0:T(8,128)(2,1)S(1)}, bf16[256,1024]{1,0:T(8,128)(2,1)S(1)}, u32[]{:S(2)}, u32[]{:S(2)}) collective-permute-start(bf16[256,1024]{1,0:T(8,128)(2,1)S(1)} %add_convert_fusion.10), channel_id=1, source_target_pairs={{0,16},{8,24},{16,0},{24,8},{1,17},{9,25},{17,1},{25,9},{2,18},{10... | collective-permute-start | bytes 1572872 | tf_op jit(solution)/shard_map/ppermute | solution.py:422
  533.7 48.0 %collective-permute-start.53 = (bf16[256,1024]{1,0:T(8,128)(2,1)S(1)}, bf16[256,1024]{1,0:T(8,128)(2,1)S(1)}, u32[]{:S(2)}, u32[]{:S(2)}) collective-permute-start(bf16[256,1024]{1,0:T(8,128)(2,1)S(1)} %get-tuple-element.139), channel_id=1, source_target_pairs={{0,8},{8,0},{16,24},{24,16},{1,9},{9,1},{17,25},{25,17},{2,10},{10... | collective-permute-start | bytes 1572872 | tf_op jit(solution)/shard_map/ppermute | solution.py:422
  550.9 44.6 %collective-permute-start.55 = (bf16[256,1024]{1,0:T(8,128)(2,1)S(1)}, bf16[256,1024]{1,0:T(8,128)(2,1)S(1)}, u32[]{:S(2)}, u32[]{:S(2)}) collective-permute-start(bf16[256,1024]{1,0:T(8,128)(2,1)S(1)} %fusion.11), channel_id=1, source_target_pairs={{0,16},{8,24},{16,0},{24,8},{1,17},{9,25},{17,1},{25,9},{2,18},{10... | collective-permute-start | bytes 1572872 | tf_op jit(solution)/shard_map/ppermute | solution.py:422
  551.0 45.2 %collective-permute-start.92 = (bf16[512,256]{1,0:T(8,128)(2,1)S(1)}, bf16[512,256]{1,0:T(8,128)(2,1)S(1)}, u32[]{:S(2)}, u32[]{:S(2)}) collective-permute-start(bf16[512,256]{1,0:T(8,128)(2,1)S(1)} %get-tuple-element.163), channel_id=1, source_target_pairs={{0,24},{8,16},{16,8},{24,0},{1,25},{9,17},{17,9},{25,1},{2,26},{10... | collective-permute-start | bytes 786440 | tf_op jit(solution)/shard_map/ppermute | solution.py:422
  552.8 78.3 %collective-permute-start.104 = (bf16[512,256]{1,0:T(8,128)(2,1)S(1)}, bf16[512,256]{1,0:T(8,128)(2,1)S(1)}, u32[]{:S(2)}, u32[]{:S(2)}) collective-permute-start(bf16[512,256]{1,0:T(8,128)(2,1)S(1)} %get-tuple-element.151), channel_id=1, source_target_pairs={{0,8},{8,0},{16,24},{24,16},{1,9},{9,1},{17,25},{25,17},{2,10},{10... | collective-permute-start | bytes 786440 | tf_op jit(solution)/shard_map/ppermute | solution.py:422
  581.7 49.7 %collective-permute-start.105 = (bf16[512,256]{1,0:T(8,128)(2,1)S(1)}, bf16[512,256]{1,0:T(8,128)(2,1)S(1)}, u32[]{:S(2)}, u32[]{:S(2)}) collective-permute-start(bf16[512,256]{1,0:T(8,128)(2,1)S(1)} %get-tuple-element.150), channel_id=1, source_target_pairs={{0,16},{8,24},{16,0},{24,8},{1,17},{9,25},{17,1},{25,9},{2,18},{10... | collective-permute-start | bytes 786440 | tf_op jit(solution)/shard_map/ppermute | solution.py:422
  601.3 24.0 %collective-permute-start.69 = (bf16[256,1024]{1,0:T(8,128)(2,1)S(1)}, bf16[256,1024]{1,0:T(8,128)(2,1)S(1)}, u32[]{:S(2)}, u32[]{:S(2)}) collective-permute-start(bf16[256,1024]{1,0:T(8,128)(2,1)S(1)} %get-tuple-element.122), channel_id=1, source_target_pairs={{0,4},{1,5},{2,6},{3,7},{4,0},{5,1},{6,2},{7,3},{8,12},{9,13},{10,... | collective-permute-start | bytes 1572872 | tf_op jit(solution)/shard_map/ppermute | solution.py:408
  602.6 24.5 %collective-permute-start.70 = (bf16[256,1024]{1,0:T(8,128)(2,1)S(1)}, bf16[256,1024]{1,0:T(8,128)(2,1)S(1)}, u32[]{:S(2)}, u32[]{:S(2)}) collective-permute-start(bf16[256,1024]{1,0:T(8,128)(2,1)S(1)} %get-tuple-element.122), channel_id=1, source_target_pairs={{0,6},{1,7},{2,4},{3,5},{4,2},{5,3},{6,0},{7,1},{8,14},{9,15},{10,... | collective-permute-start | bytes 1572872 | tf_op jit(solution)/shard_map/ppermute | solution.py:408
  639.8 40.0 %collective-permute-start.57 = (bf16[256,256]{1,0:T(8,128)(2,1)}, bf16[256,256]{1,0:T(8,128)(2,1)S(1)}, u32[]{:S(2)}, u32[]{:S(2)}) collective-permute-start(bf16[256,256]{1,0:T(8,128)(2,1)} %get-tuple-element.201), channel_id=1, source_target_pairs={{0,4},{1,5},{2,6},{3,7},{4,0},{5,1},{6,2},{7,3},{8,12},{9,13},{10,... | collective-permute-start | bytes 393224 | tf_op jit(solution)/shard_map/ppermute | solution.py:408
  640.6 55.9 %collective-permute-start.58 = (bf16[256,256]{1,0:T(8,128)(2,1)S(1)}, bf16[256,256]{1,0:T(8,128)(2,1)S(1)}, u32[]{:S(2)}, u32[]{:S(2)}) collective-permute-start(bf16[256,256]{1,0:T(8,128)(2,1)S(1)} %get-tuple-element.200), channel_id=1, source_target_pairs={{0,6},{1,7},{2,4},{3,5},{4,2},{5,3},{6,0},{7,1},{8,14},{9,15},{10,... | collective-permute-start | bytes 393224 | tf_op jit(solution)/shard_map/ppermute | solution.py:408
  667.3 59.6 %collective-permute-start.72 = (bf16[1024,1024]{1,0:T(8,128)(2,1)}, bf16[1024,1024]{1,0:T(8,128)(2,1)}, u32[]{:S(2)}, u32[]{:S(2)}) collective-permute-start(bf16[1024,1024]{1,0:T(8,128)(2,1)} %get-tuple-element.98), channel_id=1, source_target_pairs={{0,1},{1,0},{2,3},{3,2},{4,5},{5,4},{6,7},{7,6},{8,9},{9,8},{10,11... | collective-permute-start | bytes 6291464 | tf_op jit(solution)/shard_map/ppermute | solution.py:405
  691.4 35.2 %collective-permute-start.81 = (bf16[512,768]{1,0:T(8,128)(2,1)S(1)}, bf16[512,768]{1,0:T(8,128)(2,1)S(1)}, u32[]{:S(2)}, u32[]{:S(2)}) collective-permute-start(bf16[512,768]{1,0:T(8,128)(2,1)S(1)} %get-tuple-element.131), channel_id=1, source_target_pairs={{0,8},{8,0},{16,24},{24,16},{1,9},{9,1},{17,25},{25,17},{2,10},{10... | collective-permute-start | bytes 2359304 | tf_op jit(solution)/shard_map/ppermute | solution.py:422
  696.5 25.5 %collective-permute-start.83 = (bf16[512,256]{1,0:T(8,128)(2,1)S(1)}, bf16[512,256]{1,0:T(8,128)(2,1)S(1)}, u32[]{:S(2)}, u32[]{:S(2)}) collective-permute-start(bf16[512,256]{1,0:T(8,128)(2,1)S(1)} %get-tuple-element.170), channel_id=1, source_target_pairs={{0,8},{8,0},{16,24},{24,16},{1,9},{9,1},{17,25},{25,17},{2,10},{10... | collective-permute-start | bytes 786440 | tf_op jit(solution)/shard_map/ppermute | solution.py:422
  717.7 37.1 %collective-permute-start.80 = (bf16[512,768]{1,0:T(8,128)(2,1)S(1)}, bf16[512,768]{1,0:T(8,128)(2,1)S(1)}, u32[]{:S(2)}, u32[]{:S(2)}) collective-permute-start(bf16[512,768]{1,0:T(8,128)(2,1)S(1)} %get-tuple-element.130), channel_id=1, source_target_pairs={{0,8},{8,0},{16,24},{24,16},{1,9},{9,1},{17,25},{25,17},{2,10},{10... | collective-permute-start | bytes 2359304 | tf_op jit(solution)/shard_map/ppermute | solution.py:422
  726.8 33.4 %collective-permute-start.82 = (bf16[512,768]{1,0:T(8,128)(2,1)S(1)}, bf16[512,768]{1,0:T(8,128)(2,1)S(1)}, u32[]{:S(2)}, u32[]{:S(2)}) collective-permute-start(bf16[512,768]{1,0:T(8,128)(2,1)S(1)} %add_convert_fusion.9), channel_id=1, source_target_pairs={{0,16},{8,24},{16,0},{24,8},{1,17},{9,25},{17,1},{25,9},{2,18},{10... | collective-permute-start | bytes 2359304 | tf_op jit(solution)/shard_map/ppermute | solution.py:422
  729.6 30.9 %collective-permute-start.75 = (bf16[256,1024]{1,0:T(8,128)(2,1)S(1)}, bf16[256,1024]{1,0:T(8,128)(2,1)S(1)}, u32[]{:S(2)}, u32[]{:S(2)}) collective-permute-start(bf16[256,1024]{1,0:T(8,128)(2,1)S(1)} %get-tuple-element.137), channel_id=1, source_target_pairs={{0,6},{1,7},{2,4},{3,5},{4,2},{5,3},{6,0},{7,1},{8,14},{9,15},{10,... | collective-permute-start | bytes 1572872 | tf_op jit(solution)/shard_map/ppermute | solution.py:408
  731.6 28.9 %collective-permute-start.74 = (bf16[256,1024]{1,0:T(8,128)(2,1)S(1)}, bf16[256,1024]{1,0:T(8,128)(2,1)S(1)}, u32[]{:S(2)}, u32[]{:S(2)}) collective-permute-start(bf16[256,1024]{1,0:T(8,128)(2,1)S(1)} %get-tuple-element.138), channel_id=1, source_target_pairs={{0,4},{1,5},{2,6},{3,7},{4,0},{5,1},{6,2},{7,3},{8,12},{9,13},{10,... | collective-permute-start | bytes 1572872 | tf_op jit(solution)/shard_map/ppermute | solution.py:408
  731.8 28.6 %collective-permute-start.73 = (bf16[256,1024]{1,0:T(8,128)(2,1)S(1)}, bf16[256,1024]{1,0:T(8,128)(2,1)S(1)}, u32[]{:S(2)}, u32[]{:S(2)}) collective-permute-start(bf16[256,1024]{1,0:T(8,128)(2,1)S(1)} %get-tuple-element.136), channel_id=1, source_target_pairs={{0,2},{1,3},{2,0},{3,1},{4,6},{5,7},{6,4},{7,5},{8,10},{9,11},{10,... | collective-permute-start | bytes 1572872 | tf_op jit(solution)/shard_map/ppermute | solution.py:408
  (141 other events, 1974.4 us)

commit v3 on v2

--- a/solution.py
+++ b/solution.py
@@ -127,16 +127,25 @@
     )(*lefts, *weights)
 
 
-def units_kernel(feat, count, m_own, m_other, g_own, g_other, *refs):
+def units_kernel(feat, parts, count, *refs):
+    m_owns, m_others, g_owns, g_others = (refs[i * parts : (i + 1) * parts] for i in range(4))
+    refs = refs[4 * parts :]
     sources = refs[: 3 * count]
-    hidden_ref, gate_ref, up_ref, own_ref, other_ref, held, arrived = refs[3 * count :]
+    refs = refs[3 * count :]
+    hidden_ref, gate_ref, up_ref = refs[:3]
+    own_refs, other_refs = refs[3 : 3 + parts], refs[3 + parts : 3 + 2 * parts]
+    held, arrived = refs[3 + 2 * parts :]
     copies = [
         pltpu.make_async_copy(source, held.at[at], arrived.at[at]) for at, source in enumerate(sources)
     ]
     for copy in copies:
         copy.start()
-    middle = weave(m_own[...], m_other[...], feat)
-    grad = weave(g_own[...], g_other[...], feat)
+
+    def together(owns, others):
+        return jnp.concatenate([weave(a[...], b[...], feat) for a, b in zip(owns, others)], axis=0)
+
+    middle = together(m_owns, m_others)
+    grad = together(g_owns, g_others)
     scale = norm_scale(middle)
     part = hidden_ref.shape[1] // count
     pairs = []
@@ -156,40 +165,46 @@
         pairs.append((up_grad.astype(BF16), held.at[3 * i + 1]))
         gate_ref[:, columns] = (gate_grad * scale).astype(BF16)
         up_ref[:, columns] = (up_grad * scale).astype(BF16)
-    for at in range(0, own_ref.shape[1], feat):
+    tokens = own_refs[0].shape[0]
+    for at in range(0, own_refs[0].shape[1], feat):
         rows = slice(2 * at, 2 * (at + feat))
         total = None
         for left, weight in pairs:
             term = nt(left, weight[rows, :])
             total = term if total is None else total + term
-        own_ref[:, at : at + feat] = total[:, :feat]
-        other_ref[:, at : at + feat] = total[:, feat:].astype(BF16)
-
-
-def units(feat, m_own, m_other, g_own, g_other, gates, ups, downs):
-    tokens, half = m_own.shape
+        for i, (own_ref, other_ref) in enumerate(zip(own_refs, other_refs)):
+            mine = total[i * tokens : (i + 1) * tokens]
+            own_ref[:, at : at + feat] = mine[:, :feat]
+            other_ref[:, at : at + feat] = mine[:, feat:].astype(BF16)
+
+
+def units(feat, m_owns, m_others, g_owns, g_others, gates, ups, downs):
+    parts = len(m_owns)
+    tokens, half = m_owns[0].shape
     count, part = len(gates), gates[0].shape[1]
-    hidden = jax.ShapeDtypeStruct((tokens, count * part), BF16)
+    hidden = jax.ShapeDtypeStruct((parts * tokens, count * part), BF16)
     weights = [w for three in zip(gates, ups, downs) for w in three]
-    return pl.pallas_call(
-        functools.partial(units_kernel, feat, count),
-        in_specs=[pl.BlockSpec(memory_space=pltpu.VMEM)] * 4
+    result = pl.pallas_call(
+        functools.partial(units_kernel, feat, parts, count),
+        in_specs=[pl.BlockSpec(memory_space=pltpu.VMEM)] * (4 * parts)
         + [pl.BlockSpec(memory_space=pl.ANY)] * len(weights),
-        out_specs=[pl.BlockSpec(memory_space=pltpu.VMEM)] * 5,
+        out_specs=[pl.BlockSpec(memory_space=pltpu.VMEM)] * (3 + 2 * parts),
         out_shape=[hidden] * 3
-        + [jax.ShapeDtypeStruct((tokens, half), F32), jax.ShapeDtypeStruct((tokens, half), BF16)],
+        + [jax.ShapeDtypeStruct((tokens, half), F32)] * parts
+        + [jax.ShapeDtypeStruct((tokens, half), BF16)] * parts,
         scratch_shapes=[
             pltpu.VMEM((len(weights),) + weights[0].shape, BF16),
             pltpu.SemaphoreType.DMA((len(weights),)),
         ],
-        compiler_params=pltpu.CompilerParams(vmem_limit_bytes=40 * 1024 * 1024),
+        compiler_params=pltpu.CompilerParams(vmem_limit_bytes=48 * 1024 * 1024),
         name="units",
-    )(m_own, m_other, g_own, g_other, *weights)
+    )(*m_owns, *m_others, *g_owns, *g_others, *weights)
+    return result[0], result[1], result[2], result[3 : 3 + parts], result[3 + parts :]
 
 
 def outer_kernel(groups, count, *refs):
-    owns, others, rights = refs[:groups], refs[groups : 2 * groups], refs[2 * groups : 3 * groups]
-    outs = refs[3 * groups : 3 * groups + count]
+    owns, others, rights = refs[:groups], refs[groups : 2 * groups], refs[2 * groups : len(refs) - count]
+    outs = refs[len(refs) - count :]
     left = jnp.concatenate(
         [jnp.concatenate([own[...], other[...]], axis=1) for own, other in zip(owns, others)], axis=0
     )
@@ -469,13 +484,20 @@
     def spread(a):
         return [a] + [plane_swap(a, step) for step in range(1, places)]
 
+    groups = [[2 * i + k for i in range(places)] for k in range(2)]
+
+    def plane_exchange(a):
+        return lax.all_to_all(
+            a, "col", split_axis=0, concat_axis=0, axis_index_groups=groups, tiled=True
+        )
+
     def to_parts(a):
-        return put_feats(
-            [token_part(a, 0)] + [plane_swap(token_part(a, s), s) for s in range(1, places)]
-        )
+        a = plane_exchange(a.reshape(places, quarter, feat))
+        return jnp.concatenate([a[s] for s in range(places)], axis=1)
 
     def to_home(a):
-        return put_rows([feat_part(a, 0)] + [plane_swap(feat_part(a, s), s) for s in range(1, places)])
+        a = jnp.stack([a[:, s * feat : (s + 1) * feat] for s in range(places)])
+        return plane_exchange(a).reshape(tokens, feat)
 
     def sum_cols(a):
         step = 1
@@ -492,8 +514,8 @@
 
     def exchange(w):
         part = w.shape[1] // rows
-        pieces = [lax.dynamic_slice_in_dim(w, (row ^ s) * part, part, 1) for s in range(rows)]
-        return join_rows([row_swap(piece, s) if s else piece for s, piece in enumerate(pieces)])
+        pieces = jnp.stack([w[:, s * part : (s + 1) * part] for s in range(rows)])
+        return lax.all_to_all(pieces, "row", split_axis=0, concat_axis=0, tiled=True).reshape(width, part)
 
     def spread_weights(whole):
         if places != 4:
@@ -523,37 +545,47 @@
                 + plane_swap(to_first.astype(BF16), 1).astype(F32)
                 + plane_swap(to_second.astype(BF16), 2).astype(F32)
             )
-        total = total.astype(BF16)
-        pieces = [row_part(total, s) for s in range(rows)]
-        pieces = [own_first(row_swap(piece, s) if s else piece).astype(F32) for s, piece in enumerate(pieces)]
-        return join_rows(pieces, 1, F32)
+        total = total.astype(BF16).reshape(rows, 2 * feat, pieces[0].shape[1])
+        total = lax.all_to_all(total, "row", split_axis=0, concat_axis=0, tiled=True).astype(F32)
+        return jnp.concatenate([own_first(total[s]) for s in range(rows)], axis=1)
 
     def give_rows(w):
-        return own_first(reduce_row([row_part(w, s) for s in range(rows)]))
-
-    qkv_list = gather_row(
-        jnp.concatenate(
-            [scaled(w, gain_one) for w in (query_weight, key_weight, value_weight)], axis=1
+        return own_first(lax.psum_scatter(w, "row", scatter_dimension=0, tiled=True)).astype(F32)
+
+    with jax.named_scope("gather_qkv"):
+        qkv_full = lax.all_gather(
+            jnp.concatenate(
+                [scaled(w, gain_one) for w in (query_weight, key_weight, value_weight)], axis=1
+            ),
+            "row",
+            axis=0,
+            tiled=True,
         )
-    )
-    gate_whole = exchange(scaled(gate_weight, gain_two))
-    up_whole = exchange(after(scaled(up_weight, gain_two), gate_whole, *qkv_list[1:3]))
-    out_list = gather_row(after(own_first(out_weight), *qkv_list))
-    down_whole = exchange(after(own_first(down_weight), up_whole, *qkv_list))
-    g_part = to_parts(out_grad)
-    g_list = gather_row(after(g_part, down_whole))
-    gates, ups, downs = (spread_weights(w) for w in (gate_whole, up_whole, down_whole))
-    qkv_full = join_rows(qkv_list)
-    out_full = join_rows(out_list)
-
-    x_own = put_feats(spread(inputs))
-    x_other = core_swap(x_own)
+        out_full = lax.all_gather(own_first(out_weight), "row", axis=0, tiled=True)
+    with jax.named_scope("gate_row"):
+        gate_whole = exchange(scaled(gate_weight, gain_two))
+    with jax.named_scope("up_row"):
+        up_whole = exchange(after(scaled(up_weight, gain_two), gate_whole))
+    with jax.named_scope("down_row"):
+        down_whole = exchange(after(own_first(down_weight), up_whole))
+    with jax.named_scope("grad_plane"):
+        g_part = to_parts(after(out_grad, down_whole))
+    with jax.named_scope("grad_row"):
+        g_list = gather_row(g_part)
+    with jax.named_scope("gate_plane"):
+        gates = spread_weights(gate_whole)
+    with jax.named_scope("up_plane"):
+        ups = spread_weights(up_whole)
+
+    with jax.named_scope("inputs"):
+        x_own = put_feats(spread(inputs))
+        x_other = core_swap(x_own)
     heads_width = query_weight.shape[1]
     cosine, front, back = rope_tables(positions, heads_width)
     start_row = jnp.sum(
         (segment_ids[None, :] < segment_ids[:, None]).astype(jnp.int32), axis=1
     )[None, :]
-    x_ready = after(x_own, gates[1], gates[2], g_part)
+    x_ready = after(x_own, gates[1], gates[2])
     query, key, value, scale_one = project(feat, x_ready, x_other, qkv_full, cosine, front, back)
     mixed, logs = attend(query, key, value, start_row)
     mixed = after(mixed, up_whole, gates[3])
@@ -566,32 +598,50 @@
             total = total + plane_swap(token_part(low, s), s).astype(F32)
         return total
 
-    middle = token_part(x_own, 0).astype(F32) + scatter_parts(*unfold(feat, "mix", (mixed, [out_full])))
+    with jax.named_scope("mix_plane"):
+        middle = token_part(x_own, 0).astype(F32) + scatter_parts(*unfold(feat, "mix", (mixed, [out_full])))
     square = jnp.sum(middle * middle, axis=1, keepdims=True)
     square = square + core_swap(square)
     scale_mid = lax.rsqrt(square / width + EPS)
 
-    m_list = gather_row(middle.astype(BF16))
-    m_others = [core_swap(m) for m in m_list]
-    g_others = [core_swap(g) for g in g_list]
-    found = [
-        units(feat, m, m_other, g, g_other, gates, ups, downs)
-        for m, m_other, g, g_other in zip(m_list, m_others, g_list, g_others)
-    ]
-    hidden = jnp.concatenate([f[0] for f in found], axis=0)
-    unit_grad = reduce_row([f[3] + core_swap(f[4]).astype(F32) for f in found])
-    feed_own, feed_other = unfold(feat, "feed", (after(hidden, found[-1][4]), downs))
-    feed_own = feed_own + core_swap(feed_other).astype(F32)
-    feed = reduce_row([feed_own[s * quarter : (s + 1) * quarter] for s in range(rows)])
-    block_out = to_home((middle + feed).astype(BF16))
+    with jax.named_scope("down_plane"):
+        downs = spread_weights(after(down_whole, middle))
+    with jax.named_scope("middle_row"):
+        m_list = gather_row(after(middle.astype(BF16), ups[1], ups[2]))
+        m_others = [core_swap(m) for m in m_list]
+    with jax.named_scope("grad_core"):
+        g_others = [core_swap(g) for g in g_list]
+    found, own_shares, other_shares = [], [], []
+    for at in range(0, rows, 2):
+        pick = slice(at, at + 2)
+        *three, owns, others = units(
+            feat, m_list[pick], m_others[pick], g_list[pick], g_others[pick], gates, ups, downs
+        )
+        found.append(three)
+        own_shares += owns
+        other_shares += others
+    with jax.named_scope("unit_grad"):
+        shares = [own + core_swap(other).astype(F32) for own, other in zip(own_shares, other_shares)]
+        last = shares[-1]
+        unit_grad = reduce_row(shares)
+    with jax.named_scope("feed"):
+        shares = []
+        for hidden, _, _ in found:
+            own, other = unfold(feat, "feed", (after(hidden, last), downs))
+            own = own + core_swap(other).astype(F32)
+            shares += [own[:quarter], own[quarter:]]
+        feed = reduce_row([after(a, unit_grad) for a in shares])
+    with jax.named_scope("block_out"):
+        block_out = to_home((middle + feed).astype(BF16))
 
     unit_mid = middle * scale_mid
     dot_two = jnp.sum(unit_grad * unit_mid, axis=1, keepdims=True)
     dot_two = dot_two + core_swap(dot_two)
     middle_grad = g_part.astype(F32) + scale_mid * (unit_grad - unit_mid * (dot_two / width))
 
-    d_own = put_rows(spread(middle_grad.astype(BF16)))
-    d_other = core_swap(d_own)
+    with jax.named_scope("middle_grad"):
+        d_own = put_rows(spread(middle_grad.astype(BF16)))
+        d_other = core_swap(d_own)
     mixed_grad = fold(feat, d_own, d_other, out_full)
     query_grad, key_grad, value_grad = attend_back(
         query, key, value, mixed, mixed_grad, start_row, logs, cosine, front, back
@@ -599,26 +649,38 @@
     grads = jnp.concatenate([query_grad, key_grad, value_grad], axis=1)
     grads_scaled = (grads.astype(F32) * scale_one).astype(BF16)
     qkv_part = outer(feat, "qkv_outer", [x_own], [x_other], [grads_scaled])[0]
-    qkv_grad = give_rows(qkv_part)
-    gain_dots = jnp.sum(qkv_part.astype(F32) * qkv_full.astype(F32), axis=1).reshape(rows, 2, feat)
-    gain_dots = sum_cols(jnp.where(core == 0, gain_dots, gain_dots[:, ::-1]).reshape(width))
-    gain_row = row_part(gain_dots, 0) + sum(row_swap(row_part(gain_dots, s), s) for s in range(1, rows))
-    first_gain_grad = gain_row / gain_one[:, 0]
-    first_unit_grad = scatter_parts(*unfold(feat, "first_grad", (grads, [qkv_full])))
+    with jax.named_scope("qkv_grad"):
+        qkv_grad = give_rows(qkv_part)
+    with jax.named_scope("first_gain"):
+        gain_dots = jnp.sum(qkv_part.astype(F32) * qkv_full.astype(F32), axis=1).reshape(rows, 2, feat)
+        gain_dots = sum_cols(jnp.where(core == 0, gain_dots, gain_dots[:, ::-1]).reshape(width))
+        gain_row = row_part(gain_dots, 0) + sum(
+            row_swap(row_part(gain_dots, s), s) for s in range(1, rows)
+        )
+        first_gain_grad = gain_row / gain_one[:, 0]
+    with jax.named_scope("first_plane"):
+        first_unit_grad = scatter_parts(*unfold(feat, "first_grad", (after(grads, qkv_part), [qkv_full])))
     scale_first = token_part(scale_one, 0)
     unit_first = token_part(x_own, 0).astype(F32) * scale_first
     dot_one = jnp.sum(first_unit_grad * unit_first, axis=1, keepdims=True)
     dot_one = dot_one + core_swap(dot_one)
-    input_grad = to_home(
-        (middle_grad + scale_first * (first_unit_grad - unit_first * (dot_one / width))).astype(BF16)
-    )
-
-    out_weight_grad = give_rows(outer(feat, "out_outer", [d_own], [d_other], [mixed])[0])
-    down_weight_grad = give_back(
-        outer(feat, "down_outer", g_list, g_others, [f[0] for f in found], places)
-    )
-    gate_unit = give_back(outer(feat, "gate_outer", m_list, m_others, [f[1] for f in found], places))
-    up_unit = give_back(outer(feat, "up_outer", m_list, m_others, [f[2] for f in found], places))
+    with jax.named_scope("input_grad"):
+        input_grad = to_home(
+            (middle_grad + scale_first * (first_unit_grad - unit_first * (dot_one / width))).astype(BF16)
+        )
+
+    with jax.named_scope("out_grad"):
+        out_weight_grad = give_rows(outer(feat, "out_outer", [d_own], [d_other], [mixed])[0])
+    with jax.named_scope("down_grad"):
+        down_weight_grad = give_back(
+            outer(feat, "down_outer", g_list, g_others, [after(f[0], last) for f in found], places)
+        )
+    with jax.named_scope("gate_grad"):
+        gate_parts = outer(feat, "gate_outer", m_list, m_others, [after(f[1], last) for f in found], places)
+        gate_unit = give_back([after(a, d_own) for a in gate_parts])
+    with jax.named_scope("up_grad"):
+        up_parts = outer(feat, "up_outer", m_list, m_others, [after(f[2], last) for f in found], places)
+        up_unit = give_back([after(a, d_own, mixed_grad) for a in up_parts])
     q_unit = qkv_grad[:, :heads_width]
     k_unit = qkv_grad[:, heads_width : 2 * heads_width]
     v_unit = qkv_grad[:, 2 * heads_width :]

time: 782 us -> 721 us (0.922)
  waiting for transfers between devices: 412 us -> 295 us
  other arithmetic: 45.4 us -> 89.6 us
  between operations: 2.83 us -> 15.9 us
  local copies, waits for them, and re-layouts: 79.3 us -> 67.7 us
  starting transfers between devices: 110 us -> 121 us
    ppermute x45 -> x15, waiting for transfers between devices: 243 us -> 121 us  [row_swap(): return lax.ppermute(a, 'row', [(i, i ^ step) for i in range(rows)])]
    ppermute x45 -> x36, waiting for transfers between devices: 159 us -> 78 us  [plane_swap(): return lax.ppermute(a, 'col', [(i, i ^ 2 * step) for i in range(cols)])]
    all_to_all x0 -> x9, waiting for transfers between devices: none -> 55.3 us  [the longest x3 24.1 us: exchange(): lax.all_to_all(pieces, 'row', split_axis=0, concat_axis=0, tiled=True)]
    all_to_all x0 -> x9, starting transfers between devices: none -> 43.4 us  [the longest x3 15.8 us: give_back(): lax.all_to_all(total, 'row', split_axis=0, concat_axis=0, tiled=True)]
    ppermute x45 -> x15, starting transfers between devices: 49.8 us -> 22.2 us  [row_swap(): return lax.ppermute(a, 'row', [(i, i ^ step) for i in range(rows)])]
    all_gather x0 -> x2, waiting for transfers between devices: none -> 17.5 us  [the longest x1 10.3 us: local(): out_full = lax.all_gather(own_first(out_weight), 'row', axis=0, tiled=True)]
    ppermute x6, waiting for transfers between devices: 7.94 us -> 22.6 us  [sum_cols(): a = a + lax.ppermute(a, 'col', [(i, i ^ step) for i in range(cols)])]
    convert_element_type x4 -> x10, other arithmetic: 2.08 us -> 15.7 us  [the longest x3 8.77 us: give_back(): total = total.astype(BF16).reshape(rows, 2 * feat, pieces[0].shape[1])]
  transfers between devices with their start and end apart: 116 -> 91, of which waited for: 51 -> 34; matrix products, arithmetic and copies ran while one was open for 13% -> 17% of each run, Pallas kernels for 13% -> 16%
where the time goes in v3:
time: 721 us; the launch traced here: 710 us
  waiting for transfers between devices  295 us (41%)
  starting transfers between devices  121 us (17%)
  Pallas kernels  121 us (17%)
  other arithmetic  89.6 us (12%)
  local copies, waits for them, and re-layouts  67.7 us (9%)
  between operations  15.9 us (2%)
    ppermute x15, waiting for transfers between devices, row_swap(): return lax.ppermute(a, 'row', [(i, i ^ step) for i in range(rows)])  121 us
    ppermute x36, waiting for transfers between devices, plane_swap(): return lax.ppermute(a, 'col', [(i, i ^ 2 * step) for i in range(cols)])  78 us
    ppermute x36, starting transfers between devices, plane_swap(): return lax.ppermute(a, 'col', [(i, i ^ 2 * step) for i in range(cols)])  46 us
    pallas_call x2, Pallas kernels, units(): pl.pallas_call(functools.partial(units_kernel, feat, parts, count), in_sp...  34.1 us
    unnamed x156, local copies, waits for them, and re-layouts  33.1 us
    pallas_call x5, Pallas kernels, outer(): pl.pallas_call(functools.partial(outer_kernel, len(owns), count), grid=(h...  27.6 us
    pallas_call x4, Pallas kernels, unfold(): pl.pallas_call(functools.partial(unfold_kernel, feat, tuple((len(ws) for...  25.5 us
    all_to_all x3, waiting for transfers between devices, exchange(): lax.all_to_all(pieces, 'row', split_axis=0, concat_axis=0, tiled=True)  24.1 us
  transfers between devices with their start and end apart: 91, of which 34 were waited for; matrix products, arithmetic and copies ran while one was open for 17% of the time, Pallas kernels for 16%

profile of v3, /device:TPU:0, one launch (start us, length us, event | category | flops | bytes accessed | tf_op | source)
XLA Modules:
  0.0 709.7 jit_solution(6278706408371717974)
XLA Ops:
  13.8 6.3 all-to-all-start
  24.9 2.7 broadcast_select_fusion.1
  27.6 7.7 %collective-permute-done = bf16[1024,256]{1,0:T(8,128)(2,1)} collective-permute-done((bf16[1024,256]{1,0:T(8,128)(2,1)}, bf16[1024,256]{1,0:T(8,128)(2,1)}, u32[]{:S(2)}, u32[]{:S(2)}) %collective-permute-start) | collective-permute-done | bytes 524320 | tf_op jit(solution)/shard_map/inputs/ppermute | solution.py:423
  36.4 9.9 %collective-permute-done.1 = bf16[1024,256]{1,0:T(8,128)(2,1)} collective-permute-done((bf16[1024,256]{1,0:T(8,128)(2,1)}, bf16[1024,256]{1,0:T(8,128)(2,1)}, u32[]{:S(2)}, u32[]{:S(2)}) %collective-permute-start.1) | collective-permute-done | bytes 524320 | tf_op jit(solution)/shard_map/inputs/ppermute | solution.py:423
  49.8 24.1 %all-to-all-done = bf16[4,512,256]{2,1,0:T(8,128)(2,1)S(1)} async-done(((bf16[4,512,256]{2,1,0:T(8,128)(2,1)}), bf16[4,512,256]{2,1,0:T(8,128)(2,1)S(1)}, u32[]{:S(2)}, u32[]{:S(2)}) %all-to-all-start) | async-done | bytes 1048608 | tf_op jit(solution)/shard_map/gate_row/all_to_all | solution.py:518
  79.3 4.4 all-to-all-start.1
  84.5 7.5 %collective-permute-done.4.refs_14_ = bf16[2048,256]{1,0:T(8,128)(2,1)} collective-permute-done((bf16[2048,256]{1,0:T(8,128)(2,1)S(1)}, bf16[2048,256]{1,0:T(8,128)(2,1)}, u32[]{:S(2)}, u32[]{:S(2)}) %collective-permute-start.4) | collective-permute-done | bytes 1048608 | tf_op jit(solution)/shard_map/gate_plane/ppermute | solution.py:423
  93.9 2.5 collective-permute-start.6
  110.8 7.2 %all-gather.3.cloned.1.call-done.weight_ref.refs_1_ = bf16[2048,768]{1,0:T(8,128)(2,1)} async-done(((bf16[512,768]{1,0:T(8,128)(2,1)}), bf16[2048,768]{1,0:T(8,128)(2,1)}) %all-gather.3.cloned.1.call-update) | async-done | bytes 3145744 | tf_op jit(solution)/shard_map/gather_qkv/all_gather | solution.py:556
  118.0 8.5 %project.1 = (bf16[1024,256]{1,0:T(8,128)(2,1)}, bf16[1024,256]{1,0:T(8,128)(2,1)}, bf16[1024,256]{1,0:T(8,128)(2,1)}, f32[1024,1]{1,0:T(8,128)}) custom-call(bf16[1024,1024]{1,0:T(8,128)(2,1)} %copy-done, bf16[1024,1024]{1,0:T(8,128)(2,1)} %collective-permute-done.5.other_ref.refs_1_, bf16[2048,768]{1,0:T(8,128)(2,1)} %all-gather.3.cloned.1.call-done.weight_ref.refs_1_, ...), custom_call_target="tpu_custom_call" | custom-call | tf_op jit(solution)/shard_map/project/pallas_call | solution.py:83
  126.5 10.1 %attend.1 = (bf16[1024,256]{1,0:T(8,128)(2,1)}, f32[2,2,1024]{2,1,0:T(2,128)}) custom-call(bf16[1024,256]{1,0:T(8,128)(2,1)} %get-tuple-element.81.q_ref, bf16[1024,256]{1,0:T(8,128)(2,1)} %get-tuple-element.82.k_ref, bf16[1024,256]{1,0:T(8,128)(2,1)} %get-tuple-element.83.v_ref, s32[1,1024]{1,0:T(1,128)} %bitcast.129), custom_call_target="tpu_custom_call" | custom-call | tf_op jit(solution)/shard_map/attend/pallas_call | solution.py:292
  136.6 10.3 %all-gather.5.cloned.1.call-done.refs_1_.weight_ref = bf16[2048,256]{1,0:T(8,128)(2,1)} async-done(((bf16[512,256]{1,0:T(8,128)(2,1)}), bf16[2048,256]{1,0:T(8,128)(2,1)}) %all-gather.5.cloned.1.call-update) | async-done | bytes 1048592 | tf_op jit(solution)/shard_map/gather_qkv/all_gather | solution.py:564
  147.0 5.4 mix.1
  153.6 4.2 all-to-all-start.2
  160.9 5.9 fusion.20
  171.5 12.7 %collective-permute-done.13.refs_15_ = bf16[2048,256]{1,0:T(8,128)(2,1)S(1)} collective-permute-done((bf16[2048,256]{1,0:T(8,128)(2,1)}, bf16[2048,256]{1,0:T(8,128)(2,1)S(1)}, u32[]{:S(2)}, u32[]{:S(2)}) %collective-permute-start.13) | collective-permute-done | bytes 1048608 | tf_op jit(solution)/shard_map/up_plane/ppermute | solution.py:423
  187.4 4.3 all-to-all-start.3
  191.8 14.9 %collective-permute-done.10 = bf16[256,1024]{1,0:T(8,128)(2,1)} collective-permute-done((bf16[256,1024]{1,0:T(8,128)(2,1)}, bf16[256,1024]{1,0:T(8,128)(2,1)}, u32[]{:S(2)}, u32[]{:S(2)}) %collective-permute-start.10) | collective-permute-done | bytes 524320 | tf_op jit(solution)/shard_map/mix_plane/ppermute | solution.py:423
  208.2 3.0 multiply_reduce_fusion.2
  215.7 9.4 %all-to-all-done.3 = bf16[4,256,256]{2,1,0:T(8,128)(2,1)} async-done(((bf16[4,256,256]{2,1,0:T(8,128)(2,1)}), bf16[4,256,256]{2,1,0:T(8,128)(2,1)}, u32[]{:S(2)}, u32[]{:S(2)}) %all-to-all-start.3) | async-done | bytes 524320 | tf_op jit(solution)/shard_map/grad_plane/all_to_all | solution.py:490
  227.1 2.9 collective-permute-start.30
  230.2 33.7 %collective-permute-done.30.refs_4_.refs_2_ = bf16[256,1024]{1,0:T(8,128)(2,1)S(1)} collective-permute-done((bf16[256,1024]{1,0:T(8,128)(2,1)S(1)}, bf16[256,1024]{1,0:T(8,128)(2,1)S(1)}, u32[]{:S(2)}, u32[]{:S(2)}) %collective-permute-start.30) | collective-permute-done | bytes 524320 | tf_op jit(solution)/shard_map/grad_row/ppermute | solution.py:437
  265.9 8.4 %collective-permute-done.26.refs_0_.refs_2_ = bf16[256,1024]{1,0:T(8,128)(2,1)S(1)} collective-permute-done((bf16[256,1024]{1,0:T(8,128)(2,1)S(1)}, bf16[256,1024]{1,0:T(8,128)(2,1)S(1)}, u32[]{:S(2)}, u32[]{:S(2)}) %collective-permute-start.26) | collective-permute-done | bytes 524320 | tf_op jit(solution)/shard_map/middle_row/ppermute | solution.py:437
  278.3 7.3 %collective-permute-done.31.refs_5_.refs_3_ = bf16[256,1024]{1,0:T(8,128)(2,1)S(1)} collective-permute-done((bf16[256,1024]{1,0:T(8,128)(2,1)S(1)}, bf16[256,1024]{1,0:T(8,128)(2,1)S(1)}, u32[]{:S(2)}, u32[]{:S(2)}) %collective-permute-start.31) | collective-permute-done | bytes 524320 | tf_op jit(solution)/shard_map/grad_row/ppermute | solution.py:437
  285.6 11.2 %collective-permute-done.17.refs_5_.refs_1_ = bf16[256,1024]{1,0:T(8,128)(2,1)S(1)} collective-permute-done((bf16[256,1024]{1,0:T(8,128)(2,1)S(1)}, bf16[256,1024]{1,0:T(8,128)(2,1)S(1)}, u32[]{:S(2)}, u32[]{:S(2)}) %collective-permute-start.17) | collective-permute-done | bytes 524320 | tf_op jit(solution)/shard_map/grad_row/ppermute | solution.py:437
  296.8 11.2 %collective-permute-done.27.refs_1_.refs_3_ = bf16[256,1024]{1,0:T(8,128)(2,1)S(1)} collective-permute-done((bf16[256,1024]{1,0:T(8,128)(2,1)S(1)}, bf16[256,1024]{1,0:T(8,128)(2,1)S(1)}, u32[]{:S(2)}, u32[]{:S(2)}) %collective-permute-start.27) | collective-permute-done | bytes 524320 | tf_op jit(solution)/shard_map/middle_row/ppermute | solution.py:437
  311.4 7.8 %collective-permute-done.14.refs_1_ = bf16[256,1024]{1,0:T(8,128)(2,1)S(1)} collective-permute-done((bf16[256,1024]{1,0:T(8,128)(2,1)S(1)}, bf16[256,1024]{1,0:T(8,128)(2,1)S(1)}, u32[]{:S(2)}, u32[]{:S(2)}) %collective-permute-start.14) | collective-permute-done | bytes 524320 | tf_op jit(solution)/shard_map/middle_row/ppermute | solution.py:437
  323.4 16.8 %units.3 = (bf16[512,1024]{1,0:T(8,128)(2,1)}, bf16[512,1024]{1,0:T(8,128)(2,1)}, bf16[512,1024]{1,0:T(8,128)(2,1)}, f32[256,1024]{1,0:T(8,128)}, f32[256,1024]{...) custom-call(bf16[256,1024]{1,0:T(8,128)(2,1)S(1)} %collective-permute-done.26.refs_0_.refs_2_, ...), custom_call_target="tpu_custom_call" | custom-call | tf_op jit(solution)/shard_map/units/pallas_call | solution.py:187
  340.8 17.3 %units.2 = (bf16[512,1024]{1,0:T(8,128)(2,1)}, bf16[512,1024]{1,0:T(8,128)(2,1)}, bf16[512,1024]{1,0:T(8,128)(2,1)}, f32[256,1024]{1,0:T(8,128)}, f32[256,1024]{...) custom-call(bf16[256,1024]{1,0:T(8,128)(2,1)S(1)} %convert_element_type.284.refs_0_, ...), custom_call_target="tpu_custom_call" | custom-call | tf_op jit(solution)/shard_map/units/pallas_call | solution.py:187
  360.1 5.8 down_outer.1
  369.7 6.3 feed.2
  378.0 6.1 feed.3
  395.7 12.9 %collective-permute-done.38 = bf16[256,1024]{1,0:T(8,128)(2,1)S(1)} collective-permute-done((bf16[256,1024]{1,0:T(8,128)(2,1)}, bf16[256,1024]{1,0:T(8,128)(2,1)S(1)}, u32[]{:S(2)}, u32[]{:S(2)}) %collective-permute-start.38) | collective-permute-done | bytes 524320 | tf_op jit(solution)/shard_map/unit_grad/ppermute | solution.py:437
  408.6 6.1 collective-permute-done.41
  426.2 17.5 %collective-permute-done.44 = bf16[256,1024]{1,0:T(8,128)(2,1)S(1)} collective-permute-done((bf16[256,1024]{1,0:T(8,128)(2,1)S(1)}, bf16[256,1024]{1,0:T(8,128)(2,1)S(1)}, u32[]{:S(2)}, u32[]{:S(2)}) %collective-permute-start.44) | collective-permute-done | bytes 524320 | tf_op jit(solution)/shard_map/feed/ppermute | solution.py:437
  452.6 6.9 collective-permute-done.50
  460.4 5.8 gate_outer.1
  466.3 5.3 collective-permute-done.45
  472.9 4.1 all-to-all-start.4
  477.0 4.9 collective-permute-done.66
  481.9 3.2 add_convert_fusion
  486.3 4.4 all-to-all-start.8
  506.8 5.8 up_outer.1
  516.6 4.9 out_outer.1
  521.5 2.6 add_convert_fusion.8
  527.7 2.7 convert_element_type.348
  530.5 4.1 fold.1.do_ref
  539.2 11.0 %attend_back.1 = (bf16[1024,256]{1,0:T(8,128)(2,1)}, bf16[1024,256]{1,0:T(8,128)(2,1)}, bf16[1024,256]{1,0:T(8,128)(2,1)}) custom-call(bf16[1024,256]{1,0:T(8,128)(2,1)} %get-tuple-element.81.q_ref, bf16[1024,256]{1,0:T(8,128)(2,1)} %get-tuple-element.82.k_ref, bf16[1024,256]{1,0:T(8,128)(2,1)} %get-tuple-element.83.v_ref, ...), custom_call_target="tpu_custom_call" | custom-call | tf_op jit(solution)/shard_map/attend_back/pallas_call | solution.py:361
  553.9 5.4 qkv_outer.1
  561.1 3.7 multiply_reduce_fusion
  565.1 7.7 %first_grad.1 = (f32[1024,1024]{1,0:T(8,128)}, bf16[1024,1024]{1,0:T(8,128)(2,1)}) custom-call(bf16[1024,768]{1,0:T(8,128)(2,1)} %copy-done.47, bf16[2048,768]{1,0:T(8,128)(2,1)} %all-gather.3.cloned.1.call-done.weight_ref.refs_1_), custom_call_target="tpu_custom_call" | custom-call | tf_op jit(solution)/shard_map/first_plane/first_grad/pallas_call | solution.py:119
  573.3 2.9 add_convert_fusion.6
  576.2 5.2 all-to-all-start.6
  582.0 2.5 add_convert_fusion.5
  592.1 20.7 %collective-permute-done.71 = f32[2048]{0:T(1024)S(1)} collective-permute-done((f32[2048]{0:T(1024)S(1)}, f32[2048]{0:T(1024)S(1)}, u32[]{:S(2)}, u32[]{:S(2)}) %collective-permute-start.71) | collective-permute-done | bytes 8224 | tf_op jit(solution)/shard_map/first_gain/ppermute | solution.py:505
  617.0 18.0 %all-to-all-done.6 = bf16[4,512,256]{2,1,0:T(8,128)(2,1)} async-done(((bf16[4,512,256]{2,1,0:T(8,128)(2,1)}), bf16[4,512,256]{2,1,0:T(8,128)(2,1)}, u32[]{:S(2)}, u32[]{:S(2)}) %all-to-all-start.6) | async-done | bytes 1048608 | tf_op jit(solution)/shard_map/gate_grad/all_to_all | solution.py:549
  635.0 2.7 convert_element_type.326
  637.7 6.0 fusion.19
  648.4 2.7 add_convert_fusion.3
  651.1 6.2 all-to-all-start.7
  660.0 4.7 collective-permute-start.74
  664.8 6.6 collective-permute-done.55
  677.6 2.7 all-to-all-done.7
  680.3 4.1 all-to-all-start.5
  (415 shorter events, 194.0 us)
Async XLA Ops:
  7.2 110.8 %all-gather.3.cloned.1.call-start = ((), (), s32[]{:S(2)}) async-start(), calls=%async_computation.11 | async-start | bytes 3932160 | tf_op jit(solution)/shard_map/gather_qkv/all_gather | solution.py:556
  13.8 60.1 %all-to-all-start = ((bf16[4,512,256]{2,1,0:T(8,128)(2,1)}), bf16[4,512,256]{2,1,0:T(8,128)(2,1)S(1)}, u32[]{:S(2)}, u32[]{:S(2)}) async-start(bf16[4,512,256]{2,1,0:T(8,128)(2,1)} %pad_maximum_fusion), calls=%async_computation | async-start | bytes 2097152 | tf_op jit(solution)/shard_map/gate_row/all_to_all | solution.py:518
  21.6 24.7 %collective-permute-start.1 = (bf16[1024,256]{1,0:T(8,128)(2,1)}, bf16[1024,256]{1,0:T(8,128)(2,1)}, u32[]{:S(2)}, u32[]{:S(2)}) collective-permute-start(bf16[1024,256]{1,0:T(8,128)(2,1)} %param.13), channel_id=1, source_target_pairs={{0,4},{1,5},{2,6},{3,7},{4,0},{5,1},{6,2},{7,3},{8,12},{9,13},{10,... | collective-permute-start | bytes 1572872 | tf_op jit(solution)/shard_map/inputs/ppermute | solution.py:423
  23.1 24.3 %collective-permute-start.2 = (bf16[1024,256]{1,0:T(8,128)(2,1)}, bf16[1024,256]{1,0:T(8,128)(2,1)}, u32[]{:S(2)}, u32[]{:S(2)}) collective-permute-start(bf16[1024,256]{1,0:T(8,128)(2,1)} %param.13), channel_id=1, source_target_pairs={{0,6},{1,7},{2,4},{3,5},{4,2},{5,3},{6,0},{7,1},{8,14},{9,15},{10,... | collective-permute-start | bytes 1572872 | tf_op jit(solution)/shard_map/inputs/ppermute | solution.py:423
  48.5 62.4 %collective-permute-start.5 = (bf16[1024,1024]{1,0:T(8,128)(2,1)S(1)}, bf16[1024,1024]{1,0:T(8,128)(2,1)}, u32[]{:S(2)}, u32[]{:S(2)}) collective-permute-start(bf16[1024,1024]{1,0:T(8,128)(2,1)S(1)} %constant_dynamic-update-slice_fusion.13.own_ref.refs_0_), channel_id=1, source_target_pairs={{0,1},{1,0},{2,3},{3,2},{4,5},{5,4},{6,7},{7,6},{8,9},{9,8},{10,11... | collective-permute-start | bytes 6291464 | tf_op jit(solution)/shard_map/inputs/ppermute | solution.py:420
  75.4 22.2 %collective-permute-start.3 = (bf16[2048,256]{1,0:T(8,128)(2,1)S(1)}, bf16[2048,256]{1,0:T(8,128)(2,1)}, u32[]{:S(2)}, u32[]{:S(2)}) collective-permute-start(bf16[2048,256]{1,0:T(8,128)(2,1)S(1)} %bitcast.119), channel_id=1, source_target_pairs={{0,2},{1,3},{2,0},{3,1},{4,6},{5,7},{6,4},{7,5},{8,10},{9,11},{10,... | collective-permute-start | bytes 3145736 | tf_op jit(solution)/shard_map/gate_plane/ppermute | solution.py:423
  79.3 57.3 %all-to-all-start.1 = ((bf16[4,512,256]{2,1,0:T(8,128)(2,1)}), bf16[4,512,256]{2,1,0:T(8,128)(2,1)}, u32[]{:S(2)}, u32[]{:S(2)}) async-start(bf16[4,512,256]{2,1,0:T(8,128)(2,1)} %pad_maximum_fusion.2), calls=%async_computation.1 | async-start | bytes 2097152 | tf_op jit(solution)/shard_map/up_row/all_to_all | solution.py:518
  83.7 63.3 %all-gather.5.cloned.1.call-start = ((), (), s32[]{:S(2)}) async-start(), calls=%async_computation.12 | async-start | bytes 1310720 | tf_op jit(solution)/shard_map/gather_qkv/all_gather | solution.py:564
  153.6 33.8 %all-to-all-start.2 = ((bf16[4,512,256]{2,1,0:T(8,128)(2,1)}), bf16[4,512,256]{2,1,0:T(8,128)(2,1)}, u32[]{:S(2)}, u32[]{:S(2)}) async-start(bf16[4,512,256]{2,1,0:T(8,128)(2,1)} %pad_maximum_fusion.4), calls=%async_computation.2 | async-start | bytes 2097152 | tf_op jit(solution)/shard_map/down_row/all_to_all | solution.py:518
  157.9 26.2 %collective-permute-start.13 = (bf16[2048,256]{1,0:T(8,128)(2,1)}, bf16[2048,256]{1,0:T(8,128)(2,1)S(1)}, u32[]{:S(2)}, u32[]{:S(2)}) collective-permute-start(bf16[2048,256]{1,0:T(8,128)(2,1)} %bitcast.13.refs_9_), channel_id=1, source_target_pairs={{0,4},{1,5},{2,6},{3,7},{4,0},{5,1},{6,2},{7,3},{8,12},{9,13},{10,... | collective-permute-start | bytes 3145736 | tf_op jit(solution)/shard_map/up_plane/ppermute | solution.py:423
  159.4 53.9 %collective-permute-start.12 = (bf16[2048,256]{1,0:T(8,128)(2,1)}, bf16[2048,256]{1,0:T(8,128)(2,1)S(1)}, u32[]{:S(2)}, u32[]{:S(2)}) collective-permute-start(bf16[2048,256]{1,0:T(8,128)(2,1)} %bitcast.13.refs_9_), channel_id=1, source_target_pairs={{0,2},{1,3},{2,0},{3,1},{4,6},{5,7},{6,4},{7,5},{8,10},{9,11},{10,... | collective-permute-start | bytes 3145736 | tf_op jit(solution)/shard_map/up_plane/ppermute | solution.py:423
  168.0 38.7 %collective-permute-start.10 = (bf16[256,1024]{1,0:T(8,128)(2,1)}, bf16[256,1024]{1,0:T(8,128)(2,1)}, u32[]{:S(2)}, u32[]{:S(2)}) collective-permute-start(bf16[256,1024]{1,0:T(8,128)(2,1)} %get-tuple-element.193), channel_id=1, source_target_pairs={{0,4},{1,5},{2,6},{3,7},{4,0},{5,1},{6,2},{7,3},{8,12},{9,13},{10,... | collective-permute-start | bytes 1572872 | tf_op jit(solution)/shard_map/mix_plane/ppermute | solution.py:423
  168.5 38.2 %collective-permute-start.11 = (bf16[256,1024]{1,0:T(8,128)(2,1)}, bf16[256,1024]{1,0:T(8,128)(2,1)}, u32[]{:S(2)}, u32[]{:S(2)}) collective-permute-start(bf16[256,1024]{1,0:T(8,128)(2,1)} %get-tuple-element.192), channel_id=1, source_target_pairs={{0,6},{1,7},{2,4},{3,5},{4,2},{5,3},{6,0},{7,1},{8,14},{9,15},{10,... | collective-permute-start | bytes 1572872 | tf_op jit(solution)/shard_map/mix_plane/ppermute | solution.py:423
  170.0 38.3 %collective-permute-start.9 = (bf16[256,1024]{1,0:T(8,128)(2,1)}, bf16[256,1024]{1,0:T(8,128)(2,1)}, u32[]{:S(2)}, u32[]{:S(2)}) collective-permute-start(bf16[256,1024]{1,0:T(8,128)(2,1)} %get-tuple-element.191), channel_id=1, source_target_pairs={{0,2},{1,3},{2,0},{3,1},{4,6},{5,7},{6,4},{7,5},{8,10},{9,11},{10,... | collective-permute-start | bytes 1572872 | tf_op jit(solution)/shard_map/mix_plane/ppermute | solution.py:423
  185.9 44.1 %collective-permute-start.22 = (bf16[1024,256]{1,0:T(8,128)(2,1)}, bf16[1024,256]{1,0:T(8,128)(2,1)}, u32[]{:S(2)}, u32[]{:S(2)}) collective-permute-start(bf16[1024,256]{1,0:T(8,128)(2,1)} %slice.464), channel_id=1, source_target_pairs={{0,2},{1,3},{2,0},{3,1},{4,6},{5,7},{6,4},{7,5},{8,10},{9,11},{10,... | collective-permute-start | bytes 1572872 | tf_op jit(solution)/shard_map/up_plane/ppermute | solution.py:423
  187.4 37.7 %all-to-all-start.3 = ((bf16[4,256,256]{2,1,0:T(8,128)(2,1)}), bf16[4,256,256]{2,1,0:T(8,128)(2,1)}, u32[]{:S(2)}, u32[]{:S(2)}) async-start(bf16[4,256,256]{2,1,0:T(8,128)(2,1)} %bitcast.128), calls=%async_computation.3 | async-start | bytes 1048576 | tf_op jit(solution)/shard_map/grad_plane/all_to_all | solution.py:490
  211.3 63.1 %collective-permute-start.21 = (bf16[2048,256]{1,0:T(8,128)(2,1)}, bf16[2048,256]{1,0:T(8,128)(2,1)}, u32[]{:S(2)}, u32[]{:S(2)}) collective-permute-start(bf16[2048,256]{1,0:T(8,128)(2,1)} %bitcast.18.refs_10_.refs_1_), channel_id=1, source_target_pairs={{0,4},{1,5},{2,6},{3,7},{4,0},{5,1},{6,2},{7,3},{8,12},{9,13},{10,... | collective-permute-start | bytes 3145736 | tf_op jit(solution)/shard_map/down_plane/ppermute | solution.py:423
  211.8 63.8 %collective-permute-start.20 = (bf16[2048,256]{1,0:T(8,128)(2,1)}, bf16[2048,256]{1,0:T(8,128)(2,1)}, u32[]{:S(2)}, u32[]{:S(2)}) collective-permute-start(bf16[2048,256]{1,0:T(8,128)(2,1)} %bitcast.18.refs_10_.refs_1_), channel_id=1, source_target_pairs={{0,2},{1,3},{2,0},{3,1},{4,6},{5,7},{6,4},{7,5},{8,10},{9,11},{10,... | collective-permute-start | bytes 3145736 | tf_op jit(solution)/shard_map/down_plane/ppermute | solution.py:423
  214.2 49.6 %collective-permute-start.23 = (bf16[1024,256]{1,0:T(8,128)(2,1)}, bf16[1024,256]{1,0:T(8,128)(2,1)}, u32[]{:S(2)}, u32[]{:S(2)}) collective-permute-start(bf16[1024,256]{1,0:T(8,128)(2,1)} %slice.465), channel_id=1, source_target_pairs={{0,4},{1,5},{2,6},{3,7},{4,0},{5,1},{6,2},{7,3},{8,12},{9,13},{10,... | collective-permute-start | bytes 1572872 | tf_op jit(solution)/shard_map/up_plane/ppermute | solution.py:423
  227.1 36.8 %collective-permute-start.30 = (bf16[256,1024]{1,0:T(8,128)(2,1)S(1)}, bf16[256,1024]{1,0:T(8,128)(2,1)S(1)}, u32[]{:S(2)}, u32[]{:S(2)}) collective-permute-start(bf16[256,1024]{1,0:T(8,128)(2,1)S(1)} %pad_maximum_fusion.5.refs_4_.refs_0_), channel_id=1, source_target_pairs={{0,16},{8,24},{16,0},{24,8},{1,17},{9,25},{17,1},{25,9},{2,18},{10... | collective-permute-start | bytes 1572872 | tf_op jit(solution)/shard_map/grad_row/ppermute | solution.py:437
  230.1 44.3 %collective-permute-start.26 = (bf16[256,1024]{1,0:T(8,128)(2,1)S(1)}, bf16[256,1024]{1,0:T(8,128)(2,1)S(1)}, u32[]{:S(2)}, u32[]{:S(2)}) collective-permute-start(bf16[256,1024]{1,0:T(8,128)(2,1)S(1)} %convert_element_type.284.refs_0_), channel_id=1, source_target_pairs={{0,16},{8,24},{16,0},{24,8},{1,17},{9,25},{17,1},{25,9},{2,18},{10... | collective-permute-start | bytes 1572872 | tf_op jit(solution)/shard_map/middle_row/ppermute | solution.py:437
  263.9 21.7 %collective-permute-start.31 = (bf16[256,1024]{1,0:T(8,128)(2,1)S(1)}, bf16[256,1024]{1,0:T(8,128)(2,1)S(1)}, u32[]{:S(2)}, u32[]{:S(2)}) collective-permute-start(bf16[256,1024]{1,0:T(8,128)(2,1)S(1)} %collective-permute-done.30.refs_4_.refs_2_), channel_id=1, source_target_pairs={{0,8},{8,0},{16,24},{24,16},{1,9},{9,1},{17,25},{25,17},{2,10},{10... | collective-permute-start | bytes 1572872 | tf_op jit(solution)/shard_map/grad_row/ppermute | solution.py:437
  263.9 32.9 %collective-permute-start.17 = (bf16[256,1024]{1,0:T(8,128)(2,1)S(1)}, bf16[256,1024]{1,0:T(8,128)(2,1)S(1)}, u32[]{:S(2)}, u32[]{:S(2)}) collective-permute-start(bf16[256,1024]{1,0:T(8,128)(2,1)S(1)} %pad_maximum_fusion.5.refs_4_.refs_0_), channel_id=1, source_target_pairs={{0,8},{8,0},{16,24},{24,16},{1,9},{9,1},{17,25},{25,17},{2,10},{10... | collective-permute-start | bytes 1572872 | tf_op jit(solution)/shard_map/grad_row/ppermute | solution.py:437
  274.4 22.5 %collective-permute-start.32 = (bf16[256,1024]{1,0:T(8,128)(2,1)S(1)}, bf16[256,1024]{1,0:T(8,128)(2,1)S(1)}, u32[]{:S(2)}, u32[]{:S(2)}) collective-permute-start(bf16[256,1024]{1,0:T(8,128)(2,1)S(1)} %collective-permute-done.30.refs_4_.refs_2_), channel_id=1, source_target_pairs={{0,1},{1,0},{2,3},{3,2},{4,5},{5,4},{6,7},{7,6},{8,9},{9,8},{10,11... | collective-permute-start | bytes 1572872 | tf_op jit(solution)/shard_map/grad_core/ppermute | solution.py:420
  274.4 33.7 %collective-permute-start.27 = (bf16[256,1024]{1,0:T(8,128)(2,1)S(1)}, bf16[256,1024]{1,0:T(8,128)(2,1)S(1)}, u32[]{:S(2)}, u32[]{:S(2)}) collective-permute-start(bf16[256,1024]{1,0:T(8,128)(2,1)S(1)} %collective-permute-done.26.refs_0_.refs_2_), channel_id=1, source_target_pairs={{0,8},{8,0},{16,24},{24,16},{1,9},{9,1},{17,25},{25,17},{2,10},{10... | collective-permute-start | bytes 1572872 | tf_op jit(solution)/shard_map/middle_row/ppermute | solution.py:437
  275.7 33.0 %collective-permute-start.24 = (bf16[1024,256]{1,0:T(8,128)(2,1)S(1)}, bf16[1024,256]{1,0:T(8,128)(2,1)S(1)}, u32[]{:S(2)}, u32[]{:S(2)}) collective-permute-start(bf16[1024,256]{1,0:T(8,128)(2,1)S(1)} %slice.466), channel_id=1, source_target_pairs={{0,2},{1,3},{2,0},{3,1},{4,6},{5,7},{6,4},{7,5},{8,10},{9,11},{10,... | collective-permute-start | bytes 1572872 | tf_op jit(solution)/shard_map/down_plane/ppermute | solution.py:423
  285.6 25.3 %collective-permute-start.33 = (bf16[256,1024]{1,0:T(8,128)(2,1)S(1)}, bf16[256,1024]{1,0:T(8,128)(2,1)S(1)}, u32[]{:S(2)}, u32[]{:S(2)}) collective-permute-start(bf16[256,1024]{1,0:T(8,128)(2,1)S(1)} %collective-permute-done.31.refs_5_.refs_3_), channel_id=1, source_target_pairs={{0,1},{1,0},{2,3},{3,2},{4,5},{5,4},{6,7},{7,6},{8,9},{9,8},{10,11... | collective-permute-start | bytes 1572872 | tf_op jit(solution)/shard_map/grad_core/ppermute | solution.py:420
  296.8 22.4 %collective-permute-start.14 = (bf16[256,1024]{1,0:T(8,128)(2,1)S(1)}, bf16[256,1024]{1,0:T(8,128)(2,1)S(1)}, u32[]{:S(2)}, u32[]{:S(2)}) collective-permute-start(bf16[256,1024]{1,0:T(8,128)(2,1)S(1)} %convert_element_type.284.refs_0_), channel_id=1, source_target_pairs={{0,8},{8,0},{16,24},{24,16},{1,9},{9,1},{17,25},{25,17},{2,10},{10... | collective-permute-start | bytes 1572872 | tf_op jit(solution)/shard_map/middle_row/ppermute | solution.py:437
  296.8 22.4 %collective-permute-start.28 = (bf16[256,1024]{1,0:T(8,128)(2,1)S(1)}, bf16[256,1024]{1,0:T(8,128)(2,1)S(1)}, u32[]{:S(2)}, u32[]{:S(2)}) collective-permute-start(bf16[256,1024]{1,0:T(8,128)(2,1)S(1)} %collective-permute-done.26.refs_0_.refs_2_), channel_id=1, source_target_pairs={{0,1},{1,0},{2,3},{3,2},{4,5},{5,4},{6,7},{7,6},{8,9},{9,8},{10,11... | collective-permute-start | bytes 1572872 | tf_op jit(solution)/shard_map/middle_row/ppermute | solution.py:420
  310.8 29.9 %collective-permute-start.18 = (bf16[256,1024]{1,0:T(8,128)(2,1)S(1)}, bf16[256,1024]{1,0:T(8,128)(2,1)S(1)}, u32[]{:S(2)}, u32[]{:S(2)}) collective-permute-start(bf16[256,1024]{1,0:T(8,128)(2,1)S(1)} %pad_maximum_fusion.5.refs_4_.refs_0_), channel_id=1, source_target_pairs={{0,1},{1,0},{2,3},{3,2},{4,5},{5,4},{6,7},{7,6},{8,9},{9,8},{10,11... | collective-permute-start | bytes 1572872 | tf_op jit(solution)/shard_map/grad_core/ppermute | solution.py:420
  358.6 37.1 %collective-permute-start.36 = (bf16[256,1024]{1,0:T(8,128)(2,1)}, bf16[256,1024]{1,0:T(8,128)(2,1)}, u32[]{:S(2)}, u32[]{:S(2)}) collective-permute-start(bf16[256,1024]{1,0:T(8,128)(2,1)} %get-tuple-element.100), channel_id=1, source_target_pairs={{0,1},{1,0},{2,3},{3,2},{4,5},{5,4},{6,7},{7,6},{8,9},{9,8},{10,11... | collective-permute-start | bytes 1572872 | tf_op jit(solution)/shard_map/unit_grad/ppermute | solution.py:420
  358.7 25.4 %collective-permute-start.39 = (bf16[256,1024]{1,0:T(8,128)(2,1)}, bf16[256,1024]{1,0:T(8,128)(2,1)}, u32[]{:S(2)}, u32[]{:S(2)}) collective-permute-start(bf16[256,1024]{1,0:T(8,128)(2,1)} %get-tuple-element.104), channel_id=1, source_target_pairs={{0,1},{1,0},{2,3},{3,2},{4,5},{5,4},{6,7},{7,6},{8,9},{9,8},{10,11... | collective-permute-start | bytes 1572872 | tf_op jit(solution)/shard_map/unit_grad/ppermute | solution.py:420
  360.1 26.1 %collective-permute-start.40 = (bf16[256,1024]{1,0:T(8,128)(2,1)}, bf16[256,1024]{1,0:T(8,128)(2,1)}, u32[]{:S(2)}, u32[]{:S(2)}) collective-permute-start(bf16[256,1024]{1,0:T(8,128)(2,1)} %convert_add_fusion.7), channel_id=1, source_target_pairs={{0,8},{8,0},{16,24},{24,16},{1,9},{9,1},{17,25},{25,17},{2,10},{10... | collective-permute-start | bytes 1572872 | tf_op jit(solution)/shard_map/unit_grad/ppermute | solution.py:437
  384.1 24.5 %collective-permute-start.38 = (bf16[256,1024]{1,0:T(8,128)(2,1)}, bf16[256,1024]{1,0:T(8,128)(2,1)S(1)}, u32[]{:S(2)}, u32[]{:S(2)}) collective-permute-start(bf16[256,1024]{1,0:T(8,128)(2,1)} %add_convert_fusion.12), channel_id=1, source_target_pairs={{0,8},{8,0},{16,24},{24,16},{1,9},{9,1},{17,25},{25,17},{2,10},{10... | collective-permute-start | bytes 1572872 | tf_op jit(solution)/shard_map/unit_grad/ppermute | solution.py:437
  386.2 30.2 %collective-permute-start.43 = (bf16[512,1024]{1,0:T(8,128)(2,1)}, bf16[512,1024]{1,0:T(8,128)(2,1)S(1)}, u32[]{:S(2)}, u32[]{:S(2)}) collective-permute-start(bf16[512,1024]{1,0:T(8,128)(2,1)} %get-tuple-element.110), channel_id=1, source_target_pairs={{0,1},{1,0},{2,3},{3,2},{4,5},{5,4},{6,7},{7,6},{8,9},{9,8},{10,11... | collective-permute-start | bytes 3145736 | tf_op jit(solution)/shard_map/feed/ppermute | solution.py:420
  388.3 26.4 %collective-permute-start.41 = (bf16[256,1024]{1,0:T(8,128)(2,1)S(1)}, bf16[256,1024]{1,0:T(8,128)(2,1)S(1)}, u32[]{:S(2)}, u32[]{:S(2)}) collective-permute-start(bf16[256,1024]{1,0:T(8,128)(2,1)S(1)} %add_convert_fusion.11), channel_id=1, source_target_pairs={{0,16},{8,24},{16,0},{24,8},{1,17},{9,25},{17,1},{25,9},{2,18},{10... | collective-permute-start | bytes 1572872 | tf_op jit(solution)/shard_map/unit_grad/ppermute | solution.py:437
  391.5 54.8 %collective-permute-start.67 = (bf16[1024,256]{1,0:T(8,128)(2,1)S(1)}, bf16[1024,256]{1,0:T(8,128)(2,1)S(1)}, u32[]{:S(2)}, u32[]{:S(2)}) collective-permute-start(bf16[1024,256]{1,0:T(8,128)(2,1)S(1)} %copy-done.68), channel_id=1, source_target_pairs={{0,2},{1,3},{2,0},{3,1},{4,6},{5,7},{6,4},{7,5},{8,10},{9,11},{10,... | collective-permute-start | bytes 1572872 | tf_op jit(solution)/shard_map/down_grad/ppermute | solution.py:423
  418.2 48.1 %collective-permute-start.42 = (bf16[256,1024]{1,0:T(8,128)(2,1)S(1)}, bf16[256,1024]{1,0:T(8,128)(2,1)S(1)}, u32[]{:S(2)}, u32[]{:S(2)}) collective-permute-start(bf16[256,1024]{1,0:T(8,128)(2,1)S(1)} %slice.469), channel_id=1, source_target_pairs={{0,8},{8,0},{16,24},{24,16},{1,9},{9,1},{17,25},{25,17},{2,10},{10... | collective-permute-start | bytes 1572872 | tf_op jit(solution)/shard_map/feed/ppermute | solution.py:437
  418.5 25.3 %collective-permute-start.44 = (bf16[256,1024]{1,0:T(8,128)(2,1)S(1)}, bf16[256,1024]{1,0:T(8,128)(2,1)S(1)}, u32[]{:S(2)}, u32[]{:S(2)}) collective-permute-start(bf16[256,1024]{1,0:T(8,128)(2,1)S(1)} %slice.471), channel_id=1, source_target_pairs={{0,8},{8,0},{16,24},{24,16},{1,9},{9,1},{17,25},{25,17},{2,10},{10... | collective-permute-start | bytes 1572872 | tf_op jit(solution)/shard_map/feed/ppermute | solution.py:437
  423.3 26.1 %collective-permute-start.48 = (bf16[256,1024]{1,0:T(8,128)(2,1)S(1)}, bf16[256,1024]{1,0:T(8,128)(2,1)S(1)}, u32[]{:S(2)}, u32[]{:S(2)}) collective-permute-start(bf16[256,1024]{1,0:T(8,128)(2,1)S(1)} %get-tuple-element.152), channel_id=1, source_target_pairs={{0,2},{1,3},{2,0},{3,1},{4,6},{5,7},{6,4},{7,5},{8,10},{9,11},{10,... | collective-permute-start | bytes 1572872 | tf_op jit(solution)/shard_map/middle_grad/ppermute | solution.py:423
  425.7 24.3 %collective-permute-start.49 = (bf16[256,1024]{1,0:T(8,128)(2,1)S(1)}, bf16[256,1024]{1,0:T(8,128)(2,1)S(1)}, u32[]{:S(2)}, u32[]{:S(2)}) collective-permute-start(bf16[256,1024]{1,0:T(8,128)(2,1)S(1)} %get-tuple-element.152), channel_id=1, source_target_pairs={{0,4},{1,5},{2,6},{3,7},{4,0},{5,1},{6,2},{7,3},{8,12},{9,13},{10,... | collective-permute-start | bytes 1572872 | tf_op jit(solution)/shard_map/middle_grad/ppermute | solution.py:423
  446.3 25.4 %collective-permute-start.45 = (bf16[256,1024]{1,0:T(8,128)(2,1)S(1)}, bf16[256,1024]{1,0:T(8,128)(2,1)S(1)}, u32[]{:S(2)}, u32[]{:S(2)}) collective-permute-start(bf16[256,1024]{1,0:T(8,128)(2,1)S(1)} %add_convert_fusion.10), channel_id=1, source_target_pairs={{0,16},{8,24},{16,0},{24,8},{1,17},{9,25},{17,1},{25,9},{2,18},{10... | collective-permute-start | bytes 1572872 | tf_op jit(solution)/shard_map/feed/ppermute | solution.py:437
  449.3 32.6 %collective-permute-start.66 = (bf16[2048,256]{1,0:T(8,128)(2,1)}, bf16[2048,256]{1,0:T(8,128)(2,1)}, u32[]{:S(2)}, u32[]{:S(2)}) collective-permute-start(bf16[2048,256]{1,0:T(8,128)(2,1)} %add_convert_fusion.2), channel_id=1, source_target_pairs={{0,2},{1,3},{2,0},{3,1},{4,6},{5,7},{6,4},{7,5},{8,10},{9,11},{10,... | collective-permute-start | bytes 3145736 | tf_op jit(solution)/shard_map/down_grad/ppermute | solution.py:423
  449.9 32.0 %collective-permute-start.68 = (bf16[2048,256]{1,0:T(8,128)(2,1)}, bf16[2048,256]{1,0:T(8,128)(2,1)}, u32[]{:S(2)}, u32[]{:S(2)}) collective-permute-start(bf16[2048,256]{1,0:T(8,128)(2,1)} %add_convert_fusion.1), channel_id=1, source_target_pairs={{0,4},{1,5},{2,6},{3,7},{4,0},{5,1},{6,2},{7,3},{8,12},{9,13},{10,... | collective-permute-start | bytes 3145736 | tf_op jit(solution)/shard_map/down_grad/ppermute | solution.py:423
  460.3 56.2 %collective-permute-start.51 = (bf16[1024,1024]{1,0:T(8,128)(2,1)}, bf16[1024,1024]{1,0:T(8,128)(2,1)}, u32[]{:S(2)}, u32[]{:S(2)}) collective-permute-start(bf16[1024,1024]{1,0:T(8,128)(2,1)} %constant_dynamic-update-slice_fusion.9.own_ref.refs_0_), channel_id=1, source_target_pairs={{0,1},{1,0},{2,3},{3,2},{4,5},{5,4},{6,7},{7,6},{8,9},{9,8},{10,11... | collective-permute-start | bytes 6291464 | tf_op jit(solution)/shard_map/middle_grad/ppermute | solution.py:420
  486.3 41.4 %all-to-all-start.8 = ((bf16[4,512,256]{2,1,0:T(8,128)(2,1)}), bf16[4,512,256]{2,1,0:T(8,128)(2,1)}, u32[]{:S(2)}, u32[]{:S(2)}) async-start(bf16[4,512,256]{2,1,0:T(8,128)(2,1)} %bitcast.125), calls=%async_computation.10 | async-start | bytes 2097152 | tf_op jit(solution)/shard_map/down_grad/all_to_all | solution.py:549
  490.7 199.9 %reduce-scatter.5.cloned.1.call-start = ((), (), s32[]{:S(2)}) async-start(), calls=%async_computation.14 | async-start | bytes 1310720 | tf_op jit(solution)/shard_map/out_grad/reduce_scatter | solution.py:553
  493.0 28.6 %collective-permute-start.57 = (bf16[1024,256]{1,0:T(8,128)(2,1)}, bf16[1024,256]{1,0:T(8,128)(2,1)}, u32[]{:S(2)}, u32[]{:S(2)}) collective-permute-start(bf16[1024,256]{1,0:T(8,128)(2,1)} %get-tuple-element.201), channel_id=1, source_target_pairs={{0,4},{1,5},{2,6},{3,7},{4,0},{5,1},{6,2},{7,3},{8,12},{9,13},{10,... | collective-permute-start | bytes 1572872 | tf_op jit(solution)/shard_map/gate_grad/ppermute | solution.py:423
  494.3 30.3 %collective-permute-start.59 = (bf16[1024,256]{1,0:T(8,128)(2,1)}, bf16[1024,256]{1,0:T(8,128)(2,1)}, u32[]{:S(2)}, u32[]{:S(2)}) collective-permute-start(bf16[1024,256]{1,0:T(8,128)(2,1)} %get-tuple-element.202), channel_id=1, source_target_pairs={{0,2},{1,3},{2,0},{3,1},{4,6},{5,7},{6,4},{7,5},{8,10},{9,11},{10,... | collective-permute-start | bytes 1572872 | tf_op jit(solution)/shard_map/gate_grad/ppermute | solution.py:423
  521.5 175.0 %reduce-scatter.3.cloned.1.call-start = ((), (), s32[]{:S(2)}) async-start(), calls=%async_computation.13 | async-start | bytes 3932160 | tf_op jit(solution)/shard_map/qkv_grad/reduce_scatter | solution.py:553
  524.1 48.7 %collective-permute-start.58 = (bf16[2048,256]{1,0:T(8,128)(2,1)}, bf16[2048,256]{1,0:T(8,128)(2,1)}, u32[]{:S(2)}, u32[]{:S(2)}) collective-permute-start(bf16[2048,256]{1,0:T(8,128)(2,1)} %add_convert_fusion.8), channel_id=1, source_target_pairs={{0,2},{1,3},{2,0},{3,1},{4,6},{5,7},{6,4},{7,5},{8,10},{9,11},{10,... | collective-permute-start | bytes 3145736 | tf_op jit(solution)/shard_map/gate_grad/ppermute | solution.py:423
  526.8 46.5 %collective-permute-start.60 = (bf16[2048,256]{1,0:T(8,128)(2,1)}, bf16[2048,256]{1,0:T(8,128)(2,1)}, u32[]{:S(2)}, u32[]{:S(2)}) collective-permute-start(bf16[2048,256]{1,0:T(8,128)(2,1)} %add_convert_fusion.7), channel_id=1, source_target_pairs={{0,4},{1,5},{2,6},{3,7},{4,0},{5,1},{6,2},{7,3},{8,12},{9,13},{10,... | collective-permute-start | bytes 3145736 | tf_op jit(solution)/shard_map/gate_grad/ppermute | solution.py:423
  536.5 45.5 %collective-permute-start.61 = (bf16[1024,256]{1,0:T(8,128)(2,1)}, bf16[1024,256]{1,0:T(8,128)(2,1)}, u32[]{:S(2)}, u32[]{:S(2)}) collective-permute-start(bf16[1024,256]{1,0:T(8,128)(2,1)} %get-tuple-element.199), channel_id=1, source_target_pairs={{0,4},{1,5},{2,6},{3,7},{4,0},{5,1},{6,2},{7,3},{8,12},{9,13},{10,... | collective-permute-start | bytes 1572872 | tf_op jit(solution)/shard_map/up_grad/ppermute | solution.py:423
  537.6 48.3 %collective-permute-start.63 = (bf16[1024,256]{1,0:T(8,128)(2,1)}, bf16[1024,256]{1,0:T(8,128)(2,1)}, u32[]{:S(2)}, u32[]{:S(2)}) collective-permute-start(bf16[1024,256]{1,0:T(8,128)(2,1)} %get-tuple-element.200), channel_id=1, source_target_pairs={{0,2},{1,3},{2,0},{3,1},{4,6},{5,7},{6,4},{7,5},{8,10},{9,11},{10,... | collective-permute-start | bytes 1572872 | tf_op jit(solution)/shard_map/up_grad/ppermute | solution.py:423
  572.8 64.9 %collective-permute-start.52 = (bf16[1024,1024]{1,0:T(8,128)(2,1)}, bf16[1024,1024]{1,0:T(8,128)(2,1)}, u32[]{:S(2)}, u32[]{:S(2)}) collective-permute-start(bf16[1024,1024]{1,0:T(8,128)(2,1)} %get-tuple-element.120), channel_id=1, source_target_pairs={{0,1},{1,0},{2,3},{3,2},{4,5},{5,4},{6,7},{7,6},{8,9},{9,8},{10,11... | collective-permute-start | bytes 6291464 | tf_op jit(solution)/shard_map/first_plane/ppermute | solution.py:420
  576.2 58.8 %all-to-all-start.6 = ((bf16[4,512,256]{2,1,0:T(8,128)(2,1)}), bf16[4,512,256]{2,1,0:T(8,128)(2,1)}, u32[]{:S(2)}, u32[]{:S(2)}) async-start(bf16[4,512,256]{2,1,0:T(8,128)(2,1)} %bitcast.126), calls=%async_computation.8 | async-start | bytes 2097152 | tf_op jit(solution)/shard_map/gate_grad/all_to_all | solution.py:549
  584.5 61.7 %collective-permute-start.62 = (bf16[2048,256]{1,0:T(8,128)(2,1)}, bf16[2048,256]{1,0:T(8,128)(2,1)}, u32[]{:S(2)}, u32[]{:S(2)}) collective-permute-start(bf16[2048,256]{1,0:T(8,128)(2,1)} %add_convert_fusion.5), channel_id=1, source_target_pairs={{0,2},{1,3},{2,0},{3,1},{4,6},{5,7},{6,4},{7,5},{8,10},{9,11},{10,... | collective-permute-start | bytes 3145736 | tf_op jit(solution)/shard_map/up_grad/ppermute | solution.py:423
  588.1 59.4 %collective-permute-start.64 = (bf16[2048,256]{1,0:T(8,128)(2,1)}, bf16[2048,256]{1,0:T(8,128)(2,1)S(1)}, u32[]{:S(2)}, u32[]{:S(2)}) collective-permute-start(bf16[2048,256]{1,0:T(8,128)(2,1)} %add_convert_fusion.4), channel_id=1, source_target_pairs={{0,4},{1,5},{2,6},{3,7},{4,0},{5,1},{6,2},{7,3},{8,12},{9,13},{10,... | collective-permute-start | bytes 3145736 | tf_op jit(solution)/shard_map/up_grad/ppermute | solution.py:423
  589.8 22.9 %collective-permute-start.71 = (f32[2048]{0:T(1024)S(1)}, f32[2048]{0:T(1024)S(1)}, u32[]{:S(2)}, u32[]{:S(2)}) collective-permute-start(f32[2048]{0:T(1024)S(1)} %add.264), channel_id=1, source_target_pairs={{0,4},{1,5},{2,6},{3,7},{4,0},{5,1},{6,2},{7,3},{8,12},{9,13},{10,... | collective-permute-start | bytes 24584 | tf_op jit(solution)/shard_map/first_gain/ppermute | solution.py:505
  612.8 74.7 %collective-permute-start.72 = (f32[512]{0:T(512)S(1)}, f32[512]{0:T(512)S(1)}, u32[]{:S(2)}, u32[]{:S(2)}) collective-permute-start(f32[512]{0:T(512)S(1)} %get-tuple-element.247), channel_id=1, source_target_pairs={{0,8},{8,0},{16,24},{24,16},{1,9},{9,1},{17,25},{25,17},{2,10},{10... | collective-permute-start | bytes 6152 | tf_op jit(solution)/shard_map/first_gain/ppermute | solution.py:437
  614.6 72.9 %collective-permute-start.73 = (f32[512]{0:T(512)S(1)}, f32[512]{0:T(512)S(1)}, u32[]{:S(2)}, u32[]{:S(2)}) collective-permute-start(f32[512]{0:T(512)S(1)} %get-tuple-element.245), channel_id=1, source_target_pairs={{0,16},{8,24},{16,0},{24,8},{1,17},{9,25},{17,1},{25,9},{2,18},{10... | collective-permute-start | bytes 6152 | tf_op jit(solution)/shard_map/first_gain/ppermute | solution.py:437
  647.6 23.7 %collective-permute-start.55 = (bf16[256,1024]{1,0:T(8,128)(2,1)}, bf16[256,1024]{1,0:T(8,128)(2,1)}, u32[]{:S(2)}, u32[]{:S(2)}) collective-permute-start(bf16[256,1024]{1,0:T(8,128)(2,1)} %get-tuple-element.189), channel_id=1, source_target_pairs={{0,6},{1,7},{2,4},{3,5},{4,2},{5,3},{6,0},{7,1},{8,14},{9,15},{10,... | collective-permute-start | bytes 1572872 | tf_op jit(solution)/shard_map/first_plane/ppermute | solution.py:423
  651.1 29.2 %all-to-all-start.7 = ((bf16[4,512,256]{2,1,0:T(8,128)(2,1)}), bf16[4,512,256]{2,1,0:T(8,128)(2,1)S(1)}, u32[]{:S(2)}, u32[]{:S(2)}) async-start(bf16[4,512,256]{2,1,0:T(8,128)(2,1)} %bitcast.127), calls=%async_computation.9 | async-start | bytes 2097152 | tf_op jit(solution)/shard_map/up_grad/all_to_all | solution.py:549
  660.0 27.5 %collective-permute-start.74 = (f32[512]{0:T(512)S(1)}, f32[512]{0:T(512)S(1)}, u32[]{:S(2)}, u32[]{:S(2)}) collective-permute-start(f32[512]{0:T(512)S(1)} %get-tuple-element.246), channel_id=1, source_target_pairs={{0,24},{8,16},{16,8},{24,0},{1,25},{9,17},{17,9},{25,1},{2,26},{10... | collective-permute-start | bytes 6152 | tf_op jit(solution)/shard_map/first_gain/ppermute | solution.py:437
  (102 other events, 1659.2 us)
Sparse Core Ops, SparseCore 0:
  10.5 107.4 all-gather.2
  119.6 27.3 all-gather.4
  521.6 27.6 reduce-scatter.4
  565.2 78.4 reduce-scatter.2

commit v4 on v3

--- a/solution.py
+++ b/solution.py
@@ -92,69 +92,79 @@
     )(own, other, weight, cosine, front, back)
 
 
-def unfold_kernel(feat, groups, *refs):
-    count = sum(groups)
-    lefts, weights = refs[: len(groups)], refs[len(groups) : len(groups) + count]
+def unfold_kernel(feat, joined, *refs):
     own_ref, other_ref = refs[-2:]
+    lefts, weights = refs[:joined], refs[joined:-2]
+    left = jnp.concatenate([ref[...] for ref in lefts], axis=1)
+    part = weights[0].shape[1]
     for at in range(0, own_ref.shape[1], feat):
         rows = slice(2 * at, 2 * (at + feat))
         total = None
-        ids = iter(weights)
-        for left, number in zip(lefts, groups):
-            part = left.shape[1] // number
-            for i in range(number):
-                term = nt(left[:, i * part : (i + 1) * part], next(ids)[rows, :])
-                total = term if total is None else total + term
-        own_ref[:, at : at + feat] = total[:, :feat].astype(own_ref.dtype)
+        for i, weight in enumerate(weights):
+            term = nt(left[:, i * part : (i + 1) * part], weight[rows, :])
+            total = term if total is None else total + term
+        own_ref[:, at : at + feat] = total[:, :feat].astype(BF16)
         other_ref[:, at : at + feat] = total[:, feat:].astype(BF16)
 
 
-def unfold(feat, name, *pairs):
-    lefts = [left for left, _ in pairs]
-    weights = [w for _, ws in pairs for w in ws]
+def unfold(feat, name, lefts, weights):
     tokens, half = lefts[0].shape[0], weights[0].shape[0] // 2
     block = 256
-    own = jax.ShapeDtypeStruct((tokens, half), F32)
-    other = jax.ShapeDtypeStruct((tokens, half), BF16)
+    result = jax.ShapeDtypeStruct((tokens, half), BF16)
     return pl.pallas_call(
-        functools.partial(unfold_kernel, feat, tuple(len(ws) for _, ws in pairs)),
+        functools.partial(unfold_kernel, feat, len(lefts)),
         grid=(tokens // block,),
         in_specs=[row_spec(block, a) for a in lefts] + [whole_spec(w) for w in weights],
-        out_specs=[row_spec(block, own), row_spec(block, other)],
-        out_shape=[own, other],
+        out_specs=[row_spec(block, result)] * 2,
+        out_shape=[result] * 2,
         compiler_params=pltpu.CompilerParams(vmem_limit_bytes=VMEM_BYTES),
         name=name,
     )(*lefts, *weights)
 
 
-def units_kernel(feat, parts, count, *refs):
-    m_owns, m_others, g_owns, g_others = (refs[i * parts : (i + 1) * parts] for i in range(4))
-    refs = refs[4 * parts :]
-    sources = refs[: 3 * count]
-    refs = refs[3 * count :]
+def units_kernel(feat, parts, count, starts, *refs):
+    m_owns, m_others = refs[:parts], refs[parts : 2 * parts]
+    g_sources = refs[2 * parts : 2 * parts + 2]
+    refs = refs[2 * parts + 2 :]
+    sources, refs = refs[: 3 * count], refs[3 * count :]
     hidden_ref, gate_ref, up_ref = refs[:3]
     own_refs, other_refs = refs[3 : 3 + parts], refs[3 + parts : 3 + 2 * parts]
-    held, arrived = refs[3 + 2 * parts :]
+    held, arrived, g_held, g_arrived = refs[3 + 2 * parts :]
+    tokens = own_refs[0].shape[0]
     copies = [
         pltpu.make_async_copy(source, held.at[at], arrived.at[at]) for at, source in enumerate(sources)
     ]
-    for copy in copies:
+    g_copies = [
+        pltpu.make_async_copy(
+            source.at[pl.ds(pl.multiple_of(starts[i] * tokens, tokens), tokens)],
+            g_held.at[side, i],
+            g_arrived.at[side, i],
+        )
+        for side, source in enumerate(g_sources)
+        for i in range(parts)
+    ]
+    for copy in copies[:2] + g_copies + copies[2:]:
         copy.start()
-
-    def together(owns, others):
-        return jnp.concatenate([weave(a[...], b[...], feat) for a, b in zip(owns, others)], axis=0)
-
-    middle = together(m_owns, m_others)
-    grad = together(g_owns, g_others)
+    middle = jnp.concatenate(
+        [weave(a[...], b[...], feat) for a, b in zip(m_owns, m_others)], axis=0
+    )
     scale = norm_scale(middle)
     part = hidden_ref.shape[1] // count
     pairs = []
+    grad = None
     for i in range(count):
         columns = slice(i * part, (i + 1) * part)
-        for copy in copies[3 * i : 3 * i + 3]:
-            copy.wait()
+        copies[3 * i].wait()
         gate = nn(middle, held[3 * i]) * scale
+        copies[3 * i + 1].wait()
         up = nn(middle, held[3 * i + 1]) * scale
+        copies[3 * i + 2].wait()
+        if grad is None:
+            for copy in g_copies:
+                copy.wait()
+            grad = jnp.concatenate(
+                [weave(g_held[0, j], g_held[1, j], feat) for j in range(parts)], axis=0
+            )
         hidden_grad = nn(grad, held[3 * i + 2])
         sigmoid = 1.0 / (1.0 + jnp.exp(-gate))
         silu = gate * sigmoid
@@ -165,7 +175,6 @@
         pairs.append((up_grad.astype(BF16), held.at[3 * i + 1]))
         gate_ref[:, columns] = (gate_grad * scale).astype(BF16)
         up_ref[:, columns] = (up_grad * scale).astype(BF16)
-    tokens = own_refs[0].shape[0]
     for at in range(0, own_refs[0].shape[1], feat):
         rows = slice(2 * at, 2 * (at + feat))
         total = None
@@ -174,61 +183,133 @@
             total = term if total is None else total + term
         for i, (own_ref, other_ref) in enumerate(zip(own_refs, other_refs)):
             mine = total[i * tokens : (i + 1) * tokens]
-            own_ref[:, at : at + feat] = mine[:, :feat]
+            own_ref[:, at : at + feat] = mine[:, :feat].astype(BF16)
             other_ref[:, at : at + feat] = mine[:, feat:].astype(BF16)
 
 
-def units(feat, m_owns, m_others, g_owns, g_others, gates, ups, downs):
+def units(feat, starts, m_owns, m_others, g_own, g_other, gates, ups, downs):
     parts = len(m_owns)
     tokens, half = m_owns[0].shape
     count, part = len(gates), gates[0].shape[1]
     hidden = jax.ShapeDtypeStruct((parts * tokens, count * part), BF16)
+    share = jax.ShapeDtypeStruct((tokens, half), BF16)
     weights = [w for three in zip(gates, ups, downs) for w in three]
+    vmem, anywhere = pl.BlockSpec(memory_space=pltpu.VMEM), pl.BlockSpec(memory_space=pl.ANY)
     result = pl.pallas_call(
         functools.partial(units_kernel, feat, parts, count),
-        in_specs=[pl.BlockSpec(memory_space=pltpu.VMEM)] * (4 * parts)
-        + [pl.BlockSpec(memory_space=pl.ANY)] * len(weights),
-        out_specs=[pl.BlockSpec(memory_space=pltpu.VMEM)] * (3 + 2 * parts),
-        out_shape=[hidden] * 3
-        + [jax.ShapeDtypeStruct((tokens, half), F32)] * parts
-        + [jax.ShapeDtypeStruct((tokens, half), BF16)] * parts,
+        in_specs=[pl.BlockSpec(memory_space=pltpu.SMEM)]
+        + [vmem] * (2 * parts)
+        + [anywhere] * (2 + len(weights)),
+        out_specs=[vmem] * (3 + 2 * parts),
+        out_shape=[hidden] * 3 + [share] * (2 * parts),
         scratch_shapes=[
             pltpu.VMEM((len(weights),) + weights[0].shape, BF16),
             pltpu.SemaphoreType.DMA((len(weights),)),
+            pltpu.VMEM((2, parts, tokens, half), BF16),
+            pltpu.SemaphoreType.DMA((2, parts)),
         ],
-        compiler_params=pltpu.CompilerParams(vmem_limit_bytes=48 * 1024 * 1024),
+        compiler_params=pltpu.CompilerParams(vmem_limit_bytes=VMEM_BYTES),
         name="units",
-    )(*m_owns, *m_others, *g_owns, *g_others, *weights)
+    )(starts, *m_owns, *m_others, g_own, g_other, *weights)
     return result[0], result[1], result[2], result[3 : 3 + parts], result[3 + parts :]
 
 
-def outer_kernel(groups, count, *refs):
+def outer_kernel(groups, count, starts, *refs):
     owns, others, rights = refs[:groups], refs[groups : 2 * groups], refs[2 * groups : len(refs) - count]
     outs = refs[len(refs) - count :]
-    left = jnp.concatenate(
-        [jnp.concatenate([own[...], other[...]], axis=1) for own, other in zip(owns, others)], axis=0
-    )
+    if groups == 1:
+        tokens = owns[0].shape[0] // starts.shape[0]
+        picks = [
+            pl.ds(pl.multiple_of(starts[i] * tokens, tokens), tokens) for i in range(starts.shape[0])
+        ]
+        sides = [(owns[0][pick, :], others[0][pick, :]) for pick in picks]
+    else:
+        sides = [(own[...], other[...]) for own, other in zip(owns, others)]
+    left = jnp.concatenate([jnp.concatenate(pair, axis=1) for pair in sides], axis=0)
     part = outs[0].shape[1]
     for i, out in enumerate(outs):
         columns = slice(i * part, (i + 1) * part)
         right = jnp.concatenate([ref[:, columns] for ref in rights], axis=0)
-        result = tn(left, right)
-        out[...] = result.astype(BF16)
-
-
-def outer(feat, name, owns, others, rights, count=1):
+        out[...] = tn(left, right).astype(BF16)
+
+
+def outer(feat, name, starts, owns, others, rights, count):
     half, columns = owns[0].shape[1], rights[0].shape[1]
     part = columns // count
     side = pl.BlockSpec((owns[0].shape[0], feat), lambda i: (0, i))
     return pl.pallas_call(
         functools.partial(outer_kernel, len(owns), count),
         grid=(half // feat,),
-        in_specs=[side] * (2 * len(owns)) + [whole_spec(a) for a in rights],
+        in_specs=[pl.BlockSpec(memory_space=pltpu.SMEM)]
+        + [side] * (2 * len(owns))
+        + [whole_spec(a) for a in rights],
         out_specs=[pl.BlockSpec((2 * feat, part), lambda i: (i, 0))] * count,
         out_shape=[jax.ShapeDtypeStruct((2 * half, part), BF16)] * count,
-        compiler_params=pltpu.CompilerParams(vmem_limit_bytes=40 * 1024 * 1024),
+        compiler_params=pltpu.CompilerParams(vmem_limit_bytes=VMEM_BYTES),
         name=name,
-    )(*owns, *others, *rights)
+    )(starts, *owns, *others, *rights)
+
+
+def heads_outer_kernel(x_own, x_other, d_own, d_other, dq_ref, dk_ref, dv_ref, mixed_ref, scale_ref, weight_ref, out_ref, dot_ref):
+    part = mixed_ref.shape[1]
+    left = jnp.concatenate([x_own[...], x_other[...]], axis=1)
+    dots = None
+    for i, ref in enumerate((dq_ref, dk_ref, dv_ref)):
+        columns = slice(i * part, (i + 1) * part)
+        result = tn(left, (ref[...].astype(F32) * scale_ref[...]).astype(BF16))
+        out_ref[:, columns] = result.astype(BF16)
+        term = jnp.sum(result * weight_ref[:, columns].astype(F32), axis=1, keepdims=True)
+        dots = term if dots is None else dots + term
+    dot_ref[...] = dots
+    left = jnp.concatenate([d_own[...], d_other[...]], axis=1)
+    out_ref[:, 3 * part :] = tn(left, mixed_ref[...]).astype(BF16)
+
+
+def heads_outer(feat, x_own, x_other, d_own, d_other, dq, dk, dv, mixed, scale, weight):
+    tokens, half = x_own.shape
+    part = mixed.shape[1]
+    side = pl.BlockSpec((tokens, feat), lambda i: (0, i))
+    return pl.pallas_call(
+        heads_outer_kernel,
+        grid=(half // feat,),
+        in_specs=[side] * 4
+        + [whole_spec(a) for a in (dq, dk, dv, mixed, scale)]
+        + [row_spec(2 * feat, weight)],
+        out_specs=[pl.BlockSpec((2 * feat, 4 * part), lambda i: (i, 0)), pl.BlockSpec((2 * feat, 1), lambda i: (i, 0))],
+        out_shape=[
+            jax.ShapeDtypeStruct((2 * half, 4 * part), BF16),
+            jax.ShapeDtypeStruct((2 * half, 1), F32),
+        ],
+        compiler_params=pltpu.CompilerParams(vmem_limit_bytes=VMEM_BYTES),
+        name="heads_outer",
+    )(x_own, x_other, d_own, d_other, dq, dk, dv, mixed, scale, weight)
+
+
+def finish_kernel(core_ref, part_ref, gain_ref, *outs):
+    feat = gain_ref.shape[0] // 2
+    blocks, columns = part_ref.shape[0], part_ref.shape[2]
+    width = blocks * columns // len(outs)
+    for block in range(blocks):
+        at = block * columns
+        for side in range(2):
+            rows = slice(side * feat, (side + 1) * feat)
+            start = pl.multiple_of(lax.rem(core_ref[0] + side, 2) * feat, feat)
+            value = part_ref[block, pl.ds(start, feat), :].astype(F32) * gain_ref[rows, :]
+            outs[at // width][rows, at % width : at % width + columns] = value
+
+
+def finish(core, part, gain, count=1):
+    blocks, rows, columns = part.shape
+    vmem = pl.BlockSpec(memory_space=pltpu.VMEM)
+    result = jax.ShapeDtypeStruct((rows, blocks * columns // count), F32)
+    return pl.pallas_call(
+        finish_kernel,
+        in_specs=[pl.BlockSpec(memory_space=pltpu.SMEM), vmem, vmem],
+        out_specs=[vmem] * count,
+        out_shape=[result] * count,
+        compiler_params=pltpu.CompilerParams(vmem_limit_bytes=VMEM_BYTES),
+        name="finish",
+    )(core, part, gain)
 
 
 def fold_kernel(feat, own_ref, other_ref, weight_ref, out_ref):
@@ -245,7 +326,7 @@
         in_specs=[row_spec(block, own), row_spec(block, other), whole_spec(weight)],
         out_specs=row_spec(block, result),
         out_shape=result,
-        compiler_params=pltpu.CompilerParams(vmem_limit_bytes=40 * 1024 * 1024),
+        compiler_params=pltpu.CompilerParams(vmem_limit_bytes=VMEM_BYTES),
         name="fold",
     )(own, other, weight)
 
@@ -444,27 +525,19 @@
             bit //= 2
         return [got[step] for step in range(rows)]
 
-    def reduce_row(parts):
-        parts, bit = list(parts), 1
+    def reduce_row_traced(parts):
+        parts, sends, bit = list(parts), [], 1
         while bit < rows:
-            for at in range(0, rows, 2 * bit):
-                sent = row_swap(parts[at + bit].astype(BF16), bit)
-                parts[at] = parts[at].astype(F32) + sent.astype(F32)
+            for at in range(rows - 2 * bit, -1, -2 * bit):
+                low = parts[at + bit].astype(BF16)
+                sends.append(low)
+                parts[at] = parts[at].astype(F32) + row_swap(low, bit).astype(F32)
             bit *= 2
-        return parts[0]
+        return parts[0], sends
 
     def row_part(a, step):
         size = a.shape[0] // rows
         return lax.dynamic_slice_in_dim(a, (row ^ step) * size, size, 0)
-
-    def join_rows(pieces, axis=0, dtype=BF16):
-        size = pieces[0].shape[axis]
-        shape = list(pieces[0].shape)
-        shape[axis] *= rows
-        whole = jnp.zeros(shape, dtype)
-        for step, piece in enumerate(pieces):
-            whole = lax.dynamic_update_slice_in_dim(whole, piece, (row ^ step) * size, axis)
-        return whole
 
     def after(value, *others):
         return lax.optimization_barrier((value,) + others)[0]
@@ -528,29 +601,34 @@
             jnp.concatenate([plane_swap(second[:half], 1), plane_swap(first[half:], 2)], axis=0),
         ]
 
-    def give_back(pieces):
+    def plane_sum(pieces, *hold):
         if places != 4:
             total = pieces[0].astype(F32)
             for s in range(1, places):
                 total = total + plane_swap(pieces[s], s).astype(F32)
-        else:
-            to_second = pieces[2].astype(F32) + jnp.concatenate(
-                [plane_swap(pieces[3][:half], 1), jnp.zeros_like(pieces[3][half:])], axis=0
-            ).astype(F32)
-            to_first = pieces[1].astype(F32) + jnp.concatenate(
-                [jnp.zeros_like(pieces[3][:half]), plane_swap(pieces[3][half:], 2)], axis=0
-            ).astype(F32)
-            total = (
-                pieces[0].astype(F32)
-                + plane_swap(to_first.astype(BF16), 1).astype(F32)
-                + plane_swap(to_second.astype(BF16), 2).astype(F32)
-            )
-        total = total.astype(BF16).reshape(rows, 2 * feat, pieces[0].shape[1])
-        total = lax.all_to_all(total, "row", split_axis=0, concat_axis=0, tiled=True).astype(F32)
-        return jnp.concatenate([own_first(total[s]) for s in range(rows)], axis=1)
-
-    def give_rows(w):
-        return own_first(lax.psum_scatter(w, "row", scatter_dimension=0, tiled=True)).astype(F32)
+            return total.astype(BF16)
+        top, bottom = plane_swap(pieces[3][:half], 1), plane_swap(pieces[3][half:], 2)
+        top, bottom = after(top, *hold), after(bottom, *hold)
+        to_second = jnp.concatenate(
+            [(pieces[2][:half].astype(F32) + top.astype(F32)).astype(BF16), pieces[2][half:]], axis=0
+        )
+        to_first = jnp.concatenate(
+            [pieces[1][:half], (pieces[1][half:].astype(F32) + bottom.astype(F32)).astype(BF16)], axis=0
+        )
+        total = (
+            pieces[0].astype(F32)
+            + plane_swap(to_first, 1).astype(F32)
+            + plane_swap(to_second, 2).astype(F32)
+        )
+        return total.astype(BF16)
+
+    def give_back(total):
+        total = total.reshape(rows, 2 * feat, total.shape[1])
+        return lax.all_to_all(total, "row", split_axis=0, concat_axis=0, tiled=True)
+
+    starts = jnp.stack([row ^ s for s in range(rows)])
+    cores = core.reshape(1)
+    ones = jnp.ones((2 * feat, 1), F32)
 
     with jax.named_scope("gather_qkv"):
         qkv_full = lax.all_gather(
@@ -562,16 +640,17 @@
             tiled=True,
         )
         out_full = lax.all_gather(own_first(out_weight), "row", axis=0, tiled=True)
+    with jax.named_scope("grad_plane"):
+        g_part = to_parts(out_grad)
     with jax.named_scope("gate_row"):
-        gate_whole = exchange(scaled(gate_weight, gain_two))
+        gate_whole = exchange(after(scaled(gate_weight, gain_two), g_part))
     with jax.named_scope("up_row"):
         up_whole = exchange(after(scaled(up_weight, gain_two), gate_whole))
     with jax.named_scope("down_row"):
         down_whole = exchange(after(own_first(down_weight), up_whole))
-    with jax.named_scope("grad_plane"):
-        g_part = to_parts(after(out_grad, down_whole))
     with jax.named_scope("grad_row"):
-        g_list = gather_row(g_part)
+        g_own = lax.all_gather(after(g_part, out_full), "row", axis=0, tiled=True)
+        g_other = core_swap(g_own)
     with jax.named_scope("gate_plane"):
         gates = spread_weights(gate_whole)
     with jax.named_scope("up_plane"):
@@ -585,21 +664,20 @@
     start_row = jnp.sum(
         (segment_ids[None, :] < segment_ids[:, None]).astype(jnp.int32), axis=1
     )[None, :]
-    x_ready = after(x_own, gates[1], gates[2])
+    x_ready = after(x_own, gates[1], gates[2], up_whole)
     query, key, value, scale_one = project(feat, x_ready, x_other, qkv_full, cosine, front, back)
     mixed, logs = attend(query, key, value, start_row)
-    mixed = after(mixed, up_whole, gates[3])
+    mixed = after(mixed, gates[3], ups[1], ups[2], down_whole)
 
     def scatter_parts(own, other):
-        own = own + core_swap(other).astype(F32)
-        low = own.astype(BF16)
-        total = token_part(own, 0)
+        low = (own.astype(F32) + core_swap(other).astype(F32)).astype(BF16)
+        total = token_part(low, 0).astype(F32)
         for s in range(1, places):
             total = total + plane_swap(token_part(low, s), s).astype(F32)
         return total
 
     with jax.named_scope("mix_plane"):
-        middle = token_part(x_own, 0).astype(F32) + scatter_parts(*unfold(feat, "mix", (mixed, [out_full])))
+        middle = token_part(x_own, 0).astype(F32) + scatter_parts(*unfold(feat, "mix", [mixed], [out_full]))
     square = jnp.sum(middle * middle, axis=1, keepdims=True)
     square = square + core_swap(square)
     scale_mid = lax.rsqrt(square / width + EPS)
@@ -607,32 +685,26 @@
     with jax.named_scope("down_plane"):
         downs = spread_weights(after(down_whole, middle))
     with jax.named_scope("middle_row"):
-        m_list = gather_row(after(middle.astype(BF16), ups[1], ups[2]))
+        m_list = gather_row(after(middle.astype(BF16), ups[3]))
         m_others = [core_swap(m) for m in m_list]
-    with jax.named_scope("grad_core"):
-        g_others = [core_swap(g) for g in g_list]
     found, own_shares, other_shares = [], [], []
     for at in range(0, rows, 2):
         pick = slice(at, at + 2)
         *three, owns, others = units(
-            feat, m_list[pick], m_others[pick], g_list[pick], g_others[pick], gates, ups, downs
+            feat, starts[pick], m_list[pick], m_others[pick], g_own, g_other, gates, ups, downs
         )
         found.append(three)
         own_shares += owns
         other_shares += others
     with jax.named_scope("unit_grad"):
-        shares = [own + core_swap(other).astype(F32) for own, other in zip(own_shares, other_shares)]
-        last = shares[-1]
-        unit_grad = reduce_row(shares)
-    with jax.named_scope("feed"):
-        shares = []
-        for hidden, _, _ in found:
-            own, other = unfold(feat, "feed", (after(hidden, last), downs))
-            own = own + core_swap(other).astype(F32)
-            shares += [own[:quarter], own[quarter:]]
-        feed = reduce_row([after(a, unit_grad) for a in shares])
-    with jax.named_scope("block_out"):
-        block_out = to_home((middle + feed).astype(BF16))
+        unit_grad, sums = reduce_row_traced(
+            [own.astype(F32) + core_swap(other).astype(F32) for own, other in zip(own_shares, other_shares)]
+        )
+    with jax.named_scope("down_grad"):
+        down_total = plane_sum(
+            outer(feat, "down_outer", starts, [g_own], [g_other], [after(f[0], *sums[:2]) for f in found], places)
+        )
+        down_blocks = give_back(down_total)
 
     unit_mid = middle * scale_mid
     dot_two = jnp.sum(unit_grad * unit_mid, axis=1, keepdims=True)
@@ -640,26 +712,39 @@
     middle_grad = g_part.astype(F32) + scale_mid * (unit_grad - unit_mid * (dot_two / width))
 
     with jax.named_scope("middle_grad"):
-        d_own = put_rows(spread(middle_grad.astype(BF16)))
+        d_low = middle_grad.astype(BF16)
+        d_own = put_rows(spread(d_low))
         d_other = core_swap(d_own)
-    mixed_grad = fold(feat, d_own, d_other, out_full)
+    with jax.named_scope("feed"):
+        shares = []
+        for hidden, _, _ in found:
+            own, other = unfold(feat, "feed", [after(hidden, d_low)], downs)
+            low = own.astype(F32) + core_swap(other).astype(F32)
+            shares += [low[:quarter], low[quarter:]]
+        feed, _ = reduce_row_traced(shares)
+    gate_parts = outer(feat, "gate_outer", starts, m_list, m_others, [after(f[1], d_low) for f in found], places)
+    up_parts = outer(feat, "up_outer", starts, m_list, m_others, [after(f[2], d_low) for f in found], places)
+    mixed_grad = fold(feat, after(d_own, gate_parts[0], up_parts[0]), d_other, out_full)
+    with jax.named_scope("gate_grad"):
+        gate_total = plane_sum([after(a, d_own) for a in gate_parts], mixed_grad)
+        gate_blocks = give_back(gate_total)
     query_grad, key_grad, value_grad = attend_back(
         query, key, value, mixed, mixed_grad, start_row, logs, cosine, front, back
     )
-    grads = jnp.concatenate([query_grad, key_grad, value_grad], axis=1)
-    grads_scaled = (grads.astype(F32) * scale_one).astype(BF16)
-    qkv_part = outer(feat, "qkv_outer", [x_own], [x_other], [grads_scaled])[0]
-    with jax.named_scope("qkv_grad"):
-        qkv_grad = give_rows(qkv_part)
-    with jax.named_scope("first_gain"):
-        gain_dots = jnp.sum(qkv_part.astype(F32) * qkv_full.astype(F32), axis=1).reshape(rows, 2, feat)
-        gain_dots = sum_cols(jnp.where(core == 0, gain_dots, gain_dots[:, ::-1]).reshape(width))
-        gain_row = row_part(gain_dots, 0) + sum(
-            row_swap(row_part(gain_dots, s), s) for s in range(1, rows)
-        )
-        first_gain_grad = gain_row / gain_one[:, 0]
+    heads_part, gain_dots = heads_outer(
+        feat, x_own, x_other, d_own, d_other, query_grad, key_grad, value_grad, mixed, scale_one, qkv_full
+    )
+    with jax.named_scope("heads_grad"):
+        heads_blocks = lax.psum_scatter(heads_part, "row", scatter_dimension=0, tiled=True)
+    with jax.named_scope("up_grad"):
+        up_total = plane_sum([after(a, gate_total) for a in up_parts], heads_part)
+        up_blocks = give_back(up_total)
+    with jax.named_scope("block_out"):
+        block_out = to_home(after((middle + feed).astype(BF16), heads_part))
     with jax.named_scope("first_plane"):
-        first_unit_grad = scatter_parts(*unfold(feat, "first_grad", (after(grads, qkv_part), [qkv_full])))
+        first_unit_grad = scatter_parts(
+            *unfold(feat, "first_grad", [after(query_grad, heads_part), key_grad, value_grad], [qkv_full])
+        )
     scale_first = token_part(scale_one, 0)
     unit_first = token_part(x_own, 0).astype(F32) * scale_first
     dot_one = jnp.sum(first_unit_grad * unit_first, axis=1, keepdims=True)
@@ -669,35 +754,35 @@
             (middle_grad + scale_first * (first_unit_grad - unit_first * (dot_one / width))).astype(BF16)
         )
 
-    with jax.named_scope("out_grad"):
-        out_weight_grad = give_rows(outer(feat, "out_outer", [d_own], [d_other], [mixed])[0])
-    with jax.named_scope("down_grad"):
-        down_weight_grad = give_back(
-            outer(feat, "down_outer", g_list, g_others, [after(f[0], last) for f in found], places)
-        )
-    with jax.named_scope("gate_grad"):
-        gate_parts = outer(feat, "gate_outer", m_list, m_others, [after(f[1], last) for f in found], places)
-        gate_unit = give_back([after(a, d_own) for a in gate_parts])
-    with jax.named_scope("up_grad"):
-        up_parts = outer(feat, "up_outer", m_list, m_others, [after(f[2], last) for f in found], places)
-        up_unit = give_back([after(a, d_own, mixed_grad) for a in up_parts])
-    q_unit = qkv_grad[:, :heads_width]
-    k_unit = qkv_grad[:, heads_width : 2 * heads_width]
-    v_unit = qkv_grad[:, 2 * heads_width :]
-
-    def row_dots(*pairs):
-        return sum(jnp.sum(w.astype(F32) * d, axis=1) for w, d in pairs)
-
-    second_gain_grad = sum_cols(row_dots((gate_weight, gate_unit), (up_weight, up_unit)))
+    def row_dots(w, d):
+        return jnp.sum(w.astype(F32) * d.astype(F32), axis=1)
+
+    with jax.named_scope("gains"):
+        dots = jnp.stack(
+            [gain_dots[:, 0], row_dots(gates[0], gate_total) + row_dots(ups[0], up_total)]
+        ).reshape(2, rows, 2, feat)
+        dots = sum_cols(jnp.where(core == 0, dots, dots[:, :, ::-1])).transpose(1, 0, 2, 3)
+        dots = dots.reshape(rows, 2, 2 * feat)
+        mine = lax.dynamic_index_in_dim(dots, row, 0, False)
+        for s in range(1, rows):
+            mine = mine + row_swap(lax.dynamic_index_in_dim(dots, row ^ s, 0, False), s)
+        first_gain_grad = mine[0] / gain_one[:, 0]
+        second_gain_grad = mine[1] / gain_two[:, 0]
+    (down_weight_grad,) = finish(cores, down_blocks, ones)
+    (gate_weight_grad,) = finish(cores, gate_blocks, gain_two)
+    (up_weight_grad,) = finish(cores, up_blocks, gain_two)
+    part = query_weight.shape[1]
+    (qkv_grad,) = finish(cores, heads_blocks[None, :, : 3 * part], gain_one)
+    (out_weight_grad,) = finish(cores, heads_blocks[None, :, 3 * part :], ones)
     return (
         block_out,
         input_grad,
-        q_unit * gain_one,
-        k_unit * gain_one,
-        v_unit * gain_one,
+        qkv_grad[:, :part],
+        qkv_grad[:, part : 2 * part],
+        qkv_grad[:, 2 * part :],
         out_weight_grad,
-        gate_unit * gain_two,
-        up_unit * gain_two,
+        gate_weight_grad,
+        up_weight_grad,
         down_weight_grad,
         first_gain_grad,
         second_gain_grad,

time: 721 us -> 771 us (1.069)
  waiting for transfers between devices: 295 us -> 359 us
  Pallas kernels: 121 us -> 159 us
  other arithmetic: 89.6 us -> 64.5 us
  starting transfers between devices: 121 us -> 96.3 us
    all_to_all x3, waiting for transfers between devices: 24.1 us -> 61.5 us  [exchange(): lax.all_to_all(pieces, 'row', split_axis=0, concat_axis=0, tiled=True)]
    ppermute x36, waiting for transfers between devices: 78 us -> 111 us  [plane_swap(): return lax.ppermute(a, 'col', [(i, i ^ 2 * step) for i in range(cols)])]
    ppermute x15 -> x12, waiting for transfers between devices: 121 us -> 155 us  [row_swap(): return lax.ppermute(a, 'row', [(i, i ^ step) for i in range(rows)])]
    convert_element_type x22 -> x15, other arithmetic: 43.7 us -> 16.2 us  [the longest x2 3.51 us: scatter_parts(): low = (own.astype(F32) + core_swap(other).astype(F32)).astype(BF16)]
    pallas_call x4 -> x10, Pallas kernels: 25.5 us -> 49.9 us  [the longest x4 25.3 us: unfold(): pl.pallas_call(functools.partial(unfold_kernel, feat, len(lefts)), grid=(...]
    unnamed x156 -> x103, local copies, waits for them, and re-layouts: 33.1 us -> 11.6 us
    all_to_all x3, waiting for transfers between devices: 20.7 us -> 0.01 us  [give_back(): return lax.all_to_all(total, 'row', split_axis=0, concat_axis=0, tiled=True)]
    ppermute x6 -> x3, waiting for transfers between devices: 22.6 us -> 6.33 us  [sum_cols(): a = a + lax.ppermute(a, 'col', [(i, i ^ step) for i in range(cols)])]
  transfers between devices with their start and end apart: 91 -> 82, of which waited for: 34 -> 36; matrix products, arithmetic and copies ran while one was open for 17% -> 15% of each run, Pallas kernels for 16% -> 20%
where the time goes in v4:
time: 771 us; the launch traced here: 760 us
  waiting for transfers between devices  359 us (47%)
  Pallas kernels  159 us (21%)
  starting transfers between devices  96.3 us (12%)
  local copies, waits for them, and re-layouts  65.6 us (9%)
  other arithmetic  64.5 us (8%)
  between operations  15.4 us (2%)
    ppermute x12, waiting for transfers between devices, row_swap(): return lax.ppermute(a, 'row', [(i, i ^ step) for i in range(rows)])  155 us
    ppermute x36, waiting for transfers between devices, plane_swap(): return lax.ppermute(a, 'col', [(i, i ^ 2 * step) for i in range(cols)])  111 us
    all_to_all x3, waiting for transfers between devices, exchange(): lax.all_to_all(pieces, 'row', split_axis=0, concat_axis=0, tiled=True)  61.5 us
    pallas_call x2, Pallas kernels, units(): pl.pallas_call(functools.partial(units_kernel, feat, parts, count), in_sp...  49.6 us
    ppermute x36, starting transfers between devices, plane_swap(): return lax.ppermute(a, 'col', [(i, i ^ 2 * step) for i in range(cols)])  42.5 us
    pallas_call x4, Pallas kernels, unfold(): pl.pallas_call(functools.partial(unfold_kernel, feat, len(lefts)), grid=(...  25.3 us
    pallas_call x3, Pallas kernels, outer(): pl.pallas_call(functools.partial(outer_kernel, len(owns), count), grid=(h...  24.8 us
  transfers between devices with their start and end apart: 82, of which 36 were waited for; matrix products, arithmetic and copies ran while one was open for 15% of the time, Pallas kernels for 20%

profile of v4, /device:TPU:0, one launch (start us, length us, event | category | flops | bytes accessed | tf_op | source)
XLA Modules:
  0.0 759.6 jit_solution(17038653616757553664)
XLA Ops:
  7.2 5.3 all-to-all-start
  18.1 2.4 all-to-all-done
  22.6 4.9 all-to-all-start.1
  28.7 51.6 %all-to-all-done.1 = bf16[4,512,256]{2,1,0:T(8,128)(2,1)} async-done(((bf16[4,512,256]{2,1,0:T(8,128)(2,1)}), bf16[4,512,256]{2,1,0:T(8,128)(2,1)}, u32[]{:S(2)}, u32[]{:S(2)}) %all-to-all-start.1) | async-done | bytes 1048608 | tf_op jit(solution)/shard_map/gate_row/all_to_all | solution.py:591
  81.5 5.5 all-to-all-start.2
  91.9 10.2 %collective-permute-done = bf16[1024,256]{1,0:T(8,128)(2,1)} collective-permute-done((bf16[1024,256]{1,0:T(8,128)(2,1)}, bf16[1024,256]{1,0:T(8,128)(2,1)}, u32[]{:S(2)}, u32[]{:S(2)}) %collective-permute-start) | collective-permute-done | bytes 524320 | tf_op jit(solution)/shard_map/inputs/ppermute | solution.py:504
  104.3 5.0 collective-permute-done.2
  112.6 2.6 collective-permute-start.3
  115.2 9.9 %all-to-all-done.2 = bf16[4,512,256]{2,1,0:T(8,128)(2,1)S(1)} async-done(((bf16[4,512,256]{2,1,0:T(8,128)(2,1)}), bf16[4,512,256]{2,1,0:T(8,128)(2,1)S(1)}, u32[]{:S(2)}, u32[]{:S(2)}) %all-to-all-start.2) | async-done | bytes 1048608 | tf_op jit(solution)/shard_map/up_row/all_to_all | solution.py:591
  127.9 3.6 all-to-all-start.3
  135.4 2.7 collective-permute-done.4.refs_12_
  147.6 2.6 copy.34.front_ref
  152.2 2.6 copy.35.back_ref
  156.8 2.5 copy.33.cos_ref
  160.6 12.1 %collective-permute-done.6 = bf16[1024,256]{1,0:T(8,128)(2,1)} collective-permute-done((bf16[1024,256]{1,0:T(8,128)(2,1)}, bf16[1024,256]{1,0:T(8,128)(2,1)}, u32[]{:S(2)}, u32[]{:S(2)}) %collective-permute-start.6) | collective-permute-done | bytes 524320 | tf_op jit(solution)/shard_map/gate_plane/ppermute | solution.py:504
  176.4 8.5 %project.1 = (bf16[1024,256]{1,0:T(8,128)(2,1)}, bf16[1024,256]{1,0:T(8,128)(2,1)}, bf16[1024,256]{1,0:T(8,128)(2,1)}, f32[1024,1]{1,0:T(8,128)}) custom-call(bf16[1024,1024]{1,0:T(8,128)(2,1)} %copy-done, bf16[1024,1024]{1,0:T(8,128)(2,1)} %collective-permute-done.5.other_ref.x_other, bf16[2048,768]{1,0:T(8,128)(2,1)} %all-gather.4.cloned.1.call-done.weight_ref.refs_3_, ...), custom_call_target="tpu_custom_call" | custom-call | tf_op jit(solution)/shard_map/project/pallas_call | solution.py:83
  184.9 10.0 %attend.1 = (bf16[1024,256]{1,0:T(8,128)(2,1)}, f32[2,2,1024]{2,1,0:T(2,128)}) custom-call(bf16[1024,256]{1,0:T(8,128)(2,1)} %get-tuple-element.90.q_ref, bf16[1024,256]{1,0:T(8,128)(2,1)} %get-tuple-element.91.k_ref, bf16[1024,256]{1,0:T(8,128)(2,1)} %get-tuple-element.92.v_ref, s32[1,1024]{1,0:T(1,128)} %bitcast.125), custom_call_target="tpu_custom_call" | custom-call | tf_op jit(solution)/shard_map/attend/pallas_call | solution.py:373
  194.9 5.4 mix.1
  200.6 4.1 collective-permute-done.10
  204.7 2.5 add_convert_fusion.1
  217.2 5.0 collective-permute-done.11
  222.2 13.0 %collective-permute-done.12 = bf16[256,1024]{1,0:T(8,128)(2,1)S(1)} collective-permute-done((bf16[256,1024]{1,0:T(8,128)(2,1)S(1)}, bf16[256,1024]{1,0:T(8,128)(2,1)S(1)}, u32[]{:S(2)}, u32[]{:S(2)}) %collective-permute-start.12) | collective-permute-done | bytes 524320 | tf_op jit(solution)/shard_map/mix_plane/ppermute | solution.py:504
  237.6 9.7 %all-gather.8.cloned.1.call-done.refs_4_.refs_0_ = bf16[1024,1024]{1,0:T(8,128)(2,1)} async-done(((bf16[256,1024]{1,0:T(8,128)(2,1)}), bf16[1024,1024]{1,0:T(8,128)(2,1)}) %all-gather.8.cloned.1.call-update) | async-done | bytes 2097168 | tf_op jit(solution)/shard_map/grad_row/all_gather | solution.py:652
  254.5 24.8 %collective-permute-done.28.refs_0_.refs_2_ = bf16[256,1024]{1,0:T(8,128)(2,1)} collective-permute-done((bf16[256,1024]{1,0:T(8,128)(2,1)}, bf16[256,1024]{1,0:T(8,128)(2,1)}, u32[]{:S(2)}, u32[]{:S(2)}) %collective-permute-start.28) | collective-permute-done | bytes 524320 | tf_op jit(solution)/shard_map/middle_row/ppermute | solution.py:518
  285.2 9.1 %collective-permute-done.29.refs_1_.refs_3_ = bf16[256,1024]{1,0:T(8,128)(2,1)} collective-permute-done((bf16[256,1024]{1,0:T(8,128)(2,1)}, bf16[256,1024]{1,0:T(8,128)(2,1)}, u32[]{:S(2)}, u32[]{:S(2)}) %collective-permute-start.29) | collective-permute-done | bytes 524320 | tf_op jit(solution)/shard_map/middle_row/ppermute | solution.py:518
  296.5 8.1 %collective-permute-done.16.refs_1_ = bf16[256,1024]{1,0:T(8,128)(2,1)} collective-permute-done((bf16[256,1024]{1,0:T(8,128)(2,1)}, bf16[256,1024]{1,0:T(8,128)(2,1)}, u32[]{:S(2)}, u32[]{:S(2)}) %collective-permute-start.16) | collective-permute-done | bytes 524320 | tf_op jit(solution)/shard_map/middle_row/ppermute | solution.py:518
  307.2 24.9 %units.3 = (bf16[512,1024]{1,0:T(8,128)(2,1)}, bf16[512,1024]{1,0:T(8,128)(2,1)}, bf16[512,1024]{1,0:T(8,128)(2,1)}, bf16[256,1024]{1,0:T(8,128)(2,1)}, bf16[256...) custom-call(s32[2]{0:T(128)} %pad_add_fusion.1.starts, ...), custom_call_target="tpu_custom_call" | custom-call | tf_op jit(solution)/shard_map/units/pallas_call | solution.py:198
  332.9 24.7 %units.2 = (bf16[512,1024]{1,0:T(8,128)(2,1)}, bf16[512,1024]{1,0:T(8,128)(2,1)}, bf16[512,1024]{1,0:T(8,128)(2,1)}, bf16[256,1024]{1,0:T(8,128)(2,1)}, bf16[256...) custom-call(s32[2]{0:T(128)} %pad_add_fusion.starts, ...), custom_call_target="tpu_custom_call" | custom-call | tf_op jit(solution)/shard_map/units/pallas_call | solution.py:198
  362.1 11.2 %collective-permute-done.34 = bf16[256,1024]{1,0:T(8,128)(2,1)S(1)} collective-permute-done((bf16[256,1024]{1,0:T(8,128)(2,1)S(1)}, bf16[256,1024]{1,0:T(8,128)(2,1)S(1)}, u32[]{:S(2)}, u32[]{:S(2)}) %collective-permute-start.34) | collective-permute-done | bytes 524320 | tf_op jit(solution)/shard_map/unit_grad/ppermute | solution.py:518
  374.9 16.4 %collective-permute-done.27 = bf16[256,1024]{1,0:T(8,128)(2,1)S(1)} collective-permute-done((bf16[256,1024]{1,0:T(8,128)(2,1)S(1)}, bf16[256,1024]{1,0:T(8,128)(2,1)S(1)}, u32[]{:S(2)}, u32[]{:S(2)}) %collective-permute-start.27) | collective-permute-done | bytes 524320 | tf_op jit(solution)/shard_map/unit_grad/ppermute | solution.py:518
  391.3 7.6 collective-permute-done.35
  405.7 11.3 %collective-permute-done.42 = bf16[256,1024]{1,0:T(8,128)(2,1)S(1)} collective-permute-done((bf16[256,1024]{1,0:T(8,128)(2,1)S(1)}, bf16[256,1024]{1,0:T(8,128)(2,1)S(1)}, u32[]{:S(2)}, u32[]{:S(2)}) %collective-permute-start.42) | collective-permute-done | bytes 524320 | tf_op jit(solution)/shard_map/middle_grad/ppermute | solution.py:504
  417.0 9.7 %collective-permute-done.43 = bf16[256,1024]{1,0:T(8,128)(2,1)S(1)} collective-permute-done((bf16[256,1024]{1,0:T(8,128)(2,1)S(1)}, bf16[256,1024]{1,0:T(8,128)(2,1)S(1)}, u32[]{:S(2)}, u32[]{:S(2)}) %collective-permute-start.43) | collective-permute-done | bytes 524320 | tf_op jit(solution)/shard_map/middle_grad/ppermute | solution.py:504
  429.3 8.0 %down_outer.1 = (bf16[2048,256]{1,0:T(8,128)(2,1)}, bf16[2048,256]{1,0:T(8,128)(2,1)}, bf16[2048,256]{1,0:T(8,128)(2,1)}, bf16[2048,256]{1,0:T(8,128)(2,1)}) custom-call(s32[4]{0:T(128)} %pad_add_fusion.2.starts, bf16[1024,1024]{1,0:T(8,128)(2,1)} %all-gather.8.cloned.1.call-done.refs_4_.refs_0_, bf16[1024,1024]{1,0:T(8,128)(2,1)} %collective-permute-done.19.refs_5_.refs_1_, ...), custom_call_target="tpu_custom_call" | custom-call | tf_op jit(solution)/shard_map/down_grad/down_outer/pallas_call | solution.py:240
  443.1 10.7 %collective-permute-done.59 = bf16[1024,256]{1,0:T(8,128)(2,1)S(1)} collective-permute-done((bf16[1024,256]{1,0:T(8,128)(2,1)S(1)}, bf16[1024,256]{1,0:T(8,128)(2,1)S(1)}, u32[]{:S(2)}, u32[]{:S(2)}) %collective-permute-start.59) | collective-permute-done | bytes 524320 | tf_op jit(solution)/shard_map/down_grad/ppermute | solution.py:504
  453.8 6.1 feed.3
  464.4 8.3 %gate_outer.1 = (bf16[2048,256]{1,0:T(8,128)(2,1)}, bf16[2048,256]{1,0:T(8,128)(2,1)}, bf16[2048,256]{1,0:T(8,128)(2,1)}, bf16[2048,256]{1,0:T(8,128)(2,1)}) custom-call(s32[4]{0:T(128)} %pad_add_fusion.2.starts, bf16[256,1024]{1,0:T(8,128)(2,1)} %convert_element_type.295.refs_0_, bf16[256,1024]{1,0:T(8,128)(2,1)} %collective-permute-done.16.refs_1_, ...), custom_call_target="tpu_custom_call" | custom-call | tf_op jit(solution)/shard_map/gate_outer/pallas_call | solution.py:240
  478.1 5.9 feed.2
  484.0 8.5 %up_outer.1 = (bf16[2048,256]{1,0:T(8,128)(2,1)}, bf16[2048,256]{1,0:T(8,128)(2,1)}, bf16[2048,256]{1,0:T(8,128)(2,1)}, bf16[2048,256]{1,0:T(8,128)(2,1)}) custom-call(s32[4]{0:T(128)} %pad_add_fusion.2.starts, bf16[256,1024]{1,0:T(8,128)(2,1)} %convert_element_type.295.refs_0_, bf16[256,1024]{1,0:T(8,128)(2,1)} %collective-permute-done.16.refs_1_, ...), custom_call_target="tpu_custom_call" | custom-call | tf_op jit(solution)/shard_map/up_outer/pallas_call | solution.py:240
  495.4 5.0 fold.1.do_ref
  500.5 11.0 %attend_back.1 = (bf16[1024,256]{1,0:T(8,128)(2,1)}, bf16[1024,256]{1,0:T(8,128)(2,1)}, bf16[1024,256]{1,0:T(8,128)(2,1)}) custom-call(bf16[1024,256]{1,0:T(8,128)(2,1)} %get-tuple-element.90.q_ref, bf16[1024,256]{1,0:T(8,128)(2,1)} %get-tuple-element.91.k_ref, bf16[1024,256]{1,0:T(8,128)(2,1)} %get-tuple-element.92.v_ref, ...), custom_call_target="tpu_custom_call" | custom-call | tf_op jit(solution)/shard_map/attend_back/pallas_call | solution.py:442
  511.5 11.4 %heads_outer.1 = (bf16[2048,1024]{1,0:T(8,128)(2,1)}, f32[2048,1]{1,0:T(8,128)}) custom-call(bf16[1024,1024]{1,0:T(8,128)(2,1)} %copy-done, bf16[1024,1024]{1,0:T(8,128)(2,1)} %collective-permute-done.5.other_ref.x_other, bf16[1024,1024]{1,0:T(8,128)(2,1)} %copy-done.6, bf16[1024,1024]{1,0:T(8,128)(2,1)} %copy-done.10, ...), custom_call_target="tpu_custom_call" | custom-call | tf_op jit(solution)/shard_map/heads_outer/pallas_call | solution.py:272
  529.5 7.2 collective-permute-done.53
  540.0 3.0 add_convert_fusion.2
  543.0 4.2 all-to-all-start.8
  547.2 7.8 %first_grad.1 = (bf16[1024,1024]{1,0:T(8,128)(2,1)}, bf16[1024,1024]{1,0:T(8,128)(2,1)}) custom-call(bf16[1024,256]{1,0:T(8,128)(2,1)} %get-tuple-element.135.dq_ref.refs_0_, bf16[1024,256]{1,0:T(8,128)(2,1)} %get-tuple-element.130.dk_ref.refs_1_, bf16[1024,256]{1,0:T(8,128)(2,1)} %get-tuple-element.131.dv_ref.refs_2_, ...), custom_call_target="tpu_custom_call" | custom-call | tf_op jit(solution)/shard_map/first_plane/first_grad/pallas_call | solution.py:114
  558.7 12.5 %collective-permute-done.40 = bf16[256,1024]{1,0:T(8,128)(2,1)} collective-permute-done((bf16[256,1024]{1,0:T(8,128)(2,1)}, bf16[256,1024]{1,0:T(8,128)(2,1)}, u32[]{:S(2)}, u32[]{:S(2)}) %collective-permute-start.40) | collective-permute-done | bytes 524320 | tf_op jit(solution)/shard_map/feed/ppermute | solution.py:518
  572.5 3.5 multiply_reduce_fusion.1
  576.9 62.8 %collective-permute-done.38 = bf16[256,1024]{1,0:T(8,128)(2,1)S(1)} collective-permute-done((bf16[256,1024]{1,0:T(8,128)(2,1)S(1)}, bf16[256,1024]{1,0:T(8,128)(2,1)S(1)}, u32[]{:S(2)}, u32[]{:S(2)}) %collective-permute-start.38) | collective-permute-done | bytes 524320 | tf_op jit(solution)/shard_map/feed/ppermute | solution.py:518
  644.9 3.5 all-to-all-start.4
  656.9 5.5 all-to-all-done.4
  663.2 3.5 all-to-all-start.6
  673.8 11.7 %collective-permute-done.49 = bf16[256,1024]{1,0:T(8,128)(2,1)} collective-permute-done((bf16[256,1024]{1,0:T(8,128)(2,1)}, bf16[256,1024]{1,0:T(8,128)(2,1)}, u32[]{:S(2)}, u32[]{:S(2)}) %collective-permute-start.49) | collective-permute-done | bytes 524320 | tf_op jit(solution)/shard_map/first_plane/ppermute | solution.py:504
  692.4 3.5 all-to-all-start.5
  695.9 7.8 %collective-permute-done.56 = bf16[2048,256]{1,0:T(8,128)(2,1)} collective-permute-done((bf16[2048,256]{1,0:T(8,128)(2,1)}, bf16[2048,256]{1,0:T(8,128)(2,1)}, u32[]{:S(2)}, u32[]{:S(2)}) %collective-permute-start.56) | collective-permute-done | bytes 1048608 | tf_op jit(solution)/shard_map/up_grad/ppermute | solution.py:504
  703.7 3.4 multiply_reduce_fusion
  707.2 3.8 all-to-all-start.7
  713.6 2.6 collective-permute-done.64
  717.4 2.6 collective-permute-done.65
  727.0 2.9 finish.9
  730.0 2.9 finish.7
  737.3 2.9 finish.8
  742.3 2.5 finish.5
  744.8 2.6 fusion.14
  (353 shorter events, 176.9 us)
Async XLA Ops:
  12.5 163.9 %all-gather.4.cloned.1.call-start = ((), (), s32[]{:S(2)}) async-start(), calls=%async_computation.10 | async-start | bytes 3932160 | tf_op jit(solution)/shard_map/gather_qkv/all_gather | solution.py:634
  22.6 57.7 %all-to-all-start.1 = ((bf16[4,512,256]{2,1,0:T(8,128)(2,1)}), bf16[4,512,256]{2,1,0:T(8,128)(2,1)}, u32[]{:S(2)}, u32[]{:S(2)}) async-start(bf16[4,512,256]{2,1,0:T(8,128)(2,1)} %pad_maximum_fusion.1), calls=%async_computation.1 | async-start | bytes 2097152 | tf_op jit(solution)/shard_map/gate_row/all_to_all | solution.py:591
  81.5 43.6 %all-to-all-start.2 = ((bf16[4,512,256]{2,1,0:T(8,128)(2,1)}), bf16[4,512,256]{2,1,0:T(8,128)(2,1)S(1)}, u32[]{:S(2)}, u32[]{:S(2)}) async-start(bf16[4,512,256]{2,1,0:T(8,128)(2,1)} %pad_maximum_fusion.3), calls=%async_computation.2 | async-start | bytes 2097152 | tf_op jit(solution)/shard_map/up_row/all_to_all | solution.py:591
  86.9 15.2 %collective-permute-start = (bf16[1024,256]{1,0:T(8,128)(2,1)}, bf16[1024,256]{1,0:T(8,128)(2,1)}, u32[]{:S(2)}, u32[]{:S(2)}) collective-permute-start(bf16[1024,256]{1,0:T(8,128)(2,1)} %param.13), channel_id=1, source_target_pairs={{0,2},{1,3},{2,0},{3,1},{4,6},{5,7},{6,4},{7,5},{8,10},{9,11},{10,... | collective-permute-start | bytes 1572872 | tf_op jit(solution)/shard_map/inputs/ppermute | solution.py:504
  88.1 15.2 %collective-permute-start.1 = (bf16[1024,256]{1,0:T(8,128)(2,1)}, bf16[1024,256]{1,0:T(8,128)(2,1)}, u32[]{:S(2)}, u32[]{:S(2)}) collective-permute-start(bf16[1024,256]{1,0:T(8,128)(2,1)} %param.13), channel_id=1, source_target_pairs={{0,4},{1,5},{2,6},{3,7},{4,0},{5,1},{6,2},{7,3},{8,12},{9,13},{10,... | collective-permute-start | bytes 1572872 | tf_op jit(solution)/shard_map/inputs/ppermute | solution.py:504
  88.4 20.9 %collective-permute-start.2 = (bf16[1024,256]{1,0:T(8,128)(2,1)}, bf16[1024,256]{1,0:T(8,128)(2,1)}, u32[]{:S(2)}, u32[]{:S(2)}) collective-permute-start(bf16[1024,256]{1,0:T(8,128)(2,1)} %param.13), channel_id=1, source_target_pairs={{0,6},{1,7},{2,4},{3,5},{4,2},{5,3},{6,0},{7,1},{8,14},{9,15},{10,... | collective-permute-start | bytes 1572872 | tf_op jit(solution)/shard_map/inputs/ppermute | solution.py:504
  110.5 65.9 %collective-permute-start.5 = (bf16[1024,1024]{1,0:T(8,128)(2,1)S(1)}, bf16[1024,1024]{1,0:T(8,128)(2,1)}, u32[]{:S(2)}, u32[]{:S(2)}) collective-permute-start(bf16[1024,1024]{1,0:T(8,128)(2,1)S(1)} %constant_dynamic-update-slice_fusion.12.own_ref.x_own), channel_id=1, source_target_pairs={{0,1},{1,0},{2,3},{3,2},{4,5},{5,4},{6,7},{7,6},{8,9},{9,8},{10,11... | collective-permute-start | bytes 6291464 | tf_op jit(solution)/shard_map/inputs/ppermute | solution.py:501
  111.8 26.3 %collective-permute-start.4 = (bf16[2048,256]{1,0:T(8,128)(2,1)}, bf16[2048,256]{1,0:T(8,128)(2,1)}, u32[]{:S(2)}, u32[]{:S(2)}) collective-permute-start(bf16[2048,256]{1,0:T(8,128)(2,1)} %bitcast.9.refs_6_), channel_id=1, source_target_pairs={{0,4},{1,5},{2,6},{3,7},{4,0},{5,1},{6,2},{7,3},{8,12},{9,13},{10,... | collective-permute-start | bytes 3145736 | tf_op jit(solution)/shard_map/gate_plane/ppermute | solution.py:504
  112.6 29.6 %collective-permute-start.3 = (bf16[2048,256]{1,0:T(8,128)(2,1)}, bf16[2048,256]{1,0:T(8,128)(2,1)}, u32[]{:S(2)}, u32[]{:S(2)}) collective-permute-start(bf16[2048,256]{1,0:T(8,128)(2,1)} %bitcast.9.refs_6_), channel_id=1, source_target_pairs={{0,2},{1,3},{2,0},{3,1},{4,6},{5,7},{6,4},{7,5},{8,10},{9,11},{10,... | collective-permute-start | bytes 3145736 | tf_op jit(solution)/shard_map/gate_plane/ppermute | solution.py:504
  127.9 67.0 %all-to-all-start.3 = ((bf16[4,512,256]{2,1,0:T(8,128)(2,1)}), bf16[4,512,256]{2,1,0:T(8,128)(2,1)S(1)}, u32[]{:S(2)}, u32[]{:S(2)}) async-start(bf16[4,512,256]{2,1,0:T(8,128)(2,1)} %pad_maximum_fusion.5), calls=%async_computation.3 | async-start | bytes 2097152 | tf_op jit(solution)/shard_map/down_row/all_to_all | solution.py:591
  131.5 63.4 %all-gather.6.cloned.1.call-start = ((), (), s32[]{:S(2)}) async-start(), calls=%async_computation.11 | async-start | bytes 1310720 | tf_op jit(solution)/shard_map/gather_qkv/all_gather | solution.py:642
  133.3 114.0 %all-gather.8.cloned.1.call-start = ((), (), s32[]{:S(2)}) async-start(), calls=%async_computation.12 | async-start | bytes 2621440 | tf_op jit(solution)/shard_map/grad_row/all_gather | solution.py:652
  133.3 61.5 %collective-permute-start.8 = (bf16[2048,256]{1,0:T(8,128)(2,1)}, bf16[2048,256]{1,0:T(8,128)(2,1)}, u32[]{:S(2)}, u32[]{:S(2)}) collective-permute-start(bf16[2048,256]{1,0:T(8,128)(2,1)} %bitcast.110), channel_id=1, source_target_pairs={{0,2},{1,3},{2,0},{3,1},{4,6},{5,7},{6,4},{7,5},{8,10},{9,11},{10,... | collective-permute-start | bytes 3145736 | tf_op jit(solution)/shard_map/up_plane/ppermute | solution.py:504
  134.5 60.4 %collective-permute-start.9 = (bf16[2048,256]{1,0:T(8,128)(2,1)}, bf16[2048,256]{1,0:T(8,128)(2,1)}, u32[]{:S(2)}, u32[]{:S(2)}) collective-permute-start(bf16[2048,256]{1,0:T(8,128)(2,1)} %bitcast.111), channel_id=1, source_target_pairs={{0,4},{1,5},{2,6},{3,7},{4,0},{5,1},{6,2},{7,3},{8,12},{9,13},{10,... | collective-permute-start | bytes 3145736 | tf_op jit(solution)/shard_map/up_plane/ppermute | solution.py:504
  139.9 32.7 %collective-permute-start.6 = (bf16[1024,256]{1,0:T(8,128)(2,1)}, bf16[1024,256]{1,0:T(8,128)(2,1)}, u32[]{:S(2)}, u32[]{:S(2)}) collective-permute-start(bf16[1024,256]{1,0:T(8,128)(2,1)} %slice.326), channel_id=1, source_target_pairs={{0,2},{1,3},{2,0},{3,1},{4,6},{5,7},{6,4},{7,5},{8,10},{9,11},{10,... | collective-permute-start | bytes 1572872 | tf_op jit(solution)/shard_map/gate_plane/ppermute | solution.py:504
  144.0 30.5 %collective-permute-start.7 = (bf16[1024,256]{1,0:T(8,128)(2,1)}, bf16[1024,256]{1,0:T(8,128)(2,1)}, u32[]{:S(2)}, u32[]{:S(2)}) collective-permute-start(bf16[1024,256]{1,0:T(8,128)(2,1)} %slice.327), channel_id=1, source_target_pairs={{0,4},{1,5},{2,6},{3,7},{4,0},{5,1},{6,2},{7,3},{8,12},{9,13},{10,... | collective-permute-start | bytes 1572872 | tf_op jit(solution)/shard_map/gate_plane/ppermute | solution.py:504
  200.4 539.9 %reduce-scatter.2.cloned.1.call-start = ((), (), s32[]{:S(2)}) async-start(), calls=%async_computation.13 | async-start | bytes 5242880 | tf_op jit(solution)/shard_map/heads_grad/reduce_scatter | solution.py:738
  207.4 14.8 %collective-permute-start.11 = (bf16[256,1024]{1,0:T(8,128)(2,1)S(1)}, bf16[256,1024]{1,0:T(8,128)(2,1)S(1)}, u32[]{:S(2)}, u32[]{:S(2)}) collective-permute-start(bf16[256,1024]{1,0:T(8,128)(2,1)S(1)} %get-tuple-element.175), channel_id=1, source_target_pairs={{0,2},{1,3},{2,0},{3,1},{4,6},{5,7},{6,4},{7,5},{8,10},{9,11},{10,... | collective-permute-start | bytes 1572872 | tf_op jit(solution)/shard_map/mix_plane/ppermute | solution.py:504
  209.2 26.0 %collective-permute-start.12 = (bf16[256,1024]{1,0:T(8,128)(2,1)S(1)}, bf16[256,1024]{1,0:T(8,128)(2,1)S(1)}, u32[]{:S(2)}, u32[]{:S(2)}) collective-permute-start(bf16[256,1024]{1,0:T(8,128)(2,1)S(1)} %get-tuple-element.177), channel_id=1, source_target_pairs={{0,4},{1,5},{2,6},{3,7},{4,0},{5,1},{6,2},{7,3},{8,12},{9,13},{10,... | collective-permute-start | bytes 1572872 | tf_op jit(solution)/shard_map/mix_plane/ppermute | solution.py:504
  210.0 25.3 %collective-permute-start.13 = (bf16[256,1024]{1,0:T(8,128)(2,1)S(1)}, bf16[256,1024]{1,0:T(8,128)(2,1)S(1)}, u32[]{:S(2)}, u32[]{:S(2)}) collective-permute-start(bf16[256,1024]{1,0:T(8,128)(2,1)S(1)} %get-tuple-element.176), channel_id=1, source_target_pairs={{0,6},{1,7},{2,4},{3,5},{4,2},{5,3},{6,0},{7,1},{8,14},{9,15},{10,... | collective-permute-start | bytes 1572872 | tf_op jit(solution)/shard_map/mix_plane/ppermute | solution.py:504
  212.8 34.5 %collective-permute-start.14 = (bf16[1024,256]{1,0:T(8,128)(2,1)}, bf16[1024,256]{1,0:T(8,128)(2,1)}, u32[]{:S(2)}, u32[]{:S(2)}) collective-permute-start(bf16[1024,256]{1,0:T(8,128)(2,1)} %slice.328), channel_id=1, source_target_pairs={{0,2},{1,3},{2,0},{3,1},{4,6},{5,7},{6,4},{7,5},{8,10},{9,11},{10,... | collective-permute-start | bytes 1572872 | tf_op jit(solution)/shard_map/up_plane/ppermute | solution.py:504
  216.4 34.2 %collective-permute-start.15 = (bf16[1024,256]{1,0:T(8,128)(2,1)}, bf16[1024,256]{1,0:T(8,128)(2,1)}, u32[]{:S(2)}, u32[]{:S(2)}) collective-permute-start(bf16[1024,256]{1,0:T(8,128)(2,1)} %slice.329), channel_id=1, source_target_pairs={{0,4},{1,5},{2,6},{3,7},{4,0},{5,1},{6,2},{7,3},{8,12},{9,13},{10,... | collective-permute-start | bytes 1572872 | tf_op jit(solution)/shard_map/up_plane/ppermute | solution.py:504
  236.7 42.5 %collective-permute-start.21 = (bf16[2048,256]{1,0:T(8,128)(2,1)S(1)}, bf16[2048,256]{1,0:T(8,128)(2,1)S(1)}, u32[]{:S(2)}, u32[]{:S(2)}) collective-permute-start(bf16[2048,256]{1,0:T(8,128)(2,1)S(1)} %bitcast.104), channel_id=1, source_target_pairs={{0,4},{1,5},{2,6},{3,7},{4,0},{5,1},{6,2},{7,3},{8,12},{9,13},{10,... | collective-permute-start | bytes 3145736 | tf_op jit(solution)/shard_map/down_plane/ppermute | solution.py:504
  247.3 59.0 %collective-permute-start.19 = (bf16[1024,1024]{1,0:T(8,128)(2,1)}, bf16[1024,1024]{1,0:T(8,128)(2,1)}, u32[]{:S(2)}, u32[]{:S(2)}) collective-permute-start(bf16[1024,1024]{1,0:T(8,128)(2,1)} %all-gather.8.cloned.1.call-done.refs_4_.refs_0_), channel_id=1, source_target_pairs={{0,1},{1,0},{2,3},{3,2},{4,5},{5,4},{6,7},{7,6},{8,9},{9,8},{10,11... | collective-permute-start | bytes 6291464 | tf_op jit(solution)/shard_map/grad_row/ppermute | solution.py:501
  249.2 32.7 %collective-permute-start.20 = (bf16[2048,256]{1,0:T(8,128)(2,1)S(1)}, bf16[2048,256]{1,0:T(8,128)(2,1)S(1)}, u32[]{:S(2)}, u32[]{:S(2)}) collective-permute-start(bf16[2048,256]{1,0:T(8,128)(2,1)S(1)} %bitcast.105), channel_id=1, source_target_pairs={{0,2},{1,3},{2,0},{3,1},{4,6},{5,7},{6,4},{7,5},{8,10},{9,11},{10,... | collective-permute-start | bytes 3145736 | tf_op jit(solution)/shard_map/down_plane/ppermute | solution.py:504
  253.4 25.8 %collective-permute-start.28 = (bf16[256,1024]{1,0:T(8,128)(2,1)}, bf16[256,1024]{1,0:T(8,128)(2,1)}, u32[]{:S(2)}, u32[]{:S(2)}) collective-permute-start(bf16[256,1024]{1,0:T(8,128)(2,1)} %convert_element_type.295.refs_0_), channel_id=1, source_target_pairs={{0,16},{8,24},{16,0},{24,8},{1,17},{9,25},{17,1},{25,9},{2,18},{10... | collective-permute-start | bytes 1572872 | tf_op jit(solution)/shard_map/middle_row/ppermute | solution.py:518
  279.2 15.1 %collective-permute-start.29 = (bf16[256,1024]{1,0:T(8,128)(2,1)}, bf16[256,1024]{1,0:T(8,128)(2,1)}, u32[]{:S(2)}, u32[]{:S(2)}) collective-permute-start(bf16[256,1024]{1,0:T(8,128)(2,1)} %collective-permute-done.28.refs_0_.refs_2_), channel_id=1, source_target_pairs={{0,8},{8,0},{16,24},{24,16},{1,9},{9,1},{17,25},{25,17},{2,10},{10... | collective-permute-start | bytes 1572872 | tf_op jit(solution)/shard_map/middle_row/ppermute | solution.py:518
  279.3 15.1 %collective-permute-start.22 = (bf16[1024,256]{1,0:T(8,128)(2,1)S(1)}, bf16[1024,256]{1,0:T(8,128)(2,1)}, u32[]{:S(2)}, u32[]{:S(2)}) collective-permute-start(bf16[1024,256]{1,0:T(8,128)(2,1)S(1)} %slice.330), channel_id=1, source_target_pairs={{0,2},{1,3},{2,0},{3,1},{4,6},{5,7},{6,4},{7,5},{8,10},{9,11},{10,... | collective-permute-start | bytes 1572872 | tf_op jit(solution)/shard_map/down_plane/ppermute | solution.py:504
  279.9 24.7 %collective-permute-start.16 = (bf16[256,1024]{1,0:T(8,128)(2,1)}, bf16[256,1024]{1,0:T(8,128)(2,1)}, u32[]{:S(2)}, u32[]{:S(2)}) collective-permute-start(bf16[256,1024]{1,0:T(8,128)(2,1)} %convert_element_type.295.refs_0_), channel_id=1, source_target_pairs={{0,8},{8,0},{16,24},{24,16},{1,9},{9,1},{17,25},{25,17},{2,10},{10... | collective-permute-start | bytes 1572872 | tf_op jit(solution)/shard_map/middle_row/ppermute | solution.py:518
  283.7 20.9 %collective-permute-start.23 = (bf16[1024,256]{1,0:T(8,128)(2,1)}, bf16[1024,256]{1,0:T(8,128)(2,1)}, u32[]{:S(2)}, u32[]{:S(2)}) collective-permute-start(bf16[1024,256]{1,0:T(8,128)(2,1)} %slice.331), channel_id=1, source_target_pairs={{0,4},{1,5},{2,6},{3,7},{4,0},{5,1},{6,2},{7,3},{8,12},{9,13},{10,... | collective-permute-start | bytes 1572872 | tf_op jit(solution)/shard_map/down_plane/ppermute | solution.py:504
  304.7 28.3 %collective-permute-start.17 = (bf16[256,1024]{1,0:T(8,128)(2,1)}, bf16[256,1024]{1,0:T(8,128)(2,1)}, u32[]{:S(2)}, u32[]{:S(2)}) collective-permute-start(bf16[256,1024]{1,0:T(8,128)(2,1)} %convert_element_type.295.refs_0_), channel_id=1, source_target_pairs={{0,1},{1,0},{2,3},{3,2},{4,5},{5,4},{6,7},{7,6},{8,9},{9,8},{10,11... | collective-permute-start | bytes 1572872 | tf_op jit(solution)/shard_map/middle_row/ppermute | solution.py:501
  304.7 28.2 %collective-permute-start.18 = (bf16[256,1024]{1,0:T(8,128)(2,1)}, bf16[256,1024]{1,0:T(8,128)(2,1)}, u32[]{:S(2)}, u32[]{:S(2)}) collective-permute-start(bf16[256,1024]{1,0:T(8,128)(2,1)} %collective-permute-done.16.refs_1_), channel_id=1, source_target_pairs={{0,1},{1,0},{2,3},{3,2},{4,5},{5,4},{6,7},{7,6},{8,9},{9,8},{10,11... | collective-permute-start | bytes 1572872 | tf_op jit(solution)/shard_map/middle_row/ppermute | solution.py:501
  332.2 26.2 %collective-permute-start.33 = (bf16[256,1024]{1,0:T(8,128)(2,1)}, bf16[256,1024]{1,0:T(8,128)(2,1)S(1)}, u32[]{:S(2)}, u32[]{:S(2)}) collective-permute-start(bf16[256,1024]{1,0:T(8,128)(2,1)} %get-tuple-element.109), channel_id=1, source_target_pairs={{0,1},{1,0},{2,3},{3,2},{4,5},{5,4},{6,7},{7,6},{8,9},{9,8},{10,11... | collective-permute-start | bytes 1572872 | tf_op jit(solution)/shard_map/unit_grad/ppermute | solution.py:501
  358.5 14.8 %collective-permute-start.34 = (bf16[256,1024]{1,0:T(8,128)(2,1)S(1)}, bf16[256,1024]{1,0:T(8,128)(2,1)S(1)}, u32[]{:S(2)}, u32[]{:S(2)}) collective-permute-start(bf16[256,1024]{1,0:T(8,128)(2,1)S(1)} %add_convert_fusion.12), channel_id=1, source_target_pairs={{0,8},{8,0},{16,24},{24,16},{1,9},{9,1},{17,25},{25,17},{2,10},{10... | collective-permute-start | bytes 1572872 | tf_op jit(solution)/shard_map/unit_grad/ppermute | solution.py:518
  358.9 16.0 %collective-permute-start.25 = (bf16[256,1024]{1,0:T(8,128)(2,1)}, bf16[256,1024]{1,0:T(8,128)(2,1)S(1)}, u32[]{:S(2)}, u32[]{:S(2)}) collective-permute-start(bf16[256,1024]{1,0:T(8,128)(2,1)} %get-tuple-element.103), channel_id=1, source_target_pairs={{0,1},{1,0},{2,3},{3,2},{4,5},{5,4},{6,7},{7,6},{8,9},{9,8},{10,11... | collective-permute-start | bytes 1572872 | tf_op jit(solution)/shard_map/unit_grad/ppermute | solution.py:501
  361.2 30.1 %collective-permute-start.27 = (bf16[256,1024]{1,0:T(8,128)(2,1)S(1)}, bf16[256,1024]{1,0:T(8,128)(2,1)S(1)}, u32[]{:S(2)}, u32[]{:S(2)}) collective-permute-start(bf16[256,1024]{1,0:T(8,128)(2,1)S(1)} %add_convert_fusion.13), channel_id=1, source_target_pairs={{0,8},{8,0},{16,24},{24,16},{1,9},{9,1},{17,25},{25,17},{2,10},{10... | collective-permute-start | bytes 1572872 | tf_op jit(solution)/shard_map/unit_grad/ppermute | solution.py:518
  373.6 25.3 %collective-permute-start.35 = (bf16[256,1024]{1,0:T(8,128)(2,1)S(1)}, bf16[256,1024]{1,0:T(8,128)(2,1)S(1)}, u32[]{:S(2)}, u32[]{:S(2)}) collective-permute-start(bf16[256,1024]{1,0:T(8,128)(2,1)S(1)} %add_convert_fusion.11), channel_id=1, source_target_pairs={{0,16},{8,24},{16,0},{24,8},{1,17},{9,25},{17,1},{25,9},{2,18},{10... | collective-permute-start | bytes 1572872 | tf_op jit(solution)/shard_map/unit_grad/ppermute | solution.py:518
  402.8 24.0 %collective-permute-start.43 = (bf16[256,1024]{1,0:T(8,128)(2,1)S(1)}, bf16[256,1024]{1,0:T(8,128)(2,1)S(1)}, u32[]{:S(2)}, u32[]{:S(2)}) collective-permute-start(bf16[256,1024]{1,0:T(8,128)(2,1)S(1)} %get-tuple-element.168), channel_id=1, source_target_pairs={{0,4},{1,5},{2,6},{3,7},{4,0},{5,1},{6,2},{7,3},{8,12},{9,13},{10,... | collective-permute-start | bytes 1572872 | tf_op jit(solution)/shard_map/middle_grad/ppermute | solution.py:504
  404.2 24.1 %collective-permute-start.44 = (bf16[256,1024]{1,0:T(8,128)(2,1)S(1)}, bf16[256,1024]{1,0:T(8,128)(2,1)S(1)}, u32[]{:S(2)}, u32[]{:S(2)}) collective-permute-start(bf16[256,1024]{1,0:T(8,128)(2,1)S(1)} %get-tuple-element.168), channel_id=1, source_target_pairs={{0,6},{1,7},{2,4},{3,5},{4,2},{5,3},{6,0},{7,1},{8,14},{9,15},{10,... | collective-permute-start | bytes 1572872 | tf_op jit(solution)/shard_map/middle_grad/ppermute | solution.py:504
  428.4 65.7 %collective-permute-start.45 = (bf16[1024,1024]{1,0:T(8,128)(2,1)S(1)}, bf16[1024,1024]{1,0:T(8,128)(2,1)S(1)}, u32[]{:S(2)}, u32[]{:S(2)}) collective-permute-start(bf16[1024,1024]{1,0:T(8,128)(2,1)S(1)} %constant_dynamic-update-slice_fusion.8.own_ref.d_own), channel_id=1, source_target_pairs={{0,1},{1,0},{2,3},{3,2},{4,5},{5,4},{6,7},{7,6},{8,9},{9,8},{10,11... | collective-permute-start | bytes 6291464 | tf_op jit(solution)/shard_map/middle_grad/ppermute | solution.py:501
  440.5 22.7 %collective-permute-start.61 = (bf16[1024,256]{1,0:T(8,128)(2,1)}, bf16[1024,256]{1,0:T(8,128)(2,1)}, u32[]{:S(2)}, u32[]{:S(2)}) collective-permute-start(bf16[1024,256]{1,0:T(8,128)(2,1)} %get-tuple-element.182), channel_id=1, source_target_pairs={{0,2},{1,3},{2,0},{3,1},{4,6},{5,7},{6,4},{7,5},{8,10},{9,11},{10,... | collective-permute-start | bytes 1572872 | tf_op jit(solution)/shard_map/down_grad/ppermute | solution.py:504
  459.9 63.0 %collective-permute-start.39 = (bf16[512,1024]{1,0:T(8,128)(2,1)}, bf16[512,1024]{1,0:T(8,128)(2,1)}, u32[]{:S(2)}, u32[]{:S(2)}) collective-permute-start(bf16[512,1024]{1,0:T(8,128)(2,1)} %get-tuple-element.116), channel_id=1, source_target_pairs={{0,1},{1,0},{2,3},{3,2},{4,5},{5,4},{6,7},{7,6},{8,9},{9,8},{10,11... | collective-permute-start | bytes 3145736 | tf_op jit(solution)/shard_map/feed/ppermute | solution.py:501
  462.3 76.8 %collective-permute-start.60 = (bf16[2048,256]{1,0:T(8,128)(2,1)}, bf16[2048,256]{1,0:T(8,128)(2,1)}, u32[]{:S(2)}, u32[]{:S(2)}) collective-permute-start(bf16[2048,256]{1,0:T(8,128)(2,1)} %pad_maximum_fusion.10), channel_id=1, source_target_pairs={{0,2},{1,3},{2,0},{3,1},{4,6},{5,7},{6,4},{7,5},{8,10},{9,11},{10,... | collective-permute-start | bytes 3145736 | tf_op jit(solution)/shard_map/down_grad/ppermute | solution.py:504
  475.0 52.0 %collective-permute-start.51 = (bf16[1024,256]{1,0:T(8,128)(2,1)}, bf16[1024,256]{1,0:T(8,128)(2,1)}, u32[]{:S(2)}, u32[]{:S(2)}) collective-permute-start(bf16[1024,256]{1,0:T(8,128)(2,1)} %get-tuple-element.185), channel_id=1, source_target_pairs={{0,4},{1,5},{2,6},{3,7},{4,0},{5,1},{6,2},{7,3},{8,12},{9,13},{10,... | collective-permute-start | bytes 1572872 | tf_op jit(solution)/shard_map/gate_grad/ppermute | solution.py:504
  477.5 62.5 %collective-permute-start.62 = (bf16[2048,256]{1,0:T(8,128)(2,1)}, bf16[2048,256]{1,0:T(8,128)(2,1)}, u32[]{:S(2)}, u32[]{:S(2)}) collective-permute-start(bf16[2048,256]{1,0:T(8,128)(2,1)} %pad_maximum_fusion.11), channel_id=1, source_target_pairs={{0,4},{1,5},{2,6},{3,7},{4,0},{5,1},{6,2},{7,3},{8,12},{9,13},{10,... | collective-permute-start | bytes 3145736 | tf_op jit(solution)/shard_map/down_grad/ppermute | solution.py:504
  494.1 61.0 %collective-permute-start.37 = (bf16[512,1024]{1,0:T(8,128)(2,1)}, bf16[512,1024]{1,0:T(8,128)(2,1)}, u32[]{:S(2)}, u32[]{:S(2)}) collective-permute-start(bf16[512,1024]{1,0:T(8,128)(2,1)} %get-tuple-element.112), channel_id=1, source_target_pairs={{0,1},{1,0},{2,3},{3,2},{4,5},{5,4},{6,7},{7,6},{8,9},{9,8},{10,11... | collective-permute-start | bytes 3145736 | tf_op jit(solution)/shard_map/feed/ppermute | solution.py:501
  527.0 44.2 %collective-permute-start.40 = (bf16[256,1024]{1,0:T(8,128)(2,1)}, bf16[256,1024]{1,0:T(8,128)(2,1)}, u32[]{:S(2)}, u32[]{:S(2)}) collective-permute-start(bf16[256,1024]{1,0:T(8,128)(2,1)} %slice.419), channel_id=1, source_target_pairs={{0,8},{8,0},{16,24},{24,16},{1,9},{9,1},{17,25},{25,17},{2,10},{10... | collective-permute-start | bytes 1572872 | tf_op jit(solution)/shard_map/feed/ppermute | solution.py:518
  536.7 35.8 %collective-permute-start.52 = (bf16[2048,256]{1,0:T(8,128)(2,1)}, bf16[2048,256]{1,0:T(8,128)(2,1)}, u32[]{:S(2)}, u32[]{:S(2)}) collective-permute-start(bf16[2048,256]{1,0:T(8,128)(2,1)} %pad_maximum_fusion.6), channel_id=1, source_target_pairs={{0,2},{1,3},{2,0},{3,1},{4,6},{5,7},{6,4},{7,5},{8,10},{9,11},{10,... | collective-permute-start | bytes 3145736 | tf_op jit(solution)/shard_map/gate_grad/ppermute | solution.py:504
  539.1 33.4 %collective-permute-start.54 = (bf16[2048,256]{1,0:T(8,128)(2,1)}, bf16[2048,256]{1,0:T(8,128)(2,1)}, u32[]{:S(2)}, u32[]{:S(2)}) collective-permute-start(bf16[2048,256]{1,0:T(8,128)(2,1)} %pad_maximum_fusion.7), channel_id=1, source_target_pairs={{0,4},{1,5},{2,6},{3,7},{4,0},{5,1},{6,2},{7,3},{8,12},{9,13},{10,... | collective-permute-start | bytes 3145736 | tf_op jit(solution)/shard_map/gate_grad/ppermute | solution.py:504
  543.0 101.9 %all-to-all-start.8 = ((bf16[4,512,256]{2,1,0:T(8,128)(2,1)}), bf16[4,512,256]{2,1,0:T(8,128)(2,1)}, u32[]{:S(2)}, u32[]{:S(2)}) async-start(bf16[4,512,256]{2,1,0:T(8,128)(2,1)} %bitcast.117), calls=%async_computation.9 | async-start | bytes 2097152 | tf_op jit(solution)/shard_map/down_grad/all_to_all | solution.py:627
  555.1 88.8 %collective-permute-start.46 = (bf16[1024,1024]{1,0:T(8,128)(2,1)}, bf16[1024,1024]{1,0:T(8,128)(2,1)S(1)}, u32[]{:S(2)}, u32[]{:S(2)}) collective-permute-start(bf16[1024,1024]{1,0:T(8,128)(2,1)} %get-tuple-element.137), channel_id=1, source_target_pairs={{0,1},{1,0},{2,3},{3,2},{4,5},{5,4},{6,7},{7,6},{8,9},{9,8},{10,11... | collective-permute-start | bytes 6291464 | tf_op jit(solution)/shard_map/first_plane/ppermute | solution.py:501
  556.8 82.9 %collective-permute-start.38 = (bf16[256,1024]{1,0:T(8,128)(2,1)S(1)}, bf16[256,1024]{1,0:T(8,128)(2,1)S(1)}, u32[]{:S(2)}, u32[]{:S(2)}) collective-permute-start(bf16[256,1024]{1,0:T(8,128)(2,1)S(1)} %slice.420), channel_id=1, source_target_pairs={{0,8},{8,0},{16,24},{24,16},{1,9},{9,1},{17,25},{25,17},{2,10},{10... | collective-permute-start | bytes 1572872 | tf_op jit(solution)/shard_map/feed/ppermute | solution.py:518
  572.4 67.3 %collective-permute-start.41 = (bf16[256,1024]{1,0:T(8,128)(2,1)S(1)}, bf16[256,1024]{1,0:T(8,128)(2,1)S(1)}, u32[]{:S(2)}, u32[]{:S(2)}) collective-permute-start(bf16[256,1024]{1,0:T(8,128)(2,1)S(1)} %fusion.7), channel_id=1, source_target_pairs={{0,16},{8,24},{16,0},{24,8},{1,17},{9,25},{17,1},{25,9},{2,18},{10... | collective-permute-start | bytes 1572872 | tf_op jit(solution)/shard_map/feed/ppermute | solution.py:518
  576.9 66.8 %collective-permute-start.55 = (bf16[1024,256]{1,0:T(8,128)(2,1)S(1)}, bf16[1024,256]{1,0:T(8,128)(2,1)S(1)}, u32[]{:S(2)}, u32[]{:S(2)}) collective-permute-start(bf16[1024,256]{1,0:T(8,128)(2,1)S(1)} %get-tuple-element.183), channel_id=1, source_target_pairs={{0,4},{1,5},{2,6},{3,7},{4,0},{5,1},{6,2},{7,3},{8,12},{9,13},{10,... | collective-permute-start | bytes 1572872 | tf_op jit(solution)/shard_map/up_grad/ppermute | solution.py:504
  641.8 15.2 %collective-permute-start.57 = (bf16[1024,256]{1,0:T(8,128)(2,1)}, bf16[1024,256]{1,0:T(8,128)(2,1)}, u32[]{:S(2)}, u32[]{:S(2)}) collective-permute-start(bf16[1024,256]{1,0:T(8,128)(2,1)} %get-tuple-element.184), channel_id=1, source_target_pairs={{0,2},{1,3},{2,0},{3,1},{4,6},{5,7},{6,4},{7,5},{8,10},{9,11},{10,... | collective-permute-start | bytes 1572872 | tf_op jit(solution)/shard_map/up_grad/ppermute | solution.py:504
  644.9 17.6 %all-to-all-start.4 = ((bf16[4,256,256]{2,1,0:T(8,128)(2,1)}), bf16[4,256,256]{2,1,0:T(8,128)(2,1)S(1)}, u32[]{:S(2)}, u32[]{:S(2)}) async-start(bf16[4,256,256]{2,1,0:T(8,128)(2,1)} %pad_maximum_fusion.13), calls=%async_computation.4 | async-start | bytes 1048576 | tf_op jit(solution)/shard_map/block_out/all_to_all | solution.py:563
  649.5 24.3 %collective-permute-start.47 = (bf16[256,1024]{1,0:T(8,128)(2,1)}, bf16[256,1024]{1,0:T(8,128)(2,1)}, u32[]{:S(2)}, u32[]{:S(2)}) collective-permute-start(bf16[256,1024]{1,0:T(8,128)(2,1)} %get-tuple-element.172), channel_id=1, source_target_pairs={{0,2},{1,3},{2,0},{3,1},{4,6},{5,7},{6,4},{7,5},{8,10},{9,11},{10,... | collective-permute-start | bytes 1572872 | tf_op jit(solution)/shard_map/first_plane/ppermute | solution.py:504
  651.5 22.3 %collective-permute-start.48 = (bf16[256,1024]{1,0:T(8,128)(2,1)}, bf16[256,1024]{1,0:T(8,128)(2,1)}, u32[]{:S(2)}, u32[]{:S(2)}) collective-permute-start(bf16[256,1024]{1,0:T(8,128)(2,1)} %get-tuple-element.174), channel_id=1, source_target_pairs={{0,4},{1,5},{2,6},{3,7},{4,0},{5,1},{6,2},{7,3},{8,12},{9,13},{10,... | collective-permute-start | bytes 1572872 | tf_op jit(solution)/shard_map/first_plane/ppermute | solution.py:504
  653.0 32.5 %collective-permute-start.49 = (bf16[256,1024]{1,0:T(8,128)(2,1)}, bf16[256,1024]{1,0:T(8,128)(2,1)}, u32[]{:S(2)}, u32[]{:S(2)}) collective-permute-start(bf16[256,1024]{1,0:T(8,128)(2,1)} %get-tuple-element.173), channel_id=1, source_target_pairs={{0,6},{1,7},{2,4},{3,5},{4,2},{5,3},{6,0},{7,1},{8,14},{9,15},{10,... | collective-permute-start | bytes 1572872 | tf_op jit(solution)/shard_map/first_plane/ppermute | solution.py:504
  654.1 49.6 %collective-permute-start.56 = (bf16[2048,256]{1,0:T(8,128)(2,1)}, bf16[2048,256]{1,0:T(8,128)(2,1)}, u32[]{:S(2)}, u32[]{:S(2)}) collective-permute-start(bf16[2048,256]{1,0:T(8,128)(2,1)} %pad_maximum_fusion.8), channel_id=1, source_target_pairs={{0,2},{1,3},{2,0},{3,1},{4,6},{5,7},{6,4},{7,5},{8,10},{9,11},{10,... | collective-permute-start | bytes 3145736 | tf_op jit(solution)/shard_map/up_grad/ppermute | solution.py:504
  663.2 29.1 %all-to-all-start.6 = ((bf16[4,512,256]{2,1,0:T(8,128)(2,1)}), bf16[4,512,256]{2,1,0:T(8,128)(2,1)S(1)}, u32[]{:S(2)}, u32[]{:S(2)}) async-start(bf16[4,512,256]{2,1,0:T(8,128)(2,1)} %bitcast.48), calls=%async_computation.7 | async-start | bytes 2097152 | tf_op jit(solution)/shard_map/gate_grad/all_to_all | solution.py:627
  670.3 33.4 %collective-permute-start.58 = (bf16[2048,256]{1,0:T(8,128)(2,1)}, bf16[2048,256]{1,0:T(8,128)(2,1)}, u32[]{:S(2)}, u32[]{:S(2)}) collective-permute-start(bf16[2048,256]{1,0:T(8,128)(2,1)} %pad_maximum_fusion.9), channel_id=1, source_target_pairs={{0,4},{1,5},{2,6},{3,7},{4,0},{5,1},{6,2},{7,3},{8,12},{9,13},{10,... | collective-permute-start | bytes 3145736 | tf_op jit(solution)/shard_map/up_grad/ppermute | solution.py:504
  692.4 14.8 %all-to-all-start.5 = ((bf16[4,256,256]{2,1,0:T(8,128)(2,1)}), bf16[4,256,256]{2,1,0:T(8,128)(2,1)S(1)}, u32[]{:S(2)}, u32[]{:S(2)}) async-start(bf16[4,256,256]{2,1,0:T(8,128)(2,1)} %pad_maximum_fusion.14), calls=%async_computation.5 | async-start | bytes 1048576 | tf_op jit(solution)/shard_map/input_grad/all_to_all | solution.py:563
  707.2 29.2 %all-to-all-start.7 = ((bf16[4,512,256]{2,1,0:T(8,128)(2,1)}), bf16[4,512,256]{2,1,0:T(8,128)(2,1)S(1)}, u32[]{:S(2)}, u32[]{:S(2)}) async-start(bf16[4,512,256]{2,1,0:T(8,128)(2,1)} %bitcast.50), calls=%async_computation.8 | async-start | bytes 2097152 | tf_op jit(solution)/shard_map/up_grad/all_to_all | solution.py:627
  (65 other events, 692.2 us)
Sparse Core Ops, SparseCore 0:
  16.4 107.9 all-gather.3
  133.9 40.3 all-gather.5
  200.5 46.7 all-gather.7
  523.0 125.1 reduce-scatter.1

commit v5 on v4

--- a/solution.py
+++ b/solution.py
@@ -208,7 +208,7 @@
             pltpu.VMEM((2, parts, tokens, half), BF16),
             pltpu.SemaphoreType.DMA((2, parts)),
         ],
-        compiler_params=pltpu.CompilerParams(vmem_limit_bytes=VMEM_BYTES),
+        compiler_params=pltpu.CompilerParams(vmem_limit_bytes=48 * 1024 * 1024),
         name="units",
     )(starts, *m_owns, *m_others, g_own, g_other, *weights)
     return result[0], result[1], result[2], result[3 : 3 + parts], result[3 + parts :]
@@ -245,7 +245,7 @@
         + [whole_spec(a) for a in rights],
         out_specs=[pl.BlockSpec((2 * feat, part), lambda i: (i, 0))] * count,
         out_shape=[jax.ShapeDtypeStruct((2 * half, part), BF16)] * count,
-        compiler_params=pltpu.CompilerParams(vmem_limit_bytes=VMEM_BYTES),
+        compiler_params=pltpu.CompilerParams(vmem_limit_bytes=40 * 1024 * 1024),
         name=name,
     )(starts, *owns, *others, *rights)
 
@@ -280,30 +280,31 @@
             jax.ShapeDtypeStruct((2 * half, 4 * part), BF16),
             jax.ShapeDtypeStruct((2 * half, 1), F32),
         ],
-        compiler_params=pltpu.CompilerParams(vmem_limit_bytes=VMEM_BYTES),
+        compiler_params=pltpu.CompilerParams(vmem_limit_bytes=40 * 1024 * 1024),
         name="heads_outer",
     )(x_own, x_other, d_own, d_other, dq, dk, dv, mixed, scale, weight)
 
 
-def finish_kernel(core_ref, part_ref, gain_ref, *outs):
+def finish_kernel(scaled, core_ref, part_ref, gain_ref, *outs):
     feat = gain_ref.shape[0] // 2
-    blocks, columns = part_ref.shape[0], part_ref.shape[2]
-    width = blocks * columns // len(outs)
-    for block in range(blocks):
-        at = block * columns
-        for side in range(2):
-            rows = slice(side * feat, (side + 1) * feat)
-            start = pl.multiple_of(lax.rem(core_ref[0] + side, 2) * feat, feat)
-            value = part_ref[block, pl.ds(start, feat), :].astype(F32) * gain_ref[rows, :]
-            outs[at // width][rows, at % width : at % width + columns] = value
-
-
-def finish(core, part, gain, count=1):
+    blocks, columns = part_ref.shape[0], part_ref.shape[2] // len(outs)
+    for side in range(2):
+        rows = slice(side * feat, (side + 1) * feat)
+        start = pl.multiple_of(lax.rem(core_ref[0] + side, 2) * feat, feat)
+        gain = gain_ref[rows, :]
+        for block in range(blocks):
+            for i, out in enumerate(outs):
+                value = part_ref[block, pl.ds(start, feat), i * columns : (i + 1) * columns].astype(F32)
+                at = block * columns
+                out[rows, at : at + columns] = value * gain if i < scaled else value
+
+
+def finish(core, part, gain, scaled, count=1):
     blocks, rows, columns = part.shape
     vmem = pl.BlockSpec(memory_space=pltpu.VMEM)
     result = jax.ShapeDtypeStruct((rows, blocks * columns // count), F32)
     return pl.pallas_call(
-        finish_kernel,
+        functools.partial(finish_kernel, scaled),
         in_specs=[pl.BlockSpec(memory_space=pltpu.SMEM), vmem, vmem],
         out_specs=[vmem] * count,
         out_shape=[result] * count,
@@ -326,7 +327,7 @@
         in_specs=[row_spec(block, own), row_spec(block, other), whole_spec(weight)],
         out_specs=row_spec(block, result),
         out_shape=result,
-        compiler_params=pltpu.CompilerParams(vmem_limit_bytes=VMEM_BYTES),
+        compiler_params=pltpu.CompilerParams(vmem_limit_bytes=40 * 1024 * 1024),
         name="fold",
     )(own, other, weight)
 
@@ -525,15 +526,15 @@
             bit //= 2
         return [got[step] for step in range(rows)]
 
-    def reduce_row_traced(parts):
-        parts, sends, bit = list(parts), [], 1
+    def reduce_row(parts, *works):
+        parts, bit, step = list(parts), 1, 0
         while bit < rows:
-            for at in range(rows - 2 * bit, -1, -2 * bit):
-                low = parts[at + bit].astype(BF16)
-                sends.append(low)
-                parts[at] = parts[at].astype(F32) + row_swap(low, bit).astype(F32)
-            bit *= 2
-        return parts[0], sends
+            lows = {at: parts[at + bit].astype(BF16) for at in range(rows - 2 * bit, -1, -2 * bit)}
+            held = works[step](*lows.values()) if step < len(works) else ()
+            for at, low in lows.items():
+                parts[at] = parts[at].astype(F32) + after(row_swap(low, bit), *held).astype(F32)
+            bit, step = 2 * bit, step + 1
+        return parts[0]
 
     def row_part(a, step):
         size = a.shape[0] // rows
@@ -601,25 +602,22 @@
             jnp.concatenate([plane_swap(second[:half], 1), plane_swap(first[half:], 2)], axis=0),
         ]
 
-    def plane_sum(pieces, *hold):
+    def plane_first(pieces):
         if places != 4:
-            total = pieces[0].astype(F32)
-            for s in range(1, places):
-                total = total + plane_swap(pieces[s], s).astype(F32)
-            return total.astype(BF16)
+            return pieces
         top, bottom = plane_swap(pieces[3][:half], 1), plane_swap(pieces[3][half:], 2)
-        top, bottom = after(top, *hold), after(bottom, *hold)
         to_second = jnp.concatenate(
             [(pieces[2][:half].astype(F32) + top.astype(F32)).astype(BF16), pieces[2][half:]], axis=0
         )
         to_first = jnp.concatenate(
             [pieces[1][:half], (pieces[1][half:].astype(F32) + bottom.astype(F32)).astype(BF16)], axis=0
         )
-        total = (
-            pieces[0].astype(F32)
-            + plane_swap(to_first, 1).astype(F32)
-            + plane_swap(to_second, 2).astype(F32)
-        )
+        return [pieces[0], to_first, to_second]
+
+    def plane_second(pieces):
+        total = pieces[0].astype(F32)
+        for s, piece in enumerate(pieces[1:], 1):
+            total = total + plane_swap(piece, s).astype(F32)
         return total.astype(BF16)
 
     def give_back(total):
@@ -628,7 +626,6 @@
 
     starts = jnp.stack([row ^ s for s in range(rows)])
     cores = core.reshape(1)
-    ones = jnp.ones((2 * feat, 1), F32)
 
     with jax.named_scope("gather_qkv"):
         qkv_full = lax.all_gather(
@@ -640,12 +637,15 @@
             tiled=True,
         )
         out_full = lax.all_gather(own_first(out_weight), "row", axis=0, tiled=True)
+    with jax.named_scope("inputs"):
+        x_own = put_feats(spread(inputs))
+        x_other = core_swap(x_own)
+    with jax.named_scope("gate_row"):
+        gate_whole = exchange(scaled(gate_weight, gain_two))
     with jax.named_scope("grad_plane"):
-        g_part = to_parts(out_grad)
-    with jax.named_scope("gate_row"):
-        gate_whole = exchange(after(scaled(gate_weight, gain_two), g_part))
+        g_part = to_parts(after(out_grad, gate_whole))
     with jax.named_scope("up_row"):
-        up_whole = exchange(after(scaled(up_weight, gain_two), gate_whole))
+        up_whole = exchange(after(scaled(up_weight, gain_two), g_part, x_other, qkv_full))
     with jax.named_scope("down_row"):
         down_whole = exchange(after(own_first(down_weight), up_whole))
     with jax.named_scope("grad_row"):
@@ -656,18 +656,15 @@
     with jax.named_scope("up_plane"):
         ups = spread_weights(up_whole)
 
-    with jax.named_scope("inputs"):
-        x_own = put_feats(spread(inputs))
-        x_other = core_swap(x_own)
     heads_width = query_weight.shape[1]
     cosine, front, back = rope_tables(positions, heads_width)
     start_row = jnp.sum(
         (segment_ids[None, :] < segment_ids[:, None]).astype(jnp.int32), axis=1
     )[None, :]
-    x_ready = after(x_own, gates[1], gates[2], up_whole)
+    x_ready = after(x_own, gates[1], gates[2])
     query, key, value, scale_one = project(feat, x_ready, x_other, qkv_full, cosine, front, back)
     mixed, logs = attend(query, key, value, start_row)
-    mixed = after(mixed, gates[3], ups[1], ups[2], down_whole)
+    mixed = after(mixed, gates[3])
 
     def scatter_parts(own, other):
         low = (own.astype(F32) + core_swap(other).astype(F32)).astype(BF16)
@@ -685,7 +682,7 @@
     with jax.named_scope("down_plane"):
         downs = spread_weights(after(down_whole, middle))
     with jax.named_scope("middle_row"):
-        m_list = gather_row(after(middle.astype(BF16), ups[3]))
+        m_list = gather_row(after(middle.astype(BF16), ups[1], ups[2], down_whole))
         m_others = [core_swap(m) for m in m_list]
     found, own_shares, other_shares = [], [], []
     for at in range(0, rows, 2):
@@ -696,14 +693,28 @@
         found.append(three)
         own_shares += owns
         other_shares += others
+    kept = {}
+
+    def down_work(*lows):
+        with jax.named_scope("down_grad"):
+            kept["down"] = outer(
+                feat, "down_outer", starts, [g_own], [g_other], [after(f[0], *lows) for f in found], places
+            )
+        return kept["down"][:1]
+
+    def feed_work(*lows):
+        with jax.named_scope("feed"):
+            kept["feed"] = [unfold(feat, "feed", [after(f[0], *lows)], downs) for f in found]
+        return [own for own, _ in kept["feed"]]
+
     with jax.named_scope("unit_grad"):
-        unit_grad, sums = reduce_row_traced(
-            [own.astype(F32) + core_swap(other).astype(F32) for own, other in zip(own_shares, other_shares)]
+        unit_grad = reduce_row(
+            [own.astype(F32) + core_swap(other).astype(F32) for own, other in zip(own_shares, other_shares)],
+            down_work,
+            feed_work,
         )
     with jax.named_scope("down_grad"):
-        down_total = plane_sum(
-            outer(feat, "down_outer", starts, [g_own], [g_other], [after(f[0], *sums[:2]) for f in found], places)
-        )
+        down_total = plane_second(plane_first(kept["down"]))
         down_blocks = give_back(down_total)
 
     unit_mid = middle * scale_mid
@@ -711,36 +722,49 @@
     dot_two = dot_two + core_swap(dot_two)
     middle_grad = g_part.astype(F32) + scale_mid * (unit_grad - unit_mid * (dot_two / width))
 
-    with jax.named_scope("middle_grad"):
-        d_low = middle_grad.astype(BF16)
-        d_own = put_rows(spread(d_low))
-        d_other = core_swap(d_own)
+    d_low = after(middle_grad.astype(BF16), down_total)
     with jax.named_scope("feed"):
         shares = []
-        for hidden, _, _ in found:
-            own, other = unfold(feat, "feed", [after(hidden, d_low)], downs)
+        for own, other in kept["feed"]:
             low = own.astype(F32) + core_swap(other).astype(F32)
+            low = after(low.astype(BF16), d_low)
             shares += [low[:quarter], low[quarter:]]
-        feed, _ = reduce_row_traced(shares)
     gate_parts = outer(feat, "gate_outer", starts, m_list, m_others, [after(f[1], d_low) for f in found], places)
     up_parts = outer(feat, "up_outer", starts, m_list, m_others, [after(f[2], d_low) for f in found], places)
-    mixed_grad = fold(feat, after(d_own, gate_parts[0], up_parts[0]), d_other, out_full)
+    with jax.named_scope("feed"):
+        feed_sent = []
+
+        def note(*lows):
+            feed_sent.extend(lows)
+            return ()
+
+        feed = reduce_row(shares, note, note)
+        feed_low = (middle + feed).astype(BF16)
+    with jax.named_scope("middle_grad"):
+        pieces = spread(d_low)
+        d_own = put_rows(
+            [pieces[0]] + [after(a, gate_parts[0], up_parts[0], feed_sent[-1]) for a in pieces[1:]]
+        )
+        d_other = core_swap(d_own)
+    mixed_grad = fold(feat, d_own, d_other, out_full)
     with jax.named_scope("gate_grad"):
-        gate_total = plane_sum([after(a, d_own) for a in gate_parts], mixed_grad)
+        gate_middle = plane_first([after(a, d_own) for a in gate_parts])
+        gate_total = plane_second(gate_middle)
         gate_blocks = give_back(gate_total)
     query_grad, key_grad, value_grad = attend_back(
-        query, key, value, mixed, mixed_grad, start_row, logs, cosine, front, back
+        query, key, value, mixed, after(mixed_grad, *gate_middle), start_row, logs, cosine, front, back
     )
+    query_grad = after(query_grad, feed_low, down_blocks)
     heads_part, gain_dots = heads_outer(
         feat, x_own, x_other, d_own, d_other, query_grad, key_grad, value_grad, mixed, scale_one, qkv_full
     )
     with jax.named_scope("heads_grad"):
         heads_blocks = lax.psum_scatter(heads_part, "row", scatter_dimension=0, tiled=True)
     with jax.named_scope("up_grad"):
-        up_total = plane_sum([after(a, gate_total) for a in up_parts], heads_part)
+        up_total = plane_second(plane_first([after(a, gate_total, heads_part) for a in up_parts]))
         up_blocks = give_back(up_total)
     with jax.named_scope("block_out"):
-        block_out = to_home(after((middle + feed).astype(BF16), heads_part))
+        block_out = to_home(after(feed_low, gate_blocks))
     with jax.named_scope("first_plane"):
         first_unit_grad = scatter_parts(
             *unfold(feat, "first_grad", [after(query_grad, heads_part), key_grad, value_grad], [qkv_full])
@@ -768,18 +792,21 @@
             mine = mine + row_swap(lax.dynamic_index_in_dim(dots, row ^ s, 0, False), s)
         first_gain_grad = mine[0] / gain_one[:, 0]
         second_gain_grad = mine[1] / gain_two[:, 0]
-    (down_weight_grad,) = finish(cores, down_blocks, ones)
-    (gate_weight_grad,) = finish(cores, gate_blocks, gain_two)
-    (up_weight_grad,) = finish(cores, up_blocks, gain_two)
-    part = query_weight.shape[1]
-    (qkv_grad,) = finish(cores, heads_blocks[None, :, : 3 * part], gain_one)
-    (out_weight_grad,) = finish(cores, heads_blocks[None, :, 3 * part :], ones)
+    (down_weight_grad,) = finish(cores, down_blocks, gain_two, 0)
+    (gate_weight_grad,) = finish(cores, gate_blocks, gain_two, 1)
+    (up_weight_grad,) = finish(cores, up_blocks, gain_two, 1)
+    heads_blocks = after(
+        heads_blocks, down_weight_grad, gate_weight_grad, up_weight_grad, second_gain_grad, input_grad
+    )
+    query_weight_grad, key_weight_grad, value_weight_grad, out_weight_grad = finish(
+        cores, heads_blocks[None], gain_one, 3, 4
+    )
     return (
         block_out,
         input_grad,
-        qkv_grad[:, :part],
-        qkv_grad[:, part : 2 * part],
-        qkv_grad[:, 2 * part :],
+        query_weight_grad,
+        key_weight_grad,
+        value_weight_grad,
         out_weight_grad,
         gate_weight_grad,
         up_weight_grad,

time: 771 us -> 676 us (0.88)
  waiting for transfers between devices: 359 us -> 265 us
  Pallas kernels: 159 us -> 147 us
    ppermute x12, waiting for transfers between devices: 155 us -> 73.1 us  [row_swap(): return lax.ppermute(a, 'row', [(i, i ^ step) for i in range(rows)])]
    all_to_all x3, waiting for transfers between devices: 0.01 us -> 31.3 us  [give_back(): return lax.all_to_all(total, 'row', split_axis=0, concat_axis=0, tiled=True)]
    ppermute x36, waiting for transfers between devices: 111 us -> 89.5 us  [plane_swap(): return lax.ppermute(a, 'col', [(i, i ^ 2 * step) for i in range(cols)])]
    unnamed x103 -> x153, local copies, waits for them, and re-layouts: 11.6 us -> 21.9 us
    all_to_all x3, waiting for transfers between devices: 61.5 us -> 51.8 us  [exchange(): lax.all_to_all(pieces, 'row', split_axis=0, concat_axis=0, tiled=True)]
    convert_element_type x13 -> x16, other arithmetic: 12.7 us -> 18 us  [the longest x4 3.99 us: reduce_row(): parts[at + bit].astype(BF16)]
  transfers between devices with their start and end apart: 82 -> 82, of which waited for: 36 -> 30; matrix products, arithmetic and copies ran while one was open for 15% -> 17% of each run, Pallas kernels for 20% -> 20%
where the time goes in v5:
time: 676 us; the launch traced here: 665 us
  waiting for transfers between devices  265 us (39%)
  Pallas kernels  147 us (22%)
  starting transfers between devices  103 us (15%)
  local copies, waits for them, and re-layouts  70.5 us (10%)
  other arithmetic  62.6 us (9%)
  between operations  15.6 us (2%)
    ppermute x36, waiting for transfers between devices, plane_swap(): return lax.ppermute(a, 'col', [(i, i ^ 2 * step) for i in range(cols)])  89.5 us
    ppermute x12, waiting for transfers between devices, row_swap(): return lax.ppermute(a, 'row', [(i, i ^ step) for i in range(rows)])  73.1 us
    all_to_all x3, waiting for transfers between devices, exchange(): lax.all_to_all(pieces, 'row', split_axis=0, concat_axis=0, tiled=True)  51.8 us
    pallas_call x2, Pallas kernels, units(): pl.pallas_call(functools.partial(units_kernel, feat, parts, count), in_sp...  48.4 us
    ppermute x36, starting transfers between devices, plane_swap(): return lax.ppermute(a, 'col', [(i, i ^ 2 * step) for i in range(cols)])  43.5 us
    all_to_all x3, waiting for transfers between devices, give_back(): return lax.all_to_all(total, 'row', split_axis=0, concat_axis=0, tiled=True)  31.3 us
    pallas_call x4, Pallas kernels, unfold(): pl.pallas_call(functools.partial(unfold_kernel, feat, len(lefts)), grid=(...  24.8 us
    unnamed x153, local copies, waits for them, and re-layouts  21.9 us
  transfers between devices with their start and end apart: 82, of which 30 were waited for; matrix products, arithmetic and copies ran while one was open for 17% of the time, Pallas kernels for 20%

profile of v5, /device:TPU:0, one launch (start us, length us, event | category | flops | bytes accessed | tf_op | source)
XLA Modules:
  0.0 664.6 jit_solution(7356757275093820874)
XLA Ops:
  13.7 6.3 all-to-all-start
  24.9 10.3 %collective-permute-done = bf16[1024,256]{1,0:T(8,128)(2,1)} collective-permute-done((bf16[1024,256]{1,0:T(8,128)(2,1)}, bf16[1024,256]{1,0:T(8,128)(2,1)}, u32[]{:S(2)}, u32[]{:S(2)}) %collective-permute-start) | collective-permute-done | bytes 524320 | tf_op jit(solution)/shard_map/inputs/ppermute | solution.py:505
  36.3 9.9 %collective-permute-done.1 = bf16[1024,256]{1,0:T(8,128)(2,1)} collective-permute-done((bf16[1024,256]{1,0:T(8,128)(2,1)}, bf16[1024,256]{1,0:T(8,128)(2,1)}, u32[]{:S(2)}, u32[]{:S(2)}) %collective-permute-start.1) | collective-permute-done | bytes 524320 | tf_op jit(solution)/shard_map/inputs/ppermute | solution.py:505
  48.5 25.3 %all-to-all-done = bf16[4,512,256]{2,1,0:T(8,128)(2,1)S(1)} async-done(((bf16[4,512,256]{2,1,0:T(8,128)(2,1)}), bf16[4,512,256]{2,1,0:T(8,128)(2,1)S(1)}, u32[]{:S(2)}, u32[]{:S(2)}) %all-to-all-start) | async-done | bytes 1048608 | tf_op jit(solution)/shard_map/gate_row/all_to_all | solution.py:592
  77.7 3.0 broadcast_select_fusion.1
  80.7 4.2 all-to-all-start.1
  86.5 2.5 copy.35.front_ref
  90.2 2.5 copy.36.back_ref
  93.8 2.6 copy.34.cos_ref
  96.4 2.2 pad_maximum_fusion.1
  114.3 4.2 all-to-all-start.2
  119.7 8.8 %project.1 = (bf16[1024,256]{1,0:T(8,128)(2,1)}, bf16[1024,256]{1,0:T(8,128)(2,1)}, bf16[1024,256]{1,0:T(8,128)(2,1)}, f32[1024,1]{1,0:T(8,128)}) custom-call(bf16[1024,1024]{1,0:T(8,128)(2,1)} %copy-done, bf16[1024,1024]{1,0:T(8,128)(2,1)} %collective-permute-done.5.other_ref.x_other, bf16[2048,768]{1,0:T(8,128)(2,1)} %all-gather.4.cloned.1.call-done.weight_ref.refs_3_, ...), custom_call_target="tpu_custom_call" | custom-call | tf_op jit(solution)/shard_map/project/pallas_call | solution.py:83
  128.6 10.1 %attend.1 = (bf16[1024,256]{1,0:T(8,128)(2,1)}, f32[2,2,1024]{2,1,0:T(2,128)}) custom-call(bf16[1024,256]{1,0:T(8,128)(2,1)} %get-tuple-element.99.q_ref, bf16[1024,256]{1,0:T(8,128)(2,1)} %get-tuple-element.100.k_ref, bf16[1024,256]{1,0:T(8,128)(2,1)} %get-tuple-element.101.v_ref, s32[1,1024]{1,0:T(1,128)} %bitcast.117), custom_call_target="tpu_custom_call" | custom-call | tf_op jit(solution)/shard_map/attend/pallas_call | solution.py:374
  138.6 5.1 mix.1
  143.9 5.1 all-to-all-done.2
  150.1 4.5 all-to-all-start.3
  154.6 2.5 add_convert_fusion.1
  163.8 19.7 %collective-permute-done.10 = bf16[256,1024]{1,0:T(8,128)(2,1)S(1)} collective-permute-done((bf16[256,1024]{1,0:T(8,128)(2,1)S(1)}, bf16[256,1024]{1,0:T(8,128)(2,1)S(1)}, u32[]{:S(2)}, u32[]{:S(2)}) %collective-permute-start.10) | collective-permute-done | bytes 524320 | tf_op jit(solution)/shard_map/mix_plane/ppermute | solution.py:505
  186.3 21.4 %all-to-all-done.3 = bf16[4,512,256]{2,1,0:T(8,128)(2,1)} async-done(((bf16[4,512,256]{2,1,0:T(8,128)(2,1)}), bf16[4,512,256]{2,1,0:T(8,128)(2,1)}, u32[]{:S(2)}, u32[]{:S(2)}) %all-to-all-start.3) | async-done | bytes 1048608 | tf_op jit(solution)/shard_map/down_row/all_to_all | solution.py:592
  210.7 2.5 all-gather.8.cloned.1.call-done.refs_4_.refs_0_
  218.4 21.2 %collective-permute-done.24.refs_0_.refs_2_ = bf16[256,1024]{1,0:T(8,128)(2,1)S(1)} collective-permute-done((bf16[256,1024]{1,0:T(8,128)(2,1)S(1)}, bf16[256,1024]{1,0:T(8,128)(2,1)S(1)}, u32[]{:S(2)}, u32[]{:S(2)}) %collective-permute-start.24) | collective-permute-done | bytes 524320 | tf_op jit(solution)/shard_map/middle_row/ppermute | solution.py:519
  248.3 5.2 collective-permute-done.21
  256.0 10.0 %collective-permute-done.25.refs_1_.refs_3_ = bf16[256,1024]{1,0:T(8,128)(2,1)} collective-permute-done((bf16[256,1024]{1,0:T(8,128)(2,1)S(1)}, bf16[256,1024]{1,0:T(8,128)(2,1)}, u32[]{:S(2)}, u32[]{:S(2)}) %collective-permute-start.25) | collective-permute-done | bytes 524320 | tf_op jit(solution)/shard_map/middle_row/ppermute | solution.py:519
  272.5 24.6 %units.2 = (bf16[512,1024]{1,0:T(8,128)(2,1)S(1)}, bf16[512,1024]{1,0:T(8,128)(2,1)}, bf16[512,1024]{1,0:T(8,128)(2,1)}, bf16[256,1024]{1,0:T(8,128)(2,1)S(1)}, ...) custom-call(s32[2]{0:T(128)S(1)} %pad_add_fusion.starts, ...), custom_call_target="tpu_custom_call" | custom-call | tf_op jit(solution)/shard_map/units/pallas_call | solution.py:198
  301.0 23.8 %units.3 = (bf16[512,1024]{1,0:T(8,128)(2,1)S(1)}, bf16[512,1024]{1,0:T(8,128)(2,1)}, bf16[512,1024]{1,0:T(8,128)(2,1)}, bf16[256,1024]{1,0:T(8,128)(2,1)S(1)}, ...) custom-call(s32[2]{0:T(128)S(1)} %pad_add_fusion.1.starts, ...), custom_call_target="tpu_custom_call" | custom-call | tf_op jit(solution)/shard_map/units/pallas_call | solution.py:198
  327.4 6.5 down_outer.1
  335.4 6.2 collective-permute-done.30
  341.8 6.4 collective-permute-done.38
  352.6 10.5 %collective-permute-done.40 = bf16[1024,256]{1,0:T(8,128)(2,1)S(1)} collective-permute-done((bf16[1024,256]{1,0:T(8,128)(2,1)S(1)}, bf16[1024,256]{1,0:T(8,128)(2,1)S(1)}, u32[]{:S(2)}, u32[]{:S(2)}) %collective-permute-start.40) | collective-permute-done | bytes 524320 | tf_op jit(solution)/shard_map/down_grad/ppermute | solution.py:505
  363.1 2.8 collective-permute-start.36
  367.5 5.9 feed.2
  373.5 6.1 feed.3
  379.6 6.8 %collective-permute-done.36 = bf16[256,1024]{1,0:T(8,128)(2,1)S(1)} collective-permute-done((bf16[256,1024]{1,0:T(8,128)(2,1)}, bf16[256,1024]{1,0:T(8,128)(2,1)S(1)}, u32[]{:S(2)}, u32[]{:S(2)}) %collective-permute-start.36) | collective-permute-done | bytes 524320 | tf_op jit(solution)/shard_map/unit_grad/ppermute | solution.py:519
  388.1 2.5 fusion.17
  390.6 3.0 add_convert_fusion.5
  401.0 6.5 up_outer.1
  411.5 6.5 gate_outer.1
  427.4 4.2 all-to-all-start.6
  434.3 23.7 %collective-permute-done.45 = bf16[256,1024]{1,0:T(8,128)(2,1)} collective-permute-done((bf16[256,1024]{1,0:T(8,128)(2,1)}, bf16[256,1024]{1,0:T(8,128)(2,1)}, u32[]{:S(2)}, u32[]{:S(2)}) %collective-permute-start.45) | collective-permute-done | bytes 524320 | tf_op jit(solution)/shard_map/feed/ppermute | solution.py:519
  462.2 2.4 add_convert_fusion.11
  464.6 3.8 fold.1.do_ref
  469.3 11.0 %attend_back.1 = (bf16[1024,256]{1,0:T(8,128)(2,1)}, bf16[1024,256]{1,0:T(8,128)(2,1)}, bf16[1024,256]{1,0:T(8,128)(2,1)}) custom-call(bf16[1024,256]{1,0:T(8,128)(2,1)} %get-tuple-element.99.q_ref, bf16[1024,256]{1,0:T(8,128)(2,1)} %get-tuple-element.100.k_ref, bf16[1024,256]{1,0:T(8,128)(2,1)} %get-tuple-element.101.v_ref, ...), custom_call_target="tpu_custom_call" | custom-call | tf_op jit(solution)/shard_map/attend_back/pallas_call | solution.py:443
  483.5 9.5 %heads_outer.1 = (bf16[2048,1024]{1,0:T(8,128)(2,1)}, f32[2048,1]{1,0:T(8,128)S(1)}) custom-call(bf16[1024,1024]{1,0:T(8,128)(2,1)S(1)} %copy-done.1, bf16[1024,1024]{1,0:T(8,128)(2,1)} %collective-permute-done.5.other_ref.x_other, bf16[1024,1024]{1,0:T(8,128)(2,1)} %constant_dynamic-update-slice_fusion.8.own_ref.d_own, ...), custom_call_target="tpu_custom_call" | custom-call | tf_op jit(solution)/shard_map/heads_outer/pallas_call | solution.py:272
  496.4 7.7 %first_grad.1 = (bf16[1024,1024]{1,0:T(8,128)(2,1)}, bf16[1024,1024]{1,0:T(8,128)(2,1)}) custom-call(bf16[1024,256]{1,0:T(8,128)(2,1)} %get-tuple-element.169.dq_ref.refs_0_, bf16[1024,256]{1,0:T(8,128)(2,1)} %get-tuple-element.166.dk_ref.refs_1_, bf16[1024,256]{1,0:T(8,128)(2,1)} %get-tuple-element.167.dv_ref.refs_2_, ...), custom_call_target="tpu_custom_call" | custom-call | tf_op jit(solution)/shard_map/first_plane/first_grad/pallas_call | solution.py:114
  504.1 15.1 %collective-permute-done.50 = bf16[2048,256]{1,0:T(8,128)(2,1)S(1)} collective-permute-done((bf16[2048,256]{1,0:T(8,128)(2,1)}, bf16[2048,256]{1,0:T(8,128)(2,1)S(1)}, u32[]{:S(2)}, u32[]{:S(2)}) %collective-permute-start.50) | collective-permute-done | bytes 1048608 | tf_op jit(solution)/shard_map/gate_grad/ppermute | solution.py:505
  524.0 4.5 all-to-all-start.4
  537.4 2.2 pad_maximum_fusion.9
  540.1 2.5 add_convert_fusion
  550.7 31.3 %all-to-all-done.4.part_ref = bf16[4,512,256]{2,1,0:T(8,128)(2,1)} async-done(((bf16[4,512,256]{2,1,0:T(8,128)(2,1)}), bf16[4,512,256]{2,1,0:T(8,128)(2,1)}, u32[]{:S(2)}, u32[]{:S(2)}) %all-to-all-start.4) | async-done | bytes 1048608 | tf_op jit(solution)/shard_map/gate_grad/all_to_all | solution.py:625
  583.1 6.6 collective-permute-done.57
  592.6 4.2 all-to-all-start.5
  599.7 6.1 all-to-all-done.5
  605.8 3.5 all-to-all-start.7
  609.3 3.4 multiply_reduce_fusion
  612.7 4.7 all-to-all-done.7
  617.4 4.7 all-to-all-start.8
  625.0 2.3 collective-permute-done.64
  628.9 2.3 collective-permute-done.65
  633.3 2.4 collective-permute-start.67
  637.5 2.7 finish.4
  640.2 2.8 finish.5
  643.0 4.2 collective-permute-done.67
  649.4 2.8 finish.6
  652.2 2.8 finish.7
  (398 shorter events, 168.3 us)
Async XLA Ops:
  7.2 104.7 %all-gather.4.cloned.1.call-start = ((), (), s32[]{:S(2)}) async-start(), calls=%async_computation.10 | async-start | bytes 3932160 | tf_op jit(solution)/shard_map/gather_qkv/all_gather | solution.py:631
  13.7 60.1 %all-to-all-start = ((bf16[4,512,256]{2,1,0:T(8,128)(2,1)}), bf16[4,512,256]{2,1,0:T(8,128)(2,1)S(1)}, u32[]{:S(2)}, u32[]{:S(2)}) async-start(bf16[4,512,256]{2,1,0:T(8,128)(2,1)} %pad_maximum_fusion), calls=%async_computation | async-start | bytes 2097152 | tf_op jit(solution)/shard_map/gate_row/all_to_all | solution.py:592
  20.1 118.6 %all-gather.6.cloned.1.call-start = ((), (), s32[]{:S(2)}) async-start(), calls=%async_computation.11 | async-start | bytes 1310720 | tf_op jit(solution)/shard_map/gather_qkv/all_gather | solution.py:639
  20.1 15.2 %collective-permute-start = (bf16[1024,256]{1,0:T(8,128)(2,1)}, bf16[1024,256]{1,0:T(8,128)(2,1)}, u32[]{:S(2)}, u32[]{:S(2)}) collective-permute-start(bf16[1024,256]{1,0:T(8,128)(2,1)} %param.13), channel_id=1, source_target_pairs={{0,2},{1,3},{2,0},{3,1},{4,6},{5,7},{6,4},{7,5},{8,10},{9,11},{10,... | collective-permute-start | bytes 1572872 | tf_op jit(solution)/shard_map/inputs/ppermute | solution.py:505
  21.6 24.7 %collective-permute-start.1 = (bf16[1024,256]{1,0:T(8,128)(2,1)}, bf16[1024,256]{1,0:T(8,128)(2,1)}, u32[]{:S(2)}, u32[]{:S(2)}) collective-permute-start(bf16[1024,256]{1,0:T(8,128)(2,1)} %param.13), channel_id=1, source_target_pairs={{0,4},{1,5},{2,6},{3,7},{4,0},{5,1},{6,2},{7,3},{8,12},{9,13},{10,... | collective-permute-start | bytes 1572872 | tf_op jit(solution)/shard_map/inputs/ppermute | solution.py:505
  23.1 24.3 %collective-permute-start.2 = (bf16[1024,256]{1,0:T(8,128)(2,1)}, bf16[1024,256]{1,0:T(8,128)(2,1)}, u32[]{:S(2)}, u32[]{:S(2)}) collective-permute-start(bf16[1024,256]{1,0:T(8,128)(2,1)} %param.13), channel_id=1, source_target_pairs={{0,6},{1,7},{2,4},{3,5},{4,2},{5,3},{6,0},{7,1},{8,14},{9,15},{10,... | collective-permute-start | bytes 1572872 | tf_op jit(solution)/shard_map/inputs/ppermute | solution.py:505
  48.5 63.4 %collective-permute-start.5 = (bf16[1024,1024]{1,0:T(8,128)(2,1)S(1)}, bf16[1024,1024]{1,0:T(8,128)(2,1)}, u32[]{:S(2)}, u32[]{:S(2)}) collective-permute-start(bf16[1024,1024]{1,0:T(8,128)(2,1)S(1)} %constant_dynamic-update-slice_fusion.12.own_ref.x_own), channel_id=1, source_target_pairs={{0,1},{1,0},{2,3},{3,2},{4,5},{5,4},{6,7},{7,6},{8,9},{9,8},{10,11... | collective-permute-start | bytes 6291464 | tf_op jit(solution)/shard_map/inputs/ppermute | solution.py:502
  73.9 24.7 %collective-permute-start.4 = (bf16[2048,256]{1,0:T(8,128)(2,1)S(1)}, bf16[2048,256]{1,0:T(8,128)(2,1)}, u32[]{:S(2)}, u32[]{:S(2)}) collective-permute-start(bf16[2048,256]{1,0:T(8,128)(2,1)S(1)} %bitcast.101), channel_id=1, source_target_pairs={{0,4},{1,5},{2,6},{3,7},{4,0},{5,1},{6,2},{7,3},{8,12},{9,13},{10,... | collective-permute-start | bytes 3145736 | tf_op jit(solution)/shard_map/gate_plane/ppermute | solution.py:505
  76.1 28.7 %collective-permute-start.3 = (bf16[2048,256]{1,0:T(8,128)(2,1)S(1)}, bf16[2048,256]{1,0:T(8,128)(2,1)}, u32[]{:S(2)}, u32[]{:S(2)}) collective-permute-start(bf16[2048,256]{1,0:T(8,128)(2,1)S(1)} %bitcast.102), channel_id=1, source_target_pairs={{0,2},{1,3},{2,0},{3,1},{4,6},{5,7},{6,4},{7,5},{8,10},{9,11},{10,... | collective-permute-start | bytes 3145736 | tf_op jit(solution)/shard_map/gate_plane/ppermute | solution.py:505
  80.7 23.0 %all-to-all-start.1 = ((bf16[4,256,256]{2,1,0:T(8,128)(2,1)}), bf16[4,256,256]{2,1,0:T(8,128)(2,1)}, u32[]{:S(2)}, u32[]{:S(2)}) async-start(bf16[4,256,256]{2,1,0:T(8,128)(2,1)} %bitcast.112), calls=%async_computation.1 | async-start | bytes 1048576 | tf_op jit(solution)/shard_map/grad_plane/all_to_all | solution.py:564
  114.3 34.6 %all-to-all-start.2 = ((bf16[4,512,256]{2,1,0:T(8,128)(2,1)}), bf16[4,512,256]{2,1,0:T(8,128)(2,1)}, u32[]{:S(2)}, u32[]{:S(2)}) async-start(bf16[4,512,256]{2,1,0:T(8,128)(2,1)} %pad_maximum_fusion.2), calls=%async_computation.2 | async-start | bytes 2097152 | tf_op jit(solution)/shard_map/up_row/all_to_all | solution.py:592
  118.5 94.7 %all-gather.8.cloned.1.call-start = ((), (), s32[]{:S(2)}) async-start(), calls=%async_computation.12 | async-start | bytes 2621440 | tf_op jit(solution)/shard_map/grad_row/all_gather | solution.py:652
  150.1 57.7 %all-to-all-start.3 = ((bf16[4,512,256]{2,1,0:T(8,128)(2,1)}), bf16[4,512,256]{2,1,0:T(8,128)(2,1)}, u32[]{:S(2)}, u32[]{:S(2)}) async-start(bf16[4,512,256]{2,1,0:T(8,128)(2,1)} %pad_maximum_fusion.4), calls=%async_computation.3 | async-start | bytes 2097152 | tf_op jit(solution)/shard_map/down_row/all_to_all | solution.py:592
  157.3 26.2 %collective-permute-start.10 = (bf16[256,1024]{1,0:T(8,128)(2,1)S(1)}, bf16[256,1024]{1,0:T(8,128)(2,1)S(1)}, u32[]{:S(2)}, u32[]{:S(2)}) collective-permute-start(bf16[256,1024]{1,0:T(8,128)(2,1)S(1)} %get-tuple-element.198), channel_id=1, source_target_pairs={{0,4},{1,5},{2,6},{3,7},{4,0},{5,1},{6,2},{7,3},{8,12},{9,13},{10,... | collective-permute-start | bytes 1572872 | tf_op jit(solution)/shard_map/mix_plane/ppermute | solution.py:505
  158.9 24.6 %collective-permute-start.11 = (bf16[256,1024]{1,0:T(8,128)(2,1)S(1)}, bf16[256,1024]{1,0:T(8,128)(2,1)S(1)}, u32[]{:S(2)}, u32[]{:S(2)}) collective-permute-start(bf16[256,1024]{1,0:T(8,128)(2,1)S(1)} %get-tuple-element.197), channel_id=1, source_target_pairs={{0,6},{1,7},{2,4},{3,5},{4,2},{5,3},{6,0},{7,1},{8,14},{9,15},{10,... | collective-permute-start | bytes 1572872 | tf_op jit(solution)/shard_map/mix_plane/ppermute | solution.py:505
  160.3 24.6 %collective-permute-start.9 = (bf16[256,1024]{1,0:T(8,128)(2,1)S(1)}, bf16[256,1024]{1,0:T(8,128)(2,1)S(1)}, u32[]{:S(2)}, u32[]{:S(2)}) collective-permute-start(bf16[256,1024]{1,0:T(8,128)(2,1)S(1)} %get-tuple-element.196), channel_id=1, source_target_pairs={{0,2},{1,3},{2,0},{3,1},{4,6},{5,7},{6,4},{7,5},{8,10},{9,11},{10,... | collective-permute-start | bytes 1572872 | tf_op jit(solution)/shard_map/mix_plane/ppermute | solution.py:505
  160.9 53.7 %collective-permute-start.13 = (bf16[2048,256]{1,0:T(8,128)(2,1)}, bf16[2048,256]{1,0:T(8,128)(2,1)}, u32[]{:S(2)}, u32[]{:S(2)}) collective-permute-start(bf16[2048,256]{1,0:T(8,128)(2,1)} %bitcast.20.refs_7_), channel_id=1, source_target_pairs={{0,4},{1,5},{2,6},{3,7},{4,0},{5,1},{6,2},{7,3},{8,12},{9,13},{10,... | collective-permute-start | bytes 3145736 | tf_op jit(solution)/shard_map/up_plane/ppermute | solution.py:505
  162.4 52.2 %collective-permute-start.12 = (bf16[2048,256]{1,0:T(8,128)(2,1)}, bf16[2048,256]{1,0:T(8,128)(2,1)}, u32[]{:S(2)}, u32[]{:S(2)}) collective-permute-start(bf16[2048,256]{1,0:T(8,128)(2,1)} %bitcast.20.refs_7_), channel_id=1, source_target_pairs={{0,2},{1,3},{2,0},{3,1},{4,6},{5,7},{6,4},{7,5},{8,10},{9,11},{10,... | collective-permute-start | bytes 3145736 | tf_op jit(solution)/shard_map/up_plane/ppermute | solution.py:505
  207.8 33.3 %collective-permute-start.19 = (bf16[2048,256]{1,0:T(8,128)(2,1)}, bf16[2048,256]{1,0:T(8,128)(2,1)}, u32[]{:S(2)}, u32[]{:S(2)}) collective-permute-start(bf16[2048,256]{1,0:T(8,128)(2,1)} %bitcast.25.refs_8_.refs_1_), channel_id=1, source_target_pairs={{0,4},{1,5},{2,6},{3,7},{4,0},{5,1},{6,2},{7,3},{8,12},{9,13},{10,... | collective-permute-start | bytes 3145736 | tf_op jit(solution)/shard_map/down_plane/ppermute | solution.py:505
  209.3 31.8 %collective-permute-start.18 = (bf16[2048,256]{1,0:T(8,128)(2,1)}, bf16[2048,256]{1,0:T(8,128)(2,1)}, u32[]{:S(2)}, u32[]{:S(2)}) collective-permute-start(bf16[2048,256]{1,0:T(8,128)(2,1)} %bitcast.25.refs_8_.refs_1_), channel_id=1, source_target_pairs={{0,2},{1,3},{2,0},{3,1},{4,6},{5,7},{6,4},{7,5},{8,10},{9,11},{10,... | collective-permute-start | bytes 3145736 | tf_op jit(solution)/shard_map/down_plane/ppermute | solution.py:505
  213.3 58.2 %collective-permute-start.17 = (bf16[1024,1024]{1,0:T(8,128)(2,1)}, bf16[1024,1024]{1,0:T(8,128)(2,1)}, u32[]{:S(2)}, u32[]{:S(2)}) collective-permute-start(bf16[1024,1024]{1,0:T(8,128)(2,1)} %all-gather.8.cloned.1.call-done.refs_4_.refs_0_), channel_id=1, source_target_pairs={{0,1},{1,0},{2,3},{3,2},{4,5},{5,4},{6,7},{7,6},{8,9},{9,8},{10,11... | collective-permute-start | bytes 6291464 | tf_op jit(solution)/shard_map/grad_row/ppermute | solution.py:502
  214.6 24.9 %collective-permute-start.24 = (bf16[256,1024]{1,0:T(8,128)(2,1)S(1)}, bf16[256,1024]{1,0:T(8,128)(2,1)S(1)}, u32[]{:S(2)}, u32[]{:S(2)}) collective-permute-start(bf16[256,1024]{1,0:T(8,128)(2,1)S(1)} %convert_element_type.303.refs_0_), channel_id=1, source_target_pairs={{0,16},{8,24},{16,0},{24,8},{1,17},{9,25},{17,1},{25,9},{2,18},{10... | collective-permute-start | bytes 1572872 | tf_op jit(solution)/shard_map/middle_row/ppermute | solution.py:519
  215.8 31.1 %collective-permute-start.20 = (bf16[1024,256]{1,0:T(8,128)(2,1)S(1)}, bf16[1024,256]{1,0:T(8,128)(2,1)}, u32[]{:S(2)}, u32[]{:S(2)}) collective-permute-start(bf16[1024,256]{1,0:T(8,128)(2,1)S(1)} %slice.312), channel_id=1, source_target_pairs={{0,2},{1,3},{2,0},{3,1},{4,6},{5,7},{6,4},{7,5},{8,10},{9,11},{10,... | collective-permute-start | bytes 1572872 | tf_op jit(solution)/shard_map/up_plane/ppermute | solution.py:505
  239.6 14.0 %collective-permute-start.21 = (bf16[1024,256]{1,0:T(8,128)(2,1)S(1)}, bf16[1024,256]{1,0:T(8,128)(2,1)}, u32[]{:S(2)}, u32[]{:S(2)}) collective-permute-start(bf16[1024,256]{1,0:T(8,128)(2,1)S(1)} %slice.313), channel_id=1, source_target_pairs={{0,4},{1,5},{2,6},{3,7},{4,0},{5,1},{6,2},{7,3},{8,12},{9,13},{10,... | collective-permute-start | bytes 1572872 | tf_op jit(solution)/shard_map/up_plane/ppermute | solution.py:505
  241.1 14.9 %collective-permute-start.14 = (bf16[256,1024]{1,0:T(8,128)(2,1)S(1)}, bf16[256,1024]{1,0:T(8,128)(2,1)}, u32[]{:S(2)}, u32[]{:S(2)}) collective-permute-start(bf16[256,1024]{1,0:T(8,128)(2,1)S(1)} %convert_element_type.303.refs_0_), channel_id=1, source_target_pairs={{0,8},{8,0},{16,24},{24,16},{1,9},{9,1},{17,25},{25,17},{2,10},{10... | collective-permute-start | bytes 1572872 | tf_op jit(solution)/shard_map/middle_row/ppermute | solution.py:519
  241.1 25.0 %collective-permute-start.25 = (bf16[256,1024]{1,0:T(8,128)(2,1)S(1)}, bf16[256,1024]{1,0:T(8,128)(2,1)}, u32[]{:S(2)}, u32[]{:S(2)}) collective-permute-start(bf16[256,1024]{1,0:T(8,128)(2,1)S(1)} %collective-permute-done.24.refs_0_.refs_2_), channel_id=1, source_target_pairs={{0,8},{8,0},{16,24},{24,16},{1,9},{9,1},{17,25},{25,17},{2,10},{10... | collective-permute-start | bytes 1572872 | tf_op jit(solution)/shard_map/middle_row/ppermute | solution.py:519
  246.9 20.4 %collective-permute-start.22 = (bf16[1024,256]{1,0:T(8,128)(2,1)}, bf16[1024,256]{1,0:T(8,128)(2,1)}, u32[]{:S(2)}, u32[]{:S(2)}) collective-permute-start(bf16[1024,256]{1,0:T(8,128)(2,1)} %slice.314), channel_id=1, source_target_pairs={{0,2},{1,3},{2,0},{3,1},{4,6},{5,7},{6,4},{7,5},{8,10},{9,11},{10,... | collective-permute-start | bytes 1572872 | tf_op jit(solution)/shard_map/down_plane/ppermute | solution.py:505
  253.6 14.2 %collective-permute-start.23 = (bf16[1024,256]{1,0:T(8,128)(2,1)}, bf16[1024,256]{1,0:T(8,128)(2,1)}, u32[]{:S(2)}, u32[]{:S(2)}) collective-permute-start(bf16[1024,256]{1,0:T(8,128)(2,1)} %slice.315), channel_id=1, source_target_pairs={{0,4},{1,5},{2,6},{3,7},{4,0},{5,1},{6,2},{7,3},{8,12},{9,13},{10,... | collective-permute-start | bytes 1572872 | tf_op jit(solution)/shard_map/down_plane/ppermute | solution.py:505
  256.0 15.5 %collective-permute-start.15 = (bf16[256,1024]{1,0:T(8,128)(2,1)S(1)}, bf16[256,1024]{1,0:T(8,128)(2,1)S(1)}, u32[]{:S(2)}, u32[]{:S(2)}) collective-permute-start(bf16[256,1024]{1,0:T(8,128)(2,1)S(1)} %convert_element_type.303.refs_0_), channel_id=1, source_target_pairs={{0,1},{1,0},{2,3},{3,2},{4,5},{5,4},{6,7},{7,6},{8,9},{9,8},{10,11... | collective-permute-start | bytes 1572872 | tf_op jit(solution)/shard_map/middle_row/ppermute | solution.py:502
  267.2 33.8 %collective-permute-start.26 = (bf16[256,1024]{1,0:T(8,128)(2,1)S(1)}, bf16[256,1024]{1,0:T(8,128)(2,1)}, u32[]{:S(2)}, u32[]{:S(2)}) collective-permute-start(bf16[256,1024]{1,0:T(8,128)(2,1)S(1)} %collective-permute-done.24.refs_0_.refs_2_), channel_id=1, source_target_pairs={{0,1},{1,0},{2,3},{3,2},{4,5},{5,4},{6,7},{7,6},{8,9},{9,8},{10,11... | collective-permute-start | bytes 1572872 | tf_op jit(solution)/shard_map/middle_row/ppermute | solution.py:502
  267.8 33.2 %collective-permute-start.27 = (bf16[256,1024]{1,0:T(8,128)(2,1)}, bf16[256,1024]{1,0:T(8,128)(2,1)}, u32[]{:S(2)}, u32[]{:S(2)}) collective-permute-start(bf16[256,1024]{1,0:T(8,128)(2,1)} %collective-permute-done.25.refs_1_.refs_3_), channel_id=1, source_target_pairs={{0,1},{1,0},{2,3},{3,2},{4,5},{5,4},{6,7},{7,6},{8,9},{9,8},{10,11... | collective-permute-start | bytes 1572872 | tf_op jit(solution)/shard_map/middle_row/ppermute | solution.py:502
  300.5 24.6 %collective-permute-start.31 = (bf16[256,1024]{1,0:T(8,128)(2,1)}, bf16[256,1024]{1,0:T(8,128)(2,1)}, u32[]{:S(2)}, u32[]{:S(2)}) collective-permute-start(bf16[256,1024]{1,0:T(8,128)(2,1)} %get-tuple-element.118), channel_id=1, source_target_pairs={{0,1},{1,0},{2,3},{3,2},{4,5},{5,4},{6,7},{7,6},{8,9},{9,8},{10,11... | collective-permute-start | bytes 1572872 | tf_op jit(solution)/shard_map/unit_grad/ppermute | solution.py:502
  327.1 14.5 %collective-permute-start.30 = (bf16[256,1024]{1,0:T(8,128)(2,1)S(1)}, bf16[256,1024]{1,0:T(8,128)(2,1)S(1)}, u32[]{:S(2)}, u32[]{:S(2)}) collective-permute-start(bf16[256,1024]{1,0:T(8,128)(2,1)S(1)} %add_convert_fusion.17), channel_id=1, source_target_pairs={{0,8},{8,0},{16,24},{24,16},{1,9},{9,1},{17,25},{25,17},{2,10},{10... | collective-permute-start | bytes 1572872 | tf_op jit(solution)/shard_map/unit_grad/ppermute | solution.py:519
  334.0 14.2 %collective-permute-start.38 = (bf16[1024,256]{1,0:T(8,128)(2,1)S(1)}, bf16[1024,256]{1,0:T(8,128)(2,1)S(1)}, u32[]{:S(2)}, u32[]{:S(2)}) collective-permute-start(bf16[1024,256]{1,0:T(8,128)(2,1)S(1)} %get-tuple-element.203), channel_id=1, source_target_pairs={{0,4},{1,5},{2,6},{3,7},{4,0},{5,1},{6,2},{7,3},{8,12},{9,13},{10,... | collective-permute-start | bytes 1572872 | tf_op jit(solution)/shard_map/down_grad/ppermute | solution.py:505
  334.5 16.4 %collective-permute-start.28 = (bf16[256,1024]{1,0:T(8,128)(2,1)S(1)}, bf16[256,1024]{1,0:T(8,128)(2,1)S(1)}, u32[]{:S(2)}, u32[]{:S(2)}) collective-permute-start(bf16[256,1024]{1,0:T(8,128)(2,1)S(1)} %get-tuple-element.114), channel_id=1, source_target_pairs={{0,1},{1,0},{2,3},{3,2},{4,5},{5,4},{6,7},{7,6},{8,9},{9,8},{10,11... | collective-permute-start | bytes 1572872 | tf_op jit(solution)/shard_map/unit_grad/ppermute | solution.py:502
  334.8 32.2 %collective-permute-start.33 = (f32[256,1]{0,1:T(1,128)S(1)}, f32[256,1]{0,1:T(1,128)S(1)}, u32[]{:S(2)}, u32[]{:S(2)}) collective-permute-start(f32[256,1]{0,1:T(1,128)S(1)} %bitcast.127), channel_id=1, source_target_pairs={{0,1},{1,0},{2,3},{3,2},{4,5},{5,4},{6,7},{7,6},{8,9},{9,8},{10,11... | collective-permute-start | bytes 3080 | tf_op jit(solution)/shard_map/ppermute | solution.py:502
  335.1 51.3 %collective-permute-start.34 = (bf16[256,1024]{1,0:T(8,128)(2,1)S(1)}, bf16[256,1024]{1,0:T(8,128)(2,1)S(1)}, u32[]{:S(2)}, u32[]{:S(2)}) collective-permute-start(bf16[256,1024]{1,0:T(8,128)(2,1)S(1)} %copy-done.40), channel_id=1, source_target_pairs={{0,1},{1,0},{2,3},{3,2},{4,5},{5,4},{6,7},{7,6},{8,9},{9,8},{10,11... | collective-permute-start | bytes 1572872 | tf_op jit(solution)/shard_map/unit_grad/ppermute | solution.py:502
  341.5 26.0 %collective-permute-start.35 = (bf16[256,1024]{1,0:T(8,128)(2,1)S(1)}, bf16[256,1024]{1,0:T(8,128)(2,1)S(1)}, u32[]{:S(2)}, u32[]{:S(2)}) collective-permute-start(bf16[256,1024]{1,0:T(8,128)(2,1)S(1)} %add_convert_fusion.16), channel_id=1, source_target_pairs={{0,8},{8,0},{16,24},{24,16},{1,9},{9,1},{17,25},{25,17},{2,10},{10... | collective-permute-start | bytes 1572872 | tf_op jit(solution)/shard_map/unit_grad/ppermute | solution.py:519
  348.2 14.9 %collective-permute-start.40 = (bf16[1024,256]{1,0:T(8,128)(2,1)S(1)}, bf16[1024,256]{1,0:T(8,128)(2,1)S(1)}, u32[]{:S(2)}, u32[]{:S(2)}) collective-permute-start(bf16[1024,256]{1,0:T(8,128)(2,1)S(1)} %get-tuple-element.204), channel_id=1, source_target_pairs={{0,2},{1,3},{2,0},{3,1},{4,6},{5,7},{6,4},{7,5},{8,10},{9,11},{10,... | collective-permute-start | bytes 1572872 | tf_op jit(solution)/shard_map/down_grad/ppermute | solution.py:505
  351.0 39.6 %collective-permute-start.39 = (bf16[2048,256]{1,0:T(8,128)(2,1)}, bf16[2048,256]{1,0:T(8,128)(2,1)}, u32[]{:S(2)}, u32[]{:S(2)}) collective-permute-start(bf16[2048,256]{1,0:T(8,128)(2,1)} %pad_maximum_fusion.5), channel_id=1, source_target_pairs={{0,2},{1,3},{2,0},{3,1},{4,6},{5,7},{6,4},{7,5},{8,10},{9,11},{10,... | collective-permute-start | bytes 3145736 | tf_op jit(solution)/shard_map/down_grad/ppermute | solution.py:505
  363.1 23.3 %collective-permute-start.36 = (bf16[256,1024]{1,0:T(8,128)(2,1)}, bf16[256,1024]{1,0:T(8,128)(2,1)S(1)}, u32[]{:S(2)}, u32[]{:S(2)}) collective-permute-start(bf16[256,1024]{1,0:T(8,128)(2,1)} %add_convert_fusion.15), channel_id=1, source_target_pairs={{0,16},{8,24},{16,0},{24,8},{1,17},{9,25},{17,1},{25,9},{2,18},{10... | collective-permute-start | bytes 1572872 | tf_op jit(solution)/shard_map/unit_grad/ppermute | solution.py:519
  367.0 23.6 %collective-permute-start.41 = (bf16[2048,256]{1,0:T(8,128)(2,1)}, bf16[2048,256]{1,0:T(8,128)(2,1)}, u32[]{:S(2)}, u32[]{:S(2)}) collective-permute-start(bf16[2048,256]{1,0:T(8,128)(2,1)} %pad_maximum_fusion.6), channel_id=1, source_target_pairs={{0,4},{1,5},{2,6},{3,7},{4,0},{5,1},{6,2},{7,3},{8,12},{9,13},{10,... | collective-permute-start | bytes 3145736 | tf_op jit(solution)/shard_map/down_grad/ppermute | solution.py:505
  394.0 26.6 %collective-permute-start.44 = (bf16[256,1024]{1,0:T(8,128)(2,1)S(1)}, bf16[256,1024]{1,0:T(8,128)(2,1)S(1)}, u32[]{:S(2)}, u32[]{:S(2)}) collective-permute-start(bf16[256,1024]{1,0:T(8,128)(2,1)S(1)} %slice.267), channel_id=1, source_target_pairs={{0,8},{8,0},{16,24},{24,16},{1,9},{9,1},{17,25},{25,17},{2,10},{10... | collective-permute-start | bytes 1572872 | tf_op jit(solution)/shard_map/feed/ppermute | solution.py:519
  394.1 28.8 %collective-permute-start.48 = (bf16[256,1024]{1,0:T(8,128)(2,1)S(1)}, bf16[256,1024]{1,0:T(8,128)(2,1)S(1)}, u32[]{:S(2)}, u32[]{:S(2)}) collective-permute-start(bf16[256,1024]{1,0:T(8,128)(2,1)S(1)} %get-tuple-element.136), channel_id=1, source_target_pairs={{0,6},{1,7},{2,4},{3,5},{4,2},{5,3},{6,0},{7,1},{8,14},{9,15},{10,... | collective-permute-start | bytes 1572872 | tf_op jit(solution)/shard_map/middle_grad/ppermute | solution.py:505
  396.0 26.9 %collective-permute-start.47 = (bf16[256,1024]{1,0:T(8,128)(2,1)S(1)}, bf16[256,1024]{1,0:T(8,128)(2,1)S(1)}, u32[]{:S(2)}, u32[]{:S(2)}) collective-permute-start(bf16[256,1024]{1,0:T(8,128)(2,1)S(1)} %get-tuple-element.136), channel_id=1, source_target_pairs={{0,4},{1,5},{2,6},{3,7},{4,0},{5,1},{6,2},{7,3},{8,12},{9,13},{10,... | collective-permute-start | bytes 1572872 | tf_op jit(solution)/shard_map/middle_grad/ppermute | solution.py:505
  397.1 25.8 %collective-permute-start.46 = (bf16[256,1024]{1,0:T(8,128)(2,1)S(1)}, bf16[256,1024]{1,0:T(8,128)(2,1)S(1)}, u32[]{:S(2)}, u32[]{:S(2)}) collective-permute-start(bf16[256,1024]{1,0:T(8,128)(2,1)S(1)} %get-tuple-element.136), channel_id=1, source_target_pairs={{0,2},{1,3},{2,0},{3,1},{4,6},{5,7},{6,4},{7,5},{8,10},{9,11},{10,... | collective-permute-start | bytes 1572872 | tf_op jit(solution)/shard_map/middle_grad/ppermute | solution.py:505
  399.0 35.3 %collective-permute-start.42 = (bf16[256,1024]{1,0:T(8,128)(2,1)}, bf16[256,1024]{1,0:T(8,128)(2,1)}, u32[]{:S(2)}, u32[]{:S(2)}) collective-permute-start(bf16[256,1024]{1,0:T(8,128)(2,1)} %slice.265), channel_id=1, source_target_pairs={{0,8},{8,0},{16,24},{24,16},{1,9},{9,1},{17,25},{25,17},{2,10},{10... | collective-permute-start | bytes 1572872 | tf_op jit(solution)/shard_map/feed/ppermute | solution.py:519
  421.7 36.4 %collective-permute-start.45 = (bf16[256,1024]{1,0:T(8,128)(2,1)}, bf16[256,1024]{1,0:T(8,128)(2,1)}, u32[]{:S(2)}, u32[]{:S(2)}) collective-permute-start(bf16[256,1024]{1,0:T(8,128)(2,1)} %add_convert_fusion.12), channel_id=1, source_target_pairs={{0,16},{8,24},{16,0},{24,8},{1,17},{9,25},{17,1},{25,9},{2,18},{10... | collective-permute-start | bytes 1572872 | tf_op jit(solution)/shard_map/feed/ppermute | solution.py:519
  425.4 39.2 %collective-permute-start.53 = (bf16[1024,1024]{1,0:T(8,128)(2,1)}, bf16[1024,1024]{1,0:T(8,128)(2,1)}, u32[]{:S(2)}, u32[]{:S(2)}) collective-permute-start(bf16[1024,1024]{1,0:T(8,128)(2,1)} %constant_dynamic-update-slice_fusion.8.own_ref.d_own), channel_id=1, source_target_pairs={{0,1},{1,0},{2,3},{3,2},{4,5},{5,4},{6,7},{7,6},{8,9},{9,8},{10,11... | collective-permute-start | bytes 6291464 | tf_op jit(solution)/shard_map/middle_grad/ppermute | solution.py:502
  426.6 31.5 %collective-permute-start.49 = (bf16[1024,256]{1,0:T(8,128)(2,1)}, bf16[1024,256]{1,0:T(8,128)(2,1)}, u32[]{:S(2)}, u32[]{:S(2)}) collective-permute-start(bf16[1024,256]{1,0:T(8,128)(2,1)} %get-tuple-element.201), channel_id=1, source_target_pairs={{0,4},{1,5},{2,6},{3,7},{4,0},{5,1},{6,2},{7,3},{8,12},{9,13},{10,... | collective-permute-start | bytes 1572872 | tf_op jit(solution)/shard_map/gate_grad/ppermute | solution.py:505
  427.4 52.9 %all-to-all-start.6 = ((bf16[4,512,256]{2,1,0:T(8,128)(2,1)}), bf16[4,512,256]{2,1,0:T(8,128)(2,1)}, u32[]{:S(2)}, u32[]{:S(2)}) async-start(bf16[4,512,256]{2,1,0:T(8,128)(2,1)} %bitcast.109), calls=%async_computation.6 | async-start | bytes 2097152 | tf_op jit(solution)/shard_map/down_grad/all_to_all | solution.py:625
  431.7 220.5 %reduce-scatter.2.cloned.1.call-start = ((), (), s32[]{:S(2)}) async-start(), calls=%async_computation.13 | async-start | bytes 5242880 | tf_op jit(solution)/shard_map/heads_grad/reduce_scatter | solution.py:762
  431.9 28.4 %collective-permute-start.51 = (bf16[1024,256]{1,0:T(8,128)(2,1)}, bf16[1024,256]{1,0:T(8,128)(2,1)S(1)}, u32[]{:S(2)}, u32[]{:S(2)}) collective-permute-start(bf16[1024,256]{1,0:T(8,128)(2,1)} %get-tuple-element.202), channel_id=1, source_target_pairs={{0,2},{1,3},{2,0},{3,1},{4,6},{5,7},{6,4},{7,5},{8,10},{9,11},{10,... | collective-permute-start | bytes 1572872 | tf_op jit(solution)/shard_map/gate_grad/ppermute | solution.py:505
  494.0 25.3 %collective-permute-start.50 = (bf16[2048,256]{1,0:T(8,128)(2,1)}, bf16[2048,256]{1,0:T(8,128)(2,1)S(1)}, u32[]{:S(2)}, u32[]{:S(2)}) collective-permute-start(bf16[2048,256]{1,0:T(8,128)(2,1)} %pad_maximum_fusion.7), channel_id=1, source_target_pairs={{0,2},{1,3},{2,0},{3,1},{4,6},{5,7},{6,4},{7,5},{8,10},{9,11},{10,... | collective-permute-start | bytes 3145736 | tf_op jit(solution)/shard_map/gate_grad/ppermute | solution.py:505
  495.5 24.9 %collective-permute-start.52 = (bf16[2048,256]{1,0:T(8,128)(2,1)}, bf16[2048,256]{1,0:T(8,128)(2,1)S(1)}, u32[]{:S(2)}, u32[]{:S(2)}) collective-permute-start(bf16[2048,256]{1,0:T(8,128)(2,1)} %pad_maximum_fusion.8), channel_id=1, source_target_pairs={{0,4},{1,5},{2,6},{3,7},{4,0},{5,1},{6,2},{7,3},{8,12},{9,13},{10,... | collective-permute-start | bytes 3145736 | tf_op jit(solution)/shard_map/gate_grad/ppermute | solution.py:505
  504.1 36.0 %collective-permute-start.54 = (bf16[1024,1024]{1,0:T(8,128)(2,1)}, bf16[1024,1024]{1,0:T(8,128)(2,1)}, u32[]{:S(2)}, u32[]{:S(2)}) collective-permute-start(bf16[1024,1024]{1,0:T(8,128)(2,1)} %get-tuple-element.171), channel_id=1, source_target_pairs={{0,1},{1,0},{2,3},{3,2},{4,5},{5,4},{6,7},{7,6},{8,9},{9,8},{10,11... | collective-permute-start | bytes 6291464 | tf_op jit(solution)/shard_map/first_plane/ppermute | solution.py:502
  524.0 58.0 %all-to-all-start.4 = ((bf16[4,512,256]{2,1,0:T(8,128)(2,1)}), bf16[4,512,256]{2,1,0:T(8,128)(2,1)}, u32[]{:S(2)}, u32[]{:S(2)}) async-start(bf16[4,512,256]{2,1,0:T(8,128)(2,1)} %bitcast.105), calls=%async_computation.4 | async-start | bytes 2097152 | tf_op jit(solution)/shard_map/gate_grad/all_to_all | solution.py:625
  531.4 16.0 %collective-permute-start.61 = (bf16[1024,256]{1,0:T(8,128)(2,1)}, bf16[1024,256]{1,0:T(8,128)(2,1)}, u32[]{:S(2)}, u32[]{:S(2)}) collective-permute-start(bf16[1024,256]{1,0:T(8,128)(2,1)} %get-tuple-element.200), channel_id=1, source_target_pairs={{0,2},{1,3},{2,0},{3,1},{4,6},{5,7},{6,4},{7,5},{8,10},{9,11},{10,... | collective-permute-start | bytes 1572872 | tf_op jit(solution)/shard_map/up_grad/ppermute | solution.py:505
  539.5 69.8 %collective-permute-start.60 = (bf16[2048,256]{1,0:T(8,128)(2,1)}, bf16[2048,256]{1,0:T(8,128)(2,1)}, u32[]{:S(2)}, u32[]{:S(2)}) collective-permute-start(bf16[2048,256]{1,0:T(8,128)(2,1)} %pad_maximum_fusion.9), channel_id=1, source_target_pairs={{0,2},{1,3},{2,0},{3,1},{4,6},{5,7},{6,4},{7,5},{8,10},{9,11},{10,... | collective-permute-start | bytes 3145736 | tf_op jit(solution)/shard_map/up_grad/ppermute | solution.py:505
  543.9 39.2 %collective-permute-start.55 = (bf16[256,1024]{1,0:T(8,128)(2,1)}, bf16[256,1024]{1,0:T(8,128)(2,1)}, u32[]{:S(2)}, u32[]{:S(2)}) collective-permute-start(bf16[256,1024]{1,0:T(8,128)(2,1)} %get-tuple-element.193), channel_id=1, source_target_pairs={{0,2},{1,3},{2,0},{3,1},{4,6},{5,7},{6,4},{7,5},{8,10},{9,11},{10,... | collective-permute-start | bytes 1572872 | tf_op jit(solution)/shard_map/first_plane/ppermute | solution.py:505
  545.3 37.8 %collective-permute-start.56 = (bf16[256,1024]{1,0:T(8,128)(2,1)}, bf16[256,1024]{1,0:T(8,128)(2,1)}, u32[]{:S(2)}, u32[]{:S(2)}) collective-permute-start(bf16[256,1024]{1,0:T(8,128)(2,1)} %get-tuple-element.195), channel_id=1, source_target_pairs={{0,4},{1,5},{2,6},{3,7},{4,0},{5,1},{6,2},{7,3},{8,12},{9,13},{10,... | collective-permute-start | bytes 1572872 | tf_op jit(solution)/shard_map/first_plane/ppermute | solution.py:505
  546.3 43.4 %collective-permute-start.57 = (bf16[256,1024]{1,0:T(8,128)(2,1)}, bf16[256,1024]{1,0:T(8,128)(2,1)}, u32[]{:S(2)}, u32[]{:S(2)}) collective-permute-start(bf16[256,1024]{1,0:T(8,128)(2,1)} %get-tuple-element.194), channel_id=1, source_target_pairs={{0,6},{1,7},{2,4},{3,5},{4,2},{5,3},{6,0},{7,1},{8,14},{9,15},{10,... | collective-permute-start | bytes 1572872 | tf_op jit(solution)/shard_map/first_plane/ppermute | solution.py:505
  549.6 59.7 %collective-permute-start.62 = (bf16[2048,256]{1,0:T(8,128)(2,1)}, bf16[2048,256]{1,0:T(8,128)(2,1)}, u32[]{:S(2)}, u32[]{:S(2)}) collective-permute-start(bf16[2048,256]{1,0:T(8,128)(2,1)} %pad_maximum_fusion.10), channel_id=1, source_target_pairs={{0,4},{1,5},{2,6},{3,7},{4,0},{5,1},{6,2},{7,3},{8,12},{9,13},{10,... | collective-permute-start | bytes 3145736 | tf_op jit(solution)/shard_map/up_grad/ppermute | solution.py:505
  617.4 31.0 %all-to-all-start.8 = ((bf16[4,512,256]{2,1,0:T(8,128)(2,1)}), bf16[4,512,256]{2,1,0:T(8,128)(2,1)S(1)}, u32[]{:S(2)}, u32[]{:S(2)}) async-start(bf16[4,512,256]{2,1,0:T(8,128)(2,1)} %bitcast.48), calls=%async_computation.9 | async-start | bytes 2097152 | tf_op jit(solution)/shard_map/up_grad/all_to_all | solution.py:625
  (90 other events, 706.9 us)
Sparse Core Ops, SparseCore 0:
  10.5 86.1 all-gather.3
  98.9 37.1 all-gather.5
  143.9 69.3 all-gather.7
  494.1 92.7 reduce-scatter.1

commit v6 on v5

--- a/solution.py
+++ b/solution.py
@@ -61,35 +61,39 @@
     return pl.BlockSpec((block, a.shape[1]), lambda i: (i, 0))
 
 
-def project_kernel(feat, own_ref, other_ref, weight_ref, cos_ref, front_ref, back_ref, q_ref, k_ref, v_ref, scale_ref):
-    values = weave(own_ref[...], other_ref[...], feat)
-    scale = norm_scale(values)
-    scale_ref[...] = scale
-    heads = q_ref.shape[1]
+def project_kernel(feat, starts, own_ref, other_ref, *refs):
+    weights, (cos_ref, front_ref, back_ref), outs = refs[:-7], refs[-7:-4], refs[-4:]
+    scale = norm_scale(jnp.concatenate([own_ref[...], other_ref[...]], axis=1))
+    outs[3][...] = scale
+    heads = outs[0].shape[1]
+    picks = [pl.ds(pl.multiple_of(starts[i] * feat, feat), feat) for i in range(len(weights))]
+    values = jnp.concatenate([ref[:, pick] for pick in picks for ref in (own_ref, other_ref)], axis=1)
     cosine, front, back = cos_ref[...], front_ref[...], back_ref[...]
-    for at, ref in enumerate((q_ref, k_ref, v_ref)):
-        result = nn(values, weight_ref[:, at * heads : (at + 1) * heads]) * scale
+    for at, ref in enumerate(outs[:3]):
+        columns = slice(at * heads, (at + 1) * heads)
+        result = nn(values, jnp.concatenate([w[:, columns] for w in weights], axis=0)) * scale
         if at < 2:
             result = spin(result, cosine, front, back)
         ref[...] = result.astype(BF16)
 
 
-def project(feat, own, other, weight, cosine, front, back):
+def project(feat, starts, own, other, weights, cosine, front, back):
     tokens = own.shape[0]
-    heads = weight.shape[1] // 3
+    heads = weights[0].shape[1] // 3
     block = 256
     result = jax.ShapeDtypeStruct((tokens, heads), BF16)
     scale = jax.ShapeDtypeStruct((tokens, 1), F32)
     return pl.pallas_call(
         functools.partial(project_kernel, feat),
         grid=(tokens // block,),
-        in_specs=[row_spec(block, own), row_spec(block, other), whole_spec(weight)]
+        in_specs=[pl.BlockSpec(memory_space=pltpu.SMEM), row_spec(block, own), row_spec(block, other)]
+        + [whole_spec(w) for w in weights]
         + [row_spec(block, cosine)] * 3,
         out_specs=[row_spec(block, result)] * 3 + [row_spec(block, scale)],
         out_shape=[result] * 3 + [scale],
-        compiler_params=pltpu.CompilerParams(vmem_limit_bytes=VMEM_BYTES),
+        compiler_params=pltpu.CompilerParams(vmem_limit_bytes=40 * 1024 * 1024),
         name="project",
-    )(own, other, weight, cosine, front, back)
+    )(starts, own, other, *weights, cosine, front, back)
 
 
 def unfold_kernel(feat, joined, *refs):
@@ -122,15 +126,61 @@
     )(*lefts, *weights)
 
 
-def units_kernel(feat, parts, count, starts, *refs):
-    m_owns, m_others = refs[:parts], refs[parts : 2 * parts]
-    g_sources = refs[2 * parts : 2 * parts + 2]
-    refs = refs[2 * parts + 2 :]
-    sources, refs = refs[: 3 * count], refs[3 * count :]
-    hidden_ref, gate_ref, up_ref = refs[:3]
-    own_refs, other_refs = refs[3 : 3 + parts], refs[3 + parts : 3 + 2 * parts]
-    held, arrived, g_held, g_arrived = refs[3 + 2 * parts :]
-    tokens = own_refs[0].shape[0]
+def activate_kernel(feat, parts, count, *refs):
+    m_owns, m_others, refs = refs[:parts], refs[parts : 2 * parts], refs[2 * parts :]
+    sources, refs = refs[: 2 * count], refs[2 * count :]
+    hidden_ref, gate_ref, up_ref, scale_ref, held, arrived = refs
+    copies = [
+        pltpu.make_async_copy(source, held.at[at], arrived.at[at]) for at, source in enumerate(sources)
+    ]
+    for copy in copies:
+        copy.start()
+    middle = jnp.concatenate(
+        [weave(a[...], b[...], feat) for a, b in zip(m_owns, m_others)], axis=0
+    )
+    scale = norm_scale(middle)
+    scale_ref[...] = scale
+    part = hidden_ref.shape[1] // count
+    for i in range(count):
+        if i % 2 == 0:
+            for copy in copies[2 * i : 2 * i + 4]:
+                copy.wait()
+        columns = slice(i * part, (i + 1) * part)
+        gate = nn(middle, held[2 * i]) * scale
+        up = nn(middle, held[2 * i + 1]) * scale
+        sigmoid = 1.0 / (1.0 + jnp.exp(-gate))
+        silu = gate * sigmoid
+        hidden_ref[:, columns] = (silu * up).astype(BF16)
+        gate_ref[:, columns] = (up * (sigmoid + silu * (1.0 - sigmoid))).astype(BF16)
+        up_ref[:, columns] = silu.astype(BF16)
+
+
+def activate(feat, m_owns, m_others, gates, ups):
+    parts = len(m_owns)
+    tokens = m_owns[0].shape[0]
+    count, part = len(gates), gates[0].shape[1]
+    hidden = jax.ShapeDtypeStruct((parts * tokens, count * part), BF16)
+    weights = [w for two in zip(gates, ups) for w in two]
+    vmem, anywhere = pl.BlockSpec(memory_space=pltpu.VMEM), pl.BlockSpec(memory_space=pl.ANY)
+    return pl.pallas_call(
+        functools.partial(activate_kernel, feat, parts, count),
+        in_specs=[vmem] * (2 * parts) + [anywhere] * len(weights),
+        out_specs=[vmem] * 4,
+        out_shape=[hidden] * 3 + [jax.ShapeDtypeStruct((parts * tokens, 1), F32)],
+        scratch_shapes=[
+            pltpu.VMEM((len(weights),) + weights[0].shape, BF16),
+            pltpu.SemaphoreType.DMA((len(weights),)),
+        ],
+        compiler_params=pltpu.CompilerParams(vmem_limit_bytes=36 * 1024 * 1024),
+        name="activate",
+    )(*m_owns, *m_others, *weights)
+
+
+def units_back_kernel(feat, parts, count, starts, *refs):
+    g_sources, (gate_in, up_in, scale_in) = refs[:2], refs[2:5]
+    sources, refs = refs[5 : 5 + 3 * count], refs[5 + 3 * count :]
+    gate_ref, up_ref, own_ref, other_ref, held, arrived, g_held, g_arrived = refs
+    tokens = own_ref.shape[0] // parts
     copies = [
         pltpu.make_async_copy(source, held.at[at], arrived.at[at]) for at, source in enumerate(sources)
     ]
@@ -143,75 +193,57 @@
         for side, source in enumerate(g_sources)
         for i in range(parts)
     ]
-    for copy in copies[:2] + g_copies + copies[2:]:
+    for copy in g_copies + copies:
         copy.start()
-    middle = jnp.concatenate(
-        [weave(a[...], b[...], feat) for a, b in zip(m_owns, m_others)], axis=0
-    )
-    scale = norm_scale(middle)
-    part = hidden_ref.shape[1] // count
-    pairs = []
-    grad = None
+    for copy in g_copies + copies[:count]:
+        copy.wait()
+    grad = jnp.concatenate([weave(g_held[0, j], g_held[1, j], feat) for j in range(parts)], axis=0)
+    scale = scale_in[...]
+    part = gate_ref.shape[1] // count
+    lefts = [], []
     for i in range(count):
         columns = slice(i * part, (i + 1) * part)
-        copies[3 * i].wait()
-        gate = nn(middle, held[3 * i]) * scale
-        copies[3 * i + 1].wait()
-        up = nn(middle, held[3 * i + 1]) * scale
-        copies[3 * i + 2].wait()
-        if grad is None:
-            for copy in g_copies:
-                copy.wait()
-            grad = jnp.concatenate(
-                [weave(g_held[0, j], g_held[1, j], feat) for j in range(parts)], axis=0
-            )
-        hidden_grad = nn(grad, held[3 * i + 2])
-        sigmoid = 1.0 / (1.0 + jnp.exp(-gate))
-        silu = gate * sigmoid
-        hidden_ref[:, columns] = (silu * up).astype(BF16)
-        gate_grad = hidden_grad * up * (sigmoid + silu * (1.0 - sigmoid))
-        up_grad = hidden_grad * silu
-        pairs.append((gate_grad.astype(BF16), held.at[3 * i]))
-        pairs.append((up_grad.astype(BF16), held.at[3 * i + 1]))
-        gate_ref[:, columns] = (gate_grad * scale).astype(BF16)
-        up_ref[:, columns] = (up_grad * scale).astype(BF16)
-    for at in range(0, own_refs[0].shape[1], feat):
+        hidden_grad = nn(grad, held[i])
+        for side, (slope, out) in enumerate(((gate_in, gate_ref), (up_in, up_ref))):
+            value = hidden_grad * slope[:, columns].astype(F32)
+            out[:, columns] = (value * scale).astype(BF16)
+            lefts[side].append(value.astype(BF16))
+    left = jnp.concatenate(lefts[0] + lefts[1], axis=1)
+    for copy in copies[count:]:
+        copy.wait()
+    for at in range(0, own_ref.shape[1], feat):
         rows = slice(2 * at, 2 * (at + feat))
-        total = None
-        for left, weight in pairs:
-            term = nt(left, weight[rows, :])
-            total = term if total is None else total + term
-        for i, (own_ref, other_ref) in enumerate(zip(own_refs, other_refs)):
-            mine = total[i * tokens : (i + 1) * tokens]
-            own_ref[:, at : at + feat] = mine[:, :feat].astype(BF16)
-            other_ref[:, at : at + feat] = mine[:, feat:].astype(BF16)
-
-
-def units(feat, starts, m_owns, m_others, g_own, g_other, gates, ups, downs):
-    parts = len(m_owns)
-    tokens, half = m_owns[0].shape
-    count, part = len(gates), gates[0].shape[1]
-    hidden = jax.ShapeDtypeStruct((parts * tokens, count * part), BF16)
+        right = jnp.concatenate([held[i, rows, :] for i in range(count, 3 * count)], axis=1)
+        total = nt(left, right)
+        own_ref[:, at : at + feat] = total[:, :feat].astype(BF16)
+        other_ref[:, at : at + feat] = total[:, feat:].astype(BF16)
+
+
+def units_back(feat, starts, g_own, g_other, gate, up, scale, gates, ups, downs):
+    tokens, half = gate.shape[0], g_own.shape[1]
+    parts = starts.shape[0]
+    count = len(gates)
+    hidden = jax.ShapeDtypeStruct(gate.shape, BF16)
     share = jax.ShapeDtypeStruct((tokens, half), BF16)
-    weights = [w for three in zip(gates, ups, downs) for w in three]
+    weights = downs + gates + ups
     vmem, anywhere = pl.BlockSpec(memory_space=pltpu.VMEM), pl.BlockSpec(memory_space=pl.ANY)
-    result = pl.pallas_call(
-        functools.partial(units_kernel, feat, parts, count),
+    return pl.pallas_call(
+        functools.partial(units_back_kernel, feat, parts, count),
         in_specs=[pl.BlockSpec(memory_space=pltpu.SMEM)]
-        + [vmem] * (2 * parts)
-        + [anywhere] * (2 + len(weights)),
-        out_specs=[vmem] * (3 + 2 * parts),
-        out_shape=[hidden] * 3 + [share] * (2 * parts),
+        + [anywhere] * 2
+        + [vmem] * 3
+        + [anywhere] * len(weights),
+        out_specs=[vmem] * 4,
+        out_shape=[hidden] * 2 + [share] * 2,
         scratch_shapes=[
             pltpu.VMEM((len(weights),) + weights[0].shape, BF16),
             pltpu.SemaphoreType.DMA((len(weights),)),
-            pltpu.VMEM((2, parts, tokens, half), BF16),
+            pltpu.VMEM((2, parts, tokens // parts, half), BF16),
             pltpu.SemaphoreType.DMA((2, parts)),
         ],
-        compiler_params=pltpu.CompilerParams(vmem_limit_bytes=48 * 1024 * 1024),
-        name="units",
-    )(starts, *m_owns, *m_others, g_own, g_other, *weights)
-    return result[0], result[1], result[2], result[3 : 3 + parts], result[3 + parts :]
+        compiler_params=pltpu.CompilerParams(vmem_limit_bytes=40 * 1024 * 1024),
+        name="units_back",
+    )(starts, g_own, g_other, gate, up, scale, *weights)
 
 
 def outer_kernel(groups, count, starts, *refs):
@@ -526,13 +558,16 @@
             bit //= 2
         return [got[step] for step in range(rows)]
 
-    def reduce_row(parts, *works):
+    def reduce_row(parts, *works, split=False):
         parts, bit, step = list(parts), 1, 0
         while bit < rows:
             lows = {at: parts[at + bit].astype(BF16) for at in range(rows - 2 * bit, -1, -2 * bit)}
             held = works[step](*lows.values()) if step < len(works) else ()
             for at, low in lows.items():
-                parts[at] = parts[at].astype(F32) + after(row_swap(low, bit), *held).astype(F32)
+                came = after(row_swap(low, bit), *held)
+                if split and 2 * bit == rows:
+                    return parts[0], came
+                parts[at] = parts[at].astype(F32) + came.astype(F32)
             bit, step = 2 * bit, step + 1
         return parts[0]
 
@@ -572,6 +607,9 @@
     def to_home(a):
         a = jnp.stack([a[:, s * feat : (s + 1) * feat] for s in range(places)])
         return plane_exchange(a).reshape(tokens, feat)
+
+    def to_home_swaps(a):
+        return put_rows([feat_part(a, 0)] + [plane_swap(feat_part(a, s), s) for s in range(1, places)])
 
     def sum_cols(a):
         step = 1
@@ -624,46 +662,49 @@
         total = total.reshape(rows, 2 * feat, total.shape[1])
         return lax.all_to_all(total, "row", split_axis=0, concat_axis=0, tiled=True)
 
+    def join_rows(pieces):
+        size = pieces[0].shape[0]
+        whole = jnp.zeros((rows * size, pieces[0].shape[1]), BF16)
+        for step, piece in enumerate(pieces):
+            whole = lax.dynamic_update_slice_in_dim(whole, piece, (row ^ step) * size, 0)
+        return whole
+
     starts = jnp.stack([row ^ s for s in range(rows)])
     cores = core.reshape(1)
 
-    with jax.named_scope("gather_qkv"):
-        qkv_full = lax.all_gather(
+    with jax.named_scope("qkv_row"):
+        qkv_list = gather_row(
             jnp.concatenate(
                 [scaled(w, gain_one) for w in (query_weight, key_weight, value_weight)], axis=1
-            ),
-            "row",
-            axis=0,
-            tiled=True,
-        )
-        out_full = lax.all_gather(own_first(out_weight), "row", axis=0, tiled=True)
+            )
+        )
     with jax.named_scope("inputs"):
         x_own = put_feats(spread(inputs))
         x_other = core_swap(x_own)
     with jax.named_scope("gate_row"):
         gate_whole = exchange(scaled(gate_weight, gain_two))
+    with jax.named_scope("out_row"):
+        out_full = lax.all_gather(
+            after(own_first(out_weight), *qkv_list[1:3]), "row", axis=0, tiled=True
+        )
     with jax.named_scope("grad_plane"):
         g_part = to_parts(after(out_grad, gate_whole))
     with jax.named_scope("up_row"):
-        up_whole = exchange(after(scaled(up_weight, gain_two), g_part, x_other, qkv_full))
+        up_whole = exchange(after(scaled(up_weight, gain_two), g_part, x_other, *qkv_list))
     with jax.named_scope("down_row"):
         down_whole = exchange(after(own_first(down_weight), up_whole))
-    with jax.named_scope("grad_row"):
-        g_own = lax.all_gather(after(g_part, out_full), "row", axis=0, tiled=True)
-        g_other = core_swap(g_own)
     with jax.named_scope("gate_plane"):
         gates = spread_weights(gate_whole)
-    with jax.named_scope("up_plane"):
-        ups = spread_weights(up_whole)
-
     heads_width = query_weight.shape[1]
     cosine, front, back = rope_tables(positions, heads_width)
     start_row = jnp.sum(
         (segment_ids[None, :] < segment_ids[:, None]).astype(jnp.int32), axis=1
     )[None, :]
-    x_ready = after(x_own, gates[1], gates[2])
-    query, key, value, scale_one = project(feat, x_ready, x_other, qkv_full, cosine, front, back)
-    mixed, logs = attend(query, key, value, start_row)
+    query, key, value, scale_one = project(
+        feat, starts, x_own, x_other, qkv_list, cosine, front, back
+    )
+    qkv_full = join_rows([after(a, query) for a in qkv_list])
+    mixed, logs = attend(after(query, gates[1], gates[2]), key, value, start_row)
     mixed = after(mixed, gates[3])
 
     def scatter_parts(own, other):
@@ -674,47 +715,54 @@
         return total
 
     with jax.named_scope("mix_plane"):
-        middle = token_part(x_own, 0).astype(F32) + scatter_parts(*unfold(feat, "mix", [mixed], [out_full]))
+        own, other = unfold(feat, "mix", [mixed], [out_full])
+        middle = token_part(x_own, 0).astype(F32) + scatter_parts(after(own, up_whole), other)
+        middle = after(middle, down_whole)
+    middle_low = middle.astype(BF16)
+    with jax.named_scope("middle_row"):
+        m_list = gather_row(middle_low)
+        m_others = [core_swap(m) for m in m_list]
+    with jax.named_scope("up_plane"):
+        ups = spread_weights(after(up_whole, middle_low))
+    with jax.named_scope("down_plane"):
+        downs = spread_weights(after(down_whole, ups[1], ups[2]))
+    with jax.named_scope("grad_row"):
+        g_own = lax.all_gather(after(g_part, out_full, *m_list[1:3]), "row", axis=0, tiled=True)
+        g_other = core_swap(g_own)
     square = jnp.sum(middle * middle, axis=1, keepdims=True)
     square = square + core_swap(square)
     scale_mid = lax.rsqrt(square / width + EPS)
 
-    with jax.named_scope("down_plane"):
-        downs = spread_weights(after(down_whole, middle))
-    with jax.named_scope("middle_row"):
-        m_list = gather_row(after(middle.astype(BF16), ups[1], ups[2], down_whole))
-        m_others = [core_swap(m) for m in m_list]
-    found, own_shares, other_shares = [], [], []
-    for at in range(0, rows, 2):
-        pick = slice(at, at + 2)
-        *three, owns, others = units(
-            feat, starts[pick], m_list[pick], m_others[pick], g_own, g_other, gates, ups, downs
-        )
-        found.append(three)
-        own_shares += owns
-        other_shares += others
-    kept = {}
-
-    def down_work(*lows):
-        with jax.named_scope("down_grad"):
-            kept["down"] = outer(
-                feat, "down_outer", starts, [g_own], [g_other], [after(f[0], *lows) for f in found], places
+    pairs = [slice(at, at + 2) for at in range(0, rows, 2)]
+    found = [activate(feat, m_list[pair], m_others[pair], gates, ups) for pair in pairs]
+    hiddens = [f[0] for f in found]
+    parts, scaled_grads, held, down_parts = [None] * rows, [None] * len(pairs), (), None
+    for at in reversed(range(len(pairs))):
+        with jax.named_scope("unit_grad"):
+            _, slope_gate, slope_up, scale = found[at]
+            gate_grad, up_grad, own, other = units_back(
+                feat, starts[pairs[at]], g_own, g_other, after(slope_gate, *held), slope_up, scale, gates, ups, downs
             )
-        return kept["down"][:1]
+            scaled_grads[at] = gate_grad, up_grad
+            low = own.astype(F32) + core_swap(other).astype(F32)
+            parts[2 * at], parts[2 * at + 1] = low[:quarter], low[quarter:].astype(BF16)
+        if down_parts is None:
+            with jax.named_scope("down_grad"):
+                down_parts = outer(
+                    feat, "down_outer", starts, [g_own], [g_other], [after(h, parts[-1]) for h in hiddens], places
+                )
+            held = down_parts[:1]
+    kept = []
 
     def feed_work(*lows):
         with jax.named_scope("feed"):
-            kept["feed"] = [unfold(feat, "feed", [after(f[0], *lows)], downs) for f in found]
-        return [own for own, _ in kept["feed"]]
+            kept.extend(unfold(feat, "feed", [after(h, *lows)], downs) for h in hiddens)
+        return [own for own, _ in kept]
 
     with jax.named_scope("unit_grad"):
-        unit_grad = reduce_row(
-            [own.astype(F32) + core_swap(other).astype(F32) for own, other in zip(own_shares, other_shares)],
-            down_work,
-            feed_work,
-        )
+        unit_grad = reduce_row(parts, lambda *lows: (), feed_work)
     with jax.named_scope("down_grad"):
-        down_total = plane_second(plane_first(kept["down"]))
+        down_total = plane_second(plane_first(down_parts))
         down_blocks = give_back(down_total)
 
     unit_mid = middle * scale_mid
@@ -725,12 +773,12 @@
     d_low = after(middle_grad.astype(BF16), down_total)
     with jax.named_scope("feed"):
         shares = []
-        for own, other in kept["feed"]:
+        for own, other in kept:
             low = own.astype(F32) + core_swap(other).astype(F32)
             low = after(low.astype(BF16), d_low)
             shares += [low[:quarter], low[quarter:]]
-    gate_parts = outer(feat, "gate_outer", starts, m_list, m_others, [after(f[1], d_low) for f in found], places)
-    up_parts = outer(feat, "up_outer", starts, m_list, m_others, [after(f[2], d_low) for f in found], places)
+    gate_parts = outer(feat, "gate_outer", starts, m_list, m_others, [after(a, d_low) for a, _ in scaled_grads], places)
+    up_parts = outer(feat, "up_outer", starts, m_list, m_others, [after(a, d_low) for _, a in scaled_grads], places)
     with jax.named_scope("feed"):
         feed_sent = []
 
@@ -738,8 +786,7 @@
             feed_sent.extend(lows)
             return ()
 
-        feed = reduce_row(shares, note, note)
-        feed_low = (middle + feed).astype(BF16)
+        feed_first, feed_last = reduce_row(shares, note, split=True)
     with jax.named_scope("middle_grad"):
         pieces = spread(d_low)
         d_own = put_rows(
@@ -754,7 +801,9 @@
     query_grad, key_grad, value_grad = attend_back(
         query, key, value, mixed, after(mixed_grad, *gate_middle), start_row, logs, cosine, front, back
     )
-    query_grad = after(query_grad, feed_low, down_blocks)
+    with jax.named_scope("feed"):
+        feed_low = (middle + feed_first.astype(F32) + after(feed_last, query_grad).astype(F32)).astype(BF16)
+    query_grad = after(query_grad, down_blocks, gate_total)
     heads_part, gain_dots = heads_outer(
         feat, x_own, x_other, d_own, d_other, query_grad, key_grad, value_grad, mixed, scale_one, qkv_full
     )
@@ -774,7 +823,7 @@
     dot_one = jnp.sum(first_unit_grad * unit_first, axis=1, keepdims=True)
     dot_one = dot_one + core_swap(dot_one)
     with jax.named_scope("input_grad"):
-        input_grad = to_home(
+        input_grad = to_home_swaps(
             (middle_grad + scale_first * (first_unit_grad - unit_first * (dot_one / width))).astype(BF16)
         )
 

time: 676 us -> 721 us (1.067)
  waiting for transfers between devices: 265 us -> 322 us
  Pallas kernels: 147 us -> 130 us
  other arithmetic: 62.6 us -> 71.1 us
    ppermute x12 -> x15, waiting for transfers between devices: 73.1 us -> 125 us  [row_swap(): return lax.ppermute(a, 'row', [(i, i ^ step) for i in range(rows)])]
    all_gather x3 -> x2, waiting for transfers between devices: 2.56 us -> 43.5 us  [the longest x1 43.5 us: local(): lax.all_gather(after(g_part, out_full, *m_list[1:3]), 'row', axis=0, tile...]
    all_to_all x3, waiting for transfers between devices: 51.8 us -> 21.4 us  [exchange(): lax.all_to_all(pieces, 'row', split_axis=0, concat_axis=0, tiled=True)]
    pallas_call x2 -> x4, Pallas kernels: 48.4 us -> 34.1 us  [the longest x2 19 us: units_back(): pl.pallas_call(functools.partial(units_back_kernel, feat, parts, count),...]
    ppermute x36 -> x39, waiting for transfers between devices: 89.5 us -> 102 us  [plane_swap(): return lax.ppermute(a, 'col', [(i, i ^ 2 * step) for i in range(cols)])]
    unnamed x153 -> x204, local copies, waits for them, and re-layouts: 21.9 us -> 32.8 us
    all_to_all x3 -> x2, waiting for transfers between devices: 10.8 us -> 0.02 us  [plane_exchange(): lax.all_to_all(a, 'col', split_axis=0, concat_axis=0, axis_index_groups=g...]
    all_to_all x3, waiting for transfers between devices: 31.3 us -> 22.4 us  [give_back(): return lax.all_to_all(total, 'row', split_axis=0, concat_axis=0, tiled=True)]
  transfers between devices with their start and end apart: 82 -> 84, of which waited for: 30 -> 35; matrix products, arithmetic and copies ran while one was open for 17% -> 15% of each run, Pallas kernels for 20% -> 14%
where the time goes in v6:
time: 721 us; the launch traced here: 710 us
  waiting for transfers between devices  322 us (45%)
  Pallas kernels  130 us (18%)
  starting transfers between devices  96.7 us (13%)
  local copies, waits for them, and re-layouts  73.6 us (10%)
  other arithmetic  71.1 us (10%)
  between operations  15.9 us (2%)
    ppermute x15, waiting for transfers between devices, row_swap(): return lax.ppermute(a, 'row', [(i, i ^ step) for i in range(rows)])  125 us
    ppermute x39, waiting for transfers between devices, plane_swap(): return lax.ppermute(a, 'col', [(i, i ^ 2 * step) for i in range(cols)])  102 us
    ppermute x39, starting transfers between devices, plane_swap(): return lax.ppermute(a, 'col', [(i, i ^ 2 * step) for i in range(cols)])  44 us
    all_gather x1, waiting for transfers between devices, local(): lax.all_gather(after(g_part, out_full, *m_list[1:3]), 'row', axis=0, tile...  43.5 us
    unnamed x204, local copies, waits for them, and re-layouts  32.8 us
    pallas_call x4, Pallas kernels, unfold(): pl.pallas_call(functools.partial(unfold_kernel, feat, len(lefts)), grid=(...  25 us
    all_to_all x3, waiting for transfers between devices, give_back(): return lax.all_to_all(total, 'row', split_axis=0, concat_axis=0, tiled=True)  22.4 us
    all_to_all x3, waiting for transfers between devices, exchange(): lax.all_to_all(pieces, 'row', split_axis=0, concat_axis=0, tiled=True)  21.4 us
  transfers between devices with their start and end apart: 84, of which 35 were waited for; matrix products, arithmetic and copies ran while one was open for 15% of the time, Pallas kernels for 14%

profile of v6, /device:TPU:0, one launch (start us, length us, event | category | flops | bytes accessed | tf_op | source)
XLA Modules:
  0.0 709.9 jit_solution(569189592203261889)
XLA Ops:
  7.2 3.0 collective-permute-start
  12.4 2.9 multiply_convert_fusion
  16.6 5.3 all-to-all-start
  26.7 8.4 %collective-permute-done.1 = bf16[1024,256]{1,0:T(8,128)(2,1)} collective-permute-done((bf16[1024,256]{1,0:T(8,128)(2,1)}, bf16[1024,256]{1,0:T(8,128)(2,1)}, u32[]{:S(2)}, u32[]{:S(2)}) %collective-permute-start.1) | collective-permute-done | bytes 524320 | tf_op jit(solution)/shard_map/inputs/ppermute | solution.py:537
  43.5 21.4 %all-to-all-done = bf16[4,512,256]{2,1,0:T(8,128)(2,1)S(1)} async-done(((bf16[4,512,256]{2,1,0:T(8,128)(2,1)}), bf16[4,512,256]{2,1,0:T(8,128)(2,1)S(1)}, u32[]{:S(2)}, u32[]{:S(2)}) %all-to-all-start) | async-done | bytes 1048608 | tf_op jit(solution)/shard_map/gate_row/all_to_all | solution.py:630
  66.4 2.9 broadcast_select_fusion.1
  72.1 8.7 %collective-permute-done.5.refs_2_ = bf16[512,768]{1,0:T(8,128)(2,1)} collective-permute-done((bf16[512,768]{1,0:T(8,128)(2,1)}, bf16[512,768]{1,0:T(8,128)(2,1)}, u32[]{:S(2)}, u32[]{:S(2)}) %collective-permute-start.5) | collective-permute-done | bytes 786464 | tf_op jit(solution)/shard_map/qkv_row/ppermute | solution.py:551
  93.3 4.3 all-to-all-start.1
  110.4 6.1 collective-permute-done.6.refs_3_
  118.8 3.5 all-to-all-start.2
  126.4 6.9 project.1
  136.6 10.0 %attend.1 = (bf16[1024,256]{1,0:T(8,128)(2,1)}, f32[2,2,1024]{2,1,0:T(2,128)}) custom-call(bf16[1024,256]{1,0:T(8,128)(2,1)} %copy-done.46, bf16[1024,256]{1,0:T(8,128)(2,1)} %copy-done.47, bf16[1024,256]{1,0:T(8,128)(2,1)} %copy-done.48, s32[1,1024]{1,0:T(1,128)} %bitcast.121), custom_call_target="tpu_custom_call" | custom-call | tf_op jit(solution)/shard_map/attend/pallas_call | solution.py:406
  149.8 5.1 mix.1
  157.4 5.0 all-to-all-start.3
  162.6 3.2 add_convert_fusion.1
  169.5 11.3 %collective-permute-done.12 = bf16[256,1024]{1,0:T(8,128)(2,1)S(1)} collective-permute-done((bf16[256,1024]{1,0:T(8,128)(2,1)S(1)}, bf16[256,1024]{1,0:T(8,128)(2,1)S(1)}, u32[]{:S(2)}, u32[]{:S(2)}) %collective-permute-start.12) | collective-permute-done | bytes 524320 | tf_op jit(solution)/shard_map/mix_plane/ppermute | solution.py:537
  180.8 11.7 %collective-permute-done.13 = bf16[256,1024]{1,0:T(8,128)(2,1)S(1)} collective-permute-done((bf16[256,1024]{1,0:T(8,128)(2,1)S(1)}, bf16[256,1024]{1,0:T(8,128)(2,1)S(1)}, u32[]{:S(2)}, u32[]{:S(2)}) %collective-permute-start.13) | collective-permute-done | bytes 524320 | tf_op jit(solution)/shard_map/mix_plane/ppermute | solution.py:537
  195.0 2.6 multiply_reduce_fusion.3
  201.8 19.9 %collective-permute-done.15.refs_1_ = bf16[256,1024]{1,0:T(8,128)(2,1)S(1)} collective-permute-done((bf16[256,1024]{1,0:T(8,128)(2,1)S(1)}, bf16[256,1024]{1,0:T(8,128)(2,1)S(1)}, u32[]{:S(2)}, u32[]{:S(2)}) %collective-permute-start.15) | collective-permute-done | bytes 524320 | tf_op jit(solution)/shard_map/middle_row/ppermute | solution.py:551
  226.2 43.5 %all-gather.5.cloned.1.call-done.refs_0_ = bf16[1024,1024]{1,0:T(8,128)(2,1)} async-done(((bf16[256,1024]{1,0:T(8,128)(2,1)}), bf16[1024,1024]{1,0:T(8,128)(2,1)}) %all-gather.5.cloned.1.call-update) | async-done | bytes 2097168 | tf_op jit(solution)/shard_map/grad_row/all_gather | solution.py:730
  275.6 11.1 %collective-permute-done.24.refs_1_.refs_3_ = bf16[256,1024]{1,0:T(8,128)(2,1)S(1)} collective-permute-done((bf16[256,1024]{1,0:T(8,128)(2,1)}, bf16[256,1024]{1,0:T(8,128)(2,1)S(1)}, u32[]{:S(2)}, u32[]{:S(2)}) %collective-permute-start.24) | collective-permute-done | bytes 524320 | tf_op jit(solution)/shard_map/middle_row/ppermute | solution.py:551
  287.2 20.5 %collective-permute-done.20 = bf16[1024,256]{1,0:T(8,128)(2,1)S(1)} collective-permute-done((bf16[1024,256]{1,0:T(8,128)(2,1)S(1)}, bf16[1024,256]{1,0:T(8,128)(2,1)S(1)}, u32[]{:S(2)}, u32[]{:S(2)}) %collective-permute-start.20) | collective-permute-done | bytes 524320 | tf_op jit(solution)/shard_map/up_plane/ppermute | solution.py:537
  310.8 8.2 %activate.3 = (bf16[512,1024]{1,0:T(8,128)(2,1)S(1)}, bf16[512,1024]{1,0:T(8,128)(2,1)S(1)}, bf16[512,1024]{1,0:T(8,128)(2,1)S(1)}, f32[512,1]{1,0:T(8,128)S(1)}) custom-call(bf16[256,1024]{1,0:T(8,128)(2,1)} %collective-permute-done.22.refs_0_.refs_2_, bf16[256,1024]{1,0:T(8,128)(2,1)S(1)} %collective-permute-done.24.refs_1_.refs_3_, ...), custom_call_target="tpu_custom_call" | custom-call | tf_op jit(solution)/shard_map/activate/pallas_call | solution.py:165
  325.0 9.6 %units_back.2 = (bf16[512,1024]{1,0:T(8,128)(2,1)S(1)}, bf16[512,1024]{1,0:T(8,128)(2,1)S(1)}, bf16[512,1024]{1,0:T(8,128)(2,1)S(1)}, bf16[512,1024]{1,0:T(8,128)(2,1)S(1)}) custom-call(s32[2]{0:T(128)S(1)} %pad_add_fusion.1.starts, bf16[1024,1024]{1,0:T(8,128)(2,1)} %all-gather.5.cloned.1.call-done.refs_0_, bf16[1024,1024]{1,0:T(8,128)(2,1)} %copy-done.18, ...), custom_call_target="tpu_custom_call" | custom-call | tf_op jit(solution)/shard_map/unit_grad/units_back/pallas_call | solution.py:230
  337.3 2.8 collective-permute-done.16.refs_2_.refs_4_
  340.9 6.9 activate.2
  351.5 6.2 down_outer.1
  359.1 9.3 %units_back.3 = (bf16[512,1024]{1,0:T(8,128)(2,1)S(1)}, bf16[512,1024]{1,0:T(8,128)(2,1)S(1)}, bf16[512,1024]{1,0:T(8,128)(2,1)S(1)}, bf16[512,1024]{1,0:T(8,128)(2,1)S(1)}) custom-call(s32[2]{0:T(128)S(1)} %pad_add_fusion.2.starts, bf16[1024,1024]{1,0:T(8,128)(2,1)} %all-gather.5.cloned.1.call-done.refs_0_, bf16[1024,1024]{1,0:T(8,128)(2,1)} %copy-done.18, ...), custom_call_target="tpu_custom_call" | custom-call | tf_op jit(solution)/shard_map/unit_grad/units_back/pallas_call | solution.py:230
  368.6 3.2 collective-permute-done.39
  380.4 6.1 feed.2
  386.7 6.0 feed.3
  392.8 8.7 %collective-permute-done.37 = bf16[256,1024]{1,0:T(8,128)(2,1)} collective-permute-done((bf16[256,1024]{1,0:T(8,128)(2,1)}, bf16[256,1024]{1,0:T(8,128)(2,1)}, u32[]{:S(2)}, u32[]{:S(2)}) %collective-permute-start.37) | collective-permute-done | bytes 524320 | tf_op jit(solution)/shard_map/unit_grad/ppermute | solution.py:551
  403.3 2.9 add_convert_fusion.5
  406.3 2.7 fusion.19
  408.9 3.1 collective-permute-start.49
  415.6 6.5 up_outer.1
  426.2 6.4 gate_outer.1
  433.0 2.9 collective-permute-done.48
  439.6 4.3 all-to-all-start.6
  446.3 5.1 collective-permute-done.52
  463.0 15.2 %collective-permute-done.54 = bf16[2048,256]{1,0:T(8,128)(2,1)} collective-permute-done((bf16[2048,256]{1,0:T(8,128)(2,1)}, bf16[2048,256]{1,0:T(8,128)(2,1)}, u32[]{:S(2)}, u32[]{:S(2)}) %collective-permute-start.54) | collective-permute-done | bytes 1048608 | tf_op jit(solution)/shard_map/gate_grad/ppermute | solution.py:537
  478.2 3.3 collective-permute-done.53
  481.5 3.2 multiply_reduce_fusion.1
  484.7 3.7 fold.1.do_ref
  489.2 11.2 %attend_back.1 = (bf16[1024,256]{1,0:T(8,128)(2,1)}, bf16[1024,256]{1,0:T(8,128)(2,1)}, bf16[1024,256]{1,0:T(8,128)(2,1)}) custom-call(bf16[1024,256]{1,0:T(8,128)(2,1)} %copy-done.46, bf16[1024,256]{1,0:T(8,128)(2,1)} %copy-done.47, bf16[1024,256]{1,0:T(8,128)(2,1)} %copy-done.48, bf16[1024,256]{1,0:T(8,128)(2,1)} %get-tuple-element.112.refs_0_.o_ref.mixed_ref, ...), custom_call_target="tpu_custom_call" | custom-call | tf_op jit(solution)/shard_map/attend_back/pallas_call | solution.py:475
  505.2 9.2 %heads_outer.1 = (bf16[2048,1024]{1,0:T(8,128)(2,1)}, f32[2048,1]{1,0:T(8,128)S(1)}) custom-call(bf16[1024,1024]{1,0:T(8,128)(2,1)S(1)} %copy-done.5, bf16[1024,1024]{1,0:T(8,128)(2,1)} %collective-permute-done.3.other_ref.x_other, bf16[1024,1024]{1,0:T(8,128)(2,1)S(1)} %copy-done.16, bf16[1024,1024]{1,0:T(8,128)(2,1)} %collective-permute-done.50.other_ref.d_other, ...), custom_call_target="tpu_custom_call" | custom-call | tf_op jit(solution)/shard_map/heads_outer/pallas_call | solution.py:304
  519.0 10.9 %collective-permute-done.63 = bf16[1024,256]{1,0:T(8,128)(2,1)S(1)} collective-permute-done((bf16[1024,256]{1,0:T(8,128)(2,1)S(1)}, bf16[1024,256]{1,0:T(8,128)(2,1)S(1)}, u32[]{:S(2)}, u32[]{:S(2)}) %collective-permute-start.63) | collective-permute-done | bytes 524320 | tf_op jit(solution)/shard_map/up_grad/ppermute | solution.py:537
  534.1 19.1 %collective-permute-done.45 = bf16[256,1024]{1,0:T(8,128)(2,1)S(1)} collective-permute-done((bf16[256,1024]{1,0:T(8,128)(2,1)S(1)}, bf16[256,1024]{1,0:T(8,128)(2,1)S(1)}, u32[]{:S(2)}, u32[]{:S(2)}) %collective-permute-start.45) | collective-permute-done | bytes 524320 | tf_op jit(solution)/shard_map/feed/ppermute | solution.py:551
  554.2 4.3 all-to-all-start.4
  558.5 7.7 %first_grad.1 = (bf16[1024,1024]{1,0:T(8,128)(2,1)}, bf16[1024,1024]{1,0:T(8,128)(2,1)}) custom-call(bf16[1024,256]{1,0:T(8,128)(2,1)} %get-tuple-element.187.dq_ref.refs_0_, bf16[1024,256]{1,0:T(8,128)(2,1)} %get-tuple-element.180.dk_ref.refs_1_, bf16[1024,256]{1,0:T(8,128)(2,1)} %get-tuple-element.181.dv_ref.refs_2_, bf16[2048,768]{1,0:T(8,128)(2,1)} %copy-done.74), custom_call_target="tpu_custom_call" | custom-call | tf_op jit(solution)/shard_map/first_plane/first_grad/pallas_call | solution.py:118
  566.2 37.7 %collective-permute-done.43 = bf16[256,1024]{1,0:T(8,128)(2,1)} collective-permute-done((bf16[256,1024]{1,0:T(8,128)(2,1)}, bf16[256,1024]{1,0:T(8,128)(2,1)}, u32[]{:S(2)}, u32[]{:S(2)}) %collective-permute-start.43) | collective-permute-done | bytes 524320 | tf_op jit(solution)/shard_map/feed/ppermute | solution.py:551
  603.9 9.8 %collective-permute-done.46 = bf16[256,1024]{1,0:T(8,128)(2,1)} collective-permute-done((bf16[256,1024]{1,0:T(8,128)(2,1)}, bf16[256,1024]{1,0:T(8,128)(2,1)}, u32[]{:S(2)}, u32[]{:S(2)}) %collective-permute-start.46) | collective-permute-done | bytes 524320 | tf_op jit(solution)/shard_map/feed/ppermute | solution.py:551
  615.3 3.4 multiply_reduce_fusion
  621.0 19.6 %all-to-all-done.4.part_ref = bf16[4,512,256]{2,1,0:T(8,128)(2,1)} async-done(((bf16[4,512,256]{2,1,0:T(8,128)(2,1)}), bf16[4,512,256]{2,1,0:T(8,128)(2,1)}, u32[]{:S(2)}, u32[]{:S(2)}) %all-to-all-start.4) | async-done | bytes 1048608 | tf_op jit(solution)/shard_map/gate_grad/all_to_all | solution.py:663
  641.8 2.6 collective-permute-done.68
  646.7 3.7 all-to-all-start.5
  650.5 3.2 add_convert_fusion
  667.4 2.7 finish.4
  670.2 2.8 finish.5
  673.8 4.4 all-to-all-start.7
  689.5 4.2 collective-permute-done.61
  693.8 2.7 all-to-all-done.7.part_ref
  696.6 2.8 finish.6
  699.4 2.8 finish.7
  (464 shorter events, 185.1 us)
Async XLA Ops:
  7.2 18.4 %collective-permute-start = (bf16[1024,256]{1,0:T(8,128)(2,1)}, bf16[1024,256]{1,0:T(8,128)(2,1)}, u32[]{:S(2)}, u32[]{:S(2)}) collective-permute-start(bf16[1024,256]{1,0:T(8,128)(2,1)} %param.13), channel_id=1, source_target_pairs={{0,2},{1,3},{2,0},{3,1},{4,6},{5,7},{6,4},{7,5},{8,10},{9,11},{10,... | collective-permute-start | bytes 1572872 | tf_op jit(solution)/shard_map/inputs/ppermute | solution.py:537
  10.2 24.9 %collective-permute-start.1 = (bf16[1024,256]{1,0:T(8,128)(2,1)}, bf16[1024,256]{1,0:T(8,128)(2,1)}, u32[]{:S(2)}, u32[]{:S(2)}) collective-permute-start(bf16[1024,256]{1,0:T(8,128)(2,1)} %param.13), channel_id=1, source_target_pairs={{0,4},{1,5},{2,6},{3,7},{4,0},{5,1},{6,2},{7,3},{8,12},{9,13},{10,... | collective-permute-start | bytes 1572872 | tf_op jit(solution)/shard_map/inputs/ppermute | solution.py:537
  11.7 24.5 %collective-permute-start.2 = (bf16[1024,256]{1,0:T(8,128)(2,1)}, bf16[1024,256]{1,0:T(8,128)(2,1)}, u32[]{:S(2)}, u32[]{:S(2)}) collective-permute-start(bf16[1024,256]{1,0:T(8,128)(2,1)} %param.13), channel_id=1, source_target_pairs={{0,6},{1,7},{2,4},{3,5},{4,2},{5,3},{6,0},{7,1},{8,14},{9,15},{10,... | collective-permute-start | bytes 1572872 | tf_op jit(solution)/shard_map/inputs/ppermute | solution.py:537
  16.6 48.2 %all-to-all-start = ((bf16[4,512,256]{2,1,0:T(8,128)(2,1)}), bf16[4,512,256]{2,1,0:T(8,128)(2,1)S(1)}, u32[]{:S(2)}, u32[]{:S(2)}) async-start(bf16[4,512,256]{2,1,0:T(8,128)(2,1)} %pad_maximum_fusion), calls=%async_computation | async-start | bytes 2097152 | tf_op jit(solution)/shard_map/gate_row/all_to_all | solution.py:630
  22.0 127.8 %all-gather.3.cloned.1.call-start = ((), (), s32[]{:S(2)}) async-start(), calls=%async_computation.9 | async-start | bytes 1310720 | tf_op jit(solution)/shard_map/out_row/all_gather | solution.py:687
  37.4 79.1 %collective-permute-start.3 = (bf16[1024,1024]{1,0:T(8,128)(2,1)S(1)}, bf16[1024,1024]{1,0:T(8,128)(2,1)}, u32[]{:S(2)}, u32[]{:S(2)}) collective-permute-start(bf16[1024,1024]{1,0:T(8,128)(2,1)S(1)} %constant_dynamic-update-slice_fusion.19.own_ref.x_own), channel_id=1, source_target_pairs={{0,1},{1,0},{2,3},{3,2},{4,5},{5,4},{6,7},{7,6},{8,9},{9,8},{10,11... | collective-permute-start | bytes 6291464 | tf_op jit(solution)/shard_map/inputs/ppermute | solution.py:534
  39.3 41.5 %collective-permute-start.5 = (bf16[512,768]{1,0:T(8,128)(2,1)}, bf16[512,768]{1,0:T(8,128)(2,1)}, u32[]{:S(2)}, u32[]{:S(2)}) collective-permute-start(bf16[512,768]{1,0:T(8,128)(2,1)} %maximum_maximum_fusion.refs_0_), channel_id=1, source_target_pairs={{0,16},{8,24},{16,0},{24,8},{1,17},{9,25},{17,1},{25,9},{2,18},{10... | collective-permute-start | bytes 2359304 | tf_op jit(solution)/shard_map/qkv_row/ppermute | solution.py:551
  41.9 39.1 %collective-permute-start.4 = (bf16[512,768]{1,0:T(8,128)(2,1)}, bf16[512,768]{1,0:T(8,128)(2,1)}, u32[]{:S(2)}, u32[]{:S(2)}) collective-permute-start(bf16[512,768]{1,0:T(8,128)(2,1)} %maximum_maximum_fusion.refs_0_), channel_id=1, source_target_pairs={{0,8},{8,0},{16,24},{24,16},{1,9},{9,1},{17,25},{25,17},{2,10},{10... | collective-permute-start | bytes 2359304 | tf_op jit(solution)/shard_map/qkv_row/ppermute | solution.py:551
  64.8 36.3 %collective-permute-start.8 = (bf16[2048,256]{1,0:T(8,128)(2,1)S(1)}, bf16[2048,256]{1,0:T(8,128)(2,1)}, u32[]{:S(2)}, u32[]{:S(2)}) collective-permute-start(bf16[2048,256]{1,0:T(8,128)(2,1)S(1)} %bitcast.91), channel_id=1, source_target_pairs={{0,4},{1,5},{2,6},{3,7},{4,0},{5,1},{6,2},{7,3},{8,12},{9,13},{10,... | collective-permute-start | bytes 3145736 | tf_op jit(solution)/shard_map/gate_plane/ppermute | solution.py:537
  69.3 36.8 %collective-permute-start.7 = (bf16[2048,256]{1,0:T(8,128)(2,1)S(1)}, bf16[2048,256]{1,0:T(8,128)(2,1)}, u32[]{:S(2)}, u32[]{:S(2)}) collective-permute-start(bf16[2048,256]{1,0:T(8,128)(2,1)S(1)} %bitcast.92), channel_id=1, source_target_pairs={{0,2},{1,3},{2,0},{3,1},{4,6},{5,7},{6,4},{7,5},{8,10},{9,11},{10,... | collective-permute-start | bytes 3145736 | tf_op jit(solution)/shard_map/gate_plane/ppermute | solution.py:537
  81.0 35.5 %collective-permute-start.6 = (bf16[512,768]{1,0:T(8,128)(2,1)}, bf16[512,768]{1,0:T(8,128)(2,1)}, u32[]{:S(2)}, u32[]{:S(2)}) collective-permute-start(bf16[512,768]{1,0:T(8,128)(2,1)} %collective-permute-done.5.refs_2_), channel_id=1, source_target_pairs={{0,8},{8,0},{16,24},{24,16},{1,9},{9,1},{17,25},{25,17},{2,10},{10... | collective-permute-start | bytes 2359304 | tf_op jit(solution)/shard_map/qkv_row/ppermute | solution.py:551
  103.0 43.6 %collective-permute-start.9 = (bf16[1024,256]{1,0:T(8,128)(2,1)}, bf16[1024,256]{1,0:T(8,128)(2,1)}, u32[]{:S(2)}, u32[]{:S(2)}) collective-permute-start(bf16[1024,256]{1,0:T(8,128)(2,1)} %slice.306), channel_id=1, source_target_pairs={{0,2},{1,3},{2,0},{3,1},{4,6},{5,7},{6,4},{7,5},{8,10},{9,11},{10,... | collective-permute-start | bytes 1572872 | tf_op jit(solution)/shard_map/gate_plane/ppermute | solution.py:537
  108.0 39.6 %collective-permute-start.10 = (bf16[1024,256]{1,0:T(8,128)(2,1)}, bf16[1024,256]{1,0:T(8,128)(2,1)}, u32[]{:S(2)}, u32[]{:S(2)}) collective-permute-start(bf16[1024,256]{1,0:T(8,128)(2,1)} %slice.307), channel_id=1, source_target_pairs={{0,4},{1,5},{2,6},{3,7},{4,0},{5,1},{6,2},{7,3},{8,12},{9,13},{10,... | collective-permute-start | bytes 1572872 | tf_op jit(solution)/shard_map/gate_plane/ppermute | solution.py:537
  118.8 37.3 %all-to-all-start.2 = ((bf16[4,512,256]{2,1,0:T(8,128)(2,1)}), bf16[4,512,256]{2,1,0:T(8,128)(2,1)S(1)}, u32[]{:S(2)}, u32[]{:S(2)}) async-start(bf16[4,512,256]{2,1,0:T(8,128)(2,1)} %pad_maximum_fusion.2), calls=%async_computation.2 | async-start | bytes 2097152 | tf_op jit(solution)/shard_map/up_row/all_to_all | solution.py:630
  157.4 37.6 %all-to-all-start.3 = ((bf16[4,512,256]{2,1,0:T(8,128)(2,1)}), bf16[4,512,256]{2,1,0:T(8,128)(2,1)S(1)}, u32[]{:S(2)}, u32[]{:S(2)}) async-start(bf16[4,512,256]{2,1,0:T(8,128)(2,1)} %pad_maximum_fusion.4), calls=%async_computation.3 | async-start | bytes 2097152 | tf_op jit(solution)/shard_map/down_row/all_to_all | solution.py:630
  162.4 107.4 %all-gather.5.cloned.1.call-start = ((), (), s32[]{:S(2)}) async-start(), calls=%async_computation.10 | async-start | bytes 2621440 | tf_op jit(solution)/shard_map/grad_row/all_gather | solution.py:730
  166.0 14.8 %collective-permute-start.12 = (bf16[256,1024]{1,0:T(8,128)(2,1)S(1)}, bf16[256,1024]{1,0:T(8,128)(2,1)S(1)}, u32[]{:S(2)}, u32[]{:S(2)}) collective-permute-start(bf16[256,1024]{1,0:T(8,128)(2,1)S(1)} %get-tuple-element.212), channel_id=1, source_target_pairs={{0,2},{1,3},{2,0},{3,1},{4,6},{5,7},{6,4},{7,5},{8,10},{9,11},{10,... | collective-permute-start | bytes 1572872 | tf_op jit(solution)/shard_map/mix_plane/ppermute | solution.py:537
  167.5 25.0 %collective-permute-start.13 = (bf16[256,1024]{1,0:T(8,128)(2,1)S(1)}, bf16[256,1024]{1,0:T(8,128)(2,1)S(1)}, u32[]{:S(2)}, u32[]{:S(2)}) collective-permute-start(bf16[256,1024]{1,0:T(8,128)(2,1)S(1)} %get-tuple-element.214), channel_id=1, source_target_pairs={{0,4},{1,5},{2,6},{3,7},{4,0},{5,1},{6,2},{7,3},{8,12},{9,13},{10,... | collective-permute-start | bytes 1572872 | tf_op jit(solution)/shard_map/mix_plane/ppermute | solution.py:537
  169.0 23.5 %collective-permute-start.14 = (bf16[256,1024]{1,0:T(8,128)(2,1)S(1)}, bf16[256,1024]{1,0:T(8,128)(2,1)S(1)}, u32[]{:S(2)}, u32[]{:S(2)}) collective-permute-start(bf16[256,1024]{1,0:T(8,128)(2,1)S(1)} %get-tuple-element.213), channel_id=1, source_target_pairs={{0,6},{1,7},{2,4},{3,5},{4,2},{5,3},{6,0},{7,1},{8,14},{9,15},{10,... | collective-permute-start | bytes 1572872 | tf_op jit(solution)/shard_map/mix_plane/ppermute | solution.py:537
  197.6 24.0 %collective-permute-start.15 = (bf16[256,1024]{1,0:T(8,128)(2,1)S(1)}, bf16[256,1024]{1,0:T(8,128)(2,1)S(1)}, u32[]{:S(2)}, u32[]{:S(2)}) collective-permute-start(bf16[256,1024]{1,0:T(8,128)(2,1)S(1)} %get-tuple-element.222.refs_0_), channel_id=1, source_target_pairs={{0,8},{8,0},{16,24},{24,16},{1,9},{9,1},{17,25},{25,17},{2,10},{10... | collective-permute-start | bytes 1572872 | tf_op jit(solution)/shard_map/middle_row/ppermute | solution.py:551
  199.4 24.7 %collective-permute-start.22 = (bf16[256,1024]{1,0:T(8,128)(2,1)S(1)}, bf16[256,1024]{1,0:T(8,128)(2,1)}, u32[]{:S(2)}, u32[]{:S(2)}) collective-permute-start(bf16[256,1024]{1,0:T(8,128)(2,1)S(1)} %get-tuple-element.222.refs_0_), channel_id=1, source_target_pairs={{0,16},{8,24},{16,0},{24,8},{1,17},{9,25},{17,1},{25,9},{2,18},{10... | collective-permute-start | bytes 1572872 | tf_op jit(solution)/shard_map/middle_row/ppermute | solution.py:551
  224.1 45.6 %collective-permute-start.19 = (bf16[2048,256]{1,0:T(8,128)(2,1)S(1)}, bf16[2048,256]{1,0:T(8,128)(2,1)}, u32[]{:S(2)}, u32[]{:S(2)}) collective-permute-start(bf16[2048,256]{1,0:T(8,128)(2,1)S(1)} %bitcast.97), channel_id=1, source_target_pairs={{0,4},{1,5},{2,6},{3,7},{4,0},{5,1},{6,2},{7,3},{8,12},{9,13},{10,... | collective-permute-start | bytes 3145736 | tf_op jit(solution)/shard_map/up_plane/ppermute | solution.py:537
  225.3 44.5 %collective-permute-start.18 = (bf16[2048,256]{1,0:T(8,128)(2,1)S(1)}, bf16[2048,256]{1,0:T(8,128)(2,1)}, u32[]{:S(2)}, u32[]{:S(2)}) collective-permute-start(bf16[2048,256]{1,0:T(8,128)(2,1)S(1)} %bitcast.98), channel_id=1, source_target_pairs={{0,2},{1,3},{2,0},{3,1},{4,6},{5,7},{6,4},{7,5},{8,10},{9,11},{10,... | collective-permute-start | bytes 3145736 | tf_op jit(solution)/shard_map/up_plane/ppermute | solution.py:537
  269.7 53.9 %collective-permute-start.23 = (bf16[1024,1024]{1,0:T(8,128)(2,1)}, bf16[1024,1024]{1,0:T(8,128)(2,1)S(1)}, u32[]{:S(2)}, u32[]{:S(2)}) collective-permute-start(bf16[1024,1024]{1,0:T(8,128)(2,1)} %all-gather.5.cloned.1.call-done.refs_0_), channel_id=1, source_target_pairs={{0,1},{1,0},{2,3},{3,2},{4,5},{5,4},{6,7},{7,6},{8,9},{9,8},{10,11... | collective-permute-start | bytes 6291464 | tf_op jit(solution)/shard_map/grad_row/ppermute | solution.py:534
  269.8 38.0 %collective-permute-start.28 = (bf16[2048,256]{1,0:T(8,128)(2,1)S(1)}, bf16[2048,256]{1,0:T(8,128)(2,1)S(1)}, u32[]{:S(2)}, u32[]{:S(2)}) collective-permute-start(bf16[2048,256]{1,0:T(8,128)(2,1)S(1)} %bitcast.104), channel_id=1, source_target_pairs={{0,4},{1,5},{2,6},{3,7},{4,0},{5,1},{6,2},{7,3},{8,12},{9,13},{10,... | collective-permute-start | bytes 3145736 | tf_op jit(solution)/shard_map/down_plane/ppermute | solution.py:537
  271.3 37.0 %collective-permute-start.27 = (bf16[2048,256]{1,0:T(8,128)(2,1)S(1)}, bf16[2048,256]{1,0:T(8,128)(2,1)S(1)}, u32[]{:S(2)}, u32[]{:S(2)}) collective-permute-start(bf16[2048,256]{1,0:T(8,128)(2,1)S(1)} %bitcast.105), channel_id=1, source_target_pairs={{0,2},{1,3},{2,0},{3,1},{4,6},{5,7},{6,4},{7,5},{8,10},{9,11},{10,... | collective-permute-start | bytes 3145736 | tf_op jit(solution)/shard_map/down_plane/ppermute | solution.py:537
  272.7 13.9 %collective-permute-start.24 = (bf16[256,1024]{1,0:T(8,128)(2,1)}, bf16[256,1024]{1,0:T(8,128)(2,1)S(1)}, u32[]{:S(2)}, u32[]{:S(2)}) collective-permute-start(bf16[256,1024]{1,0:T(8,128)(2,1)} %collective-permute-done.22.refs_0_.refs_2_), channel_id=1, source_target_pairs={{0,8},{8,0},{16,24},{24,16},{1,9},{9,1},{17,25},{25,17},{2,10},{10... | collective-permute-start | bytes 1572872 | tf_op jit(solution)/shard_map/middle_row/ppermute | solution.py:551
  273.8 33.9 %collective-permute-start.20 = (bf16[1024,256]{1,0:T(8,128)(2,1)S(1)}, bf16[1024,256]{1,0:T(8,128)(2,1)S(1)}, u32[]{:S(2)}, u32[]{:S(2)}) collective-permute-start(bf16[1024,256]{1,0:T(8,128)(2,1)S(1)} %slice.314), channel_id=1, source_target_pairs={{0,2},{1,3},{2,0},{3,1},{4,6},{5,7},{6,4},{7,5},{8,10},{9,11},{10,... | collective-permute-start | bytes 1572872 | tf_op jit(solution)/shard_map/up_plane/ppermute | solution.py:537
  286.7 23.2 %collective-permute-start.21 = (bf16[1024,256]{1,0:T(8,128)(2,1)S(1)}, bf16[1024,256]{1,0:T(8,128)(2,1)S(1)}, u32[]{:S(2)}, u32[]{:S(2)}) collective-permute-start(bf16[1024,256]{1,0:T(8,128)(2,1)S(1)} %slice.315), channel_id=1, source_target_pairs={{0,4},{1,5},{2,6},{3,7},{4,0},{5,1},{6,2},{7,3},{8,12},{9,13},{10,... | collective-permute-start | bytes 1572872 | tf_op jit(solution)/shard_map/up_plane/ppermute | solution.py:537
  308.3 14.0 %collective-permute-start.29 = (bf16[1024,256]{1,0:T(8,128)(2,1)S(1)}, bf16[1024,256]{1,0:T(8,128)(2,1)S(1)}, u32[]{:S(2)}, u32[]{:S(2)}) collective-permute-start(bf16[1024,256]{1,0:T(8,128)(2,1)S(1)} %slice.316), channel_id=1, source_target_pairs={{0,2},{1,3},{2,0},{3,1},{4,6},{5,7},{6,4},{7,5},{8,10},{9,11},{10,... | collective-permute-start | bytes 1572872 | tf_op jit(solution)/shard_map/down_plane/ppermute | solution.py:537
  357.7 14.0 %collective-permute-start.39 = (bf16[1024,256]{1,0:T(8,128)(2,1)S(1)}, bf16[1024,256]{1,0:T(8,128)(2,1)S(1)}, u32[]{:S(2)}, u32[]{:S(2)}) collective-permute-start(bf16[1024,256]{1,0:T(8,128)(2,1)S(1)} %get-tuple-element.219), channel_id=1, source_target_pairs={{0,4},{1,5},{2,6},{3,7},{4,0},{5,1},{6,2},{7,3},{8,12},{9,13},{10,... | collective-permute-start | bytes 1572872 | tf_op jit(solution)/shard_map/down_grad/ppermute | solution.py:537
  358.4 15.2 %collective-permute-start.41 = (bf16[1024,256]{1,0:T(8,128)(2,1)S(1)}, bf16[1024,256]{1,0:T(8,128)(2,1)S(1)}, u32[]{:S(2)}, u32[]{:S(2)}) collective-permute-start(bf16[1024,256]{1,0:T(8,128)(2,1)S(1)} %get-tuple-element.220), channel_id=1, source_target_pairs={{0,2},{1,3},{2,0},{3,1},{4,6},{5,7},{6,4},{7,5},{8,10},{9,11},{10,... | collective-permute-start | bytes 1572872 | tf_op jit(solution)/shard_map/down_grad/ppermute | solution.py:537
  359.0 16.3 %collective-permute-start.32 = (bf16[256,1024]{1,0:T(8,128)(2,1)S(1)}, bf16[256,1024]{1,0:T(8,128)(2,1)S(1)}, u32[]{:S(2)}, u32[]{:S(2)}) collective-permute-start(bf16[256,1024]{1,0:T(8,128)(2,1)S(1)} %slice.413), channel_id=1, source_target_pairs={{0,8},{8,0},{16,24},{24,16},{1,9},{9,1},{17,25},{25,17},{2,10},{10... | collective-permute-start | bytes 1572872 | tf_op jit(solution)/shard_map/unit_grad/ppermute | solution.py:551
  373.0 30.3 %collective-permute-start.40 = (bf16[2048,256]{1,0:T(8,128)(2,1)}, bf16[2048,256]{1,0:T(8,128)(2,1)}, u32[]{:S(2)}, u32[]{:S(2)}) collective-permute-start(bf16[2048,256]{1,0:T(8,128)(2,1)} %pad_maximum_fusion.5), channel_id=1, source_target_pairs={{0,2},{1,3},{2,0},{3,1},{4,6},{5,7},{6,4},{7,5},{8,10},{9,11},{10,... | collective-permute-start | bytes 3145736 | tf_op jit(solution)/shard_map/down_grad/ppermute | solution.py:537
  374.7 28.5 %collective-permute-start.42 = (bf16[2048,256]{1,0:T(8,128)(2,1)}, bf16[2048,256]{1,0:T(8,128)(2,1)}, u32[]{:S(2)}, u32[]{:S(2)}) collective-permute-start(bf16[2048,256]{1,0:T(8,128)(2,1)} %pad_maximum_fusion.6), channel_id=1, source_target_pairs={{0,4},{1,5},{2,6},{3,7},{4,0},{5,1},{6,2},{7,3},{8,12},{9,13},{10,... | collective-permute-start | bytes 3145736 | tf_op jit(solution)/shard_map/down_grad/ppermute | solution.py:537
  376.2 25.2 %collective-permute-start.37 = (bf16[256,1024]{1,0:T(8,128)(2,1)}, bf16[256,1024]{1,0:T(8,128)(2,1)}, u32[]{:S(2)}, u32[]{:S(2)}) collective-permute-start(bf16[256,1024]{1,0:T(8,128)(2,1)} %fusion.8), channel_id=1, source_target_pairs={{0,16},{8,24},{16,0},{24,8},{1,17},{9,25},{17,1},{25,9},{2,18},{10... | collective-permute-start | bytes 1572872 | tf_op jit(solution)/shard_map/unit_grad/ppermute | solution.py:551
  378.6 23.1 %collective-permute-start.36 = (bf16[256,1024]{1,0:T(8,128)(2,1)}, bf16[256,1024]{1,0:T(8,128)(2,1)}, u32[]{:S(2)}, u32[]{:S(2)}) collective-permute-start(bf16[256,1024]{1,0:T(8,128)(2,1)} %slice.412), channel_id=1, source_target_pairs={{0,8},{8,0},{16,24},{24,16},{1,9},{9,1},{17,25},{25,17},{2,10},{10... | collective-permute-start | bytes 1572872 | tf_op jit(solution)/shard_map/unit_grad/ppermute | solution.py:551
  386.5 26.2 %collective-permute-start.33 = (bf16[512,1024]{1,0:T(8,128)(2,1)}, bf16[512,1024]{1,0:T(8,128)(2,1)}, u32[]{:S(2)}, u32[]{:S(2)}) collective-permute-start(bf16[512,1024]{1,0:T(8,128)(2,1)} %get-tuple-element.132), channel_id=1, source_target_pairs={{0,1},{1,0},{2,3},{3,2},{4,5},{5,4},{6,7},{7,6},{8,9},{9,8},{10,11... | collective-permute-start | bytes 3145736 | tf_op jit(solution)/shard_map/feed/ppermute | solution.py:534
  408.9 24.1 %collective-permute-start.49 = (bf16[256,1024]{1,0:T(8,128)(2,1)S(1)}, bf16[256,1024]{1,0:T(8,128)(2,1)S(1)}, u32[]{:S(2)}, u32[]{:S(2)}) collective-permute-start(bf16[256,1024]{1,0:T(8,128)(2,1)S(1)} %get-tuple-element.149), channel_id=1, source_target_pairs={{0,6},{1,7},{2,4},{3,5},{4,2},{5,3},{6,0},{7,1},{8,14},{9,15},{10,... | collective-permute-start | bytes 1572872 | tf_op jit(solution)/shard_map/middle_grad/ppermute | solution.py:537
  412.1 23.8 %collective-permute-start.48 = (bf16[256,1024]{1,0:T(8,128)(2,1)S(1)}, bf16[256,1024]{1,0:T(8,128)(2,1)S(1)}, u32[]{:S(2)}, u32[]{:S(2)}) collective-permute-start(bf16[256,1024]{1,0:T(8,128)(2,1)S(1)} %get-tuple-element.149), channel_id=1, source_target_pairs={{0,4},{1,5},{2,6},{3,7},{4,0},{5,1},{6,2},{7,3},{8,12},{9,13},{10,... | collective-permute-start | bytes 1572872 | tf_op jit(solution)/shard_map/middle_grad/ppermute | solution.py:537
  412.3 23.6 %collective-permute-start.47 = (bf16[256,1024]{1,0:T(8,128)(2,1)S(1)}, bf16[256,1024]{1,0:T(8,128)(2,1)S(1)}, u32[]{:S(2)}, u32[]{:S(2)}) collective-permute-start(bf16[256,1024]{1,0:T(8,128)(2,1)S(1)} %get-tuple-element.149), channel_id=1, source_target_pairs={{0,2},{1,3},{2,0},{3,1},{4,6},{5,7},{6,4},{7,5},{8,10},{9,11},{10,... | collective-permute-start | bytes 1572872 | tf_op jit(solution)/shard_map/middle_grad/ppermute | solution.py:537
  437.2 14.2 %collective-permute-start.52 = (bf16[1024,256]{1,0:T(8,128)(2,1)}, bf16[1024,256]{1,0:T(8,128)(2,1)}, u32[]{:S(2)}, u32[]{:S(2)}) collective-permute-start(bf16[1024,256]{1,0:T(8,128)(2,1)} %get-tuple-element.217), channel_id=1, source_target_pairs={{0,2},{1,3},{2,0},{3,1},{4,6},{5,7},{6,4},{7,5},{8,10},{9,11},{10,... | collective-permute-start | bytes 1572872 | tf_op jit(solution)/shard_map/gate_grad/ppermute | solution.py:537
  439.0 16.0 %collective-permute-start.51 = (bf16[1024,256]{1,0:T(8,128)(2,1)}, bf16[1024,256]{1,0:T(8,128)(2,1)}, u32[]{:S(2)}, u32[]{:S(2)}) collective-permute-start(bf16[1024,256]{1,0:T(8,128)(2,1)} %get-tuple-element.218), channel_id=1, source_target_pairs={{0,4},{1,5},{2,6},{3,7},{4,0},{5,1},{6,2},{7,3},{8,12},{9,13},{10,... | collective-permute-start | bytes 1572872 | tf_op jit(solution)/shard_map/gate_grad/ppermute | solution.py:537
  439.6 60.8 %all-to-all-start.6 = ((bf16[4,512,256]{2,1,0:T(8,128)(2,1)}), bf16[4,512,256]{2,1,0:T(8,128)(2,1)}, u32[]{:S(2)}, u32[]{:S(2)}) async-start(bf16[4,512,256]{2,1,0:T(8,128)(2,1)} %bitcast.113), calls=%async_computation.6 | async-start | bytes 2097152 | tf_op jit(solution)/shard_map/down_grad/all_to_all | solution.py:663
  443.9 255.5 %reduce-scatter.2.cloned.1.call-start = ((), (), s32[]{:S(2)}) async-start(), calls=%async_computation.11 | async-start | bytes 5242880 | tf_op jit(solution)/shard_map/heads_grad/reduce_scatter | solution.py:811
  444.0 40.8 %collective-permute-start.50 = (bf16[1024,1024]{1,0:T(8,128)(2,1)S(1)}, bf16[1024,1024]{1,0:T(8,128)(2,1)}, u32[]{:S(2)}, u32[]{:S(2)}) collective-permute-start(bf16[1024,1024]{1,0:T(8,128)(2,1)S(1)} %constant_dynamic-update-slice_fusion.15.own_ref.d_own), channel_id=1, source_target_pairs={{0,1},{1,0},{2,3},{3,2},{4,5},{5,4},{6,7},{7,6},{8,9},{9,8},{10,11... | collective-permute-start | bytes 6291464 | tf_op jit(solution)/shard_map/middle_grad/ppermute | solution.py:534
  453.6 24.6 %collective-permute-start.54 = (bf16[2048,256]{1,0:T(8,128)(2,1)}, bf16[2048,256]{1,0:T(8,128)(2,1)}, u32[]{:S(2)}, u32[]{:S(2)}) collective-permute-start(bf16[2048,256]{1,0:T(8,128)(2,1)} %pad_maximum_fusion.8), channel_id=1, source_target_pairs={{0,4},{1,5},{2,6},{3,7},{4,0},{5,1},{6,2},{7,3},{8,12},{9,13},{10,... | collective-permute-start | bytes 3145736 | tf_op jit(solution)/shard_map/gate_grad/ppermute | solution.py:537
  457.2 24.3 %collective-permute-start.53 = (bf16[2048,256]{1,0:T(8,128)(2,1)}, bf16[2048,256]{1,0:T(8,128)(2,1)}, u32[]{:S(2)}, u32[]{:S(2)}) collective-permute-start(bf16[2048,256]{1,0:T(8,128)(2,1)} %pad_maximum_fusion.7), channel_id=1, source_target_pairs={{0,2},{1,3},{2,0},{3,1},{4,6},{5,7},{6,4},{7,5},{8,10},{9,11},{10,... | collective-permute-start | bytes 3145736 | tf_op jit(solution)/shard_map/gate_grad/ppermute | solution.py:537
  517.4 14.1 %collective-permute-start.65 = (bf16[1024,256]{1,0:T(8,128)(2,1)S(1)}, bf16[1024,256]{1,0:T(8,128)(2,1)S(1)}, u32[]{:S(2)}, u32[]{:S(2)}) collective-permute-start(bf16[1024,256]{1,0:T(8,128)(2,1)S(1)} %get-tuple-element.216), channel_id=1, source_target_pairs={{0,2},{1,3},{2,0},{3,1},{4,6},{5,7},{6,4},{7,5},{8,10},{9,11},{10,... | collective-permute-start | bytes 1572872 | tf_op jit(solution)/shard_map/up_grad/ppermute | solution.py:537
  518.9 34.3 %collective-permute-start.45 = (bf16[256,1024]{1,0:T(8,128)(2,1)S(1)}, bf16[256,1024]{1,0:T(8,128)(2,1)S(1)}, u32[]{:S(2)}, u32[]{:S(2)}) collective-permute-start(bf16[256,1024]{1,0:T(8,128)(2,1)S(1)} %slice.273), channel_id=1, source_target_pairs={{0,8},{8,0},{16,24},{24,16},{1,9},{9,1},{17,25},{25,17},{2,10},{10... | collective-permute-start | bytes 1572872 | tf_op jit(solution)/shard_map/feed/ppermute | solution.py:551
  531.2 84.1 %collective-permute-start.64 = (bf16[2048,256]{1,0:T(8,128)(2,1)}, bf16[2048,256]{1,0:T(8,128)(2,1)}, u32[]{:S(2)}, u32[]{:S(2)}) collective-permute-start(bf16[2048,256]{1,0:T(8,128)(2,1)} %pad_maximum_fusion.9), channel_id=1, source_target_pairs={{0,2},{1,3},{2,0},{3,1},{4,6},{5,7},{6,4},{7,5},{8,10},{9,11},{10,... | collective-permute-start | bytes 3145736 | tf_op jit(solution)/shard_map/up_grad/ppermute | solution.py:537
  532.7 82.7 %collective-permute-start.66 = (bf16[2048,256]{1,0:T(8,128)(2,1)}, bf16[2048,256]{1,0:T(8,128)(2,1)}, u32[]{:S(2)}, u32[]{:S(2)}) collective-permute-start(bf16[2048,256]{1,0:T(8,128)(2,1)} %pad_maximum_fusion.10), channel_id=1, source_target_pairs={{0,4},{1,5},{2,6},{3,7},{4,0},{5,1},{6,2},{7,3},{8,12},{9,13},{10,... | collective-permute-start | bytes 3145736 | tf_op jit(solution)/shard_map/up_grad/ppermute | solution.py:537
  534.0 69.8 %collective-permute-start.43 = (bf16[256,1024]{1,0:T(8,128)(2,1)}, bf16[256,1024]{1,0:T(8,128)(2,1)}, u32[]{:S(2)}, u32[]{:S(2)}) collective-permute-start(bf16[256,1024]{1,0:T(8,128)(2,1)} %slice.271), channel_id=1, source_target_pairs={{0,8},{8,0},{16,24},{24,16},{1,9},{9,1},{17,25},{25,17},{2,10},{10... | collective-permute-start | bytes 1572872 | tf_op jit(solution)/shard_map/feed/ppermute | solution.py:551
  554.2 59.6 %collective-permute-start.46 = (bf16[256,1024]{1,0:T(8,128)(2,1)}, bf16[256,1024]{1,0:T(8,128)(2,1)}, u32[]{:S(2)}, u32[]{:S(2)}) collective-permute-start(bf16[256,1024]{1,0:T(8,128)(2,1)} %add_convert_fusion.12), channel_id=1, source_target_pairs={{0,16},{8,24},{16,0},{24,8},{1,17},{9,25},{17,1},{25,9},{2,18},{10... | collective-permute-start | bytes 1572872 | tf_op jit(solution)/shard_map/feed/ppermute | solution.py:551
  554.2 86.5 %all-to-all-start.4 = ((bf16[4,512,256]{2,1,0:T(8,128)(2,1)}), bf16[4,512,256]{2,1,0:T(8,128)(2,1)}, u32[]{:S(2)}, u32[]{:S(2)}) async-start(bf16[4,512,256]{2,1,0:T(8,128)(2,1)} %bitcast.32), calls=%async_computation.4 | async-start | bytes 2097152 | tf_op jit(solution)/shard_map/gate_grad/all_to_all | solution.py:663
  566.2 84.3 %collective-permute-start.55 = (bf16[1024,1024]{1,0:T(8,128)(2,1)}, bf16[1024,1024]{1,0:T(8,128)(2,1)}, u32[]{:S(2)}, u32[]{:S(2)}) collective-permute-start(bf16[1024,1024]{1,0:T(8,128)(2,1)} %get-tuple-element.189), channel_id=1, source_target_pairs={{0,1},{1,0},{2,3},{3,2},{4,5},{5,4},{6,7},{7,6},{8,9},{9,8},{10,11... | collective-permute-start | bytes 6291464 | tf_op jit(solution)/shard_map/first_plane/ppermute | solution.py:534
  618.9 21.7 %collective-permute-start.67 = (f32[2,4,2,256]{3,2,1,0:T(2,128)S(1)}, f32[2,4,2,256]{3,2,1,0:T(2,128)S(1)}, u32[]{:S(2)}, u32[]{:S(2)}) collective-permute-start(f32[2,4,2,256]{3,2,1,0:T(2,128)S(1)} %bitcast.118), channel_id=1, source_target_pairs={{0,1},{1,0},{2,3},{3,2},{4,5},{5,4},{6,7},{7,6},{8,9},{9,8},{10,11... | collective-permute-start | bytes 49160 | tf_op jit(solution)/shard_map/gains/ppermute | solution.py:617
  646.7 26.2 %all-to-all-start.5 = ((bf16[4,256,256]{2,1,0:T(8,128)(2,1)}), bf16[4,256,256]{2,1,0:T(8,128)(2,1)S(1)}, u32[]{:S(2)}, u32[]{:S(2)}) async-start(bf16[4,256,256]{2,1,0:T(8,128)(2,1)} %pad_maximum_fusion.12), calls=%async_computation.5 | async-start | bytes 1048576 | tf_op jit(solution)/shard_map/block_out/all_to_all | solution.py:599
  656.2 22.0 %collective-permute-start.56 = (bf16[256,1024]{1,0:T(8,128)(2,1)}, bf16[256,1024]{1,0:T(8,128)(2,1)}, u32[]{:S(2)}, u32[]{:S(2)}) collective-permute-start(bf16[256,1024]{1,0:T(8,128)(2,1)} %get-tuple-element.209), channel_id=1, source_target_pairs={{0,2},{1,3},{2,0},{3,1},{4,6},{5,7},{6,4},{7,5},{8,10},{9,11},{10,... | collective-permute-start | bytes 1572872 | tf_op jit(solution)/shard_map/first_plane/ppermute | solution.py:537
  658.2 20.0 %collective-permute-start.57 = (bf16[256,1024]{1,0:T(8,128)(2,1)}, bf16[256,1024]{1,0:T(8,128)(2,1)}, u32[]{:S(2)}, u32[]{:S(2)}) collective-permute-start(bf16[256,1024]{1,0:T(8,128)(2,1)} %get-tuple-element.211), channel_id=1, source_target_pairs={{0,4},{1,5},{2,6},{3,7},{4,0},{5,1},{6,2},{7,3},{8,12},{9,13},{10,... | collective-permute-start | bytes 1572872 | tf_op jit(solution)/shard_map/first_plane/ppermute | solution.py:537
  659.7 18.5 %collective-permute-start.58 = (bf16[256,1024]{1,0:T(8,128)(2,1)}, bf16[256,1024]{1,0:T(8,128)(2,1)}, u32[]{:S(2)}, u32[]{:S(2)}) collective-permute-start(bf16[256,1024]{1,0:T(8,128)(2,1)} %get-tuple-element.210), channel_id=1, source_target_pairs={{0,6},{1,7},{2,4},{3,5},{4,2},{5,3},{6,0},{7,1},{8,14},{9,15},{10,... | collective-permute-start | bytes 1572872 | tf_op jit(solution)/shard_map/first_plane/ppermute | solution.py:537
  659.8 18.3 %collective-permute-start.71 = (f32[2,512]{1,0:T(2,128)S(1)}, f32[2,512]{1,0:T(2,128)S(1)}, u32[]{:S(2)}, u32[]{:S(2)}) collective-permute-start(f32[2,512]{1,0:T(2,128)S(1)} %bitcast.134), channel_id=1, source_target_pairs={{0,16},{8,24},{16,0},{24,8},{1,17},{9,25},{17,1},{25,9},{2,18},{10... | collective-permute-start | bytes 12296 | tf_op jit(solution)/shard_map/gains/ppermute | solution.py:551
  663.4 14.7 %collective-permute-start.72 = (f32[2,512]{1,0:T(2,128)S(1)}, f32[2,512]{1,0:T(2,128)S(1)}, u32[]{:S(2)}, u32[]{:S(2)}) collective-permute-start(f32[2,512]{1,0:T(2,128)S(1)} %bitcast.135), channel_id=1, source_target_pairs={{0,24},{8,16},{16,8},{24,0},{1,25},{9,17},{17,9},{25,1},{2,26},{10... | collective-permute-start | bytes 12296 | tf_op jit(solution)/shard_map/gains/ppermute | solution.py:551
  673.8 22.8 %all-to-all-start.7 = ((bf16[4,512,256]{2,1,0:T(8,128)(2,1)}), bf16[4,512,256]{2,1,0:T(8,128)(2,1)}, u32[]{:S(2)}, u32[]{:S(2)}) async-start(bf16[4,512,256]{2,1,0:T(8,128)(2,1)} %bitcast.43), calls=%async_computation.8 | async-start | bytes 2097152 | tf_op jit(solution)/shard_map/up_grad/all_to_all | solution.py:663
  (118 other events, 1259.4 us)
Sparse Core Ops, SparseCore 0:
  81.1 34.0 all-gather.2
  224.3 45.4 all-gather.4
  515.5 123.3 reduce-scatter.1

commit v7 on v6

--- a/solution.py
+++ b/solution.py
@@ -652,10 +652,10 @@
         )
         return [pieces[0], to_first, to_second]
 
-    def plane_second(pieces):
+    def plane_second(pieces, *hold):
         total = pieces[0].astype(F32)
         for s, piece in enumerate(pieces[1:], 1):
-            total = total + plane_swap(piece, s).astype(F32)
+            total = total + after(plane_swap(piece, s), *hold).astype(F32)
         return total.astype(BF16)
 
     def give_back(total):
@@ -685,7 +685,7 @@
         gate_whole = exchange(scaled(gate_weight, gain_two))
     with jax.named_scope("out_row"):
         out_full = lax.all_gather(
-            after(own_first(out_weight), *qkv_list[1:3]), "row", axis=0, tiled=True
+            after(own_first(out_weight), *qkv_list), "row", axis=0, tiled=True
         )
     with jax.named_scope("grad_plane"):
         g_part = to_parts(after(out_grad, gate_whole))
@@ -706,6 +706,8 @@
     qkv_full = join_rows([after(a, query) for a in qkv_list])
     mixed, logs = attend(after(query, gates[1], gates[2]), key, value, start_row)
     mixed = after(mixed, gates[3])
+    with jax.named_scope("grad_row"):
+        g_own = lax.all_gather(after(g_part, out_full), "row", axis=0, tiled=True)
 
     def scatter_parts(own, other):
         low = (own.astype(F32) + core_swap(other).astype(F32)).astype(BF16)
@@ -726,9 +728,6 @@
         ups = spread_weights(after(up_whole, middle_low))
     with jax.named_scope("down_plane"):
         downs = spread_weights(after(down_whole, ups[1], ups[2]))
-    with jax.named_scope("grad_row"):
-        g_own = lax.all_gather(after(g_part, out_full, *m_list[1:3]), "row", axis=0, tiled=True)
-        g_other = core_swap(g_own)
     square = jnp.sum(middle * middle, axis=1, keepdims=True)
     square = square + core_swap(square)
     scale_mid = lax.rsqrt(square / width + EPS)
@@ -736,7 +735,10 @@
     pairs = [slice(at, at + 2) for at in range(0, rows, 2)]
     found = [activate(feat, m_list[pair], m_others[pair], gates, ups) for pair in pairs]
     hiddens = [f[0] for f in found]
-    parts, scaled_grads, held, down_parts = [None] * rows, [None] * len(pairs), (), None
+    with jax.named_scope("grad_row"):
+        g_own = after(g_own, *m_others)
+        g_other = core_swap(g_own)
+    parts, scaled_grads, held, down_parts = [None] * rows, [None] * len(pairs), hiddens, None
     for at in reversed(range(len(pairs))):
         with jax.named_scope("unit_grad"):
             _, slope_gate, slope_up, scale = found[at]
@@ -786,7 +788,7 @@
             feed_sent.extend(lows)
             return ()
 
-        feed_first, feed_last = reduce_row(shares, note, split=True)
+        feed_first, feed_last = reduce_row(shares, note, note, split=True)
     with jax.named_scope("middle_grad"):
         pieces = spread(d_low)
         d_own = put_rows(
@@ -796,14 +798,15 @@
     mixed_grad = fold(feat, d_own, d_other, out_full)
     with jax.named_scope("gate_grad"):
         gate_middle = plane_first([after(a, d_own) for a in gate_parts])
-        gate_total = plane_second(gate_middle)
-        gate_blocks = give_back(gate_total)
     query_grad, key_grad, value_grad = attend_back(
         query, key, value, mixed, after(mixed_grad, *gate_middle), start_row, logs, cosine, front, back
     )
     with jax.named_scope("feed"):
         feed_low = (middle + feed_first.astype(F32) + after(feed_last, query_grad).astype(F32)).astype(BF16)
-    query_grad = after(query_grad, down_blocks, gate_total)
+    with jax.named_scope("gate_grad"):
+        gate_total = plane_second(gate_middle, query_grad)
+        gate_blocks = give_back(gate_total)
+    query_grad = after(query_grad, down_blocks, gate_total, feed_low)
     heads_part, gain_dots = heads_outer(
         feat, x_own, x_other, d_own, d_other, query_grad, key_grad, value_grad, mixed, scale_one, qkv_full
     )

time: 721 us -> 720 us (level)
  starting transfers between devices: 96.7 us -> 104 us
    all_gather x2, waiting for transfers between devices: 43.5 us -> 0.01 us  [the longest x1 0.01 us: local(): lax.all_gather(after(own_first(out_weight), *qkv_list), 'row', axis=0, ti...]
    ppermute x15, waiting for transfers between devices: 125 us -> 144 us  [row_swap(): return lax.ppermute(a, 'row', [(i, i ^ step) for i in range(rows)])]
    all_to_all x2, waiting for transfers between devices: 0.02 us -> 18.4 us  [plane_exchange(): lax.all_to_all(a, 'col', split_axis=0, concat_axis=0, axis_index_groups=g...]
    all_to_all x3, waiting for transfers between devices: 22.4 us -> 31 us  [give_back(): return lax.all_to_all(total, 'row', split_axis=0, concat_axis=0, tiled=True)]
    all_to_all x3, waiting for transfers between devices: 21.4 us -> 13.2 us  [exchange(): lax.all_to_all(pieces, 'row', split_axis=0, concat_axis=0, tiled=True)]
    unnamed x204 -> x178, local copies, waits for them, and re-layouts: 32.8 us -> 30.5 us
  transfers between devices with their start and end apart: 84 -> 84, of which waited for: 35 -> 30; matrix products, arithmetic and copies ran while one was open for 15% -> 14% of each run, Pallas kernels for 14% -> 15%
where the time goes in v7:
time: 720 us; the launch traced here: 709 us
  waiting for transfers between devices  324 us (45%)
  Pallas kernels  132 us (18%)
  starting transfers between devices  104 us (14%)
  local copies, waits for them, and re-layouts  67.3 us (9%)
  other arithmetic  65.4 us (9%)
  between operations  15.8 us (2%)
    ppermute x15, waiting for transfers between devices, row_swap(): return lax.ppermute(a, 'row', [(i, i ^ step) for i in range(rows)])  144 us
    ppermute x39, waiting for transfers between devices, plane_swap(): return lax.ppermute(a, 'col', [(i, i ^ 2 * step) for i in range(cols)])  107 us
    ppermute x39, starting transfers between devices, plane_swap(): return lax.ppermute(a, 'col', [(i, i ^ 2 * step) for i in range(cols)])  45.2 us
    all_to_all x3, waiting for transfers between devices, give_back(): return lax.all_to_all(total, 'row', split_axis=0, concat_axis=0, tiled=True)  31 us
    unnamed x178, local copies, waits for them, and re-layouts  30.5 us
    pallas_call x4, Pallas kernels, unfold(): pl.pallas_call(functools.partial(unfold_kernel, feat, len(lefts)), grid=(...  25.2 us
    pallas_call x3, Pallas kernels, outer(): pl.pallas_call(functools.partial(outer_kernel, len(owns), count), grid=(h...  19.7 us
    ppermute x15, starting transfers between devices, row_swap(): return lax.ppermute(a, 'row', [(i, i ^ step) for i in range(rows)])  19.4 us
  transfers between devices with their start and end apart: 84, of which 30 were waited for; matrix products, arithmetic and copies ran while one was open for 14% of the time, Pallas kernels for 15%

profile of v7, /device:TPU:0, one launch (start us, length us, event | category | flops | bytes accessed | tf_op | source)
XLA Modules:
  0.0 708.5 jit_solution(16264539542698122033)
XLA Ops:
  7.2 3.0 collective-permute-start
  12.4 2.9 multiply_convert_fusion
  16.6 5.5 all-to-all-start
  23.4 2.9 collective-permute-start.5
  28.8 6.3 collective-permute-done.1
  39.1 41.7 %collective-permute-done.5.refs_2_ = bf16[512,768]{1,0:T(8,128)(2,1)} collective-permute-done((bf16[512,768]{1,0:T(8,128)(2,1)}, bf16[512,768]{1,0:T(8,128)(2,1)}, u32[]{:S(2)}, u32[]{:S(2)}) %collective-permute-start.5) | collective-permute-done | bytes 786464 | tf_op jit(solution)/shard_map/qkv_row/ppermute | solution.py:551
  82.3 2.9 broadcast_select_fusion.1
  87.5 12.1 %collective-permute-done.6.refs_3_ = bf16[512,768]{1,0:T(8,128)(2,1)} collective-permute-done((bf16[512,768]{1,0:T(8,128)(2,1)}, bf16[512,768]{1,0:T(8,128)(2,1)}, u32[]{:S(2)}, u32[]{:S(2)}) %collective-permute-start.6) | collective-permute-done | bytes 786464 | tf_op jit(solution)/shard_map/qkv_row/ppermute | solution.py:551
  104.9 2.6 copy.36.refs_6_.back_ref
  108.6 2.5 copy.34.refs_4_.cos_ref
  111.2 4.3 all-to-all-start.1
  130.8 3.5 all-to-all-start.2
  138.4 6.7 project.1
  148.3 10.0 %attend.1 = (bf16[1024,256]{1,0:T(8,128)(2,1)}, f32[2,2,1024]{2,1,0:T(2,128)}) custom-call(bf16[1024,256]{1,0:T(8,128)(2,1)} %copy-done.31, bf16[1024,256]{1,0:T(8,128)(2,1)} %copy-done.32, bf16[1024,256]{1,0:T(8,128)(2,1)} %copy-done.33, s32[1,1024]{1,0:T(1,128)} %bitcast.121), custom_call_target="tpu_custom_call" | custom-call | tf_op jit(solution)/shard_map/attend/pallas_call | solution.py:406
  161.6 5.1 mix.1
  169.3 5.0 all-to-all-start.3
  175.1 3.2 add_convert_fusion.1
  182.0 11.3 %collective-permute-done.12 = bf16[256,1024]{1,0:T(8,128)(2,1)S(1)} collective-permute-done((bf16[256,1024]{1,0:T(8,128)(2,1)S(1)}, bf16[256,1024]{1,0:T(8,128)(2,1)S(1)}, u32[]{:S(2)}, u32[]{:S(2)}) %collective-permute-start.12) | collective-permute-done | bytes 524320 | tf_op jit(solution)/shard_map/mix_plane/ppermute | solution.py:537
  193.2 10.8 %collective-permute-done.13 = bf16[256,1024]{1,0:T(8,128)(2,1)S(1)} collective-permute-done((bf16[256,1024]{1,0:T(8,128)(2,1)S(1)}, bf16[256,1024]{1,0:T(8,128)(2,1)S(1)}, u32[]{:S(2)}, u32[]{:S(2)}) %collective-permute-start.13) | collective-permute-done | bytes 524320 | tf_op jit(solution)/shard_map/mix_plane/ppermute | solution.py:537
  206.5 13.2 %all-to-all-done.3 = bf16[4,512,256]{2,1,0:T(8,128)(2,1)S(1)} async-done(((bf16[4,512,256]{2,1,0:T(8,128)(2,1)}), bf16[4,512,256]{2,1,0:T(8,128)(2,1)S(1)}, u32[]{:S(2)}, u32[]{:S(2)}) %all-to-all-start.3) | async-done | bytes 1048608 | tf_op jit(solution)/shard_map/down_row/all_to_all | solution.py:630
  219.8 2.6 multiply_reduce_fusion.3
  224.1 33.1 %collective-permute-done.22.refs_0_.refs_2_ = bf16[256,1024]{1,0:T(8,128)(2,1)} collective-permute-done((bf16[256,1024]{1,0:T(8,128)(2,1)S(1)}, bf16[256,1024]{1,0:T(8,128)(2,1)}, u32[]{:S(2)}, u32[]{:S(2)}) %collective-permute-start.22) | collective-permute-done | bytes 524320 | tf_op jit(solution)/shard_map/middle_row/ppermute | solution.py:551
  259.8 11.3 %collective-permute-done.24.refs_1_.refs_3_ = bf16[256,1024]{1,0:T(8,128)(2,1)} collective-permute-done((bf16[256,1024]{1,0:T(8,128)(2,1)}, bf16[256,1024]{1,0:T(8,128)(2,1)}, u32[]{:S(2)}, u32[]{:S(2)}) %collective-permute-start.24) | collective-permute-done | bytes 524320 | tf_op jit(solution)/shard_map/middle_row/ppermute | solution.py:551
  273.4 8.6 %collective-permute-done.18.refs_7_.refs_14_ = bf16[2048,256]{1,0:T(8,128)(2,1)} collective-permute-done((bf16[2048,256]{1,0:T(8,128)(2,1)S(1)}, bf16[2048,256]{1,0:T(8,128)(2,1)}, u32[]{:S(2)}, u32[]{:S(2)}) %collective-permute-start.18) | collective-permute-done | bytes 1048608 | tf_op jit(solution)/shard_map/up_plane/ppermute | solution.py:537
  288.7 19.7 %collective-permute-done.28.refs_7_.refs_3_ = bf16[2048,256]{1,0:T(8,128)(2,1)S(1)} collective-permute-done((bf16[2048,256]{1,0:T(8,128)(2,1)S(1)}, bf16[2048,256]{1,0:T(8,128)(2,1)S(1)}, u32[]{:S(2)}, u32[]{:S(2)}) %collective-permute-start.28) | collective-permute-done | bytes 1048608 | tf_op jit(solution)/shard_map/down_plane/ppermute | solution.py:537
  310.8 9.5 %collective-permute-done.20 = bf16[1024,256]{1,0:T(8,128)(2,1)S(1)} collective-permute-done((bf16[1024,256]{1,0:T(8,128)(2,1)S(1)}, bf16[1024,256]{1,0:T(8,128)(2,1)S(1)}, u32[]{:S(2)}, u32[]{:S(2)}) %collective-permute-start.20) | collective-permute-done | bytes 524320 | tf_op jit(solution)/shard_map/up_plane/ppermute | solution.py:537
  320.4 8.4 %activate.2 = (bf16[512,1024]{1,0:T(8,128)(2,1)S(1)}, bf16[512,1024]{1,0:T(8,128)(2,1)S(1)}, bf16[512,1024]{1,0:T(8,128)(2,1)S(1)}, f32[512,1]{1,0:T(8,128)S(1)}) custom-call(bf16[256,1024]{1,0:T(8,128)(2,1)S(1)} %copy-done.21, bf16[256,1024]{1,0:T(8,128)(2,1)} %collective-permute-done.15.refs_1_, bf16[256,1024]{1,0:T(8,128)(2,1)S(1)} %copy-done.24, ...), custom_call_target="tpu_custom_call" | custom-call | tf_op jit(solution)/shard_map/activate/pallas_call | solution.py:165
  328.9 8.7 %activate.3 = (bf16[512,1024]{1,0:T(8,128)(2,1)S(1)}, bf16[512,1024]{1,0:T(8,128)(2,1)S(1)}, bf16[512,1024]{1,0:T(8,128)(2,1)S(1)}, f32[512,1]{1,0:T(8,128)S(1)}) custom-call(bf16[256,1024]{1,0:T(8,128)(2,1)} %collective-permute-done.22.refs_0_.refs_2_, bf16[256,1024]{1,0:T(8,128)(2,1)} %collective-permute-done.24.refs_1_.refs_3_, ...), custom_call_target="tpu_custom_call" | custom-call | tf_op jit(solution)/shard_map/activate/pallas_call | solution.py:165
  339.2 9.3 %units_back.2 = (bf16[512,1024]{1,0:T(8,128)(2,1)S(1)}, bf16[512,1024]{1,0:T(8,128)(2,1)S(1)}, bf16[512,1024]{1,0:T(8,128)(2,1)S(1)}, bf16[512,1024]{1,0:T(8,128)(2,1)S(1)}) custom-call(s32[2]{0:T(128)S(1)} %pad_add_fusion.1.starts, bf16[1024,1024]{1,0:T(8,128)(2,1)} %all-gather.5.cloned.1.call-done.refs_0_, bf16[1024,1024]{1,0:T(8,128)(2,1)} %copy-done.15, ...), custom_call_target="tpu_custom_call" | custom-call | tf_op jit(solution)/shard_map/unit_grad/units_back/pallas_call | solution.py:230
  348.6 2.6 collective-permute-done.31
  354.4 6.2 down_outer.1
  365.6 9.3 %units_back.3 = (bf16[512,1024]{1,0:T(8,128)(2,1)S(1)}, bf16[512,1024]{1,0:T(8,128)(2,1)S(1)}, bf16[512,1024]{1,0:T(8,128)(2,1)S(1)}, bf16[512,1024]{1,0:T(8,128)(2,1)S(1)}) custom-call(s32[2]{0:T(128)S(1)} %pad_add_fusion.2.starts, bf16[1024,1024]{1,0:T(8,128)(2,1)} %all-gather.5.cloned.1.call-done.refs_0_, bf16[1024,1024]{1,0:T(8,128)(2,1)} %copy-done.15, ...), custom_call_target="tpu_custom_call" | custom-call | tf_op jit(solution)/shard_map/unit_grad/units_back/pallas_call | solution.py:230
  383.7 6.2 feed.3
  390.2 6.0 feed.2
  396.3 9.5 %collective-permute-done.37 = bf16[256,1024]{1,0:T(8,128)(2,1)S(1)} collective-permute-done((bf16[256,1024]{1,0:T(8,128)(2,1)}, bf16[256,1024]{1,0:T(8,128)(2,1)S(1)}, u32[]{:S(2)}, u32[]{:S(2)}) %collective-permute-start.37) | collective-permute-done | bytes 524320 | tf_op jit(solution)/shard_map/unit_grad/ppermute | solution.py:551
  407.7 3.0 add_convert_fusion.5
  418.9 6.6 up_outer.1
  428.5 6.9 gate_outer.1
  436.7 4.7 collective-permute-done.48
  443.8 11.7 %collective-permute-done.51 = bf16[1024,256]{1,0:T(8,128)(2,1)S(1)} collective-permute-done((bf16[1024,256]{1,0:T(8,128)(2,1)S(1)}, bf16[1024,256]{1,0:T(8,128)(2,1)S(1)}, u32[]{:S(2)}, u32[]{:S(2)}) %collective-permute-start.51) | collective-permute-done | bytes 524320 | tf_op jit(solution)/shard_map/gate_grad/ppermute | solution.py:537
  459.8 4.2 all-to-all-start.6
  475.6 24.9 %collective-permute-done.43 = bf16[256,1024]{1,0:T(8,128)(2,1)S(1)} collective-permute-done((bf16[256,1024]{1,0:T(8,128)(2,1)S(1)}, bf16[256,1024]{1,0:T(8,128)(2,1)S(1)}, u32[]{:S(2)}, u32[]{:S(2)}) %collective-permute-start.43) | collective-permute-done | bytes 524320 | tf_op jit(solution)/shard_map/feed/ppermute | solution.py:551
  500.5 11.1 %collective-permute-done.46 = bf16[256,1024]{1,0:T(8,128)(2,1)S(1)} collective-permute-done((bf16[256,1024]{1,0:T(8,128)(2,1)S(1)}, bf16[256,1024]{1,0:T(8,128)(2,1)S(1)}, u32[]{:S(2)}, u32[]{:S(2)}) %collective-permute-start.46) | collective-permute-done | bytes 524320 | tf_op jit(solution)/shard_map/feed/ppermute | solution.py:551
  511.7 3.5 fold.1.do_ref
  515.9 11.1 %attend_back.1 = (bf16[1024,256]{1,0:T(8,128)(2,1)}, bf16[1024,256]{1,0:T(8,128)(2,1)}, bf16[1024,256]{1,0:T(8,128)(2,1)}) custom-call(bf16[1024,256]{1,0:T(8,128)(2,1)} %copy-done.31, bf16[1024,256]{1,0:T(8,128)(2,1)} %copy-done.32, bf16[1024,256]{1,0:T(8,128)(2,1)} %copy-done.33, bf16[1024,256]{1,0:T(8,128)(2,1)} %get-tuple-element.116.refs_0_.o_ref.mixed_ref, ...), custom_call_target="tpu_custom_call" | custom-call | tf_op jit(solution)/shard_map/attend_back/pallas_call | solution.py:475
  528.2 3.3 multiply_reduce_fusion.1
  538.3 9.2 %heads_outer.1 = (bf16[2048,1024]{1,0:T(8,128)(2,1)}, f32[2048,1]{1,0:T(8,128)S(1)}) custom-call(bf16[1024,1024]{1,0:T(8,128)(2,1)S(1)} %copy-done.4, bf16[1024,1024]{1,0:T(8,128)(2,1)} %collective-permute-done.3.other_ref.x_other, bf16[1024,1024]{1,0:T(8,128)(2,1)S(1)} %copy-done.13, bf16[1024,1024]{1,0:T(8,128)(2,1)} %collective-permute-done.50.other_ref.d_other, ...), custom_call_target="tpu_custom_call" | custom-call | tf_op jit(solution)/shard_map/heads_outer/pallas_call | solution.py:304
  551.9 10.9 %collective-permute-done.63 = bf16[1024,256]{1,0:T(8,128)(2,1)S(1)} collective-permute-done((bf16[1024,256]{1,0:T(8,128)(2,1)S(1)}, bf16[1024,256]{1,0:T(8,128)(2,1)S(1)}, u32[]{:S(2)}, u32[]{:S(2)}) %collective-permute-start.63) | collective-permute-done | bytes 524320 | tf_op jit(solution)/shard_map/up_grad/ppermute | solution.py:537
  567.0 4.5 all-to-all-start.4
  571.6 7.8 %first_grad.1 = (bf16[1024,1024]{1,0:T(8,128)(2,1)}, bf16[1024,1024]{1,0:T(8,128)(2,1)}) custom-call(bf16[1024,256]{1,0:T(8,128)(2,1)} %get-tuple-element.195.dq_ref.refs_0_, bf16[1024,256]{1,0:T(8,128)(2,1)} %get-tuple-element.188.dk_ref.refs_1_, bf16[1024,256]{1,0:T(8,128)(2,1)} %get-tuple-element.189.dv_ref.refs_2_, bf16[2048,768]{1,0:T(8,128)(2,1)} %copy-done.53), custom_call_target="tpu_custom_call" | custom-call | tf_op jit(solution)/shard_map/first_plane/first_grad/pallas_call | solution.py:118
  581.0 6.7 collective-permute-done.64
  589.0 3.4 multiply_reduce_fusion
  598.2 2.7 finish.4
  600.9 23.1 %all-to-all-done.4.part_ref = bf16[4,512,256]{2,1,0:T(8,128)(2,1)} async-done(((bf16[4,512,256]{2,1,0:T(8,128)(2,1)}), bf16[4,512,256]{2,1,0:T(8,128)(2,1)}, u32[]{:S(2)}, u32[]{:S(2)}) %all-to-all-start.4) | async-done | bytes 1048608 | tf_op jit(solution)/shard_map/gate_grad/all_to_all | solution.py:663
  628.3 3.4 collective-permute-start.71
  632.3 3.2 add_convert_fusion
  642.4 3.5 all-to-all-start.5
  645.9 2.8 finish.5
  648.7 18.4 %all-to-all-done.5 = bf16[4,256,256]{2,1,0:T(8,128)(2,1)S(1)} async-done(((bf16[4,256,256]{2,1,0:T(8,128)(2,1)}), bf16[4,256,256]{2,1,0:T(8,128)(2,1)S(1)}, u32[]{:S(2)}, u32[]{:S(2)}) %all-to-all-start.5) | async-done | bytes 524320 | tf_op jit(solution)/shard_map/block_out/all_to_all | solution.py:599
  667.9 4.4 all-to-all-start.7
  683.3 3.9 collective-permute-done.61
  687.3 7.9 %all-to-all-done.7.part_ref = bf16[4,512,256]{2,1,0:T(8,128)(2,1)} async-done(((bf16[4,512,256]{2,1,0:T(8,128)(2,1)}), bf16[4,512,256]{2,1,0:T(8,128)(2,1)}, u32[]{:S(2)}, u32[]{:S(2)}) %all-to-all-start.7) | async-done | bytes 1048608 | tf_op jit(solution)/shard_map/up_grad/all_to_all | solution.py:663
  695.2 2.8 finish.6
  698.0 2.8 finish.7
  (438 shorter events, 173.5 us)
Async XLA Ops:
  7.2 20.5 %collective-permute-start = (bf16[1024,256]{1,0:T(8,128)(2,1)}, bf16[1024,256]{1,0:T(8,128)(2,1)}, u32[]{:S(2)}, u32[]{:S(2)}) collective-permute-start(bf16[1024,256]{1,0:T(8,128)(2,1)} %param.13), channel_id=1, source_target_pairs={{0,2},{1,3},{2,0},{3,1},{4,6},{5,7},{6,4},{7,5},{8,10},{9,11},{10,... | collective-permute-start | bytes 1572872 | tf_op jit(solution)/shard_map/inputs/ppermute | solution.py:537
  10.2 24.9 %collective-permute-start.1 = (bf16[1024,256]{1,0:T(8,128)(2,1)}, bf16[1024,256]{1,0:T(8,128)(2,1)}, u32[]{:S(2)}, u32[]{:S(2)}) collective-permute-start(bf16[1024,256]{1,0:T(8,128)(2,1)} %param.13), channel_id=1, source_target_pairs={{0,4},{1,5},{2,6},{3,7},{4,0},{5,1},{6,2},{7,3},{8,12},{9,13},{10,... | collective-permute-start | bytes 1572872 | tf_op jit(solution)/shard_map/inputs/ppermute | solution.py:537
  11.7 24.5 %collective-permute-start.2 = (bf16[1024,256]{1,0:T(8,128)(2,1)}, bf16[1024,256]{1,0:T(8,128)(2,1)}, u32[]{:S(2)}, u32[]{:S(2)}) collective-permute-start(bf16[1024,256]{1,0:T(8,128)(2,1)} %param.13), channel_id=1, source_target_pairs={{0,6},{1,7},{2,4},{3,5},{4,2},{5,3},{6,0},{7,1},{8,14},{9,15},{10,... | collective-permute-start | bytes 1572872 | tf_op jit(solution)/shard_map/inputs/ppermute | solution.py:537
  16.6 64.2 %all-to-all-start = ((bf16[4,512,256]{2,1,0:T(8,128)(2,1)}), bf16[4,512,256]{2,1,0:T(8,128)(2,1)S(1)}, u32[]{:S(2)}, u32[]{:S(2)}) async-start(bf16[4,512,256]{2,1,0:T(8,128)(2,1)} %pad_maximum_fusion), calls=%async_computation | async-start | bytes 2097152 | tf_op jit(solution)/shard_map/gate_row/all_to_all | solution.py:630
  22.1 139.5 %all-gather.3.cloned.1.call-start = ((), (), s32[]{:S(2)}) async-start(), calls=%async_computation.9 | async-start | bytes 1310720 | tf_op jit(solution)/shard_map/out_row/all_gather | solution.py:687
  23.4 57.4 %collective-permute-start.5 = (bf16[512,768]{1,0:T(8,128)(2,1)}, bf16[512,768]{1,0:T(8,128)(2,1)}, u32[]{:S(2)}, u32[]{:S(2)}) collective-permute-start(bf16[512,768]{1,0:T(8,128)(2,1)} %maximum_maximum_fusion.refs_0_), channel_id=1, source_target_pairs={{0,16},{8,24},{16,0},{24,8},{1,17},{9,25},{17,1},{25,9},{2,18},{10... | collective-permute-start | bytes 2359304 | tf_op jit(solution)/shard_map/qkv_row/ppermute | solution.py:551
  37.4 91.0 %collective-permute-start.3 = (bf16[1024,1024]{1,0:T(8,128)(2,1)S(1)}, bf16[1024,1024]{1,0:T(8,128)(2,1)}, u32[]{:S(2)}, u32[]{:S(2)}) collective-permute-start(bf16[1024,1024]{1,0:T(8,128)(2,1)S(1)} %constant_dynamic-update-slice_fusion.19.own_ref.x_own), channel_id=1, source_target_pairs={{0,1},{1,0},{2,3},{3,2},{4,5},{5,4},{6,7},{7,6},{8,9},{9,8},{10,11... | collective-permute-start | bytes 6291464 | tf_op jit(solution)/shard_map/inputs/ppermute | solution.py:534
  37.4 50.0 %collective-permute-start.4 = (bf16[512,768]{1,0:T(8,128)(2,1)}, bf16[512,768]{1,0:T(8,128)(2,1)}, u32[]{:S(2)}, u32[]{:S(2)}) collective-permute-start(bf16[512,768]{1,0:T(8,128)(2,1)} %maximum_maximum_fusion.refs_0_), channel_id=1, source_target_pairs={{0,8},{8,0},{16,24},{24,16},{1,9},{9,1},{17,25},{25,17},{2,10},{10... | collective-permute-start | bytes 2359304 | tf_op jit(solution)/shard_map/qkv_row/ppermute | solution.py:551
  80.8 18.8 %collective-permute-start.6 = (bf16[512,768]{1,0:T(8,128)(2,1)}, bf16[512,768]{1,0:T(8,128)(2,1)}, u32[]{:S(2)}, u32[]{:S(2)}) collective-permute-start(bf16[512,768]{1,0:T(8,128)(2,1)} %collective-permute-done.5.refs_2_), channel_id=1, source_target_pairs={{0,8},{8,0},{16,24},{24,16},{1,9},{9,1},{17,25},{25,17},{2,10},{10... | collective-permute-start | bytes 2359304 | tf_op jit(solution)/shard_map/qkv_row/ppermute | solution.py:551
  80.8 38.2 %collective-permute-start.8 = (bf16[2048,256]{1,0:T(8,128)(2,1)S(1)}, bf16[2048,256]{1,0:T(8,128)(2,1)}, u32[]{:S(2)}, u32[]{:S(2)}) collective-permute-start(bf16[2048,256]{1,0:T(8,128)(2,1)S(1)} %bitcast.91), channel_id=1, source_target_pairs={{0,4},{1,5},{2,6},{3,7},{4,0},{5,1},{6,2},{7,3},{8,12},{9,13},{10,... | collective-permute-start | bytes 3145736 | tf_op jit(solution)/shard_map/gate_plane/ppermute | solution.py:537
  85.2 38.8 %collective-permute-start.7 = (bf16[2048,256]{1,0:T(8,128)(2,1)S(1)}, bf16[2048,256]{1,0:T(8,128)(2,1)}, u32[]{:S(2)}, u32[]{:S(2)}) collective-permute-start(bf16[2048,256]{1,0:T(8,128)(2,1)S(1)} %bitcast.92), channel_id=1, source_target_pairs={{0,2},{1,3},{2,0},{3,1},{4,6},{5,7},{6,4},{7,5},{8,10},{9,11},{10,... | collective-permute-start | bytes 3145736 | tf_op jit(solution)/shard_map/gate_plane/ppermute | solution.py:537
  120.9 37.4 %collective-permute-start.9 = (bf16[1024,256]{1,0:T(8,128)(2,1)}, bf16[1024,256]{1,0:T(8,128)(2,1)}, u32[]{:S(2)}, u32[]{:S(2)}) collective-permute-start(bf16[1024,256]{1,0:T(8,128)(2,1)} %slice.306), channel_id=1, source_target_pairs={{0,2},{1,3},{2,0},{3,1},{4,6},{5,7},{6,4},{7,5},{8,10},{9,11},{10,... | collective-permute-start | bytes 1572872 | tf_op jit(solution)/shard_map/gate_plane/ppermute | solution.py:537
  126.1 33.4 %collective-permute-start.10 = (bf16[1024,256]{1,0:T(8,128)(2,1)}, bf16[1024,256]{1,0:T(8,128)(2,1)}, u32[]{:S(2)}, u32[]{:S(2)}) collective-permute-start(bf16[1024,256]{1,0:T(8,128)(2,1)} %slice.307), channel_id=1, source_target_pairs={{0,4},{1,5},{2,6},{3,7},{4,0},{5,1},{6,2},{7,3},{8,12},{9,13},{10,... | collective-permute-start | bytes 1572872 | tf_op jit(solution)/shard_map/gate_plane/ppermute | solution.py:537
  130.8 37.1 %all-to-all-start.2 = ((bf16[4,512,256]{2,1,0:T(8,128)(2,1)}), bf16[4,512,256]{2,1,0:T(8,128)(2,1)S(1)}, u32[]{:S(2)}, u32[]{:S(2)}) async-start(bf16[4,512,256]{2,1,0:T(8,128)(2,1)} %pad_maximum_fusion.2), calls=%async_computation.2 | async-start | bytes 2097152 | tf_op jit(solution)/shard_map/up_row/all_to_all | solution.py:630
  169.3 50.5 %all-to-all-start.3 = ((bf16[4,512,256]{2,1,0:T(8,128)(2,1)}), bf16[4,512,256]{2,1,0:T(8,128)(2,1)S(1)}, u32[]{:S(2)}, u32[]{:S(2)}) async-start(bf16[4,512,256]{2,1,0:T(8,128)(2,1)} %pad_maximum_fusion.4), calls=%async_computation.3 | async-start | bytes 2097152 | tf_op jit(solution)/shard_map/down_row/all_to_all | solution.py:630
  174.3 96.7 %all-gather.5.cloned.1.call-start = ((), (), s32[]{:S(2)}) async-start(), calls=%async_computation.10 | async-start | bytes 2621440 | tf_op jit(solution)/shard_map/grad_row/all_gather | solution.py:710
  178.4 14.8 %collective-permute-start.12 = (bf16[256,1024]{1,0:T(8,128)(2,1)S(1)}, bf16[256,1024]{1,0:T(8,128)(2,1)S(1)}, u32[]{:S(2)}, u32[]{:S(2)}) collective-permute-start(bf16[256,1024]{1,0:T(8,128)(2,1)S(1)} %get-tuple-element.220), channel_id=1, source_target_pairs={{0,2},{1,3},{2,0},{3,1},{4,6},{5,7},{6,4},{7,5},{8,10},{9,11},{10,... | collective-permute-start | bytes 1572872 | tf_op jit(solution)/shard_map/mix_plane/ppermute | solution.py:537
  179.0 25.0 %collective-permute-start.13 = (bf16[256,1024]{1,0:T(8,128)(2,1)S(1)}, bf16[256,1024]{1,0:T(8,128)(2,1)S(1)}, u32[]{:S(2)}, u32[]{:S(2)}) collective-permute-start(bf16[256,1024]{1,0:T(8,128)(2,1)S(1)} %get-tuple-element.222), channel_id=1, source_target_pairs={{0,4},{1,5},{2,6},{3,7},{4,0},{5,1},{6,2},{7,3},{8,12},{9,13},{10,... | collective-permute-start | bytes 1572872 | tf_op jit(solution)/shard_map/mix_plane/ppermute | solution.py:537
  179.7 24.3 %collective-permute-start.14 = (bf16[256,1024]{1,0:T(8,128)(2,1)S(1)}, bf16[256,1024]{1,0:T(8,128)(2,1)S(1)}, u32[]{:S(2)}, u32[]{:S(2)}) collective-permute-start(bf16[256,1024]{1,0:T(8,128)(2,1)S(1)} %get-tuple-element.221), channel_id=1, source_target_pairs={{0,6},{1,7},{2,4},{3,5},{4,2},{5,3},{6,0},{7,1},{8,14},{9,15},{10,... | collective-permute-start | bytes 1572872 | tf_op jit(solution)/shard_map/mix_plane/ppermute | solution.py:537
  222.4 34.8 %collective-permute-start.22 = (bf16[256,1024]{1,0:T(8,128)(2,1)S(1)}, bf16[256,1024]{1,0:T(8,128)(2,1)}, u32[]{:S(2)}, u32[]{:S(2)}) collective-permute-start(bf16[256,1024]{1,0:T(8,128)(2,1)S(1)} %get-tuple-element.230.refs_0_), channel_id=1, source_target_pairs={{0,16},{8,24},{16,0},{24,8},{1,17},{9,25},{17,1},{25,9},{2,18},{10... | collective-permute-start | bytes 1572872 | tf_op jit(solution)/shard_map/middle_row/ppermute | solution.py:551
  222.4 36.0 %collective-permute-start.15 = (bf16[256,1024]{1,0:T(8,128)(2,1)S(1)}, bf16[256,1024]{1,0:T(8,128)(2,1)}, u32[]{:S(2)}, u32[]{:S(2)}) collective-permute-start(bf16[256,1024]{1,0:T(8,128)(2,1)S(1)} %get-tuple-element.230.refs_0_), channel_id=1, source_target_pairs={{0,8},{8,0},{16,24},{24,16},{1,9},{9,1},{17,25},{25,17},{2,10},{10... | collective-permute-start | bytes 1572872 | tf_op jit(solution)/shard_map/middle_row/ppermute | solution.py:551
  223.3 35.2 %collective-permute-start.16 = (bf16[256,1024]{1,0:T(8,128)(2,1)S(1)}, bf16[256,1024]{1,0:T(8,128)(2,1)S(1)}, u32[]{:S(2)}, u32[]{:S(2)}) collective-permute-start(bf16[256,1024]{1,0:T(8,128)(2,1)S(1)} %get-tuple-element.230.refs_0_), channel_id=1, source_target_pairs={{0,1},{1,0},{2,3},{3,2},{4,5},{5,4},{6,7},{7,6},{8,9},{9,8},{10,11... | collective-permute-start | bytes 1572872 | tf_op jit(solution)/shard_map/middle_row/ppermute | solution.py:534
  257.2 24.9 %collective-permute-start.18 = (bf16[2048,256]{1,0:T(8,128)(2,1)S(1)}, bf16[2048,256]{1,0:T(8,128)(2,1)}, u32[]{:S(2)}, u32[]{:S(2)}) collective-permute-start(bf16[2048,256]{1,0:T(8,128)(2,1)S(1)} %bitcast.97), channel_id=1, source_target_pairs={{0,2},{1,3},{2,0},{3,1},{4,6},{5,7},{6,4},{7,5},{8,10},{9,11},{10,... | collective-permute-start | bytes 3145736 | tf_op jit(solution)/shard_map/up_plane/ppermute | solution.py:537
  257.8 24.6 %collective-permute-start.19 = (bf16[2048,256]{1,0:T(8,128)(2,1)S(1)}, bf16[2048,256]{1,0:T(8,128)(2,1)}, u32[]{:S(2)}, u32[]{:S(2)}) collective-permute-start(bf16[2048,256]{1,0:T(8,128)(2,1)S(1)} %bitcast.98), channel_id=1, source_target_pairs={{0,4},{1,5},{2,6},{3,7},{4,0},{5,1},{6,2},{7,3},{8,12},{9,13},{10,... | collective-permute-start | bytes 3145736 | tf_op jit(solution)/shard_map/up_plane/ppermute | solution.py:537
  273.3 64.5 %collective-permute-start.26 = (bf16[1024,1024]{1,0:T(8,128)(2,1)}, bf16[1024,1024]{1,0:T(8,128)(2,1)S(1)}, u32[]{:S(2)}, u32[]{:S(2)}) collective-permute-start(bf16[1024,1024]{1,0:T(8,128)(2,1)} %all-gather.5.cloned.1.call-done.refs_0_), channel_id=1, source_target_pairs={{0,1},{1,0},{2,3},{3,2},{4,5},{5,4},{6,7},{7,6},{8,9},{9,8},{10,11... | collective-permute-start | bytes 6291464 | tf_op jit(solution)/shard_map/grad_row/ppermute | solution.py:534
  282.4 26.1 %collective-permute-start.28 = (bf16[2048,256]{1,0:T(8,128)(2,1)S(1)}, bf16[2048,256]{1,0:T(8,128)(2,1)S(1)}, u32[]{:S(2)}, u32[]{:S(2)}) collective-permute-start(bf16[2048,256]{1,0:T(8,128)(2,1)S(1)} %bitcast.104), channel_id=1, source_target_pairs={{0,4},{1,5},{2,6},{3,7},{4,0},{5,1},{6,2},{7,3},{8,12},{9,13},{10,... | collective-permute-start | bytes 3145736 | tf_op jit(solution)/shard_map/down_plane/ppermute | solution.py:537
  283.0 27.0 %collective-permute-start.27 = (bf16[2048,256]{1,0:T(8,128)(2,1)S(1)}, bf16[2048,256]{1,0:T(8,128)(2,1)S(1)}, u32[]{:S(2)}, u32[]{:S(2)}) collective-permute-start(bf16[2048,256]{1,0:T(8,128)(2,1)S(1)} %bitcast.105), channel_id=1, source_target_pairs={{0,2},{1,3},{2,0},{3,1},{4,6},{5,7},{6,4},{7,5},{8,10},{9,11},{10,... | collective-permute-start | bytes 3145736 | tf_op jit(solution)/shard_map/down_plane/ppermute | solution.py:537
  285.5 34.8 %collective-permute-start.20 = (bf16[1024,256]{1,0:T(8,128)(2,1)S(1)}, bf16[1024,256]{1,0:T(8,128)(2,1)S(1)}, u32[]{:S(2)}, u32[]{:S(2)}) collective-permute-start(bf16[1024,256]{1,0:T(8,128)(2,1)S(1)} %slice.314), channel_id=1, source_target_pairs={{0,2},{1,3},{2,0},{3,1},{4,6},{5,7},{6,4},{7,5},{8,10},{9,11},{10,... | collective-permute-start | bytes 1572872 | tf_op jit(solution)/shard_map/up_plane/ppermute | solution.py:537
  287.2 33.1 %collective-permute-start.21 = (bf16[1024,256]{1,0:T(8,128)(2,1)S(1)}, bf16[1024,256]{1,0:T(8,128)(2,1)S(1)}, u32[]{:S(2)}, u32[]{:S(2)}) collective-permute-start(bf16[1024,256]{1,0:T(8,128)(2,1)S(1)} %slice.315), channel_id=1, source_target_pairs={{0,4},{1,5},{2,6},{3,7},{4,0},{5,1},{6,2},{7,3},{8,12},{9,13},{10,... | collective-permute-start | bytes 1572872 | tf_op jit(solution)/shard_map/up_plane/ppermute | solution.py:537
  308.5 29.1 %collective-permute-start.29 = (bf16[1024,256]{1,0:T(8,128)(2,1)S(1)}, bf16[1024,256]{1,0:T(8,128)(2,1)S(1)}, u32[]{:S(2)}, u32[]{:S(2)}) collective-permute-start(bf16[1024,256]{1,0:T(8,128)(2,1)S(1)} %slice.316), channel_id=1, source_target_pairs={{0,2},{1,3},{2,0},{3,1},{4,6},{5,7},{6,4},{7,5},{8,10},{9,11},{10,... | collective-permute-start | bytes 1572872 | tf_op jit(solution)/shard_map/down_plane/ppermute | solution.py:537
  310.1 27.6 %collective-permute-start.30 = (bf16[1024,256]{1,0:T(8,128)(2,1)S(1)}, bf16[1024,256]{1,0:T(8,128)(2,1)S(1)}, u32[]{:S(2)}, u32[]{:S(2)}) collective-permute-start(bf16[1024,256]{1,0:T(8,128)(2,1)S(1)} %slice.317), channel_id=1, source_target_pairs={{0,4},{1,5},{2,6},{3,7},{4,0},{5,1},{6,2},{7,3},{8,12},{9,13},{10,... | collective-permute-start | bytes 1572872 | tf_op jit(solution)/shard_map/down_plane/ppermute | solution.py:537
  360.7 14.3 %collective-permute-start.39 = (bf16[1024,256]{1,0:T(8,128)(2,1)S(1)}, bf16[1024,256]{1,0:T(8,128)(2,1)S(1)}, u32[]{:S(2)}, u32[]{:S(2)}) collective-permute-start(bf16[1024,256]{1,0:T(8,128)(2,1)S(1)} %get-tuple-element.227), channel_id=1, source_target_pairs={{0,4},{1,5},{2,6},{3,7},{4,0},{5,1},{6,2},{7,3},{8,12},{9,13},{10,... | collective-permute-start | bytes 1572872 | tf_op jit(solution)/shard_map/down_grad/ppermute | solution.py:537
  362.2 15.1 %collective-permute-start.41 = (bf16[1024,256]{1,0:T(8,128)(2,1)S(1)}, bf16[1024,256]{1,0:T(8,128)(2,1)S(1)}, u32[]{:S(2)}, u32[]{:S(2)}) collective-permute-start(bf16[1024,256]{1,0:T(8,128)(2,1)S(1)} %get-tuple-element.228), channel_id=1, source_target_pairs={{0,2},{1,3},{2,0},{3,1},{4,6},{5,7},{6,4},{7,5},{8,10},{9,11},{10,... | collective-permute-start | bytes 1572872 | tf_op jit(solution)/shard_map/down_grad/ppermute | solution.py:537
  363.7 16.3 %collective-permute-start.32 = (bf16[256,1024]{1,0:T(8,128)(2,1)}, bf16[256,1024]{1,0:T(8,128)(2,1)S(1)}, u32[]{:S(2)}, u32[]{:S(2)}) collective-permute-start(bf16[256,1024]{1,0:T(8,128)(2,1)} %slice.413), channel_id=1, source_target_pairs={{0,8},{8,0},{16,24},{24,16},{1,9},{9,1},{17,25},{25,17},{2,10},{10... | collective-permute-start | bytes 1572872 | tf_op jit(solution)/shard_map/unit_grad/ppermute | solution.py:551
  376.4 31.2 %collective-permute-start.40 = (bf16[2048,256]{1,0:T(8,128)(2,1)}, bf16[2048,256]{1,0:T(8,128)(2,1)}, u32[]{:S(2)}, u32[]{:S(2)}) collective-permute-start(bf16[2048,256]{1,0:T(8,128)(2,1)} %pad_maximum_fusion.5), channel_id=1, source_target_pairs={{0,2},{1,3},{2,0},{3,1},{4,6},{5,7},{6,4},{7,5},{8,10},{9,11},{10,... | collective-permute-start | bytes 3145736 | tf_op jit(solution)/shard_map/down_grad/ppermute | solution.py:537
  378.5 29.2 %collective-permute-start.42 = (bf16[2048,256]{1,0:T(8,128)(2,1)}, bf16[2048,256]{1,0:T(8,128)(2,1)}, u32[]{:S(2)}, u32[]{:S(2)}) collective-permute-start(bf16[2048,256]{1,0:T(8,128)(2,1)} %pad_maximum_fusion.6), channel_id=1, source_target_pairs={{0,4},{1,5},{2,6},{3,7},{4,0},{5,1},{6,2},{7,3},{8,12},{9,13},{10,... | collective-permute-start | bytes 3145736 | tf_op jit(solution)/shard_map/down_grad/ppermute | solution.py:537
  380.9 24.9 %collective-permute-start.37 = (bf16[256,1024]{1,0:T(8,128)(2,1)}, bf16[256,1024]{1,0:T(8,128)(2,1)S(1)}, u32[]{:S(2)}, u32[]{:S(2)}) collective-permute-start(bf16[256,1024]{1,0:T(8,128)(2,1)} %fusion.8), channel_id=1, source_target_pairs={{0,16},{8,24},{16,0},{24,8},{1,17},{9,25},{17,1},{25,9},{2,18},{10... | collective-permute-start | bytes 1572872 | tf_op jit(solution)/shard_map/unit_grad/ppermute | solution.py:551
  383.4 22.5 %collective-permute-start.36 = (bf16[256,1024]{1,0:T(8,128)(2,1)S(1)}, bf16[256,1024]{1,0:T(8,128)(2,1)S(1)}, u32[]{:S(2)}, u32[]{:S(2)}) collective-permute-start(bf16[256,1024]{1,0:T(8,128)(2,1)S(1)} %slice.412), channel_id=1, source_target_pairs={{0,8},{8,0},{16,24},{24,16},{1,9},{9,1},{17,25},{25,17},{2,10},{10... | collective-permute-start | bytes 1572872 | tf_op jit(solution)/shard_map/unit_grad/ppermute | solution.py:551
  389.9 20.7 %collective-permute-start.44 = (bf16[512,1024]{1,0:T(8,128)(2,1)}, bf16[512,1024]{1,0:T(8,128)(2,1)}, u32[]{:S(2)}, u32[]{:S(2)}) collective-permute-start(bf16[512,1024]{1,0:T(8,128)(2,1)} %get-tuple-element.157), channel_id=1, source_target_pairs={{0,1},{1,0},{2,3},{3,2},{4,5},{5,4},{6,7},{7,6},{8,9},{9,8},{10,11... | collective-permute-start | bytes 3145736 | tf_op jit(solution)/shard_map/feed/ppermute | solution.py:534
  414.2 21.6 %collective-permute-start.45 = (bf16[256,1024]{1,0:T(8,128)(2,1)S(1)}, bf16[256,1024]{1,0:T(8,128)(2,1)S(1)}, u32[]{:S(2)}, u32[]{:S(2)}) collective-permute-start(bf16[256,1024]{1,0:T(8,128)(2,1)S(1)} %slice.273), channel_id=1, source_target_pairs={{0,8},{8,0},{16,24},{24,16},{1,9},{9,1},{17,25},{25,17},{2,10},{10... | collective-permute-start | bytes 1572872 | tf_op jit(solution)/shard_map/feed/ppermute | solution.py:551
  415.4 21.4 %collective-permute-start.49 = (bf16[256,1024]{1,0:T(8,128)(2,1)S(1)}, bf16[256,1024]{1,0:T(8,128)(2,1)S(1)}, u32[]{:S(2)}, u32[]{:S(2)}) collective-permute-start(bf16[256,1024]{1,0:T(8,128)(2,1)S(1)} %get-tuple-element.155), channel_id=1, source_target_pairs={{0,6},{1,7},{2,4},{3,5},{4,2},{5,3},{6,0},{7,1},{8,14},{9,15},{10,... | collective-permute-start | bytes 1572872 | tf_op jit(solution)/shard_map/middle_grad/ppermute | solution.py:537
  416.2 25.2 %collective-permute-start.48 = (bf16[256,1024]{1,0:T(8,128)(2,1)S(1)}, bf16[256,1024]{1,0:T(8,128)(2,1)S(1)}, u32[]{:S(2)}, u32[]{:S(2)}) collective-permute-start(bf16[256,1024]{1,0:T(8,128)(2,1)S(1)} %get-tuple-element.155), channel_id=1, source_target_pairs={{0,4},{1,5},{2,6},{3,7},{4,0},{5,1},{6,2},{7,3},{8,12},{9,13},{10,... | collective-permute-start | bytes 1572872 | tf_op jit(solution)/shard_map/middle_grad/ppermute | solution.py:537
  417.2 24.3 %collective-permute-start.47 = (bf16[256,1024]{1,0:T(8,128)(2,1)S(1)}, bf16[256,1024]{1,0:T(8,128)(2,1)S(1)}, u32[]{:S(2)}, u32[]{:S(2)}) collective-permute-start(bf16[256,1024]{1,0:T(8,128)(2,1)S(1)} %get-tuple-element.155), channel_id=1, source_target_pairs={{0,2},{1,3},{2,0},{3,1},{4,6},{5,7},{6,4},{7,5},{8,10},{9,11},{10,... | collective-permute-start | bytes 1572872 | tf_op jit(solution)/shard_map/middle_grad/ppermute | solution.py:537
  442.4 69.2 %collective-permute-start.50 = (bf16[1024,1024]{1,0:T(8,128)(2,1)S(1)}, bf16[1024,1024]{1,0:T(8,128)(2,1)}, u32[]{:S(2)}, u32[]{:S(2)}) collective-permute-start(bf16[1024,1024]{1,0:T(8,128)(2,1)S(1)} %constant_dynamic-update-slice_fusion.15.own_ref.d_own), channel_id=1, source_target_pairs={{0,1},{1,0},{2,3},{3,2},{4,5},{5,4},{6,7},{7,6},{8,9},{9,8},{10,11... | collective-permute-start | bytes 6291464 | tf_op jit(solution)/shard_map/middle_grad/ppermute | solution.py:534
  442.4 14.9 %collective-permute-start.52 = (bf16[1024,256]{1,0:T(8,128)(2,1)S(1)}, bf16[1024,256]{1,0:T(8,128)(2,1)S(1)}, u32[]{:S(2)}, u32[]{:S(2)}) collective-permute-start(bf16[1024,256]{1,0:T(8,128)(2,1)S(1)} %get-tuple-element.225), channel_id=1, source_target_pairs={{0,2},{1,3},{2,0},{3,1},{4,6},{5,7},{6,4},{7,5},{8,10},{9,11},{10,... | collective-permute-start | bytes 1572872 | tf_op jit(solution)/shard_map/gate_grad/ppermute | solution.py:537
  443.5 20.6 %collective-permute-start.33 = (bf16[512,1024]{1,0:T(8,128)(2,1)}, bf16[512,1024]{1,0:T(8,128)(2,1)}, u32[]{:S(2)}, u32[]{:S(2)}) collective-permute-start(bf16[512,1024]{1,0:T(8,128)(2,1)} %get-tuple-element.139), channel_id=1, source_target_pairs={{0,1},{1,0},{2,3},{3,2},{4,5},{5,4},{6,7},{7,6},{8,9},{9,8},{10,11... | collective-permute-start | bytes 3145736 | tf_op jit(solution)/shard_map/feed/ppermute | solution.py:534
  456.8 70.2 %collective-permute-start.53 = (bf16[2048,256]{1,0:T(8,128)(2,1)}, bf16[2048,256]{1,0:T(8,128)(2,1)}, u32[]{:S(2)}, u32[]{:S(2)}) collective-permute-start(bf16[2048,256]{1,0:T(8,128)(2,1)} %pad_maximum_fusion.7), channel_id=1, source_target_pairs={{0,2},{1,3},{2,0},{3,1},{4,6},{5,7},{6,4},{7,5},{8,10},{9,11},{10,... | collective-permute-start | bytes 3145736 | tf_op jit(solution)/shard_map/gate_grad/ppermute | solution.py:537
  458.5 68.5 %collective-permute-start.54 = (bf16[2048,256]{1,0:T(8,128)(2,1)}, bf16[2048,256]{1,0:T(8,128)(2,1)}, u32[]{:S(2)}, u32[]{:S(2)}) collective-permute-start(bf16[2048,256]{1,0:T(8,128)(2,1)} %pad_maximum_fusion.8), channel_id=1, source_target_pairs={{0,4},{1,5},{2,6},{3,7},{4,0},{5,1},{6,2},{7,3},{8,12},{9,13},{10,... | collective-permute-start | bytes 3145736 | tf_op jit(solution)/shard_map/gate_grad/ppermute | solution.py:537
  459.8 71.8 %all-to-all-start.6 = ((bf16[4,512,256]{2,1,0:T(8,128)(2,1)}), bf16[4,512,256]{2,1,0:T(8,128)(2,1)}, u32[]{:S(2)}, u32[]{:S(2)}) async-start(bf16[4,512,256]{2,1,0:T(8,128)(2,1)} %bitcast.113), calls=%async_computation.6 | async-start | bytes 2097152 | tf_op jit(solution)/shard_map/down_grad/all_to_all | solution.py:663
  464.0 234.0 %reduce-scatter.2.cloned.1.call-start = ((), (), s32[]{:S(2)}) async-start(), calls=%async_computation.11 | async-start | bytes 5242880 | tf_op jit(solution)/shard_map/heads_grad/reduce_scatter | solution.py:814
  466.2 34.3 %collective-permute-start.43 = (bf16[256,1024]{1,0:T(8,128)(2,1)S(1)}, bf16[256,1024]{1,0:T(8,128)(2,1)S(1)}, u32[]{:S(2)}, u32[]{:S(2)}) collective-permute-start(bf16[256,1024]{1,0:T(8,128)(2,1)S(1)} %slice.271), channel_id=1, source_target_pairs={{0,8},{8,0},{16,24},{24,16},{1,9},{9,1},{17,25},{25,17},{2,10},{10... | collective-permute-start | bytes 1572872 | tf_op jit(solution)/shard_map/feed/ppermute | solution.py:551
  468.1 43.5 %collective-permute-start.46 = (bf16[256,1024]{1,0:T(8,128)(2,1)S(1)}, bf16[256,1024]{1,0:T(8,128)(2,1)S(1)}, u32[]{:S(2)}, u32[]{:S(2)}) collective-permute-start(bf16[256,1024]{1,0:T(8,128)(2,1)S(1)} %copy-done.74), channel_id=1, source_target_pairs={{0,16},{8,24},{16,0},{24,8},{1,17},{9,25},{17,1},{25,9},{2,18},{10... | collective-permute-start | bytes 1572872 | tf_op jit(solution)/shard_map/feed/ppermute | solution.py:551
  564.0 23.6 %collective-permute-start.64 = (bf16[2048,256]{1,0:T(8,128)(2,1)}, bf16[2048,256]{1,0:T(8,128)(2,1)}, u32[]{:S(2)}, u32[]{:S(2)}) collective-permute-start(bf16[2048,256]{1,0:T(8,128)(2,1)} %pad_maximum_fusion.9), channel_id=1, source_target_pairs={{0,2},{1,3},{2,0},{3,1},{4,6},{5,7},{6,4},{7,5},{8,10},{9,11},{10,... | collective-permute-start | bytes 3145736 | tf_op jit(solution)/shard_map/up_grad/ppermute | solution.py:537
  565.7 23.3 %collective-permute-start.66 = (bf16[2048,256]{1,0:T(8,128)(2,1)}, bf16[2048,256]{1,0:T(8,128)(2,1)}, u32[]{:S(2)}, u32[]{:S(2)}) collective-permute-start(bf16[2048,256]{1,0:T(8,128)(2,1)} %pad_maximum_fusion.10), channel_id=1, source_target_pairs={{0,4},{1,5},{2,6},{3,7},{4,0},{5,1},{6,2},{7,3},{8,12},{9,13},{10,... | collective-permute-start | bytes 3145736 | tf_op jit(solution)/shard_map/up_grad/ppermute | solution.py:537
  567.0 56.9 %all-to-all-start.4 = ((bf16[4,512,256]{2,1,0:T(8,128)(2,1)}), bf16[4,512,256]{2,1,0:T(8,128)(2,1)}, u32[]{:S(2)}, u32[]{:S(2)}) async-start(bf16[4,512,256]{2,1,0:T(8,128)(2,1)} %bitcast.32), calls=%async_computation.4 | async-start | bytes 2097152 | tf_op jit(solution)/shard_map/gate_grad/all_to_all | solution.py:663
  579.4 53.0 %collective-permute-start.55 = (bf16[1024,1024]{1,0:T(8,128)(2,1)}, bf16[1024,1024]{1,0:T(8,128)(2,1)}, u32[]{:S(2)}, u32[]{:S(2)}) collective-permute-start(bf16[1024,1024]{1,0:T(8,128)(2,1)} %get-tuple-element.197), channel_id=1, source_target_pairs={{0,1},{1,0},{2,3},{3,2},{4,5},{5,4},{6,7},{7,6},{8,9},{9,8},{10,11... | collective-permute-start | bytes 6291464 | tf_op jit(solution)/shard_map/first_plane/ppermute | solution.py:534
  593.8 30.1 %collective-permute-start.68 = (f32[2,4,2,256]{3,2,1,0:T(2,128)S(1)}, f32[2,4,2,256]{3,2,1,0:T(2,128)S(1)}, u32[]{:S(2)}, u32[]{:S(2)}) collective-permute-start(f32[2,4,2,256]{3,2,1,0:T(2,128)S(1)} %add.270), channel_id=1, source_target_pairs={{0,2},{1,3},{2,0},{3,1},{4,6},{5,7},{6,4},{7,5},{8,10},{9,11},{10,... | collective-permute-start | bytes 49160 | tf_op jit(solution)/shard_map/gains/ppermute | solution.py:617
  628.3 20.4 %collective-permute-start.71 = (f32[2,512]{1,0:T(2,128)S(1)}, f32[2,512]{1,0:T(2,128)S(1)}, u32[]{:S(2)}, u32[]{:S(2)}) collective-permute-start(f32[2,512]{1,0:T(2,128)S(1)} %bitcast.134), channel_id=1, source_target_pairs={{0,16},{8,24},{16,0},{24,8},{1,17},{9,25},{17,1},{25,9},{2,18},{10... | collective-permute-start | bytes 12296 | tf_op jit(solution)/shard_map/gains/ppermute | solution.py:551
  631.7 17.0 %collective-permute-start.72 = (f32[2,512]{1,0:T(2,128)S(1)}, f32[2,512]{1,0:T(2,128)S(1)}, u32[]{:S(2)}, u32[]{:S(2)}) collective-permute-start(f32[2,512]{1,0:T(2,128)S(1)} %bitcast.135), channel_id=1, source_target_pairs={{0,24},{8,16},{16,8},{24,0},{1,25},{9,17},{17,9},{25,1},{2,26},{10... | collective-permute-start | bytes 12296 | tf_op jit(solution)/shard_map/gains/ppermute | solution.py:551
  638.0 34.3 %collective-permute-start.56 = (bf16[256,1024]{1,0:T(8,128)(2,1)}, bf16[256,1024]{1,0:T(8,128)(2,1)}, u32[]{:S(2)}, u32[]{:S(2)}) collective-permute-start(bf16[256,1024]{1,0:T(8,128)(2,1)} %get-tuple-element.217), channel_id=1, source_target_pairs={{0,2},{1,3},{2,0},{3,1},{4,6},{5,7},{6,4},{7,5},{8,10},{9,11},{10,... | collective-permute-start | bytes 1572872 | tf_op jit(solution)/shard_map/first_plane/ppermute | solution.py:537
  639.3 33.0 %collective-permute-start.57 = (bf16[256,1024]{1,0:T(8,128)(2,1)}, bf16[256,1024]{1,0:T(8,128)(2,1)}, u32[]{:S(2)}, u32[]{:S(2)}) collective-permute-start(bf16[256,1024]{1,0:T(8,128)(2,1)} %get-tuple-element.219), channel_id=1, source_target_pairs={{0,4},{1,5},{2,6},{3,7},{4,0},{5,1},{6,2},{7,3},{8,12},{9,13},{10,... | collective-permute-start | bytes 1572872 | tf_op jit(solution)/shard_map/first_plane/ppermute | solution.py:537
  640.7 31.6 %collective-permute-start.58 = (bf16[256,1024]{1,0:T(8,128)(2,1)}, bf16[256,1024]{1,0:T(8,128)(2,1)}, u32[]{:S(2)}, u32[]{:S(2)}) collective-permute-start(bf16[256,1024]{1,0:T(8,128)(2,1)} %get-tuple-element.218), channel_id=1, source_target_pairs={{0,6},{1,7},{2,4},{3,5},{4,2},{5,3},{6,0},{7,1},{8,14},{9,15},{10,... | collective-permute-start | bytes 1572872 | tf_op jit(solution)/shard_map/first_plane/ppermute | solution.py:537
  642.4 24.7 %all-to-all-start.5 = ((bf16[4,256,256]{2,1,0:T(8,128)(2,1)}), bf16[4,256,256]{2,1,0:T(8,128)(2,1)S(1)}, u32[]{:S(2)}, u32[]{:S(2)}) async-start(bf16[4,256,256]{2,1,0:T(8,128)(2,1)} %pad_maximum_fusion.12), calls=%async_computation.5 | async-start | bytes 1048576 | tf_op jit(solution)/shard_map/block_out/all_to_all | solution.py:599
  667.9 27.3 %all-to-all-start.7 = ((bf16[4,512,256]{2,1,0:T(8,128)(2,1)}), bf16[4,512,256]{2,1,0:T(8,128)(2,1)}, u32[]{:S(2)}, u32[]{:S(2)}) async-start(bf16[4,512,256]{2,1,0:T(8,128)(2,1)} %bitcast.43), calls=%async_computation.8 | async-start | bytes 2097152 | tf_op jit(solution)/shard_map/up_grad/all_to_all | solution.py:663
  (105 other events, 1249.3 us)
Sparse Core Ops, SparseCore 0:
  99.7 26.1 all-gather.2
  176.7 76.4 all-gather.4
  548.7 91.7 reduce-scatter.1

commit v8 on v7

--- a/solution.py
+++ b/solution.py
@@ -68,7 +68,10 @@
     heads = outs[0].shape[1]
     picks = [pl.ds(pl.multiple_of(starts[i] * feat, feat), feat) for i in range(len(weights))]
     values = jnp.concatenate([ref[:, pick] for pick in picks for ref in (own_ref, other_ref)], axis=1)
-    cosine, front, back = cos_ref[...], front_ref[...], back_ref[...]
+    times = heads // cos_ref.shape[1]
+    cosine, front, back = (
+        jnp.concatenate([ref[...]] * times, axis=1) for ref in (cos_ref, front_ref, back_ref)
+    )
     for at, ref in enumerate(outs[:3]):
         columns = slice(at * heads, (at + 1) * heads)
         result = nn(values, jnp.concatenate([w[:, columns] for w in weights], axis=0)) * scale
@@ -497,9 +500,9 @@
     zero = jnp.zeros_like(sine)
     heads = width // HEAD_DIM
     return (
-        jnp.tile(cosine, (1, 2 * heads)),
-        jnp.tile(jnp.concatenate([-sine, zero], axis=1), (1, heads)),
-        jnp.tile(jnp.concatenate([zero, sine], axis=1), (1, heads)),
+        jnp.concatenate([cosine] * (2 * heads), axis=1),
+        jnp.concatenate([-sine, zero] * heads, axis=1),
+        jnp.concatenate([zero, sine] * heads, axis=1),
     )
 
 
@@ -550,23 +553,22 @@
     def row_swap(a, step):
         return lax.ppermute(a, "row", [(i, i ^ step) for i in range(rows)])
 
-    def gather_row(a):
+    def gather_row(a, held=()):
         got, bit = {0: a}, rows // 2
         while bit:
             for step in list(got):
-                got[step ^ bit] = row_swap(got[step], bit)
+                came = row_swap(got[step], bit)
+                got[step ^ bit] = after(came, *held) if 2 * bit == rows else came
             bit //= 2
         return [got[step] for step in range(rows)]
 
-    def reduce_row(parts, *works, split=False):
+    def reduce_row(parts, *works):
         parts, bit, step = list(parts), 1, 0
         while bit < rows:
             lows = {at: parts[at + bit].astype(BF16) for at in range(rows - 2 * bit, -1, -2 * bit)}
             held = works[step](*lows.values()) if step < len(works) else ()
             for at, low in lows.items():
                 came = after(row_swap(low, bit), *held)
-                if split and 2 * bit == rows:
-                    return parts[0], came
                 parts[at] = parts[at].astype(F32) + came.astype(F32)
             bit, step = 2 * bit, step + 1
         return parts[0]
@@ -601,8 +603,9 @@
         )
 
     def to_parts(a):
-        a = plane_exchange(a.reshape(places, quarter, feat))
-        return jnp.concatenate([a[s] for s in range(places)], axis=1)
+        return put_feats(
+            [token_part(a, 0)] + [plane_swap(token_part(a, s), s) for s in range(1, places)]
+        )
 
     def to_home(a):
         a = jnp.stack([a[:, s * feat : (s + 1) * feat] for s in range(places)])
@@ -624,10 +627,13 @@
     def scaled(w, gain):
         return own_first((w.astype(F32) * gain).astype(BF16))
 
-    def exchange(w):
+    def cut(w):
         part = w.shape[1] // rows
-        pieces = jnp.stack([w[:, s * part : (s + 1) * part] for s in range(rows)])
-        return lax.all_to_all(pieces, "row", split_axis=0, concat_axis=0, tiled=True).reshape(width, part)
+        return jnp.stack([w[:, s * part : (s + 1) * part] for s in range(rows)])
+
+    def exchange(pieces):
+        got = lax.all_to_all(pieces, "row", split_axis=0, concat_axis=0, tiled=True)
+        return got.reshape(width, pieces.shape[2])
 
     def spread_weights(whole):
         if places != 4:
@@ -672,34 +678,36 @@
     starts = jnp.stack([row ^ s for s in range(rows)])
     cores = core.reshape(1)
 
+    with jax.named_scope("prepare"):
+        cosine, front, back = rope_tables(positions, LANES)
+        start_row = jnp.sum(
+            (segment_ids[None, :] < segment_ids[:, None]).astype(jnp.int32), axis=1
+        )[None, :]
+        up_cut = cut(scaled(up_weight, gain_two))
+        down_cut = cut(own_first(down_weight))
+        out_block = own_first(out_weight)
+    with jax.named_scope("inputs"):
+        x_own = put_feats(spread(inputs))
+        x_other = core_swap(x_own)
+    with jax.named_scope("grad_plane"):
+        g_part = to_parts(after(out_grad, x_own))
     with jax.named_scope("qkv_row"):
         qkv_list = gather_row(
             jnp.concatenate(
                 [scaled(w, gain_one) for w in (query_weight, key_weight, value_weight)], axis=1
-            )
-        )
-    with jax.named_scope("inputs"):
-        x_own = put_feats(spread(inputs))
-        x_other = core_swap(x_own)
+            ),
+            (cosine, front, back, start_row, up_cut, down_cut, out_block, g_part),
+        )
     with jax.named_scope("gate_row"):
-        gate_whole = exchange(scaled(gate_weight, gain_two))
+        gate_whole = exchange(cut(scaled(gate_weight, gain_two)))
     with jax.named_scope("out_row"):
-        out_full = lax.all_gather(
-            after(own_first(out_weight), *qkv_list), "row", axis=0, tiled=True
-        )
-    with jax.named_scope("grad_plane"):
-        g_part = to_parts(after(out_grad, gate_whole))
+        out_full = lax.all_gather(after(out_block, *qkv_list[1:3]), "row", axis=0, tiled=True)
     with jax.named_scope("up_row"):
-        up_whole = exchange(after(scaled(up_weight, gain_two), g_part, x_other, *qkv_list))
+        up_whole = exchange(after(up_cut, gate_whole))
     with jax.named_scope("down_row"):
-        down_whole = exchange(after(own_first(down_weight), up_whole))
+        down_whole = exchange(after(down_cut, up_whole))
     with jax.named_scope("gate_plane"):
         gates = spread_weights(gate_whole)
-    heads_width = query_weight.shape[1]
-    cosine, front, back = rope_tables(positions, heads_width)
-    start_row = jnp.sum(
-        (segment_ids[None, :] < segment_ids[:, None]).astype(jnp.int32), axis=1
-    )[None, :]
     query, key, value, scale_one = project(
         feat, starts, x_own, x_other, qkv_list, cosine, front, back
     )
@@ -720,14 +728,14 @@
         own, other = unfold(feat, "mix", [mixed], [out_full])
         middle = token_part(x_own, 0).astype(F32) + scatter_parts(after(own, up_whole), other)
         middle = after(middle, down_whole)
-    middle_low = middle.astype(BF16)
+    with jax.named_scope("up_plane"):
+        ups = spread_weights(up_whole)
+    middle_low = after(middle.astype(BF16), ups[1], ups[2])
     with jax.named_scope("middle_row"):
         m_list = gather_row(middle_low)
         m_others = [core_swap(m) for m in m_list]
-    with jax.named_scope("up_plane"):
-        ups = spread_weights(after(up_whole, middle_low))
     with jax.named_scope("down_plane"):
-        downs = spread_weights(after(down_whole, ups[1], ups[2]))
+        downs = spread_weights(down_whole)
     square = jnp.sum(middle * middle, axis=1, keepdims=True)
     square = square + core_swap(square)
     scale_mid = lax.rsqrt(square / width + EPS)
@@ -736,7 +744,7 @@
     found = [activate(feat, m_list[pair], m_others[pair], gates, ups) for pair in pairs]
     hiddens = [f[0] for f in found]
     with jax.named_scope("grad_row"):
-        g_own = after(g_own, *m_others)
+        g_own = after(g_own, hiddens[0])
         g_other = core_swap(g_own)
     parts, scaled_grads, held, down_parts = [None] * rows, [None] * len(pairs), hiddens, None
     for at in reversed(range(len(pairs))):
@@ -774,25 +782,20 @@
 
     d_low = after(middle_grad.astype(BF16), down_total)
     with jax.named_scope("feed"):
-        shares = []
-        for own, other in kept:
-            low = own.astype(F32) + core_swap(other).astype(F32)
-            low = after(low.astype(BF16), d_low)
-            shares += [low[:quarter], low[quarter:]]
+        shares = jnp.zeros((rows * quarter, half), BF16)
+        for pair, (own, other) in zip(pairs, kept):
+            low = (own.astype(F32) + core_swap(other).astype(F32)).astype(BF16)
+            for i in range(2):
+                shares = lax.dynamic_update_slice_in_dim(
+                    shares, low[i * quarter : (i + 1) * quarter], starts[pair.start + i] * quarter, 0
+                )
+        feed = lax.psum_scatter(after(shares, d_low), "row", scatter_dimension=0, tiled=True)
     gate_parts = outer(feat, "gate_outer", starts, m_list, m_others, [after(a, d_low) for a, _ in scaled_grads], places)
     up_parts = outer(feat, "up_outer", starts, m_list, m_others, [after(a, d_low) for _, a in scaled_grads], places)
-    with jax.named_scope("feed"):
-        feed_sent = []
-
-        def note(*lows):
-            feed_sent.extend(lows)
-            return ()
-
-        feed_first, feed_last = reduce_row(shares, note, note, split=True)
     with jax.named_scope("middle_grad"):
         pieces = spread(d_low)
         d_own = put_rows(
-            [pieces[0]] + [after(a, gate_parts[0], up_parts[0], feed_sent[-1]) for a in pieces[1:]]
+            [pieces[0]] + [after(a, gate_parts[0], up_parts[0], shares) for a in pieces[1:]]
         )
         d_other = core_swap(d_own)
     mixed_grad = fold(feat, d_own, d_other, out_full)
@@ -802,11 +805,11 @@
         query, key, value, mixed, after(mixed_grad, *gate_middle), start_row, logs, cosine, front, back
     )
     with jax.named_scope("feed"):
-        feed_low = (middle + feed_first.astype(F32) + after(feed_last, query_grad).astype(F32)).astype(BF16)
+        feed_low = (middle + after(feed, query_grad).astype(F32)).astype(BF16)
     with jax.named_scope("gate_grad"):
         gate_total = plane_second(gate_middle, query_grad)
         gate_blocks = give_back(gate_total)
-    query_grad = after(query_grad, down_blocks, gate_total, feed_low)
+    query_grad = after(query_grad, down_blocks, gate_total)
     heads_part, gain_dots = heads_outer(
         feat, x_own, x_other, d_own, d_other, query_grad, key_grad, value_grad, mixed, scale_one, qkv_full
     )
@@ -816,7 +819,7 @@
         up_total = plane_second(plane_first([after(a, gate_total, heads_part) for a in up_parts]))
         up_blocks = give_back(up_total)
     with jax.named_scope("block_out"):
-        block_out = to_home(after(feed_low, gate_blocks))
+        block_out = to_home(after(feed_low, gate_blocks, heads_part))
     with jax.named_scope("first_plane"):
         first_unit_grad = scatter_parts(
             *unfold(feat, "first_grad", [after(query_grad, heads_part), key_grad, value_grad], [qkv_full])

time: 720 us -> 673 us (0.935)
  waiting for transfers between devices: 324 us -> 269 us
  local copies, waits for them, and re-layouts: 67.3 us -> 82.4 us
    ppermute x15 -> x12, waiting for transfers between devices: 144 us -> 62.4 us  [row_swap(): return lax.ppermute(a, 'row', [(i, i ^ step) for i in range(rows)])]
    all_to_all x3, waiting for transfers between devices: 13.2 us -> 72.2 us  [exchange(): got = lax.all_to_all(pieces, 'row', split_axis=0, concat_axis=0, tiled=True)]
    ppermute x39 -> x42, waiting for transfers between devices: 107 us -> 87.4 us  [plane_swap(): return lax.ppermute(a, 'col', [(i, i ^ 2 * step) for i in range(cols)])]
    unnamed x178 -> x212, local copies, waits for them, and re-layouts: 30.5 us -> 45.5 us
    another operation x10 -> x3, local copies, waits for them, and re-layouts: 12.8 us -> 2.09 us  [the longest x2 3.69 us: rope_tables(): jnp.tile(jnp.concatenate([zero, sine], axis=1), (1, heads))]
    all_to_all x2 -> x1, waiting for transfers between devices: 18.4 us -> 14.8 us  [plane_exchange(): lax.all_to_all(a, 'col', split_axis=0, concat_axis=0, axis_index_groups=g...]
    ppermute x39 -> x42, starting transfers between devices: 45.2 us -> 48.2 us  [plane_swap(): return lax.ppermute(a, 'col', [(i, i ^ 2 * step) for i in range(cols)])]
    ppermute x15 -> x12, starting transfers between devices: 19.4 us -> 17.7 us  [row_swap(): return lax.ppermute(a, 'row', [(i, i ^ step) for i in range(rows)])]
  transfers between devices with their start and end apart: 84 -> 84, of which waited for: 30 -> 33; matrix products, arithmetic and copies ran while one was open for 14% -> 15% of each run, Pallas kernels for 15% -> 17%
where the time goes in v8:
time: 673 us; the launch traced here: 661 us
  waiting for transfers between devices  269 us (40%)
  Pallas kernels  128 us (19%)
  starting transfers between devices  101 us (15%)
  local copies, waits for them, and re-layouts  82.4 us (12%)
  other arithmetic  64.8 us (10%)
  between operations  15.7 us (2%)
    ppermute x42, waiting for transfers between devices, plane_swap(): return lax.ppermute(a, 'col', [(i, i ^ 2 * step) for i in range(cols)])  87.4 us
    all_to_all x3, waiting for transfers between devices, exchange(): got = lax.all_to_all(pieces, 'row', split_axis=0, concat_axis=0, tiled=True)  72.2 us
    ppermute x12, waiting for transfers between devices, row_swap(): return lax.ppermute(a, 'row', [(i, i ^ step) for i in range(rows)])  62.4 us
    ppermute x42, starting transfers between devices, plane_swap(): return lax.ppermute(a, 'col', [(i, i ^ 2 * step) for i in range(cols)])  48.2 us
    unnamed x212, local copies, waits for them, and re-layouts  45.5 us
    all_to_all x3, waiting for transfers between devices, give_back(): return lax.all_to_all(total, 'row', split_axis=0, concat_axis=0, tiled=True)  26.3 us
    pallas_call x4, Pallas kernels, unfold(): pl.pallas_call(functools.partial(unfold_kernel, feat, len(lefts)), grid=(...  24.9 us
    pallas_call x3, Pallas kernels, outer(): pl.pallas_call(functools.partial(outer_kernel, len(owns), count), grid=(h...  18.8 us
  transfers between devices with their start and end apart: 84, of which 33 were waited for; matrix products, arithmetic and copies ran while one was open for 15% of the time, Pallas kernels for 17%

profile of v8, /device:TPU:0, one launch (start us, length us, event | category | flops | bytes accessed | tf_op | source)
XLA Modules:
  0.0 661.0 jit_solution(12489053016534806247)
XLA Ops:
  7.2 3.0 collective-permute-start
  14.8 3.0 collective-permute-start.5
  22.0 3.6 all-to-all-start
  45.0 2.3 collective-permute-start.8
  48.0 26.1 %all-to-all-done = bf16[4,512,256]{2,1,0:T(8,128)(2,1)S(1)} async-done(((bf16[4,512,256]{2,1,0:T(8,128)(2,1)}), bf16[4,512,256]{2,1,0:T(8,128)(2,1)S(1)}, u32[]{:S(2)}, u32[]{:S(2)}) %all-to-all-start) | async-done | bytes 1048608 | tf_op jit(solution)/shard_map/gate_row/all_to_all | solution.py:635
  81.9 16.3 %collective-permute-done.11.refs_8_.refs_11_ = bf16[2048,256]{1,0:T(8,128)(2,1)} collective-permute-done((bf16[2048,256]{1,0:T(8,128)(2,1)S(1)}, bf16[2048,256]{1,0:T(8,128)(2,1)}, u32[]{:S(2)}, u32[]{:S(2)}) %collective-permute-start.11) | collective-permute-done | bytes 1048608 | tf_op jit(solution)/shard_map/gate_plane/ppermute | solution.py:540
  105.1 9.1 %collective-permute-done.9.refs_3_ = bf16[512,768]{1,0:T(8,128)(2,1)} collective-permute-done((bf16[512,768]{1,0:T(8,128)(2,1)}, bf16[512,768]{1,0:T(8,128)(2,1)}, u32[]{:S(2)}, u32[]{:S(2)}) %collective-permute-start.9) | collective-permute-done | bytes 786464 | tf_op jit(solution)/shard_map/qkv_row/ppermute | solution.py:554
  117.3 6.7 %project.1 = (bf16[1024,256]{1,0:T(8,128)(2,1)S(1)}, bf16[1024,256]{1,0:T(8,128)(2,1)S(1)}, bf16[1024,256]{1,0:T(8,128)(2,1)S(1)}, f32[1024,1]{1,0:T(8,128)S(1)}) custom-call(s32[4]{0:T(128)S(1)} %pad_add_fusion.starts, bf16[1024,1024]{1,0:T(8,128)(2,1)S(1)} %constant_dynamic-update-slice_fusion.22.own_ref.x_own, ...), custom_call_target="tpu_custom_call" | custom-call | tf_op jit(solution)/shard_map/project/pallas_call | solution.py:89
  127.2 10.0 %attend.1 = (bf16[1024,256]{1,0:T(8,128)(2,1)}, f32[2,2,1024]{2,1,0:T(2,128)}) custom-call(bf16[1024,256]{1,0:T(8,128)(2,1)} %copy-done.45, bf16[1024,256]{1,0:T(8,128)(2,1)} %copy-done.46, bf16[1024,256]{1,0:T(8,128)(2,1)} %copy-done.47, s32[1,1024]{1,0:T(1,128)} %bitcast.105), custom_call_target="tpu_custom_call" | custom-call | tf_op jit(solution)/shard_map/attend/pallas_call | solution.py:409
  140.4 5.1 mix.1
  145.5 7.7 %all-to-all-start.1 = ((bf16[4,512,256]{2,1,0:T(8,128)(2,1)}), bf16[4,512,256]{2,1,0:T(8,128)(2,1)S(1)}, u32[]{:S(2)}, u32[]{:S(2)}) async-start(bf16[4,512,256]{2,1,0:T(8,128)(2,1)} %pad_maximum_fusion), calls=%async_computation.1 | async-start | bytes 2097152 | tf_op jit(solution)/shard_map/up_row/all_to_all | solution.py:635
  154.0 44.8 %all-to-all-done.1 = bf16[4,512,256]{2,1,0:T(8,128)(2,1)S(1)} async-done(((bf16[4,512,256]{2,1,0:T(8,128)(2,1)}), bf16[4,512,256]{2,1,0:T(8,128)(2,1)S(1)}, u32[]{:S(2)}, u32[]{:S(2)}) %all-to-all-start.1) | async-done | bytes 1048608 | tf_op jit(solution)/shard_map/up_row/all_to_all | solution.py:635
  198.8 3.5 all-to-all-start.2
  202.6 3.2 add_convert_fusion.1
  206.1 3.4 collective-permute-start.17
  210.1 10.8 %collective-permute-done.15 = bf16[256,1024]{1,0:T(8,128)(2,1)S(1)} collective-permute-done((bf16[256,1024]{1,0:T(8,128)(2,1)S(1)}, bf16[256,1024]{1,0:T(8,128)(2,1)S(1)}, u32[]{:S(2)}, u32[]{:S(2)}) %collective-permute-start.15) | collective-permute-done | bytes 524320 | tf_op jit(solution)/shard_map/mix_plane/ppermute | solution.py:540
  220.9 11.3 %collective-permute-done.16 = bf16[256,1024]{1,0:T(8,128)(2,1)S(1)} collective-permute-done((bf16[256,1024]{1,0:T(8,128)(2,1)S(1)}, bf16[256,1024]{1,0:T(8,128)(2,1)S(1)}, u32[]{:S(2)}, u32[]{:S(2)}) %collective-permute-start.16) | collective-permute-done | bytes 524320 | tf_op jit(solution)/shard_map/mix_plane/ppermute | solution.py:540
  232.2 2.5 convert_add_fusion.2
  236.0 2.1 multiply_reduce_fusion.3
  238.1 12.3 %collective-permute-done.19.refs_9_.refs_15_ = bf16[2048,256]{1,0:T(8,128)(2,1)} collective-permute-done((bf16[2048,256]{1,0:T(8,128)(2,1)S(1)}, bf16[2048,256]{1,0:T(8,128)(2,1)}, u32[]{:S(2)}, u32[]{:S(2)}) %collective-permute-start.19) | collective-permute-done | bytes 1048608 | tf_op jit(solution)/shard_map/up_plane/ppermute | solution.py:540
  256.2 3.6 collective-permute-done.20.refs_1_
  259.9 2.7 collective-permute-done.23
  262.6 2.6 collective-permute-done.24
  265.2 6.8 %activate.2 = (bf16[512,1024]{1,0:T(8,128)(2,1)S(1)}, bf16[512,1024]{1,0:T(8,128)(2,1)S(1)}, bf16[512,1024]{1,0:T(8,128)(2,1)S(1)}, f32[512,1]{1,0:T(8,128)S(1)}) custom-call(bf16[256,1024]{1,0:T(8,128)(2,1)S(1)} %get-tuple-element.125.refs_0_, bf16[256,1024]{1,0:T(8,128)(2,1)S(1)} %collective-permute-done.20.refs_1_, ...), custom_call_target="tpu_custom_call" | custom-call | tf_op jit(solution)/shard_map/activate/pallas_call | solution.py:168
  278.5 2.5 collective-permute-start.26
  281.0 23.6 %collective-permute-done.26.refs_0_.refs_2_ = bf16[256,1024]{1,0:T(8,128)(2,1)S(1)} collective-permute-done((bf16[256,1024]{1,0:T(8,128)(2,1)}, bf16[256,1024]{1,0:T(8,128)(2,1)S(1)}, u32[]{:S(2)}, u32[]{:S(2)}) %collective-permute-start.26) | collective-permute-done | bytes 524320 | tf_op jit(solution)/shard_map/middle_row/ppermute | solution.py:554
  308.0 10.4 %collective-permute-done.27.refs_1_.refs_3_ = bf16[256,1024]{1,0:T(8,128)(2,1)S(1)} collective-permute-done((bf16[256,1024]{1,0:T(8,128)(2,1)S(1)}, bf16[256,1024]{1,0:T(8,128)(2,1)S(1)}, u32[]{:S(2)}, u32[]{:S(2)}) %collective-permute-start.27) | collective-permute-done | bytes 524320 | tf_op jit(solution)/shard_map/middle_row/ppermute | solution.py:554
  320.3 7.0 %activate.3 = (bf16[512,1024]{1,0:T(8,128)(2,1)S(1)}, bf16[512,1024]{1,0:T(8,128)(2,1)S(1)}, bf16[512,1024]{1,0:T(8,128)(2,1)S(1)}, f32[512,1]{1,0:T(8,128)S(1)}) custom-call(bf16[256,1024]{1,0:T(8,128)(2,1)S(1)} %collective-permute-done.26.refs_0_.refs_2_, bf16[256,1024]{1,0:T(8,128)(2,1)S(1)} %collective-permute-done.27.refs_1_.refs_3_, ...), custom_call_target="tpu_custom_call" | custom-call | tf_op jit(solution)/shard_map/activate/pallas_call | solution.py:168
  328.7 9.3 %units_back.2 = (bf16[512,1024]{1,0:T(8,128)(2,1)S(1)}, bf16[512,1024]{1,0:T(8,128)(2,1)S(1)}, bf16[512,1024]{1,0:T(8,128)(2,1)S(1)}, bf16[512,1024]{1,0:T(8,128)(2,1)S(1)}) custom-call(s32[2]{0:T(128)S(1)} %pad_add_fusion.1.starts, bf16[1024,1024]{1,0:T(8,128)(2,1)} %all-gather.5.cloned.1.call-done.refs_0_, bf16[1024,1024]{1,0:T(8,128)(2,1)} %copy-done.16, ...), custom_call_target="tpu_custom_call" | custom-call | tf_op jit(solution)/shard_map/unit_grad/units_back/pallas_call | solution.py:233
  338.1 2.6 collective-permute-done.34
  343.2 6.1 down_outer.1
  354.0 9.3 %units_back.3 = (bf16[512,1024]{1,0:T(8,128)(2,1)S(1)}, bf16[512,1024]{1,0:T(8,128)(2,1)S(1)}, bf16[512,1024]{1,0:T(8,128)(2,1)S(1)}, bf16[512,1024]{1,0:T(8,128)(2,1)S(1)}) custom-call(s32[2]{0:T(128)S(1)} %pad_add_fusion.2.starts, bf16[1024,1024]{1,0:T(8,128)(2,1)} %all-gather.5.cloned.1.call-done.refs_0_, bf16[1024,1024]{1,0:T(8,128)(2,1)} %copy-done.16, ...), custom_call_target="tpu_custom_call" | custom-call | tf_op jit(solution)/shard_map/unit_grad/units_back/pallas_call | solution.py:233
  370.1 5.9 feed.2
  380.7 6.1 feed.3
  386.8 4.6 collective-permute-done.41
  391.4 11.1 %collective-permute-done.40 = bf16[256,1024]{1,0:T(8,128)(2,1)} collective-permute-done((bf16[256,1024]{1,0:T(8,128)(2,1)}, bf16[256,1024]{1,0:T(8,128)(2,1)}, u32[]{:S(2)}, u32[]{:S(2)}) %collective-permute-start.40) | collective-permute-done | bytes 524320 | tf_op jit(solution)/shard_map/unit_grad/ppermute | solution.py:554
  409.1 3.0 add_convert_fusion.4
  414.2 3.2 fusion.33
  427.6 6.2 up_outer.1
  437.8 6.4 gate_outer.1
  448.3 4.2 all-to-all-start.4
  454.9 6.2 collective-permute-done.51
  473.5 3.5 fold.1.do_ref
  477.8 11.1 %attend_back.1 = (bf16[1024,256]{1,0:T(8,128)(2,1)}, bf16[1024,256]{1,0:T(8,128)(2,1)}, bf16[1024,256]{1,0:T(8,128)(2,1)}) custom-call(bf16[1024,256]{1,0:T(8,128)(2,1)} %copy-done.45, bf16[1024,256]{1,0:T(8,128)(2,1)} %copy-done.46, bf16[1024,256]{1,0:T(8,128)(2,1)} %copy-done.47, bf16[1024,256]{1,0:T(8,128)(2,1)} %get-tuple-element.117.refs_0_.o_ref.mixed_ref, ...), custom_call_target="tpu_custom_call" | custom-call | tf_op jit(solution)/shard_map/attend_back/pallas_call | solution.py:478
  490.1 3.2 multiply_reduce_fusion.1
  500.1 9.2 %heads_outer.1 = (bf16[2048,1024]{1,0:T(8,128)(2,1)}, f32[2048,1]{1,0:T(8,128)S(1)}) custom-call(bf16[1024,1024]{1,0:T(8,128)(2,1)S(1)} %copy-done.3, bf16[1024,1024]{1,0:T(8,128)(2,1)} %collective-permute-done.3.other_ref.x_other, bf16[1024,1024]{1,0:T(8,128)(2,1)S(1)} %copy-done.14, bf16[1024,1024]{1,0:T(8,128)(2,1)} %collective-permute-done.50.other_ref.d_other, ...), custom_call_target="tpu_custom_call" | custom-call | tf_op jit(solution)/shard_map/heads_outer/pallas_call | solution.py:307
  513.8 9.7 %collective-permute-done.63 = bf16[1024,256]{1,0:T(8,128)(2,1)S(1)} collective-permute-done((bf16[1024,256]{1,0:T(8,128)(2,1)S(1)}, bf16[1024,256]{1,0:T(8,128)(2,1)S(1)}, u32[]{:S(2)}, u32[]{:S(2)}) %collective-permute-start.63) | collective-permute-done | bytes 524320 | tf_op jit(solution)/shard_map/up_grad/ppermute | solution.py:540
  528.1 4.5 all-to-all-start.3
  532.7 7.8 %first_grad.1 = (bf16[1024,1024]{1,0:T(8,128)(2,1)}, bf16[1024,1024]{1,0:T(8,128)(2,1)}) custom-call(bf16[1024,256]{1,0:T(8,128)(2,1)} %get-tuple-element.193.dq_ref.refs_0_, bf16[1024,256]{1,0:T(8,128)(2,1)} %get-tuple-element.184.dk_ref.refs_1_, bf16[1024,256]{1,0:T(8,128)(2,1)} %get-tuple-element.185.dv_ref.refs_2_, bf16[2048,768]{1,0:T(8,128)(2,1)} %copy-done.77), custom_call_target="tpu_custom_call" | custom-call | tf_op jit(solution)/shard_map/first_plane/first_grad/pallas_call | solution.py:121
  542.0 5.4 collective-permute-done.64
  548.9 3.4 multiply_reduce_fusion
  555.4 2.7 finish.4
  561.7 23.7 %all-to-all-done.3.part_ref = bf16[4,512,256]{2,1,0:T(8,128)(2,1)} async-done(((bf16[4,512,256]{2,1,0:T(8,128)(2,1)}), bf16[4,512,256]{2,1,0:T(8,128)(2,1)}, u32[]{:S(2)}, u32[]{:S(2)}) %all-to-all-start.3) | async-done | bytes 1048608 | tf_op jit(solution)/shard_map/gate_grad/all_to_all | solution.py:669
  589.6 3.4 collective-permute-start.71
  593.8 3.2 add_convert_fusion
  603.8 3.5 all-to-all-start.5
  607.3 2.8 finish.5
  610.1 14.8 %all-to-all-done.5 = bf16[4,256,256]{2,1,0:T(8,128)(2,1)S(1)} async-done(((bf16[4,256,256]{2,1,0:T(8,128)(2,1)}), bf16[4,256,256]{2,1,0:T(8,128)(2,1)S(1)}, u32[]{:S(2)}, u32[]{:S(2)}) %all-to-all-start.5) | async-done | bytes 524320 | tf_op jit(solution)/shard_map/block_out/all_to_all | solution.py:601
  625.7 4.4 all-to-all-start.6
  633.3 2.0 fusion.6
  642.9 2.0 collective-permute-done.62
  645.0 2.6 all-to-all-done.6.part_ref
  647.6 2.8 finish.6
  650.4 2.8 finish.7
  (471 shorter events, 186.3 us)
Async XLA Ops:
  7.2 26.6 %collective-permute-start = (bf16[1024,256]{1,0:T(8,128)(2,1)}, bf16[1024,256]{1,0:T(8,128)(2,1)}, u32[]{:S(2)}, u32[]{:S(2)}) collective-permute-start(bf16[1024,256]{1,0:T(8,128)(2,1)} %param.13), channel_id=1, source_target_pairs={{0,2},{1,3},{2,0},{3,1},{4,6},{5,7},{6,4},{7,5},{8,10},{9,11},{10,... | collective-permute-start | bytes 1572872 | tf_op jit(solution)/shard_map/inputs/ppermute | solution.py:540
  10.2 24.9 %collective-permute-start.1 = (bf16[1024,256]{1,0:T(8,128)(2,1)}, bf16[1024,256]{1,0:T(8,128)(2,1)}, u32[]{:S(2)}, u32[]{:S(2)}) collective-permute-start(bf16[1024,256]{1,0:T(8,128)(2,1)} %param.13), channel_id=1, source_target_pairs={{0,4},{1,5},{2,6},{3,7},{4,0},{5,1},{6,2},{7,3},{8,12},{9,13},{10,... | collective-permute-start | bytes 1572872 | tf_op jit(solution)/shard_map/inputs/ppermute | solution.py:540
  11.7 24.5 %collective-permute-start.2 = (bf16[1024,256]{1,0:T(8,128)(2,1)}, bf16[1024,256]{1,0:T(8,128)(2,1)}, u32[]{:S(2)}, u32[]{:S(2)}) collective-permute-start(bf16[1024,256]{1,0:T(8,128)(2,1)} %param.13), channel_id=1, source_target_pairs={{0,6},{1,7},{2,4},{3,5},{4,2},{5,3},{6,0},{7,1},{8,14},{9,15},{10,... | collective-permute-start | bytes 1572872 | tf_op jit(solution)/shard_map/inputs/ppermute | solution.py:540
  14.8 66.2 %collective-permute-start.5 = (bf16[512,768]{1,0:T(8,128)(2,1)}, bf16[512,768]{1,0:T(8,128)(2,1)}, u32[]{:S(2)}, u32[]{:S(2)}) collective-permute-start(bf16[512,768]{1,0:T(8,128)(2,1)} %maximum_maximum_fusion.refs_0_), channel_id=1, source_target_pairs={{0,16},{8,24},{16,0},{24,8},{1,17},{9,25},{17,1},{25,9},{2,18},{10... | collective-permute-start | bytes 2359304 | tf_op jit(solution)/shard_map/qkv_row/ppermute | solution.py:554
  17.8 63.2 %collective-permute-start.4 = (bf16[512,768]{1,0:T(8,128)(2,1)}, bf16[512,768]{1,0:T(8,128)(2,1)}, u32[]{:S(2)}, u32[]{:S(2)}) collective-permute-start(bf16[512,768]{1,0:T(8,128)(2,1)} %maximum_maximum_fusion.refs_0_), channel_id=1, source_target_pairs={{0,8},{8,0},{16,24},{24,16},{1,9},{9,1},{17,25},{25,17},{2,10},{10... | collective-permute-start | bytes 2359304 | tf_op jit(solution)/shard_map/qkv_row/ppermute | solution.py:554
  22.0 52.1 %all-to-all-start = ((bf16[4,512,256]{2,1,0:T(8,128)(2,1)}), bf16[4,512,256]{2,1,0:T(8,128)(2,1)S(1)}, u32[]{:S(2)}, u32[]{:S(2)}) async-start(bf16[4,512,256]{2,1,0:T(8,128)(2,1)} %pad_maximum_fusion.2), calls=%async_computation | async-start | bytes 2097152 | tf_op jit(solution)/shard_map/gate_row/all_to_all | solution.py:635
  25.6 114.8 %all-gather.3.cloned.1.call-start = ((), (), s32[]{:S(2)}) async-start(), calls=%async_computation.9 | async-start | bytes 1310720 | tf_op jit(solution)/shard_map/out_row/all_gather | solution.py:704
  37.4 76.8 %collective-permute-start.3 = (bf16[1024,1024]{1,0:T(8,128)(2,1)S(1)}, bf16[1024,1024]{1,0:T(8,128)(2,1)}, u32[]{:S(2)}, u32[]{:S(2)}) collective-permute-start(bf16[1024,1024]{1,0:T(8,128)(2,1)S(1)} %constant_dynamic-update-slice_fusion.22.own_ref.x_own), channel_id=1, source_target_pairs={{0,1},{1,0},{2,3},{3,2},{4,5},{5,4},{6,7},{7,6},{8,9},{9,8},{10,11... | collective-permute-start | bytes 6291464 | tf_op jit(solution)/shard_map/inputs/ppermute | solution.py:537
  45.0 31.4 %collective-permute-start.8 = (bf16[256,256]{1,0:T(8,128)(2,1)}, bf16[256,256]{1,0:T(8,128)(2,1)}, u32[]{:S(2)}, u32[]{:S(2)}) collective-permute-start(bf16[256,256]{1,0:T(8,128)(2,1)} %get-tuple-element.255), channel_id=1, source_target_pairs={{0,6},{1,7},{2,4},{3,5},{4,2},{5,3},{6,0},{7,1},{8,14},{9,15},{10,... | collective-permute-start | bytes 393224 | tf_op jit(solution)/shard_map/grad_plane/ppermute | solution.py:540
  74.1 24.1 %collective-permute-start.11 = (bf16[2048,256]{1,0:T(8,128)(2,1)S(1)}, bf16[2048,256]{1,0:T(8,128)(2,1)}, u32[]{:S(2)}, u32[]{:S(2)}) collective-permute-start(bf16[2048,256]{1,0:T(8,128)(2,1)S(1)} %bitcast.80), channel_id=1, source_target_pairs={{0,4},{1,5},{2,6},{3,7},{4,0},{5,1},{6,2},{7,3},{8,12},{9,13},{10,... | collective-permute-start | bytes 3145736 | tf_op jit(solution)/shard_map/gate_plane/ppermute | solution.py:540
  76.4 25.3 %collective-permute-start.10 = (bf16[2048,256]{1,0:T(8,128)(2,1)S(1)}, bf16[2048,256]{1,0:T(8,128)(2,1)}, u32[]{:S(2)}, u32[]{:S(2)}) collective-permute-start(bf16[2048,256]{1,0:T(8,128)(2,1)S(1)} %bitcast.81), channel_id=1, source_target_pairs={{0,2},{1,3},{2,0},{3,1},{4,6},{5,7},{6,4},{7,5},{8,10},{9,11},{10,... | collective-permute-start | bytes 3145736 | tf_op jit(solution)/shard_map/gate_plane/ppermute | solution.py:540
  81.0 33.1 %collective-permute-start.9 = (bf16[512,768]{1,0:T(8,128)(2,1)}, bf16[512,768]{1,0:T(8,128)(2,1)}, u32[]{:S(2)}, u32[]{:S(2)}) collective-permute-start(bf16[512,768]{1,0:T(8,128)(2,1)} %collective-permute-done.5.refs_2_), channel_id=1, source_target_pairs={{0,8},{8,0},{16,24},{24,16},{1,9},{9,1},{17,25},{25,17},{2,10},{10... | collective-permute-start | bytes 2359304 | tf_op jit(solution)/shard_map/qkv_row/ppermute | solution.py:554
  100.0 37.2 %collective-permute-start.12 = (bf16[1024,256]{1,0:T(8,128)(2,1)}, bf16[1024,256]{1,0:T(8,128)(2,1)}, u32[]{:S(2)}, u32[]{:S(2)}) collective-permute-start(bf16[1024,256]{1,0:T(8,128)(2,1)} %slice.304), channel_id=1, source_target_pairs={{0,2},{1,3},{2,0},{3,1},{4,6},{5,7},{6,4},{7,5},{8,10},{9,11},{10,... | collective-permute-start | bytes 1572872 | tf_op jit(solution)/shard_map/gate_plane/ppermute | solution.py:540
  103.5 34.8 %collective-permute-start.13 = (bf16[1024,256]{1,0:T(8,128)(2,1)}, bf16[1024,256]{1,0:T(8,128)(2,1)}, u32[]{:S(2)}, u32[]{:S(2)}) collective-permute-start(bf16[1024,256]{1,0:T(8,128)(2,1)} %slice.305), channel_id=1, source_target_pairs={{0,4},{1,5},{2,6},{3,7},{4,0},{5,1},{6,2},{7,3},{8,12},{9,13},{10,... | collective-permute-start | bytes 1572872 | tf_op jit(solution)/shard_map/gate_plane/ppermute | solution.py:540
  145.5 57.1 %collective-permute-start.14 = (bf16[1024,1024]{1,0:T(8,128)(2,1)}, bf16[1024,1024]{1,0:T(8,128)(2,1)}, u32[]{:S(2)}, u32[]{:S(2)}) collective-permute-start(bf16[1024,1024]{1,0:T(8,128)(2,1)} %get-tuple-element.122), channel_id=1, source_target_pairs={{0,1},{1,0},{2,3},{3,2},{4,5},{5,4},{6,7},{7,6},{8,9},{9,8},{10,11... | collective-permute-start | bytes 6291464 | tf_op jit(solution)/shard_map/mix_plane/ppermute | solution.py:537
  145.5 53.3 %all-to-all-start.1 = ((bf16[4,512,256]{2,1,0:T(8,128)(2,1)}), bf16[4,512,256]{2,1,0:T(8,128)(2,1)S(1)}, u32[]{:S(2)}, u32[]{:S(2)}) async-start(bf16[4,512,256]{2,1,0:T(8,128)(2,1)} %pad_maximum_fusion), calls=%async_computation.1 | async-start | bytes 2097152 | tf_op jit(solution)/shard_map/up_row/all_to_all | solution.py:635
  153.2 124.5 %all-gather.5.cloned.1.call-start = ((), (), s32[]{:S(2)}) async-start(), calls=%async_computation.10 | async-start | bytes 2621440 | tf_op jit(solution)/shard_map/grad_row/all_gather | solution.py:718
  198.8 37.2 %all-to-all-start.2 = ((bf16[4,512,256]{2,1,0:T(8,128)(2,1)}), bf16[4,512,256]{2,1,0:T(8,128)(2,1)S(1)}, u32[]{:S(2)}, u32[]{:S(2)}) async-start(bf16[4,512,256]{2,1,0:T(8,128)(2,1)} %pad_maximum_fusion.1), calls=%async_computation.2 | async-start | bytes 2097152 | tf_op jit(solution)/shard_map/down_row/all_to_all | solution.py:635
  202.3 355.8 %reduce-scatter.3.cloned.1.call-start = ((), (), s32[]{:S(2)}) async-start(), calls=%async_computation.11 | async-start | bytes 2621440 | tf_op jit(solution)/shard_map/feed/reduce_scatter | solution.py:792
  206.0 14.9 %collective-permute-start.15 = (bf16[256,1024]{1,0:T(8,128)(2,1)S(1)}, bf16[256,1024]{1,0:T(8,128)(2,1)S(1)}, u32[]{:S(2)}, u32[]{:S(2)}) collective-permute-start(bf16[256,1024]{1,0:T(8,128)(2,1)S(1)} %get-tuple-element.218), channel_id=1, source_target_pairs={{0,2},{1,3},{2,0},{3,1},{4,6},{5,7},{6,4},{7,5},{8,10},{9,11},{10,... | collective-permute-start | bytes 1572872 | tf_op jit(solution)/shard_map/mix_plane/ppermute | solution.py:540
  206.0 26.2 %collective-permute-start.16 = (bf16[256,1024]{1,0:T(8,128)(2,1)S(1)}, bf16[256,1024]{1,0:T(8,128)(2,1)S(1)}, u32[]{:S(2)}, u32[]{:S(2)}) collective-permute-start(bf16[256,1024]{1,0:T(8,128)(2,1)S(1)} %get-tuple-element.220), channel_id=1, source_target_pairs={{0,4},{1,5},{2,6},{3,7},{4,0},{5,1},{6,2},{7,3},{8,12},{9,13},{10,... | collective-permute-start | bytes 1572872 | tf_op jit(solution)/shard_map/mix_plane/ppermute | solution.py:540
  206.1 26.1 %collective-permute-start.17 = (bf16[256,1024]{1,0:T(8,128)(2,1)S(1)}, bf16[256,1024]{1,0:T(8,128)(2,1)S(1)}, u32[]{:S(2)}, u32[]{:S(2)}) collective-permute-start(bf16[256,1024]{1,0:T(8,128)(2,1)S(1)} %get-tuple-element.219), channel_id=1, source_target_pairs={{0,6},{1,7},{2,4},{3,5},{4,2},{5,3},{6,0},{7,1},{8,14},{9,15},{10,... | collective-permute-start | bytes 1572872 | tf_op jit(solution)/shard_map/mix_plane/ppermute | solution.py:540
  209.5 40.8 %collective-permute-start.19 = (bf16[2048,256]{1,0:T(8,128)(2,1)S(1)}, bf16[2048,256]{1,0:T(8,128)(2,1)}, u32[]{:S(2)}, u32[]{:S(2)}) collective-permute-start(bf16[2048,256]{1,0:T(8,128)(2,1)S(1)} %bitcast.86), channel_id=1, source_target_pairs={{0,4},{1,5},{2,6},{3,7},{4,0},{5,1},{6,2},{7,3},{8,12},{9,13},{10,... | collective-permute-start | bytes 3145736 | tf_op jit(solution)/shard_map/up_plane/ppermute | solution.py:540
  209.5 40.8 %collective-permute-start.18 = (bf16[2048,256]{1,0:T(8,128)(2,1)S(1)}, bf16[2048,256]{1,0:T(8,128)(2,1)}, u32[]{:S(2)}, u32[]{:S(2)}) collective-permute-start(bf16[2048,256]{1,0:T(8,128)(2,1)S(1)} %bitcast.87), channel_id=1, source_target_pairs={{0,2},{1,3},{2,0},{3,1},{4,6},{5,7},{6,4},{7,5},{8,10},{9,11},{10,... | collective-permute-start | bytes 3145736 | tf_op jit(solution)/shard_map/up_plane/ppermute | solution.py:540
  277.8 49.6 %collective-permute-start.25 = (bf16[1024,1024]{1,0:T(8,128)(2,1)}, bf16[1024,1024]{1,0:T(8,128)(2,1)S(1)}, u32[]{:S(2)}, u32[]{:S(2)}) collective-permute-start(bf16[1024,1024]{1,0:T(8,128)(2,1)} %all-gather.5.cloned.1.call-done.refs_0_), channel_id=1, source_target_pairs={{0,1},{1,0},{2,3},{3,2},{4,5},{5,4},{6,7},{7,6},{8,9},{9,8},{10,11... | collective-permute-start | bytes 6291464 | tf_op jit(solution)/shard_map/grad_row/ppermute | solution.py:537
  277.8 26.8 %collective-permute-start.31 = (bf16[2048,256]{1,0:T(8,128)(2,1)S(1)}, bf16[2048,256]{1,0:T(8,128)(2,1)S(1)}, u32[]{:S(2)}, u32[]{:S(2)}) collective-permute-start(bf16[2048,256]{1,0:T(8,128)(2,1)S(1)} %bitcast.92), channel_id=1, source_target_pairs={{0,4},{1,5},{2,6},{3,7},{4,0},{5,1},{6,2},{7,3},{8,12},{9,13},{10,... | collective-permute-start | bytes 3145736 | tf_op jit(solution)/shard_map/down_plane/ppermute | solution.py:540
  278.1 28.0 %collective-permute-start.30 = (bf16[2048,256]{1,0:T(8,128)(2,1)S(1)}, bf16[2048,256]{1,0:T(8,128)(2,1)S(1)}, u32[]{:S(2)}, u32[]{:S(2)}) collective-permute-start(bf16[2048,256]{1,0:T(8,128)(2,1)S(1)} %bitcast.93), channel_id=1, source_target_pairs={{0,2},{1,3},{2,0},{3,1},{4,6},{5,7},{6,4},{7,5},{8,10},{9,11},{10,... | collective-permute-start | bytes 3145736 | tf_op jit(solution)/shard_map/down_plane/ppermute | solution.py:540
  278.5 26.0 %collective-permute-start.26 = (bf16[256,1024]{1,0:T(8,128)(2,1)}, bf16[256,1024]{1,0:T(8,128)(2,1)S(1)}, u32[]{:S(2)}, u32[]{:S(2)}) collective-permute-start(bf16[256,1024]{1,0:T(8,128)(2,1)} %copy-done.18), channel_id=1, source_target_pairs={{0,16},{8,24},{16,0},{24,8},{1,17},{9,25},{17,1},{25,9},{2,18},{10... | collective-permute-start | bytes 1572872 | tf_op jit(solution)/shard_map/middle_row/ppermute | solution.py:554
  304.5 13.9 %collective-permute-start.27 = (bf16[256,1024]{1,0:T(8,128)(2,1)S(1)}, bf16[256,1024]{1,0:T(8,128)(2,1)S(1)}, u32[]{:S(2)}, u32[]{:S(2)}) collective-permute-start(bf16[256,1024]{1,0:T(8,128)(2,1)S(1)} %collective-permute-done.26.refs_0_.refs_2_), channel_id=1, source_target_pairs={{0,8},{8,0},{16,24},{24,16},{1,9},{9,1},{17,25},{25,17},{2,10},{10... | collective-permute-start | bytes 1572872 | tf_op jit(solution)/shard_map/middle_row/ppermute | solution.py:554
  304.6 13.9 %collective-permute-start.32 = (bf16[1024,256]{1,0:T(8,128)(2,1)S(1)}, bf16[1024,256]{1,0:T(8,128)(2,1)S(1)}, u32[]{:S(2)}, u32[]{:S(2)}) collective-permute-start(bf16[1024,256]{1,0:T(8,128)(2,1)S(1)} %slice.308), channel_id=1, source_target_pairs={{0,2},{1,3},{2,0},{3,1},{4,6},{5,7},{6,4},{7,5},{8,10},{9,11},{10,... | collective-permute-start | bytes 1572872 | tf_op jit(solution)/shard_map/down_plane/ppermute | solution.py:540
  306.2 13.6 %collective-permute-start.33 = (bf16[1024,256]{1,0:T(8,128)(2,1)S(1)}, bf16[1024,256]{1,0:T(8,128)(2,1)S(1)}, u32[]{:S(2)}, u32[]{:S(2)}) collective-permute-start(bf16[1024,256]{1,0:T(8,128)(2,1)S(1)} %slice.309), channel_id=1, source_target_pairs={{0,4},{1,5},{2,6},{3,7},{4,0},{5,1},{6,2},{7,3},{8,12},{9,13},{10,... | collective-permute-start | bytes 1572872 | tf_op jit(solution)/shard_map/down_plane/ppermute | solution.py:540
  341.2 22.4 %collective-permute-start.35 = (bf16[256,1024]{1,0:T(8,128)(2,1)S(1)}, bf16[256,1024]{1,0:T(8,128)(2,1)S(1)}, u32[]{:S(2)}, u32[]{:S(2)}) collective-permute-start(bf16[256,1024]{1,0:T(8,128)(2,1)S(1)} %slice.447), channel_id=1, source_target_pairs={{0,8},{8,0},{16,24},{24,16},{1,9},{9,1},{17,25},{25,17},{2,10},{10... | collective-permute-start | bytes 1572872 | tf_op jit(solution)/shard_map/unit_grad/ppermute | solution.py:554
  350.4 15.2 %collective-permute-start.43 = (bf16[1024,256]{1,0:T(8,128)(2,1)S(1)}, bf16[1024,256]{1,0:T(8,128)(2,1)S(1)}, u32[]{:S(2)}, u32[]{:S(2)}) collective-permute-start(bf16[1024,256]{1,0:T(8,128)(2,1)S(1)} %get-tuple-element.225), channel_id=1, source_target_pairs={{0,4},{1,5},{2,6},{3,7},{4,0},{5,1},{6,2},{7,3},{8,12},{9,13},{10,... | collective-permute-start | bytes 1572872 | tf_op jit(solution)/shard_map/down_grad/ppermute | solution.py:540
  352.3 27.5 %collective-permute-start.38 = (f32[256,1]{0,1:T(1,128)S(1)}, f32[256,1]{0,1:T(1,128)S(1)}, u32[]{:S(2)}, u32[]{:S(2)}) collective-permute-start(f32[256,1]{0,1:T(1,128)S(1)} %bitcast.121), channel_id=1, source_target_pairs={{0,1},{1,0},{2,3},{3,2},{4,5},{5,4},{6,7},{7,6},{8,9},{9,8},{10,11... | collective-permute-start | bytes 3080 | tf_op jit(solution)/shard_map/ppermute | solution.py:537
  352.4 16.1 %collective-permute-start.45 = (bf16[1024,256]{1,0:T(8,128)(2,1)S(1)}, bf16[1024,256]{1,0:T(8,128)(2,1)S(1)}, u32[]{:S(2)}, u32[]{:S(2)}) collective-permute-start(bf16[1024,256]{1,0:T(8,128)(2,1)S(1)} %get-tuple-element.226), channel_id=1, source_target_pairs={{0,2},{1,3},{2,0},{3,1},{4,6},{5,7},{6,4},{7,5},{8,10},{9,11},{10,... | collective-permute-start | bytes 1572872 | tf_op jit(solution)/shard_map/down_grad/ppermute | solution.py:540
  364.8 26.6 %collective-permute-start.41 = (bf16[256,1024]{1,0:T(8,128)(2,1)}, bf16[256,1024]{1,0:T(8,128)(2,1)}, u32[]{:S(2)}, u32[]{:S(2)}) collective-permute-start(bf16[256,1024]{1,0:T(8,128)(2,1)} %fusion.8), channel_id=1, source_target_pairs={{0,16},{8,24},{16,0},{24,8},{1,17},{9,25},{17,1},{25,9},{2,18},{10... | collective-permute-start | bytes 1572872 | tf_op jit(solution)/shard_map/unit_grad/ppermute | solution.py:554
  366.9 37.3 %collective-permute-start.44 = (bf16[2048,256]{1,0:T(8,128)(2,1)}, bf16[2048,256]{1,0:T(8,128)(2,1)}, u32[]{:S(2)}, u32[]{:S(2)}) collective-permute-start(bf16[2048,256]{1,0:T(8,128)(2,1)} %pad_maximum_fusion.3), channel_id=1, source_target_pairs={{0,2},{1,3},{2,0},{3,1},{4,6},{5,7},{6,4},{7,5},{8,10},{9,11},{10,... | collective-permute-start | bytes 3145736 | tf_op jit(solution)/shard_map/down_grad/ppermute | solution.py:540
  369.7 34.5 %collective-permute-start.46 = (bf16[2048,256]{1,0:T(8,128)(2,1)}, bf16[2048,256]{1,0:T(8,128)(2,1)}, u32[]{:S(2)}, u32[]{:S(2)}) collective-permute-start(bf16[2048,256]{1,0:T(8,128)(2,1)} %pad_maximum_fusion.4), channel_id=1, source_target_pairs={{0,4},{1,5},{2,6},{3,7},{4,0},{5,1},{6,2},{7,3},{8,12},{9,13},{10,... | collective-permute-start | bytes 3145736 | tf_op jit(solution)/shard_map/down_grad/ppermute | solution.py:540
  376.0 28.2 %collective-permute-start.36 = (bf16[512,1024]{1,0:T(8,128)(2,1)}, bf16[512,1024]{1,0:T(8,128)(2,1)}, u32[]{:S(2)}, u32[]{:S(2)}) collective-permute-start(bf16[512,1024]{1,0:T(8,128)(2,1)} %get-tuple-element.138), channel_id=1, source_target_pairs={{0,1},{1,0},{2,3},{3,2},{4,5},{5,4},{6,7},{7,6},{8,9},{9,8},{10,11... | collective-permute-start | bytes 3145736 | tf_op jit(solution)/shard_map/feed/ppermute | solution.py:537
  379.9 22.7 %collective-permute-start.40 = (bf16[256,1024]{1,0:T(8,128)(2,1)}, bf16[256,1024]{1,0:T(8,128)(2,1)}, u32[]{:S(2)}, u32[]{:S(2)}) collective-permute-start(bf16[256,1024]{1,0:T(8,128)(2,1)} %slice.446), channel_id=1, source_target_pairs={{0,8},{8,0},{16,24},{24,16},{1,9},{9,1},{17,25},{25,17},{2,10},{10... | collective-permute-start | bytes 1572872 | tf_op jit(solution)/shard_map/unit_grad/ppermute | solution.py:554
  391.4 20.7 %collective-permute-start.37 = (bf16[512,1024]{1,0:T(8,128)(2,1)}, bf16[512,1024]{1,0:T(8,128)(2,1)S(1)}, u32[]{:S(2)}, u32[]{:S(2)}) collective-permute-start(bf16[512,1024]{1,0:T(8,128)(2,1)} %get-tuple-element.141), channel_id=1, source_target_pairs={{0,1},{1,0},{2,3},{3,2},{4,5},{5,4},{6,7},{7,6},{8,9},{9,8},{10,11... | collective-permute-start | bytes 3145736 | tf_op jit(solution)/shard_map/feed/ppermute | solution.py:537
  417.4 28.3 %collective-permute-start.49 = (bf16[256,1024]{1,0:T(8,128)(2,1)}, bf16[256,1024]{1,0:T(8,128)(2,1)S(1)}, u32[]{:S(2)}, u32[]{:S(2)}) collective-permute-start(bf16[256,1024]{1,0:T(8,128)(2,1)} %get-tuple-element.155), channel_id=1, source_target_pairs={{0,6},{1,7},{2,4},{3,5},{4,2},{5,3},{6,0},{7,1},{8,14},{9,15},{10,... | collective-permute-start | bytes 1572872 | tf_op jit(solution)/shard_map/middle_grad/ppermute | solution.py:540
  417.9 27.8 %collective-permute-start.48 = (bf16[256,1024]{1,0:T(8,128)(2,1)}, bf16[256,1024]{1,0:T(8,128)(2,1)S(1)}, u32[]{:S(2)}, u32[]{:S(2)}) collective-permute-start(bf16[256,1024]{1,0:T(8,128)(2,1)} %get-tuple-element.155), channel_id=1, source_target_pairs={{0,4},{1,5},{2,6},{3,7},{4,0},{5,1},{6,2},{7,3},{8,12},{9,13},{10,... | collective-permute-start | bytes 1572872 | tf_op jit(solution)/shard_map/middle_grad/ppermute | solution.py:540
  419.5 26.2 %collective-permute-start.47 = (bf16[256,1024]{1,0:T(8,128)(2,1)}, bf16[256,1024]{1,0:T(8,128)(2,1)S(1)}, u32[]{:S(2)}, u32[]{:S(2)}) collective-permute-start(bf16[256,1024]{1,0:T(8,128)(2,1)} %get-tuple-element.155), channel_id=1, source_target_pairs={{0,2},{1,3},{2,0},{3,1},{4,6},{5,7},{6,4},{7,5},{8,10},{9,11},{10,... | collective-permute-start | bytes 1572872 | tf_op jit(solution)/shard_map/middle_grad/ppermute | solution.py:540
  447.2 13.9 %collective-permute-start.51 = (bf16[1024,256]{1,0:T(8,128)(2,1)}, bf16[1024,256]{1,0:T(8,128)(2,1)}, u32[]{:S(2)}, u32[]{:S(2)}) collective-permute-start(bf16[1024,256]{1,0:T(8,128)(2,1)} %get-tuple-element.224), channel_id=1, source_target_pairs={{0,4},{1,5},{2,6},{3,7},{4,0},{5,1},{6,2},{7,3},{8,12},{9,13},{10,... | collective-permute-start | bytes 1572872 | tf_op jit(solution)/shard_map/gate_grad/ppermute | solution.py:540
  447.6 25.9 %collective-permute-start.50 = (bf16[1024,1024]{1,0:T(8,128)(2,1)S(1)}, bf16[1024,1024]{1,0:T(8,128)(2,1)}, u32[]{:S(2)}, u32[]{:S(2)}) collective-permute-start(bf16[1024,1024]{1,0:T(8,128)(2,1)S(1)} %constant_dynamic-update-slice_fusion.15.own_ref.d_own), channel_id=1, source_target_pairs={{0,1},{1,0},{2,3},{3,2},{4,5},{5,4},{6,7},{7,6},{8,9},{9,8},{10,11... | collective-permute-start | bytes 6291464 | tf_op jit(solution)/shard_map/middle_grad/ppermute | solution.py:537
  447.6 16.3 %collective-permute-start.52 = (bf16[1024,256]{1,0:T(8,128)(2,1)}, bf16[1024,256]{1,0:T(8,128)(2,1)}, u32[]{:S(2)}, u32[]{:S(2)}) collective-permute-start(bf16[1024,256]{1,0:T(8,128)(2,1)} %get-tuple-element.223), channel_id=1, source_target_pairs={{0,2},{1,3},{2,0},{3,1},{4,6},{5,7},{6,4},{7,5},{8,10},{9,11},{10,... | collective-permute-start | bytes 1572872 | tf_op jit(solution)/shard_map/gate_grad/ppermute | solution.py:540
  448.3 45.0 %all-to-all-start.4 = ((bf16[4,512,256]{2,1,0:T(8,128)(2,1)}), bf16[4,512,256]{2,1,0:T(8,128)(2,1)}, u32[]{:S(2)}, u32[]{:S(2)}) async-start(bf16[4,512,256]{2,1,0:T(8,128)(2,1)} %bitcast.98), calls=%async_computation.5 | async-start | bytes 2097152 | tf_op jit(solution)/shard_map/down_grad/all_to_all | solution.py:669
  452.5 197.9 %reduce-scatter.5.cloned.1.call-start = ((), (), s32[]{:S(2)}) async-start(), calls=%async_computation.12 | async-start | bytes 5242880 | tf_op jit(solution)/shard_map/heads_grad/reduce_scatter | solution.py:817
  463.3 25.6 %collective-permute-start.53 = (bf16[2048,256]{1,0:T(8,128)(2,1)}, bf16[2048,256]{1,0:T(8,128)(2,1)}, u32[]{:S(2)}, u32[]{:S(2)}) collective-permute-start(bf16[2048,256]{1,0:T(8,128)(2,1)} %pad_maximum_fusion.5), channel_id=1, source_target_pairs={{0,2},{1,3},{2,0},{3,1},{4,6},{5,7},{6,4},{7,5},{8,10},{9,11},{10,... | collective-permute-start | bytes 3145736 | tf_op jit(solution)/shard_map/gate_grad/ppermute | solution.py:540
  466.2 23.9 %collective-permute-start.54 = (bf16[2048,256]{1,0:T(8,128)(2,1)}, bf16[2048,256]{1,0:T(8,128)(2,1)}, u32[]{:S(2)}, u32[]{:S(2)}) collective-permute-start(bf16[2048,256]{1,0:T(8,128)(2,1)} %pad_maximum_fusion.6), channel_id=1, source_target_pairs={{0,4},{1,5},{2,6},{3,7},{4,0},{5,1},{6,2},{7,3},{8,12},{9,13},{10,... | collective-permute-start | bytes 3145736 | tf_op jit(solution)/shard_map/gate_grad/ppermute | solution.py:540
  512.9 12.9 %collective-permute-start.65 = (bf16[1024,256]{1,0:T(8,128)(2,1)S(1)}, bf16[1024,256]{1,0:T(8,128)(2,1)S(1)}, u32[]{:S(2)}, u32[]{:S(2)}) collective-permute-start(bf16[1024,256]{1,0:T(8,128)(2,1)S(1)} %get-tuple-element.222), channel_id=1, source_target_pairs={{0,2},{1,3},{2,0},{3,1},{4,6},{5,7},{6,4},{7,5},{8,10},{9,11},{10,... | collective-permute-start | bytes 1572872 | tf_op jit(solution)/shard_map/up_grad/ppermute | solution.py:540
  524.7 22.7 %collective-permute-start.64 = (bf16[2048,256]{1,0:T(8,128)(2,1)}, bf16[2048,256]{1,0:T(8,128)(2,1)}, u32[]{:S(2)}, u32[]{:S(2)}) collective-permute-start(bf16[2048,256]{1,0:T(8,128)(2,1)} %pad_maximum_fusion.7), channel_id=1, source_target_pairs={{0,2},{1,3},{2,0},{3,1},{4,6},{5,7},{6,4},{7,5},{8,10},{9,11},{10,... | collective-permute-start | bytes 3145736 | tf_op jit(solution)/shard_map/up_grad/ppermute | solution.py:540
  527.0 21.9 %collective-permute-start.66 = (bf16[2048,256]{1,0:T(8,128)(2,1)}, bf16[2048,256]{1,0:T(8,128)(2,1)}, u32[]{:S(2)}, u32[]{:S(2)}) collective-permute-start(bf16[2048,256]{1,0:T(8,128)(2,1)} %pad_maximum_fusion.8), channel_id=1, source_target_pairs={{0,4},{1,5},{2,6},{3,7},{4,0},{5,1},{6,2},{7,3},{8,12},{9,13},{10,... | collective-permute-start | bytes 3145736 | tf_op jit(solution)/shard_map/up_grad/ppermute | solution.py:540
  528.1 57.3 %all-to-all-start.3 = ((bf16[4,512,256]{2,1,0:T(8,128)(2,1)}), bf16[4,512,256]{2,1,0:T(8,128)(2,1)}, u32[]{:S(2)}, u32[]{:S(2)}) async-start(bf16[4,512,256]{2,1,0:T(8,128)(2,1)} %bitcast.24), calls=%async_computation.4 | async-start | bytes 2097152 | tf_op jit(solution)/shard_map/gate_grad/all_to_all | solution.py:669
  540.4 53.3 %collective-permute-start.55 = (bf16[1024,1024]{1,0:T(8,128)(2,1)}, bf16[1024,1024]{1,0:T(8,128)(2,1)}, u32[]{:S(2)}, u32[]{:S(2)}) collective-permute-start(bf16[1024,1024]{1,0:T(8,128)(2,1)} %get-tuple-element.195), channel_id=1, source_target_pairs={{0,1},{1,0},{2,3},{3,2},{4,5},{5,4},{6,7},{7,6},{8,9},{9,8},{10,11... | collective-permute-start | bytes 6291464 | tf_op jit(solution)/shard_map/first_plane/ppermute | solution.py:537
  558.1 27.3 %collective-permute-start.68 = (f32[2,4,2,256]{3,2,1,0:T(2,128)S(1)}, f32[2,4,2,256]{3,2,1,0:T(2,128)S(1)}, u32[]{:S(2)}, u32[]{:S(2)}) collective-permute-start(f32[2,4,2,256]{3,2,1,0:T(2,128)S(1)} %add.280), channel_id=1, source_target_pairs={{0,2},{1,3},{2,0},{3,1},{4,6},{5,7},{6,4},{7,5},{8,10},{9,11},{10,... | collective-permute-start | bytes 49160 | tf_op jit(solution)/shard_map/gains/ppermute | solution.py:620
  589.6 20.5 %collective-permute-start.71 = (f32[2,512]{1,0:T(2,128)S(1)}, f32[2,512]{1,0:T(2,128)S(1)}, u32[]{:S(2)}, u32[]{:S(2)}) collective-permute-start(f32[2,512]{1,0:T(2,128)S(1)} %bitcast.118), channel_id=1, source_target_pairs={{0,16},{8,24},{16,0},{24,8},{1,17},{9,25},{17,1},{25,9},{2,18},{10... | collective-permute-start | bytes 12296 | tf_op jit(solution)/shard_map/gains/ppermute | solution.py:554
  592.9 17.2 %collective-permute-start.72 = (f32[2,512]{1,0:T(2,128)S(1)}, f32[2,512]{1,0:T(2,128)S(1)}, u32[]{:S(2)}, u32[]{:S(2)}) collective-permute-start(f32[2,512]{1,0:T(2,128)S(1)} %bitcast.119), channel_id=1, source_target_pairs={{0,24},{8,16},{16,8},{24,0},{1,25},{9,17},{17,9},{25,1},{2,26},{10... | collective-permute-start | bytes 12296 | tf_op jit(solution)/shard_map/gains/ppermute | solution.py:554
  599.5 30.6 %collective-permute-start.56 = (bf16[256,1024]{1,0:T(8,128)(2,1)}, bf16[256,1024]{1,0:T(8,128)(2,1)}, u32[]{:S(2)}, u32[]{:S(2)}) collective-permute-start(bf16[256,1024]{1,0:T(8,128)(2,1)} %get-tuple-element.215), channel_id=1, source_target_pairs={{0,2},{1,3},{2,0},{3,1},{4,6},{5,7},{6,4},{7,5},{8,10},{9,11},{10,... | collective-permute-start | bytes 1572872 | tf_op jit(solution)/shard_map/first_plane/ppermute | solution.py:540
  601.0 29.1 %collective-permute-start.57 = (bf16[256,1024]{1,0:T(8,128)(2,1)}, bf16[256,1024]{1,0:T(8,128)(2,1)}, u32[]{:S(2)}, u32[]{:S(2)}) collective-permute-start(bf16[256,1024]{1,0:T(8,128)(2,1)} %get-tuple-element.217), channel_id=1, source_target_pairs={{0,4},{1,5},{2,6},{3,7},{4,0},{5,1},{6,2},{7,3},{8,12},{9,13},{10,... | collective-permute-start | bytes 1572872 | tf_op jit(solution)/shard_map/first_plane/ppermute | solution.py:540
  601.9 28.2 %collective-permute-start.58 = (bf16[256,1024]{1,0:T(8,128)(2,1)}, bf16[256,1024]{1,0:T(8,128)(2,1)}, u32[]{:S(2)}, u32[]{:S(2)}) collective-permute-start(bf16[256,1024]{1,0:T(8,128)(2,1)} %get-tuple-element.216), channel_id=1, source_target_pairs={{0,6},{1,7},{2,4},{3,5},{4,2},{5,3},{6,0},{7,1},{8,14},{9,15},{10,... | collective-permute-start | bytes 1572872 | tf_op jit(solution)/shard_map/first_plane/ppermute | solution.py:540
  603.8 21.1 %all-to-all-start.5 = ((bf16[4,256,256]{2,1,0:T(8,128)(2,1)}), bf16[4,256,256]{2,1,0:T(8,128)(2,1)S(1)}, u32[]{:S(2)}, u32[]{:S(2)}) async-start(bf16[4,256,256]{2,1,0:T(8,128)(2,1)} %pad_maximum_fusion.12), calls=%async_computation.6 | async-start | bytes 1048576 | tf_op jit(solution)/shard_map/block_out/all_to_all | solution.py:601
  625.7 21.9 %all-to-all-start.6 = ((bf16[4,512,256]{2,1,0:T(8,128)(2,1)}), bf16[4,512,256]{2,1,0:T(8,128)(2,1)}, u32[]{:S(2)}, u32[]{:S(2)}) async-start(bf16[4,512,256]{2,1,0:T(8,128)(2,1)} %bitcast.35), calls=%async_computation.8 | async-start | bytes 2097152 | tf_op jit(solution)/shard_map/up_grad/all_to_all | solution.py:669
  (122 other events, 1107.4 us)
Sparse Core Ops, SparseCore 0:
  81.2 35.3 all-gather.2
  155.6 75.5 all-gather.4
  417.5 41.5 reduce-scatter.2
  510.5 92.1 reduce-scatter.4

commit v9 on v8

--- a/solution.py
+++ b/solution.py
@@ -595,23 +595,12 @@
     def spread(a):
         return [a] + [plane_swap(a, step) for step in range(1, places)]
 
-    groups = [[2 * i + k for i in range(places)] for k in range(2)]
-
-    def plane_exchange(a):
-        return lax.all_to_all(
-            a, "col", split_axis=0, concat_axis=0, axis_index_groups=groups, tiled=True
-        )
-
     def to_parts(a):
         return put_feats(
             [token_part(a, 0)] + [plane_swap(token_part(a, s), s) for s in range(1, places)]
         )
 
     def to_home(a):
-        a = jnp.stack([a[:, s * feat : (s + 1) * feat] for s in range(places)])
-        return plane_exchange(a).reshape(tokens, feat)
-
-    def to_home_swaps(a):
         return put_rows([feat_part(a, 0)] + [plane_swap(feat_part(a, s), s) for s in range(1, places)])
 
     def sum_cols(a):
@@ -712,7 +701,7 @@
         feat, starts, x_own, x_other, qkv_list, cosine, front, back
     )
     qkv_full = join_rows([after(a, query) for a in qkv_list])
-    mixed, logs = attend(after(query, gates[1], gates[2]), key, value, start_row)
+    mixed, logs = attend(after(query, gates[1], gates[2], up_whole), key, value, start_row)
     mixed = after(mixed, gates[3])
     with jax.named_scope("grad_row"):
         g_own = lax.all_gather(after(g_part, out_full), "row", axis=0, tiled=True)
@@ -726,8 +715,7 @@
 
     with jax.named_scope("mix_plane"):
         own, other = unfold(feat, "mix", [mixed], [out_full])
-        middle = token_part(x_own, 0).astype(F32) + scatter_parts(after(own, up_whole), other)
-        middle = after(middle, down_whole)
+        middle = token_part(x_own, 0).astype(F32) + scatter_parts(after(own, down_whole), other)
     with jax.named_scope("up_plane"):
         ups = spread_weights(up_whole)
     middle_low = after(middle.astype(BF16), ups[1], ups[2])
@@ -740,6 +728,7 @@
     square = square + core_swap(square)
     scale_mid = lax.rsqrt(square / width + EPS)
 
+    m_list = list(lax.optimization_barrier((*m_list, downs[1], downs[2])))[:rows]
     pairs = [slice(at, at + 2) for at in range(0, rows, 2)]
     found = [activate(feat, m_list[pair], m_others[pair], gates, ups) for pair in pairs]
     hiddens = [f[0] for f in found]
@@ -762,15 +751,8 @@
                     feat, "down_outer", starts, [g_own], [g_other], [after(h, parts[-1]) for h in hiddens], places
                 )
             held = down_parts[:1]
-    kept = []
-
-    def feed_work(*lows):
-        with jax.named_scope("feed"):
-            kept.extend(unfold(feat, "feed", [after(h, *lows)], downs) for h in hiddens)
-        return [own for own, _ in kept]
-
     with jax.named_scope("unit_grad"):
-        unit_grad = reduce_row(parts, lambda *lows: (), feed_work)
+        unit_grad = reduce_row(parts)
     with jax.named_scope("down_grad"):
         down_total = plane_second(plane_first(down_parts))
         down_blocks = give_back(down_total)
@@ -782,6 +764,8 @@
 
     d_low = after(middle_grad.astype(BF16), down_total)
     with jax.named_scope("feed"):
+        pieces = spread(d_low)
+        kept = [unfold(feat, "feed", [after(h, pieces[1])], downs) for h in hiddens]
         shares = jnp.zeros((rows * quarter, half), BF16)
         for pair, (own, other) in zip(pairs, kept):
             low = (own.astype(F32) + core_swap(other).astype(F32)).astype(BF16)
@@ -793,9 +777,8 @@
     gate_parts = outer(feat, "gate_outer", starts, m_list, m_others, [after(a, d_low) for a, _ in scaled_grads], places)
     up_parts = outer(feat, "up_outer", starts, m_list, m_others, [after(a, d_low) for _, a in scaled_grads], places)
     with jax.named_scope("middle_grad"):
-        pieces = spread(d_low)
         d_own = put_rows(
-            [pieces[0]] + [after(a, gate_parts[0], up_parts[0], shares) for a in pieces[1:]]
+            pieces[:2] + [after(a, gate_parts[0], up_parts[0], shares) for a in pieces[2:]]
         )
         d_other = core_swap(d_own)
     mixed_grad = fold(feat, d_own, d_other, out_full)
@@ -819,7 +802,7 @@
         up_total = plane_second(plane_first([after(a, gate_total, heads_part) for a in up_parts]))
         up_blocks = give_back(up_total)
     with jax.named_scope("block_out"):
-        block_out = to_home(after(feed_low, gate_blocks, heads_part))
+        block_out = to_home(after(feed_low, up_total))
     with jax.named_scope("first_plane"):
         first_unit_grad = scatter_parts(
             *unfold(feat, "first_grad", [after(query_grad, heads_part), key_grad, value_grad], [qkv_full])
@@ -829,7 +812,7 @@
     dot_one = jnp.sum(first_unit_grad * unit_first, axis=1, keepdims=True)
     dot_one = dot_one + core_swap(dot_one)
     with jax.named_scope("input_grad"):
-        input_grad = to_home_swaps(
+        input_grad = to_home(
             (middle_grad + scale_first * (first_unit_grad - unit_first * (dot_one / width))).astype(BF16)
         )
 

time: 673 us -> 672 us (level)
  other arithmetic: 64.8 us -> 51.6 us
  waiting for transfers between devices: 269 us -> 280 us
    ppermute x42 -> x45, waiting for transfers between devices: 87.4 us -> 126 us  [plane_swap(): return lax.ppermute(a, 'col', [(i, i ^ 2 * step) for i in range(cols)])]
    all_to_all x1 -> x0, waiting for transfers between devices: 14.8 us -> none  [plane_exchange(): lax.all_to_all(a, 'col', split_axis=0, concat_axis=0, axis_index_groups=g...]
    all_to_all x3, waiting for transfers between devices: 26.3 us -> 14 us  [give_back(): return lax.all_to_all(total, 'row', split_axis=0, concat_axis=0, tiled=True)]
    all_to_all x3, waiting for transfers between devices: 72.2 us -> 60.4 us  [exchange(): got = lax.all_to_all(pieces, 'row', split_axis=0, concat_axis=0, tiled=True)]
    ppermute x42 -> x45, starting transfers between devices: 48.2 us -> 53.3 us  [plane_swap(): return lax.ppermute(a, 'col', [(i, i ^ 2 * step) for i in range(cols)])]
    unnamed x212 -> x219, local copies, waits for them, and re-layouts: 45.5 us -> 43.3 us
  transfers between devices with their start and end apart: 84 -> 86, of which waited for: 33 -> 33; matrix products, arithmetic and copies ran while one was open for 15% -> 14% of each run, Pallas kernels for 17% -> 15%
where the time goes in v9:
time: 672 us; the launch traced here: 664 us
  waiting for transfers between devices  280 us (42%)
  Pallas kernels  130 us (19%)
  starting transfers between devices  100 us (15%)
  local copies, waits for them, and re-layouts  86.2 us (13%)
  other arithmetic  51.6 us (8%)
  between operations  15.9 us (2%)
    ppermute x45, waiting for transfers between devices, plane_swap(): return lax.ppermute(a, 'col', [(i, i ^ 2 * step) for i in range(cols)])  126 us
    ppermute x12, waiting for transfers between devices, row_swap(): return lax.ppermute(a, 'row', [(i, i ^ step) for i in range(rows)])  66.9 us
    all_to_all x3, waiting for transfers between devices, exchange(): got = lax.all_to_all(pieces, 'row', split_axis=0, concat_axis=0, tiled=True)  60.4 us
    ppermute x45, starting transfers between devices, plane_swap(): return lax.ppermute(a, 'col', [(i, i ^ 2 * step) for i in range(cols)])  53.3 us
    unnamed x219, local copies, waits for them, and re-layouts  43.3 us
    pallas_call x4, Pallas kernels, unfold(): pl.pallas_call(functools.partial(unfold_kernel, feat, len(lefts)), grid=(...  24.9 us
    pallas_call x3, Pallas kernels, outer(): pl.pallas_call(functools.partial(outer_kernel, len(owns), count), grid=(h...  18.8 us
    pallas_call x2, Pallas kernels, units_back(): pl.pallas_call(functools.partial(units_back_kernel, feat, parts, count),...  18.6 us
  transfers between devices with their start and end apart: 86, of which 33 were waited for; matrix products, arithmetic and copies ran while one was open for 14% of the time, Pallas kernels for 15%

profile of v9, /device:TPU:0, one launch (start us, length us, event | category | flops | bytes accessed | tf_op | source)
XLA Modules:
  0.0 663.8 jit_solution(228909113215936015)
XLA Ops:
  7.2 3.0 collective-permute-start
  14.8 3.0 collective-permute-start.5
  22.0 3.6 all-to-all-start
  48.8 2.4 collective-permute-start.8
  51.9 22.2 %all-to-all-done = bf16[4,512,256]{2,1,0:T(8,128)(2,1)S(1)} async-done(((bf16[4,512,256]{2,1,0:T(8,128)(2,1)}), bf16[4,512,256]{2,1,0:T(8,128)(2,1)S(1)}, u32[]{:S(2)}, u32[]{:S(2)}) %all-to-all-start) | async-done | bytes 1048608 | tf_op jit(solution)/shard_map/gate_row/all_to_all | solution.py:624
  74.1 4.8 all-to-all-start.1
  86.1 2.1 collective-permute-start.9
  88.2 15.8 %collective-permute-done.11.refs_8_.refs_11_ = bf16[2048,256]{1,0:T(8,128)(2,1)S(1)} collective-permute-done((bf16[2048,256]{1,0:T(8,128)(2,1)S(1)}, bf16[2048,256]{1,0:T(8,128)(2,1)S(1)}, u32[]{:S(2)}, u32[]{:S(2)}) %collective-permute-start.11) | collective-permute-done | bytes 1048608 | tf_op jit(solution)/shard_map/gate_plane/ppermute | solution.py:540
  109.9 22.2 %collective-permute-done.9.refs_3_ = bf16[512,768]{1,0:T(8,128)(2,1)} collective-permute-done((bf16[512,768]{1,0:T(8,128)(2,1)}, bf16[512,768]{1,0:T(8,128)(2,1)}, u32[]{:S(2)}, u32[]{:S(2)}) %collective-permute-start.9) | collective-permute-done | bytes 786464 | tf_op jit(solution)/shard_map/qkv_row/ppermute | solution.py:554
  135.3 6.9 %project.1 = (bf16[1024,256]{1,0:T(8,128)(2,1)S(1)}, bf16[1024,256]{1,0:T(8,128)(2,1)S(1)}, bf16[1024,256]{1,0:T(8,128)(2,1)S(1)}, f32[1024,1]{1,0:T(8,128)S(1)}) custom-call(s32[4]{0:T(128)S(1)} %pad_add_fusion.starts, bf16[1024,1024]{1,0:T(8,128)(2,1)} %constant_dynamic-update-slice_fusion.25.own_ref.x_own, ...), custom_call_target="tpu_custom_call" | custom-call | tf_op jit(solution)/shard_map/project/pallas_call | solution.py:89
  145.4 10.4 %attend.1 = (bf16[1024,256]{1,0:T(8,128)(2,1)}, f32[2,2,1024]{2,1,0:T(2,128)}) custom-call(bf16[1024,256]{1,0:T(8,128)(2,1)} %copy-done.48, bf16[1024,256]{1,0:T(8,128)(2,1)} %copy-done.49, bf16[1024,256]{1,0:T(8,128)(2,1)} %copy-done.50, s32[1,1024]{1,0:T(1,128)} %bitcast.95), custom_call_target="tpu_custom_call" | custom-call | tf_op jit(solution)/shard_map/attend/pallas_call | solution.py:409
  159.0 5.1 mix.1
  164.1 3.8 all-to-all-start.2
  172.0 38.2 %all-to-all-done.2 = bf16[4,512,256]{2,1,0:T(8,128)(2,1)S(1)} async-done(((bf16[4,512,256]{2,1,0:T(8,128)(2,1)}), bf16[4,512,256]{2,1,0:T(8,128)(2,1)S(1)}, u32[]{:S(2)}, u32[]{:S(2)}) %all-to-all-start.2) | async-done | bytes 1048608 | tf_op jit(solution)/shard_map/down_row/all_to_all | solution.py:624
  210.2 3.6 add_convert_fusion.1
  217.5 11.4 %collective-permute-done.15 = bf16[256,1024]{1,0:T(8,128)(2,1)S(1)} collective-permute-done((bf16[256,1024]{1,0:T(8,128)(2,1)S(1)}, bf16[256,1024]{1,0:T(8,128)(2,1)S(1)}, u32[]{:S(2)}, u32[]{:S(2)}) %collective-permute-start.15) | collective-permute-done | bytes 524320 | tf_op jit(solution)/shard_map/mix_plane/ppermute | solution.py:540
  228.9 8.0 %collective-permute-done.16 = bf16[256,1024]{1,0:T(8,128)(2,1)S(1)} collective-permute-done((bf16[256,1024]{1,0:T(8,128)(2,1)S(1)}, bf16[256,1024]{1,0:T(8,128)(2,1)S(1)}, u32[]{:S(2)}, u32[]{:S(2)}) %collective-permute-start.16) | collective-permute-done | bytes 524320 | tf_op jit(solution)/shard_map/mix_plane/ppermute | solution.py:540
  245.5 14.5 %collective-permute-done.21.refs_0_.refs_2_ = bf16[256,1024]{1,0:T(8,128)(2,1)S(1)} collective-permute-done((bf16[256,1024]{1,0:T(8,128)(2,1)S(1)}, bf16[256,1024]{1,0:T(8,128)(2,1)S(1)}, u32[]{:S(2)}, u32[]{:S(2)}) %collective-permute-start.21) | collective-permute-done | bytes 524320 | tf_op jit(solution)/shard_map/middle_row/ppermute | solution.py:554
  260.0 2.0 collective-permute-start.22
  262.1 11.2 %collective-permute-done.28 = bf16[1024,256]{1,0:T(8,128)(2,1)S(1)} collective-permute-done((bf16[1024,256]{1,0:T(8,128)(2,1)S(1)}, bf16[1024,256]{1,0:T(8,128)(2,1)S(1)}, u32[]{:S(2)}, u32[]{:S(2)}) %collective-permute-start.28) | collective-permute-done | bytes 524320 | tf_op jit(solution)/shard_map/up_plane/ppermute | solution.py:540
  276.0 6.8 %collective-permute-done.22.refs_1_.refs_3_ = bf16[256,1024]{1,0:T(8,128)(2,1)S(1)} collective-permute-done((bf16[256,1024]{1,0:T(8,128)(2,1)S(1)}, bf16[256,1024]{1,0:T(8,128)(2,1)S(1)}, u32[]{:S(2)}, u32[]{:S(2)}) %collective-permute-start.22) | collective-permute-done | bytes 524320 | tf_op jit(solution)/shard_map/middle_row/ppermute | solution.py:554
  283.7 6.8 %activate.2 = (bf16[512,1024]{1,0:T(8,128)(2,1)S(1)}, bf16[512,1024]{1,0:T(8,128)(2,1)S(1)}, bf16[512,1024]{1,0:T(8,128)(2,1)S(1)}, f32[512,1]{1,0:T(8,128)S(1)}) custom-call(bf16[256,1024]{1,0:T(8,128)(2,1)S(1)} %convert_element_type.274.refs_0_, bf16[256,1024]{1,0:T(8,128)(2,1)S(1)} %collective-permute-done.20.refs_1_, ...), custom_call_target="tpu_custom_call" | custom-call | tf_op jit(solution)/shard_map/activate/pallas_call | solution.py:168
  301.2 10.5 %collective-permute-done.33 = bf16[1024,256]{1,0:T(8,128)(2,1)S(1)} collective-permute-done((bf16[1024,256]{1,0:T(8,128)(2,1)S(1)}, bf16[1024,256]{1,0:T(8,128)(2,1)S(1)}, u32[]{:S(2)}, u32[]{:S(2)}) %collective-permute-start.33) | collective-permute-done | bytes 524320 | tf_op jit(solution)/shard_map/down_plane/ppermute | solution.py:540
  311.7 2.3 collective-permute-done.34
  314.2 7.7 %activate.3 = (bf16[512,1024]{1,0:T(8,128)(2,1)S(1)}, bf16[512,1024]{1,0:T(8,128)(2,1)S(1)}, bf16[512,1024]{1,0:T(8,128)(2,1)S(1)}, f32[512,1]{1,0:T(8,128)S(1)}) custom-call(bf16[256,1024]{1,0:T(8,128)(2,1)S(1)} %copy-done.25, bf16[256,1024]{1,0:T(8,128)(2,1)S(1)} %copy-done.30, bf16[256,1024]{1,0:T(8,128)(2,1)S(1)} %collective-permute-done.31.refs_2_.refs_6_, ...), custom_call_target="tpu_custom_call" | custom-call | tf_op jit(solution)/shard_map/activate/pallas_call | solution.py:168
  323.3 9.3 %units_back.2 = (bf16[512,1024]{1,0:T(8,128)(2,1)S(1)}, bf16[512,1024]{1,0:T(8,128)(2,1)S(1)}, bf16[512,1024]{1,0:T(8,128)(2,1)S(1)}, bf16[512,1024]{1,0:T(8,128)(2,1)S(1)}) custom-call(s32[2]{0:T(128)S(1)} %pad_add_fusion.2.starts, bf16[1024,1024]{1,0:T(8,128)(2,1)} %all-gather.5.cloned.1.call-done.refs_0_, bf16[1024,1024]{1,0:T(8,128)(2,1)} %copy-done.17, ...), custom_call_target="tpu_custom_call" | custom-call | tf_op jit(solution)/shard_map/unit_grad/units_back/pallas_call | solution.py:233
  332.7 2.6 collective-permute-done.35
  338.0 6.2 down_outer.1
  346.9 9.3 %units_back.3 = (bf16[512,1024]{1,0:T(8,128)(2,1)S(1)}, bf16[512,1024]{1,0:T(8,128)(2,1)S(1)}, bf16[512,1024]{1,0:T(8,128)(2,1)S(1)}, bf16[512,1024]{1,0:T(8,128)(2,1)S(1)}) custom-call(s32[2]{0:T(128)S(1)} %pad_add_fusion.1.starts, bf16[1024,1024]{1,0:T(8,128)(2,1)} %all-gather.5.cloned.1.call-done.refs_0_, bf16[1024,1024]{1,0:T(8,128)(2,1)} %copy-done.17, ...), custom_call_target="tpu_custom_call" | custom-call | tf_op jit(solution)/shard_map/unit_grad/units_back/pallas_call | solution.py:233
  356.4 2.9 collective-permute-done.41
  362.5 2.4 collective-permute-start.39
  368.2 20.0 %collective-permute-done.39 = bf16[256,1024]{1,0:T(8,128)(2,1)S(1)} collective-permute-done((bf16[256,1024]{1,0:T(8,128)(2,1)S(1)}, bf16[256,1024]{1,0:T(8,128)(2,1)S(1)}, u32[]{:S(2)}, u32[]{:S(2)}) %collective-permute-start.39) | collective-permute-done | bytes 524320 | tf_op jit(solution)/shard_map/unit_grad/ppermute | solution.py:554
  391.8 2.4 fusion.33
  395.0 14.3 %collective-permute-done.45 = bf16[256,1024]{1,0:T(8,128)(2,1)} collective-permute-done((bf16[256,1024]{1,0:T(8,128)(2,1)S(1)}, bf16[256,1024]{1,0:T(8,128)(2,1)}, u32[]{:S(2)}, u32[]{:S(2)}) %collective-permute-start.45) | collective-permute-done | bytes 524320 | tf_op jit(solution)/shard_map/feed/ppermute | solution.py:540
  409.4 5.9 feed.2
  415.3 6.1 feed.3
  437.3 6.4 up_outer.1
  447.9 6.2 gate_outer.1
  459.7 4.2 all-to-all-start.3
  466.3 5.3 collective-permute-done.51
  485.0 3.5 fold.1.do_ref
  489.2 11.1 %attend_back.1 = (bf16[1024,256]{1,0:T(8,128)(2,1)}, bf16[1024,256]{1,0:T(8,128)(2,1)}, bf16[1024,256]{1,0:T(8,128)(2,1)}) custom-call(bf16[1024,256]{1,0:T(8,128)(2,1)} %copy-done.48, bf16[1024,256]{1,0:T(8,128)(2,1)} %copy-done.49, bf16[1024,256]{1,0:T(8,128)(2,1)} %copy-done.50, bf16[1024,256]{1,0:T(8,128)(2,1)} %get-tuple-element.119.refs_0_.o_ref.mixed_ref, ...), custom_call_target="tpu_custom_call" | custom-call | tf_op jit(solution)/shard_map/attend_back/pallas_call | solution.py:478
  501.5 3.2 multiply_reduce_fusion.1
  509.9 9.4 %heads_outer.1 = (bf16[2048,1024]{1,0:T(8,128)(2,1)}, f32[2048,1]{1,0:T(8,128)S(1)}) custom-call(bf16[1024,1024]{1,0:T(8,128)(2,1)} %constant_dynamic-update-slice_fusion.25.own_ref.x_own, bf16[1024,1024]{1,0:T(8,128)(2,1)} %collective-permute-done.3.other_ref.x_other, bf16[1024,1024]{1,0:T(8,128)(2,1)S(1)} %constant_dynamic-update-slice_fusion.18.own_ref.d_own, ...), custom_call_target="tpu_custom_call" | custom-call | tf_op jit(solution)/shard_map/heads_outer/pallas_call | solution.py:307
  524.0 8.9 %collective-permute-done.55 = bf16[1024,256]{1,0:T(8,128)(2,1)S(1)} collective-permute-done((bf16[1024,256]{1,0:T(8,128)(2,1)S(1)}, bf16[1024,256]{1,0:T(8,128)(2,1)S(1)}, u32[]{:S(2)}, u32[]{:S(2)}) %collective-permute-start.55) | collective-permute-done | bytes 524320 | tf_op jit(solution)/shard_map/up_grad/ppermute | solution.py:540
  538.7 4.5 all-to-all-start.4
  543.2 7.8 %first_grad.1 = (bf16[1024,1024]{1,0:T(8,128)(2,1)}, bf16[1024,1024]{1,0:T(8,128)(2,1)}) custom-call(bf16[1024,256]{1,0:T(8,128)(2,1)} %get-tuple-element.202.dq_ref.refs_0_, bf16[1024,256]{1,0:T(8,128)(2,1)} %get-tuple-element.186.dk_ref.refs_1_, bf16[1024,256]{1,0:T(8,128)(2,1)} %get-tuple-element.187.dv_ref.refs_2_, bf16[2048,768]{1,0:T(8,128)(2,1)} %copy-done.82), custom_call_target="tpu_custom_call" | custom-call | tf_op jit(solution)/shard_map/first_plane/first_grad/pallas_call | solution.py:121
  551.4 5.7 collective-permute-done.56
  557.2 2.7 collective-permute-done.58
  559.8 3.2 multiply_reduce_fusion
  564.8 3.5 collective-permute-done.71
  570.1 2.0 collective-permute-done.72
  573.5 3.1 collective-permute-start.75
  579.3 2.7 finish.4
  582.1 14.0 %all-to-all-done.4.part_ref = bf16[4,512,256]{2,1,0:T(8,128)(2,1)} async-done(((bf16[4,512,256]{2,1,0:T(8,128)(2,1)}), bf16[4,512,256]{2,1,0:T(8,128)(2,1)}, u32[]{:S(2)}, u32[]{:S(2)}) %all-to-all-start.4) | async-done | bytes 1048608 | tf_op jit(solution)/shard_map/gate_grad/all_to_all | solution.py:658
  596.1 4.3 all-to-all-start.5
  600.3 3.0 finish.5
  603.9 2.6 add_convert_fusion
  615.0 7.9 %collective-permute-done.63 = bf16[256,1024]{1,0:T(8,128)(2,1)} collective-permute-done((bf16[256,1024]{1,0:T(8,128)(2,1)}, bf16[256,1024]{1,0:T(8,128)(2,1)}, u32[]{:S(2)}, u32[]{:S(2)}) %collective-permute-start.63) | collective-permute-done | bytes 524320 | tf_op jit(solution)/shard_map/first_plane/ppermute | solution.py:540
  624.1 11.5 %collective-permute-done.64 = bf16[256,1024]{1,0:T(8,128)(2,1)} collective-permute-done((bf16[256,1024]{1,0:T(8,128)(2,1)}, bf16[256,1024]{1,0:T(8,128)(2,1)}, u32[]{:S(2)}, u32[]{:S(2)}) %collective-permute-start.64) | collective-permute-done | bytes 524320 | tf_op jit(solution)/shard_map/first_plane/ppermute | solution.py:540
  638.8 2.0 fusion.6
  646.6 4.3 collective-permute-done.68
  651.1 3.0 finish.6
  654.0 2.8 finish.7
  (485 shorter events, 189.2 us)
Async XLA Ops:
  7.2 28.4 %collective-permute-start = (bf16[1024,256]{1,0:T(8,128)(2,1)}, bf16[1024,256]{1,0:T(8,128)(2,1)}, u32[]{:S(2)}, u32[]{:S(2)}) collective-permute-start(bf16[1024,256]{1,0:T(8,128)(2,1)} %param.13), channel_id=1, source_target_pairs={{0,2},{1,3},{2,0},{3,1},{4,6},{5,7},{6,4},{7,5},{8,10},{9,11},{10,... | collective-permute-start | bytes 1572872 | tf_op jit(solution)/shard_map/inputs/ppermute | solution.py:540
  10.2 27.3 %collective-permute-start.1 = (bf16[1024,256]{1,0:T(8,128)(2,1)}, bf16[1024,256]{1,0:T(8,128)(2,1)}, u32[]{:S(2)}, u32[]{:S(2)}) collective-permute-start(bf16[1024,256]{1,0:T(8,128)(2,1)} %param.13), channel_id=1, source_target_pairs={{0,4},{1,5},{2,6},{3,7},{4,0},{5,1},{6,2},{7,3},{8,12},{9,13},{10,... | collective-permute-start | bytes 1572872 | tf_op jit(solution)/shard_map/inputs/ppermute | solution.py:540
  11.7 27.6 %collective-permute-start.2 = (bf16[1024,256]{1,0:T(8,128)(2,1)}, bf16[1024,256]{1,0:T(8,128)(2,1)}, u32[]{:S(2)}, u32[]{:S(2)}) collective-permute-start(bf16[1024,256]{1,0:T(8,128)(2,1)} %param.13), channel_id=1, source_target_pairs={{0,6},{1,7},{2,4},{3,5},{4,2},{5,3},{6,0},{7,1},{8,14},{9,15},{10,... | collective-permute-start | bytes 1572872 | tf_op jit(solution)/shard_map/inputs/ppermute | solution.py:540
  14.8 71.3 %collective-permute-start.5 = (bf16[512,768]{1,0:T(8,128)(2,1)}, bf16[512,768]{1,0:T(8,128)(2,1)}, u32[]{:S(2)}, u32[]{:S(2)}) collective-permute-start(bf16[512,768]{1,0:T(8,128)(2,1)} %maximum_maximum_fusion.refs_0_), channel_id=1, source_target_pairs={{0,16},{8,24},{16,0},{24,8},{1,17},{9,25},{17,1},{25,9},{2,18},{10... | collective-permute-start | bytes 2359304 | tf_op jit(solution)/shard_map/qkv_row/ppermute | solution.py:554
  17.8 68.2 %collective-permute-start.4 = (bf16[512,768]{1,0:T(8,128)(2,1)}, bf16[512,768]{1,0:T(8,128)(2,1)}, u32[]{:S(2)}, u32[]{:S(2)}) collective-permute-start(bf16[512,768]{1,0:T(8,128)(2,1)} %maximum_maximum_fusion.refs_0_), channel_id=1, source_target_pairs={{0,8},{8,0},{16,24},{24,16},{1,9},{9,1},{17,25},{25,17},{2,10},{10... | collective-permute-start | bytes 2359304 | tf_op jit(solution)/shard_map/qkv_row/ppermute | solution.py:554
  22.0 52.1 %all-to-all-start = ((bf16[4,512,256]{2,1,0:T(8,128)(2,1)}), bf16[4,512,256]{2,1,0:T(8,128)(2,1)S(1)}, u32[]{:S(2)}, u32[]{:S(2)}) async-start(bf16[4,512,256]{2,1,0:T(8,128)(2,1)} %pad_maximum_fusion.2), calls=%async_computation | async-start | bytes 2097152 | tf_op jit(solution)/shard_map/gate_row/all_to_all | solution.py:624
  41.2 90.9 %collective-permute-start.3 = (bf16[1024,1024]{1,0:T(8,128)(2,1)}, bf16[1024,1024]{1,0:T(8,128)(2,1)}, u32[]{:S(2)}, u32[]{:S(2)}) collective-permute-start(bf16[1024,1024]{1,0:T(8,128)(2,1)} %constant_dynamic-update-slice_fusion.25.own_ref.x_own), channel_id=1, source_target_pairs={{0,1},{1,0},{2,3},{3,2},{4,5},{5,4},{6,7},{7,6},{8,9},{9,8},{10,11... | collective-permute-start | bytes 6291464 | tf_op jit(solution)/shard_map/inputs/ppermute | solution.py:537
  45.4 33.7 %collective-permute-start.7 = (bf16[256,256]{1,0:T(8,128)(2,1)S(1)}, bf16[256,256]{1,0:T(8,128)(2,1)}, u32[]{:S(2)}, u32[]{:S(2)}) collective-permute-start(bf16[256,256]{1,0:T(8,128)(2,1)S(1)} %get-tuple-element.258), channel_id=1, source_target_pairs={{0,4},{1,5},{2,6},{3,7},{4,0},{5,1},{6,2},{7,3},{8,12},{9,13},{10,... | collective-permute-start | bytes 393224 | tf_op jit(solution)/shard_map/grad_plane/ppermute | solution.py:540
  48.8 32.7 %collective-permute-start.8 = (bf16[256,256]{1,0:T(8,128)(2,1)}, bf16[256,256]{1,0:T(8,128)(2,1)}, u32[]{:S(2)}, u32[]{:S(2)}) collective-permute-start(bf16[256,256]{1,0:T(8,128)(2,1)} %get-tuple-element.257), channel_id=1, source_target_pairs={{0,6},{1,7},{2,4},{3,5},{4,2},{5,3},{6,0},{7,1},{8,14},{9,15},{10,... | collective-permute-start | bytes 393224 | tf_op jit(solution)/shard_map/grad_plane/ppermute | solution.py:540
  74.1 71.3 %all-to-all-start.1 = ((bf16[4,512,256]{2,1,0:T(8,128)(2,1)}), bf16[4,512,256]{2,1,0:T(8,128)(2,1)S(1)}, u32[]{:S(2)}, u32[]{:S(2)}) async-start(bf16[4,512,256]{2,1,0:T(8,128)(2,1)} %pad_maximum_fusion), calls=%async_computation.1 | async-start | bytes 2097152 | tf_op jit(solution)/shard_map/up_row/all_to_all | solution.py:624
  78.9 80.1 %all-gather.3.cloned.1.call-start = ((), (), s32[]{:S(2)}) async-start(), calls=%async_computation.8 | async-start | bytes 1310720 | tf_op jit(solution)/shard_map/out_row/all_gather | solution.py:693
  79.2 24.9 %collective-permute-start.11 = (bf16[2048,256]{1,0:T(8,128)(2,1)S(1)}, bf16[2048,256]{1,0:T(8,128)(2,1)S(1)}, u32[]{:S(2)}, u32[]{:S(2)}) collective-permute-start(bf16[2048,256]{1,0:T(8,128)(2,1)S(1)} %bitcast.71), channel_id=1, source_target_pairs={{0,4},{1,5},{2,6},{3,7},{4,0},{5,1},{6,2},{7,3},{8,12},{9,13},{10,... | collective-permute-start | bytes 3145736 | tf_op jit(solution)/shard_map/gate_plane/ppermute | solution.py:540
  81.4 25.0 %collective-permute-start.10 = (bf16[2048,256]{1,0:T(8,128)(2,1)S(1)}, bf16[2048,256]{1,0:T(8,128)(2,1)}, u32[]{:S(2)}, u32[]{:S(2)}) collective-permute-start(bf16[2048,256]{1,0:T(8,128)(2,1)S(1)} %bitcast.72), channel_id=1, source_target_pairs={{0,2},{1,3},{2,0},{3,1},{4,6},{5,7},{6,4},{7,5},{8,10},{9,11},{10,... | collective-permute-start | bytes 3145736 | tf_op jit(solution)/shard_map/gate_plane/ppermute | solution.py:540
  86.1 46.0 %collective-permute-start.9 = (bf16[512,768]{1,0:T(8,128)(2,1)}, bf16[512,768]{1,0:T(8,128)(2,1)}, u32[]{:S(2)}, u32[]{:S(2)}) collective-permute-start(bf16[512,768]{1,0:T(8,128)(2,1)} %collective-permute-done.5.refs_2_), channel_id=1, source_target_pairs={{0,8},{8,0},{16,24},{24,16},{1,9},{9,1},{17,25},{25,17},{2,10},{10... | collective-permute-start | bytes 2359304 | tf_op jit(solution)/shard_map/qkv_row/ppermute | solution.py:554
  104.9 50.9 %collective-permute-start.12 = (bf16[1024,256]{1,0:T(8,128)(2,1)}, bf16[1024,256]{1,0:T(8,128)(2,1)}, u32[]{:S(2)}, u32[]{:S(2)}) collective-permute-start(bf16[1024,256]{1,0:T(8,128)(2,1)} %slice.288), channel_id=1, source_target_pairs={{0,2},{1,3},{2,0},{3,1},{4,6},{5,7},{6,4},{7,5},{8,10},{9,11},{10,... | collective-permute-start | bytes 1572872 | tf_op jit(solution)/shard_map/gate_plane/ppermute | solution.py:540
  108.3 48.6 %collective-permute-start.13 = (bf16[1024,256]{1,0:T(8,128)(2,1)}, bf16[1024,256]{1,0:T(8,128)(2,1)}, u32[]{:S(2)}, u32[]{:S(2)}) collective-permute-start(bf16[1024,256]{1,0:T(8,128)(2,1)} %slice.289), channel_id=1, source_target_pairs={{0,4},{1,5},{2,6},{3,7},{4,0},{5,1},{6,2},{7,3},{8,12},{9,13},{10,... | collective-permute-start | bytes 1572872 | tf_op jit(solution)/shard_map/gate_plane/ppermute | solution.py:540
  164.1 46.1 %collective-permute-start.14 = (bf16[1024,1024]{1,0:T(8,128)(2,1)}, bf16[1024,1024]{1,0:T(8,128)(2,1)}, u32[]{:S(2)}, u32[]{:S(2)}) collective-permute-start(bf16[1024,1024]{1,0:T(8,128)(2,1)} %get-tuple-element.124), channel_id=1, source_target_pairs={{0,1},{1,0},{2,3},{3,2},{4,5},{5,4},{6,7},{7,6},{8,9},{9,8},{10,11... | collective-permute-start | bytes 6291464 | tf_op jit(solution)/shard_map/mix_plane/ppermute | solution.py:537
  164.1 46.1 %all-to-all-start.2 = ((bf16[4,512,256]{2,1,0:T(8,128)(2,1)}), bf16[4,512,256]{2,1,0:T(8,128)(2,1)S(1)}, u32[]{:S(2)}, u32[]{:S(2)}) async-start(bf16[4,512,256]{2,1,0:T(8,128)(2,1)} %pad_maximum_fusion.1), calls=%async_computation.2 | async-start | bytes 2097152 | tf_op jit(solution)/shard_map/down_row/all_to_all | solution.py:624
  167.9 128.3 %all-gather.5.cloned.1.call-start = ((), (), s32[]{:S(2)}) async-start(), calls=%async_computation.9 | async-start | bytes 2621440 | tf_op jit(solution)/shard_map/grad_row/all_gather | solution.py:707
  168.6 443.2 %reduce-scatter.3.cloned.1.call-start = ((), (), s32[]{:S(2)}) async-start(), calls=%async_computation.10 | async-start | bytes 2621440 | tf_op jit(solution)/shard_map/feed/reduce_scatter | solution.py:776
  168.9 69.6 %collective-permute-start.19 = (bf16[2048,256]{1,0:T(8,128)(2,1)S(1)}, bf16[2048,256]{1,0:T(8,128)(2,1)}, u32[]{:S(2)}, u32[]{:S(2)}) collective-permute-start(bf16[2048,256]{1,0:T(8,128)(2,1)S(1)} %bitcast.77), channel_id=1, source_target_pairs={{0,4},{1,5},{2,6},{3,7},{4,0},{5,1},{6,2},{7,3},{8,12},{9,13},{10,... | collective-permute-start | bytes 3145736 | tf_op jit(solution)/shard_map/up_plane/ppermute | solution.py:540
  170.5 68.0 %collective-permute-start.18 = (bf16[2048,256]{1,0:T(8,128)(2,1)S(1)}, bf16[2048,256]{1,0:T(8,128)(2,1)}, u32[]{:S(2)}, u32[]{:S(2)}) collective-permute-start(bf16[2048,256]{1,0:T(8,128)(2,1)S(1)} %bitcast.78), channel_id=1, source_target_pairs={{0,2},{1,3},{2,0},{3,1},{4,6},{5,7},{6,4},{7,5},{8,10},{9,11},{10,... | collective-permute-start | bytes 3145736 | tf_op jit(solution)/shard_map/up_plane/ppermute | solution.py:540
  213.9 14.9 %collective-permute-start.15 = (bf16[256,1024]{1,0:T(8,128)(2,1)S(1)}, bf16[256,1024]{1,0:T(8,128)(2,1)S(1)}, u32[]{:S(2)}, u32[]{:S(2)}) collective-permute-start(bf16[256,1024]{1,0:T(8,128)(2,1)S(1)} %get-tuple-element.222), channel_id=1, source_target_pairs={{0,2},{1,3},{2,0},{3,1},{4,6},{5,7},{6,4},{7,5},{8,10},{9,11},{10,... | collective-permute-start | bytes 1572872 | tf_op jit(solution)/shard_map/mix_plane/ppermute | solution.py:540
  215.5 21.4 %collective-permute-start.16 = (bf16[256,1024]{1,0:T(8,128)(2,1)S(1)}, bf16[256,1024]{1,0:T(8,128)(2,1)S(1)}, u32[]{:S(2)}, u32[]{:S(2)}) collective-permute-start(bf16[256,1024]{1,0:T(8,128)(2,1)S(1)} %get-tuple-element.224), channel_id=1, source_target_pairs={{0,4},{1,5},{2,6},{3,7},{4,0},{5,1},{6,2},{7,3},{8,12},{9,13},{10,... | collective-permute-start | bytes 1572872 | tf_op jit(solution)/shard_map/mix_plane/ppermute | solution.py:540
  217.0 19.9 %collective-permute-start.17 = (bf16[256,1024]{1,0:T(8,128)(2,1)S(1)}, bf16[256,1024]{1,0:T(8,128)(2,1)S(1)}, u32[]{:S(2)}, u32[]{:S(2)}) collective-permute-start(bf16[256,1024]{1,0:T(8,128)(2,1)S(1)} %get-tuple-element.223), channel_id=1, source_target_pairs={{0,6},{1,7},{2,4},{3,5},{4,2},{5,3},{6,0},{7,1},{8,14},{9,15},{10,... | collective-permute-start | bytes 1572872 | tf_op jit(solution)/shard_map/mix_plane/ppermute | solution.py:540
  238.5 21.5 %collective-permute-start.21 = (bf16[256,1024]{1,0:T(8,128)(2,1)S(1)}, bf16[256,1024]{1,0:T(8,128)(2,1)S(1)}, u32[]{:S(2)}, u32[]{:S(2)}) collective-permute-start(bf16[256,1024]{1,0:T(8,128)(2,1)S(1)} %convert_element_type.274.refs_0_), channel_id=1, source_target_pairs={{0,16},{8,24},{16,0},{24,8},{1,17},{9,25},{17,1},{25,9},{2,18},{10... | collective-permute-start | bytes 1572872 | tf_op jit(solution)/shard_map/middle_row/ppermute | solution.py:554
  240.2 19.8 %collective-permute-start.27 = (bf16[1024,256]{1,0:T(8,128)(2,1)S(1)}, bf16[1024,256]{1,0:T(8,128)(2,1)S(1)}, u32[]{:S(2)}, u32[]{:S(2)}) collective-permute-start(bf16[1024,256]{1,0:T(8,128)(2,1)S(1)} %slice.290), channel_id=1, source_target_pairs={{0,2},{1,3},{2,0},{3,1},{4,6},{5,7},{6,4},{7,5},{8,10},{9,11},{10,... | collective-permute-start | bytes 1572872 | tf_op jit(solution)/shard_map/up_plane/ppermute | solution.py:540
  241.5 33.4 %collective-permute-start.24 = (bf16[2048,256]{1,0:T(8,128)(2,1)S(1)}, bf16[2048,256]{1,0:T(8,128)(2,1)S(1)}, u32[]{:S(2)}, u32[]{:S(2)}) collective-permute-start(bf16[2048,256]{1,0:T(8,128)(2,1)S(1)} %bitcast.83), channel_id=1, source_target_pairs={{0,4},{1,5},{2,6},{3,7},{4,0},{5,1},{6,2},{7,3},{8,12},{9,13},{10,... | collective-permute-start | bytes 3145736 | tf_op jit(solution)/shard_map/down_plane/ppermute | solution.py:540
  242.4 32.6 %collective-permute-start.23 = (bf16[2048,256]{1,0:T(8,128)(2,1)S(1)}, bf16[2048,256]{1,0:T(8,128)(2,1)S(1)}, u32[]{:S(2)}, u32[]{:S(2)}) collective-permute-start(bf16[2048,256]{1,0:T(8,128)(2,1)S(1)} %bitcast.84), channel_id=1, source_target_pairs={{0,2},{1,3},{2,0},{3,1},{4,6},{5,7},{6,4},{7,5},{8,10},{9,11},{10,... | collective-permute-start | bytes 3145736 | tf_op jit(solution)/shard_map/down_plane/ppermute | solution.py:540
  244.9 28.3 %collective-permute-start.28 = (bf16[1024,256]{1,0:T(8,128)(2,1)S(1)}, bf16[1024,256]{1,0:T(8,128)(2,1)S(1)}, u32[]{:S(2)}, u32[]{:S(2)}) collective-permute-start(bf16[1024,256]{1,0:T(8,128)(2,1)S(1)} %slice.291), channel_id=1, source_target_pairs={{0,4},{1,5},{2,6},{3,7},{4,0},{5,1},{6,2},{7,3},{8,12},{9,13},{10,... | collective-permute-start | bytes 1572872 | tf_op jit(solution)/shard_map/up_plane/ppermute | solution.py:540
  260.0 14.9 %collective-permute-start.20 = (bf16[256,1024]{1,0:T(8,128)(2,1)S(1)}, bf16[256,1024]{1,0:T(8,128)(2,1)S(1)}, u32[]{:S(2)}, u32[]{:S(2)}) collective-permute-start(bf16[256,1024]{1,0:T(8,128)(2,1)S(1)} %convert_element_type.274.refs_0_), channel_id=1, source_target_pairs={{0,8},{8,0},{16,24},{24,16},{1,9},{9,1},{17,25},{25,17},{2,10},{10... | collective-permute-start | bytes 1572872 | tf_op jit(solution)/shard_map/middle_row/ppermute | solution.py:554
  260.0 22.8 %collective-permute-start.22 = (bf16[256,1024]{1,0:T(8,128)(2,1)S(1)}, bf16[256,1024]{1,0:T(8,128)(2,1)S(1)}, u32[]{:S(2)}, u32[]{:S(2)}) collective-permute-start(bf16[256,1024]{1,0:T(8,128)(2,1)S(1)} %collective-permute-done.21.refs_0_.refs_2_), channel_id=1, source_target_pairs={{0,8},{8,0},{16,24},{24,16},{1,9},{9,1},{17,25},{25,17},{2,10},{10... | collective-permute-start | bytes 1572872 | tf_op jit(solution)/shard_map/middle_row/ppermute | solution.py:554
  296.1 25.8 %collective-permute-start.30 = (bf16[1024,1024]{1,0:T(8,128)(2,1)}, bf16[1024,1024]{1,0:T(8,128)(2,1)S(1)}, u32[]{:S(2)}, u32[]{:S(2)}) collective-permute-start(bf16[1024,1024]{1,0:T(8,128)(2,1)} %all-gather.5.cloned.1.call-done.refs_0_), channel_id=1, source_target_pairs={{0,1},{1,0},{2,3},{3,2},{4,5},{5,4},{6,7},{7,6},{8,9},{9,8},{10,11... | collective-permute-start | bytes 6291464 | tf_op jit(solution)/shard_map/grad_row/ppermute | solution.py:537
  297.4 14.2 %collective-permute-start.33 = (bf16[1024,256]{1,0:T(8,128)(2,1)S(1)}, bf16[1024,256]{1,0:T(8,128)(2,1)S(1)}, u32[]{:S(2)}, u32[]{:S(2)}) collective-permute-start(bf16[1024,256]{1,0:T(8,128)(2,1)S(1)} %slice.292), channel_id=1, source_target_pairs={{0,2},{1,3},{2,0},{3,1},{4,6},{5,7},{6,4},{7,5},{8,10},{9,11},{10,... | collective-permute-start | bytes 1572872 | tf_op jit(solution)/shard_map/down_plane/ppermute | solution.py:540
  345.2 14.0 %collective-permute-start.41 = (bf16[1024,256]{1,0:T(8,128)(2,1)S(1)}, bf16[1024,256]{1,0:T(8,128)(2,1)S(1)}, u32[]{:S(2)}, u32[]{:S(2)}) collective-permute-start(bf16[1024,256]{1,0:T(8,128)(2,1)S(1)} %get-tuple-element.229), channel_id=1, source_target_pairs={{0,4},{1,5},{2,6},{3,7},{4,0},{5,1},{6,2},{7,3},{8,12},{9,13},{10,... | collective-permute-start | bytes 1572872 | tf_op jit(solution)/shard_map/down_grad/ppermute | solution.py:540
  345.8 14.3 %collective-permute-start.43 = (bf16[1024,256]{1,0:T(8,128)(2,1)S(1)}, bf16[1024,256]{1,0:T(8,128)(2,1)S(1)}, u32[]{:S(2)}, u32[]{:S(2)}) collective-permute-start(bf16[1024,256]{1,0:T(8,128)(2,1)S(1)} %get-tuple-element.230), channel_id=1, source_target_pairs={{0,2},{1,3},{2,0},{3,1},{4,6},{5,7},{6,4},{7,5},{8,10},{9,11},{10,... | collective-permute-start | bytes 1572872 | tf_op jit(solution)/shard_map/down_grad/ppermute | solution.py:540
  346.3 15.0 %collective-permute-start.38 = (bf16[256,1024]{1,0:T(8,128)(2,1)}, bf16[256,1024]{1,0:T(8,128)(2,1)}, u32[]{:S(2)}, u32[]{:S(2)}) collective-permute-start(bf16[256,1024]{1,0:T(8,128)(2,1)} %slice.427), channel_id=1, source_target_pairs={{0,8},{8,0},{16,24},{24,16},{1,9},{9,1},{17,25},{25,17},{2,10},{10... | collective-permute-start | bytes 1572872 | tf_op jit(solution)/shard_map/unit_grad/ppermute | solution.py:554
  359.5 30.8 %collective-permute-start.42 = (bf16[2048,256]{1,0:T(8,128)(2,1)S(1)}, bf16[2048,256]{1,0:T(8,128)(2,1)S(1)}, u32[]{:S(2)}, u32[]{:S(2)}) collective-permute-start(bf16[2048,256]{1,0:T(8,128)(2,1)S(1)} %pad_maximum_fusion.3), channel_id=1, source_target_pairs={{0,2},{1,3},{2,0},{3,1},{4,6},{5,7},{6,4},{7,5},{8,10},{9,11},{10,... | collective-permute-start | bytes 3145736 | tf_op jit(solution)/shard_map/down_grad/ppermute | solution.py:540
  360.3 29.9 %collective-permute-start.44 = (bf16[2048,256]{1,0:T(8,128)(2,1)S(1)}, bf16[2048,256]{1,0:T(8,128)(2,1)S(1)}, u32[]{:S(2)}, u32[]{:S(2)}) collective-permute-start(bf16[2048,256]{1,0:T(8,128)(2,1)S(1)} %pad_maximum_fusion.4), channel_id=1, source_target_pairs={{0,4},{1,5},{2,6},{3,7},{4,0},{5,1},{6,2},{7,3},{8,12},{9,13},{10,... | collective-permute-start | bytes 3145736 | tf_op jit(solution)/shard_map/down_grad/ppermute | solution.py:540
  362.5 25.7 %collective-permute-start.39 = (bf16[256,1024]{1,0:T(8,128)(2,1)S(1)}, bf16[256,1024]{1,0:T(8,128)(2,1)S(1)}, u32[]{:S(2)}, u32[]{:S(2)}) collective-permute-start(bf16[256,1024]{1,0:T(8,128)(2,1)S(1)} %fusion.7), channel_id=1, source_target_pairs={{0,16},{8,24},{16,0},{24,8},{1,17},{9,25},{17,1},{25,9},{2,18},{10... | collective-permute-start | bytes 1572872 | tf_op jit(solution)/shard_map/unit_grad/ppermute | solution.py:554
  365.4 24.4 %collective-permute-start.37 = (bf16[256,1024]{1,0:T(8,128)(2,1)S(1)}, bf16[256,1024]{1,0:T(8,128)(2,1)S(1)}, u32[]{:S(2)}, u32[]{:S(2)}) collective-permute-start(bf16[256,1024]{1,0:T(8,128)(2,1)S(1)} %slice.426), channel_id=1, source_target_pairs={{0,8},{8,0},{16,24},{24,16},{1,9},{9,1},{17,25},{25,17},{2,10},{10... | collective-permute-start | bytes 1572872 | tf_op jit(solution)/shard_map/unit_grad/ppermute | solution.py:554
  394.9 14.4 %collective-permute-start.45 = (bf16[256,1024]{1,0:T(8,128)(2,1)S(1)}, bf16[256,1024]{1,0:T(8,128)(2,1)}, u32[]{:S(2)}, u32[]{:S(2)}) collective-permute-start(bf16[256,1024]{1,0:T(8,128)(2,1)S(1)} %get-tuple-element.152), channel_id=1, source_target_pairs={{0,2},{1,3},{2,0},{3,1},{4,6},{5,7},{6,4},{7,5},{8,10},{9,11},{10,... | collective-permute-start | bytes 1572872 | tf_op jit(solution)/shard_map/feed/ppermute | solution.py:540
  428.8 27.9 %collective-permute-start.49 = (bf16[256,1024]{1,0:T(8,128)(2,1)}, bf16[256,1024]{1,0:T(8,128)(2,1)S(1)}, u32[]{:S(2)}, u32[]{:S(2)}) collective-permute-start(bf16[256,1024]{1,0:T(8,128)(2,1)} %copy-done.88), channel_id=1, source_target_pairs={{0,6},{1,7},{2,4},{3,5},{4,2},{5,3},{6,0},{7,1},{8,14},{9,15},{10,... | collective-permute-start | bytes 1572872 | tf_op jit(solution)/shard_map/feed/ppermute | solution.py:540
  429.3 27.5 %collective-permute-start.48 = (bf16[256,1024]{1,0:T(8,128)(2,1)}, bf16[256,1024]{1,0:T(8,128)(2,1)S(1)}, u32[]{:S(2)}, u32[]{:S(2)}) collective-permute-start(bf16[256,1024]{1,0:T(8,128)(2,1)} %copy-done.88), channel_id=1, source_target_pairs={{0,4},{1,5},{2,6},{3,7},{4,0},{5,1},{6,2},{7,3},{8,12},{9,13},{10,... | collective-permute-start | bytes 1572872 | tf_op jit(solution)/shard_map/feed/ppermute | solution.py:540
  458.6 26.3 %collective-permute-start.50 = (bf16[1024,1024]{1,0:T(8,128)(2,1)S(1)}, bf16[1024,1024]{1,0:T(8,128)(2,1)}, u32[]{:S(2)}, u32[]{:S(2)}) collective-permute-start(bf16[1024,1024]{1,0:T(8,128)(2,1)S(1)} %constant_dynamic-update-slice_fusion.18.own_ref.d_own), channel_id=1, source_target_pairs={{0,1},{1,0},{2,3},{3,2},{4,5},{5,4},{6,7},{7,6},{8,9},{9,8},{10,11... | collective-permute-start | bytes 6291464 | tf_op jit(solution)/shard_map/middle_grad/ppermute | solution.py:537
  458.6 16.9 %collective-permute-start.52 = (bf16[1024,256]{1,0:T(8,128)(2,1)}, bf16[1024,256]{1,0:T(8,128)(2,1)}, u32[]{:S(2)}, u32[]{:S(2)}) collective-permute-start(bf16[1024,256]{1,0:T(8,128)(2,1)} %get-tuple-element.227), channel_id=1, source_target_pairs={{0,2},{1,3},{2,0},{3,1},{4,6},{5,7},{6,4},{7,5},{8,10},{9,11},{10,... | collective-permute-start | bytes 1572872 | tf_op jit(solution)/shard_map/gate_grad/ppermute | solution.py:540
  459.7 44.9 %all-to-all-start.3 = ((bf16[4,512,256]{2,1,0:T(8,128)(2,1)}), bf16[4,512,256]{2,1,0:T(8,128)(2,1)}, u32[]{:S(2)}, u32[]{:S(2)}) async-start(bf16[4,512,256]{2,1,0:T(8,128)(2,1)} %bitcast.89), calls=%async_computation.4 | async-start | bytes 2097152 | tf_op jit(solution)/shard_map/down_grad/all_to_all | solution.py:658
  464.0 190.0 %reduce-scatter.5.cloned.1.call-start = ((), (), s32[]{:S(2)}) async-start(), calls=%async_computation.11 | async-start | bytes 5242880 | tf_op jit(solution)/shard_map/heads_grad/reduce_scatter | solution.py:800
  473.8 26.6 %collective-permute-start.53 = (bf16[2048,256]{1,0:T(8,128)(2,1)}, bf16[2048,256]{1,0:T(8,128)(2,1)}, u32[]{:S(2)}, u32[]{:S(2)}) collective-permute-start(bf16[2048,256]{1,0:T(8,128)(2,1)} %pad_maximum_fusion.5), channel_id=1, source_target_pairs={{0,2},{1,3},{2,0},{3,1},{4,6},{5,7},{6,4},{7,5},{8,10},{9,11},{10,... | collective-permute-start | bytes 3145736 | tf_op jit(solution)/shard_map/gate_grad/ppermute | solution.py:540
  477.8 23.7 %collective-permute-start.54 = (bf16[2048,256]{1,0:T(8,128)(2,1)}, bf16[2048,256]{1,0:T(8,128)(2,1)}, u32[]{:S(2)}, u32[]{:S(2)}) collective-permute-start(bf16[2048,256]{1,0:T(8,128)(2,1)} %pad_maximum_fusion.6), channel_id=1, source_target_pairs={{0,4},{1,5},{2,6},{3,7},{4,0},{5,1},{6,2},{7,3},{8,12},{9,13},{10,... | collective-permute-start | bytes 3145736 | tf_op jit(solution)/shard_map/gate_grad/ppermute | solution.py:540
  534.1 23.1 %collective-permute-start.56 = (bf16[2048,256]{1,0:T(8,128)(2,1)}, bf16[2048,256]{1,0:T(8,128)(2,1)}, u32[]{:S(2)}, u32[]{:S(2)}) collective-permute-start(bf16[2048,256]{1,0:T(8,128)(2,1)} %pad_maximum_fusion.7), channel_id=1, source_target_pairs={{0,2},{1,3},{2,0},{3,1},{4,6},{5,7},{6,4},{7,5},{8,10},{9,11},{10,... | collective-permute-start | bytes 3145736 | tf_op jit(solution)/shard_map/up_grad/ppermute | solution.py:540
  536.9 22.9 %collective-permute-start.58 = (bf16[2048,256]{1,0:T(8,128)(2,1)}, bf16[2048,256]{1,0:T(8,128)(2,1)}, u32[]{:S(2)}, u32[]{:S(2)}) collective-permute-start(bf16[2048,256]{1,0:T(8,128)(2,1)} %pad_maximum_fusion.8), channel_id=1, source_target_pairs={{0,4},{1,5},{2,6},{3,7},{4,0},{5,1},{6,2},{7,3},{8,12},{9,13},{10,... | collective-permute-start | bytes 3145736 | tf_op jit(solution)/shard_map/up_grad/ppermute | solution.py:540
  538.7 57.4 %all-to-all-start.4 = ((bf16[4,512,256]{2,1,0:T(8,128)(2,1)}), bf16[4,512,256]{2,1,0:T(8,128)(2,1)}, u32[]{:S(2)}, u32[]{:S(2)}) async-start(bf16[4,512,256]{2,1,0:T(8,128)(2,1)} %bitcast.29), calls=%async_computation.6 | async-start | bytes 2097152 | tf_op jit(solution)/shard_map/gate_grad/all_to_all | solution.py:658
  551.1 52.9 %collective-permute-start.62 = (bf16[1024,1024]{1,0:T(8,128)(2,1)}, bf16[1024,1024]{1,0:T(8,128)(2,1)}, u32[]{:S(2)}, u32[]{:S(2)}) collective-permute-start(bf16[1024,1024]{1,0:T(8,128)(2,1)} %get-tuple-element.204), channel_id=1, source_target_pairs={{0,1},{1,0},{2,3},{3,2},{4,5},{5,4},{6,7},{7,6},{8,9},{9,8},{10,11... | collective-permute-start | bytes 6291464 | tf_op jit(solution)/shard_map/first_plane/ppermute | solution.py:537
  572.2 31.2 %collective-permute-start.73 = (f32[2,512]{1,0:T(2,128)S(1)}, f32[2,512]{1,0:T(2,128)S(1)}, u32[]{:S(2)}, u32[]{:S(2)}) collective-permute-start(f32[2,512]{1,0:T(2,128)S(1)} %bitcast.110), channel_id=1, source_target_pairs={{0,8},{8,0},{16,24},{24,16},{1,9},{9,1},{17,25},{25,17},{2,10},{10... | collective-permute-start | bytes 12296 | tf_op jit(solution)/shard_map/gains/ppermute | solution.py:554
  572.2 31.1 %collective-permute-start.74 = (f32[2,512]{1,0:T(2,128)S(1)}, f32[2,512]{1,0:T(2,128)S(1)}, u32[]{:S(2)}, u32[]{:S(2)}) collective-permute-start(f32[2,512]{1,0:T(2,128)S(1)} %bitcast.111), channel_id=1, source_target_pairs={{0,16},{8,24},{16,0},{24,8},{1,17},{9,25},{17,1},{25,9},{2,18},{10... | collective-permute-start | bytes 12296 | tf_op jit(solution)/shard_map/gains/ppermute | solution.py:554
  573.5 29.8 %collective-permute-start.75 = (f32[2,512]{1,0:T(2,128)S(1)}, f32[2,512]{1,0:T(2,128)S(1)}, u32[]{:S(2)}, u32[]{:S(2)}) collective-permute-start(f32[2,512]{1,0:T(2,128)S(1)} %bitcast.112), channel_id=1, source_target_pairs={{0,24},{8,16},{16,8},{24,0},{1,25},{9,17},{17,9},{25,1},{2,26},{10... | collective-permute-start | bytes 12296 | tf_op jit(solution)/shard_map/gains/ppermute | solution.py:554
  596.1 55.0 %all-to-all-start.5 = ((bf16[4,512,256]{2,1,0:T(8,128)(2,1)}), bf16[4,512,256]{2,1,0:T(8,128)(2,1)}, u32[]{:S(2)}, u32[]{:S(2)}) async-start(bf16[4,512,256]{2,1,0:T(8,128)(2,1)} %bitcast.30), calls=%async_computation.7 | async-start | bytes 2097152 | tf_op jit(solution)/shard_map/up_grad/all_to_all | solution.py:658
  607.7 15.2 %collective-permute-start.63 = (bf16[256,1024]{1,0:T(8,128)(2,1)}, bf16[256,1024]{1,0:T(8,128)(2,1)}, u32[]{:S(2)}, u32[]{:S(2)}) collective-permute-start(bf16[256,1024]{1,0:T(8,128)(2,1)} %get-tuple-element.219), channel_id=1, source_target_pairs={{0,2},{1,3},{2,0},{3,1},{4,6},{5,7},{6,4},{7,5},{8,10},{9,11},{10,... | collective-permute-start | bytes 1572872 | tf_op jit(solution)/shard_map/first_plane/ppermute | solution.py:540
  608.6 27.0 %collective-permute-start.64 = (bf16[256,1024]{1,0:T(8,128)(2,1)}, bf16[256,1024]{1,0:T(8,128)(2,1)}, u32[]{:S(2)}, u32[]{:S(2)}) collective-permute-start(bf16[256,1024]{1,0:T(8,128)(2,1)} %get-tuple-element.221), channel_id=1, source_target_pairs={{0,4},{1,5},{2,6},{3,7},{4,0},{5,1},{6,2},{7,3},{8,12},{9,13},{10,... | collective-permute-start | bytes 1572872 | tf_op jit(solution)/shard_map/first_plane/ppermute | solution.py:540
  609.5 26.2 %collective-permute-start.65 = (bf16[256,1024]{1,0:T(8,128)(2,1)}, bf16[256,1024]{1,0:T(8,128)(2,1)}, u32[]{:S(2)}, u32[]{:S(2)}) collective-permute-start(bf16[256,1024]{1,0:T(8,128)(2,1)} %get-tuple-element.220), channel_id=1, source_target_pairs={{0,6},{1,7},{2,4},{3,5},{4,2},{5,3},{6,0},{7,1},{8,14},{9,15},{10,... | collective-permute-start | bytes 1572872 | tf_op jit(solution)/shard_map/first_plane/ppermute | solution.py:540
  613.1 24.6 %collective-permute-start.59 = (bf16[256,256]{1,0:T(8,128)(2,1)S(1)}, bf16[256,256]{1,0:T(8,128)(2,1)S(1)}, u32[]{:S(2)}, u32[]{:S(2)}) collective-permute-start(bf16[256,256]{1,0:T(8,128)(2,1)S(1)} %get-tuple-element.255), channel_id=1, source_target_pairs={{0,2},{1,3},{2,0},{3,1},{4,6},{5,7},{6,4},{7,5},{8,10},{9,11},{10,... | collective-permute-start | bytes 393224 | tf_op jit(solution)/shard_map/block_out/ppermute | solution.py:540
  614.1 28.7 %collective-permute-start.60 = (bf16[256,256]{1,0:T(8,128)(2,1)S(1)}, bf16[256,256]{1,0:T(8,128)(2,1)S(1)}, u32[]{:S(2)}, u32[]{:S(2)}) collective-permute-start(bf16[256,256]{1,0:T(8,128)(2,1)S(1)} %get-tuple-element.254), channel_id=1, source_target_pairs={{0,4},{1,5},{2,6},{3,7},{4,0},{5,1},{6,2},{7,3},{8,12},{9,13},{10,... | collective-permute-start | bytes 393224 | tf_op jit(solution)/shard_map/block_out/ppermute | solution.py:540
  622.9 20.0 %collective-permute-start.61 = (bf16[256,256]{1,0:T(8,128)(2,1)S(1)}, bf16[256,256]{1,0:T(8,128)(2,1)S(1)}, u32[]{:S(2)}, u32[]{:S(2)}) collective-permute-start(bf16[256,256]{1,0:T(8,128)(2,1)S(1)} %get-tuple-element.253), channel_id=1, source_target_pairs={{0,6},{1,7},{2,4},{3,5},{4,2},{5,3},{6,0},{7,1},{8,14},{9,15},{10,... | collective-permute-start | bytes 393224 | tf_op jit(solution)/shard_map/block_out/ppermute | solution.py:540
  (128 other events, 1168.3 us)
Sparse Core Ops, SparseCore 0:
  86.2 41.5 all-gather.2
  170.3 58.2 all-gather.4
  428.9 42.5 reduce-scatter.2
  520.5 101.9 reduce-scatter.4

commit v10 on v9

--- a/solution.py
+++ b/solution.py
@@ -17,6 +17,10 @@
 BF16 = jnp.bfloat16
 F32 = jnp.float32
 VMEM_BYTES = 56 * 1024 * 1024
+
+
+def lasts(microseconds):
+    return pl.CostEstimate(flops=int(microseconds * 1.15e9), bytes_accessed=1, transcendentals=0)
 
 
 def nn(left, right):
@@ -95,6 +99,7 @@
         out_specs=[row_spec(block, result)] * 3 + [row_spec(block, scale)],
         out_shape=[result] * 3 + [scale],
         compiler_params=pltpu.CompilerParams(vmem_limit_bytes=40 * 1024 * 1024),
+        cost_estimate=lasts(7),
         name="project",
     )(starts, own, other, *weights, cosine, front, back)
 
@@ -125,6 +130,7 @@
         out_specs=[row_spec(block, result)] * 2,
         out_shape=[result] * 2,
         compiler_params=pltpu.CompilerParams(vmem_limit_bytes=VMEM_BYTES),
+        cost_estimate=lasts(6),
         name=name,
     )(*lefts, *weights)
 
@@ -175,6 +181,7 @@
             pltpu.SemaphoreType.DMA((len(weights),)),
         ],
         compiler_params=pltpu.CompilerParams(vmem_limit_bytes=36 * 1024 * 1024),
+        cost_estimate=lasts(7.5),
         name="activate",
     )(*m_owns, *m_others, *weights)
 
@@ -245,6 +252,7 @@
             pltpu.SemaphoreType.DMA((2, parts)),
         ],
         compiler_params=pltpu.CompilerParams(vmem_limit_bytes=40 * 1024 * 1024),
+        cost_estimate=lasts(9.3),
         name="units_back",
     )(starts, g_own, g_other, gate, up, scale, *weights)
 
@@ -281,6 +289,7 @@
         out_specs=[pl.BlockSpec((2 * feat, part), lambda i: (i, 0))] * count,
         out_shape=[jax.ShapeDtypeStruct((2 * half, part), BF16)] * count,
         compiler_params=pltpu.CompilerParams(vmem_limit_bytes=40 * 1024 * 1024),
+        cost_estimate=lasts(6.3),
         name=name,
     )(starts, *owns, *others, *rights)
 
@@ -316,6 +325,7 @@
             jax.ShapeDtypeStruct((2 * half, 1), F32),
         ],
         compiler_params=pltpu.CompilerParams(vmem_limit_bytes=40 * 1024 * 1024),
+        cost_estimate=lasts(9.4),
         name="heads_outer",
     )(x_own, x_other, d_own, d_other, dq, dk, dv, mixed, scale, weight)
 
@@ -344,6 +354,7 @@
         out_specs=[vmem] * count,
         out_shape=[result] * count,
         compiler_params=pltpu.CompilerParams(vmem_limit_bytes=VMEM_BYTES),
+        cost_estimate=lasts(2.8),
         name="finish",
     )(core, part, gain)
 
@@ -363,6 +374,7 @@
         out_specs=row_spec(block, result),
         out_shape=result,
         compiler_params=pltpu.CompilerParams(vmem_limit_bytes=40 * 1024 * 1024),
+        cost_estimate=lasts(3.5),
         name="fold",
     )(own, other, weight)
 
@@ -416,6 +428,7 @@
             jax.ShapeDtypeStruct((pairs, 2, tokens), F32),
         ],
         compiler_params=pltpu.CompilerParams(vmem_limit_bytes=VMEM_BYTES),
+        cost_estimate=lasts(10),
         name="attend",
     )(query, key, value, start_row)
 
@@ -488,6 +501,7 @@
         out_shape=[jax.ShapeDtypeStruct((tokens, width), BF16)] * 3,
         scratch_shapes=[pltpu.VMEM((LANES, tokens), F32)],
         compiler_params=pltpu.CompilerParams(vmem_limit_bytes=VMEM_BYTES),
+        cost_estimate=lasts(11),
         name="attend_back",
     )(query, key, value, mixed, mixed_grad, start_row, logs, cosine, front, back)
 
@@ -562,15 +576,13 @@
             bit //= 2
         return [got[step] for step in range(rows)]
 
-    def reduce_row(parts, *works):
-        parts, bit, step = list(parts), 1, 0
+    def reduce_row(parts, bit):
+        parts = list(parts)
         while bit < rows:
-            lows = {at: parts[at + bit].astype(BF16) for at in range(rows - 2 * bit, -1, -2 * bit)}
-            held = works[step](*lows.values()) if step < len(works) else ()
-            for at, low in lows.items():
-                came = after(row_swap(low, bit), *held)
-                parts[at] = parts[at].astype(F32) + came.astype(F32)
-            bit, step = 2 * bit, step + 1
+            for at in range(rows - 2 * bit, -1, -2 * bit):
+                sent = row_swap(parts[at + bit].astype(BF16), bit)
+                parts[at] = parts[at].astype(F32) + sent.astype(F32)
+            bit *= 2
         return parts[0]
 
     def row_part(a, step):
@@ -678,19 +690,19 @@
     with jax.named_scope("inputs"):
         x_own = put_feats(spread(inputs))
         x_other = core_swap(x_own)
-    with jax.named_scope("grad_plane"):
-        g_part = to_parts(after(out_grad, x_own))
     with jax.named_scope("qkv_row"):
         qkv_list = gather_row(
             jnp.concatenate(
                 [scaled(w, gain_one) for w in (query_weight, key_weight, value_weight)], axis=1
             ),
-            (cosine, front, back, start_row, up_cut, down_cut, out_block, g_part),
-        )
+            (cosine, front, back, start_row, up_cut, down_cut, out_block),
+        )
+    with jax.named_scope("grad_plane"):
+        g_part = to_parts(after(out_grad, *qkv_list))
     with jax.named_scope("gate_row"):
         gate_whole = exchange(cut(scaled(gate_weight, gain_two)))
     with jax.named_scope("out_row"):
-        out_full = lax.all_gather(after(out_block, *qkv_list[1:3]), "row", axis=0, tiled=True)
+        out_full = lax.all_gather(after(out_block, *qkv_list), "row", axis=0, tiled=True)
     with jax.named_scope("up_row"):
         up_whole = exchange(after(up_cut, gate_whole))
     with jax.named_scope("down_row"):
@@ -702,12 +714,16 @@
     )
     qkv_full = join_rows([after(a, query) for a in qkv_list])
     mixed, logs = attend(after(query, gates[1], gates[2], up_whole), key, value, start_row)
-    mixed = after(mixed, gates[3])
     with jax.named_scope("grad_row"):
-        g_own = lax.all_gather(after(g_part, out_full), "row", axis=0, tiled=True)
-
-    def scatter_parts(own, other):
-        low = (own.astype(F32) + core_swap(other).astype(F32)).astype(BF16)
+        g_own = lax.all_gather(after(g_part, mixed), "row", axis=0, tiled=True)
+    with jax.named_scope("up_plane"):
+        ups = spread_weights(up_whole)
+    mixed = after(mixed, gates[3], ups[1], ups[2], down_whole)
+
+    def join_cores(own, other):
+        return (own.astype(F32) + core_swap(other).astype(F32)).astype(BF16)
+
+    def scatter_parts(low):
         total = token_part(low, 0).astype(F32)
         for s in range(1, places):
             total = total + plane_swap(token_part(low, s), s).astype(F32)
@@ -715,10 +731,8 @@
 
     with jax.named_scope("mix_plane"):
         own, other = unfold(feat, "mix", [mixed], [out_full])
-        middle = token_part(x_own, 0).astype(F32) + scatter_parts(after(own, down_whole), other)
-    with jax.named_scope("up_plane"):
-        ups = spread_weights(up_whole)
-    middle_low = after(middle.astype(BF16), ups[1], ups[2])
+        middle = token_part(x_own, 0).astype(F32) + scatter_parts(join_cores(after(own, ups[3]), other))
+    middle_low = middle.astype(BF16)
     with jax.named_scope("middle_row"):
         m_list = gather_row(middle_low)
         m_others = [core_swap(m) for m in m_list]
@@ -728,9 +742,12 @@
     square = square + core_swap(square)
     scale_mid = lax.rsqrt(square / width + EPS)
 
-    m_list = list(lax.optimization_barrier((*m_list, downs[1], downs[2])))[:rows]
+    m_list = list(lax.optimization_barrier(tuple(m_list)))
     pairs = [slice(at, at + 2) for at in range(0, rows, 2)]
-    found = [activate(feat, m_list[pair], m_others[pair], gates, ups) for pair in pairs]
+    found = [
+        activate(feat, [after(a, *(downs[1:3] if pair.start else ())) for a in m_list[pair]], m_others[pair], gates, ups)
+        for pair in pairs
+    ]
     hiddens = [f[0] for f in found]
     with jax.named_scope("grad_row"):
         g_own = after(g_own, hiddens[0])
@@ -744,15 +761,17 @@
             )
             scaled_grads[at] = gate_grad, up_grad
             low = own.astype(F32) + core_swap(other).astype(F32)
-            parts[2 * at], parts[2 * at + 1] = low[:quarter], low[quarter:].astype(BF16)
+            sent = low[quarter:].astype(BF16)
+            parts[2 * at] = low[:quarter] + row_swap(sent, 1).astype(F32)
         if down_parts is None:
             with jax.named_scope("down_grad"):
                 down_parts = outer(
-                    feat, "down_outer", starts, [g_own], [g_other], [after(h, parts[-1]) for h in hiddens], places
+                    feat, "down_outer", starts, [g_own], [g_other], [after(h, sent) for h in hiddens], places
                 )
             held = down_parts[:1]
+        held = *held, parts[2 * at].astype(BF16)
     with jax.named_scope("unit_grad"):
-        unit_grad = reduce_row(parts)
+        unit_grad = reduce_row(parts, 2)
     with jax.named_scope("down_grad"):
         down_total = plane_second(plane_first(down_parts))
         down_blocks = give_back(down_total)
@@ -798,22 +817,23 @@
     )
     with jax.named_scope("heads_grad"):
         heads_blocks = lax.psum_scatter(heads_part, "row", scatter_dimension=0, tiled=True)
+    with jax.named_scope("first_plane"):
+        first_low = join_cores(
+            *unfold(feat, "first_grad", [after(query_grad, heads_part), key_grad, value_grad], [qkv_full])
+        )
+        first_unit_grad = scatter_parts(first_low)
     with jax.named_scope("up_grad"):
-        up_total = plane_second(plane_first([after(a, gate_total, heads_part) for a in up_parts]))
+        up_total = plane_second(plane_first([after(a, gate_total, first_low) for a in up_parts]))
         up_blocks = give_back(up_total)
     with jax.named_scope("block_out"):
         block_out = to_home(after(feed_low, up_total))
-    with jax.named_scope("first_plane"):
-        first_unit_grad = scatter_parts(
-            *unfold(feat, "first_grad", [after(query_grad, heads_part), key_grad, value_grad], [qkv_full])
-        )
     scale_first = token_part(scale_one, 0)
     unit_first = token_part(x_own, 0).astype(F32) * scale_first
     dot_one = jnp.sum(first_unit_grad * unit_first, axis=1, keepdims=True)
     dot_one = dot_one + core_swap(dot_one)
     with jax.named_scope("input_grad"):
         input_grad = to_home(
-            (middle_grad + scale_first * (first_unit_grad - unit_first * (dot_one / width))).astype(BF16)
+            (after(middle_grad, up_total) + scale_first * (first_unit_grad - unit_first * (dot_one / width))).astype(BF16)
         )
 
     def row_dots(w, d):

time: 672 us -> 701 us (1.043)
  other arithmetic: 51.6 us -> 67.8 us
  local copies, waits for them, and re-layouts: 86.2 us -> 97.5 us
    ppermute x12, waiting for transfers between devices: 66.9 us -> 98.3 us  [row_swap(): return lax.ppermute(a, 'row', [(i, i ^ step) for i in range(rows)])]
    all_to_all x3, waiting for transfers between devices: 60.4 us -> 29.3 us  [exchange(): got = lax.all_to_all(pieces, 'row', split_axis=0, concat_axis=0, tiled=True)]
    all_to_all x3, waiting for transfers between devices: 14 us -> 43.1 us  [give_back(): return lax.all_to_all(total, 'row', split_axis=0, concat_axis=0, tiled=True)]
    ppermute x45, waiting for transfers between devices: 126 us -> 100 us  [plane_swap(): return lax.ppermute(a, 'col', [(i, i ^ 2 * step) for i in range(cols)])]
    unnamed x219 -> x231, local copies, waits for them, and re-layouts: 43.3 us -> 42.8 us
  transfers between devices with their start and end apart: 86 -> 86, of which waited for: 33 -> 35; matrix products, arithmetic and copies ran while one was open for 14% -> 17% of each run, Pallas kernels for 15% -> 16%
where the time goes in v10:
time: 701 us; the launch traced here: 693 us
  waiting for transfers between devices  281 us (40%)
  Pallas kernels  131 us (19%)
  starting transfers between devices  99.3 us (14%)
  local copies, waits for them, and re-layouts  97.5 us (14%)
  other arithmetic  67.8 us (10%)
  between operations  15.9 us (2%)
    ppermute x45, waiting for transfers between devices, plane_swap(): return lax.ppermute(a, 'col', [(i, i ^ 2 * step) for i in range(cols)])  100 us
    ppermute x12, waiting for transfers between devices, row_swap(): return lax.ppermute(a, 'row', [(i, i ^ step) for i in range(rows)])  98.3 us
    ppermute x45, starting transfers between devices, plane_swap(): return lax.ppermute(a, 'col', [(i, i ^ 2 * step) for i in range(cols)])  52.7 us
    all_to_all x3, waiting for transfers between devices, give_back(): return lax.all_to_all(total, 'row', split_axis=0, concat_axis=0, tiled=True)  43.1 us
    unnamed x231, local copies, waits for them, and re-layouts  42.8 us
    all_to_all x3, waiting for transfers between devices, exchange(): got = lax.all_to_all(pieces, 'row', split_axis=0, concat_axis=0, tiled=True)  29.3 us
    pallas_call x4, Pallas kernels, unfold(): pl.pallas_call(functools.partial(unfold_kernel, feat, len(lefts)), grid=(...  24.8 us
    pallas_call x2, Pallas kernels, units_back(): pl.pallas_call(functools.partial(units_back_kernel, feat, parts, count),...  20.6 us
  transfers between devices with their start and end apart: 86, of which 35 were waited for; matrix products, arithmetic and copies ran while one was open for 17% of the time, Pallas kernels for 16%

profile of v10, /device:TPU:0, one launch (start us, length us, event | category | flops | bytes accessed | tf_op | source)
XLA Modules:
  0.0 692.7 jit_solution(17025097417326214560)
XLA Ops:
  7.2 3.0 collective-permute-start
  16.8 5.5 all-to-all-start
  24.0 2.9 collective-permute-start.5
  31.1 4.0 collective-permute-done.1
  38.5 3.1 multiply_sine_fusion
  41.7 23.5 %all-to-all-done = bf16[4,512,256]{2,1,0:T(8,128)(2,1)} async-done(((bf16[4,512,256]{2,1,0:T(8,128)(2,1)}), bf16[4,512,256]{2,1,0:T(8,128)(2,1)}, u32[]{:S(2)}, u32[]{:S(2)}) %all-to-all-start) | async-done | bytes 1048608 | tf_op jit(solution)/shard_map/gate_row/all_to_all | solution.py:636
  65.2 4.0 all-to-all-start.1
  69.2 3.1 pad_maximum_fusion.9.refs_4_.cos_ref
  81.7 8.3 %collective-permute-done.5.refs_2_ = bf16[512,768]{1,0:T(8,128)(2,1)} collective-permute-done((bf16[512,768]{1,0:T(8,128)(2,1)}, bf16[512,768]{1,0:T(8,128)(2,1)}, u32[]{:S(2)}, u32[]{:S(2)}) %collective-permute-start.5) | collective-permute-done | bytes 786464 | tf_op jit(solution)/shard_map/qkv_row/ppermute | solution.py:568
  90.0 3.1 collective-permute-start.6
  93.1 21.5 %collective-permute-done.6.refs_3_ = bf16[512,768]{1,0:T(8,128)(2,1)} collective-permute-done((bf16[512,768]{1,0:T(8,128)(2,1)}, bf16[512,768]{1,0:T(8,128)(2,1)}, u32[]{:S(2)}, u32[]{:S(2)}) %collective-permute-start.6) | collective-permute-done | bytes 786464 | tf_op jit(solution)/shard_map/qkv_row/ppermute | solution.py:568
  121.5 4.2 all-to-all-start.2
  129.2 6.7 project.1
  139.2 10.4 %attend.1 = (bf16[1024,256]{1,0:T(8,128)(2,1)}, f32[2,2,1024]{2,1,0:T(2,128)}) custom-call(bf16[1024,256]{1,0:T(8,128)(2,1)} %copy-done.78, bf16[1024,256]{1,0:T(8,128)(2,1)} %copy-done.79, bf16[1024,256]{1,0:T(8,128)(2,1)} %copy-done.80, s32[1,1024]{1,0:T(1,128)} %bitcast.95), custom_call_target="tpu_custom_call" | custom-call | flops 11500000256 | bytes 1 | tf_op jit(solution)/shard_map/attend/pallas_call | solution.py:421
  149.6 8.2 %collective-permute-done.12.refs_9_.refs_15_ = bf16[2048,256]{1,0:T(8,128)(2,1)S(1)} collective-permute-done((bf16[2048,256]{1,0:T(8,128)(2,1)S(1)}, bf16[2048,256]{1,0:T(8,128)(2,1)S(1)}, u32[]{:S(2)}, u32[]{:S(2)}) %collective-permute-start.12) | collective-permute-done | bytes 1048608 | tf_op jit(solution)/shard_map/up_plane/ppermute | solution.py:554
  158.8 5.8 all-to-all-done.2
  164.7 5.2 mix.1
  178.2 9.9 %collective-permute-done.24 = bf16[256,256]{1,0:T(8,128)(2,1)S(1)} collective-permute-done((bf16[256,256]{1,0:T(8,128)(2,1)S(1)}, bf16[256,256]{1,0:T(8,128)(2,1)S(1)}, u32[]{:S(2)}, u32[]{:S(2)}) %collective-permute-start.24) | collective-permute-done | bytes 131104 | tf_op jit(solution)/shard_map/grad_plane/ppermute | solution.py:554
  190.2 5.6 collective-permute-done.25
  199.6 2.9 add_convert_fusion.1
  206.2 11.4 %collective-permute-done.16 = bf16[256,1024]{1,0:T(8,128)(2,1)S(1)} collective-permute-done((bf16[256,1024]{1,0:T(8,128)(2,1)S(1)}, bf16[256,1024]{1,0:T(8,128)(2,1)S(1)}, u32[]{:S(2)}, u32[]{:S(2)}) %collective-permute-start.16) | collective-permute-done | bytes 524320 | tf_op jit(solution)/shard_map/mix_plane/ppermute | solution.py:554
  217.6 10.5 %collective-permute-done.17 = bf16[256,1024]{1,0:T(8,128)(2,1)S(1)} collective-permute-done((bf16[256,1024]{1,0:T(8,128)(2,1)S(1)}, bf16[256,1024]{1,0:T(8,128)(2,1)S(1)}, u32[]{:S(2)}, u32[]{:S(2)}) %collective-permute-start.17) | collective-permute-done | bytes 524320 | tf_op jit(solution)/shard_map/mix_plane/ppermute | solution.py:554
  231.7 31.7 %collective-permute-done.20.refs_0_.refs_2_ = bf16[256,1024]{1,0:T(8,128)(2,1)S(1)} collective-permute-done((bf16[256,1024]{1,0:T(8,128)(2,1)S(1)}, bf16[256,1024]{1,0:T(8,128)(2,1)S(1)}, u32[]{:S(2)}, u32[]{:S(2)}) %collective-permute-start.20) | collective-permute-done | bytes 524320 | tf_op jit(solution)/shard_map/middle_row/ppermute | solution.py:568
  266.9 10.2 %collective-permute-done.21.refs_1_.refs_3_ = bf16[256,1024]{1,0:T(8,128)(2,1)S(1)} collective-permute-done((bf16[256,1024]{1,0:T(8,128)(2,1)S(1)}, bf16[256,1024]{1,0:T(8,128)(2,1)S(1)}, u32[]{:S(2)}, u32[]{:S(2)}) %collective-permute-start.21) | collective-permute-done | bytes 524320 | tf_op jit(solution)/shard_map/middle_row/ppermute | solution.py:568
  277.9 7.0 %activate.2 = (bf16[512,1024]{1,0:T(8,128)(2,1)S(1)}, bf16[512,1024]{1,0:T(8,128)(2,1)S(1)}, bf16[512,1024]{1,0:T(8,128)(2,1)S(1)}, f32[512,1]{1,0:T(8,128)S(1)}) custom-call(bf16[256,1024]{1,0:T(8,128)(2,1)S(1)} %convert_element_type.275.refs_0_, bf16[256,1024]{1,0:T(8,128)(2,1)S(1)} %collective-permute-done.19.refs_1_, ...), custom_call_target="tpu_custom_call" | custom-call | flops 8625000448 | bytes 1 | tf_op jit(solution)/shard_map/activate/pallas_call | solution.py:174
  297.3 9.3 %collective-permute-done.33 = bf16[1024,256]{1,0:T(8,128)(2,1)S(1)} collective-permute-done((bf16[1024,256]{1,0:T(8,128)(2,1)S(1)}, bf16[1024,256]{1,0:T(8,128)(2,1)S(1)}, u32[]{:S(2)}, u32[]{:S(2)}) %collective-permute-start.33) | collective-permute-done | bytes 524320 | tf_op jit(solution)/shard_map/down_plane/ppermute | solution.py:554
  306.7 2.5 collective-permute-done.34
  309.3 7.7 %activate.3 = (bf16[512,1024]{1,0:T(8,128)(2,1)S(1)}, bf16[512,1024]{1,0:T(8,128)(2,1)S(1)}, bf16[512,1024]{1,0:T(8,128)(2,1)S(1)}, f32[512,1]{1,0:T(8,128)S(1)}) custom-call(bf16[256,1024]{1,0:T(8,128)(2,1)S(1)} %copy-done.40, bf16[256,1024]{1,0:T(8,128)(2,1)S(1)} %copy-done.45, bf16[256,1024]{1,0:T(8,128)(2,1)S(1)} %collective-permute-done.31.refs_2_.refs_6_, ...), custom_call_target="tpu_custom_call" | custom-call | flops 8625000448 | bytes 1 | tf_op jit(solution)/shard_map/activate/pallas_call | solution.py:174
  322.8 10.3 %units_back.2 = (bf16[512,1024]{1,0:T(8,128)(2,1)S(1)}, bf16[512,1024]{1,0:T(8,128)(2,1)S(1)}, bf16[512,1024]{1,0:T(8,128)(2,1)S(1)}, bf16[512,1024]{1,0:T(8,128)(2,1)S(1)}) custom-call(s32[2]{0:T(128)S(1)} %pad_add_fusion.2.starts, bf16[1024,1024]{1,0:T(8,128)(2,1)} %all-gather.5.cloned.1.call-done.refs_0_, bf16[1024,1024]{1,0:T(8,128)(2,1)} %copy-done.36, ...), custom_call_target="tpu_custom_call" | custom-call | flops 10695000064 | bytes 1 | tf_op jit(solution)/shard_map/unit_grad/units_back/pallas_call | solution.py:240
  335.3 2.6 collective-permute-done.35
  340.3 6.2 down_outer.1
  349.8 2.5 collective-permute-done.36
  353.3 10.3 %units_back.3 = (bf16[512,1024]{1,0:T(8,128)(2,1)S(1)}, bf16[512,1024]{1,0:T(8,128)(2,1)S(1)}, bf16[512,1024]{1,0:T(8,128)(2,1)S(1)}, bf16[512,1024]{1,0:T(8,128)(2,1)S(1)}) custom-call(s32[2]{0:T(128)S(1)} %pad_add_fusion.1.starts, bf16[1024,1024]{1,0:T(8,128)(2,1)} %all-gather.5.cloned.1.call-done.refs_0_, bf16[1024,1024]{1,0:T(8,128)(2,1)} %copy-done.36, ...), custom_call_target="tpu_custom_call" | custom-call | flops 10695000064 | bytes 1 | tf_op jit(solution)/shard_map/unit_grad/units_back/pallas_call | solution.py:240
  373.6 17.2 %collective-permute-done.42 = bf16[2048,256]{1,0:T(8,128)(2,1)} collective-permute-done((bf16[2048,256]{1,0:T(8,128)(2,1)}, bf16[2048,256]{1,0:T(8,128)(2,1)}, u32[]{:S(2)}, u32[]{:S(2)}) %collective-permute-start.42) | collective-permute-done | bytes 1048608 | tf_op jit(solution)/shard_map/down_grad/ppermute | solution.py:554
  398.3 3.0 add_convert_fusion.6
  401.5 3.0 fusion.33
  408.0 6.2 up_outer.1
  419.4 5.9 feed.2
  425.4 5.9 feed.3
  434.2 6.4 gate_outer.1
  469.4 4.2 all-to-all-start.3
  483.9 3.5 fold.1.do_ref
  488.2 11.0 %attend_back.1 = (bf16[1024,256]{1,0:T(8,128)(2,1)}, bf16[1024,256]{1,0:T(8,128)(2,1)}, bf16[1024,256]{1,0:T(8,128)(2,1)}) custom-call(bf16[1024,256]{1,0:T(8,128)(2,1)} %copy-done.78, bf16[1024,256]{1,0:T(8,128)(2,1)} %copy-done.79, bf16[1024,256]{1,0:T(8,128)(2,1)} %copy-done.80, bf16[1024,256]{1,0:T(8,128)(2,1)} %get-tuple-element.121.refs_0_.o_ref.mixed_ref, ...), custom_call_target="tpu_custom_call" | custom-call | flops 12650000384 | bytes 1 | tf_op jit(solution)/shard_map/attend_back/pallas_call | solution.py:491
  499.2 6.0 collective-permute-done.53
  506.8 2.8 multiply_reduce_fusion.1
  509.6 10.9 %all-to-all-done.3.part_ref = bf16[4,512,256]{2,1,0:T(8,128)(2,1)} async-done(((bf16[4,512,256]{2,1,0:T(8,128)(2,1)}), bf16[4,512,256]{2,1,0:T(8,128)(2,1)}, u32[]{:S(2)}, u32[]{:S(2)}) %all-to-all-start.3) | async-done | bytes 1048608 | tf_op jit(solution)/shard_map/down_grad/all_to_all | solution.py:670
  527.4 9.3 %heads_outer.1 = (bf16[2048,1024]{1,0:T(8,128)(2,1)}, f32[2048,1]{1,0:T(8,128)S(1)}) custom-call(bf16[1024,1024]{1,0:T(8,128)(2,1)S(1)} %constant_dynamic-update-slice_fusion.25.own_ref.x_own, bf16[1024,1024]{1,0:T(8,128)(2,1)} %collective-permute-done.3.other_ref.x_other, bf16[1024,1024]{1,0:T(8,128)(2,1)S(1)} %copy-done.4, ...), custom_call_target="tpu_custom_call" | custom-call | flops 10810000384 | bytes 1 | tf_op jit(solution)/shard_map/heads_outer/pallas_call | solution.py:316
  537.6 7.7 %first_grad.1 = (bf16[1024,1024]{1,0:T(8,128)(2,1)}, bf16[1024,1024]{1,0:T(8,128)(2,1)}) custom-call(bf16[1024,256]{1,0:T(8,128)(2,1)} %get-tuple-element.197.dq_ref.refs_0_, bf16[1024,256]{1,0:T(8,128)(2,1)} %get-tuple-element.189.dk_ref.refs_1_, bf16[1024,256]{1,0:T(8,128)(2,1)} %get-tuple-element.190.dv_ref.refs_2_, ...), custom_call_target="tpu_custom_call" | custom-call | flops 6899999744 | bytes 1 | tf_op jit(solution)/shard_map/first_plane/first_grad/pallas_call | solution.py:126
  545.3 4.5 collective-permute-done.55
  549.8 4.6 add_convert_fusion
  559.7 4.5 all-to-all-start.4
  564.7 2.7 finish.4
  574.3 5.1 collective-permute-done.58
  586.9 32.1 %all-to-all-done.4.part_ref = bf16[4,512,256]{2,1,0:T(8,128)(2,1)} async-done(((bf16[4,512,256]{2,1,0:T(8,128)(2,1)}), bf16[4,512,256]{2,1,0:T(8,128)(2,1)}, u32[]{:S(2)}, u32[]{:S(2)}) %all-to-all-start.4) | async-done | bytes 1048608 | tf_op jit(solution)/shard_map/gate_grad/all_to_all | solution.py:670
  619.0 2.8 finish.5
  621.8 2.4 add_convert_fusion.9
  624.3 3.0 collective-permute-done.64
  629.4 3.2 multiply_reduce_fusion
  641.0 4.5 all-to-all-start.5
  650.2 11.9 %collective-permute-done.73 = f32[2,512]{1,0:T(2,128)S(1)} collective-permute-done((f32[2,512]{1,0:T(2,128)S(1)}, f32[2,512]{1,0:T(2,128)S(1)}, u32[]{:S(2)}, u32[]{:S(2)}) %collective-permute-start.73) | collective-permute-done | bytes 4128 | tf_op jit(solution)/shard_map/gains/ppermute | solution.py:568
  662.7 8.2 %collective-permute-done.74 = f32[2,512]{1,0:T(2,128)S(1)} collective-permute-done((f32[2,512]{1,0:T(2,128)S(1)}, f32[2,512]{1,0:T(2,128)S(1)}, u32[]{:S(2)}, u32[]{:S(2)}) %collective-permute-start.74) | collective-permute-done | bytes 4128 | tf_op jit(solution)/shard_map/gains/ppermute | solution.py:568
  676.7 2.4 collective-permute-done.61
  680.2 2.8 finish.6
  683.0 2.8 finish.7
  (497 shorter events, 212.7 us)
Async XLA Ops:
  7.2 22.8 %collective-permute-start = (bf16[1024,256]{1,0:T(8,128)(2,1)}, bf16[1024,256]{1,0:T(8,128)(2,1)}, u32[]{:S(2)}, u32[]{:S(2)}) collective-permute-start(bf16[1024,256]{1,0:T(8,128)(2,1)} %param.13), channel_id=1, source_target_pairs={{0,2},{1,3},{2,0},{3,1},{4,6},{5,7},{6,4},{7,5},{8,10},{9,11},{10,... | collective-permute-start | bytes 1572872 | tf_op jit(solution)/shard_map/inputs/ppermute | solution.py:554
  10.2 24.9 %collective-permute-start.1 = (bf16[1024,256]{1,0:T(8,128)(2,1)}, bf16[1024,256]{1,0:T(8,128)(2,1)}, u32[]{:S(2)}, u32[]{:S(2)}) collective-permute-start(bf16[1024,256]{1,0:T(8,128)(2,1)} %param.13), channel_id=1, source_target_pairs={{0,4},{1,5},{2,6},{3,7},{4,0},{5,1},{6,2},{7,3},{8,12},{9,13},{10,... | collective-permute-start | bytes 1572872 | tf_op jit(solution)/shard_map/inputs/ppermute | solution.py:554
  11.7 24.5 %collective-permute-start.2 = (bf16[1024,256]{1,0:T(8,128)(2,1)}, bf16[1024,256]{1,0:T(8,128)(2,1)}, u32[]{:S(2)}, u32[]{:S(2)}) collective-permute-start(bf16[1024,256]{1,0:T(8,128)(2,1)} %param.13), channel_id=1, source_target_pairs={{0,6},{1,7},{2,4},{3,5},{4,2},{5,3},{6,0},{7,1},{8,14},{9,15},{10,... | collective-permute-start | bytes 1572872 | tf_op jit(solution)/shard_map/inputs/ppermute | solution.py:554
  16.8 48.4 %all-to-all-start = ((bf16[4,512,256]{2,1,0:T(8,128)(2,1)}), bf16[4,512,256]{2,1,0:T(8,128)(2,1)}, u32[]{:S(2)}, u32[]{:S(2)}) async-start(bf16[4,512,256]{2,1,0:T(8,128)(2,1)} %pad_maximum_fusion.2), calls=%async_computation | async-start | bytes 2097152 | tf_op jit(solution)/shard_map/gate_row/all_to_all | solution.py:636
  24.0 66.0 %collective-permute-start.5 = (bf16[512,768]{1,0:T(8,128)(2,1)}, bf16[512,768]{1,0:T(8,128)(2,1)}, u32[]{:S(2)}, u32[]{:S(2)}) collective-permute-start(bf16[512,768]{1,0:T(8,128)(2,1)} %maximum_maximum_fusion.refs_0_), channel_id=1, source_target_pairs={{0,16},{8,24},{16,0},{24,8},{1,17},{9,25},{17,1},{25,9},{2,18},{10... | collective-permute-start | bytes 2359304 | tf_op jit(solution)/shard_map/qkv_row/ppermute | solution.py:568
  26.9 66.2 %collective-permute-start.4 = (bf16[512,768]{1,0:T(8,128)(2,1)}, bf16[512,768]{1,0:T(8,128)(2,1)}, u32[]{:S(2)}, u32[]{:S(2)}) collective-permute-start(bf16[512,768]{1,0:T(8,128)(2,1)} %maximum_maximum_fusion.refs_0_), channel_id=1, source_target_pairs={{0,8},{8,0},{16,24},{24,16},{1,9},{9,1},{17,25},{25,17},{2,10},{10... | collective-permute-start | bytes 2359304 | tf_op jit(solution)/shard_map/qkv_row/ppermute | solution.py:568
  37.3 88.7 %collective-permute-start.3 = (bf16[1024,1024]{1,0:T(8,128)(2,1)S(1)}, bf16[1024,1024]{1,0:T(8,128)(2,1)}, u32[]{:S(2)}, u32[]{:S(2)}) collective-permute-start(bf16[1024,1024]{1,0:T(8,128)(2,1)S(1)} %constant_dynamic-update-slice_fusion.25.own_ref.x_own), channel_id=1, source_target_pairs={{0,1},{1,0},{2,3},{3,2},{4,5},{5,4},{6,7},{7,6},{8,9},{9,8},{10,11... | collective-permute-start | bytes 6291464 | tf_op jit(solution)/shard_map/inputs/ppermute | solution.py:551
  65.2 56.4 %all-to-all-start.1 = ((bf16[4,512,256]{2,1,0:T(8,128)(2,1)}), bf16[4,512,256]{2,1,0:T(8,128)(2,1)S(1)}, u32[]{:S(2)}, u32[]{:S(2)}) async-start(bf16[4,512,256]{2,1,0:T(8,128)(2,1)} %pad_maximum_fusion), calls=%async_computation.1 | async-start | bytes 2097152 | tf_op jit(solution)/shard_map/up_row/all_to_all | solution.py:636
  69.2 95.5 %all-gather.3.cloned.1.call-start = ((), (), s32[]{:S(2)}) async-start(), calls=%async_computation.8 | async-start | bytes 1310720 | tf_op jit(solution)/shard_map/out_row/all_gather | solution.py:705
  76.7 38.0 %collective-permute-start.8 = (bf16[2048,256]{1,0:T(8,128)(2,1)}, bf16[2048,256]{1,0:T(8,128)(2,1)}, u32[]{:S(2)}, u32[]{:S(2)}) collective-permute-start(bf16[2048,256]{1,0:T(8,128)(2,1)} %bitcast.17.refs_4_.refs_9_), channel_id=1, source_target_pairs={{0,4},{1,5},{2,6},{3,7},{4,0},{5,1},{6,2},{7,3},{8,12},{9,13},{10,... | collective-permute-start | bytes 3145736 | tf_op jit(solution)/shard_map/gate_plane/ppermute | solution.py:554
  78.2 39.9 %collective-permute-start.7 = (bf16[2048,256]{1,0:T(8,128)(2,1)}, bf16[2048,256]{1,0:T(8,128)(2,1)}, u32[]{:S(2)}, u32[]{:S(2)}) collective-permute-start(bf16[2048,256]{1,0:T(8,128)(2,1)} %bitcast.17.refs_4_.refs_9_), channel_id=1, source_target_pairs={{0,2},{1,3},{2,0},{3,1},{4,6},{5,7},{6,4},{7,5},{8,10},{9,11},{10,... | collective-permute-start | bytes 3145736 | tf_op jit(solution)/shard_map/gate_plane/ppermute | solution.py:554
  90.0 24.7 %collective-permute-start.6 = (bf16[512,768]{1,0:T(8,128)(2,1)}, bf16[512,768]{1,0:T(8,128)(2,1)}, u32[]{:S(2)}, u32[]{:S(2)}) collective-permute-start(bf16[512,768]{1,0:T(8,128)(2,1)} %collective-permute-done.5.refs_2_), channel_id=1, source_target_pairs={{0,8},{8,0},{16,24},{24,16},{1,9},{9,1},{17,25},{25,17},{2,10},{10... | collective-permute-start | bytes 2359304 | tf_op jit(solution)/shard_map/qkv_row/ppermute | solution.py:568
  116.6 20.5 %collective-permute-start.9 = (bf16[1024,256]{1,0:T(8,128)(2,1)}, bf16[1024,256]{1,0:T(8,128)(2,1)}, u32[]{:S(2)}, u32[]{:S(2)}) collective-permute-start(bf16[1024,256]{1,0:T(8,128)(2,1)} %slice.288), channel_id=1, source_target_pairs={{0,2},{1,3},{2,0},{3,1},{4,6},{5,7},{6,4},{7,5},{8,10},{9,11},{10,... | collective-permute-start | bytes 1572872 | tf_op jit(solution)/shard_map/gate_plane/ppermute | solution.py:554
  120.0 18.1 %collective-permute-start.10 = (bf16[1024,256]{1,0:T(8,128)(2,1)}, bf16[1024,256]{1,0:T(8,128)(2,1)}, u32[]{:S(2)}, u32[]{:S(2)}) collective-permute-start(bf16[1024,256]{1,0:T(8,128)(2,1)} %slice.289), channel_id=1, source_target_pairs={{0,4},{1,5},{2,6},{3,7},{4,0},{5,1},{6,2},{7,3},{8,12},{9,13},{10,... | collective-permute-start | bytes 1572872 | tf_op jit(solution)/shard_map/gate_plane/ppermute | solution.py:554
  121.5 43.1 %all-to-all-start.2 = ((bf16[4,512,256]{2,1,0:T(8,128)(2,1)}), bf16[4,512,256]{2,1,0:T(8,128)(2,1)}, u32[]{:S(2)}, u32[]{:S(2)}) async-start(bf16[4,512,256]{2,1,0:T(8,128)(2,1)} %pad_maximum_fusion.1), calls=%async_computation.2 | async-start | bytes 2097152 | tf_op jit(solution)/shard_map/down_row/all_to_all | solution.py:636
  125.8 165.3 %all-gather.5.cloned.1.call-start = ((), (), s32[]{:S(2)}) async-start(), calls=%async_computation.9 | async-start | bytes 2621440 | tf_op jit(solution)/shard_map/grad_row/all_gather | solution.py:718
  135.9 21.9 %collective-permute-start.12 = (bf16[2048,256]{1,0:T(8,128)(2,1)S(1)}, bf16[2048,256]{1,0:T(8,128)(2,1)S(1)}, u32[]{:S(2)}, u32[]{:S(2)}) collective-permute-start(bf16[2048,256]{1,0:T(8,128)(2,1)S(1)} %bitcast.71), channel_id=1, source_target_pairs={{0,4},{1,5},{2,6},{3,7},{4,0},{5,1},{6,2},{7,3},{8,12},{9,13},{10,... | collective-permute-start | bytes 3145736 | tf_op jit(solution)/shard_map/up_plane/ppermute | solution.py:554
  136.5 22.3 %collective-permute-start.11 = (bf16[2048,256]{1,0:T(8,128)(2,1)S(1)}, bf16[2048,256]{1,0:T(8,128)(2,1)}, u32[]{:S(2)}, u32[]{:S(2)}) collective-permute-start(bf16[2048,256]{1,0:T(8,128)(2,1)S(1)} %bitcast.72), channel_id=1, source_target_pairs={{0,2},{1,3},{2,0},{3,1},{4,6},{5,7},{6,4},{7,5},{8,10},{9,11},{10,... | collective-permute-start | bytes 3145736 | tf_op jit(solution)/shard_map/up_plane/ppermute | solution.py:554
  169.9 29.7 %collective-permute-start.15 = (bf16[1024,1024]{1,0:T(8,128)(2,1)}, bf16[1024,1024]{1,0:T(8,128)(2,1)}, u32[]{:S(2)}, u32[]{:S(2)}) collective-permute-start(bf16[1024,1024]{1,0:T(8,128)(2,1)} %get-tuple-element.125), channel_id=1, source_target_pairs={{0,1},{1,0},{2,3},{3,2},{4,5},{5,4},{6,7},{7,6},{8,9},{9,8},{10,11... | collective-permute-start | bytes 6291464 | tf_op jit(solution)/shard_map/mix_plane/ppermute | solution.py:551
  170.7 26.5 %collective-permute-start.13 = (bf16[1024,256]{1,0:T(8,128)(2,1)}, bf16[1024,256]{1,0:T(8,128)(2,1)}, u32[]{:S(2)}, u32[]{:S(2)}) collective-permute-start(bf16[1024,256]{1,0:T(8,128)(2,1)} %slice.290), channel_id=1, source_target_pairs={{0,2},{1,3},{2,0},{3,1},{4,6},{5,7},{6,4},{7,5},{8,10},{9,11},{10,... | collective-permute-start | bytes 1572872 | tf_op jit(solution)/shard_map/up_plane/ppermute | solution.py:554
  176.2 22.2 %collective-permute-start.14 = (bf16[1024,256]{1,0:T(8,128)(2,1)}, bf16[1024,256]{1,0:T(8,128)(2,1)}, u32[]{:S(2)}, u32[]{:S(2)}) collective-permute-start(bf16[1024,256]{1,0:T(8,128)(2,1)} %slice.291), channel_id=1, source_target_pairs={{0,4},{1,5},{2,6},{3,7},{4,0},{5,1},{6,2},{7,3},{8,12},{9,13},{10,... | collective-permute-start | bytes 1572872 | tf_op jit(solution)/shard_map/up_plane/ppermute | solution.py:554
  177.7 18.1 %collective-permute-start.25 = (bf16[256,256]{1,0:T(8,128)(2,1)S(1)}, bf16[256,256]{1,0:T(8,128)(2,1)S(1)}, u32[]{:S(2)}, u32[]{:S(2)}) collective-permute-start(bf16[256,256]{1,0:T(8,128)(2,1)S(1)} %get-tuple-element.262), channel_id=1, source_target_pairs={{0,4},{1,5},{2,6},{3,7},{4,0},{5,1},{6,2},{7,3},{8,12},{9,13},{10,... | collective-permute-start | bytes 393224 | tf_op jit(solution)/shard_map/grad_plane/ppermute | solution.py:554
  202.7 14.9 %collective-permute-start.16 = (bf16[256,1024]{1,0:T(8,128)(2,1)S(1)}, bf16[256,1024]{1,0:T(8,128)(2,1)S(1)}, u32[]{:S(2)}, u32[]{:S(2)}) collective-permute-start(bf16[256,1024]{1,0:T(8,128)(2,1)S(1)} %get-tuple-element.226), channel_id=1, source_target_pairs={{0,2},{1,3},{2,0},{3,1},{4,6},{5,7},{6,4},{7,5},{8,10},{9,11},{10,... | collective-permute-start | bytes 1572872 | tf_op jit(solution)/shard_map/mix_plane/ppermute | solution.py:554
  204.2 23.9 %collective-permute-start.17 = (bf16[256,1024]{1,0:T(8,128)(2,1)S(1)}, bf16[256,1024]{1,0:T(8,128)(2,1)S(1)}, u32[]{:S(2)}, u32[]{:S(2)}) collective-permute-start(bf16[256,1024]{1,0:T(8,128)(2,1)S(1)} %get-tuple-element.228), channel_id=1, source_target_pairs={{0,4},{1,5},{2,6},{3,7},{4,0},{5,1},{6,2},{7,3},{8,12},{9,13},{10,... | collective-permute-start | bytes 1572872 | tf_op jit(solution)/shard_map/mix_plane/ppermute | solution.py:554
  204.7 23.3 %collective-permute-start.18 = (bf16[256,1024]{1,0:T(8,128)(2,1)S(1)}, bf16[256,1024]{1,0:T(8,128)(2,1)S(1)}, u32[]{:S(2)}, u32[]{:S(2)}) collective-permute-start(bf16[256,1024]{1,0:T(8,128)(2,1)S(1)} %get-tuple-element.227), channel_id=1, source_target_pairs={{0,6},{1,7},{2,4},{3,5},{4,2},{5,3},{6,0},{7,1},{8,14},{9,15},{10,... | collective-permute-start | bytes 1572872 | tf_op jit(solution)/shard_map/mix_plane/ppermute | solution.py:554
  229.7 33.7 %collective-permute-start.20 = (bf16[256,1024]{1,0:T(8,128)(2,1)S(1)}, bf16[256,1024]{1,0:T(8,128)(2,1)S(1)}, u32[]{:S(2)}, u32[]{:S(2)}) collective-permute-start(bf16[256,1024]{1,0:T(8,128)(2,1)S(1)} %convert_element_type.275.refs_0_), channel_id=1, source_target_pairs={{0,16},{8,24},{16,0},{24,8},{1,17},{9,25},{17,1},{25,9},{2,18},{10... | collective-permute-start | bytes 1572872 | tf_op jit(solution)/shard_map/middle_row/ppermute | solution.py:568
  229.8 33.7 %collective-permute-start.19 = (bf16[256,1024]{1,0:T(8,128)(2,1)S(1)}, bf16[256,1024]{1,0:T(8,128)(2,1)S(1)}, u32[]{:S(2)}, u32[]{:S(2)}) collective-permute-start(bf16[256,1024]{1,0:T(8,128)(2,1)S(1)} %convert_element_type.275.refs_0_), channel_id=1, source_target_pairs={{0,8},{8,0},{16,24},{24,16},{1,9},{9,1},{17,25},{25,17},{2,10},{10... | collective-permute-start | bytes 1572872 | tf_op jit(solution)/shard_map/middle_row/ppermute | solution.py:568
  263.5 14.4 %collective-permute-start.23 = (bf16[256,1024]{1,0:T(8,128)(2,1)S(1)}, bf16[256,1024]{1,0:T(8,128)(2,1)S(1)}, u32[]{:S(2)}, u32[]{:S(2)}) collective-permute-start(bf16[256,1024]{1,0:T(8,128)(2,1)S(1)} %collective-permute-done.19.refs_1_), channel_id=1, source_target_pairs={{0,1},{1,0},{2,3},{3,2},{4,5},{5,4},{6,7},{7,6},{8,9},{9,8},{10,11... | collective-permute-start | bytes 1572872 | tf_op jit(solution)/shard_map/middle_row/ppermute | solution.py:551
  264.0 27.2 %collective-permute-start.30 = (bf16[2048,256]{1,0:T(8,128)(2,1)}, bf16[2048,256]{1,0:T(8,128)(2,1)}, u32[]{:S(2)}, u32[]{:S(2)}) collective-permute-start(bf16[2048,256]{1,0:T(8,128)(2,1)} %bitcast.19.refs_5_.refs_1_), channel_id=1, source_target_pairs={{0,4},{1,5},{2,6},{3,7},{4,0},{5,1},{6,2},{7,3},{8,12},{9,13},{10,... | collective-permute-start | bytes 3145736 | tf_op jit(solution)/shard_map/down_plane/ppermute | solution.py:554
  265.4 28.7 %collective-permute-start.29 = (bf16[2048,256]{1,0:T(8,128)(2,1)}, bf16[2048,256]{1,0:T(8,128)(2,1)}, u32[]{:S(2)}, u32[]{:S(2)}) collective-permute-start(bf16[2048,256]{1,0:T(8,128)(2,1)} %bitcast.19.refs_5_.refs_1_), channel_id=1, source_target_pairs={{0,2},{1,3},{2,0},{3,1},{4,6},{5,7},{6,4},{7,5},{8,10},{9,11},{10,... | collective-permute-start | bytes 3145736 | tf_op jit(solution)/shard_map/down_plane/ppermute | solution.py:554
  291.1 28.0 %collective-permute-start.28 = (bf16[1024,1024]{1,0:T(8,128)(2,1)}, bf16[1024,1024]{1,0:T(8,128)(2,1)S(1)}, u32[]{:S(2)}, u32[]{:S(2)}) collective-permute-start(bf16[1024,1024]{1,0:T(8,128)(2,1)} %all-gather.5.cloned.1.call-done.refs_0_), channel_id=1, source_target_pairs={{0,1},{1,0},{2,3},{3,2},{4,5},{5,4},{6,7},{7,6},{8,9},{9,8},{10,11... | collective-permute-start | bytes 6291464 | tf_op jit(solution)/shard_map/grad_row/ppermute | solution.py:551
  347.6 16.2 %collective-permute-start.41 = (bf16[1024,256]{1,0:T(8,128)(2,1)S(1)}, bf16[1024,256]{1,0:T(8,128)(2,1)S(1)}, u32[]{:S(2)}, u32[]{:S(2)}) collective-permute-start(bf16[1024,256]{1,0:T(8,128)(2,1)S(1)} %get-tuple-element.233), channel_id=1, source_target_pairs={{0,4},{1,5},{2,6},{3,7},{4,0},{5,1},{6,2},{7,3},{8,12},{9,13},{10,... | collective-permute-start | bytes 1572872 | tf_op jit(solution)/shard_map/down_grad/ppermute | solution.py:554
  349.2 16.4 %collective-permute-start.43 = (bf16[1024,256]{1,0:T(8,128)(2,1)S(1)}, bf16[1024,256]{1,0:T(8,128)(2,1)S(1)}, u32[]{:S(2)}, u32[]{:S(2)}) collective-permute-start(bf16[1024,256]{1,0:T(8,128)(2,1)S(1)} %get-tuple-element.234), channel_id=1, source_target_pairs={{0,2},{1,3},{2,0},{3,1},{4,6},{5,7},{6,4},{7,5},{8,10},{9,11},{10,... | collective-permute-start | bytes 1572872 | tf_op jit(solution)/shard_map/down_grad/ppermute | solution.py:554
  365.2 25.6 %collective-permute-start.42 = (bf16[2048,256]{1,0:T(8,128)(2,1)}, bf16[2048,256]{1,0:T(8,128)(2,1)}, u32[]{:S(2)}, u32[]{:S(2)}) collective-permute-start(bf16[2048,256]{1,0:T(8,128)(2,1)} %pad_maximum_fusion.3), channel_id=1, source_target_pairs={{0,2},{1,3},{2,0},{3,1},{4,6},{5,7},{6,4},{7,5},{8,10},{9,11},{10,... | collective-permute-start | bytes 3145736 | tf_op jit(solution)/shard_map/down_grad/ppermute | solution.py:554
  366.8 25.3 %collective-permute-start.44 = (bf16[2048,256]{1,0:T(8,128)(2,1)}, bf16[2048,256]{1,0:T(8,128)(2,1)}, u32[]{:S(2)}, u32[]{:S(2)}) collective-permute-start(bf16[2048,256]{1,0:T(8,128)(2,1)} %pad_maximum_fusion.4), channel_id=1, source_target_pairs={{0,4},{1,5},{2,6},{3,7},{4,0},{5,1},{6,2},{7,3},{8,12},{9,13},{10,... | collective-permute-start | bytes 3145736 | tf_op jit(solution)/shard_map/down_grad/ppermute | solution.py:554
  368.5 26.0 %collective-permute-start.39 = (bf16[256,1024]{1,0:T(8,128)(2,1)}, bf16[256,1024]{1,0:T(8,128)(2,1)}, u32[]{:S(2)}, u32[]{:S(2)}) collective-permute-start(bf16[256,1024]{1,0:T(8,128)(2,1)} %fusion.8), channel_id=1, source_target_pairs={{0,16},{8,24},{16,0},{24,8},{1,17},{9,25},{17,1},{25,9},{2,18},{10... | collective-permute-start | bytes 1572872 | tf_op jit(solution)/shard_map/unit_grad/ppermute | solution.py:568
  371.1 25.0 %collective-permute-start.38 = (bf16[256,1024]{1,0:T(8,128)(2,1)}, bf16[256,1024]{1,0:T(8,128)(2,1)}, u32[]{:S(2)}, u32[]{:S(2)}) collective-permute-start(bf16[256,1024]{1,0:T(8,128)(2,1)} %slice.426), channel_id=1, source_target_pairs={{0,8},{8,0},{16,24},{24,16},{1,9},{9,1},{17,25},{25,17},{2,10},{10... | collective-permute-start | bytes 1572872 | tf_op jit(solution)/shard_map/unit_grad/ppermute | solution.py:568
  404.5 14.9 %collective-permute-start.45 = (bf16[256,1024]{1,0:T(8,128)(2,1)}, bf16[256,1024]{1,0:T(8,128)(2,1)S(1)}, u32[]{:S(2)}, u32[]{:S(2)}) collective-permute-start(bf16[256,1024]{1,0:T(8,128)(2,1)} %get-tuple-element.155), channel_id=1, source_target_pairs={{0,2},{1,3},{2,0},{3,1},{4,6},{5,7},{6,4},{7,5},{8,10},{9,11},{10,... | collective-permute-start | bytes 1572872 | tf_op jit(solution)/shard_map/feed/ppermute | solution.py:554
  405.9 45.1 %collective-permute-start.49 = (bf16[256,1024]{1,0:T(8,128)(2,1)}, bf16[256,1024]{1,0:T(8,128)(2,1)}, u32[]{:S(2)}, u32[]{:S(2)}) collective-permute-start(bf16[256,1024]{1,0:T(8,128)(2,1)} %get-tuple-element.155), channel_id=1, source_target_pairs={{0,6},{1,7},{2,4},{3,5},{4,2},{5,3},{6,0},{7,1},{8,14},{9,15},{10,... | collective-permute-start | bytes 1572872 | tf_op jit(solution)/shard_map/feed/ppermute | solution.py:554
  406.3 44.7 %collective-permute-start.48 = (bf16[256,1024]{1,0:T(8,128)(2,1)}, bf16[256,1024]{1,0:T(8,128)(2,1)}, u32[]{:S(2)}, u32[]{:S(2)}) collective-permute-start(bf16[256,1024]{1,0:T(8,128)(2,1)} %get-tuple-element.155), channel_id=1, source_target_pairs={{0,4},{1,5},{2,6},{3,7},{4,0},{5,1},{6,2},{7,3},{8,12},{9,13},{10,... | collective-permute-start | bytes 1572872 | tf_op jit(solution)/shard_map/feed/ppermute | solution.py:554
  425.4 18.0 %collective-permute-start.46 = (bf16[512,1024]{1,0:T(8,128)(2,1)}, bf16[512,1024]{1,0:T(8,128)(2,1)}, u32[]{:S(2)}, u32[]{:S(2)}) collective-permute-start(bf16[512,1024]{1,0:T(8,128)(2,1)} %get-tuple-element.158), channel_id=1, source_target_pairs={{0,1},{1,0},{2,3},{3,2},{4,5},{5,4},{6,7},{7,6},{8,9},{9,8},{10,11... | collective-permute-start | bytes 3145736 | tf_op jit(solution)/shard_map/feed/ppermute | solution.py:551
  431.3 16.8 %collective-permute-start.47 = (bf16[512,1024]{1,0:T(8,128)(2,1)}, bf16[512,1024]{1,0:T(8,128)(2,1)S(1)}, u32[]{:S(2)}, u32[]{:S(2)}) collective-permute-start(bf16[512,1024]{1,0:T(8,128)(2,1)} %get-tuple-element.161), channel_id=1, source_target_pairs={{0,1},{1,0},{2,3},{3,2},{4,5},{5,4},{6,7},{7,6},{8,9},{9,8},{10,11... | collective-permute-start | bytes 3145736 | tf_op jit(solution)/shard_map/feed/ppermute | solution.py:551
  454.8 29.1 %collective-permute-start.50 = (bf16[1024,1024]{1,0:T(8,128)(2,1)}, bf16[1024,1024]{1,0:T(8,128)(2,1)}, u32[]{:S(2)}, u32[]{:S(2)}) collective-permute-start(bf16[1024,1024]{1,0:T(8,128)(2,1)} %constant_dynamic-update-slice_fusion.18.own_ref.d_own), channel_id=1, source_target_pairs={{0,1},{1,0},{2,3},{3,2},{4,5},{5,4},{6,7},{7,6},{8,9},{9,8},{10,11... | collective-permute-start | bytes 6291464 | tf_op jit(solution)/shard_map/middle_grad/ppermute | solution.py:551
  457.1 20.5 %collective-permute-start.51 = (bf16[1024,256]{1,0:T(8,128)(2,1)}, bf16[1024,256]{1,0:T(8,128)(2,1)}, u32[]{:S(2)}, u32[]{:S(2)}) collective-permute-start(bf16[1024,256]{1,0:T(8,128)(2,1)} %get-tuple-element.232), channel_id=1, source_target_pairs={{0,4},{1,5},{2,6},{3,7},{4,0},{5,1},{6,2},{7,3},{8,12},{9,13},{10,... | collective-permute-start | bytes 1572872 | tf_op jit(solution)/shard_map/gate_grad/ppermute | solution.py:554
  465.7 14.9 %collective-permute-start.52 = (bf16[1024,256]{1,0:T(8,128)(2,1)}, bf16[1024,256]{1,0:T(8,128)(2,1)}, u32[]{:S(2)}, u32[]{:S(2)}) collective-permute-start(bf16[1024,256]{1,0:T(8,128)(2,1)} %get-tuple-element.231), channel_id=1, source_target_pairs={{0,2},{1,3},{2,0},{3,1},{4,6},{5,7},{6,4},{7,5},{8,10},{9,11},{10,... | collective-permute-start | bytes 1572872 | tf_op jit(solution)/shard_map/gate_grad/ppermute | solution.py:554
  469.4 51.1 %all-to-all-start.3 = ((bf16[4,512,256]{2,1,0:T(8,128)(2,1)}), bf16[4,512,256]{2,1,0:T(8,128)(2,1)}, u32[]{:S(2)}, u32[]{:S(2)}) async-start(bf16[4,512,256]{2,1,0:T(8,128)(2,1)} %bitcast.77), calls=%async_computation.4 | async-start | bytes 2097152 | tf_op jit(solution)/shard_map/down_grad/all_to_all | solution.py:670
  473.7 148.2 %reduce-scatter.3.cloned.1.call-start = ((), (), s32[]{:S(2)}) async-start(), calls=%async_computation.10 | async-start | bytes 2621440 | tf_op jit(solution)/shard_map/feed/reduce_scatter | solution.py:795
  477.5 205.5 %reduce-scatter.5.cloned.1.call-start = ((), (), s32[]{:S(2)}) async-start(), calls=%async_computation.11 | async-start | bytes 5242880 | tf_op jit(solution)/shard_map/heads_grad/reduce_scatter | solution.py:819
  480.2 25.1 %collective-permute-start.53 = (bf16[2048,256]{1,0:T(8,128)(2,1)S(1)}, bf16[2048,256]{1,0:T(8,128)(2,1)S(1)}, u32[]{:S(2)}, u32[]{:S(2)}) collective-permute-start(bf16[2048,256]{1,0:T(8,128)(2,1)S(1)} %pad_maximum_fusion.5), channel_id=1, source_target_pairs={{0,2},{1,3},{2,0},{3,1},{4,6},{5,7},{6,4},{7,5},{8,10},{9,11},{10,... | collective-permute-start | bytes 3145736 | tf_op jit(solution)/shard_map/gate_grad/ppermute | solution.py:554
  482.1 24.7 %collective-permute-start.54 = (bf16[2048,256]{1,0:T(8,128)(2,1)S(1)}, bf16[2048,256]{1,0:T(8,128)(2,1)S(1)}, u32[]{:S(2)}, u32[]{:S(2)}) collective-permute-start(bf16[2048,256]{1,0:T(8,128)(2,1)S(1)} %pad_maximum_fusion.6), channel_id=1, source_target_pairs={{0,4},{1,5},{2,6},{3,7},{4,0},{5,1},{6,2},{7,3},{8,12},{9,13},{10,... | collective-permute-start | bytes 3145736 | tf_op jit(solution)/shard_map/gate_grad/ppermute | solution.py:554
  555.5 14.9 %collective-permute-start.56 = (bf16[1024,256]{1,0:T(8,128)(2,1)}, bf16[1024,256]{1,0:T(8,128)(2,1)}, u32[]{:S(2)}, u32[]{:S(2)}) collective-permute-start(bf16[1024,256]{1,0:T(8,128)(2,1)} %get-tuple-element.229), channel_id=1, source_target_pairs={{0,4},{1,5},{2,6},{3,7},{4,0},{5,1},{6,2},{7,3},{8,12},{9,13},{10,... | collective-permute-start | bytes 1572872 | tf_op jit(solution)/shard_map/up_grad/ppermute | solution.py:554
  559.7 59.3 %all-to-all-start.4 = ((bf16[4,512,256]{2,1,0:T(8,128)(2,1)}), bf16[4,512,256]{2,1,0:T(8,128)(2,1)}, u32[]{:S(2)}, u32[]{:S(2)}) async-start(bf16[4,512,256]{2,1,0:T(8,128)(2,1)} %bitcast.29), calls=%async_computation.6 | async-start | bytes 2097152 | tf_op jit(solution)/shard_map/gate_grad/all_to_all | solution.py:670
  564.2 15.2 %collective-permute-start.58 = (bf16[1024,256]{1,0:T(8,128)(2,1)}, bf16[1024,256]{1,0:T(8,128)(2,1)}, u32[]{:S(2)}, u32[]{:S(2)}) collective-permute-start(bf16[1024,256]{1,0:T(8,128)(2,1)} %get-tuple-element.230), channel_id=1, source_target_pairs={{0,2},{1,3},{2,0},{3,1},{4,6},{5,7},{6,4},{7,5},{8,10},{9,11},{10,... | collective-permute-start | bytes 1572872 | tf_op jit(solution)/shard_map/up_grad/ppermute | solution.py:554
  572.7 56.6 %collective-permute-start.57 = (bf16[2048,256]{1,0:T(8,128)(2,1)}, bf16[2048,256]{1,0:T(8,128)(2,1)}, u32[]{:S(2)}, u32[]{:S(2)}) collective-permute-start(bf16[2048,256]{1,0:T(8,128)(2,1)} %pad_maximum_fusion.7), channel_id=1, source_target_pairs={{0,2},{1,3},{2,0},{3,1},{4,6},{5,7},{6,4},{7,5},{8,10},{9,11},{10,... | collective-permute-start | bytes 3145736 | tf_op jit(solution)/shard_map/up_grad/ppermute | solution.py:554
  581.6 47.8 %collective-permute-start.59 = (bf16[2048,256]{1,0:T(8,128)(2,1)}, bf16[2048,256]{1,0:T(8,128)(2,1)}, u32[]{:S(2)}, u32[]{:S(2)}) collective-permute-start(bf16[2048,256]{1,0:T(8,128)(2,1)} %pad_maximum_fusion.8), channel_id=1, source_target_pairs={{0,4},{1,5},{2,6},{3,7},{4,0},{5,1},{6,2},{7,3},{8,12},{9,13},{10,... | collective-permute-start | bytes 3145736 | tf_op jit(solution)/shard_map/up_grad/ppermute | solution.py:554
  583.4 40.9 %collective-permute-start.63 = (bf16[256,1024]{1,0:T(8,128)(2,1)}, bf16[256,1024]{1,0:T(8,128)(2,1)}, u32[]{:S(2)}, u32[]{:S(2)}) collective-permute-start(bf16[256,1024]{1,0:T(8,128)(2,1)} %get-tuple-element.223), channel_id=1, source_target_pairs={{0,2},{1,3},{2,0},{3,1},{4,6},{5,7},{6,4},{7,5},{8,10},{9,11},{10,... | collective-permute-start | bytes 1572872 | tf_op jit(solution)/shard_map/first_plane/ppermute | solution.py:554
  583.4 43.9 %collective-permute-start.64 = (bf16[256,1024]{1,0:T(8,128)(2,1)}, bf16[256,1024]{1,0:T(8,128)(2,1)}, u32[]{:S(2)}, u32[]{:S(2)}) collective-permute-start(bf16[256,1024]{1,0:T(8,128)(2,1)} %get-tuple-element.225), channel_id=1, source_target_pairs={{0,4},{1,5},{2,6},{3,7},{4,0},{5,1},{6,2},{7,3},{8,12},{9,13},{10,... | collective-permute-start | bytes 1572872 | tf_op jit(solution)/shard_map/first_plane/ppermute | solution.py:554
  585.2 42.1 %collective-permute-start.65 = (bf16[256,1024]{1,0:T(8,128)(2,1)}, bf16[256,1024]{1,0:T(8,128)(2,1)}, u32[]{:S(2)}, u32[]{:S(2)}) collective-permute-start(bf16[256,1024]{1,0:T(8,128)(2,1)} %get-tuple-element.224), channel_id=1, source_target_pairs={{0,6},{1,7},{2,4},{3,5},{4,2},{5,3},{6,0},{7,1},{8,14},{9,15},{10,... | collective-permute-start | bytes 1572872 | tf_op jit(solution)/shard_map/first_plane/ppermute | solution.py:554
  638.8 34.4 %collective-permute-start.67 = (bf16[256,256]{1,0:T(8,128)(2,1)S(1)}, bf16[256,256]{1,0:T(8,128)(2,1)S(1)}, u32[]{:S(2)}, u32[]{:S(2)}) collective-permute-start(bf16[256,256]{1,0:T(8,128)(2,1)S(1)} %get-tuple-element.255), channel_id=1, source_target_pairs={{0,2},{1,3},{2,0},{3,1},{4,6},{5,7},{6,4},{7,5},{8,10},{9,11},{10,... | collective-permute-start | bytes 393224 | tf_op jit(solution)/shard_map/input_grad/ppermute | solution.py:554
  639.4 36.2 %collective-permute-start.68 = (bf16[256,256]{1,0:T(8,128)(2,1)S(1)}, bf16[256,256]{1,0:T(8,128)(2,1)S(1)}, u32[]{:S(2)}, u32[]{:S(2)}) collective-permute-start(bf16[256,256]{1,0:T(8,128)(2,1)S(1)} %get-tuple-element.254), channel_id=1, source_target_pairs={{0,4},{1,5},{2,6},{3,7},{4,0},{5,1},{6,2},{7,3},{8,12},{9,13},{10,... | collective-permute-start | bytes 393224 | tf_op jit(solution)/shard_map/input_grad/ppermute | solution.py:554
  641.0 38.2 %all-to-all-start.5 = ((bf16[4,512,256]{2,1,0:T(8,128)(2,1)}), bf16[4,512,256]{2,1,0:T(8,128)(2,1)S(1)}, u32[]{:S(2)}, u32[]{:S(2)}) async-start(bf16[4,512,256]{2,1,0:T(8,128)(2,1)} %bitcast.30), calls=%async_computation.7 | async-start | bytes 2097152 | tf_op jit(solution)/shard_map/up_grad/all_to_all | solution.py:670
  645.5 16.6 %collective-permute-start.73 = (f32[2,512]{1,0:T(2,128)S(1)}, f32[2,512]{1,0:T(2,128)S(1)}, u32[]{:S(2)}, u32[]{:S(2)}) collective-permute-start(f32[2,512]{1,0:T(2,128)S(1)} %bitcast.99), channel_id=1, source_target_pairs={{0,8},{8,0},{16,24},{24,16},{1,9},{9,1},{17,25},{25,17},{2,10},{10... | collective-permute-start | bytes 12296 | tf_op jit(solution)/shard_map/gains/ppermute | solution.py:568
  647.6 23.2 %collective-permute-start.74 = (f32[2,512]{1,0:T(2,128)S(1)}, f32[2,512]{1,0:T(2,128)S(1)}, u32[]{:S(2)}, u32[]{:S(2)}) collective-permute-start(f32[2,512]{1,0:T(2,128)S(1)} %bitcast.98), channel_id=1, source_target_pairs={{0,16},{8,24},{16,0},{24,8},{1,17},{9,25},{17,1},{25,9},{2,18},{10... | collective-permute-start | bytes 12296 | tf_op jit(solution)/shard_map/gains/ppermute | solution.py:568
  650.0 21.4 %collective-permute-start.75 = (f32[2,512]{1,0:T(2,128)S(1)}, f32[2,512]{1,0:T(2,128)S(1)}, u32[]{:S(2)}, u32[]{:S(2)}) collective-permute-start(f32[2,512]{1,0:T(2,128)S(1)} %bitcast.97), channel_id=1, source_target_pairs={{0,24},{8,16},{16,8},{24,0},{1,25},{9,17},{17,9},{25,1},{2,26},{10... | collective-permute-start | bytes 12296 | tf_op jit(solution)/shard_map/gains/ppermute | solution.py:568
  (134 other events, 1128.4 us)
Sparse Core Ops, SparseCore 0:
  114.8 46.3 all-gather.2
  197.3 60.2 all-gather.4
  477.6 54.4 reduce-scatter.2
  545.5 90.9 reduce-scatter.4

commit v11 on v10

--- a/solution.py
+++ b/solution.py
@@ -19,8 +19,47 @@
 VMEM_BYTES = 56 * 1024 * 1024
 
 
+COST_RATE = 1e10
+ORDER = {
+    "gate_row": (),
+    "up_row": (0,),
+    "grad_plane": (0,),
+    "out_row": (0,),
+    "down_row": (0,),
+    "grad_row": (),
+    "project": (),
+    "attend": (0, 2),
+    "mix": (1, 3, 5),
+    "mix_plane": (1,),
+    "middle_row": (3,),
+    "down_plane": (2,),
+    "activate": (),
+    "activate_more": (1,),
+    "grad_core": (0, 1),
+    "units_back": (0,),
+    "units_back_more": (0, 2),
+    "down_outer": (0,),
+    "d_low": (1,),
+    "feed": (0, 1),
+    "feed_row": (0,),
+    "gate_outer": (1,),
+    "up_outer": (),
+    "gate_plane_back": (0,),
+    "fold": (0, 1, 2),
+    "attend_back": (0,),
+    "feed_end": (0,),
+    "gate_second": (0,),
+    "heads_outer": (0, 1),
+    "first_grad": (0,),
+    "up_plane_back": (3,),
+    "block_out": (0, 3),
+    "input_grad": (0,),
+    "gain_dots": (),
+}
+
+
 def lasts(microseconds):
-    return pl.CostEstimate(flops=int(microseconds * 1.15e9), bytes_accessed=1, transcendentals=0)
+    return pl.CostEstimate(flops=int(microseconds * COST_RATE), bytes_accessed=1, transcendentals=0)
 
 
 def nn(left, right):
@@ -65,43 +104,39 @@
     return pl.BlockSpec((block, a.shape[1]), lambda i: (i, 0))
 
 
-def project_kernel(feat, starts, own_ref, other_ref, *refs):
-    weights, (cos_ref, front_ref, back_ref), outs = refs[:-7], refs[-7:-4], refs[-4:]
-    scale = norm_scale(jnp.concatenate([own_ref[...], other_ref[...]], axis=1))
+def project_kernel(feat, own_ref, other_ref, weight_ref, cos_ref, front_ref, back_ref, *outs):
+    values = weave(own_ref[...], other_ref[...], feat)
+    scale = norm_scale(values)
     outs[3][...] = scale
     heads = outs[0].shape[1]
-    picks = [pl.ds(pl.multiple_of(starts[i] * feat, feat), feat) for i in range(len(weights))]
-    values = jnp.concatenate([ref[:, pick] for pick in picks for ref in (own_ref, other_ref)], axis=1)
     times = heads // cos_ref.shape[1]
     cosine, front, back = (
         jnp.concatenate([ref[...]] * times, axis=1) for ref in (cos_ref, front_ref, back_ref)
     )
     for at, ref in enumerate(outs[:3]):
-        columns = slice(at * heads, (at + 1) * heads)
-        result = nn(values, jnp.concatenate([w[:, columns] for w in weights], axis=0)) * scale
+        result = nn(values, weight_ref[:, at * heads : (at + 1) * heads]) * scale
         if at < 2:
             result = spin(result, cosine, front, back)
         ref[...] = result.astype(BF16)
 
 
-def project(feat, starts, own, other, weights, cosine, front, back):
+def project(feat, own, other, weight, cosine, front, back):
     tokens = own.shape[0]
-    heads = weights[0].shape[1] // 3
+    heads = weight.shape[1] // 3
     block = 256
     result = jax.ShapeDtypeStruct((tokens, heads), BF16)
     scale = jax.ShapeDtypeStruct((tokens, 1), F32)
     return pl.pallas_call(
         functools.partial(project_kernel, feat),
         grid=(tokens // block,),
-        in_specs=[pl.BlockSpec(memory_space=pltpu.SMEM), row_spec(block, own), row_spec(block, other)]
-        + [whole_spec(w) for w in weights]
+        in_specs=[row_spec(block, own), row_spec(block, other), whole_spec(weight)]
         + [row_spec(block, cosine)] * 3,
         out_specs=[row_spec(block, result)] * 3 + [row_spec(block, scale)],
         out_shape=[result] * 3 + [scale],
         compiler_params=pltpu.CompilerParams(vmem_limit_bytes=40 * 1024 * 1024),
         cost_estimate=lasts(7),
         name="project",
-    )(starts, own, other, *weights, cosine, front, back)
+    )(own, other, weight, cosine, front, back)
 
 
 def unfold_kernel(feat, joined, *refs):
@@ -294,7 +329,7 @@
     )(starts, *owns, *others, *rights)
 
 
-def heads_outer_kernel(x_own, x_other, d_own, d_other, dq_ref, dk_ref, dv_ref, mixed_ref, scale_ref, weight_ref, out_ref, dot_ref):
+def heads_outer_kernel(core_ref, x_own, x_other, parts_ref, dq_ref, dk_ref, dv_ref, mixed_ref, scale_ref, weight_ref, out_ref, dot_ref):
     part = mixed_ref.shape[1]
     left = jnp.concatenate([x_own[...], x_other[...]], axis=1)
     dots = None
@@ -305,18 +340,30 @@
         term = jnp.sum(result * weight_ref[:, columns].astype(F32), axis=1, keepdims=True)
         dots = term if dots is None else dots + term
     dot_ref[...] = dots
-    left = jnp.concatenate([d_own[...], d_other[...]], axis=1)
+    core = core_ref[0]
+    left = jnp.concatenate(
+        [
+            jnp.concatenate([parts_ref[2 * i + core], parts_ref[2 * i + 1 - core]], axis=1)
+            for i in range(parts_ref.shape[0] // 2)
+        ],
+        axis=0,
+    )
     out_ref[:, 3 * part :] = tn(left, mixed_ref[...]).astype(BF16)
 
 
-def heads_outer(feat, x_own, x_other, d_own, d_other, dq, dk, dv, mixed, scale, weight):
+def heads_outer(feat, core, x_own, x_other, parts, dq, dk, dv, mixed, scale, weight):
     tokens, half = x_own.shape
     part = mixed.shape[1]
     side = pl.BlockSpec((tokens, feat), lambda i: (0, i))
     return pl.pallas_call(
         heads_outer_kernel,
         grid=(half // feat,),
-        in_specs=[side] * 4
+        in_specs=[
+            pl.BlockSpec(memory_space=pltpu.SMEM),
+            side,
+            side,
+            pl.BlockSpec(parts.shape[:2] + (feat,), lambda i: (0, 0, i)),
+        ]
         + [whole_spec(a) for a in (dq, dk, dv, mixed, scale)]
         + [row_spec(2 * feat, weight)],
         out_specs=[pl.BlockSpec((2 * feat, 4 * part), lambda i: (i, 0)), pl.BlockSpec((2 * feat, 1), lambda i: (i, 0))],
@@ -327,7 +374,7 @@
         compiler_params=pltpu.CompilerParams(vmem_limit_bytes=40 * 1024 * 1024),
         cost_estimate=lasts(9.4),
         name="heads_outer",
-    )(x_own, x_other, d_own, d_other, dq, dk, dv, mixed, scale, weight)
+    )(core, x_own, x_other, parts, dq, dk, dv, mixed, scale, weight)
 
 
 def finish_kernel(scaled, core_ref, part_ref, gain_ref, *outs):
@@ -359,24 +406,29 @@
     )(core, part, gain)
 
 
-def fold_kernel(feat, own_ref, other_ref, weight_ref, out_ref):
-    out_ref[...] = nn(weave(own_ref[...], other_ref[...], feat), weight_ref[...]).astype(BF16)
-
-
-def fold(feat, own, other, weight):
-    tokens = own.shape[0]
-    block = 256
-    result = jax.ShapeDtypeStruct((tokens, weight.shape[1]), BF16)
+def fold_kernel(feat, core_ref, parts_ref, weight_ref, out_ref):
+    core = core_ref[0]
+    values = weave(parts_ref[core], parts_ref[1 - core], feat)
+    out_ref[...] = nn(values, weight_ref[...]).astype(BF16)
+
+
+def fold(feat, core, parts, weight):
+    count, tokens, half = parts.shape
+    result = jax.ShapeDtypeStruct((count // 2 * tokens, weight.shape[1]), BF16)
     return pl.pallas_call(
         functools.partial(fold_kernel, feat),
-        grid=(tokens // block,),
-        in_specs=[row_spec(block, own), row_spec(block, other), whole_spec(weight)],
-        out_specs=row_spec(block, result),
+        grid=(count // 2,),
+        in_specs=[
+            pl.BlockSpec(memory_space=pltpu.SMEM),
+            pl.BlockSpec((2, tokens, half), lambda i: (i, 0, 0)),
+            whole_spec(weight),
+        ],
+        out_specs=row_spec(tokens, result),
         out_shape=result,
         compiler_params=pltpu.CompilerParams(vmem_limit_bytes=40 * 1024 * 1024),
         cost_estimate=lasts(3.5),
         name="fold",
-    )(own, other, weight)
+    )(core, parts, weight)
 
 
 def allowed_block(start_row, key_base, query_base, keys, queries):
@@ -567,12 +619,11 @@
     def row_swap(a, step):
         return lax.ppermute(a, "row", [(i, i ^ step) for i in range(rows)])
 
-    def gather_row(a, held=()):
+    def gather_row(a):
         got, bit = {0: a}, rows // 2
         while bit:
             for step in list(got):
-                came = row_swap(got[step], bit)
-                got[step ^ bit] = after(came, *held) if 2 * bit == rows else came
+                got[step ^ bit] = row_swap(got[step], bit)
             bit //= 2
         return [got[step] for step in range(rows)]
 
@@ -591,6 +642,13 @@
 
     def after(value, *others):
         return lax.optimization_barrier((value,) + others)[0]
+
+    def dep(key, value, *groups):
+        chosen = []
+        for i in ORDER.get(key, ()):
+            group = groups[i]
+            chosen += list(group) if isinstance(group, (list, tuple)) else [group]
+        return after(value, *chosen) if chosen else value
 
     def put_rows(pieces):
         whole = jnp.zeros((tokens,) + pieces[0].shape[1:], pieces[0].dtype)
@@ -662,19 +720,12 @@
     def plane_second(pieces, *hold):
         total = pieces[0].astype(F32)
         for s, piece in enumerate(pieces[1:], 1):
-            total = total + after(plane_swap(piece, s), *hold).astype(F32)
+            total = total + (after(plane_swap(piece, s), *hold) if hold else plane_swap(piece, s)).astype(F32)
         return total.astype(BF16)
 
     def give_back(total):
         total = total.reshape(rows, 2 * feat, total.shape[1])
         return lax.all_to_all(total, "row", split_axis=0, concat_axis=0, tiled=True)
-
-    def join_rows(pieces):
-        size = pieces[0].shape[0]
-        whole = jnp.zeros((rows * size, pieces[0].shape[1]), BF16)
-        for step, piece in enumerate(pieces):
-            whole = lax.dynamic_update_slice_in_dim(whole, piece, (row ^ step) * size, 0)
-        return whole
 
     starts = jnp.stack([row ^ s for s in range(rows)])
     cores = core.reshape(1)
@@ -691,34 +742,39 @@
         x_own = put_feats(spread(inputs))
         x_other = core_swap(x_own)
     with jax.named_scope("qkv_row"):
-        qkv_list = gather_row(
+        qkv_full = lax.all_gather(
             jnp.concatenate(
                 [scaled(w, gain_one) for w in (query_weight, key_weight, value_weight)], axis=1
             ),
-            (cosine, front, back, start_row, up_cut, down_cut, out_block),
+            "row",
+            axis=0,
+            tiled=True,
         )
     with jax.named_scope("grad_plane"):
-        g_part = to_parts(after(out_grad, *qkv_list))
+        g_part = to_parts(dep("grad_plane", out_grad, x_own, x_other))
     with jax.named_scope("gate_row"):
-        gate_whole = exchange(cut(scaled(gate_weight, gain_two)))
+        gate_whole = exchange(dep("gate_row", cut(scaled(gate_weight, gain_two)), x_own))
+        gate_whole = after(gate_whole, g_part, cosine, front, back, start_row, up_cut, down_cut, out_block)
+    with jax.named_scope("up_row"):
+        up_whole = exchange(dep("up_row", up_cut, gate_whole, x_other, qkv_full))
     with jax.named_scope("out_row"):
-        out_full = lax.all_gather(after(out_block, *qkv_list), "row", axis=0, tiled=True)
-    with jax.named_scope("up_row"):
-        up_whole = exchange(after(up_cut, gate_whole))
+        out_full = lax.all_gather(dep("out_row", out_block, x_own, gate_whole), "row", axis=0, tiled=True)
     with jax.named_scope("down_row"):
-        down_whole = exchange(after(down_cut, up_whole))
+        down_whole = exchange(dep("down_row", down_cut, up_whole, qkv_full, out_full, g_part))
+    with jax.named_scope("grad_row"):
+        g_own = lax.all_gather(dep("grad_row", g_part, gate_whole, qkv_full, up_whole, out_full), "row", axis=0, tiled=True)
     with jax.named_scope("gate_plane"):
         gates = spread_weights(gate_whole)
-    query, key, value, scale_one = project(
-        feat, starts, x_own, x_other, qkv_list, cosine, front, back
-    )
-    qkv_full = join_rows([after(a, query) for a in qkv_list])
-    mixed, logs = attend(after(query, gates[1], gates[2], up_whole), key, value, start_row)
-    with jax.named_scope("grad_row"):
-        g_own = lax.all_gather(after(g_part, mixed), "row", axis=0, tiled=True)
     with jax.named_scope("up_plane"):
         ups = spread_weights(up_whole)
-    mixed = after(mixed, gates[3], ups[1], ups[2], down_whole)
+    query, key, value, scale_one = project(
+        feat, dep("project", x_own, gates[1:3], gates[3:], up_whole, g_part, ups[1:3]), x_other, qkv_full, cosine, front, back
+    )
+    mixed, logs = attend(
+        dep("attend", query, gates[1:3], gates[3:], up_whole, g_part, ups[1:3], ups[3:], out_full, down_whole),
+        key, value, start_row,
+    )
+    mixed_in = dep("mix", mixed, gates[1:3], gates[3:], up_whole, ups[1:3], ups[3:], down_whole, g_part)
 
     def join_cores(own, other):
         return (own.astype(F32) + core_swap(other).astype(F32)).astype(BF16)
@@ -730,34 +786,39 @@
         return total
 
     with jax.named_scope("mix_plane"):
-        own, other = unfold(feat, "mix", [mixed], [out_full])
-        middle = token_part(x_own, 0).astype(F32) + scatter_parts(join_cores(after(own, ups[3]), other))
-    middle_low = middle.astype(BF16)
+        own, other = unfold(feat, "mix", [mixed_in], [out_full])
+        middle = token_part(x_own, 0).astype(F32) + scatter_parts(join_cores(dep("mix_plane", own, ups[1:3], ups[3:], down_whole, gates[3:], g_part), other))
+    middle_low = dep("middle_row", middle.astype(BF16), ups[1:3], ups[3:], down_whole, g_own)
     with jax.named_scope("middle_row"):
         m_list = gather_row(middle_low)
         m_others = [core_swap(m) for m in m_list]
     with jax.named_scope("down_plane"):
-        downs = spread_weights(down_whole)
+        downs = spread_weights(dep("down_plane", down_whole, ups[1:3], ups[3:], middle_low, m_list[1:3], mixed))
     square = jnp.sum(middle * middle, axis=1, keepdims=True)
     square = square + core_swap(square)
     scale_mid = lax.rsqrt(square / width + EPS)
 
-    m_list = list(lax.optimization_barrier(tuple(m_list)))
     pairs = [slice(at, at + 2) for at in range(0, rows, 2)]
-    found = [
-        activate(feat, [after(a, *(downs[1:3] if pair.start else ())) for a in m_list[pair]], m_others[pair], gates, ups)
-        for pair in pairs
-    ]
+    found = []
+    for pair in pairs:
+        key_at = "activate_more" if pair.start else "activate"
+        first = dep(key_at, m_list[pair.start], m_list, downs[1:3], downs[3:], g_own, ups)
+        found.append(activate(feat, [first, m_list[pair.start + 1]], m_others[pair], gates, ups))
     hiddens = [f[0] for f in found]
     with jax.named_scope("grad_row"):
-        g_own = after(g_own, hiddens[0])
+        g_own = dep("grad_core", g_own, m_others, hiddens[0], hiddens[-1])
         g_other = core_swap(g_own)
-    parts, scaled_grads, held, down_parts = [None] * rows, [None] * len(pairs), hiddens, None
+    parts, scaled_grads, down_parts = [None] * rows, [None] * len(pairs), None
+    down_middle = None
     for at in reversed(range(len(pairs))):
         with jax.named_scope("unit_grad"):
             _, slope_gate, slope_up, scale = found[at]
+            if down_parts is None:
+                slope_gate = dep("units_back", slope_gate, hiddens, downs)
+            else:
+                slope_gate = dep("units_back_more", slope_gate, down_parts[:1], sent, low_kept, down_middle[1:])
             gate_grad, up_grad, own, other = units_back(
-                feat, starts[pairs[at]], g_own, g_other, after(slope_gate, *held), slope_up, scale, gates, ups, downs
+                feat, starts[pairs[at]], g_own, g_other, slope_gate, slope_up, scale, gates, ups, downs
             )
             scaled_grads[at] = gate_grad, up_grad
             low = own.astype(F32) + core_swap(other).astype(F32)
@@ -766,14 +827,14 @@
         if down_parts is None:
             with jax.named_scope("down_grad"):
                 down_parts = outer(
-                    feat, "down_outer", starts, [g_own], [g_other], [after(h, sent) for h in hiddens], places
+                    feat, "down_outer", starts, [g_own], [g_other], [dep("down_outer", h, sent, hiddens) for h in hiddens], places
                 )
-            held = down_parts[:1]
-        held = *held, parts[2 * at].astype(BF16)
+                down_middle = plane_first(down_parts)
+        low_kept = parts[2 * at].astype(BF16)
     with jax.named_scope("unit_grad"):
         unit_grad = reduce_row(parts, 2)
     with jax.named_scope("down_grad"):
-        down_total = plane_second(plane_first(down_parts))
+        down_total = plane_second(down_middle)
         down_blocks = give_back(down_total)
 
     unit_mid = middle * scale_mid
@@ -781,59 +842,56 @@
     dot_two = dot_two + core_swap(dot_two)
     middle_grad = g_part.astype(F32) + scale_mid * (unit_grad - unit_mid * (dot_two / width))
 
-    d_low = after(middle_grad.astype(BF16), down_total)
+    d_low = dep("d_low", middle_grad.astype(BF16), down_middle[1:], down_total)
+    with jax.named_scope("middle_grad"):
+        d_parts = lax.all_gather(d_low, "col")
     with jax.named_scope("feed"):
-        pieces = spread(d_low)
-        kept = [unfold(feat, "feed", [after(h, pieces[1])], downs) for h in hiddens]
-        shares = jnp.zeros((rows * quarter, half), BF16)
-        for pair, (own, other) in zip(pairs, kept):
-            low = (own.astype(F32) + core_swap(other).astype(F32)).astype(BF16)
-            for i in range(2):
-                shares = lax.dynamic_update_slice_in_dim(
-                    shares, low[i * quarter : (i + 1) * quarter], starts[pair.start + i] * quarter, 0
-                )
-        feed = lax.psum_scatter(after(shares, d_low), "row", scatter_dimension=0, tiled=True)
-    gate_parts = outer(feat, "gate_outer", starts, m_list, m_others, [after(a, d_low) for a, _ in scaled_grads], places)
-    up_parts = outer(feat, "up_outer", starts, m_list, m_others, [after(a, d_low) for _, a in scaled_grads], places)
-    with jax.named_scope("middle_grad"):
-        d_own = put_rows(
-            pieces[:2] + [after(a, gate_parts[0], up_parts[0], shares) for a in pieces[2:]]
-        )
-        d_other = core_swap(d_own)
-    mixed_grad = fold(feat, d_own, d_other, out_full)
+        kept = [unfold(feat, "feed", [dep("feed", h, low_kept, d_low)], downs) for h in hiddens]
+        shares = []
+        for own, other in kept:
+            low = dep("feed_row", (own.astype(F32) + core_swap(other).astype(F32)).astype(BF16), d_low)
+            shares += [low[:quarter], low[quarter:]]
+        sent = []
+        for at in range(0, rows, 2):
+            sent.append(shares[at].astype(F32) + row_swap(shares[at + 1], 1).astype(F32))
+            shares[at] = sent[-1]
+        feed = reduce_row(shares, 2)
+    gate_parts = outer(feat, "gate_outer", starts, m_list, m_others, [dep("gate_outer", a, low_kept, d_low, [own for own, _ in kept]) for a, _ in scaled_grads], places)
+    up_parts = outer(feat, "up_outer", starts, m_list, m_others, [dep("up_outer", a, low_kept, d_low, [own for own, _ in kept], gate_parts[:1]) for _, a in scaled_grads], places)
     with jax.named_scope("gate_grad"):
-        gate_middle = plane_first([after(a, d_own) for a in gate_parts])
+        gate_middle = plane_first([dep("gate_plane_back", a, d_low, d_parts) for a in gate_parts])
+    mixed_grad = fold(feat, cores, dep("fold", d_parts, gate_parts[:1], up_parts[:1], sent, gate_middle[1:], down_total), out_full)
     query_grad, key_grad, value_grad = attend_back(
-        query, key, value, mixed, after(mixed_grad, *gate_middle), start_row, logs, cosine, front, back
+        query, key, value, mixed, dep("attend_back", mixed_grad, gate_middle[1:], down_blocks, feed), start_row, logs, cosine, front, back
     )
     with jax.named_scope("feed"):
-        feed_low = (middle + after(feed, query_grad).astype(F32)).astype(BF16)
+        feed_low = (middle + dep("feed_end", feed, query_grad).astype(F32)).astype(BF16)
     with jax.named_scope("gate_grad"):
-        gate_total = plane_second(gate_middle, query_grad)
+        gate_total = plane_second(gate_middle, *((query_grad,) if ORDER.get("gate_second") else ()))
         gate_blocks = give_back(gate_total)
-    query_grad = after(query_grad, down_blocks, gate_total)
+    heads_in = dep("heads_outer", query_grad, down_blocks, gate_total, feed_low, gate_middle[1:])
     heads_part, gain_dots = heads_outer(
-        feat, x_own, x_other, d_own, d_other, query_grad, key_grad, value_grad, mixed, scale_one, qkv_full
+        feat, cores, x_own, x_other, d_parts, heads_in, key_grad, value_grad, mixed, scale_one, qkv_full
     )
     with jax.named_scope("heads_grad"):
         heads_blocks = lax.psum_scatter(heads_part, "row", scatter_dimension=0, tiled=True)
     with jax.named_scope("first_plane"):
         first_low = join_cores(
-            *unfold(feat, "first_grad", [after(query_grad, heads_part), key_grad, value_grad], [qkv_full])
+            *unfold(feat, "first_grad", [dep("first_grad", query_grad, heads_part, gate_total), key_grad, value_grad], [qkv_full])
         )
         first_unit_grad = scatter_parts(first_low)
     with jax.named_scope("up_grad"):
-        up_total = plane_second(plane_first([after(a, gate_total, first_low) for a in up_parts]))
+        up_total = plane_second(plane_first([dep("up_plane_back", a, gate_total, heads_part, first_low, gate_middle[1:]) for a in up_parts]))
         up_blocks = give_back(up_total)
     with jax.named_scope("block_out"):
-        block_out = to_home(after(feed_low, up_total))
+        block_out = to_home(dep("block_out", feed_low, up_total, gate_total, heads_part, first_low))
     scale_first = token_part(scale_one, 0)
     unit_first = token_part(x_own, 0).astype(F32) * scale_first
     dot_one = jnp.sum(first_unit_grad * unit_first, axis=1, keepdims=True)
     dot_one = dot_one + core_swap(dot_one)
     with jax.named_scope("input_grad"):
         input_grad = to_home(
-            (after(middle_grad, up_total) + scale_first * (first_unit_grad - unit_first * (dot_one / width))).astype(BF16)
+            (dep("input_grad", middle_grad, up_total, gate_blocks) + scale_first * (first_unit_grad - unit_first * (dot_one / width))).astype(BF16)
         )
 
     def row_dots(w, d):
@@ -841,7 +899,7 @@
 
     with jax.named_scope("gains"):
         dots = jnp.stack(
-            [gain_dots[:, 0], row_dots(gates[0], gate_total) + row_dots(ups[0], up_total)]
+            [gain_dots[:, 0], row_dots(dep("gain_dots", gates[0], heads_part, up_total), gate_total) + row_dots(ups[0], up_total)]
         ).reshape(2, rows, 2, feat)
         dots = sum_cols(jnp.where(core == 0, dots, dots[:, :, ::-1])).transpose(1, 0, 2, 3)
         dots = dots.reshape(rows, 2, 2 * feat)
@@ -854,7 +912,7 @@
     (gate_weight_grad,) = finish(cores, gate_blocks, gain_two, 1)
     (up_weight_grad,) = finish(cores, up_blocks, gain_two, 1)
     heads_blocks = after(
-        heads_blocks, down_weight_grad, gate_weight_grad, up_weight_grad, second_gain_grad, input_grad
+        heads_blocks, down_weight_grad, gate_weight_grad, up_weight_grad, second_gain_grad, input_grad, block_out
     )
     query_weight_grad, key_weight_grad, value_weight_grad, out_weight_grad = finish(
         cores, heads_blocks[None], gain_one, 3, 4

time: 701 us -> 656 us (0.936)
  local copies, waits for them, and re-layouts: 97.5 us -> 67.2 us
    all_to_all x3, waiting for transfers between devices: 43.1 us -> 0.01 us  [give_back(): return lax.all_to_all(total, 'row', split_axis=0, concat_axis=0, tiled=True)]
    all_to_all x3, waiting for transfers between devices: 29.3 us -> 50.5 us  [exchange(): got = lax.all_to_all(pieces, 'row', split_axis=0, concat_axis=0, tiled=True)]
    ppermute x45 -> x42, waiting for transfers between devices: 100 us -> 120 us  [plane_swap(): return lax.ppermute(a, 'col', [(i, i ^ 2 * step) for i in range(cols)])]
    dynamic_update_slice x8 -> x0, local copies, waits for them, and re-layouts: 11.7 us -> none  [the longest x4 8.36 us: join_rows(): lax.dynamic_update_slice_in_dim(whole, piece, (row ^ step) * size, 0)]
    ppermute x16 -> x15, waiting for transfers between devices: 8.23 us -> 1.13 us  [core_swap(): return lax.ppermute(a, 'col', [(i, i ^ 1) for i in range(cols)])]
    ppermute x45 -> x42, starting transfers between devices: 52.7 us -> 46.1 us  [plane_swap(): return lax.ppermute(a, 'col', [(i, i ^ 2 * step) for i in range(cols)])]
    unnamed x231 -> x217, local copies, waits for them, and re-layouts: 42.8 us -> 42.2 us
  transfers between devices with their start and end apart: 86 -> 83, of which waited for: 35 -> 29; matrix products, arithmetic and copies ran while one was open for 17% -> 14% of each run, Pallas kernels for 16% -> 17%
where the time goes in v11:
time: 656 us; the launch traced here: 648 us
  waiting for transfers between devices  275 us (42%)
  Pallas kernels  132 us (20%)
  starting transfers between devices  94.8 us (14%)
  local copies, waits for them, and re-layouts  67.2 us (10%)
  other arithmetic  63.6 us (10%)
  between operations  15.5 us (2%)
    ppermute x42, waiting for transfers between devices, plane_swap(): return lax.ppermute(a, 'col', [(i, i ^ 2 * step) for i in range(cols)])  120 us
    ppermute x12, waiting for transfers between devices, row_swap(): return lax.ppermute(a, 'row', [(i, i ^ step) for i in range(rows)])  104 us
    all_to_all x3, waiting for transfers between devices, exchange(): got = lax.all_to_all(pieces, 'row', split_axis=0, concat_axis=0, tiled=True)  50.5 us
    ppermute x42, starting transfers between devices, plane_swap(): return lax.ppermute(a, 'col', [(i, i ^ 2 * step) for i in range(cols)])  46.1 us
    unnamed x217, local copies, waits for them, and re-layouts  42.2 us
    pallas_call x4, Pallas kernels, unfold(): pl.pallas_call(functools.partial(unfold_kernel, feat, len(lefts)), grid=(...  24.8 us
    pallas_call x2, Pallas kernels, units_back(): pl.pallas_call(functools.partial(units_back_kernel, feat, parts, count),...  21.6 us
    pallas_call x3, Pallas kernels, outer(): pl.pallas_call(functools.partial(outer_kernel, len(owns), count), grid=(h...  19.8 us
  transfers between devices with their start and end apart: 83, of which 29 were waited for; matrix products, arithmetic and copies ran while one was open for 14% of the time, Pallas kernels for 17%

profile of v11, /device:TPU:0, one launch (start us, length us, event | category | flops | bytes accessed | tf_op | source)
XLA Modules:
  0.0 648.2 jit_solution(15545493698760312975)
XLA Ops:
  7.2 3.0 collective-permute-start
  19.5 5.3 all-to-all-start
  27.3 2.9 multiply_sine_fusion
  50.2 3.4 collective-permute-done.6
  54.2 23.6 %all-to-all-done = bf16[4,512,256]{2,1,0:T(8,128)(2,1)S(1)} async-done(((bf16[4,512,256]{2,1,0:T(8,128)(2,1)}), bf16[4,512,256]{2,1,0:T(8,128)(2,1)S(1)}, u32[]{:S(2)}, u32[]{:S(2)}) %all-to-all-start) | async-done | bytes 1048608 | tf_op jit(solution)/shard_map/gate_row/all_to_all | solution.py:694
  77.8 4.2 all-to-all-start.1
  85.2 16.8 %collective-permute-done.8.refs_8_.refs_11_ = bf16[2048,256]{1,0:T(8,128)(2,1)S(1)} collective-permute-done((bf16[2048,256]{1,0:T(8,128)(2,1)S(1)}, bf16[2048,256]{1,0:T(8,128)(2,1)S(1)}, u32[]{:S(2)}, u32[]{:S(2)}) %collective-permute-start.8) | collective-permute-done | bytes 1048608 | tf_op jit(solution)/shard_map/gate_plane/ppermute | solution.py:606
  102.8 2.4 collective-permute-start.9
  108.0 14.4 %all-to-all-done.1 = bf16[4,512,256]{2,1,0:T(8,128)(2,1)} async-done(((bf16[4,512,256]{2,1,0:T(8,128)(2,1)}), bf16[4,512,256]{2,1,0:T(8,128)(2,1)}, u32[]{:S(2)}, u32[]{:S(2)}) %all-to-all-start.1) | async-done | bytes 1048608 | tf_op jit(solution)/shard_map/up_row/all_to_all | solution.py:694
  125.4 4.3 all-to-all-start.2
  138.6 5.6 project.1
  147.4 10.0 %attend.1 = (bf16[1024,256]{1,0:T(8,128)(2,1)}, f32[2,2,1024]{2,1,0:T(2,128)}) custom-call(bf16[1024,256]{1,0:T(8,128)(2,1)} %copy-done.65, bf16[1024,256]{1,0:T(8,128)(2,1)} %copy-done.66, bf16[1024,256]{1,0:T(8,128)(2,1)} %copy-done.67, s32[1,1024]{1,0:T(1,128)} %bitcast.98), custom_call_target="tpu_custom_call" | custom-call | flops 99999997952 | bytes 1 | tf_op jit(solution)/shard_map/attend/pallas_call | solution.py:473
  157.4 12.5 %all-to-all-done.2 = bf16[4,512,256]{2,1,0:T(8,128)(2,1)} async-done(((bf16[4,512,256]{2,1,0:T(8,128)(2,1)}), bf16[4,512,256]{2,1,0:T(8,128)(2,1)}, u32[]{:S(2)}, u32[]{:S(2)}) %all-to-all-start.2) | async-done | bytes 1048608 | tf_op jit(solution)/shard_map/down_row/all_to_all | solution.py:694
  169.8 5.1 mix.1
  178.4 12.2 %collective-permute-done.13 = bf16[1024,256]{1,0:T(8,128)(2,1)S(1)} collective-permute-done((bf16[1024,256]{1,0:T(8,128)(2,1)S(1)}, bf16[1024,256]{1,0:T(8,128)(2,1)S(1)}, u32[]{:S(2)}, u32[]{:S(2)}) %collective-permute-start.13) | collective-permute-done | bytes 524320 | tf_op jit(solution)/shard_map/up_plane/ppermute | solution.py:606
  193.0 2.6 add_convert_fusion.1
  199.3 11.4 %collective-permute-done.16 = bf16[256,1024]{1,0:T(8,128)(2,1)S(1)} collective-permute-done((bf16[256,1024]{1,0:T(8,128)(2,1)S(1)}, bf16[256,1024]{1,0:T(8,128)(2,1)S(1)}, u32[]{:S(2)}, u32[]{:S(2)}) %collective-permute-start.16) | collective-permute-done | bytes 524320 | tf_op jit(solution)/shard_map/mix_plane/ppermute | solution.py:606
  210.7 10.9 %collective-permute-done.17 = bf16[256,1024]{1,0:T(8,128)(2,1)S(1)} collective-permute-done((bf16[256,1024]{1,0:T(8,128)(2,1)S(1)}, bf16[256,1024]{1,0:T(8,128)(2,1)S(1)}, u32[]{:S(2)}, u32[]{:S(2)}) %collective-permute-start.17) | collective-permute-done | bytes 524320 | tf_op jit(solution)/shard_map/mix_plane/ppermute | solution.py:606
  228.4 21.2 %collective-permute-done.22.refs_0_.refs_2_ = bf16[256,1024]{1,0:T(8,128)(2,1)} collective-permute-done((bf16[256,1024]{1,0:T(8,128)(2,1)}, bf16[256,1024]{1,0:T(8,128)(2,1)}, u32[]{:S(2)}, u32[]{:S(2)}) %collective-permute-start.22) | collective-permute-done | bytes 524320 | tf_op jit(solution)/shard_map/middle_row/ppermute | solution.py:620
  253.8 9.9 %collective-permute-done.24.refs_1_.refs_3_ = bf16[256,1024]{1,0:T(8,128)(2,1)} collective-permute-done((bf16[256,1024]{1,0:T(8,128)(2,1)}, bf16[256,1024]{1,0:T(8,128)(2,1)}, u32[]{:S(2)}, u32[]{:S(2)}) %collective-permute-start.24) | collective-permute-done | bytes 524320 | tf_op jit(solution)/shard_map/middle_row/ppermute | solution.py:620
  267.4 8.1 %activate.2 = (bf16[512,1024]{1,0:T(8,128)(2,1)S(1)}, bf16[512,1024]{1,0:T(8,128)(2,1)S(1)}, bf16[512,1024]{1,0:T(8,128)(2,1)S(1)}, f32[512,1]{1,0:T(8,128)S(1)}) custom-call(bf16[256,1024]{1,0:T(8,128)(2,1)S(1)} %copy-done.13, bf16[256,1024]{1,0:T(8,128)(2,1)} %collective-permute-done.19.refs_1_, bf16[256,1024]{1,0:T(8,128)(2,1)} %collective-permute-done.20.refs_2_.refs_4_, ...), custom_call_target="tpu_custom_call" | custom-call | flops 74999996416 | bytes 1 | tf_op jit(solution)/shard_map/activate/pallas_call | solution.py:209
  280.1 8.0 %activate.3 = (bf16[512,1024]{1,0:T(8,128)(2,1)S(1)}, bf16[512,1024]{1,0:T(8,128)(2,1)S(1)}, bf16[512,1024]{1,0:T(8,128)(2,1)S(1)}, f32[512,1]{1,0:T(8,128)S(1)}) custom-call(bf16[256,1024]{1,0:T(8,128)(2,1)} %collective-permute-done.22.refs_0_.refs_2_, bf16[256,1024]{1,0:T(8,128)(2,1)} %collective-permute-done.24.refs_1_.refs_3_, ...), custom_call_target="tpu_custom_call" | custom-call | flops 74999996416 | bytes 1 | tf_op jit(solution)/shard_map/activate/pallas_call | solution.py:209
  290.4 11.3 %units_back.2 = (bf16[512,1024]{1,0:T(8,128)(2,1)S(1)}, bf16[512,1024]{1,0:T(8,128)(2,1)S(1)}, bf16[512,1024]{1,0:T(8,128)(2,1)S(1)}, bf16[512,1024]{1,0:T(8,128)(2,1)}) custom-call(s32[2]{0:T(128)S(1)} %pad_add_fusion.2.starts, bf16[1024,1024]{1,0:T(8,128)(2,1)} %all-gather.10.cloned.1.call-done.refs_0_, bf16[1024,1024]{1,0:T(8,128)(2,1)} %copy-done.37, ...), custom_call_target="tpu_custom_call" | custom-call | flops 92999999488 | bytes 1 | tf_op jit(solution)/shard_map/unit_grad/units_back/pallas_call | solution.py:275
  308.7 2.1 convert_add_fusion.1
  313.0 6.2 down_outer.1
  320.5 4.3 collective-permute-done.32
  325.8 10.3 %units_back.3 = (bf16[512,1024]{1,0:T(8,128)(2,1)S(1)}, bf16[512,1024]{1,0:T(8,128)(2,1)S(1)}, bf16[512,1024]{1,0:T(8,128)(2,1)S(1)}, bf16[512,1024]{1,0:T(8,128)(2,1)S(1)}) custom-call(s32[2]{0:T(128)S(1)} %pad_add_fusion.starts, bf16[1024,1024]{1,0:T(8,128)(2,1)} %all-gather.10.cloned.1.call-done.refs_0_, bf16[1024,1024]{1,0:T(8,128)(2,1)} %copy-done.37, ...), custom_call_target="tpu_custom_call" | custom-call | flops 92999999488 | bytes 1 | tf_op jit(solution)/shard_map/unit_grad/units_back/pallas_call | solution.py:275
  342.4 6.6 %up_outer.1 = (bf16[2048,256]{1,0:T(8,128)(2,1)S(1)}, bf16[2048,256]{1,0:T(8,128)(2,1)S(1)}, bf16[2048,256]{1,0:T(8,128)(2,1)S(1)}, bf16[2048,256]{1,0:T(8,128)(2,1)S(1)}) custom-call(s32[4]{0:T(128)S(1)} %pad_add_fusion.1.starts, bf16[256,1024]{1,0:T(8,128)(2,1)S(1)} %copy-done.14, bf16[256,1024]{1,0:T(8,128)(2,1)} %collective-permute-done.19.refs_1_, ...), custom_call_target="tpu_custom_call" | custom-call | flops 62999998464 | bytes 1 | tf_op jit(solution)/shard_map/up_outer/pallas_call | solution.py:318
  349.0 14.6 %collective-permute-done.36 = bf16[256,1024]{1,0:T(8,128)(2,1)S(1)} collective-permute-done((bf16[256,1024]{1,0:T(8,128)(2,1)}, bf16[256,1024]{1,0:T(8,128)(2,1)S(1)}, u32[]{:S(2)}, u32[]{:S(2)}) %collective-permute-start.36) | collective-permute-done | bytes 524320 | tf_op jit(solution)/shard_map/unit_grad/ppermute | solution.py:620
  366.9 4.3 all-to-all-start.3
  371.3 3.5 fusion.34
  380.4 7.0 %gate_outer.1 = (bf16[2048,256]{1,0:T(8,128)(2,1)S(1)}, bf16[2048,256]{1,0:T(8,128)(2,1)S(1)}, bf16[2048,256]{1,0:T(8,128)(2,1)S(1)}, bf16[2048,256]{1,0:T(8,128)(2,1)S(1)}) custom-call(s32[4]{0:T(128)S(1)} %pad_add_fusion.1.starts, bf16[256,1024]{1,0:T(8,128)(2,1)S(1)} %copy-done.15, bf16[256,1024]{1,0:T(8,128)(2,1)} %collective-permute-done.19.refs_1_, ...), custom_call_target="tpu_custom_call" | custom-call | flops 62999998464 | bytes 1 | tf_op jit(solution)/shard_map/gate_outer/pallas_call | solution.py:318
  392.3 5.9 feed.3
  398.4 9.7 %collective-permute-done.48 = bf16[1024,256]{1,0:T(8,128)(2,1)S(1)} collective-permute-done((bf16[1024,256]{1,0:T(8,128)(2,1)}, bf16[1024,256]{1,0:T(8,128)(2,1)S(1)}, u32[]{:S(2)}, u32[]{:S(2)}) %collective-permute-start.48) | collective-permute-done | bytes 524320 | tf_op jit(solution)/shard_map/gate_grad/ppermute | solution.py:606
  412.6 2.5 collective-permute-start.49
  415.5 6.1 feed.2
  423.2 4.1 collective-permute-done.49
  435.7 2.8 finish.4
  442.5 4.3 collective-permute-done.45
  450.0 21.7 %collective-permute-done.50 = bf16[2048,256]{1,0:T(8,128)(2,1)} collective-permute-done((bf16[2048,256]{1,0:T(8,128)(2,1)}, bf16[2048,256]{1,0:T(8,128)(2,1)}, u32[]{:S(2)}, u32[]{:S(2)}) %collective-permute-start.50) | collective-permute-done | bytes 1048608 | tf_op jit(solution)/shard_map/up_grad/ppermute | solution.py:606
  471.7 2.2 collective-permute-start.46
  473.9 4.0 multiply_reduce_fusion
  477.9 4.2 all-to-all-start.5
  482.3 2.2 copy-done.32
  488.4 11.1 %attend_back.1 = (bf16[1024,256]{1,0:T(8,128)(2,1)}, bf16[1024,256]{1,0:T(8,128)(2,1)}, bf16[1024,256]{1,0:T(8,128)(2,1)}) custom-call(bf16[1024,256]{1,0:T(8,128)(2,1)} %copy-done.65, bf16[1024,256]{1,0:T(8,128)(2,1)} %copy-done.66, bf16[1024,256]{1,0:T(8,128)(2,1)} %copy-done.67, bf16[1024,256]{1,0:T(8,128)(2,1)} %get-tuple-element.112.refs_0_.o_ref.mixed_ref, ...), custom_call_target="tpu_custom_call" | custom-call | flops 109999996928 | bytes 1 | tf_op jit(solution)/shard_map/attend_back/pallas_call | solution.py:543
  499.6 3.2 multiply_reduce_fusion.1
  502.9 9.1 %heads_outer.1 = (bf16[2048,1024]{1,0:T(8,128)(2,1)}, f32[2048,1]{1,0:T(8,128)S(1)}) custom-call(s32[1]{0:T(128)} %bitcast.24.core_ref, bf16[1024,1024]{1,0:T(8,128)(2,1)S(1)} %constant_dynamic-update-slice_fusion.17.own_ref.x_own, bf16[1024,1024]{1,0:T(8,128)(2,1)} %collective-permute-done.3.other_ref.x_other, bf16[8,256,1024]{2,1,0:T(8,128)(2,1)} %bitcast.78, ...), custom_call_target="tpu_custom_call" | custom-call | flops 93999996928 | bytes 1 | tf_op jit(solution)/shard_map/heads_outer/pallas_call | solution.py:358
  512.6 2.6 convert_add_fusion.4
  516.8 7.7 %first_grad.1 = (bf16[1024,1024]{1,0:T(8,128)(2,1)}, bf16[1024,1024]{1,0:T(8,128)(2,1)}) custom-call(bf16[1024,256]{1,0:T(8,128)(2,1)} %get-tuple-element.184.dq_ref.refs_0_, bf16[1024,256]{1,0:T(8,128)(2,1)} %get-tuple-element.180.dk_ref.refs_1_, bf16[1024,256]{1,0:T(8,128)(2,1)} %get-tuple-element.181.dv_ref.refs_2_, ...), custom_call_target="tpu_custom_call" | custom-call | flops 60000002048 | bytes 1 | tf_op jit(solution)/shard_map/first_plane/first_grad/pallas_call | solution.py:161
  526.3 2.8 finish.6
  529.1 5.3 all-to-all-start.4
  534.6 2.1 collective-permute-start.69
  536.6 2.4 collective-permute-start.70
  539.1 2.2 add_convert_fusion.9
  541.3 28.1 %collective-permute-done.69 = f32[2,512]{1,0:T(2,128)S(1)} collective-permute-done((f32[2,512]{1,0:T(2,128)S(1)}, f32[2,512]{1,0:T(2,128)S(1)}, u32[]{:S(2)}, u32[]{:S(2)}) %collective-permute-start.69) | collective-permute-done | bytes 4128 | tf_op jit(solution)/shard_map/gains/ppermute | solution.py:620
  569.3 19.8 %collective-permute-done.70 = f32[2,512]{1,0:T(2,128)S(1)} collective-permute-done((f32[2,512]{1,0:T(2,128)S(1)}, f32[2,512]{1,0:T(2,128)S(1)}, u32[]{:S(2)}, u32[]{:S(2)}) %collective-permute-start.70) | collective-permute-done | bytes 4128 | tf_op jit(solution)/shard_map/gains/ppermute | solution.py:620
  590.3 2.5 add_convert_fusion
  598.9 3.0 finish.5
  604.7 5.9 collective-permute-done.59
  611.5 11.5 %collective-permute-done.60 = bf16[256,1024]{1,0:T(8,128)(2,1)} collective-permute-done((bf16[256,1024]{1,0:T(8,128)(2,1)}, bf16[256,1024]{1,0:T(8,128)(2,1)}, u32[]{:S(2)}, u32[]{:S(2)}) %collective-permute-start.60) | collective-permute-done | bytes 524320 | tf_op jit(solution)/shard_map/first_plane/ppermute | solution.py:606
  628.0 2.2 collective-permute-start.63
  631.9 2.2 collective-permute-done.63
  634.1 4.3 collective-permute-done.64
  638.5 2.9 finish.7
  (467 shorter events, 164.2 us)
Async XLA Ops:
  7.2 126.4 %all-gather.6.cloned.1.call-start = ((), (), s32[]{:S(2)}) async-start(), calls=%async_computation.7 | async-start | bytes 3932160 | tf_op jit(solution)/shard_map/qkv_row/all_gather | solution.py:745
  7.2 29.2 %collective-permute-start = (bf16[1024,256]{1,0:T(8,128)(2,1)}, bf16[1024,256]{1,0:T(8,128)(2,1)}, u32[]{:S(2)}, u32[]{:S(2)}) collective-permute-start(bf16[1024,256]{1,0:T(8,128)(2,1)} %param.13), channel_id=1, source_target_pairs={{0,2},{1,3},{2,0},{3,1},{4,6},{5,7},{6,4},{7,5},{8,10},{9,11},{10,... | collective-permute-start | bytes 1572872 | tf_op jit(solution)/shard_map/inputs/ppermute | solution.py:606
  10.2 27.3 %collective-permute-start.1 = (bf16[1024,256]{1,0:T(8,128)(2,1)}, bf16[1024,256]{1,0:T(8,128)(2,1)}, u32[]{:S(2)}, u32[]{:S(2)}) collective-permute-start(bf16[1024,256]{1,0:T(8,128)(2,1)} %param.13), channel_id=1, source_target_pairs={{0,4},{1,5},{2,6},{3,7},{4,0},{5,1},{6,2},{7,3},{8,12},{9,13},{10,... | collective-permute-start | bytes 1572872 | tf_op jit(solution)/shard_map/inputs/ppermute | solution.py:606
  11.7 27.0 %collective-permute-start.2 = (bf16[1024,256]{1,0:T(8,128)(2,1)}, bf16[1024,256]{1,0:T(8,128)(2,1)}, u32[]{:S(2)}, u32[]{:S(2)}) collective-permute-start(bf16[1024,256]{1,0:T(8,128)(2,1)} %param.13), channel_id=1, source_target_pairs={{0,6},{1,7},{2,4},{3,5},{4,2},{5,3},{6,0},{7,1},{8,14},{9,15},{10,... | collective-permute-start | bytes 1572872 | tf_op jit(solution)/shard_map/inputs/ppermute | solution.py:606
  19.5 58.3 %all-to-all-start = ((bf16[4,512,256]{2,1,0:T(8,128)(2,1)}), bf16[4,512,256]{2,1,0:T(8,128)(2,1)S(1)}, u32[]{:S(2)}, u32[]{:S(2)}) async-start(bf16[4,512,256]{2,1,0:T(8,128)(2,1)} %pad_maximum_fusion), calls=%async_computation | async-start | bytes 2097152 | tf_op jit(solution)/shard_map/gate_row/all_to_all | solution.py:694
  46.5 87.0 %collective-permute-start.3 = (bf16[1024,1024]{1,0:T(8,128)(2,1)S(1)}, bf16[1024,1024]{1,0:T(8,128)(2,1)}, u32[]{:S(2)}, u32[]{:S(2)}) collective-permute-start(bf16[1024,1024]{1,0:T(8,128)(2,1)S(1)} %constant_dynamic-update-slice_fusion.17.own_ref.x_own), channel_id=1, source_target_pairs={{0,1},{1,0},{2,3},{3,2},{4,5},{5,4},{6,7},{7,6},{8,9},{9,8},{10,11... | collective-permute-start | bytes 6291464 | tf_op jit(solution)/shard_map/inputs/ppermute | solution.py:603
  77.8 44.6 %all-to-all-start.1 = ((bf16[4,512,256]{2,1,0:T(8,128)(2,1)}), bf16[4,512,256]{2,1,0:T(8,128)(2,1)}, u32[]{:S(2)}, u32[]{:S(2)}) async-start(bf16[4,512,256]{2,1,0:T(8,128)(2,1)} %pad_maximum_fusion.1), calls=%async_computation.1 | async-start | bytes 2097152 | tf_op jit(solution)/shard_map/up_row/all_to_all | solution.py:694
  82.1 87.8 %all-gather.8.cloned.1.call-start = ((), (), s32[]{:S(2)}) async-start(), calls=%async_computation.8 | async-start | bytes 1310720 | tf_op jit(solution)/shard_map/out_row/all_gather | solution.py:761
  82.1 19.8 %collective-permute-start.8 = (bf16[2048,256]{1,0:T(8,128)(2,1)S(1)}, bf16[2048,256]{1,0:T(8,128)(2,1)S(1)}, u32[]{:S(2)}, u32[]{:S(2)}) collective-permute-start(bf16[2048,256]{1,0:T(8,128)(2,1)S(1)} %bitcast.71), channel_id=1, source_target_pairs={{0,4},{1,5},{2,6},{3,7},{4,0},{5,1},{6,2},{7,3},{8,12},{9,13},{10,... | collective-permute-start | bytes 3145736 | tf_op jit(solution)/shard_map/gate_plane/ppermute | solution.py:606
  83.7 23.1 %collective-permute-start.7 = (bf16[2048,256]{1,0:T(8,128)(2,1)S(1)}, bf16[2048,256]{1,0:T(8,128)(2,1)S(1)}, u32[]{:S(2)}, u32[]{:S(2)}) collective-permute-start(bf16[2048,256]{1,0:T(8,128)(2,1)S(1)} %bitcast.72), channel_id=1, source_target_pairs={{0,2},{1,3},{2,0},{3,1},{4,6},{5,7},{6,4},{7,5},{8,10},{9,11},{10,... | collective-permute-start | bytes 3145736 | tf_op jit(solution)/shard_map/gate_plane/ppermute | solution.py:606
  102.8 27.5 %collective-permute-start.9 = (bf16[1024,256]{1,0:T(8,128)(2,1)}, bf16[1024,256]{1,0:T(8,128)(2,1)}, u32[]{:S(2)}, u32[]{:S(2)}) collective-permute-start(bf16[1024,256]{1,0:T(8,128)(2,1)} %slice.288), channel_id=1, source_target_pairs={{0,2},{1,3},{2,0},{3,1},{4,6},{5,7},{6,4},{7,5},{8,10},{9,11},{10,... | collective-permute-start | bytes 1572872 | tf_op jit(solution)/shard_map/gate_plane/ppermute | solution.py:606
  108.0 23.4 %collective-permute-start.10 = (bf16[1024,256]{1,0:T(8,128)(2,1)}, bf16[1024,256]{1,0:T(8,128)(2,1)}, u32[]{:S(2)}, u32[]{:S(2)}) collective-permute-start(bf16[1024,256]{1,0:T(8,128)(2,1)} %slice.289), channel_id=1, source_target_pairs={{0,4},{1,5},{2,6},{3,7},{4,0},{5,1},{6,2},{7,3},{8,12},{9,13},{10,... | collective-permute-start | bytes 1572872 | tf_op jit(solution)/shard_map/gate_plane/ppermute | solution.py:606
  122.4 34.9 %collective-permute-start.12 = (bf16[2048,256]{1,0:T(8,128)(2,1)}, bf16[2048,256]{1,0:T(8,128)(2,1)}, u32[]{:S(2)}, u32[]{:S(2)}) collective-permute-start(bf16[2048,256]{1,0:T(8,128)(2,1)} %bitcast.14.refs_5_.refs_13_), channel_id=1, source_target_pairs={{0,4},{1,5},{2,6},{3,7},{4,0},{5,1},{6,2},{7,3},{8,12},{9,13},{10,... | collective-permute-start | bytes 3145736 | tf_op jit(solution)/shard_map/up_plane/ppermute | solution.py:606
  123.9 33.4 %collective-permute-start.11 = (bf16[2048,256]{1,0:T(8,128)(2,1)}, bf16[2048,256]{1,0:T(8,128)(2,1)}, u32[]{:S(2)}, u32[]{:S(2)}) collective-permute-start(bf16[2048,256]{1,0:T(8,128)(2,1)} %bitcast.14.refs_5_.refs_13_), channel_id=1, source_target_pairs={{0,2},{1,3},{2,0},{3,1},{4,6},{5,7},{6,4},{7,5},{8,10},{9,11},{10,... | collective-permute-start | bytes 3145736 | tf_op jit(solution)/shard_map/up_plane/ppermute | solution.py:606
  125.4 44.4 %all-to-all-start.2 = ((bf16[4,512,256]{2,1,0:T(8,128)(2,1)}), bf16[4,512,256]{2,1,0:T(8,128)(2,1)}, u32[]{:S(2)}, u32[]{:S(2)}) async-start(bf16[4,512,256]{2,1,0:T(8,128)(2,1)} %pad_maximum_fusion.2), calls=%async_computation.2 | async-start | bytes 2097152 | tf_op jit(solution)/shard_map/down_row/all_to_all | solution.py:694
  129.7 95.0 %all-gather.10.cloned.1.call-start = ((), (), s32[]{:S(2)}) async-start(), calls=%async_computation.9 | async-start | bytes 2621440 | tf_op jit(solution)/shard_map/grad_row/all_gather | solution.py:765
  174.9 18.1 %collective-permute-start.15 = (bf16[1024,1024]{1,0:T(8,128)(2,1)}, bf16[1024,1024]{1,0:T(8,128)(2,1)}, u32[]{:S(2)}, u32[]{:S(2)}) collective-permute-start(bf16[1024,1024]{1,0:T(8,128)(2,1)} %get-tuple-element.116), channel_id=1, source_target_pairs={{0,1},{1,0},{2,3},{3,2},{4,5},{5,4},{6,7},{7,6},{8,9},{9,8},{10,11... | collective-permute-start | bytes 6291464 | tf_op jit(solution)/shard_map/mix_plane/ppermute | solution.py:603
  176.2 14.4 %collective-permute-start.13 = (bf16[1024,256]{1,0:T(8,128)(2,1)S(1)}, bf16[1024,256]{1,0:T(8,128)(2,1)S(1)}, u32[]{:S(2)}, u32[]{:S(2)}) collective-permute-start(bf16[1024,256]{1,0:T(8,128)(2,1)S(1)} %slice.290), channel_id=1, source_target_pairs={{0,2},{1,3},{2,0},{3,1},{4,6},{5,7},{6,4},{7,5},{8,10},{9,11},{10,... | collective-permute-start | bytes 1572872 | tf_op jit(solution)/shard_map/up_plane/ppermute | solution.py:606
  177.9 14.1 %collective-permute-start.14 = (bf16[1024,256]{1,0:T(8,128)(2,1)S(1)}, bf16[1024,256]{1,0:T(8,128)(2,1)S(1)}, u32[]{:S(2)}, u32[]{:S(2)}) collective-permute-start(bf16[1024,256]{1,0:T(8,128)(2,1)S(1)} %slice.291), channel_id=1, source_target_pairs={{0,4},{1,5},{2,6},{3,7},{4,0},{5,1},{6,2},{7,3},{8,12},{9,13},{10,... | collective-permute-start | bytes 1572872 | tf_op jit(solution)/shard_map/up_plane/ppermute | solution.py:606
  195.8 14.9 %collective-permute-start.16 = (bf16[256,1024]{1,0:T(8,128)(2,1)S(1)}, bf16[256,1024]{1,0:T(8,128)(2,1)S(1)}, u32[]{:S(2)}, u32[]{:S(2)}) collective-permute-start(bf16[256,1024]{1,0:T(8,128)(2,1)S(1)} %get-tuple-element.207), channel_id=1, source_target_pairs={{0,2},{1,3},{2,0},{3,1},{4,6},{5,7},{6,4},{7,5},{8,10},{9,11},{10,... | collective-permute-start | bytes 1572872 | tf_op jit(solution)/shard_map/mix_plane/ppermute | solution.py:606
  197.3 24.3 %collective-permute-start.17 = (bf16[256,1024]{1,0:T(8,128)(2,1)S(1)}, bf16[256,1024]{1,0:T(8,128)(2,1)S(1)}, u32[]{:S(2)}, u32[]{:S(2)}) collective-permute-start(bf16[256,1024]{1,0:T(8,128)(2,1)S(1)} %get-tuple-element.209), channel_id=1, source_target_pairs={{0,4},{1,5},{2,6},{3,7},{4,0},{5,1},{6,2},{7,3},{8,12},{9,13},{10,... | collective-permute-start | bytes 1572872 | tf_op jit(solution)/shard_map/mix_plane/ppermute | solution.py:606
  197.7 23.8 %collective-permute-start.18 = (bf16[256,1024]{1,0:T(8,128)(2,1)S(1)}, bf16[256,1024]{1,0:T(8,128)(2,1)S(1)}, u32[]{:S(2)}, u32[]{:S(2)}) collective-permute-start(bf16[256,1024]{1,0:T(8,128)(2,1)S(1)} %get-tuple-element.208), channel_id=1, source_target_pairs={{0,6},{1,7},{2,4},{3,5},{4,2},{5,3},{6,0},{7,1},{8,14},{9,15},{10,... | collective-permute-start | bytes 1572872 | tf_op jit(solution)/shard_map/mix_plane/ppermute | solution.py:606
  224.6 25.3 %collective-permute-start.28 = (bf16[2048,256]{1,0:T(8,128)(2,1)}, bf16[2048,256]{1,0:T(8,128)(2,1)}, u32[]{:S(2)}, u32[]{:S(2)}) collective-permute-start(bf16[2048,256]{1,0:T(8,128)(2,1)} %bitcast.15.refs_5_.refs_1_), channel_id=1, source_target_pairs={{0,4},{1,5},{2,6},{3,7},{4,0},{5,1},{6,2},{7,3},{8,12},{9,13},{10,... | collective-permute-start | bytes 3145736 | tf_op jit(solution)/shard_map/down_plane/ppermute | solution.py:606
  225.1 26.4 %collective-permute-start.27 = (bf16[2048,256]{1,0:T(8,128)(2,1)}, bf16[2048,256]{1,0:T(8,128)(2,1)}, u32[]{:S(2)}, u32[]{:S(2)}) collective-permute-start(bf16[2048,256]{1,0:T(8,128)(2,1)} %bitcast.15.refs_5_.refs_1_), channel_id=1, source_target_pairs={{0,2},{1,3},{2,0},{3,1},{4,6},{5,7},{6,4},{7,5},{8,10},{9,11},{10,... | collective-permute-start | bytes 3145736 | tf_op jit(solution)/shard_map/down_plane/ppermute | solution.py:606
  226.4 23.2 %collective-permute-start.22 = (bf16[256,1024]{1,0:T(8,128)(2,1)}, bf16[256,1024]{1,0:T(8,128)(2,1)}, u32[]{:S(2)}, u32[]{:S(2)}) collective-permute-start(bf16[256,1024]{1,0:T(8,128)(2,1)} %convert_element_type.293.refs_0_), channel_id=1, source_target_pairs={{0,16},{8,24},{16,0},{24,8},{1,17},{9,25},{17,1},{25,9},{2,18},{10... | collective-permute-start | bytes 1572872 | tf_op jit(solution)/shard_map/middle_row/ppermute | solution.py:620
  226.4 23.4 %collective-permute-start.19 = (bf16[256,1024]{1,0:T(8,128)(2,1)}, bf16[256,1024]{1,0:T(8,128)(2,1)}, u32[]{:S(2)}, u32[]{:S(2)}) collective-permute-start(bf16[256,1024]{1,0:T(8,128)(2,1)} %convert_element_type.293.refs_0_), channel_id=1, source_target_pairs={{0,8},{8,0},{16,24},{24,16},{1,9},{9,1},{17,25},{25,17},{2,10},{10... | collective-permute-start | bytes 1572872 | tf_op jit(solution)/shard_map/middle_row/ppermute | solution.py:620
  228.4 24.9 %collective-permute-start.20 = (bf16[256,1024]{1,0:T(8,128)(2,1)}, bf16[256,1024]{1,0:T(8,128)(2,1)}, u32[]{:S(2)}, u32[]{:S(2)}) collective-permute-start(bf16[256,1024]{1,0:T(8,128)(2,1)} %convert_element_type.293.refs_0_), channel_id=1, source_target_pairs={{0,1},{1,0},{2,3},{3,2},{4,5},{5,4},{6,7},{7,6},{8,9},{9,8},{10,11... | collective-permute-start | bytes 1572872 | tf_op jit(solution)/shard_map/middle_row/ppermute | solution.py:603
  249.6 14.1 %collective-permute-start.24 = (bf16[256,1024]{1,0:T(8,128)(2,1)}, bf16[256,1024]{1,0:T(8,128)(2,1)}, u32[]{:S(2)}, u32[]{:S(2)}) collective-permute-start(bf16[256,1024]{1,0:T(8,128)(2,1)} %collective-permute-done.22.refs_0_.refs_2_), channel_id=1, source_target_pairs={{0,8},{8,0},{16,24},{24,16},{1,9},{9,1},{17,25},{25,17},{2,10},{10... | collective-permute-start | bytes 1572872 | tf_op jit(solution)/shard_map/middle_row/ppermute | solution.py:620
  249.9 26.7 %collective-permute-start.23 = (bf16[256,1024]{1,0:T(8,128)(2,1)}, bf16[256,1024]{1,0:T(8,128)(2,1)S(1)}, u32[]{:S(2)}, u32[]{:S(2)}) collective-permute-start(bf16[256,1024]{1,0:T(8,128)(2,1)} %collective-permute-done.22.refs_0_.refs_2_), channel_id=1, source_target_pairs={{0,1},{1,0},{2,3},{3,2},{4,5},{5,4},{6,7},{7,6},{8,9},{9,8},{10,11... | collective-permute-start | bytes 1572872 | tf_op jit(solution)/shard_map/middle_row/ppermute | solution.py:603
  251.5 25.0 %collective-permute-start.29 = (bf16[1024,256]{1,0:T(8,128)(2,1)S(1)}, bf16[1024,256]{1,0:T(8,128)(2,1)S(1)}, u32[]{:S(2)}, u32[]{:S(2)}) collective-permute-start(bf16[1024,256]{1,0:T(8,128)(2,1)S(1)} %slice.292), channel_id=1, source_target_pairs={{0,2},{1,3},{2,0},{3,1},{4,6},{5,7},{6,4},{7,5},{8,10},{9,11},{10,... | collective-permute-start | bytes 1572872 | tf_op jit(solution)/shard_map/down_plane/ppermute | solution.py:606
  253.3 23.3 %collective-permute-start.30 = (bf16[1024,256]{1,0:T(8,128)(2,1)S(1)}, bf16[1024,256]{1,0:T(8,128)(2,1)S(1)}, u32[]{:S(2)}, u32[]{:S(2)}) collective-permute-start(bf16[1024,256]{1,0:T(8,128)(2,1)S(1)} %slice.293), channel_id=1, source_target_pairs={{0,4},{1,5},{2,6},{3,7},{4,0},{5,1},{6,2},{7,3},{8,12},{9,13},{10,... | collective-permute-start | bytes 1572872 | tf_op jit(solution)/shard_map/down_plane/ppermute | solution.py:606
  308.2 28.0 %collective-permute-start.35 = (f32[256,1]{0,1:T(1,128)}, f32[256,1]{0,1:T(1,128)}, u32[]{:S(2)}, u32[]{:S(2)}) collective-permute-start(f32[256,1]{0,1:T(1,128)} %bitcast.20), channel_id=1, source_target_pairs={{0,1},{1,0},{2,3},{3,2},{4,5},{5,4},{6,7},{7,6},{8,9},{9,8},{10,11... | collective-permute-start | bytes 3080 | tf_op jit(solution)/shard_map/ppermute | solution.py:603
  319.3 19.0 %collective-permute-start.38 = (bf16[1024,256]{1,0:T(8,128)(2,1)S(1)}, bf16[1024,256]{1,0:T(8,128)(2,1)S(1)}, u32[]{:S(2)}, u32[]{:S(2)}) collective-permute-start(bf16[1024,256]{1,0:T(8,128)(2,1)S(1)} %get-tuple-element.214), channel_id=1, source_target_pairs={{0,4},{1,5},{2,6},{3,7},{4,0},{5,1},{6,2},{7,3},{8,12},{9,13},{10,... | collective-permute-start | bytes 1572872 | tf_op jit(solution)/shard_map/down_grad/ppermute | solution.py:606
  319.9 19.3 %collective-permute-start.40 = (bf16[1024,256]{1,0:T(8,128)(2,1)S(1)}, bf16[1024,256]{1,0:T(8,128)(2,1)S(1)}, u32[]{:S(2)}, u32[]{:S(2)}) collective-permute-start(bf16[1024,256]{1,0:T(8,128)(2,1)S(1)} %get-tuple-element.215), channel_id=1, source_target_pairs={{0,2},{1,3},{2,0},{3,1},{4,6},{5,7},{6,4},{7,5},{8,10},{9,11},{10,... | collective-permute-start | bytes 1572872 | tf_op jit(solution)/shard_map/down_grad/ppermute | solution.py:606
  337.0 26.6 %collective-permute-start.36 = (bf16[256,1024]{1,0:T(8,128)(2,1)}, bf16[256,1024]{1,0:T(8,128)(2,1)S(1)}, u32[]{:S(2)}, u32[]{:S(2)}) collective-permute-start(bf16[256,1024]{1,0:T(8,128)(2,1)} %fusion.7), channel_id=1, source_target_pairs={{0,16},{8,24},{16,0},{24,8},{1,17},{9,25},{17,1},{25,9},{2,18},{10... | collective-permute-start | bytes 1572872 | tf_op jit(solution)/shard_map/unit_grad/ppermute | solution.py:620
  338.5 27.0 %collective-permute-start.39 = (bf16[2048,256]{1,0:T(8,128)(2,1)S(1)}, bf16[2048,256]{1,0:T(8,128)(2,1)S(1)}, u32[]{:S(2)}, u32[]{:S(2)}) collective-permute-start(bf16[2048,256]{1,0:T(8,128)(2,1)S(1)} %pad_maximum_fusion.3), channel_id=1, source_target_pairs={{0,2},{1,3},{2,0},{3,1},{4,6},{5,7},{6,4},{7,5},{8,10},{9,11},{10,... | collective-permute-start | bytes 3145736 | tf_op jit(solution)/shard_map/down_grad/ppermute | solution.py:606
  339.5 26.1 %collective-permute-start.41 = (bf16[2048,256]{1,0:T(8,128)(2,1)S(1)}, bf16[2048,256]{1,0:T(8,128)(2,1)S(1)}, u32[]{:S(2)}, u32[]{:S(2)}) collective-permute-start(bf16[2048,256]{1,0:T(8,128)(2,1)S(1)} %pad_maximum_fusion.4), channel_id=1, source_target_pairs={{0,4},{1,5},{2,6},{3,7},{4,0},{5,1},{6,2},{7,3},{8,12},{9,13},{10,... | collective-permute-start | bytes 3145736 | tf_op jit(solution)/shard_map/down_grad/ppermute | solution.py:606
  340.4 24.7 %collective-permute-start.34 = (bf16[256,1024]{1,0:T(8,128)(2,1)S(1)}, bf16[256,1024]{1,0:T(8,128)(2,1)S(1)}, u32[]{:S(2)}, u32[]{:S(2)}) collective-permute-start(bf16[256,1024]{1,0:T(8,128)(2,1)S(1)} %slice.424), channel_id=1, source_target_pairs={{0,8},{8,0},{16,24},{24,16},{1,9},{9,1},{17,25},{25,17},{2,10},{10... | collective-permute-start | bytes 1572872 | tf_op jit(solution)/shard_map/unit_grad/ppermute | solution.py:620
  366.9 68.8 %all-to-all-start.3 = ((bf16[4,512,256]{2,1,0:T(8,128)(2,1)}), bf16[4,512,256]{2,1,0:T(8,128)(2,1)}, u32[]{:S(2)}, u32[]{:S(2)}) async-start(bf16[4,512,256]{2,1,0:T(8,128)(2,1)} %bitcast.82), calls=%async_computation.3 | async-start | bytes 2097152 | tf_op jit(solution)/shard_map/down_grad/all_to_all | solution.py:728
  371.2 111.1 %all-gather.12.cloned.1.call-start = ((), (), s32[]{:S(2)}) async-start(), calls=%async_computation.11 | async-start | bytes 4718592 | tf_op jit(solution)/shard_map/middle_grad/all_gather | solution.py:847
  389.3 18.8 %collective-permute-start.48 = (bf16[1024,256]{1,0:T(8,128)(2,1)}, bf16[1024,256]{1,0:T(8,128)(2,1)S(1)}, u32[]{:S(2)}, u32[]{:S(2)}) collective-permute-start(bf16[1024,256]{1,0:T(8,128)(2,1)} %get-tuple-element.212), channel_id=1, source_target_pairs={{0,2},{1,3},{2,0},{3,1},{4,6},{5,7},{6,4},{7,5},{8,10},{9,11},{10,... | collective-permute-start | bytes 1572872 | tf_op jit(solution)/shard_map/gate_grad/ppermute | solution.py:606
  390.8 19.7 %collective-permute-start.47 = (bf16[1024,256]{1,0:T(8,128)(2,1)S(1)}, bf16[1024,256]{1,0:T(8,128)(2,1)S(1)}, u32[]{:S(2)}, u32[]{:S(2)}) collective-permute-start(bf16[1024,256]{1,0:T(8,128)(2,1)S(1)} %get-tuple-element.213), channel_id=1, source_target_pairs={{0,4},{1,5},{2,6},{3,7},{4,0},{5,1},{6,2},{7,3},{8,12},{9,13},{10,... | collective-permute-start | bytes 1572872 | tf_op jit(solution)/shard_map/gate_grad/ppermute | solution.py:606
  398.3 33.5 %collective-permute-start.44 = (bf16[512,1024]{1,0:T(8,128)(2,1)}, bf16[512,1024]{1,0:T(8,128)(2,1)S(1)}, u32[]{:S(2)}, u32[]{:S(2)}) collective-permute-start(bf16[512,1024]{1,0:T(8,128)(2,1)} %get-tuple-element.148), channel_id=1, source_target_pairs={{0,1},{1,0},{2,3},{3,2},{4,5},{5,4},{6,7},{7,6},{8,9},{9,8},{10,11... | collective-permute-start | bytes 3145736 | tf_op jit(solution)/shard_map/feed/ppermute | solution.py:603
  412.6 14.7 %collective-permute-start.49 = (bf16[1024,256]{1,0:T(8,128)(2,1)}, bf16[1024,256]{1,0:T(8,128)(2,1)S(1)}, u32[]{:S(2)}, u32[]{:S(2)}) collective-permute-start(bf16[1024,256]{1,0:T(8,128)(2,1)} %get-tuple-element.210), channel_id=1, source_target_pairs={{0,4},{1,5},{2,6},{3,7},{4,0},{5,1},{6,2},{7,3},{8,12},{9,13},{10,... | collective-permute-start | bytes 1572872 | tf_op jit(solution)/shard_map/up_grad/ppermute | solution.py:606
  421.6 16.9 %collective-permute-start.42 = (bf16[512,1024]{1,0:T(8,128)(2,1)}, bf16[512,1024]{1,0:T(8,128)(2,1)}, u32[]{:S(2)}, u32[]{:S(2)}) collective-permute-start(bf16[512,1024]{1,0:T(8,128)(2,1)} %get-tuple-element.144), channel_id=1, source_target_pairs={{0,1},{1,0},{2,3},{3,2},{4,5},{5,4},{6,7},{7,6},{8,9},{9,8},{10,11... | collective-permute-start | bytes 3145736 | tf_op jit(solution)/shard_map/feed/ppermute | solution.py:603
  421.6 77.9 %collective-permute-start.53 = (bf16[2048,256]{1,0:T(8,128)(2,1)}, bf16[2048,256]{1,0:T(8,128)(2,1)}, u32[]{:S(2)}, u32[]{:S(2)}) collective-permute-start(bf16[2048,256]{1,0:T(8,128)(2,1)} %pad_maximum_fusion.5), channel_id=1, source_target_pairs={{0,2},{1,3},{2,0},{3,1},{4,6},{5,7},{6,4},{7,5},{8,10},{9,11},{10,... | collective-permute-start | bytes 3145736 | tf_op jit(solution)/shard_map/gate_grad/ppermute | solution.py:606
  428.5 43.2 %collective-permute-start.50 = (bf16[2048,256]{1,0:T(8,128)(2,1)}, bf16[2048,256]{1,0:T(8,128)(2,1)}, u32[]{:S(2)}, u32[]{:S(2)}) collective-permute-start(bf16[2048,256]{1,0:T(8,128)(2,1)} %pad_maximum_fusion.7), channel_id=1, source_target_pairs={{0,2},{1,3},{2,0},{3,1},{4,6},{5,7},{6,4},{7,5},{8,10},{9,11},{10,... | collective-permute-start | bytes 3145736 | tf_op jit(solution)/shard_map/up_grad/ppermute | solution.py:606
  430.3 43.7 %collective-permute-start.52 = (bf16[2048,256]{1,0:T(8,128)(2,1)}, bf16[2048,256]{1,0:T(8,128)(2,1)}, u32[]{:S(2)}, u32[]{:S(2)}) collective-permute-start(bf16[2048,256]{1,0:T(8,128)(2,1)} %pad_maximum_fusion.8), channel_id=1, source_target_pairs={{0,4},{1,5},{2,6},{3,7},{4,0},{5,1},{6,2},{7,3},{8,12},{9,13},{10,... | collective-permute-start | bytes 3145736 | tf_op jit(solution)/shard_map/up_grad/ppermute | solution.py:606
  438.6 61.0 %collective-permute-start.54 = (bf16[2048,256]{1,0:T(8,128)(2,1)}, bf16[2048,256]{1,0:T(8,128)(2,1)}, u32[]{:S(2)}, u32[]{:S(2)}) collective-permute-start(bf16[2048,256]{1,0:T(8,128)(2,1)} %pad_maximum_fusion.6), channel_id=1, source_target_pairs={{0,4},{1,5},{2,6},{3,7},{4,0},{5,1},{6,2},{7,3},{8,12},{9,13},{10,... | collective-permute-start | bytes 3145736 | tf_op jit(solution)/shard_map/gate_grad/ppermute | solution.py:606
  446.7 65.9 %collective-permute-start.43 = (bf16[256,1024]{1,0:T(8,128)(2,1)}, bf16[256,1024]{1,0:T(8,128)(2,1)}, u32[]{:S(2)}, u32[]{:S(2)}) collective-permute-start(bf16[256,1024]{1,0:T(8,128)(2,1)} %slice.243), channel_id=1, source_target_pairs={{0,8},{8,0},{16,24},{24,16},{1,9},{9,1},{17,25},{25,17},{2,10},{10... | collective-permute-start | bytes 1572872 | tf_op jit(solution)/shard_map/feed/ppermute | solution.py:620
  471.7 40.9 %collective-permute-start.46 = (bf16[256,1024]{1,0:T(8,128)(2,1)}, bf16[256,1024]{1,0:T(8,128)(2,1)}, u32[]{:S(2)}, u32[]{:S(2)}) collective-permute-start(bf16[256,1024]{1,0:T(8,128)(2,1)} %fusion.33), channel_id=1, source_target_pairs={{0,16},{8,24},{16,0},{24,8},{1,17},{9,25},{17,1},{25,9},{2,18},{10... | collective-permute-start | bytes 1572872 | tf_op jit(solution)/shard_map/feed/ppermute | solution.py:620
  477.9 48.4 %all-to-all-start.5 = ((bf16[4,512,256]{2,1,0:T(8,128)(2,1)}), bf16[4,512,256]{2,1,0:T(8,128)(2,1)}, u32[]{:S(2)}, u32[]{:S(2)}) async-start(bf16[4,512,256]{2,1,0:T(8,128)(2,1)} %bitcast.81), calls=%async_computation.6 | async-start | bytes 2097152 | tf_op jit(solution)/shard_map/up_grad/all_to_all | solution.py:728
  482.2 156.3 %reduce-scatter.2.cloned.1.call-start = ((), (), s32[]{:S(2)}) async-start(), calls=%async_computation.10 | async-start | bytes 5242880 | tf_op jit(solution)/shard_map/heads_grad/reduce_scatter | solution.py:877
  524.5 65.9 %collective-permute-start.55 = (bf16[1024,1024]{1,0:T(8,128)(2,1)}, bf16[1024,1024]{1,0:T(8,128)(2,1)}, u32[]{:S(2)}, u32[]{:S(2)}) collective-permute-start(bf16[1024,1024]{1,0:T(8,128)(2,1)} %get-tuple-element.186), channel_id=1, source_target_pairs={{0,1},{1,0},{2,3},{3,2},{4,5},{5,4},{6,7},{7,6},{8,9},{9,8},{10,11... | collective-permute-start | bytes 6291464 | tf_op jit(solution)/shard_map/first_plane/ppermute | solution.py:603
  529.1 69.8 %all-to-all-start.4 = ((bf16[4,512,256]{2,1,0:T(8,128)(2,1)}), bf16[4,512,256]{2,1,0:T(8,128)(2,1)}, u32[]{:S(2)}, u32[]{:S(2)}) async-start(bf16[4,512,256]{2,1,0:T(8,128)(2,1)} %bitcast.80), calls=%async_computation.5 | async-start | bytes 2097152 | tf_op jit(solution)/shard_map/gate_grad/all_to_all | solution.py:728
  534.6 34.8 %collective-permute-start.69 = (f32[2,512]{1,0:T(2,128)S(1)}, f32[2,512]{1,0:T(2,128)S(1)}, u32[]{:S(2)}, u32[]{:S(2)}) collective-permute-start(f32[2,512]{1,0:T(2,128)S(1)} %bitcast.100), channel_id=1, source_target_pairs={{0,8},{8,0},{16,24},{24,16},{1,9},{9,1},{17,25},{25,17},{2,10},{10... | collective-permute-start | bytes 12296 | tf_op jit(solution)/shard_map/gains/ppermute | solution.py:620
  536.6 52.5 %collective-permute-start.70 = (f32[2,512]{1,0:T(2,128)S(1)}, f32[2,512]{1,0:T(2,128)S(1)}, u32[]{:S(2)}, u32[]{:S(2)}) collective-permute-start(f32[2,512]{1,0:T(2,128)S(1)} %bitcast.101), channel_id=1, source_target_pairs={{0,16},{8,24},{16,0},{24,8},{1,17},{9,25},{17,1},{25,9},{2,18},{10... | collective-permute-start | bytes 12296 | tf_op jit(solution)/shard_map/gains/ppermute | solution.py:620
  539.0 50.1 %collective-permute-start.71 = (f32[2,512]{1,0:T(2,128)S(1)}, f32[2,512]{1,0:T(2,128)S(1)}, u32[]{:S(2)}, u32[]{:S(2)}) collective-permute-start(f32[2,512]{1,0:T(2,128)S(1)} %bitcast.102), channel_id=1, source_target_pairs={{0,24},{8,16},{16,8},{24,0},{1,25},{9,17},{17,9},{25,1},{2,26},{10... | collective-permute-start | bytes 12296 | tf_op jit(solution)/shard_map/gains/ppermute | solution.py:620
  595.5 15.1 %collective-permute-start.59 = (bf16[256,1024]{1,0:T(8,128)(2,1)}, bf16[256,1024]{1,0:T(8,128)(2,1)}, u32[]{:S(2)}, u32[]{:S(2)}) collective-permute-start(bf16[256,1024]{1,0:T(8,128)(2,1)} %get-tuple-element.204), channel_id=1, source_target_pairs={{0,2},{1,3},{2,0},{3,1},{4,6},{5,7},{6,4},{7,5},{8,10},{9,11},{10,... | collective-permute-start | bytes 1572872 | tf_op jit(solution)/shard_map/first_plane/ppermute | solution.py:606
  596.4 26.6 %collective-permute-start.60 = (bf16[256,1024]{1,0:T(8,128)(2,1)}, bf16[256,1024]{1,0:T(8,128)(2,1)}, u32[]{:S(2)}, u32[]{:S(2)}) collective-permute-start(bf16[256,1024]{1,0:T(8,128)(2,1)} %get-tuple-element.206), channel_id=1, source_target_pairs={{0,4},{1,5},{2,6},{3,7},{4,0},{5,1},{6,2},{7,3},{8,12},{9,13},{10,... | collective-permute-start | bytes 1572872 | tf_op jit(solution)/shard_map/first_plane/ppermute | solution.py:606
  596.9 26.1 %collective-permute-start.61 = (bf16[256,1024]{1,0:T(8,128)(2,1)}, bf16[256,1024]{1,0:T(8,128)(2,1)}, u32[]{:S(2)}, u32[]{:S(2)}) collective-permute-start(bf16[256,1024]{1,0:T(8,128)(2,1)} %get-tuple-element.205), channel_id=1, source_target_pairs={{0,6},{1,7},{2,4},{3,5},{4,2},{5,3},{6,0},{7,1},{8,14},{9,15},{10,... | collective-permute-start | bytes 1572872 | tf_op jit(solution)/shard_map/first_plane/ppermute | solution.py:606
  603.2 21.7 %collective-permute-start.56 = (bf16[256,256]{1,0:T(8,128)(2,1)S(1)}, bf16[256,256]{1,0:T(8,128)(2,1)S(1)}, u32[]{:S(2)}, u32[]{:S(2)}) collective-permute-start(bf16[256,256]{1,0:T(8,128)(2,1)S(1)} %get-tuple-element.240), channel_id=1, source_target_pairs={{0,2},{1,3},{2,0},{3,1},{4,6},{5,7},{6,4},{7,5},{8,10},{9,11},{10,... | collective-permute-start | bytes 393224 | tf_op jit(solution)/shard_map/block_out/ppermute | solution.py:606
  604.2 26.0 %collective-permute-start.57 = (bf16[256,256]{1,0:T(8,128)(2,1)S(1)}, bf16[256,256]{1,0:T(8,128)(2,1)S(1)}, u32[]{:S(2)}, u32[]{:S(2)}) collective-permute-start(bf16[256,256]{1,0:T(8,128)(2,1)S(1)} %get-tuple-element.239), channel_id=1, source_target_pairs={{0,4},{1,5},{2,6},{3,7},{4,0},{5,1},{6,2},{7,3},{8,12},{9,13},{10,... | collective-permute-start | bytes 393224 | tf_op jit(solution)/shard_map/block_out/ppermute | solution.py:606
  610.6 19.7 %collective-permute-start.58 = (bf16[256,256]{1,0:T(8,128)(2,1)S(1)}, bf16[256,256]{1,0:T(8,128)(2,1)S(1)}, u32[]{:S(2)}, u32[]{:S(2)}) collective-permute-start(bf16[256,256]{1,0:T(8,128)(2,1)S(1)} %get-tuple-element.238), channel_id=1, source_target_pairs={{0,6},{1,7},{2,4},{3,5},{4,2},{5,3},{6,0},{7,1},{8,14},{9,15},{10,... | collective-permute-start | bytes 393224 | tf_op jit(solution)/shard_map/block_out/ppermute | solution.py:606
  (124 other events, 938.2 us)
Sparse Core Ops, SparseCore 0:
  16.7 106.4 all-gather.5
  124.7 44.3 all-gather.7
  175.1 43.3 all-gather.9
  374.9 43.8 all-gather.11
  515.3 95.3 reduce-scatter.1

commit v12 on v11

--- a/solution.py
+++ b/solution.py
@@ -20,42 +20,6 @@
 
 
 COST_RATE = 1e10
-ORDER = {
-    "gate_row": (),
-    "up_row": (0,),
-    "grad_plane": (0,),
-    "out_row": (0,),
-    "down_row": (0,),
-    "grad_row": (),
-    "project": (),
-    "attend": (0, 2),
-    "mix": (1, 3, 5),
-    "mix_plane": (1,),
-    "middle_row": (3,),
-    "down_plane": (2,),
-    "activate": (),
-    "activate_more": (1,),
-    "grad_core": (0, 1),
-    "units_back": (0,),
-    "units_back_more": (0, 2),
-    "down_outer": (0,),
-    "d_low": (1,),
-    "feed": (0, 1),
-    "feed_row": (0,),
-    "gate_outer": (1,),
-    "up_outer": (),
-    "gate_plane_back": (0,),
-    "fold": (0, 1, 2),
-    "attend_back": (0,),
-    "feed_end": (0,),
-    "gate_second": (0,),
-    "heads_outer": (0, 1),
-    "first_grad": (0,),
-    "up_plane_back": (3,),
-    "block_out": (0, 3),
-    "input_grad": (0,),
-    "gain_dots": (),
-}
 
 
 def lasts(microseconds):
@@ -643,13 +607,6 @@
     def after(value, *others):
         return lax.optimization_barrier((value,) + others)[0]
 
-    def dep(key, value, *groups):
-        chosen = []
-        for i in ORDER.get(key, ()):
-            group = groups[i]
-            chosen += list(group) if isinstance(group, (list, tuple)) else [group]
-        return after(value, *chosen) if chosen else value
-
     def put_rows(pieces):
         whole = jnp.zeros((tokens,) + pieces[0].shape[1:], pieces[0].dtype)
         for step, piece in enumerate(pieces):
@@ -751,30 +708,30 @@
             tiled=True,
         )
     with jax.named_scope("grad_plane"):
-        g_part = to_parts(dep("grad_plane", out_grad, x_own, x_other))
+        g_part = to_parts(after(out_grad, x_own))
     with jax.named_scope("gate_row"):
-        gate_whole = exchange(dep("gate_row", cut(scaled(gate_weight, gain_two)), x_own))
+        gate_whole = exchange(cut(scaled(gate_weight, gain_two)))
         gate_whole = after(gate_whole, g_part, cosine, front, back, start_row, up_cut, down_cut, out_block)
     with jax.named_scope("up_row"):
-        up_whole = exchange(dep("up_row", up_cut, gate_whole, x_other, qkv_full))
+        up_whole = exchange(after(up_cut, gate_whole))
     with jax.named_scope("out_row"):
-        out_full = lax.all_gather(dep("out_row", out_block, x_own, gate_whole), "row", axis=0, tiled=True)
+        out_full = lax.all_gather(after(out_block, x_own), "row", axis=0, tiled=True)
     with jax.named_scope("down_row"):
-        down_whole = exchange(dep("down_row", down_cut, up_whole, qkv_full, out_full, g_part))
+        down_whole = exchange(after(down_cut, up_whole))
     with jax.named_scope("grad_row"):
-        g_own = lax.all_gather(dep("grad_row", g_part, gate_whole, qkv_full, up_whole, out_full), "row", axis=0, tiled=True)
+        g_own = lax.all_gather(g_part, "row", axis=0, tiled=True)
     with jax.named_scope("gate_plane"):
         gates = spread_weights(gate_whole)
     with jax.named_scope("up_plane"):
         ups = spread_weights(up_whole)
     query, key, value, scale_one = project(
-        feat, dep("project", x_own, gates[1:3], gates[3:], up_whole, g_part, ups[1:3]), x_other, qkv_full, cosine, front, back
+        feat, x_own, x_other, qkv_full, cosine, front, back
     )
     mixed, logs = attend(
-        dep("attend", query, gates[1:3], gates[3:], up_whole, g_part, ups[1:3], ups[3:], out_full, down_whole),
+        after(query, gates[1:3], up_whole),
         key, value, start_row,
     )
-    mixed_in = dep("mix", mixed, gates[1:3], gates[3:], up_whole, ups[1:3], ups[3:], down_whole, g_part)
+    mixed_in = after(mixed, gates[3:], ups[1:3], down_whole)
 
     def join_cores(own, other):
         return (own.astype(F32) + core_swap(other).astype(F32)).astype(BF16)
@@ -787,13 +744,13 @@
 
     with jax.named_scope("mix_plane"):
         own, other = unfold(feat, "mix", [mixed_in], [out_full])
-        middle = token_part(x_own, 0).astype(F32) + scatter_parts(join_cores(dep("mix_plane", own, ups[1:3], ups[3:], down_whole, gates[3:], g_part), other))
-    middle_low = dep("middle_row", middle.astype(BF16), ups[1:3], ups[3:], down_whole, g_own)
+        middle = token_part(x_own, 0).astype(F32) + scatter_parts(join_cores(after(own, ups[3:]), other))
+    middle_low = after(middle.astype(BF16), g_own)
     with jax.named_scope("middle_row"):
         m_list = gather_row(middle_low)
         m_others = [core_swap(m) for m in m_list]
     with jax.named_scope("down_plane"):
-        downs = spread_weights(dep("down_plane", down_whole, ups[1:3], ups[3:], middle_low, m_list[1:3], mixed))
+        downs = spread_weights(after(down_whole, middle_low))
     square = jnp.sum(middle * middle, axis=1, keepdims=True)
     square = square + core_swap(square)
     scale_mid = lax.rsqrt(square / width + EPS)
@@ -801,12 +758,13 @@
     pairs = [slice(at, at + 2) for at in range(0, rows, 2)]
     found = []
     for pair in pairs:
-        key_at = "activate_more" if pair.start else "activate"
-        first = dep(key_at, m_list[pair.start], m_list, downs[1:3], downs[3:], g_own, ups)
+        first = m_list[pair.start]
+        if pair.start:
+            first = after(first, downs[1:3])
         found.append(activate(feat, [first, m_list[pair.start + 1]], m_others[pair], gates, ups))
     hiddens = [f[0] for f in found]
     with jax.named_scope("grad_row"):
-        g_own = dep("grad_core", g_own, m_others, hiddens[0], hiddens[-1])
+        g_own = after(g_own, m_others, hiddens[0])
         g_other = core_swap(g_own)
     parts, scaled_grads, down_parts = [None] * rows, [None] * len(pairs), None
     down_middle = None
@@ -814,9 +772,9 @@
         with jax.named_scope("unit_grad"):
             _, slope_gate, slope_up, scale = found[at]
             if down_parts is None:
-                slope_gate = dep("units_back", slope_gate, hiddens, downs)
+                slope_gate = after(slope_gate, hiddens)
             else:
-                slope_gate = dep("units_back_more", slope_gate, down_parts[:1], sent, low_kept, down_middle[1:])
+                slope_gate = after(slope_gate, down_parts[:1], low_kept)
             gate_grad, up_grad, own, other = units_back(
                 feat, starts[pairs[at]], g_own, g_other, slope_gate, slope_up, scale, gates, ups, downs
             )
@@ -827,7 +785,7 @@
         if down_parts is None:
             with jax.named_scope("down_grad"):
                 down_parts = outer(
-                    feat, "down_outer", starts, [g_own], [g_other], [dep("down_outer", h, sent, hiddens) for h in hiddens], places
+                    feat, "down_outer", starts, [g_own], [g_other], [after(h, sent) for h in hiddens], places
                 )
                 down_middle = plane_first(down_parts)
         low_kept = parts[2 * at].astype(BF16)
@@ -842,34 +800,34 @@
     dot_two = dot_two + core_swap(dot_two)
     middle_grad = g_part.astype(F32) + scale_mid * (unit_grad - unit_mid * (dot_two / width))
 
-    d_low = dep("d_low", middle_grad.astype(BF16), down_middle[1:], down_total)
+    d_low = after(middle_grad.astype(BF16), down_total)
     with jax.named_scope("middle_grad"):
         d_parts = lax.all_gather(d_low, "col")
     with jax.named_scope("feed"):
-        kept = [unfold(feat, "feed", [dep("feed", h, low_kept, d_low)], downs) for h in hiddens]
+        kept = [unfold(feat, "feed", [after(h, low_kept, d_low)], downs) for h in hiddens]
         shares = []
         for own, other in kept:
-            low = dep("feed_row", (own.astype(F32) + core_swap(other).astype(F32)).astype(BF16), d_low)
+            low = after((own.astype(F32) + core_swap(other).astype(F32)).astype(BF16), d_low)
             shares += [low[:quarter], low[quarter:]]
         sent = []
         for at in range(0, rows, 2):
             sent.append(shares[at].astype(F32) + row_swap(shares[at + 1], 1).astype(F32))
             shares[at] = sent[-1]
         feed = reduce_row(shares, 2)
-    gate_parts = outer(feat, "gate_outer", starts, m_list, m_others, [dep("gate_outer", a, low_kept, d_low, [own for own, _ in kept]) for a, _ in scaled_grads], places)
-    up_parts = outer(feat, "up_outer", starts, m_list, m_others, [dep("up_outer", a, low_kept, d_low, [own for own, _ in kept], gate_parts[:1]) for _, a in scaled_grads], places)
+    gate_parts = outer(feat, "gate_outer", starts, m_list, m_others, [after(a, d_low) for a, _ in scaled_grads], places)
+    up_parts = outer(feat, "up_outer", starts, m_list, m_others, [a for _, a in scaled_grads], places)
     with jax.named_scope("gate_grad"):
-        gate_middle = plane_first([dep("gate_plane_back", a, d_low, d_parts) for a in gate_parts])
-    mixed_grad = fold(feat, cores, dep("fold", d_parts, gate_parts[:1], up_parts[:1], sent, gate_middle[1:], down_total), out_full)
+        gate_middle = plane_first([after(a, d_low) for a in gate_parts])
+    mixed_grad = fold(feat, cores, after(d_parts, gate_parts[:1], up_parts[:1], sent), out_full)
     query_grad, key_grad, value_grad = attend_back(
-        query, key, value, mixed, dep("attend_back", mixed_grad, gate_middle[1:], down_blocks, feed), start_row, logs, cosine, front, back
+        query, key, value, mixed, after(mixed_grad, gate_middle[1:]), start_row, logs, cosine, front, back
     )
     with jax.named_scope("feed"):
-        feed_low = (middle + dep("feed_end", feed, query_grad).astype(F32)).astype(BF16)
+        feed_low = (middle + after(feed, query_grad).astype(F32)).astype(BF16)
     with jax.named_scope("gate_grad"):
-        gate_total = plane_second(gate_middle, *((query_grad,) if ORDER.get("gate_second") else ()))
+        gate_total = plane_second(gate_middle, *((query_grad,)))
         gate_blocks = give_back(gate_total)
-    heads_in = dep("heads_outer", query_grad, down_blocks, gate_total, feed_low, gate_middle[1:])
+    heads_in = after(query_grad, down_blocks, gate_total)
     heads_part, gain_dots = heads_outer(
         feat, cores, x_own, x_other, d_parts, heads_in, key_grad, value_grad, mixed, scale_one, qkv_full
     )
@@ -877,21 +835,21 @@
         heads_blocks = lax.psum_scatter(heads_part, "row", scatter_dimension=0, tiled=True)
     with jax.named_scope("first_plane"):
         first_low = join_cores(
-            *unfold(feat, "first_grad", [dep("first_grad", query_grad, heads_part, gate_total), key_grad, value_grad], [qkv_full])
+            *unfold(feat, "first_grad", [after(query_grad, heads_part), key_grad, value_grad], [qkv_full])
         )
         first_unit_grad = scatter_parts(first_low)
     with jax.named_scope("up_grad"):
-        up_total = plane_second(plane_first([dep("up_plane_back", a, gate_total, heads_part, first_low, gate_middle[1:]) for a in up_parts]))
+        up_total = plane_second(plane_first([after(a, gate_middle[1:]) for a in up_parts]))
         up_blocks = give_back(up_total)
     with jax.named_scope("block_out"):
-        block_out = to_home(dep("block_out", feed_low, up_total, gate_total, heads_part, first_low))
+        block_out = to_home(after(feed_low, up_total, first_low))
     scale_first = token_part(scale_one, 0)
     unit_first = token_part(x_own, 0).astype(F32) * scale_first
     dot_one = jnp.sum(first_unit_grad * unit_first, axis=1, keepdims=True)
     dot_one = dot_one + core_swap(dot_one)
     with jax.named_scope("input_grad"):
         input_grad = to_home(
-            (dep("input_grad", middle_grad, up_total, gate_blocks) + scale_first * (first_unit_grad - unit_first * (dot_one / width))).astype(BF16)
+            (after(middle_grad, up_total) + scale_first * (first_unit_grad - unit_first * (dot_one / width))).astype(BF16)
         )
 
     def row_dots(w, d):
@@ -899,8 +857,9 @@
 
     with jax.named_scope("gains"):
         dots = jnp.stack(
-            [gain_dots[:, 0], row_dots(dep("gain_dots", gates[0], heads_part, up_total), gate_total) + row_dots(ups[0], up_total)]
+            [gain_dots[:, 0], row_dots(gates[0], gate_total) + row_dots(ups[0], up_total)]
         ).reshape(2, rows, 2, feat)
+        dots = after(dots, input_grad)
         dots = sum_cols(jnp.where(core == 0, dots, dots[:, :, ::-1])).transpose(1, 0, 2, 3)
         dots = dots.reshape(rows, 2, 2 * feat)
         mine = lax.dynamic_index_in_dim(dots, row, 0, False)

time: 656 us -> 632 us (0.963)
  the two profiles are of different devices: /device:TPU:0 before, /device:TPU:9 now
where the time goes in v12:
time: 632 us; the launch traced here: 621 us
  waiting for transfers between devices  210 us (33%)
  Pallas kernels  131 us (21%)
  starting transfers between devices  128 us (20%)
  local copies, waits for them, and re-layouts  73.5 us (12%)
  other arithmetic  63.3 us (10%)
  between operations  15.5 us (2%)
    ppermute x42, waiting for transfers between devices, plane_swap(): return lax.ppermute(a, 'col', [(i, i ^ 2 * step) for i in range(cols)])  89.3 us
    unnamed x210, local copies, waits for them, and re-layouts  49.7 us
    ppermute x12, waiting for transfers between devices, row_swap(): return lax.ppermute(a, 'row', [(i, i ^ step) for i in range(rows)])  49.5 us
    ppermute x42, starting transfers between devices, plane_swap(): return lax.ppermute(a, 'col', [(i, i ^ 2 * step) for i in range(cols)])  38.7 us
    all_to_all x3, waiting for transfers between devices, exchange(): got = lax.all_to_all(pieces, 'row', split_axis=0, concat_axis=0, tiled=True)  31.2 us
    all_to_all x3, starting transfers between devices, exchange(): got = lax.all_to_all(pieces, 'row', split_axis=0, concat_axis=0, tiled=True)  27.8 us
    ppermute x15, starting transfers between devices, core_swap(): return lax.ppermute(a, 'col', [(i, i ^ 1) for i in range(cols)])  25 us
    pallas_call x4, Pallas kernels, unfold(): pl.pallas_call(functools.partial(unfold_kernel, feat, len(lefts)), grid=(...  24.9 us
  transfers between devices with their start and end apart: 83, of which 34 were waited for; matrix products, arithmetic and copies ran while one was open for 14% of the time, Pallas kernels for 18%

profile of v12, /device:TPU:9, one launch (start us, length us, event | category | flops | bytes accessed | tf_op | source)
XLA Modules:
  0.0 621.1 jit_solution(11541976616265540610)
XLA Ops:
  17.7 4.8 all-to-all-start
  24.8 2.9 multiply_sine_fusion
  43.5 2.7 collective-permute-start.3
  47.8 4.7 collective-permute-done.6
  53.2 6.4 %all-to-all-done = bf16[4,512,256]{2,1,0:T(8,128)(2,1)S(1)} async-done(((bf16[4,512,256]{2,1,0:T(8,128)(2,1)}), bf16[4,512,256]{2,1,0:T(8,128)(2,1)S(1)}, u32[]{:S(2)}, u32[]{:S(2)}) %all-to-all-start) | async-done | bytes 1048608 | tf_op jit(solution)/shard_map/gate_row/all_to_all | solution.py:651
  59.5 14.2 %all-to-all-start.1 = ((bf16[4,512,256]{2,1,0:T(8,128)(2,1)}), bf16[4,512,256]{2,1,0:T(8,128)(2,1)}, u32[]{:S(2)}, u32[]{:S(2)}) async-start(bf16[4,512,256]{2,1,0:T(8,128)(2,1)} %pad_maximum_fusion.1), calls=%async_computation.1 | async-start | bytes 2097152 | tf_op jit(solution)/shard_map/up_row/all_to_all | solution.py:651
  76.2 14.3 %collective-permute-done.8.refs_8_.refs_11_ = bf16[2048,256]{1,0:T(8,128)(2,1)S(1)} collective-permute-done((bf16[2048,256]{1,0:T(8,128)(2,1)S(1)}, bf16[2048,256]{1,0:T(8,128)(2,1)S(1)}, u32[]{:S(2)}, u32[]{:S(2)}) %collective-permute-start.8) | collective-permute-done | bytes 1048608 | tf_op jit(solution)/shard_map/gate_plane/ppermute | solution.py:570
  95.0 19.2 %all-to-all-done.1 = bf16[4,512,256]{2,1,0:T(8,128)(2,1)} async-done(((bf16[4,512,256]{2,1,0:T(8,128)(2,1)}), bf16[4,512,256]{2,1,0:T(8,128)(2,1)}, u32[]{:S(2)}, u32[]{:S(2)}) %all-to-all-start.1) | async-done | bytes 1048608 | tf_op jit(solution)/shard_map/up_row/all_to_all | solution.py:651
  116.7 8.9 %all-to-all-start.2 = ((bf16[4,512,256]{2,1,0:T(8,128)(2,1)}), bf16[4,512,256]{2,1,0:T(8,128)(2,1)}, u32[]{:S(2)}, u32[]{:S(2)}) async-start(bf16[4,512,256]{2,1,0:T(8,128)(2,1)} %pad_maximum_fusion.2), calls=%async_computation.2 | async-start | bytes 2097152 | tf_op jit(solution)/shard_map/down_row/all_to_all | solution.py:651
  133.8 5.6 project.1
  142.6 10.0 %attend.1 = (bf16[1024,256]{1,0:T(8,128)(2,1)}, f32[2,2,1024]{2,1,0:T(2,128)}) custom-call(bf16[1024,256]{1,0:T(8,128)(2,1)} %copy-done.65, bf16[1024,256]{1,0:T(8,128)(2,1)} %copy-done.66, bf16[1024,256]{1,0:T(8,128)(2,1)} %copy-done.67, s32[1,1024]{1,0:T(1,128)} %bitcast.98), custom_call_target="tpu_custom_call" | custom-call | flops 99999997952 | bytes 1 | tf_op jit(solution)/shard_map/attend/pallas_call | solution.py:437
  152.6 5.6 all-to-all-done.2
  158.2 6.2 all-gather.8.cloned.1.call-done.refs_1_.weight_ref
  164.4 5.1 mix.1
  174.5 12.0 %collective-permute-done.13 = bf16[1024,256]{1,0:T(8,128)(2,1)S(1)} collective-permute-done((bf16[1024,256]{1,0:T(8,128)(2,1)S(1)}, bf16[1024,256]{1,0:T(8,128)(2,1)S(1)}, u32[]{:S(2)}, u32[]{:S(2)}) %collective-permute-start.13) | collective-permute-done | bytes 524320 | tf_op jit(solution)/shard_map/up_plane/ppermute | solution.py:570
  188.5 2.5 add_convert_fusion.1
  193.9 9.8 %collective-permute-done.16 = bf16[256,1024]{1,0:T(8,128)(2,1)S(1)} collective-permute-done((bf16[256,1024]{1,0:T(8,128)(2,1)S(1)}, bf16[256,1024]{1,0:T(8,128)(2,1)S(1)}, u32[]{:S(2)}, u32[]{:S(2)}) %collective-permute-start.16) | collective-permute-done | bytes 524320 | tf_op jit(solution)/shard_map/mix_plane/ppermute | solution.py:570
  205.3 9.8 %collective-permute-done.18 = bf16[256,1024]{1,0:T(8,128)(2,1)S(1)} collective-permute-done((bf16[256,1024]{1,0:T(8,128)(2,1)S(1)}, bf16[256,1024]{1,0:T(8,128)(2,1)S(1)}, u32[]{:S(2)}, u32[]{:S(2)}) %collective-permute-start.18) | collective-permute-done | bytes 524320 | tf_op jit(solution)/shard_map/mix_plane/ppermute | solution.py:570
  220.3 3.2 collective-permute-start.22
  223.6 2.7 collective-permute-start.20
  226.3 20.2 %collective-permute-done.22.refs_0_.refs_2_ = bf16[256,1024]{1,0:T(8,128)(2,1)} collective-permute-done((bf16[256,1024]{1,0:T(8,128)(2,1)}, bf16[256,1024]{1,0:T(8,128)(2,1)}, u32[]{:S(2)}, u32[]{:S(2)}) %collective-permute-start.22) | collective-permute-done | bytes 524320 | tf_op jit(solution)/shard_map/middle_row/ppermute | solution.py:584
  252.6 8.3 %collective-permute-done.24.refs_1_.refs_3_ = bf16[256,1024]{1,0:T(8,128)(2,1)} collective-permute-done((bf16[256,1024]{1,0:T(8,128)(2,1)}, bf16[256,1024]{1,0:T(8,128)(2,1)}, u32[]{:S(2)}, u32[]{:S(2)}) %collective-permute-start.24) | collective-permute-done | bytes 524320 | tf_op jit(solution)/shard_map/middle_row/ppermute | solution.py:584
  265.6 8.1 %activate.2 = (bf16[512,1024]{1,0:T(8,128)(2,1)S(1)}, bf16[512,1024]{1,0:T(8,128)(2,1)S(1)}, bf16[512,1024]{1,0:T(8,128)(2,1)S(1)}, f32[512,1]{1,0:T(8,128)S(1)}) custom-call(bf16[256,1024]{1,0:T(8,128)(2,1)S(1)} %copy-done.13, bf16[256,1024]{1,0:T(8,128)(2,1)} %collective-permute-done.19.refs_1_, bf16[256,1024]{1,0:T(8,128)(2,1)} %collective-permute-done.20.refs_2_.refs_4_, ...), custom_call_target="tpu_custom_call" | custom-call | flops 74999996416 | bytes 1 | tf_op jit(solution)/shard_map/activate/pallas_call | solution.py:173
  277.8 8.1 %activate.3 = (bf16[512,1024]{1,0:T(8,128)(2,1)S(1)}, bf16[512,1024]{1,0:T(8,128)(2,1)S(1)}, bf16[512,1024]{1,0:T(8,128)(2,1)S(1)}, f32[512,1]{1,0:T(8,128)S(1)}) custom-call(bf16[256,1024]{1,0:T(8,128)(2,1)} %collective-permute-done.22.refs_0_.refs_2_, bf16[256,1024]{1,0:T(8,128)(2,1)} %collective-permute-done.24.refs_1_.refs_3_, ...), custom_call_target="tpu_custom_call" | custom-call | flops 74999996416 | bytes 1 | tf_op jit(solution)/shard_map/activate/pallas_call | solution.py:173
  288.2 11.3 %units_back.2 = (bf16[512,1024]{1,0:T(8,128)(2,1)S(1)}, bf16[512,1024]{1,0:T(8,128)(2,1)S(1)}, bf16[512,1024]{1,0:T(8,128)(2,1)S(1)}, bf16[512,1024]{1,0:T(8,128)(2,1)}) custom-call(s32[2]{0:T(128)S(1)} %pad_add_fusion.2.starts, bf16[1024,1024]{1,0:T(8,128)(2,1)} %all-gather.10.cloned.1.call-done.refs_0_, bf16[1024,1024]{1,0:T(8,128)(2,1)} %copy-done.37, ...), custom_call_target="tpu_custom_call" | custom-call | flops 92999999488 | bytes 1 | tf_op jit(solution)/shard_map/unit_grad/units_back/pallas_call | solution.py:239
  303.1 2.4 collective-permute-done.31
  310.5 6.2 down_outer.1
  317.3 3.6 collective-permute-done.32
  321.9 10.3 %units_back.3 = (bf16[512,1024]{1,0:T(8,128)(2,1)S(1)}, bf16[512,1024]{1,0:T(8,128)(2,1)S(1)}, bf16[512,1024]{1,0:T(8,128)(2,1)S(1)}, bf16[512,1024]{1,0:T(8,128)(2,1)S(1)}) custom-call(s32[2]{0:T(128)S(1)} %pad_add_fusion.starts, bf16[1024,1024]{1,0:T(8,128)(2,1)} %all-gather.10.cloned.1.call-done.refs_0_, bf16[1024,1024]{1,0:T(8,128)(2,1)} %copy-done.37, ...), custom_call_target="tpu_custom_call" | custom-call | flops 92999999488 | bytes 1 | tf_op jit(solution)/shard_map/unit_grad/units_back/pallas_call | solution.py:239
  334.2 2.5 collective-permute-start.36
  339.4 6.6 %up_outer.1 = (bf16[2048,256]{1,0:T(8,128)(2,1)S(1)}, bf16[2048,256]{1,0:T(8,128)(2,1)S(1)}, bf16[2048,256]{1,0:T(8,128)(2,1)S(1)}, bf16[2048,256]{1,0:T(8,128)(2,1)S(1)}) custom-call(s32[4]{0:T(128)S(1)} %pad_add_fusion.1.starts, bf16[256,1024]{1,0:T(8,128)(2,1)S(1)} %copy-done.14, bf16[256,1024]{1,0:T(8,128)(2,1)} %collective-permute-done.19.refs_1_, ...), custom_call_target="tpu_custom_call" | custom-call | flops 62999998464 | bytes 1 | tf_op jit(solution)/shard_map/up_outer/pallas_call | solution.py:282
  346.1 13.6 %collective-permute-done.36 = bf16[256,1024]{1,0:T(8,128)(2,1)S(1)} collective-permute-done((bf16[256,1024]{1,0:T(8,128)(2,1)}, bf16[256,1024]{1,0:T(8,128)(2,1)S(1)}, u32[]{:S(2)}, u32[]{:S(2)}) %collective-permute-start.36) | collective-permute-done | bytes 524320 | tf_op jit(solution)/shard_map/unit_grad/ppermute | solution.py:584
  363.3 2.6 fusion.34
  371.6 6.5 %gate_outer.1 = (bf16[2048,256]{1,0:T(8,128)(2,1)S(1)}, bf16[2048,256]{1,0:T(8,128)(2,1)S(1)}, bf16[2048,256]{1,0:T(8,128)(2,1)S(1)}, bf16[2048,256]{1,0:T(8,128)(2,1)S(1)}) custom-call(s32[4]{0:T(128)S(1)} %pad_add_fusion.1.starts, bf16[256,1024]{1,0:T(8,128)(2,1)S(1)} %copy-done.15, bf16[256,1024]{1,0:T(8,128)(2,1)} %collective-permute-done.19.refs_1_, ...), custom_call_target="tpu_custom_call" | custom-call | flops 62999998464 | bytes 1 | tf_op jit(solution)/shard_map/gate_outer/pallas_call | solution.py:282
  382.5 5.9 feed.3
  389.1 4.9 collective-permute-done.48
  395.3 2.7 collective-permute-done.47
  403.6 6.2 feed.2
  412.1 4.4 collective-permute-done.49
  428.1 4.2 all-to-all-start.3
  441.1 2.8 collective-permute-start.46
  443.9 4.1 multiply_reduce_fusion
  454.0 11.1 %attend_back.1 = (bf16[1024,256]{1,0:T(8,128)(2,1)}, bf16[1024,256]{1,0:T(8,128)(2,1)}, bf16[1024,256]{1,0:T(8,128)(2,1)}) custom-call(bf16[1024,256]{1,0:T(8,128)(2,1)} %copy-done.65, bf16[1024,256]{1,0:T(8,128)(2,1)} %copy-done.66, bf16[1024,256]{1,0:T(8,128)(2,1)} %copy-done.67, bf16[1024,256]{1,0:T(8,128)(2,1)} %get-tuple-element.113.refs_0_.o_ref.mixed_ref, ...), custom_call_target="tpu_custom_call" | custom-call | flops 109999996928 | bytes 1 | tf_op jit(solution)/shard_map/attend_back/pallas_call | solution.py:507
  465.2 3.7 multiply_reduce_fusion.1
  469.0 5.6 all-to-all-start.5
  481.7 9.2 %heads_outer.1 = (bf16[2048,1024]{1,0:T(8,128)(2,1)}, f32[2048,1]{1,0:T(8,128)S(1)}) custom-call(s32[1]{0:T(128)} %bitcast.24.core_ref, bf16[1024,1024]{1,0:T(8,128)(2,1)S(1)} %constant_dynamic-update-slice_fusion.15.own_ref.x_own, bf16[1024,1024]{1,0:T(8,128)(2,1)} %collective-permute-done.3.other_ref.x_other, bf16[8,256,1024]{2,1,0:T(8,128)(2,1)} %bitcast.78, ...), custom_call_target="tpu_custom_call" | custom-call | flops 93999996928 | bytes 1 | tf_op jit(solution)/shard_map/heads_outer/pallas_call | solution.py:322
  490.9 7.7 %first_grad.1 = (bf16[1024,1024]{1,0:T(8,128)(2,1)}, bf16[1024,1024]{1,0:T(8,128)(2,1)}) custom-call(bf16[1024,256]{1,0:T(8,128)(2,1)} %get-tuple-element.185.dq_ref.refs_0_, bf16[1024,256]{1,0:T(8,128)(2,1)} %get-tuple-element.181.dk_ref.refs_1_, bf16[1024,256]{1,0:T(8,128)(2,1)} %get-tuple-element.182.dv_ref.refs_2_, ...), custom_call_target="tpu_custom_call" | custom-call | flops 60000002048 | bytes 1 | tf_op jit(solution)/shard_map/first_plane/first_grad/pallas_call | solution.py:125
  498.6 8.9 %collective-permute-start.55 = (bf16[1024,1024]{1,0:T(8,128)(2,1)}, bf16[1024,1024]{1,0:T(8,128)(2,1)}, u32[]{:S(2)}, u32[]{:S(2)}) collective-permute-start(bf16[1024,1024]{1,0:T(8,128)(2,1)} %get-tuple-element.187), channel_id=1, source_target_pairs={{0,1},{1,0},{2,3},{3,2},{4,5},{5,4},{6,7},{7,6},{8,9},{9,8},{10,11... | collective-permute-start | bytes 6291464 | tf_op jit(solution)/shard_map/first_plane/ppermute | solution.py:567
  507.6 2.7 finish.4
  510.3 2.5 convert_add_fusion.4
  512.8 3.2 add_convert_fusion
  521.1 2.8 finish.6
  523.9 4.7 all-to-all-start.4
  528.6 3.7 collective-permute-done.59
  532.3 11.5 %collective-permute-done.61 = bf16[256,1024]{1,0:T(8,128)(2,1)} collective-permute-done((bf16[256,1024]{1,0:T(8,128)(2,1)}, bf16[256,1024]{1,0:T(8,128)(2,1)}, u32[]{:S(2)}, u32[]{:S(2)}) %collective-permute-start.61) | collective-permute-done | bytes 524320 | tf_op jit(solution)/shard_map/first_plane/ppermute | solution.py:570
  556.8 5.3 collective-permute-done.65
  563.1 13.5 %all-to-all-done.4.part_ref = bf16[4,512,256]{2,1,0:T(8,128)(2,1)} async-done(((bf16[4,512,256]{2,1,0:T(8,128)(2,1)}), bf16[4,512,256]{2,1,0:T(8,128)(2,1)}, u32[]{:S(2)}, u32[]{:S(2)}) %all-to-all-start.4) | async-done | bytes 1048608 | tf_op jit(solution)/shard_map/gate_grad/all_to_all | solution.py:685
  576.6 2.8 finish.5
  579.4 2.6 collective-permute-start.58
  582.3 2.8 collective-permute-done.67
  585.4 2.7 collective-permute-done.68
  588.3 5.0 collective-permute-start.69
  599.0 12.4 %reduce-scatter.2.cloned.1.call-done = bf16[512,1024]{1,0:T(8,128)(2,1)} async-done(((bf16[2048,1024]{1,0:T(8,128)(2,1)}), bf16[512,1024]{1,0:T(8,128)(2,1)}) %reduce-scatter.2.cloned.1.call-update) | async-done | bytes 1048592 | tf_op jit(solution)/shard_map/heads_grad/reduce_scatter | solution.py:835
  611.4 2.8 finish.7
  (460 shorter events, 182.2 us)
Async XLA Ops:
  7.2 121.6 %all-gather.6.cloned.1.call-start = ((), (), s32[]{:S(2)}) async-start(), calls=%async_computation.7 | async-start | bytes 3932160 | tf_op jit(solution)/shard_map/qkv_row/all_gather | solution.py:702
  7.2 26.7 %collective-permute-start = (bf16[1024,256]{1,0:T(8,128)(2,1)}, bf16[1024,256]{1,0:T(8,128)(2,1)}, u32[]{:S(2)}, u32[]{:S(2)}) collective-permute-start(bf16[1024,256]{1,0:T(8,128)(2,1)} %param.13), channel_id=1, source_target_pairs={{0,2},{1,3},{2,0},{3,1},{4,6},{5,7},{6,4},{7,5},{8,10},{9,11},{10,... | collective-permute-start | bytes 1572872 | tf_op jit(solution)/shard_map/inputs/ppermute | solution.py:570
  8.5 26.5 %collective-permute-start.1 = (bf16[1024,256]{1,0:T(8,128)(2,1)}, bf16[1024,256]{1,0:T(8,128)(2,1)}, u32[]{:S(2)}, u32[]{:S(2)}) collective-permute-start(bf16[1024,256]{1,0:T(8,128)(2,1)} %param.13), channel_id=1, source_target_pairs={{0,4},{1,5},{2,6},{3,7},{4,0},{5,1},{6,2},{7,3},{8,12},{9,13},{10,... | collective-permute-start | bytes 1572872 | tf_op jit(solution)/shard_map/inputs/ppermute | solution.py:570
  9.7 26.5 %collective-permute-start.2 = (bf16[1024,256]{1,0:T(8,128)(2,1)}, bf16[1024,256]{1,0:T(8,128)(2,1)}, u32[]{:S(2)}, u32[]{:S(2)}) collective-permute-start(bf16[1024,256]{1,0:T(8,128)(2,1)} %param.13), channel_id=1, source_target_pairs={{0,6},{1,7},{2,4},{3,5},{4,2},{5,3},{6,0},{7,1},{8,14},{9,15},{10,... | collective-permute-start | bytes 1572872 | tf_op jit(solution)/shard_map/inputs/ppermute | solution.py:570
  17.7 41.9 %all-to-all-start = ((bf16[4,512,256]{2,1,0:T(8,128)(2,1)}), bf16[4,512,256]{2,1,0:T(8,128)(2,1)S(1)}, u32[]{:S(2)}, u32[]{:S(2)}) async-start(bf16[4,512,256]{2,1,0:T(8,128)(2,1)} %pad_maximum_fusion), calls=%async_computation | async-start | bytes 2097152 | tf_op jit(solution)/shard_map/gate_row/all_to_all | solution.py:651
  43.5 85.2 %collective-permute-start.3 = (bf16[1024,1024]{1,0:T(8,128)(2,1)S(1)}, bf16[1024,1024]{1,0:T(8,128)(2,1)}, u32[]{:S(2)}, u32[]{:S(2)}) collective-permute-start(bf16[1024,1024]{1,0:T(8,128)(2,1)S(1)} %constant_dynamic-update-slice_fusion.15.own_ref.x_own), channel_id=1, source_target_pairs={{0,1},{1,0},{2,3},{3,2},{4,5},{5,4},{6,7},{7,6},{8,9},{9,8},{10,11... | collective-permute-start | bytes 6291464 | tf_op jit(solution)/shard_map/inputs/ppermute | solution.py:567
  59.5 54.7 %all-to-all-start.1 = ((bf16[4,512,256]{2,1,0:T(8,128)(2,1)}), bf16[4,512,256]{2,1,0:T(8,128)(2,1)}, u32[]{:S(2)}, u32[]{:S(2)}) async-start(bf16[4,512,256]{2,1,0:T(8,128)(2,1)} %pad_maximum_fusion.1), calls=%async_computation.1 | async-start | bytes 2097152 | tf_op jit(solution)/shard_map/up_row/all_to_all | solution.py:651
  73.7 90.7 %all-gather.8.cloned.1.call-start = ((), (), s32[]{:S(2)}) async-start(), calls=%async_computation.8 | async-start | bytes 1310720 | tf_op jit(solution)/shard_map/out_row/all_gather | solution.py:718
  73.7 16.8 %collective-permute-start.8 = (bf16[2048,256]{1,0:T(8,128)(2,1)S(1)}, bf16[2048,256]{1,0:T(8,128)(2,1)S(1)}, u32[]{:S(2)}, u32[]{:S(2)}) collective-permute-start(bf16[2048,256]{1,0:T(8,128)(2,1)S(1)} %bitcast.71), channel_id=1, source_target_pairs={{0,4},{1,5},{2,6},{3,7},{4,0},{5,1},{6,2},{7,3},{8,12},{9,13},{10,... | collective-permute-start | bytes 3145736 | tf_op jit(solution)/shard_map/gate_plane/ppermute | solution.py:570
  75.0 17.6 %collective-permute-start.7 = (bf16[2048,256]{1,0:T(8,128)(2,1)S(1)}, bf16[2048,256]{1,0:T(8,128)(2,1)S(1)}, u32[]{:S(2)}, u32[]{:S(2)}) collective-permute-start(bf16[2048,256]{1,0:T(8,128)(2,1)S(1)} %bitcast.72), channel_id=1, source_target_pairs={{0,2},{1,3},{2,0},{3,1},{4,6},{5,7},{6,4},{7,5},{8,10},{9,11},{10,... | collective-permute-start | bytes 3145736 | tf_op jit(solution)/shard_map/gate_plane/ppermute | solution.py:570
  91.4 34.2 %collective-permute-start.9 = (bf16[1024,256]{1,0:T(8,128)(2,1)}, bf16[1024,256]{1,0:T(8,128)(2,1)}, u32[]{:S(2)}, u32[]{:S(2)}) collective-permute-start(bf16[1024,256]{1,0:T(8,128)(2,1)} %slice.288), channel_id=1, source_target_pairs={{0,2},{1,3},{2,0},{3,1},{4,6},{5,7},{6,4},{7,5},{8,10},{9,11},{10,... | collective-permute-start | bytes 1572872 | tf_op jit(solution)/shard_map/gate_plane/ppermute | solution.py:570
  93.8 32.9 %collective-permute-start.10 = (bf16[1024,256]{1,0:T(8,128)(2,1)}, bf16[1024,256]{1,0:T(8,128)(2,1)}, u32[]{:S(2)}, u32[]{:S(2)}) collective-permute-start(bf16[1024,256]{1,0:T(8,128)(2,1)} %slice.289), channel_id=1, source_target_pairs={{0,4},{1,5},{2,6},{3,7},{4,0},{5,1},{6,2},{7,3},{8,12},{9,13},{10,... | collective-permute-start | bytes 1572872 | tf_op jit(solution)/shard_map/gate_plane/ppermute | solution.py:570
  114.3 38.3 %collective-permute-start.12 = (bf16[2048,256]{1,0:T(8,128)(2,1)}, bf16[2048,256]{1,0:T(8,128)(2,1)}, u32[]{:S(2)}, u32[]{:S(2)}) collective-permute-start(bf16[2048,256]{1,0:T(8,128)(2,1)} %bitcast.14.refs_5_.refs_13_), channel_id=1, source_target_pairs={{0,4},{1,5},{2,6},{3,7},{4,0},{5,1},{6,2},{7,3},{8,12},{9,13},{10,... | collective-permute-start | bytes 3145736 | tf_op jit(solution)/shard_map/up_plane/ppermute | solution.py:570
  115.5 37.1 %collective-permute-start.11 = (bf16[2048,256]{1,0:T(8,128)(2,1)}, bf16[2048,256]{1,0:T(8,128)(2,1)}, u32[]{:S(2)}, u32[]{:S(2)}) collective-permute-start(bf16[2048,256]{1,0:T(8,128)(2,1)} %bitcast.14.refs_5_.refs_13_), channel_id=1, source_target_pairs={{0,2},{1,3},{2,0},{3,1},{4,6},{5,7},{6,4},{7,5},{8,10},{9,11},{10,... | collective-permute-start | bytes 3145736 | tf_op jit(solution)/shard_map/up_plane/ppermute | solution.py:570
  116.7 41.5 %all-to-all-start.2 = ((bf16[4,512,256]{2,1,0:T(8,128)(2,1)}), bf16[4,512,256]{2,1,0:T(8,128)(2,1)}, u32[]{:S(2)}, u32[]{:S(2)}) async-start(bf16[4,512,256]{2,1,0:T(8,128)(2,1)} %pad_maximum_fusion.2), calls=%async_computation.2 | async-start | bytes 2097152 | tf_op jit(solution)/shard_map/down_row/all_to_all | solution.py:651
  125.6 92.6 %all-gather.10.cloned.1.call-start = ((), (), s32[]{:S(2)}) async-start(), calls=%async_computation.9 | async-start | bytes 2621440 | tf_op jit(solution)/shard_map/grad_row/all_gather | solution.py:722
  169.5 19.0 %collective-permute-start.15 = (bf16[1024,1024]{1,0:T(8,128)(2,1)}, bf16[1024,1024]{1,0:T(8,128)(2,1)}, u32[]{:S(2)}, u32[]{:S(2)}) collective-permute-start(bf16[1024,1024]{1,0:T(8,128)(2,1)} %get-tuple-element.117), channel_id=1, source_target_pairs={{0,1},{1,0},{2,3},{3,2},{4,5},{5,4},{6,7},{7,6},{8,9},{9,8},{10,11... | collective-permute-start | bytes 6291464 | tf_op jit(solution)/shard_map/mix_plane/ppermute | solution.py:567
  171.3 276.7 %all-gather.12.cloned.1.call-start = ((), (), s32[]{:S(2)}) async-start(), calls=%async_computation.11 | async-start | bytes 4718592 | tf_op jit(solution)/shard_map/middle_grad/all_gather | solution.py:805
  172.8 13.7 %collective-permute-start.13 = (bf16[1024,256]{1,0:T(8,128)(2,1)S(1)}, bf16[1024,256]{1,0:T(8,128)(2,1)S(1)}, u32[]{:S(2)}, u32[]{:S(2)}) collective-permute-start(bf16[1024,256]{1,0:T(8,128)(2,1)S(1)} %slice.290), channel_id=1, source_target_pairs={{0,2},{1,3},{2,0},{3,1},{4,6},{5,7},{6,4},{7,5},{8,10},{9,11},{10,... | collective-permute-start | bytes 1572872 | tf_op jit(solution)/shard_map/up_plane/ppermute | solution.py:570
  174.2 13.3 %collective-permute-start.14 = (bf16[1024,256]{1,0:T(8,128)(2,1)S(1)}, bf16[1024,256]{1,0:T(8,128)(2,1)S(1)}, u32[]{:S(2)}, u32[]{:S(2)}) collective-permute-start(bf16[1024,256]{1,0:T(8,128)(2,1)S(1)} %slice.291), channel_id=1, source_target_pairs={{0,4},{1,5},{2,6},{3,7},{4,0},{5,1},{6,2},{7,3},{8,12},{9,13},{10,... | collective-permute-start | bytes 1572872 | tf_op jit(solution)/shard_map/up_plane/ppermute | solution.py:570
  192.8 22.4 %collective-permute-start.18 = (bf16[256,1024]{1,0:T(8,128)(2,1)S(1)}, bf16[256,1024]{1,0:T(8,128)(2,1)S(1)}, u32[]{:S(2)}, u32[]{:S(2)}) collective-permute-start(bf16[256,1024]{1,0:T(8,128)(2,1)S(1)} %get-tuple-element.210), channel_id=1, source_target_pairs={{0,6},{1,7},{2,4},{3,5},{4,2},{5,3},{6,0},{7,1},{8,14},{9,15},{10,... | collective-permute-start | bytes 1572872 | tf_op jit(solution)/shard_map/mix_plane/ppermute | solution.py:570
  218.2 31.4 %collective-permute-start.28 = (bf16[2048,256]{1,0:T(8,128)(2,1)}, bf16[2048,256]{1,0:T(8,128)(2,1)}, u32[]{:S(2)}, u32[]{:S(2)}) collective-permute-start(bf16[2048,256]{1,0:T(8,128)(2,1)} %bitcast.15.refs_5_.refs_1_), channel_id=1, source_target_pairs={{0,4},{1,5},{2,6},{3,7},{4,0},{5,1},{6,2},{7,3},{8,12},{9,13},{10,... | collective-permute-start | bytes 3145736 | tf_op jit(solution)/shard_map/down_plane/ppermute | solution.py:570
  219.2 31.7 %collective-permute-start.27 = (bf16[2048,256]{1,0:T(8,128)(2,1)}, bf16[2048,256]{1,0:T(8,128)(2,1)}, u32[]{:S(2)}, u32[]{:S(2)}) collective-permute-start(bf16[2048,256]{1,0:T(8,128)(2,1)} %bitcast.15.refs_5_.refs_1_), channel_id=1, source_target_pairs={{0,2},{1,3},{2,0},{3,1},{4,6},{5,7},{6,4},{7,5},{8,10},{9,11},{10,... | collective-permute-start | bytes 3145736 | tf_op jit(solution)/shard_map/down_plane/ppermute | solution.py:570
  220.3 26.2 %collective-permute-start.22 = (bf16[256,1024]{1,0:T(8,128)(2,1)}, bf16[256,1024]{1,0:T(8,128)(2,1)}, u32[]{:S(2)}, u32[]{:S(2)}) collective-permute-start(bf16[256,1024]{1,0:T(8,128)(2,1)} %convert_element_type.293.refs_0_), channel_id=1, source_target_pairs={{0,16},{8,24},{16,0},{24,8},{1,17},{9,25},{17,1},{25,9},{2,18},{10... | collective-permute-start | bytes 1572872 | tf_op jit(solution)/shard_map/middle_row/ppermute | solution.py:584
  223.5 25.2 %collective-permute-start.19 = (bf16[256,1024]{1,0:T(8,128)(2,1)}, bf16[256,1024]{1,0:T(8,128)(2,1)}, u32[]{:S(2)}, u32[]{:S(2)}) collective-permute-start(bf16[256,1024]{1,0:T(8,128)(2,1)} %convert_element_type.293.refs_0_), channel_id=1, source_target_pairs={{0,8},{8,0},{16,24},{24,16},{1,9},{9,1},{17,25},{25,17},{2,10},{10... | collective-permute-start | bytes 1572872 | tf_op jit(solution)/shard_map/middle_row/ppermute | solution.py:584
  223.6 28.7 %collective-permute-start.20 = (bf16[256,1024]{1,0:T(8,128)(2,1)}, bf16[256,1024]{1,0:T(8,128)(2,1)}, u32[]{:S(2)}, u32[]{:S(2)}) collective-permute-start(bf16[256,1024]{1,0:T(8,128)(2,1)} %convert_element_type.293.refs_0_), channel_id=1, source_target_pairs={{0,1},{1,0},{2,3},{3,2},{4,5},{5,4},{6,7},{7,6},{8,9},{9,8},{10,11... | collective-permute-start | bytes 1572872 | tf_op jit(solution)/shard_map/middle_row/ppermute | solution.py:567
  246.6 14.3 %collective-permute-start.24 = (bf16[256,1024]{1,0:T(8,128)(2,1)}, bf16[256,1024]{1,0:T(8,128)(2,1)}, u32[]{:S(2)}, u32[]{:S(2)}) collective-permute-start(bf16[256,1024]{1,0:T(8,128)(2,1)} %collective-permute-done.22.refs_0_.refs_2_), channel_id=1, source_target_pairs={{0,8},{8,0},{16,24},{24,16},{1,9},{9,1},{17,25},{25,17},{2,10},{10... | collective-permute-start | bytes 1572872 | tf_op jit(solution)/shard_map/middle_row/ppermute | solution.py:584
  249.6 25.2 %collective-permute-start.23 = (bf16[256,1024]{1,0:T(8,128)(2,1)}, bf16[256,1024]{1,0:T(8,128)(2,1)S(1)}, u32[]{:S(2)}, u32[]{:S(2)}) collective-permute-start(bf16[256,1024]{1,0:T(8,128)(2,1)} %collective-permute-done.22.refs_0_.refs_2_), channel_id=1, source_target_pairs={{0,1},{1,0},{2,3},{3,2},{4,5},{5,4},{6,7},{7,6},{8,9},{9,8},{10,11... | collective-permute-start | bytes 1572872 | tf_op jit(solution)/shard_map/middle_row/ppermute | solution.py:567
  250.8 23.9 %collective-permute-start.29 = (bf16[1024,256]{1,0:T(8,128)(2,1)S(1)}, bf16[1024,256]{1,0:T(8,128)(2,1)S(1)}, u32[]{:S(2)}, u32[]{:S(2)}) collective-permute-start(bf16[1024,256]{1,0:T(8,128)(2,1)S(1)} %slice.292), channel_id=1, source_target_pairs={{0,2},{1,3},{2,0},{3,1},{4,6},{5,7},{6,4},{7,5},{8,10},{9,11},{10,... | collective-permute-start | bytes 1572872 | tf_op jit(solution)/shard_map/down_plane/ppermute | solution.py:570
  252.3 22.5 %collective-permute-start.30 = (bf16[1024,256]{1,0:T(8,128)(2,1)S(1)}, bf16[1024,256]{1,0:T(8,128)(2,1)S(1)}, u32[]{:S(2)}, u32[]{:S(2)}) collective-permute-start(bf16[1024,256]{1,0:T(8,128)(2,1)S(1)} %slice.293), channel_id=1, source_target_pairs={{0,4},{1,5},{2,6},{3,7},{4,0},{5,1},{6,2},{7,3},{8,12},{9,13},{10,... | collective-permute-start | bytes 1572872 | tf_op jit(solution)/shard_map/down_plane/ppermute | solution.py:570
  260.8 14.0 %collective-permute-start.25 = (bf16[256,1024]{1,0:T(8,128)(2,1)}, bf16[256,1024]{1,0:T(8,128)(2,1)S(1)}, u32[]{:S(2)}, u32[]{:S(2)}) collective-permute-start(bf16[256,1024]{1,0:T(8,128)(2,1)} %collective-permute-done.24.refs_1_.refs_3_), channel_id=1, source_target_pairs={{0,1},{1,0},{2,3},{3,2},{4,5},{5,4},{6,7},{7,6},{8,9},{9,8},{10,11... | collective-permute-start | bytes 1572872 | tf_op jit(solution)/shard_map/middle_row/ppermute | solution.py:567
  303.0 30.5 %collective-permute-start.35 = (f32[256,1]{0,1:T(1,128)}, f32[256,1]{0,1:T(1,128)}, u32[]{:S(2)}, u32[]{:S(2)}) collective-permute-start(f32[256,1]{0,1:T(1,128)} %bitcast.20), channel_id=1, source_target_pairs={{0,1},{1,0},{2,3},{3,2},{4,5},{5,4},{6,7},{7,6},{8,9},{9,8},{10,11... | collective-permute-start | bytes 3080 | tf_op jit(solution)/shard_map/ppermute | solution.py:567
  307.7 13.2 %collective-permute-start.32 = (bf16[256,1024]{1,0:T(8,128)(2,1)S(1)}, bf16[256,1024]{1,0:T(8,128)(2,1)S(1)}, u32[]{:S(2)}, u32[]{:S(2)}) collective-permute-start(bf16[256,1024]{1,0:T(8,128)(2,1)S(1)} %slice.425), channel_id=1, source_target_pairs={{0,8},{8,0},{16,24},{24,16},{1,9},{9,1},{17,25},{25,17},{2,10},{10... | collective-permute-start | bytes 1572872 | tf_op jit(solution)/shard_map/unit_grad/ppermute | solution.py:584
  316.8 19.9 %collective-permute-start.38 = (bf16[1024,256]{1,0:T(8,128)(2,1)S(1)}, bf16[1024,256]{1,0:T(8,128)(2,1)S(1)}, u32[]{:S(2)}, u32[]{:S(2)}) collective-permute-start(bf16[1024,256]{1,0:T(8,128)(2,1)S(1)} %get-tuple-element.216), channel_id=1, source_target_pairs={{0,4},{1,5},{2,6},{3,7},{4,0},{5,1},{6,2},{7,3},{8,12},{9,13},{10,... | collective-permute-start | bytes 1572872 | tf_op jit(solution)/shard_map/down_grad/ppermute | solution.py:570
  317.0 20.3 %collective-permute-start.40 = (bf16[1024,256]{1,0:T(8,128)(2,1)S(1)}, bf16[1024,256]{1,0:T(8,128)(2,1)S(1)}, u32[]{:S(2)}, u32[]{:S(2)}) collective-permute-start(bf16[1024,256]{1,0:T(8,128)(2,1)S(1)} %get-tuple-element.217), channel_id=1, source_target_pairs={{0,2},{1,3},{2,0},{3,1},{4,6},{5,7},{6,4},{7,5},{8,10},{9,11},{10,... | collective-permute-start | bytes 1572872 | tf_op jit(solution)/shard_map/down_grad/ppermute | solution.py:570
  334.2 25.5 %collective-permute-start.36 = (bf16[256,1024]{1,0:T(8,128)(2,1)}, bf16[256,1024]{1,0:T(8,128)(2,1)S(1)}, u32[]{:S(2)}, u32[]{:S(2)}) collective-permute-start(bf16[256,1024]{1,0:T(8,128)(2,1)} %fusion.7), channel_id=1, source_target_pairs={{0,16},{8,24},{16,0},{24,8},{1,17},{9,25},{17,1},{25,9},{2,18},{10... | collective-permute-start | bytes 1572872 | tf_op jit(solution)/shard_map/unit_grad/ppermute | solution.py:584
  336.9 25.0 %collective-permute-start.39 = (bf16[2048,256]{1,0:T(8,128)(2,1)S(1)}, bf16[2048,256]{1,0:T(8,128)(2,1)S(1)}, u32[]{:S(2)}, u32[]{:S(2)}) collective-permute-start(bf16[2048,256]{1,0:T(8,128)(2,1)S(1)} %pad_maximum_fusion.3), channel_id=1, source_target_pairs={{0,2},{1,3},{2,0},{3,1},{4,6},{5,7},{6,4},{7,5},{8,10},{9,11},{10,... | collective-permute-start | bytes 3145736 | tf_op jit(solution)/shard_map/down_grad/ppermute | solution.py:570
  337.5 24.4 %collective-permute-start.41 = (bf16[2048,256]{1,0:T(8,128)(2,1)S(1)}, bf16[2048,256]{1,0:T(8,128)(2,1)S(1)}, u32[]{:S(2)}, u32[]{:S(2)}) collective-permute-start(bf16[2048,256]{1,0:T(8,128)(2,1)S(1)} %pad_maximum_fusion.4), channel_id=1, source_target_pairs={{0,4},{1,5},{2,6},{3,7},{4,0},{5,1},{6,2},{7,3},{8,12},{9,13},{10,... | collective-permute-start | bytes 3145736 | tf_op jit(solution)/shard_map/down_grad/ppermute | solution.py:570
  338.2 22.1 %collective-permute-start.34 = (bf16[256,1024]{1,0:T(8,128)(2,1)S(1)}, bf16[256,1024]{1,0:T(8,128)(2,1)S(1)}, u32[]{:S(2)}, u32[]{:S(2)}) collective-permute-start(bf16[256,1024]{1,0:T(8,128)(2,1)S(1)} %slice.424), channel_id=1, source_target_pairs={{0,8},{8,0},{16,24},{24,16},{1,9},{9,1},{17,25},{25,17},{2,10},{10... | collective-permute-start | bytes 1572872 | tf_op jit(solution)/shard_map/unit_grad/ppermute | solution.py:584
  380.0 14.1 %collective-permute-start.48 = (bf16[1024,256]{1,0:T(8,128)(2,1)}, bf16[1024,256]{1,0:T(8,128)(2,1)S(1)}, u32[]{:S(2)}, u32[]{:S(2)}) collective-permute-start(bf16[1024,256]{1,0:T(8,128)(2,1)} %get-tuple-element.214), channel_id=1, source_target_pairs={{0,2},{1,3},{2,0},{3,1},{4,6},{5,7},{6,4},{7,5},{8,10},{9,11},{10,... | collective-permute-start | bytes 1572872 | tf_op jit(solution)/shard_map/gate_grad/ppermute | solution.py:570
  381.2 16.7 %collective-permute-start.47 = (bf16[1024,256]{1,0:T(8,128)(2,1)S(1)}, bf16[1024,256]{1,0:T(8,128)(2,1)S(1)}, u32[]{:S(2)}, u32[]{:S(2)}) collective-permute-start(bf16[1024,256]{1,0:T(8,128)(2,1)S(1)} %get-tuple-element.215), channel_id=1, source_target_pairs={{0,4},{1,5},{2,6},{3,7},{4,0},{5,1},{6,2},{7,3},{8,12},{9,13},{10,... | collective-permute-start | bytes 1572872 | tf_op jit(solution)/shard_map/gate_grad/ppermute | solution.py:570
  388.5 32.5 %collective-permute-start.44 = (bf16[512,1024]{1,0:T(8,128)(2,1)}, bf16[512,1024]{1,0:T(8,128)(2,1)S(1)}, u32[]{:S(2)}, u32[]{:S(2)}) collective-permute-start(bf16[512,1024]{1,0:T(8,128)(2,1)} %get-tuple-element.149), channel_id=1, source_target_pairs={{0,1},{1,0},{2,3},{3,2},{4,5},{5,4},{6,7},{7,6},{8,9},{9,8},{10,11... | collective-permute-start | bytes 3145736 | tf_op jit(solution)/shard_map/feed/ppermute | solution.py:567
  400.0 16.4 %collective-permute-start.49 = (bf16[1024,256]{1,0:T(8,128)(2,1)}, bf16[1024,256]{1,0:T(8,128)(2,1)S(1)}, u32[]{:S(2)}, u32[]{:S(2)}) collective-permute-start(bf16[1024,256]{1,0:T(8,128)(2,1)} %get-tuple-element.212), channel_id=1, source_target_pairs={{0,4},{1,5},{2,6},{3,7},{4,0},{5,1},{6,2},{7,3},{8,12},{9,13},{10,... | collective-permute-start | bytes 1572872 | tf_op jit(solution)/shard_map/up_grad/ppermute | solution.py:570
  402.3 15.3 %collective-permute-start.51 = (bf16[1024,256]{1,0:T(8,128)(2,1)S(1)}, bf16[1024,256]{1,0:T(8,128)(2,1)S(1)}, u32[]{:S(2)}, u32[]{:S(2)}) collective-permute-start(bf16[1024,256]{1,0:T(8,128)(2,1)S(1)} %get-tuple-element.213), channel_id=1, source_target_pairs={{0,2},{1,3},{2,0},{3,1},{4,6},{5,7},{6,4},{7,5},{8,10},{9,11},{10,... | collective-permute-start | bytes 1572872 | tf_op jit(solution)/shard_map/up_grad/ppermute | solution.py:570
  409.8 23.2 %collective-permute-start.42 = (bf16[512,1024]{1,0:T(8,128)(2,1)}, bf16[512,1024]{1,0:T(8,128)(2,1)}, u32[]{:S(2)}, u32[]{:S(2)}) collective-permute-start(bf16[512,1024]{1,0:T(8,128)(2,1)} %get-tuple-element.145), channel_id=1, source_target_pairs={{0,1},{1,0},{2,3},{3,2},{4,5},{5,4},{6,7},{7,6},{8,9},{9,8},{10,11... | collective-permute-start | bytes 3145736 | tf_op jit(solution)/shard_map/feed/ppermute | solution.py:567
  417.7 23.4 %collective-permute-start.50 = (bf16[2048,256]{1,0:T(8,128)(2,1)}, bf16[2048,256]{1,0:T(8,128)(2,1)}, u32[]{:S(2)}, u32[]{:S(2)}) collective-permute-start(bf16[2048,256]{1,0:T(8,128)(2,1)} %pad_maximum_fusion.7), channel_id=1, source_target_pairs={{0,2},{1,3},{2,0},{3,1},{4,6},{5,7},{6,4},{7,5},{8,10},{9,11},{10,... | collective-permute-start | bytes 3145736 | tf_op jit(solution)/shard_map/up_grad/ppermute | solution.py:570
  418.9 25.0 %collective-permute-start.52 = (bf16[2048,256]{1,0:T(8,128)(2,1)}, bf16[2048,256]{1,0:T(8,128)(2,1)}, u32[]{:S(2)}, u32[]{:S(2)}) collective-permute-start(bf16[2048,256]{1,0:T(8,128)(2,1)} %pad_maximum_fusion.8), channel_id=1, source_target_pairs={{0,4},{1,5},{2,6},{3,7},{4,0},{5,1},{6,2},{7,3},{8,12},{9,13},{10,... | collective-permute-start | bytes 3145736 | tf_op jit(solution)/shard_map/up_grad/ppermute | solution.py:570
  423.2 13.9 %collective-permute-start.45 = (bf16[256,1024]{1,0:T(8,128)(2,1)}, bf16[256,1024]{1,0:T(8,128)(2,1)}, u32[]{:S(2)}, u32[]{:S(2)}) collective-permute-start(bf16[256,1024]{1,0:T(8,128)(2,1)} %slice.245), channel_id=1, source_target_pairs={{0,8},{8,0},{16,24},{24,16},{1,9},{9,1},{17,25},{25,17},{2,10},{10... | collective-permute-start | bytes 1572872 | tf_op jit(solution)/shard_map/feed/ppermute | solution.py:584
  428.1 40.9 %all-to-all-start.3 = ((bf16[4,512,256]{2,1,0:T(8,128)(2,1)}), bf16[4,512,256]{2,1,0:T(8,128)(2,1)}, u32[]{:S(2)}, u32[]{:S(2)}) async-start(bf16[4,512,256]{2,1,0:T(8,128)(2,1)} %bitcast.82), calls=%async_computation.3 | async-start | bytes 2097152 | tf_op jit(solution)/shard_map/down_grad/all_to_all | solution.py:685
  432.4 32.7 %collective-permute-start.53 = (bf16[2048,256]{1,0:T(8,128)(2,1)}, bf16[2048,256]{1,0:T(8,128)(2,1)}, u32[]{:S(2)}, u32[]{:S(2)}) collective-permute-start(bf16[2048,256]{1,0:T(8,128)(2,1)} %pad_maximum_fusion.5), channel_id=1, source_target_pairs={{0,2},{1,3},{2,0},{3,1},{4,6},{5,7},{6,4},{7,5},{8,10},{9,11},{10,... | collective-permute-start | bytes 3145736 | tf_op jit(solution)/shard_map/gate_grad/ppermute | solution.py:570
  433.0 32.2 %collective-permute-start.54 = (bf16[2048,256]{1,0:T(8,128)(2,1)}, bf16[2048,256]{1,0:T(8,128)(2,1)}, u32[]{:S(2)}, u32[]{:S(2)}) collective-permute-start(bf16[2048,256]{1,0:T(8,128)(2,1)} %pad_maximum_fusion.6), channel_id=1, source_target_pairs={{0,4},{1,5},{2,6},{3,7},{4,0},{5,1},{6,2},{7,3},{8,12},{9,13},{10,... | collective-permute-start | bytes 3145736 | tf_op jit(solution)/shard_map/gate_grad/ppermute | solution.py:570
  437.0 73.3 %collective-permute-start.43 = (bf16[256,1024]{1,0:T(8,128)(2,1)}, bf16[256,1024]{1,0:T(8,128)(2,1)}, u32[]{:S(2)}, u32[]{:S(2)}) collective-permute-start(bf16[256,1024]{1,0:T(8,128)(2,1)} %slice.243), channel_id=1, source_target_pairs={{0,8},{8,0},{16,24},{24,16},{1,9},{9,1},{17,25},{25,17},{2,10},{10... | collective-permute-start | bytes 1572872 | tf_op jit(solution)/shard_map/feed/ppermute | solution.py:584
  441.1 69.2 %collective-permute-start.46 = (bf16[256,1024]{1,0:T(8,128)(2,1)}, bf16[256,1024]{1,0:T(8,128)(2,1)}, u32[]{:S(2)}, u32[]{:S(2)}) collective-permute-start(bf16[256,1024]{1,0:T(8,128)(2,1)} %fusion.33), channel_id=1, source_target_pairs={{0,16},{8,24},{16,0},{24,8},{1,17},{9,25},{17,1},{25,9},{2,18},{10... | collective-permute-start | bytes 1572872 | tf_op jit(solution)/shard_map/feed/ppermute | solution.py:584
  469.0 52.2 %all-to-all-start.5 = ((bf16[4,512,256]{2,1,0:T(8,128)(2,1)}), bf16[4,512,256]{2,1,0:T(8,128)(2,1)}, u32[]{:S(2)}, u32[]{:S(2)}) async-start(bf16[4,512,256]{2,1,0:T(8,128)(2,1)} %bitcast.81), calls=%async_computation.6 | async-start | bytes 2097152 | tf_op jit(solution)/shard_map/up_grad/all_to_all | solution.py:685
  474.6 136.8 %reduce-scatter.2.cloned.1.call-start = ((), (), s32[]{:S(2)}) async-start(), calls=%async_computation.10 | async-start | bytes 5242880 | tf_op jit(solution)/shard_map/heads_grad/reduce_scatter | solution.py:835
  498.6 14.2 %collective-permute-start.55 = (bf16[1024,1024]{1,0:T(8,128)(2,1)}, bf16[1024,1024]{1,0:T(8,128)(2,1)}, u32[]{:S(2)}, u32[]{:S(2)}) collective-permute-start(bf16[1024,1024]{1,0:T(8,128)(2,1)} %get-tuple-element.187), channel_id=1, source_target_pairs={{0,1},{1,0},{2,3},{3,2},{4,5},{5,4},{6,7},{7,6},{8,9},{9,8},{10,11... | collective-permute-start | bytes 6291464 | tf_op jit(solution)/shard_map/first_plane/ppermute | solution.py:567
  518.5 13.8 %collective-permute-start.59 = (bf16[256,1024]{1,0:T(8,128)(2,1)}, bf16[256,1024]{1,0:T(8,128)(2,1)}, u32[]{:S(2)}, u32[]{:S(2)}) collective-permute-start(bf16[256,1024]{1,0:T(8,128)(2,1)} %get-tuple-element.206), channel_id=1, source_target_pairs={{0,2},{1,3},{2,0},{3,1},{4,6},{5,7},{6,4},{7,5},{8,10},{9,11},{10,... | collective-permute-start | bytes 1572872 | tf_op jit(solution)/shard_map/first_plane/ppermute | solution.py:570
  518.5 13.8 %collective-permute-start.60 = (bf16[256,1024]{1,0:T(8,128)(2,1)}, bf16[256,1024]{1,0:T(8,128)(2,1)}, u32[]{:S(2)}, u32[]{:S(2)}) collective-permute-start(bf16[256,1024]{1,0:T(8,128)(2,1)} %get-tuple-element.208), channel_id=1, source_target_pairs={{0,4},{1,5},{2,6},{3,7},{4,0},{5,1},{6,2},{7,3},{8,12},{9,13},{10,... | collective-permute-start | bytes 1572872 | tf_op jit(solution)/shard_map/first_plane/ppermute | solution.py:570
  519.1 24.7 %collective-permute-start.61 = (bf16[256,1024]{1,0:T(8,128)(2,1)}, bf16[256,1024]{1,0:T(8,128)(2,1)}, u32[]{:S(2)}, u32[]{:S(2)}) collective-permute-start(bf16[256,1024]{1,0:T(8,128)(2,1)} %get-tuple-element.207), channel_id=1, source_target_pairs={{0,6},{1,7},{2,4},{3,5},{4,2},{5,3},{6,0},{7,1},{8,14},{9,15},{10,... | collective-permute-start | bytes 1572872 | tf_op jit(solution)/shard_map/first_plane/ppermute | solution.py:570
  523.9 52.7 %all-to-all-start.4 = ((bf16[4,512,256]{2,1,0:T(8,128)(2,1)}), bf16[4,512,256]{2,1,0:T(8,128)(2,1)}, u32[]{:S(2)}, u32[]{:S(2)}) async-start(bf16[4,512,256]{2,1,0:T(8,128)(2,1)} %bitcast.80), calls=%async_computation.5 | async-start | bytes 2097152 | tf_op jit(solution)/shard_map/gate_grad/all_to_all | solution.py:685
  552.6 29.7 %collective-permute-start.56 = (bf16[256,256]{1,0:T(8,128)(2,1)S(1)}, bf16[256,256]{1,0:T(8,128)(2,1)S(1)}, u32[]{:S(2)}, u32[]{:S(2)}) collective-permute-start(bf16[256,256]{1,0:T(8,128)(2,1)S(1)} %get-tuple-element.242), channel_id=1, source_target_pairs={{0,2},{1,3},{2,0},{3,1},{4,6},{5,7},{6,4},{7,5},{8,10},{9,11},{10,... | collective-permute-start | bytes 393224 | tf_op jit(solution)/shard_map/block_out/ppermute | solution.py:570
  553.2 32.2 %collective-permute-start.57 = (bf16[256,256]{1,0:T(8,128)(2,1)S(1)}, bf16[256,256]{1,0:T(8,128)(2,1)S(1)}, u32[]{:S(2)}, u32[]{:S(2)}) collective-permute-start(bf16[256,256]{1,0:T(8,128)(2,1)S(1)} %get-tuple-element.241), channel_id=1, source_target_pairs={{0,4},{1,5},{2,6},{3,7},{4,0},{5,1},{6,2},{7,3},{8,12},{9,13},{10,... | collective-permute-start | bytes 393224 | tf_op jit(solution)/shard_map/block_out/ppermute | solution.py:570
  562.3 19.7 %collective-permute-start.66 = (f32[2,4,2,256]{3,2,1,0:T(2,128)S(1)}, f32[2,4,2,256]{3,2,1,0:T(2,128)S(1)}, u32[]{:S(2)}, u32[]{:S(2)}) collective-permute-start(f32[2,4,2,256]{3,2,1,0:T(2,128)S(1)} %bitcast.84), channel_id=1, source_target_pairs={{0,1},{1,0},{2,3},{3,2},{4,5},{5,4},{6,7},{7,6},{8,9},{9,8},{10,11... | collective-permute-start | bytes 49160 | tf_op jit(solution)/shard_map/gains/ppermute | solution.py:636
  579.4 15.1 %collective-permute-start.58 = (bf16[256,256]{1,0:T(8,128)(2,1)S(1)}, bf16[256,256]{1,0:T(8,128)(2,1)S(1)}, u32[]{:S(2)}, u32[]{:S(2)}) collective-permute-start(bf16[256,256]{1,0:T(8,128)(2,1)S(1)} %get-tuple-element.240), channel_id=1, source_target_pairs={{0,6},{1,7},{2,4},{3,5},{4,2},{5,3},{6,0},{7,1},{8,14},{9,15},{10,... | collective-permute-start | bytes 393224 | tf_op jit(solution)/shard_map/block_out/ppermute | solution.py:570
  (121 other events, 718.4 us)
Sparse Core Ops, SparseCore 0:
  14.8 103.9 all-gather.5
  120.3 44.0 all-gather.7
  171.4 43.6 all-gather.9
  366.1 43.5 all-gather.11
  512.9 98.4 reduce-scatter.1

commit v13 on v12

--- a/solution.py
+++ b/solution.py
@@ -713,7 +713,7 @@
         gate_whole = exchange(cut(scaled(gate_weight, gain_two)))
         gate_whole = after(gate_whole, g_part, cosine, front, back, start_row, up_cut, down_cut, out_block)
     with jax.named_scope("up_row"):
-        up_whole = exchange(after(up_cut, gate_whole))
+        up_whole = exchange(after(up_cut, gate_whole, x_other))
     with jax.named_scope("out_row"):
         out_full = lax.all_gather(after(out_block, x_own), "row", axis=0, tiled=True)
     with jax.named_scope("down_row"):
@@ -728,7 +728,7 @@
         feat, x_own, x_other, qkv_full, cosine, front, back
     )
     mixed, logs = attend(
-        after(query, gates[1:3], up_whole),
+        after(query, gates[1:3], up_whole, ups[1:3]),
         key, value, start_row,
     )
     mixed_in = after(mixed, gates[3:], ups[1:3], down_whole)
@@ -744,8 +744,8 @@
 
     with jax.named_scope("mix_plane"):
         own, other = unfold(feat, "mix", [mixed_in], [out_full])
-        middle = token_part(x_own, 0).astype(F32) + scatter_parts(join_cores(after(own, ups[3:]), other))
-    middle_low = after(middle.astype(BF16), g_own)
+        middle = token_part(x_own, 0).astype(F32) + scatter_parts(join_cores(own, other))
+    middle_low = after(middle.astype(BF16), ups[3:], g_own)
     with jax.named_scope("middle_row"):
         m_list = gather_row(middle_low)
         m_others = [core_swap(m) for m in m_list]
@@ -764,7 +764,7 @@
         found.append(activate(feat, [first, m_list[pair.start + 1]], m_others[pair], gates, ups))
     hiddens = [f[0] for f in found]
     with jax.named_scope("grad_row"):
-        g_own = after(g_own, m_others, hiddens[0])
+        g_own = after(g_own, hiddens[0])
         g_other = core_swap(g_own)
     parts, scaled_grads, down_parts = [None] * rows, [None] * len(pairs), None
     down_middle = None
@@ -774,7 +774,7 @@
             if down_parts is None:
                 slope_gate = after(slope_gate, hiddens)
             else:
-                slope_gate = after(slope_gate, down_parts[:1], low_kept)
+                slope_gate = slope_gate
             gate_grad, up_grad, own, other = units_back(
                 feat, starts[pairs[at]], g_own, g_other, slope_gate, slope_up, scale, gates, ups, downs
             )
@@ -804,7 +804,7 @@
     with jax.named_scope("middle_grad"):
         d_parts = lax.all_gather(d_low, "col")
     with jax.named_scope("feed"):
-        kept = [unfold(feat, "feed", [after(h, low_kept, d_low)], downs) for h in hiddens]
+        kept = [unfold(feat, "feed", [after(h, low_kept)], downs) for h in hiddens]
         shares = []
         for own, other in kept:
             low = after((own.astype(F32) + core_swap(other).astype(F32)).astype(BF16), d_low)
@@ -827,7 +827,10 @@
     with jax.named_scope("gate_grad"):
         gate_total = plane_second(gate_middle, *((query_grad,)))
         gate_blocks = give_back(gate_total)
-    heads_in = after(query_grad, down_blocks, gate_total)
+    with jax.named_scope("up_grad"):
+        up_total = plane_second(plane_first([after(a, gate_middle[1:]) for a in up_parts]))
+        up_blocks = give_back(up_total)
+    heads_in = after(query_grad, down_blocks)
     heads_part, gain_dots = heads_outer(
         feat, cores, x_own, x_other, d_parts, heads_in, key_grad, value_grad, mixed, scale_one, qkv_full
     )
@@ -838,9 +841,6 @@
             *unfold(feat, "first_grad", [after(query_grad, heads_part), key_grad, value_grad], [qkv_full])
         )
         first_unit_grad = scatter_parts(first_low)
-    with jax.named_scope("up_grad"):
-        up_total = plane_second(plane_first([after(a, gate_middle[1:]) for a in up_parts]))
-        up_blocks = give_back(up_total)
     with jax.named_scope("block_out"):
         block_out = to_home(after(feed_low, up_total, first_low))
     scale_first = token_part(scale_one, 0)

time: 632 us -> 622 us (0.984)
  the two profiles are of different devices: /device:TPU:9 before, /device:TPU:0 now
where the time goes in v13:
time: 622 us; the launch traced here: 611 us
  waiting for transfers between devices  225 us (36%)
  Pallas kernels  130 us (21%)
  starting transfers between devices  95.8 us (15%)
  local copies, waits for them, and re-layouts  79.8 us (13%)
  other arithmetic  65.1 us (10%)
  between operations  15.4 us (2%)
    ppermute x42, waiting for transfers between devices, plane_swap(): return lax.ppermute(a, 'col', [(i, i ^ 2 * step) for i in range(cols)])  104 us
    ppermute x42, starting transfers between devices, plane_swap(): return lax.ppermute(a, 'col', [(i, i ^ 2 * step) for i in range(cols)])  50.7 us
    unnamed x200, local copies, waits for them, and re-layouts  50.6 us
    ppermute x12, waiting for transfers between devices, row_swap(): return lax.ppermute(a, 'row', [(i, i ^ step) for i in range(rows)])  48 us
    all_to_all x3, waiting for transfers between devices, exchange(): got = lax.all_to_all(pieces, 'row', split_axis=0, concat_axis=0, tiled=True)  39.4 us
    pallas_call x4, Pallas kernels, unfold(): pl.pallas_call(functools.partial(unfold_kernel, feat, len(lefts)), grid=(...  24.6 us
    all_to_all x3, waiting for transfers between devices, give_back(): return lax.all_to_all(total, 'row', split_axis=0, concat_axis=0, tiled=True)  23.9 us
    pallas_call x2, Pallas kernels, units_back(): pl.pallas_call(functools.partial(units_back_kernel, feat, parts, count),...  20.6 us
  transfers between devices with their start and end apart: 83, of which 41 were waited for; matrix products, arithmetic and copies ran while one was open for 15% of the time, Pallas kernels for 17%

profile of v13, /device:TPU:0, one launch (start us, length us, event | category | flops | bytes accessed | tf_op | source)
XLA Modules:
  0.0 610.6 jit_solution(13442869758332900776)
XLA Ops:
  7.2 3.0 collective-permute-start
  18.8 5.3 all-to-all-start
  28.4 6.8 %collective-permute-done.1 = bf16[1024,256]{1,0:T(8,128)(2,1)} collective-permute-done((bf16[1024,256]{1,0:T(8,128)(2,1)}, bf16[1024,256]{1,0:T(8,128)(2,1)}, u32[]{:S(2)}, u32[]{:S(2)}) %collective-permute-start.1) | collective-permute-done | bytes 524320 | tf_op jit(solution)/shard_map/inputs/ppermute | solution.py:570
  53.9 2.8 collective-permute-done.5
  58.9 18.1 %all-to-all-done = bf16[4,512,256]{2,1,0:T(8,128)(2,1)S(1)} async-done(((bf16[4,512,256]{2,1,0:T(8,128)(2,1)}), bf16[4,512,256]{2,1,0:T(8,128)(2,1)S(1)}, u32[]{:S(2)}, u32[]{:S(2)}) %all-to-all-start) | async-done | bytes 1048608 | tf_op jit(solution)/shard_map/gate_row/all_to_all | solution.py:651
  80.1 4.2 all-to-all-start.1
  84.4 10.8 %collective-permute-done.8.refs_8_.refs_11_ = bf16[2048,256]{1,0:T(8,128)(2,1)} collective-permute-done((bf16[2048,256]{1,0:T(8,128)(2,1)S(1)}, bf16[2048,256]{1,0:T(8,128)(2,1)}, u32[]{:S(2)}, u32[]{:S(2)}) %collective-permute-start.8) | collective-permute-done | bytes 1048608 | tf_op jit(solution)/shard_map/gate_plane/ppermute | solution.py:570
  97.1 2.5 collective-permute-start.11
  102.9 4.6 collective-permute-done.11
  108.6 3.5 collective-permute-done.12
  114.2 7.9 %all-to-all-done.1 = bf16[4,512,256]{2,1,0:T(8,128)(2,1)} async-done(((bf16[4,512,256]{2,1,0:T(8,128)(2,1)}), bf16[4,512,256]{2,1,0:T(8,128)(2,1)}, u32[]{:S(2)}, u32[]{:S(2)}) %all-to-all-start.1) | async-done | bytes 1048608 | tf_op jit(solution)/shard_map/up_row/all_to_all | solution.py:651
  124.8 4.2 all-to-all-start.2
  134.4 5.6 project.1
  146.3 10.0 %attend.1 = (bf16[1024,256]{1,0:T(8,128)(2,1)}, f32[2,2,1024]{2,1,0:T(2,128)}) custom-call(bf16[1024,256]{1,0:T(8,128)(2,1)} %copy-done.65, bf16[1024,256]{1,0:T(8,128)(2,1)} %copy-done.66, bf16[1024,256]{1,0:T(8,128)(2,1)} %copy-done.67, s32[1,1024]{1,0:T(1,128)} %bitcast.100), custom_call_target="tpu_custom_call" | custom-call | flops 99999997952 | bytes 1 | tf_op jit(solution)/shard_map/attend/pallas_call | solution.py:437
  156.3 13.4 %all-to-all-done.2 = bf16[4,512,256]{2,1,0:T(8,128)(2,1)} async-done(((bf16[4,512,256]{2,1,0:T(8,128)(2,1)}), bf16[4,512,256]{2,1,0:T(8,128)(2,1)}, u32[]{:S(2)}, u32[]{:S(2)}) %all-to-all-start.2) | async-done | bytes 1048608 | tf_op jit(solution)/shard_map/down_row/all_to_all | solution.py:651
  169.7 5.1 mix.1
  179.3 2.7 add_convert_fusion.1
  185.6 5.2 collective-permute-done.17
  190.9 12.7 %collective-permute-done.18 = bf16[1024,256]{1,0:T(8,128)(2,1)S(1)} collective-permute-done((bf16[1024,256]{1,0:T(8,128)(2,1)S(1)}, bf16[1024,256]{1,0:T(8,128)(2,1)S(1)}, u32[]{:S(2)}, u32[]{:S(2)}) %collective-permute-start.18) | collective-permute-done | bytes 524320 | tf_op jit(solution)/shard_map/up_plane/ppermute | solution.py:570
  204.6 9.5 %collective-permute-done.15 = bf16[256,1024]{1,0:T(8,128)(2,1)S(1)} collective-permute-done((bf16[256,1024]{1,0:T(8,128)(2,1)S(1)}, bf16[256,1024]{1,0:T(8,128)(2,1)S(1)}, u32[]{:S(2)}, u32[]{:S(2)}) %collective-permute-start.15) | collective-permute-done | bytes 524320 | tf_op jit(solution)/shard_map/mix_plane/ppermute | solution.py:570
  224.2 19.3 %collective-permute-done.31.refs_0_.refs_2_ = bf16[256,1024]{1,0:T(8,128)(2,1)} collective-permute-done((bf16[256,1024]{1,0:T(8,128)(2,1)}, bf16[256,1024]{1,0:T(8,128)(2,1)}, u32[]{:S(2)}, u32[]{:S(2)}) %collective-permute-start.31) | collective-permute-done | bytes 524320 | tf_op jit(solution)/shard_map/middle_row/ppermute | solution.py:584
  250.8 6.7 %collective-permute-done.32.refs_1_.refs_3_ = bf16[256,1024]{1,0:T(8,128)(2,1)S(1)} collective-permute-done((bf16[256,1024]{1,0:T(8,128)(2,1)}, bf16[256,1024]{1,0:T(8,128)(2,1)S(1)}, u32[]{:S(2)}, u32[]{:S(2)}) %collective-permute-start.32) | collective-permute-done | bytes 524320 | tf_op jit(solution)/shard_map/middle_row/ppermute | solution.py:584
  259.0 8.3 %activate.2 = (bf16[512,1024]{1,0:T(8,128)(2,1)S(1)}, bf16[512,1024]{1,0:T(8,128)(2,1)S(1)}, bf16[512,1024]{1,0:T(8,128)(2,1)S(1)}, f32[512,1]{1,0:T(8,128)S(1)}) custom-call(bf16[256,1024]{1,0:T(8,128)(2,1)S(1)} %copy-done.18, bf16[256,1024]{1,0:T(8,128)(2,1)} %collective-permute-done.19.refs_1_, ...), custom_call_target="tpu_custom_call" | custom-call | flops 74999996416 | bytes 1 | tf_op jit(solution)/shard_map/activate/pallas_call | solution.py:173
  269.4 8.5 %activate.3 = (bf16[512,1024]{1,0:T(8,128)(2,1)S(1)}, bf16[512,1024]{1,0:T(8,128)(2,1)S(1)}, bf16[512,1024]{1,0:T(8,128)(2,1)S(1)}, f32[512,1]{1,0:T(8,128)S(1)}) custom-call(bf16[256,1024]{1,0:T(8,128)(2,1)} %collective-permute-done.31.refs_0_.refs_2_, bf16[256,1024]{1,0:T(8,128)(2,1)S(1)} %collective-permute-done.32.refs_1_.refs_3_, ...), custom_call_target="tpu_custom_call" | custom-call | flops 74999996416 | bytes 1 | tf_op jit(solution)/shard_map/activate/pallas_call | solution.py:173
  280.2 10.3 %units_back.3 = (bf16[512,1024]{1,0:T(8,128)(2,1)S(1)}, bf16[512,1024]{1,0:T(8,128)(2,1)S(1)}, bf16[512,1024]{1,0:T(8,128)(2,1)S(1)}, bf16[512,1024]{1,0:T(8,128)(2,1)S(1)}) custom-call(s32[2]{0:T(128)S(1)} %pad_add_fusion.1.starts, bf16[1024,1024]{1,0:T(8,128)(2,1)} %all-gather.10.cloned.1.call-done.refs_0_, bf16[1024,1024]{1,0:T(8,128)(2,1)} %copy-done.34, ...), custom_call_target="tpu_custom_call" | custom-call | flops 92999999488 | bytes 1 | tf_op jit(solution)/shard_map/unit_grad/units_back/pallas_call | solution.py:239
  294.3 10.3 %units_back.2 = (bf16[512,1024]{1,0:T(8,128)(2,1)S(1)}, bf16[512,1024]{1,0:T(8,128)(2,1)S(1)}, bf16[512,1024]{1,0:T(8,128)(2,1)S(1)}, bf16[512,1024]{1,0:T(8,128)(2,1)S(1)}) custom-call(s32[2]{0:T(128)S(1)} %pad_add_fusion.starts, bf16[1024,1024]{1,0:T(8,128)(2,1)} %all-gather.10.cloned.1.call-done.refs_0_, bf16[1024,1024]{1,0:T(8,128)(2,1)} %copy-done.34, ...), custom_call_target="tpu_custom_call" | custom-call | flops 92999999488 | bytes 1 | tf_op jit(solution)/shard_map/unit_grad/units_back/pallas_call | solution.py:239
  308.7 6.4 %down_outer.1 = (bf16[2048,256]{1,0:T(8,128)(2,1)S(1)}, bf16[2048,256]{1,0:T(8,128)(2,1)S(1)}, bf16[2048,256]{1,0:T(8,128)(2,1)S(1)}, bf16[2048,256]{1,0:T(8,128)(2,1)S(1)}) custom-call(s32[4]{0:T(128)S(1)} %pad_add_fusion.2.starts, bf16[1024,1024]{1,0:T(8,128)(2,1)S(1)} %copy-done.33, bf16[1024,1024]{1,0:T(8,128)(2,1)S(1)} %copy-done.35, ...), custom_call_target="tpu_custom_call" | custom-call | flops 62999998464 | bytes 1 | tf_op jit(solution)/shard_map/down_grad/down_outer/pallas_call | solution.py:282
  322.9 6.4 %collective-permute-done.41 = bf16[1024,256]{1,0:T(8,128)(2,1)S(1)} collective-permute-done((bf16[1024,256]{1,0:T(8,128)(2,1)S(1)}, bf16[1024,256]{1,0:T(8,128)(2,1)S(1)}, u32[]{:S(2)}, u32[]{:S(2)}) %collective-permute-start.41) | collective-permute-done | bytes 524320 | tf_op jit(solution)/shard_map/down_grad/ppermute | solution.py:570
  331.1 3.2 collective-permute-done.39
  334.6 6.6 %collective-permute-done.28 = bf16[256,1024]{1,0:T(8,128)(2,1)S(1)} collective-permute-done((bf16[256,1024]{1,0:T(8,128)(2,1)S(1)}, bf16[256,1024]{1,0:T(8,128)(2,1)S(1)}, u32[]{:S(2)}, u32[]{:S(2)}) %collective-permute-start.28) | collective-permute-done | bytes 524320 | tf_op jit(solution)/shard_map/unit_grad/ppermute | solution.py:584
  341.2 6.3 %collective-permute-done.37 = bf16[256,1024]{1,0:T(8,128)(2,1)S(1)} collective-permute-done((bf16[256,1024]{1,0:T(8,128)(2,1)S(1)}, bf16[256,1024]{1,0:T(8,128)(2,1)S(1)}, u32[]{:S(2)}, u32[]{:S(2)}) %collective-permute-start.37) | collective-permute-done | bytes 524320 | tf_op jit(solution)/shard_map/unit_grad/ppermute | solution.py:584
  348.1 6.5 %up_outer.1 = (bf16[2048,256]{1,0:T(8,128)(2,1)S(1)}, bf16[2048,256]{1,0:T(8,128)(2,1)S(1)}, bf16[2048,256]{1,0:T(8,128)(2,1)S(1)}, bf16[2048,256]{1,0:T(8,128)(2,1)S(1)}) custom-call(s32[4]{0:T(128)S(1)} %pad_add_fusion.2.starts, bf16[256,1024]{1,0:T(8,128)(2,1)S(1)} %copy-done.19, bf16[256,1024]{1,0:T(8,128)(2,1)} %collective-permute-done.19.refs_1_, ...), custom_call_target="tpu_custom_call" | custom-call | flops 62999998464 | bytes 1 | tf_op jit(solution)/shard_map/up_outer/pallas_call | solution.py:282
  354.6 3.1 fusion.34
  367.8 6.4 %gate_outer.1 = (bf16[2048,256]{1,0:T(8,128)(2,1)S(1)}, bf16[2048,256]{1,0:T(8,128)(2,1)S(1)}, bf16[2048,256]{1,0:T(8,128)(2,1)S(1)}, bf16[2048,256]{1,0:T(8,128)(2,1)S(1)}) custom-call(s32[4]{0:T(128)S(1)} %pad_add_fusion.2.starts, bf16[256,1024]{1,0:T(8,128)(2,1)S(1)} %copy-done.20, bf16[256,1024]{1,0:T(8,128)(2,1)} %collective-permute-done.19.refs_1_, ...), custom_call_target="tpu_custom_call" | custom-call | flops 62999998464 | bytes 1 | tf_op jit(solution)/shard_map/gate_outer/pallas_call | solution.py:282
  381.3 5.9 feed.3
  389.6 3.4 collective-permute-done.47
  400.6 5.9 feed.2
  406.6 6.1 collective-permute-done.51
  425.4 4.4 all-to-all-start.3
  435.8 3.1 collective-permute-done.45
  441.0 6.0 collective-permute-done.52
  446.9 2.3 collective-permute-start.46
  449.3 4.0 multiply_reduce_fusion
  453.3 2.2 copy-done.29
  459.3 11.0 %attend_back.1 = (bf16[1024,256]{1,0:T(8,128)(2,1)}, bf16[1024,256]{1,0:T(8,128)(2,1)}, bf16[1024,256]{1,0:T(8,128)(2,1)}) custom-call(bf16[1024,256]{1,0:T(8,128)(2,1)} %copy-done.65, bf16[1024,256]{1,0:T(8,128)(2,1)} %copy-done.66, bf16[1024,256]{1,0:T(8,128)(2,1)} %copy-done.67, bf16[1024,256]{1,0:T(8,128)(2,1)} %get-tuple-element.111.refs_0_.o_ref.mixed_ref, ...), custom_call_target="tpu_custom_call" | custom-call | flops 109999996928 | bytes 1 | tf_op jit(solution)/shard_map/attend_back/pallas_call | solution.py:507
  470.3 4.3 all-to-all-start.5
  481.7 9.0 %heads_outer.1 = (bf16[2048,1024]{1,0:T(8,128)(2,1)}, f32[2048,1]{1,0:T(8,128)S(1)}) custom-call(s32[1]{0:T(128)} %bitcast.24.core_ref, bf16[1024,1024]{1,0:T(8,128)(2,1)S(1)} %constant_dynamic-update-slice_fusion.15.own_ref.x_own, bf16[1024,1024]{1,0:T(8,128)(2,1)} %collective-permute-done.3.other_ref.x_other, bf16[8,256,1024]{2,1,0:T(8,128)(2,1)} %bitcast.78, ...), custom_call_target="tpu_custom_call" | custom-call | flops 93999996928 | bytes 1 | tf_op jit(solution)/shard_map/heads_outer/pallas_call | solution.py:322
  491.6 7.7 %first_grad.1 = (bf16[1024,1024]{1,0:T(8,128)(2,1)}, bf16[1024,1024]{1,0:T(8,128)(2,1)}) custom-call(bf16[1024,256]{1,0:T(8,128)(2,1)} %get-tuple-element.178.dq_ref.refs_0_, bf16[1024,256]{1,0:T(8,128)(2,1)} %get-tuple-element.174.dk_ref.refs_1_, bf16[1024,256]{1,0:T(8,128)(2,1)} %get-tuple-element.175.dv_ref.refs_2_, ...), custom_call_target="tpu_custom_call" | custom-call | flops 60000002048 | bytes 1 | tf_op jit(solution)/shard_map/first_plane/first_grad/pallas_call | solution.py:125
  499.3 2.8 finish.4
  502.1 2.4 convert_add_fusion.4
  504.6 3.2 add_convert_fusion
  513.8 2.9 finish.6
  516.7 3.1 multiply_reduce_fusion.1
  519.8 5.4 all-to-all-start.4
  526.3 10.7 %collective-permute-done.58 = bf16[256,1024]{1,0:T(8,128)(2,1)} collective-permute-done((bf16[256,1024]{1,0:T(8,128)(2,1)}, bf16[256,1024]{1,0:T(8,128)(2,1)}, u32[]{:S(2)}, u32[]{:S(2)}) %collective-permute-start.58) | collective-permute-done | bytes 524320 | tf_op jit(solution)/shard_map/first_plane/ppermute | solution.py:570
  541.7 2.3 fusion.6
  551.4 4.5 collective-permute-done.63
  556.1 23.9 %all-to-all-done.4.part_ref = bf16[4,512,256]{2,1,0:T(8,128)(2,1)} async-done(((bf16[4,512,256]{2,1,0:T(8,128)(2,1)}), bf16[4,512,256]{2,1,0:T(8,128)(2,1)}, u32[]{:S(2)}, u32[]{:S(2)}) %all-to-all-start.4) | async-done | bytes 1048608 | tf_op jit(solution)/shard_map/gate_grad/all_to_all | solution.py:685
  580.0 2.8 finish.5
  584.3 3.0 collective-permute-done.67
  587.3 2.2 collective-permute-start.68
  591.4 3.7 collective-permute-start.71
  597.1 2.7 collective-permute-done.70
  601.0 2.8 finish.7
  (450 shorter events, 195.2 us)
Async XLA Ops:
  7.2 122.1 %all-gather.6.cloned.1.call-start = ((), (), s32[]{:S(2)}) async-start(), calls=%async_computation.7 | async-start | bytes 3932160 | tf_op jit(solution)/shard_map/qkv_row/all_gather | solution.py:702
  7.2 20.0 %collective-permute-start = (bf16[1024,256]{1,0:T(8,128)(2,1)}, bf16[1024,256]{1,0:T(8,128)(2,1)}, u32[]{:S(2)}, u32[]{:S(2)}) collective-permute-start(bf16[1024,256]{1,0:T(8,128)(2,1)} %param.13), channel_id=1, source_target_pairs={{0,2},{1,3},{2,0},{3,1},{4,6},{5,7},{6,4},{7,5},{8,10},{9,11},{10,... | collective-permute-start | bytes 1572872 | tf_op jit(solution)/shard_map/inputs/ppermute | solution.py:570
  10.2 24.9 %collective-permute-start.1 = (bf16[1024,256]{1,0:T(8,128)(2,1)}, bf16[1024,256]{1,0:T(8,128)(2,1)}, u32[]{:S(2)}, u32[]{:S(2)}) collective-permute-start(bf16[1024,256]{1,0:T(8,128)(2,1)} %param.13), channel_id=1, source_target_pairs={{0,4},{1,5},{2,6},{3,7},{4,0},{5,1},{6,2},{7,3},{8,12},{9,13},{10,... | collective-permute-start | bytes 1572872 | tf_op jit(solution)/shard_map/inputs/ppermute | solution.py:570
  11.7 24.5 %collective-permute-start.2 = (bf16[1024,256]{1,0:T(8,128)(2,1)}, bf16[1024,256]{1,0:T(8,128)(2,1)}, u32[]{:S(2)}, u32[]{:S(2)}) collective-permute-start(bf16[1024,256]{1,0:T(8,128)(2,1)} %param.13), channel_id=1, source_target_pairs={{0,6},{1,7},{2,4},{3,5},{4,2},{5,3},{6,0},{7,1},{8,14},{9,15},{10,... | collective-permute-start | bytes 1572872 | tf_op jit(solution)/shard_map/inputs/ppermute | solution.py:570
  18.8 58.3 %all-to-all-start = ((bf16[4,512,256]{2,1,0:T(8,128)(2,1)}), bf16[4,512,256]{2,1,0:T(8,128)(2,1)S(1)}, u32[]{:S(2)}, u32[]{:S(2)}) async-start(bf16[4,512,256]{2,1,0:T(8,128)(2,1)} %pad_maximum_fusion), calls=%async_computation | async-start | bytes 2097152 | tf_op jit(solution)/shard_map/gate_row/all_to_all | solution.py:651
  37.4 42.7 %collective-permute-start.3 = (bf16[1024,1024]{1,0:T(8,128)(2,1)S(1)}, bf16[1024,1024]{1,0:T(8,128)(2,1)}, u32[]{:S(2)}, u32[]{:S(2)}) collective-permute-start(bf16[1024,1024]{1,0:T(8,128)(2,1)S(1)} %constant_dynamic-update-slice_fusion.15.own_ref.x_own), channel_id=1, source_target_pairs={{0,1},{1,0},{2,3},{3,2},{4,5},{5,4},{6,7},{7,6},{8,9},{9,8},{10,11... | collective-permute-start | bytes 6291464 | tf_op jit(solution)/shard_map/inputs/ppermute | solution.py:567
  77.0 18.2 %collective-permute-start.8 = (bf16[2048,256]{1,0:T(8,128)(2,1)S(1)}, bf16[2048,256]{1,0:T(8,128)(2,1)}, u32[]{:S(2)}, u32[]{:S(2)}) collective-permute-start(bf16[2048,256]{1,0:T(8,128)(2,1)S(1)} %bitcast.71), channel_id=1, source_target_pairs={{0,4},{1,5},{2,6},{3,7},{4,0},{5,1},{6,2},{7,3},{8,12},{9,13},{10,... | collective-permute-start | bytes 3145736 | tf_op jit(solution)/shard_map/gate_plane/ppermute | solution.py:570
  78.6 22.2 %collective-permute-start.7 = (bf16[2048,256]{1,0:T(8,128)(2,1)S(1)}, bf16[2048,256]{1,0:T(8,128)(2,1)}, u32[]{:S(2)}, u32[]{:S(2)}) collective-permute-start(bf16[2048,256]{1,0:T(8,128)(2,1)S(1)} %bitcast.72), channel_id=1, source_target_pairs={{0,2},{1,3},{2,0},{3,1},{4,6},{5,7},{6,4},{7,5},{8,10},{9,11},{10,... | collective-permute-start | bytes 3145736 | tf_op jit(solution)/shard_map/gate_plane/ppermute | solution.py:570
  80.1 42.0 %all-to-all-start.1 = ((bf16[4,512,256]{2,1,0:T(8,128)(2,1)}), bf16[4,512,256]{2,1,0:T(8,128)(2,1)}, u32[]{:S(2)}, u32[]{:S(2)}) async-start(bf16[4,512,256]{2,1,0:T(8,128)(2,1)} %pad_maximum_fusion.1), calls=%async_computation.1 | async-start | bytes 2097152 | tf_op jit(solution)/shard_map/up_row/all_to_all | solution.py:651
  84.3 85.3 %all-gather.8.cloned.1.call-start = ((), (), s32[]{:S(2)}) async-start(), calls=%async_computation.8 | async-start | bytes 1310720 | tf_op jit(solution)/shard_map/out_row/all_gather | solution.py:718
  122.1 22.7 %collective-permute-start.9 = (bf16[2048,256]{1,0:T(8,128)(2,1)}, bf16[2048,256]{1,0:T(8,128)(2,1)}, u32[]{:S(2)}, u32[]{:S(2)}) collective-permute-start(bf16[2048,256]{1,0:T(8,128)(2,1)} %bitcast.14.refs_5_.refs_13_), channel_id=1, source_target_pairs={{0,2},{1,3},{2,0},{3,1},{4,6},{5,7},{6,4},{7,5},{8,10},{9,11},{10,... | collective-permute-start | bytes 3145736 | tf_op jit(solution)/shard_map/up_plane/ppermute | solution.py:570
  123.6 22.7 %collective-permute-start.10 = (bf16[2048,256]{1,0:T(8,128)(2,1)}, bf16[2048,256]{1,0:T(8,128)(2,1)}, u32[]{:S(2)}, u32[]{:S(2)}) collective-permute-start(bf16[2048,256]{1,0:T(8,128)(2,1)} %bitcast.14.refs_5_.refs_13_), channel_id=1, source_target_pairs={{0,4},{1,5},{2,6},{3,7},{4,0},{5,1},{6,2},{7,3},{8,12},{9,13},{10,... | collective-permute-start | bytes 3145736 | tf_op jit(solution)/shard_map/up_plane/ppermute | solution.py:570
  124.8 44.8 %all-to-all-start.2 = ((bf16[4,512,256]{2,1,0:T(8,128)(2,1)}), bf16[4,512,256]{2,1,0:T(8,128)(2,1)}, u32[]{:S(2)}, u32[]{:S(2)}) async-start(bf16[4,512,256]{2,1,0:T(8,128)(2,1)} %pad_maximum_fusion.2), calls=%async_computation.2 | async-start | bytes 2097152 | tf_op jit(solution)/shard_map/down_row/all_to_all | solution.py:651
  129.1 89.2 %all-gather.10.cloned.1.call-start = ((), (), s32[]{:S(2)}) async-start(), calls=%async_computation.9 | async-start | bytes 2621440 | tf_op jit(solution)/shard_map/grad_row/all_gather | solution.py:722
  174.8 278.5 %all-gather.12.cloned.1.call-start = ((), (), s32[]{:S(2)}) async-start(), calls=%async_computation.11 | async-start | bytes 4718592 | tf_op jit(solution)/shard_map/middle_grad/all_gather | solution.py:805
  176.1 14.8 %collective-permute-start.17 = (bf16[1024,256]{1,0:T(8,128)(2,1)S(1)}, bf16[1024,256]{1,0:T(8,128)(2,1)S(1)}, u32[]{:S(2)}, u32[]{:S(2)}) collective-permute-start(bf16[1024,256]{1,0:T(8,128)(2,1)S(1)} %slice.290), channel_id=1, source_target_pairs={{0,2},{1,3},{2,0},{3,1},{4,6},{5,7},{6,4},{7,5},{8,10},{9,11},{10,... | collective-permute-start | bytes 1572872 | tf_op jit(solution)/shard_map/up_plane/ppermute | solution.py:570
  177.5 26.1 %collective-permute-start.18 = (bf16[1024,256]{1,0:T(8,128)(2,1)S(1)}, bf16[1024,256]{1,0:T(8,128)(2,1)S(1)}, u32[]{:S(2)}, u32[]{:S(2)}) collective-permute-start(bf16[1024,256]{1,0:T(8,128)(2,1)S(1)} %slice.291), channel_id=1, source_target_pairs={{0,4},{1,5},{2,6},{3,7},{4,0},{5,1},{6,2},{7,3},{8,12},{9,13},{10,... | collective-permute-start | bytes 1572872 | tf_op jit(solution)/shard_map/up_plane/ppermute | solution.py:570
  182.1 22.5 %collective-permute-start.16 = (bf16[256,1024]{1,0:T(8,128)(2,1)S(1)}, bf16[256,1024]{1,0:T(8,128)(2,1)S(1)}, u32[]{:S(2)}, u32[]{:S(2)}) collective-permute-start(bf16[256,1024]{1,0:T(8,128)(2,1)S(1)} %get-tuple-element.206), channel_id=1, source_target_pairs={{0,6},{1,7},{2,4},{3,5},{4,2},{5,3},{6,0},{7,1},{8,14},{9,15},{10,... | collective-permute-start | bytes 1572872 | tf_op jit(solution)/shard_map/mix_plane/ppermute | solution.py:570
  183.7 30.4 %collective-permute-start.15 = (bf16[256,1024]{1,0:T(8,128)(2,1)S(1)}, bf16[256,1024]{1,0:T(8,128)(2,1)S(1)}, u32[]{:S(2)}, u32[]{:S(2)}) collective-permute-start(bf16[256,1024]{1,0:T(8,128)(2,1)S(1)} %get-tuple-element.207), channel_id=1, source_target_pairs={{0,4},{1,5},{2,6},{3,7},{4,0},{5,1},{6,2},{7,3},{8,12},{9,13},{10,... | collective-permute-start | bytes 1572872 | tf_op jit(solution)/shard_map/mix_plane/ppermute | solution.py:570
  183.9 30.2 %collective-permute-start.14 = (bf16[256,1024]{1,0:T(8,128)(2,1)S(1)}, bf16[256,1024]{1,0:T(8,128)(2,1)S(1)}, u32[]{:S(2)}, u32[]{:S(2)}) collective-permute-start(bf16[256,1024]{1,0:T(8,128)(2,1)S(1)} %get-tuple-element.205), channel_id=1, source_target_pairs={{0,2},{1,3},{2,0},{3,1},{4,6},{5,7},{6,4},{7,5},{8,10},{9,11},{10,... | collective-permute-start | bytes 1572872 | tf_op jit(solution)/shard_map/mix_plane/ppermute | solution.py:570
  218.3 25.3 %collective-permute-start.31 = (bf16[256,1024]{1,0:T(8,128)(2,1)}, bf16[256,1024]{1,0:T(8,128)(2,1)}, u32[]{:S(2)}, u32[]{:S(2)}) collective-permute-start(bf16[256,1024]{1,0:T(8,128)(2,1)} %convert_element_type.292.refs_0_), channel_id=1, source_target_pairs={{0,16},{8,24},{16,0},{24,8},{1,17},{9,25},{17,1},{25,9},{2,18},{10... | collective-permute-start | bytes 1572872 | tf_op jit(solution)/shard_map/middle_row/ppermute | solution.py:584
  219.3 24.9 %collective-permute-start.19 = (bf16[256,1024]{1,0:T(8,128)(2,1)}, bf16[256,1024]{1,0:T(8,128)(2,1)}, u32[]{:S(2)}, u32[]{:S(2)}) collective-permute-start(bf16[256,1024]{1,0:T(8,128)(2,1)} %convert_element_type.292.refs_0_), channel_id=1, source_target_pairs={{0,8},{8,0},{16,24},{24,16},{1,9},{9,1},{17,25},{25,17},{2,10},{10... | collective-permute-start | bytes 1572872 | tf_op jit(solution)/shard_map/middle_row/ppermute | solution.py:584
  220.0 25.1 %collective-permute-start.23 = (bf16[2048,256]{1,0:T(8,128)(2,1)}, bf16[2048,256]{1,0:T(8,128)(2,1)}, u32[]{:S(2)}, u32[]{:S(2)}) collective-permute-start(bf16[2048,256]{1,0:T(8,128)(2,1)} %bitcast.15.refs_5_.refs_1_), channel_id=1, source_target_pairs={{0,2},{1,3},{2,0},{3,1},{4,6},{5,7},{6,4},{7,5},{8,10},{9,11},{10,... | collective-permute-start | bytes 3145736 | tf_op jit(solution)/shard_map/down_plane/ppermute | solution.py:570
  221.4 24.6 %collective-permute-start.24 = (bf16[2048,256]{1,0:T(8,128)(2,1)}, bf16[2048,256]{1,0:T(8,128)(2,1)}, u32[]{:S(2)}, u32[]{:S(2)}) collective-permute-start(bf16[2048,256]{1,0:T(8,128)(2,1)} %bitcast.15.refs_5_.refs_1_), channel_id=1, source_target_pairs={{0,4},{1,5},{2,6},{3,7},{4,0},{5,1},{6,2},{7,3},{8,12},{9,13},{10,... | collective-permute-start | bytes 3145736 | tf_op jit(solution)/shard_map/down_plane/ppermute | solution.py:570
  224.0 25.3 %collective-permute-start.20 = (bf16[256,1024]{1,0:T(8,128)(2,1)}, bf16[256,1024]{1,0:T(8,128)(2,1)S(1)}, u32[]{:S(2)}, u32[]{:S(2)}) collective-permute-start(bf16[256,1024]{1,0:T(8,128)(2,1)} %convert_element_type.292.refs_0_), channel_id=1, source_target_pairs={{0,1},{1,0},{2,3},{3,2},{4,5},{5,4},{6,7},{7,6},{8,9},{9,8},{10,11... | collective-permute-start | bytes 1572872 | tf_op jit(solution)/shard_map/middle_row/ppermute | solution.py:567
  243.5 14.0 %collective-permute-start.32 = (bf16[256,1024]{1,0:T(8,128)(2,1)}, bf16[256,1024]{1,0:T(8,128)(2,1)S(1)}, u32[]{:S(2)}, u32[]{:S(2)}) collective-permute-start(bf16[256,1024]{1,0:T(8,128)(2,1)} %collective-permute-done.31.refs_0_.refs_2_), channel_id=1, source_target_pairs={{0,8},{8,0},{16,24},{24,16},{1,9},{9,1},{17,25},{25,17},{2,10},{10... | collective-permute-start | bytes 1572872 | tf_op jit(solution)/shard_map/middle_row/ppermute | solution.py:584
  244.2 13.3 %collective-permute-start.21 = (bf16[256,1024]{1,0:T(8,128)(2,1)}, bf16[256,1024]{1,0:T(8,128)(2,1)S(1)}, u32[]{:S(2)}, u32[]{:S(2)}) collective-permute-start(bf16[256,1024]{1,0:T(8,128)(2,1)} %collective-permute-done.19.refs_1_), channel_id=1, source_target_pairs={{0,1},{1,0},{2,3},{3,2},{4,5},{5,4},{6,7},{7,6},{8,9},{9,8},{10,11... | collective-permute-start | bytes 1572872 | tf_op jit(solution)/shard_map/middle_row/ppermute | solution.py:567
  245.1 23.7 %collective-permute-start.33 = (bf16[256,1024]{1,0:T(8,128)(2,1)}, bf16[256,1024]{1,0:T(8,128)(2,1)S(1)}, u32[]{:S(2)}, u32[]{:S(2)}) collective-permute-start(bf16[256,1024]{1,0:T(8,128)(2,1)} %collective-permute-done.31.refs_0_.refs_2_), channel_id=1, source_target_pairs={{0,1},{1,0},{2,3},{3,2},{4,5},{5,4},{6,7},{7,6},{8,9},{9,8},{10,11... | collective-permute-start | bytes 1572872 | tf_op jit(solution)/shard_map/middle_row/ppermute | solution.py:567
  247.1 21.6 %collective-permute-start.25 = (bf16[1024,256]{1,0:T(8,128)(2,1)S(1)}, bf16[1024,256]{1,0:T(8,128)(2,1)S(1)}, u32[]{:S(2)}, u32[]{:S(2)}) collective-permute-start(bf16[1024,256]{1,0:T(8,128)(2,1)S(1)} %slice.292), channel_id=1, source_target_pairs={{0,2},{1,3},{2,0},{3,1},{4,6},{5,7},{6,4},{7,5},{8,10},{9,11},{10,... | collective-permute-start | bytes 1572872 | tf_op jit(solution)/shard_map/down_plane/ppermute | solution.py:570
  249.3 19.5 %collective-permute-start.26 = (bf16[1024,256]{1,0:T(8,128)(2,1)S(1)}, bf16[1024,256]{1,0:T(8,128)(2,1)S(1)}, u32[]{:S(2)}, u32[]{:S(2)}) collective-permute-start(bf16[1024,256]{1,0:T(8,128)(2,1)S(1)} %slice.293), channel_id=1, source_target_pairs={{0,4},{1,5},{2,6},{3,7},{4,0},{5,1},{6,2},{7,3},{8,12},{9,13},{10,... | collective-permute-start | bytes 1572872 | tf_op jit(solution)/shard_map/down_plane/ppermute | solution.py:570
  257.5 11.8 %collective-permute-start.34 = (bf16[256,1024]{1,0:T(8,128)(2,1)S(1)}, bf16[256,1024]{1,0:T(8,128)(2,1)S(1)}, u32[]{:S(2)}, u32[]{:S(2)}) collective-permute-start(bf16[256,1024]{1,0:T(8,128)(2,1)S(1)} %collective-permute-done.32.refs_1_.refs_3_), channel_id=1, source_target_pairs={{0,1},{1,0},{2,3},{3,2},{4,5},{5,4},{6,7},{7,6},{8,9},{9,8},{10,11... | collective-permute-start | bytes 1572872 | tf_op jit(solution)/shard_map/middle_row/ppermute | solution.py:567
  291.5 13.3 %collective-permute-start.35 = (bf16[512,1024]{1,0:T(8,128)(2,1)S(1)}, bf16[512,1024]{1,0:T(8,128)(2,1)S(1)}, u32[]{:S(2)}, u32[]{:S(2)}) collective-permute-start(bf16[512,1024]{1,0:T(8,128)(2,1)S(1)} %get-tuple-element.134), channel_id=1, source_target_pairs={{0,1},{1,0},{2,3},{3,2},{4,5},{5,4},{6,7},{7,6},{8,9},{9,8},{10,11... | collective-permute-start | bytes 3145736 | tf_op jit(solution)/shard_map/unit_grad/ppermute | solution.py:567
  304.6 12.1 %collective-permute-start.27 = (bf16[512,1024]{1,0:T(8,128)(2,1)S(1)}, bf16[512,1024]{1,0:T(8,128)(2,1)}, u32[]{:S(2)}, u32[]{:S(2)}) collective-permute-start(bf16[512,1024]{1,0:T(8,128)(2,1)S(1)} %get-tuple-element.123), channel_id=1, source_target_pairs={{0,1},{1,0},{2,3},{3,2},{4,5},{5,4},{6,7},{7,6},{8,9},{9,8},{10,11... | collective-permute-start | bytes 3145736 | tf_op jit(solution)/shard_map/unit_grad/ppermute | solution.py:567
  307.8 14.8 %collective-permute-start.36 = (bf16[256,1024]{1,0:T(8,128)(2,1)S(1)}, bf16[256,1024]{1,0:T(8,128)(2,1)S(1)}, u32[]{:S(2)}, u32[]{:S(2)}) collective-permute-start(bf16[256,1024]{1,0:T(8,128)(2,1)S(1)} %slice.424), channel_id=1, source_target_pairs={{0,8},{8,0},{16,24},{24,16},{1,9},{9,1},{17,25},{25,17},{2,10},{10... | collective-permute-start | bytes 1572872 | tf_op jit(solution)/shard_map/unit_grad/ppermute | solution.py:584
  315.2 14.1 %collective-permute-start.41 = (bf16[1024,256]{1,0:T(8,128)(2,1)S(1)}, bf16[1024,256]{1,0:T(8,128)(2,1)S(1)}, u32[]{:S(2)}, u32[]{:S(2)}) collective-permute-start(bf16[1024,256]{1,0:T(8,128)(2,1)S(1)} %get-tuple-element.213), channel_id=1, source_target_pairs={{0,2},{1,3},{2,0},{3,1},{4,6},{5,7},{6,4},{7,5},{8,10},{9,11},{10,... | collective-permute-start | bytes 1572872 | tf_op jit(solution)/shard_map/down_grad/ppermute | solution.py:570
  318.4 22.8 %collective-permute-start.28 = (bf16[256,1024]{1,0:T(8,128)(2,1)S(1)}, bf16[256,1024]{1,0:T(8,128)(2,1)S(1)}, u32[]{:S(2)}, u32[]{:S(2)}) collective-permute-start(bf16[256,1024]{1,0:T(8,128)(2,1)S(1)} %slice.425), channel_id=1, source_target_pairs={{0,8},{8,0},{16,24},{24,16},{1,9},{9,1},{17,25},{25,17},{2,10},{10... | collective-permute-start | bytes 1572872 | tf_op jit(solution)/shard_map/unit_grad/ppermute | solution.py:584
  319.7 14.6 %collective-permute-start.39 = (bf16[1024,256]{1,0:T(8,128)(2,1)S(1)}, bf16[1024,256]{1,0:T(8,128)(2,1)S(1)}, u32[]{:S(2)}, u32[]{:S(2)}) collective-permute-start(bf16[1024,256]{1,0:T(8,128)(2,1)S(1)} %get-tuple-element.212), channel_id=1, source_target_pairs={{0,4},{1,5},{2,6},{3,7},{4,0},{5,1},{6,2},{7,3},{8,12},{9,13},{10,... | collective-permute-start | bytes 1572872 | tf_op jit(solution)/shard_map/down_grad/ppermute | solution.py:570
  322.7 24.8 %collective-permute-start.37 = (bf16[256,1024]{1,0:T(8,128)(2,1)S(1)}, bf16[256,1024]{1,0:T(8,128)(2,1)S(1)}, u32[]{:S(2)}, u32[]{:S(2)}) collective-permute-start(bf16[256,1024]{1,0:T(8,128)(2,1)S(1)} %fusion.7), channel_id=1, source_target_pairs={{0,16},{8,24},{16,0},{24,8},{1,17},{9,25},{17,1},{25,9},{2,18},{10... | collective-permute-start | bytes 1572872 | tf_op jit(solution)/shard_map/unit_grad/ppermute | solution.py:584
  329.5 28.1 %collective-permute-start.42 = (bf16[2048,256]{1,0:T(8,128)(2,1)S(1)}, bf16[2048,256]{1,0:T(8,128)(2,1)S(1)}, u32[]{:S(2)}, u32[]{:S(2)}) collective-permute-start(bf16[2048,256]{1,0:T(8,128)(2,1)S(1)} %pad_maximum_fusion.4), channel_id=1, source_target_pairs={{0,4},{1,5},{2,6},{3,7},{4,0},{5,1},{6,2},{7,3},{8,12},{9,13},{10,... | collective-permute-start | bytes 3145736 | tf_op jit(solution)/shard_map/down_grad/ppermute | solution.py:570
  334.5 23.2 %collective-permute-start.40 = (bf16[2048,256]{1,0:T(8,128)(2,1)S(1)}, bf16[2048,256]{1,0:T(8,128)(2,1)S(1)}, u32[]{:S(2)}, u32[]{:S(2)}) collective-permute-start(bf16[2048,256]{1,0:T(8,128)(2,1)S(1)} %pad_maximum_fusion.3), channel_id=1, source_target_pairs={{0,2},{1,3},{2,0},{3,1},{4,6},{5,7},{6,4},{7,5},{8,10},{9,11},{10,... | collective-permute-start | bytes 3145736 | tf_op jit(solution)/shard_map/down_grad/ppermute | solution.py:570
  378.3 14.6 %collective-permute-start.47 = (bf16[1024,256]{1,0:T(8,128)(2,1)}, bf16[1024,256]{1,0:T(8,128)(2,1)}, u32[]{:S(2)}, u32[]{:S(2)}) collective-permute-start(bf16[1024,256]{1,0:T(8,128)(2,1)} %get-tuple-element.211), channel_id=1, source_target_pairs={{0,4},{1,5},{2,6},{3,7},{4,0},{5,1},{6,2},{7,3},{8,12},{9,13},{10,... | collective-permute-start | bytes 1572872 | tf_op jit(solution)/shard_map/gate_grad/ppermute | solution.py:570
  379.8 15.4 %collective-permute-start.48 = (bf16[1024,256]{1,0:T(8,128)(2,1)}, bf16[1024,256]{1,0:T(8,128)(2,1)}, u32[]{:S(2)}, u32[]{:S(2)}) collective-permute-start(bf16[1024,256]{1,0:T(8,128)(2,1)} %get-tuple-element.210), channel_id=1, source_target_pairs={{0,2},{1,3},{2,0},{3,1},{4,6},{5,7},{6,4},{7,5},{8,10},{9,11},{10,... | collective-permute-start | bytes 1572872 | tf_op jit(solution)/shard_map/gate_grad/ppermute | solution.py:570
  387.2 30.4 %collective-permute-start.44 = (bf16[512,1024]{1,0:T(8,128)(2,1)}, bf16[512,1024]{1,0:T(8,128)(2,1)}, u32[]{:S(2)}, u32[]{:S(2)}) collective-permute-start(bf16[512,1024]{1,0:T(8,128)(2,1)} %get-tuple-element.145), channel_id=1, source_target_pairs={{0,1},{1,0},{2,3},{3,2},{4,5},{5,4},{6,7},{7,6},{8,9},{9,8},{10,11... | collective-permute-start | bytes 3145736 | tf_op jit(solution)/shard_map/feed/ppermute | solution.py:567
  397.7 15.1 %collective-permute-start.51 = (bf16[1024,256]{1,0:T(8,128)(2,1)S(1)}, bf16[1024,256]{1,0:T(8,128)(2,1)S(1)}, u32[]{:S(2)}, u32[]{:S(2)}) collective-permute-start(bf16[1024,256]{1,0:T(8,128)(2,1)S(1)} %get-tuple-element.209), channel_id=1, source_target_pairs={{0,2},{1,3},{2,0},{3,1},{4,6},{5,7},{6,4},{7,5},{8,10},{9,11},{10,... | collective-permute-start | bytes 1572872 | tf_op jit(solution)/shard_map/up_grad/ppermute | solution.py:570
  399.2 16.3 %collective-permute-start.49 = (bf16[1024,256]{1,0:T(8,128)(2,1)S(1)}, bf16[1024,256]{1,0:T(8,128)(2,1)S(1)}, u32[]{:S(2)}, u32[]{:S(2)}) collective-permute-start(bf16[1024,256]{1,0:T(8,128)(2,1)S(1)} %get-tuple-element.208), channel_id=1, source_target_pairs={{0,4},{1,5},{2,6},{3,7},{4,0},{5,1},{6,2},{7,3},{8,12},{9,13},{10,... | collective-permute-start | bytes 1572872 | tf_op jit(solution)/shard_map/up_grad/ppermute | solution.py:570
  406.5 24.0 %collective-permute-start.29 = (bf16[512,1024]{1,0:T(8,128)(2,1)}, bf16[512,1024]{1,0:T(8,128)(2,1)}, u32[]{:S(2)}, u32[]{:S(2)}) collective-permute-start(bf16[512,1024]{1,0:T(8,128)(2,1)} %get-tuple-element.126), channel_id=1, source_target_pairs={{0,1},{1,0},{2,3},{3,2},{4,5},{5,4},{6,7},{7,6},{8,9},{9,8},{10,11... | collective-permute-start | bytes 3145736 | tf_op jit(solution)/shard_map/feed/ppermute | solution.py:567
  414.0 32.9 %collective-permute-start.52 = (bf16[2048,256]{1,0:T(8,128)(2,1)}, bf16[2048,256]{1,0:T(8,128)(2,1)}, u32[]{:S(2)}, u32[]{:S(2)}) collective-permute-start(bf16[2048,256]{1,0:T(8,128)(2,1)} %pad_maximum_fusion.8), channel_id=1, source_target_pairs={{0,4},{1,5},{2,6},{3,7},{4,0},{5,1},{6,2},{7,3},{8,12},{9,13},{10,... | collective-permute-start | bytes 3145736 | tf_op jit(solution)/shard_map/up_grad/ppermute | solution.py:570
  416.6 32.6 %collective-permute-start.50 = (bf16[2048,256]{1,0:T(8,128)(2,1)}, bf16[2048,256]{1,0:T(8,128)(2,1)}, u32[]{:S(2)}, u32[]{:S(2)}) collective-permute-start(bf16[2048,256]{1,0:T(8,128)(2,1)} %pad_maximum_fusion.7), channel_id=1, source_target_pairs={{0,2},{1,3},{2,0},{3,1},{4,6},{5,7},{6,4},{7,5},{8,10},{9,11},{10,... | collective-permute-start | bytes 3145736 | tf_op jit(solution)/shard_map/up_grad/ppermute | solution.py:570
  421.1 17.8 %collective-permute-start.45 = (bf16[256,1024]{1,0:T(8,128)(2,1)}, bf16[256,1024]{1,0:T(8,128)(2,1)}, u32[]{:S(2)}, u32[]{:S(2)}) collective-permute-start(bf16[256,1024]{1,0:T(8,128)(2,1)} %slice.245), channel_id=1, source_target_pairs={{0,8},{8,0},{16,24},{24,16},{1,9},{9,1},{17,25},{25,17},{2,10},{10... | collective-permute-start | bytes 1572872 | tf_op jit(solution)/shard_map/feed/ppermute | solution.py:584
  425.4 44.9 %all-to-all-start.3 = ((bf16[4,512,256]{2,1,0:T(8,128)(2,1)}), bf16[4,512,256]{2,1,0:T(8,128)(2,1)}, u32[]{:S(2)}, u32[]{:S(2)}) async-start(bf16[4,512,256]{2,1,0:T(8,128)(2,1)} %bitcast.82), calls=%async_computation.3 | async-start | bytes 2097152 | tf_op jit(solution)/shard_map/down_grad/all_to_all | solution.py:685
  429.9 86.8 %collective-permute-start.65 = (bf16[2048,256]{1,0:T(8,128)(2,1)}, bf16[2048,256]{1,0:T(8,128)(2,1)}, u32[]{:S(2)}, u32[]{:S(2)}) collective-permute-start(bf16[2048,256]{1,0:T(8,128)(2,1)} %pad_maximum_fusion.6), channel_id=1, source_target_pairs={{0,4},{1,5},{2,6},{3,7},{4,0},{5,1},{6,2},{7,3},{8,12},{9,13},{10,... | collective-permute-start | bytes 3145736 | tf_op jit(solution)/shard_map/gate_grad/ppermute | solution.py:570
  430.5 86.2 %collective-permute-start.64 = (bf16[2048,256]{1,0:T(8,128)(2,1)}, bf16[2048,256]{1,0:T(8,128)(2,1)}, u32[]{:S(2)}, u32[]{:S(2)}) collective-permute-start(bf16[2048,256]{1,0:T(8,128)(2,1)} %pad_maximum_fusion.5), channel_id=1, source_target_pairs={{0,2},{1,3},{2,0},{3,1},{4,6},{5,7},{6,4},{7,5},{8,10},{9,11},{10,... | collective-permute-start | bytes 3145736 | tf_op jit(solution)/shard_map/gate_grad/ppermute | solution.py:570
  438.9 63.2 %collective-permute-start.43 = (bf16[256,1024]{1,0:T(8,128)(2,1)}, bf16[256,1024]{1,0:T(8,128)(2,1)}, u32[]{:S(2)}, u32[]{:S(2)}) collective-permute-start(bf16[256,1024]{1,0:T(8,128)(2,1)} %slice.243), channel_id=1, source_target_pairs={{0,8},{8,0},{16,24},{24,16},{1,9},{9,1},{17,25},{25,17},{2,10},{10... | collective-permute-start | bytes 1572872 | tf_op jit(solution)/shard_map/feed/ppermute | solution.py:584
  446.9 55.2 %collective-permute-start.46 = (bf16[256,1024]{1,0:T(8,128)(2,1)}, bf16[256,1024]{1,0:T(8,128)(2,1)}, u32[]{:S(2)}, u32[]{:S(2)}) collective-permute-start(bf16[256,1024]{1,0:T(8,128)(2,1)} %fusion.33), channel_id=1, source_target_pairs={{0,16},{8,24},{16,0},{24,8},{1,17},{9,25},{17,1},{25,9},{2,18},{10... | collective-permute-start | bytes 1572872 | tf_op jit(solution)/shard_map/feed/ppermute | solution.py:584
  470.3 43.5 %all-to-all-start.5 = ((bf16[4,512,256]{2,1,0:T(8,128)(2,1)}), bf16[4,512,256]{2,1,0:T(8,128)(2,1)}, u32[]{:S(2)}, u32[]{:S(2)}) async-start(bf16[4,512,256]{2,1,0:T(8,128)(2,1)} %bitcast.81), calls=%async_computation.6 | async-start | bytes 2097152 | tf_op jit(solution)/shard_map/up_grad/all_to_all | solution.py:685
  474.6 126.5 %reduce-scatter.2.cloned.1.call-start = ((), (), s32[]{:S(2)}) async-start(), calls=%async_computation.10 | async-start | bytes 5242880 | tf_op jit(solution)/shard_map/heads_grad/reduce_scatter | solution.py:838
  510.3 16.0 %collective-permute-start.59 = (bf16[256,1024]{1,0:T(8,128)(2,1)}, bf16[256,1024]{1,0:T(8,128)(2,1)}, u32[]{:S(2)}, u32[]{:S(2)}) collective-permute-start(bf16[256,1024]{1,0:T(8,128)(2,1)} %get-tuple-element.203), channel_id=1, source_target_pairs={{0,6},{1,7},{2,4},{3,5},{4,2},{5,3},{6,0},{7,1},{8,14},{9,15},{10,... | collective-permute-start | bytes 1572872 | tf_op jit(solution)/shard_map/first_plane/ppermute | solution.py:570
  511.7 25.3 %collective-permute-start.58 = (bf16[256,1024]{1,0:T(8,128)(2,1)}, bf16[256,1024]{1,0:T(8,128)(2,1)}, u32[]{:S(2)}, u32[]{:S(2)}) collective-permute-start(bf16[256,1024]{1,0:T(8,128)(2,1)} %get-tuple-element.204), channel_id=1, source_target_pairs={{0,4},{1,5},{2,6},{3,7},{4,0},{5,1},{6,2},{7,3},{8,12},{9,13},{10,... | collective-permute-start | bytes 1572872 | tf_op jit(solution)/shard_map/first_plane/ppermute | solution.py:570
  513.2 23.8 %collective-permute-start.57 = (bf16[256,1024]{1,0:T(8,128)(2,1)}, bf16[256,1024]{1,0:T(8,128)(2,1)}, u32[]{:S(2)}, u32[]{:S(2)}) collective-permute-start(bf16[256,1024]{1,0:T(8,128)(2,1)} %get-tuple-element.202), channel_id=1, source_target_pairs={{0,2},{1,3},{2,0},{3,1},{4,6},{5,7},{6,4},{7,5},{8,10},{9,11},{10,... | collective-permute-start | bytes 1572872 | tf_op jit(solution)/shard_map/first_plane/ppermute | solution.py:570
  519.8 60.2 %all-to-all-start.4 = ((bf16[4,512,256]{2,1,0:T(8,128)(2,1)}), bf16[4,512,256]{2,1,0:T(8,128)(2,1)}, u32[]{:S(2)}, u32[]{:S(2)}) async-start(bf16[4,512,256]{2,1,0:T(8,128)(2,1)} %bitcast.80), calls=%async_computation.5 | async-start | bytes 2097152 | tf_op jit(solution)/shard_map/gate_grad/all_to_all | solution.py:685
  546.4 37.9 %collective-permute-start.54 = (bf16[256,256]{1,0:T(8,128)(2,1)S(1)}, bf16[256,256]{1,0:T(8,128)(2,1)S(1)}, u32[]{:S(2)}, u32[]{:S(2)}) collective-permute-start(bf16[256,256]{1,0:T(8,128)(2,1)S(1)} %get-tuple-element.238), channel_id=1, source_target_pairs={{0,2},{1,3},{2,0},{3,1},{4,6},{5,7},{6,4},{7,5},{8,10},{9,11},{10,... | collective-permute-start | bytes 393224 | tf_op jit(solution)/shard_map/block_out/ppermute | solution.py:570
  547.1 42.5 %collective-permute-start.55 = (bf16[256,256]{1,0:T(8,128)(2,1)S(1)}, bf16[256,256]{1,0:T(8,128)(2,1)S(1)}, u32[]{:S(2)}, u32[]{:S(2)}) collective-permute-start(bf16[256,256]{1,0:T(8,128)(2,1)S(1)} %get-tuple-element.237), channel_id=1, source_target_pairs={{0,4},{1,5},{2,6},{3,7},{4,0},{5,1},{6,2},{7,3},{8,12},{9,13},{10,... | collective-permute-start | bytes 393224 | tf_op jit(solution)/shard_map/block_out/ppermute | solution.py:570
  556.0 26.8 %collective-permute-start.66 = (f32[2,4,2,256]{3,2,1,0:T(2,128)S(1)}, f32[2,4,2,256]{3,2,1,0:T(2,128)S(1)}, u32[]{:S(2)}, u32[]{:S(2)}) collective-permute-start(f32[2,4,2,256]{3,2,1,0:T(2,128)S(1)} %bitcast.84), channel_id=1, source_target_pairs={{0,1},{1,0},{2,3},{3,2},{4,5},{5,4},{6,7},{7,6},{8,9},{9,8},{10,11... | collective-permute-start | bytes 49160 | tf_op jit(solution)/shard_map/gains/ppermute | solution.py:636
  582.8 13.0 %collective-permute-start.56 = (bf16[256,256]{1,0:T(8,128)(2,1)S(1)}, bf16[256,256]{1,0:T(8,128)(2,1)S(1)}, u32[]{:S(2)}, u32[]{:S(2)}) collective-permute-start(bf16[256,256]{1,0:T(8,128)(2,1)S(1)} %get-tuple-element.236), channel_id=1, source_target_pairs={{0,6},{1,7},{2,4},{3,5},{4,2},{5,3},{6,0},{7,1},{8,14},{9,15},{10,... | collective-permute-start | bytes 393224 | tf_op jit(solution)/shard_map/block_out/ppermute | solution.py:570
  (116 other events, 960.3 us)
Sparse Core Ops, SparseCore 0:
  16.2 105.6 all-gather.5
  123.5 44.7 all-gather.7
  174.9 43.3 all-gather.9
  387.3 45.3 all-gather.11
  504.7 94.1 reduce-scatter.1

commit v14 on v13

--- a/solution.py
+++ b/solution.py
@@ -614,7 +614,7 @@
         return whole
 
     def put_feats(pieces):
-        whole = jnp.zeros((pieces[0].shape[0], half), pieces[0].dtype)
+        whole = jnp.concatenate([pieces[0]] * places, axis=1)
         for step, piece in enumerate(pieces):
             whole = lax.dynamic_update_slice_in_dim(whole, piece, (place ^ step) * feat, 1)
         return whole

time: 622 us -> 625 us (level)
  the two profiles are of different devices: /device:TPU:0 before, /device:TPU:9 now
where the time goes in v14:
time: 625 us; the launch traced here: 616 us
  waiting for transfers between devices  198 us (32%)
  Pallas kernels  130 us (21%)
  starting transfers between devices  126 us (20%)
  local copies, waits for them, and re-layouts  78.4 us (13%)
  other arithmetic  68.2 us (11%)
  between operations  15.3 us (2%)
    ppermute x42, waiting for transfers between devices, plane_swap(): return lax.ppermute(a, 'col', [(i, i ^ 2 * step) for i in range(cols)])  88.6 us
    unnamed x200, local copies, waits for them, and re-layouts  49.5 us
    ppermute x42, starting transfers between devices, plane_swap(): return lax.ppermute(a, 'col', [(i, i ^ 2 * step) for i in range(cols)])  40.3 us
    ppermute x12, waiting for transfers between devices, row_swap(): return lax.ppermute(a, 'row', [(i, i ^ step) for i in range(rows)])  35.9 us
    all_to_all x3, waiting for transfers between devices, exchange(): got = lax.all_to_all(pieces, 'row', split_axis=0, concat_axis=0, tiled=True)  31 us
    all_to_all x3, starting transfers between devices, exchange(): got = lax.all_to_all(pieces, 'row', split_axis=0, concat_axis=0, tiled=True)  29.9 us
    pallas_call x4, Pallas kernels, unfold(): pl.pallas_call(functools.partial(unfold_kernel, feat, len(lefts)), grid=(...  24.6 us
    pallas_call x2, Pallas kernels, units_back(): pl.pallas_call(functools.partial(units_back_kernel, feat, parts, count),...  20.6 us
  transfers between devices with their start and end apart: 83, of which 35 were waited for; matrix products, arithmetic and copies ran while one was open for 16% of the time, Pallas kernels for 17%

profile of v14, /device:TPU:9, one launch (start us, length us, event | category | flops | bytes accessed | tf_op | source)
XLA Modules:
  0.0 615.7 jit_solution(16531380782067973185)
XLA Ops:
  16.9 4.8 all-to-all-start
  21.7 2.3 pad_maximum_fusion
  29.2 3.4 collective-permute-done.2
  33.7 3.0 collective-permute-start.3
  59.9 15.5 %all-to-all-start.1 = ((bf16[4,512,256]{2,1,0:T(8,128)(2,1)}), bf16[4,512,256]{2,1,0:T(8,128)(2,1)}, u32[]{:S(2)}, u32[]{:S(2)}) async-start(bf16[4,512,256]{2,1,0:T(8,128)(2,1)} %pad_maximum_fusion.2), calls=%async_computation.1 | async-start | bytes 2097152 | tf_op jit(solution)/shard_map/up_row/all_to_all | solution.py:651
  79.7 11.9 %collective-permute-done.11 = bf16[1024,256]{1,0:T(8,128)(2,1)} collective-permute-done((bf16[1024,256]{1,0:T(8,128)(2,1)}, bf16[1024,256]{1,0:T(8,128)(2,1)}, u32[]{:S(2)}, u32[]{:S(2)}) %collective-permute-start.11) | collective-permute-done | bytes 524320 | tf_op jit(solution)/shard_map/gate_plane/ppermute | solution.py:570
  95.0 19.2 %all-to-all-done.1 = bf16[4,512,256]{2,1,0:T(8,128)(2,1)} async-done(((bf16[4,512,256]{2,1,0:T(8,128)(2,1)}), bf16[4,512,256]{2,1,0:T(8,128)(2,1)}, u32[]{:S(2)}, u32[]{:S(2)}) %all-to-all-start.1) | async-done | bytes 1048608 | tf_op jit(solution)/shard_map/up_row/all_to_all | solution.py:651
  115.8 9.6 %all-to-all-start.2 = ((bf16[4,512,256]{2,1,0:T(8,128)(2,1)}), bf16[4,512,256]{2,1,0:T(8,128)(2,1)}, u32[]{:S(2)}, u32[]{:S(2)}) async-start(bf16[4,512,256]{2,1,0:T(8,128)(2,1)} %pad_maximum_fusion.3), calls=%async_computation.2 | async-start | bytes 2097152 | tf_op jit(solution)/shard_map/down_row/all_to_all | solution.py:651
  130.8 5.6 project.1
  139.6 10.0 %attend.1 = (bf16[1024,256]{1,0:T(8,128)(2,1)}, f32[2,2,1024]{2,1,0:T(2,128)}) custom-call(bf16[1024,256]{1,0:T(8,128)(2,1)} %copy-done.65, bf16[1024,256]{1,0:T(8,128)(2,1)} %copy-done.66, bf16[1024,256]{1,0:T(8,128)(2,1)} %copy-done.67, s32[1,1024]{1,0:T(1,128)} %bitcast.100), custom_call_target="tpu_custom_call" | custom-call | flops 99999997952 | bytes 1 | tf_op jit(solution)/shard_map/attend/pallas_call | solution.py:437
  149.6 9.6 %all-to-all-done.2 = bf16[4,512,256]{2,1,0:T(8,128)(2,1)} async-done(((bf16[4,512,256]{2,1,0:T(8,128)(2,1)}), bf16[4,512,256]{2,1,0:T(8,128)(2,1)}, u32[]{:S(2)}, u32[]{:S(2)}) %all-to-all-start.2) | async-done | bytes 1048608 | tf_op jit(solution)/shard_map/down_row/all_to_all | solution.py:651
  159.2 5.0 all-gather.8.cloned.1.call-done.refs_1_.weight_ref
  164.2 5.1 mix.1
  175.2 2.6 add_convert_fusion.1
  180.6 5.5 collective-permute-done.17
  186.1 12.2 %collective-permute-done.18 = bf16[1024,256]{1,0:T(8,128)(2,1)S(1)} collective-permute-done((bf16[1024,256]{1,0:T(8,128)(2,1)S(1)}, bf16[1024,256]{1,0:T(8,128)(2,1)S(1)}, u32[]{:S(2)}, u32[]{:S(2)}) %collective-permute-start.18) | collective-permute-done | bytes 524320 | tf_op jit(solution)/shard_map/up_plane/ppermute | solution.py:570
  199.4 10.2 %collective-permute-done.15 = bf16[256,1024]{1,0:T(8,128)(2,1)S(1)} collective-permute-done((bf16[256,1024]{1,0:T(8,128)(2,1)S(1)}, bf16[256,1024]{1,0:T(8,128)(2,1)S(1)}, u32[]{:S(2)}, u32[]{:S(2)}) %collective-permute-start.15) | collective-permute-done | bytes 524320 | tf_op jit(solution)/shard_map/mix_plane/ppermute | solution.py:570
  212.0 2.9 all-gather.10.cloned.1.call-done.refs_0_
  223.1 16.4 %collective-permute-done.31.refs_0_.refs_2_ = bf16[256,1024]{1,0:T(8,128)(2,1)} collective-permute-done((bf16[256,1024]{1,0:T(8,128)(2,1)}, bf16[256,1024]{1,0:T(8,128)(2,1)}, u32[]{:S(2)}, u32[]{:S(2)}) %collective-permute-start.31) | collective-permute-done | bytes 524320 | tf_op jit(solution)/shard_map/middle_row/ppermute | solution.py:584
  239.5 2.9 collective-permute-start.32
  248.8 5.6 collective-permute-done.32.refs_1_.refs_3_
  256.7 8.3 %activate.2 = (bf16[512,1024]{1,0:T(8,128)(2,1)S(1)}, bf16[512,1024]{1,0:T(8,128)(2,1)S(1)}, bf16[512,1024]{1,0:T(8,128)(2,1)S(1)}, f32[512,1]{1,0:T(8,128)S(1)}) custom-call(bf16[256,1024]{1,0:T(8,128)(2,1)S(1)} %copy-done.18, bf16[256,1024]{1,0:T(8,128)(2,1)} %collective-permute-done.19.refs_1_, ...), custom_call_target="tpu_custom_call" | custom-call | flops 74999996416 | bytes 1 | tf_op jit(solution)/shard_map/activate/pallas_call | solution.py:173
  267.1 8.5 %activate.3 = (bf16[512,1024]{1,0:T(8,128)(2,1)S(1)}, bf16[512,1024]{1,0:T(8,128)(2,1)S(1)}, bf16[512,1024]{1,0:T(8,128)(2,1)S(1)}, f32[512,1]{1,0:T(8,128)S(1)}) custom-call(bf16[256,1024]{1,0:T(8,128)(2,1)} %collective-permute-done.31.refs_0_.refs_2_, bf16[256,1024]{1,0:T(8,128)(2,1)S(1)} %collective-permute-done.32.refs_1_.refs_3_, ...), custom_call_target="tpu_custom_call" | custom-call | flops 74999996416 | bytes 1 | tf_op jit(solution)/shard_map/activate/pallas_call | solution.py:173
  278.0 10.3 %units_back.3 = (bf16[512,1024]{1,0:T(8,128)(2,1)S(1)}, bf16[512,1024]{1,0:T(8,128)(2,1)S(1)}, bf16[512,1024]{1,0:T(8,128)(2,1)S(1)}, bf16[512,1024]{1,0:T(8,128)(2,1)S(1)}) custom-call(s32[2]{0:T(128)S(1)} %pad_add_fusion.1.starts, bf16[1024,1024]{1,0:T(8,128)(2,1)} %all-gather.10.cloned.1.call-done.refs_0_, bf16[1024,1024]{1,0:T(8,128)(2,1)} %copy-done.34, ...), custom_call_target="tpu_custom_call" | custom-call | flops 92999999488 | bytes 1 | tf_op jit(solution)/shard_map/unit_grad/units_back/pallas_call | solution.py:239
  291.9 10.3 %units_back.2 = (bf16[512,1024]{1,0:T(8,128)(2,1)S(1)}, bf16[512,1024]{1,0:T(8,128)(2,1)S(1)}, bf16[512,1024]{1,0:T(8,128)(2,1)S(1)}, bf16[512,1024]{1,0:T(8,128)(2,1)S(1)}) custom-call(s32[2]{0:T(128)S(1)} %pad_add_fusion.starts, bf16[1024,1024]{1,0:T(8,128)(2,1)} %all-gather.10.cloned.1.call-done.refs_0_, bf16[1024,1024]{1,0:T(8,128)(2,1)} %copy-done.34, ...), custom_call_target="tpu_custom_call" | custom-call | flops 92999999488 | bytes 1 | tf_op jit(solution)/shard_map/unit_grad/units_back/pallas_call | solution.py:239
  307.0 6.4 %down_outer.1 = (bf16[2048,256]{1,0:T(8,128)(2,1)S(1)}, bf16[2048,256]{1,0:T(8,128)(2,1)S(1)}, bf16[2048,256]{1,0:T(8,128)(2,1)S(1)}, bf16[2048,256]{1,0:T(8,128)(2,1)S(1)}) custom-call(s32[4]{0:T(128)S(1)} %pad_add_fusion.2.starts, bf16[1024,1024]{1,0:T(8,128)(2,1)S(1)} %copy-done.33, bf16[1024,1024]{1,0:T(8,128)(2,1)S(1)} %copy-done.35, ...), custom_call_target="tpu_custom_call" | custom-call | flops 62999998464 | bytes 1 | tf_op jit(solution)/shard_map/down_grad/down_outer/pallas_call | solution.py:282
  320.7 5.8 collective-permute-done.41
  330.6 6.7 %collective-permute-done.28 = bf16[256,1024]{1,0:T(8,128)(2,1)S(1)} collective-permute-done((bf16[256,1024]{1,0:T(8,128)(2,1)S(1)}, bf16[256,1024]{1,0:T(8,128)(2,1)S(1)}, u32[]{:S(2)}, u32[]{:S(2)}) %collective-permute-start.28) | collective-permute-done | bytes 524320 | tf_op jit(solution)/shard_map/unit_grad/ppermute | solution.py:584
  337.4 4.0 collective-permute-done.37
  341.7 2.9 collective-permute-start.38
  344.6 6.5 %up_outer.1 = (bf16[2048,256]{1,0:T(8,128)(2,1)S(1)}, bf16[2048,256]{1,0:T(8,128)(2,1)S(1)}, bf16[2048,256]{1,0:T(8,128)(2,1)S(1)}, bf16[2048,256]{1,0:T(8,128)(2,1)S(1)}) custom-call(s32[4]{0:T(128)S(1)} %pad_add_fusion.2.starts, bf16[256,1024]{1,0:T(8,128)(2,1)S(1)} %copy-done.19, bf16[256,1024]{1,0:T(8,128)(2,1)} %collective-permute-done.19.refs_1_, ...), custom_call_target="tpu_custom_call" | custom-call | flops 62999998464 | bytes 1 | tf_op jit(solution)/shard_map/up_outer/pallas_call | solution.py:282
  351.1 3.1 fusion.34
  364.4 6.4 %gate_outer.1 = (bf16[2048,256]{1,0:T(8,128)(2,1)S(1)}, bf16[2048,256]{1,0:T(8,128)(2,1)S(1)}, bf16[2048,256]{1,0:T(8,128)(2,1)S(1)}, bf16[2048,256]{1,0:T(8,128)(2,1)S(1)}) custom-call(s32[4]{0:T(128)S(1)} %pad_add_fusion.2.starts, bf16[256,1024]{1,0:T(8,128)(2,1)S(1)} %copy-done.20, bf16[256,1024]{1,0:T(8,128)(2,1)} %collective-permute-done.19.refs_1_, ...), custom_call_target="tpu_custom_call" | custom-call | flops 62999998464 | bytes 1 | tf_op jit(solution)/shard_map/gate_outer/pallas_call | solution.py:282
  377.2 5.9 feed.3
  395.7 5.9 feed.2
  401.5 2.3 collective-permute-start.29
  403.9 6.6 %collective-permute-done.51 = bf16[1024,256]{1,0:T(8,128)(2,1)S(1)} collective-permute-done((bf16[1024,256]{1,0:T(8,128)(2,1)S(1)}, bf16[1024,256]{1,0:T(8,128)(2,1)S(1)}, u32[]{:S(2)}, u32[]{:S(2)}) %collective-permute-start.51) | collective-permute-done | bytes 524320 | tf_op jit(solution)/shard_map/up_grad/ppermute | solution.py:570
  422.1 5.1 all-to-all-start.3
  434.5 9.3 %collective-permute-done.52 = bf16[2048,256]{1,0:T(8,128)(2,1)} collective-permute-done((bf16[2048,256]{1,0:T(8,128)(2,1)}, bf16[2048,256]{1,0:T(8,128)(2,1)}, u32[]{:S(2)}, u32[]{:S(2)}) %collective-permute-start.52) | collective-permute-done | bytes 1048608 | tf_op jit(solution)/shard_map/up_grad/ppermute | solution.py:570
  443.8 2.6 collective-permute-start.46
  446.3 4.0 multiply_reduce_fusion
  456.4 11.0 %attend_back.1 = (bf16[1024,256]{1,0:T(8,128)(2,1)}, bf16[1024,256]{1,0:T(8,128)(2,1)}, bf16[1024,256]{1,0:T(8,128)(2,1)}) custom-call(bf16[1024,256]{1,0:T(8,128)(2,1)} %copy-done.65, bf16[1024,256]{1,0:T(8,128)(2,1)} %copy-done.66, bf16[1024,256]{1,0:T(8,128)(2,1)} %copy-done.67, bf16[1024,256]{1,0:T(8,128)(2,1)} %get-tuple-element.111.refs_0_.o_ref.mixed_ref, ...), custom_call_target="tpu_custom_call" | custom-call | flops 109999996928 | bytes 1 | tf_op jit(solution)/shard_map/attend_back/pallas_call | solution.py:507
  467.4 4.3 all-to-all-start.5
  478.8 9.0 %heads_outer.1 = (bf16[2048,1024]{1,0:T(8,128)(2,1)}, f32[2048,1]{1,0:T(8,128)S(1)}) custom-call(s32[1]{0:T(128)} %bitcast.24.core_ref, bf16[1024,1024]{1,0:T(8,128)(2,1)S(1)} %constant_dynamic-update-slice_fusion.16.own_ref.x_own, bf16[1024,1024]{1,0:T(8,128)(2,1)} %collective-permute-done.3.other_ref.x_other, bf16[8,256,1024]{2,1,0:T(8,128)(2,1)} %bitcast.78, ...), custom_call_target="tpu_custom_call" | custom-call | flops 93999996928 | bytes 1 | tf_op jit(solution)/shard_map/heads_outer/pallas_call | solution.py:322
  488.7 7.7 %first_grad.1 = (bf16[1024,1024]{1,0:T(8,128)(2,1)}, bf16[1024,1024]{1,0:T(8,128)(2,1)}) custom-call(bf16[1024,256]{1,0:T(8,128)(2,1)} %get-tuple-element.178.dq_ref.refs_0_, bf16[1024,256]{1,0:T(8,128)(2,1)} %get-tuple-element.174.dk_ref.refs_1_, bf16[1024,256]{1,0:T(8,128)(2,1)} %get-tuple-element.175.dv_ref.refs_2_, ...), custom_call_target="tpu_custom_call" | custom-call | flops 60000002048 | bytes 1 | tf_op jit(solution)/shard_map/first_plane/first_grad/pallas_call | solution.py:125
  496.4 2.7 collective-permute-start.53
  499.1 2.7 finish.4
  501.8 2.4 convert_add_fusion.4
  504.2 3.2 add_convert_fusion
  509.9 3.8 collective-permute-start.59
  514.1 2.9 finish.6
  516.9 3.1 multiply_reduce_fusion.1
  520.1 4.9 all-to-all-start.4
  526.3 11.4 %collective-permute-done.58 = bf16[256,1024]{1,0:T(8,128)(2,1)} collective-permute-done((bf16[256,1024]{1,0:T(8,128)(2,1)}, bf16[256,1024]{1,0:T(8,128)(2,1)}, u32[]{:S(2)}, u32[]{:S(2)}) %collective-permute-start.58) | collective-permute-done | bytes 524320 | tf_op jit(solution)/shard_map/first_plane/ppermute | solution.py:570
  542.8 2.3 fusion.6
  551.8 3.9 collective-permute-done.63
  557.4 18.5 %all-to-all-done.4.part_ref = bf16[4,512,256]{2,1,0:T(8,128)(2,1)} async-done(((bf16[4,512,256]{2,1,0:T(8,128)(2,1)}), bf16[4,512,256]{2,1,0:T(8,128)(2,1)}, u32[]{:S(2)}, u32[]{:S(2)}) %all-to-all-start.4) | async-done | bytes 1048608 | tf_op jit(solution)/shard_map/gate_grad/all_to_all | solution.py:685
  575.9 2.8 finish.5
  580.6 2.9 collective-permute-done.67
  584.3 2.3 collective-permute-done.68
  586.7 2.4 collective-permute-start.71
  589.1 4.1 collective-permute-start.70
  597.5 8.6 %reduce-scatter.2.cloned.1.call-done = bf16[512,1024]{1,0:T(8,128)(2,1)} async-done(((bf16[2048,1024]{1,0:T(8,128)(2,1)}), bf16[512,1024]{1,0:T(8,128)(2,1)}) %reduce-scatter.2.cloned.1.call-update) | async-done | bytes 1048592 | tf_op jit(solution)/shard_map/heads_grad/reduce_scatter | solution.py:838
  606.1 2.8 finish.7
  (451 shorter events, 196.9 us)
Async XLA Ops:
  7.2 118.4 %all-gather.6.cloned.1.call-start = ((), (), s32[]{:S(2)}) async-start(), calls=%async_computation.7 | async-start | bytes 3932160 | tf_op jit(solution)/shard_map/qkv_row/all_gather | solution.py:702
  7.2 19.7 %collective-permute-start = (bf16[1024,256]{1,0:T(8,128)(2,1)}, bf16[1024,256]{1,0:T(8,128)(2,1)}, u32[]{:S(2)}, u32[]{:S(2)}) collective-permute-start(bf16[1024,256]{1,0:T(8,128)(2,1)} %param.13), channel_id=1, source_target_pairs={{0,2},{1,3},{2,0},{3,1},{4,6},{5,7},{6,4},{7,5},{8,10},{9,11},{10,... | collective-permute-start | bytes 1572872 | tf_op jit(solution)/shard_map/inputs/ppermute | solution.py:570
  8.5 19.6 %collective-permute-start.1 = (bf16[1024,256]{1,0:T(8,128)(2,1)}, bf16[1024,256]{1,0:T(8,128)(2,1)}, u32[]{:S(2)}, u32[]{:S(2)}) collective-permute-start(bf16[1024,256]{1,0:T(8,128)(2,1)} %param.13), channel_id=1, source_target_pairs={{0,4},{1,5},{2,6},{3,7},{4,0},{5,1},{6,2},{7,3},{8,12},{9,13},{10,... | collective-permute-start | bytes 1572872 | tf_op jit(solution)/shard_map/inputs/ppermute | solution.py:570
  9.7 22.9 %collective-permute-start.2 = (bf16[1024,256]{1,0:T(8,128)(2,1)}, bf16[1024,256]{1,0:T(8,128)(2,1)}, u32[]{:S(2)}, u32[]{:S(2)}) collective-permute-start(bf16[1024,256]{1,0:T(8,128)(2,1)} %param.13), channel_id=1, source_target_pairs={{0,6},{1,7},{2,4},{3,5},{4,2},{5,3},{6,0},{7,1},{8,14},{9,15},{10,... | collective-permute-start | bytes 1572872 | tf_op jit(solution)/shard_map/inputs/ppermute | solution.py:570
  16.9 41.5 %all-to-all-start = ((bf16[4,512,256]{2,1,0:T(8,128)(2,1)}), bf16[4,512,256]{2,1,0:T(8,128)(2,1)S(1)}, u32[]{:S(2)}, u32[]{:S(2)}) async-start(bf16[4,512,256]{2,1,0:T(8,128)(2,1)} %pad_maximum_fusion.1), calls=%async_computation | async-start | bytes 2097152 | tf_op jit(solution)/shard_map/gate_row/all_to_all | solution.py:651
  33.7 26.2 %collective-permute-start.3 = (bf16[1024,1024]{1,0:T(8,128)(2,1)S(1)}, bf16[1024,1024]{1,0:T(8,128)(2,1)}, u32[]{:S(2)}, u32[]{:S(2)}) collective-permute-start(bf16[1024,1024]{1,0:T(8,128)(2,1)S(1)} %constant_dynamic-update-slice_fusion.16.own_ref.x_own), channel_id=1, source_target_pairs={{0,1},{1,0},{2,3},{3,2},{4,5},{5,4},{6,7},{7,6},{8,9},{9,8},{10,11... | collective-permute-start | bytes 6291464 | tf_op jit(solution)/shard_map/inputs/ppermute | solution.py:567
  58.4 17.0 %collective-permute-start.8 = (bf16[2048,256]{1,0:T(8,128)(2,1)S(1)}, bf16[2048,256]{1,0:T(8,128)(2,1)}, u32[]{:S(2)}, u32[]{:S(2)}) collective-permute-start(bf16[2048,256]{1,0:T(8,128)(2,1)S(1)} %bitcast.71), channel_id=1, source_target_pairs={{0,4},{1,5},{2,6},{3,7},{4,0},{5,1},{6,2},{7,3},{8,12},{9,13},{10,... | collective-permute-start | bytes 3145736 | tf_op jit(solution)/shard_map/gate_plane/ppermute | solution.py:570
  58.7 18.9 %collective-permute-start.7 = (bf16[2048,256]{1,0:T(8,128)(2,1)S(1)}, bf16[2048,256]{1,0:T(8,128)(2,1)}, u32[]{:S(2)}, u32[]{:S(2)}) collective-permute-start(bf16[2048,256]{1,0:T(8,128)(2,1)S(1)} %bitcast.72), channel_id=1, source_target_pairs={{0,2},{1,3},{2,0},{3,1},{4,6},{5,7},{6,4},{7,5},{8,10},{9,11},{10,... | collective-permute-start | bytes 3145736 | tf_op jit(solution)/shard_map/gate_plane/ppermute | solution.py:570
  59.9 54.3 %all-to-all-start.1 = ((bf16[4,512,256]{2,1,0:T(8,128)(2,1)}), bf16[4,512,256]{2,1,0:T(8,128)(2,1)}, u32[]{:S(2)}, u32[]{:S(2)}) async-start(bf16[4,512,256]{2,1,0:T(8,128)(2,1)} %pad_maximum_fusion.2), calls=%async_computation.1 | async-start | bytes 2097152 | tf_op jit(solution)/shard_map/up_row/all_to_all | solution.py:651
  75.4 88.7 %all-gather.8.cloned.1.call-start = ((), (), s32[]{:S(2)}) async-start(), calls=%async_computation.8 | async-start | bytes 1310720 | tf_op jit(solution)/shard_map/out_row/all_gather | solution.py:718
  77.3 14.3 %collective-permute-start.11 = (bf16[1024,256]{1,0:T(8,128)(2,1)}, bf16[1024,256]{1,0:T(8,128)(2,1)}, u32[]{:S(2)}, u32[]{:S(2)}) collective-permute-start(bf16[1024,256]{1,0:T(8,128)(2,1)} %slice.288), channel_id=1, source_target_pairs={{0,2},{1,3},{2,0},{3,1},{4,6},{5,7},{6,4},{7,5},{8,10},{9,11},{10,... | collective-permute-start | bytes 1572872 | tf_op jit(solution)/shard_map/gate_plane/ppermute | solution.py:570
  79.4 13.5 %collective-permute-start.12 = (bf16[1024,256]{1,0:T(8,128)(2,1)}, bf16[1024,256]{1,0:T(8,128)(2,1)}, u32[]{:S(2)}, u32[]{:S(2)}) collective-permute-start(bf16[1024,256]{1,0:T(8,128)(2,1)} %slice.289), channel_id=1, source_target_pairs={{0,4},{1,5},{2,6},{3,7},{4,0},{5,1},{6,2},{7,3},{8,12},{9,13},{10,... | collective-permute-start | bytes 1572872 | tf_op jit(solution)/shard_map/gate_plane/ppermute | solution.py:570
  114.2 25.3 %collective-permute-start.9 = (bf16[2048,256]{1,0:T(8,128)(2,1)}, bf16[2048,256]{1,0:T(8,128)(2,1)}, u32[]{:S(2)}, u32[]{:S(2)}) collective-permute-start(bf16[2048,256]{1,0:T(8,128)(2,1)} %bitcast.14.refs_5_.refs_13_), channel_id=1, source_target_pairs={{0,2},{1,3},{2,0},{3,1},{4,6},{5,7},{6,4},{7,5},{8,10},{9,11},{10,... | collective-permute-start | bytes 3145736 | tf_op jit(solution)/shard_map/up_plane/ppermute | solution.py:570
  114.3 25.2 %collective-permute-start.10 = (bf16[2048,256]{1,0:T(8,128)(2,1)}, bf16[2048,256]{1,0:T(8,128)(2,1)}, u32[]{:S(2)}, u32[]{:S(2)}) collective-permute-start(bf16[2048,256]{1,0:T(8,128)(2,1)} %bitcast.14.refs_5_.refs_13_), channel_id=1, source_target_pairs={{0,4},{1,5},{2,6},{3,7},{4,0},{5,1},{6,2},{7,3},{8,12},{9,13},{10,... | collective-permute-start | bytes 3145736 | tf_op jit(solution)/shard_map/up_plane/ppermute | solution.py:570
  115.8 43.4 %all-to-all-start.2 = ((bf16[4,512,256]{2,1,0:T(8,128)(2,1)}), bf16[4,512,256]{2,1,0:T(8,128)(2,1)}, u32[]{:S(2)}, u32[]{:S(2)}) async-start(bf16[4,512,256]{2,1,0:T(8,128)(2,1)} %pad_maximum_fusion.3), calls=%async_computation.2 | async-start | bytes 2097152 | tf_op jit(solution)/shard_map/down_row/all_to_all | solution.py:651
  125.4 89.5 %all-gather.10.cloned.1.call-start = ((), (), s32[]{:S(2)}) async-start(), calls=%async_computation.9 | async-start | bytes 2621440 | tf_op jit(solution)/shard_map/grad_row/all_gather | solution.py:722
  171.1 279.3 %all-gather.12.cloned.1.call-start = ((), (), s32[]{:S(2)}) async-start(), calls=%async_computation.11 | async-start | bytes 4718592 | tf_op jit(solution)/shard_map/middle_grad/all_gather | solution.py:805
  172.4 13.7 %collective-permute-start.17 = (bf16[1024,256]{1,0:T(8,128)(2,1)S(1)}, bf16[1024,256]{1,0:T(8,128)(2,1)S(1)}, u32[]{:S(2)}, u32[]{:S(2)}) collective-permute-start(bf16[1024,256]{1,0:T(8,128)(2,1)S(1)} %slice.290), channel_id=1, source_target_pairs={{0,2},{1,3},{2,0},{3,1},{4,6},{5,7},{6,4},{7,5},{8,10},{9,11},{10,... | collective-permute-start | bytes 1572872 | tf_op jit(solution)/shard_map/up_plane/ppermute | solution.py:570
  173.8 24.5 %collective-permute-start.18 = (bf16[1024,256]{1,0:T(8,128)(2,1)S(1)}, bf16[1024,256]{1,0:T(8,128)(2,1)S(1)}, u32[]{:S(2)}, u32[]{:S(2)}) collective-permute-start(bf16[1024,256]{1,0:T(8,128)(2,1)S(1)} %slice.291), channel_id=1, source_target_pairs={{0,4},{1,5},{2,6},{3,7},{4,0},{5,1},{6,2},{7,3},{8,12},{9,13},{10,... | collective-permute-start | bytes 1572872 | tf_op jit(solution)/shard_map/up_plane/ppermute | solution.py:570
  177.9 21.5 %collective-permute-start.16 = (bf16[256,1024]{1,0:T(8,128)(2,1)S(1)}, bf16[256,1024]{1,0:T(8,128)(2,1)S(1)}, u32[]{:S(2)}, u32[]{:S(2)}) collective-permute-start(bf16[256,1024]{1,0:T(8,128)(2,1)S(1)} %get-tuple-element.206), channel_id=1, source_target_pairs={{0,6},{1,7},{2,4},{3,5},{4,2},{5,3},{6,0},{7,1},{8,14},{9,15},{10,... | collective-permute-start | bytes 1572872 | tf_op jit(solution)/shard_map/mix_plane/ppermute | solution.py:570
  179.0 30.6 %collective-permute-start.15 = (bf16[256,1024]{1,0:T(8,128)(2,1)S(1)}, bf16[256,1024]{1,0:T(8,128)(2,1)S(1)}, u32[]{:S(2)}, u32[]{:S(2)}) collective-permute-start(bf16[256,1024]{1,0:T(8,128)(2,1)S(1)} %get-tuple-element.207), channel_id=1, source_target_pairs={{0,4},{1,5},{2,6},{3,7},{4,0},{5,1},{6,2},{7,3},{8,12},{9,13},{10,... | collective-permute-start | bytes 1572872 | tf_op jit(solution)/shard_map/mix_plane/ppermute | solution.py:570
  179.4 30.1 %collective-permute-start.14 = (bf16[256,1024]{1,0:T(8,128)(2,1)S(1)}, bf16[256,1024]{1,0:T(8,128)(2,1)S(1)}, u32[]{:S(2)}, u32[]{:S(2)}) collective-permute-start(bf16[256,1024]{1,0:T(8,128)(2,1)S(1)} %get-tuple-element.205), channel_id=1, source_target_pairs={{0,2},{1,3},{2,0},{3,1},{4,6},{5,7},{6,4},{7,5},{8,10},{9,11},{10,... | collective-permute-start | bytes 1572872 | tf_op jit(solution)/shard_map/mix_plane/ppermute | solution.py:570
  214.9 24.6 %collective-permute-start.31 = (bf16[256,1024]{1,0:T(8,128)(2,1)}, bf16[256,1024]{1,0:T(8,128)(2,1)}, u32[]{:S(2)}, u32[]{:S(2)}) collective-permute-start(bf16[256,1024]{1,0:T(8,128)(2,1)} %convert_element_type.292.refs_0_), channel_id=1, source_target_pairs={{0,16},{8,24},{16,0},{24,8},{1,17},{9,25},{17,1},{25,9},{2,18},{10... | collective-permute-start | bytes 1572872 | tf_op jit(solution)/shard_map/middle_row/ppermute | solution.py:584
  216.9 25.5 %collective-permute-start.19 = (bf16[256,1024]{1,0:T(8,128)(2,1)}, bf16[256,1024]{1,0:T(8,128)(2,1)}, u32[]{:S(2)}, u32[]{:S(2)}) collective-permute-start(bf16[256,1024]{1,0:T(8,128)(2,1)} %convert_element_type.292.refs_0_), channel_id=1, source_target_pairs={{0,8},{8,0},{16,24},{24,16},{1,9},{9,1},{17,25},{25,17},{2,10},{10... | collective-permute-start | bytes 1572872 | tf_op jit(solution)/shard_map/middle_row/ppermute | solution.py:584
  217.8 26.3 %collective-permute-start.23 = (bf16[2048,256]{1,0:T(8,128)(2,1)}, bf16[2048,256]{1,0:T(8,128)(2,1)}, u32[]{:S(2)}, u32[]{:S(2)}) collective-permute-start(bf16[2048,256]{1,0:T(8,128)(2,1)} %bitcast.15.refs_5_.refs_1_), channel_id=1, source_target_pairs={{0,2},{1,3},{2,0},{3,1},{4,6},{5,7},{6,4},{7,5},{8,10},{9,11},{10,... | collective-permute-start | bytes 3145736 | tf_op jit(solution)/shard_map/down_plane/ppermute | solution.py:570
  219.0 25.1 %collective-permute-start.24 = (bf16[2048,256]{1,0:T(8,128)(2,1)}, bf16[2048,256]{1,0:T(8,128)(2,1)}, u32[]{:S(2)}, u32[]{:S(2)}) collective-permute-start(bf16[2048,256]{1,0:T(8,128)(2,1)} %bitcast.15.refs_5_.refs_1_), channel_id=1, source_target_pairs={{0,4},{1,5},{2,6},{3,7},{4,0},{5,1},{6,2},{7,3},{8,12},{9,13},{10,... | collective-permute-start | bytes 3145736 | tf_op jit(solution)/shard_map/down_plane/ppermute | solution.py:570
  222.8 24.7 %collective-permute-start.20 = (bf16[256,1024]{1,0:T(8,128)(2,1)}, bf16[256,1024]{1,0:T(8,128)(2,1)S(1)}, u32[]{:S(2)}, u32[]{:S(2)}) collective-permute-start(bf16[256,1024]{1,0:T(8,128)(2,1)} %convert_element_type.292.refs_0_), channel_id=1, source_target_pairs={{0,1},{1,0},{2,3},{3,2},{4,5},{5,4},{6,7},{7,6},{8,9},{9,8},{10,11... | collective-permute-start | bytes 1572872 | tf_op jit(solution)/shard_map/middle_row/ppermute | solution.py:567
  239.5 14.9 %collective-permute-start.32 = (bf16[256,1024]{1,0:T(8,128)(2,1)}, bf16[256,1024]{1,0:T(8,128)(2,1)S(1)}, u32[]{:S(2)}, u32[]{:S(2)}) collective-permute-start(bf16[256,1024]{1,0:T(8,128)(2,1)} %collective-permute-done.31.refs_0_.refs_2_), channel_id=1, source_target_pairs={{0,8},{8,0},{16,24},{24,16},{1,9},{9,1},{17,25},{25,17},{2,10},{10... | collective-permute-start | bytes 1572872 | tf_op jit(solution)/shard_map/middle_row/ppermute | solution.py:584
  242.4 13.1 %collective-permute-start.21 = (bf16[256,1024]{1,0:T(8,128)(2,1)}, bf16[256,1024]{1,0:T(8,128)(2,1)S(1)}, u32[]{:S(2)}, u32[]{:S(2)}) collective-permute-start(bf16[256,1024]{1,0:T(8,128)(2,1)} %collective-permute-done.19.refs_1_), channel_id=1, source_target_pairs={{0,1},{1,0},{2,3},{3,2},{4,5},{5,4},{6,7},{7,6},{8,9},{9,8},{10,11... | collective-permute-start | bytes 1572872 | tf_op jit(solution)/shard_map/middle_row/ppermute | solution.py:567
  244.1 22.4 %collective-permute-start.33 = (bf16[256,1024]{1,0:T(8,128)(2,1)}, bf16[256,1024]{1,0:T(8,128)(2,1)S(1)}, u32[]{:S(2)}, u32[]{:S(2)}) collective-permute-start(bf16[256,1024]{1,0:T(8,128)(2,1)} %collective-permute-done.31.refs_0_.refs_2_), channel_id=1, source_target_pairs={{0,1},{1,0},{2,3},{3,2},{4,5},{5,4},{6,7},{7,6},{8,9},{9,8},{10,11... | collective-permute-start | bytes 1572872 | tf_op jit(solution)/shard_map/middle_row/ppermute | solution.py:567
  245.2 21.2 %collective-permute-start.25 = (bf16[1024,256]{1,0:T(8,128)(2,1)S(1)}, bf16[1024,256]{1,0:T(8,128)(2,1)S(1)}, u32[]{:S(2)}, u32[]{:S(2)}) collective-permute-start(bf16[1024,256]{1,0:T(8,128)(2,1)S(1)} %slice.292), channel_id=1, source_target_pairs={{0,2},{1,3},{2,0},{3,1},{4,6},{5,7},{6,4},{7,5},{8,10},{9,11},{10,... | collective-permute-start | bytes 1572872 | tf_op jit(solution)/shard_map/down_plane/ppermute | solution.py:570
  247.5 18.9 %collective-permute-start.26 = (bf16[1024,256]{1,0:T(8,128)(2,1)S(1)}, bf16[1024,256]{1,0:T(8,128)(2,1)S(1)}, u32[]{:S(2)}, u32[]{:S(2)}) collective-permute-start(bf16[1024,256]{1,0:T(8,128)(2,1)S(1)} %slice.293), channel_id=1, source_target_pairs={{0,4},{1,5},{2,6},{3,7},{4,0},{5,1},{6,2},{7,3},{8,12},{9,13},{10,... | collective-permute-start | bytes 1572872 | tf_op jit(solution)/shard_map/down_plane/ppermute | solution.py:570
  254.4 12.7 %collective-permute-start.34 = (bf16[256,1024]{1,0:T(8,128)(2,1)S(1)}, bf16[256,1024]{1,0:T(8,128)(2,1)S(1)}, u32[]{:S(2)}, u32[]{:S(2)}) collective-permute-start(bf16[256,1024]{1,0:T(8,128)(2,1)S(1)} %collective-permute-done.32.refs_1_.refs_3_), channel_id=1, source_target_pairs={{0,1},{1,0},{2,3},{3,2},{4,5},{5,4},{6,7},{7,6},{8,9},{9,8},{10,11... | collective-permute-start | bytes 1572872 | tf_op jit(solution)/shard_map/middle_row/ppermute | solution.py:567
  289.3 13.3 %collective-permute-start.35 = (bf16[512,1024]{1,0:T(8,128)(2,1)S(1)}, bf16[512,1024]{1,0:T(8,128)(2,1)S(1)}, u32[]{:S(2)}, u32[]{:S(2)}) collective-permute-start(bf16[512,1024]{1,0:T(8,128)(2,1)S(1)} %get-tuple-element.134), channel_id=1, source_target_pairs={{0,1},{1,0},{2,3},{3,2},{4,5},{5,4},{6,7},{7,6},{8,9},{9,8},{10,11... | collective-permute-start | bytes 3145736 | tf_op jit(solution)/shard_map/unit_grad/ppermute | solution.py:567
  305.5 13.3 %collective-permute-start.36 = (bf16[256,1024]{1,0:T(8,128)(2,1)S(1)}, bf16[256,1024]{1,0:T(8,128)(2,1)S(1)}, u32[]{:S(2)}, u32[]{:S(2)}) collective-permute-start(bf16[256,1024]{1,0:T(8,128)(2,1)S(1)} %slice.424), channel_id=1, source_target_pairs={{0,8},{8,0},{16,24},{24,16},{1,9},{9,1},{17,25},{25,17},{2,10},{10... | collective-permute-start | bytes 1572872 | tf_op jit(solution)/shard_map/unit_grad/ppermute | solution.py:584
  313.5 13.0 %collective-permute-start.41 = (bf16[1024,256]{1,0:T(8,128)(2,1)S(1)}, bf16[1024,256]{1,0:T(8,128)(2,1)S(1)}, u32[]{:S(2)}, u32[]{:S(2)}) collective-permute-start(bf16[1024,256]{1,0:T(8,128)(2,1)S(1)} %get-tuple-element.213), channel_id=1, source_target_pairs={{0,2},{1,3},{2,0},{3,1},{4,6},{5,7},{6,4},{7,5},{8,10},{9,11},{10,... | collective-permute-start | bytes 1572872 | tf_op jit(solution)/shard_map/down_grad/ppermute | solution.py:570
  316.4 20.9 %collective-permute-start.28 = (bf16[256,1024]{1,0:T(8,128)(2,1)S(1)}, bf16[256,1024]{1,0:T(8,128)(2,1)S(1)}, u32[]{:S(2)}, u32[]{:S(2)}) collective-permute-start(bf16[256,1024]{1,0:T(8,128)(2,1)S(1)} %slice.425), channel_id=1, source_target_pairs={{0,8},{8,0},{16,24},{24,16},{1,9},{9,1},{17,25},{25,17},{2,10},{10... | collective-permute-start | bytes 1572872 | tf_op jit(solution)/shard_map/unit_grad/ppermute | solution.py:584
  317.4 12.7 %collective-permute-start.39 = (bf16[1024,256]{1,0:T(8,128)(2,1)S(1)}, bf16[1024,256]{1,0:T(8,128)(2,1)S(1)}, u32[]{:S(2)}, u32[]{:S(2)}) collective-permute-start(bf16[1024,256]{1,0:T(8,128)(2,1)S(1)} %get-tuple-element.212), channel_id=1, source_target_pairs={{0,4},{1,5},{2,6},{3,7},{4,0},{5,1},{6,2},{7,3},{8,12},{9,13},{10,... | collective-permute-start | bytes 1572872 | tf_op jit(solution)/shard_map/down_grad/ppermute | solution.py:570
  318.9 22.4 %collective-permute-start.37 = (bf16[256,1024]{1,0:T(8,128)(2,1)S(1)}, bf16[256,1024]{1,0:T(8,128)(2,1)S(1)}, u32[]{:S(2)}, u32[]{:S(2)}) collective-permute-start(bf16[256,1024]{1,0:T(8,128)(2,1)S(1)} %fusion.7), channel_id=1, source_target_pairs={{0,16},{8,24},{16,0},{24,8},{1,17},{9,25},{17,1},{25,9},{2,18},{10... | collective-permute-start | bytes 1572872 | tf_op jit(solution)/shard_map/unit_grad/ppermute | solution.py:584
  326.7 27.5 %collective-permute-start.42 = (bf16[2048,256]{1,0:T(8,128)(2,1)S(1)}, bf16[2048,256]{1,0:T(8,128)(2,1)S(1)}, u32[]{:S(2)}, u32[]{:S(2)}) collective-permute-start(bf16[2048,256]{1,0:T(8,128)(2,1)S(1)} %pad_maximum_fusion.5), channel_id=1, source_target_pairs={{0,4},{1,5},{2,6},{3,7},{4,0},{5,1},{6,2},{7,3},{8,12},{9,13},{10,... | collective-permute-start | bytes 3145736 | tf_op jit(solution)/shard_map/down_grad/ppermute | solution.py:570
  330.3 23.9 %collective-permute-start.40 = (bf16[2048,256]{1,0:T(8,128)(2,1)S(1)}, bf16[2048,256]{1,0:T(8,128)(2,1)S(1)}, u32[]{:S(2)}, u32[]{:S(2)}) collective-permute-start(bf16[2048,256]{1,0:T(8,128)(2,1)S(1)} %pad_maximum_fusion.4), channel_id=1, source_target_pairs={{0,2},{1,3},{2,0},{3,1},{4,6},{5,7},{6,4},{7,5},{8,10},{9,11},{10,... | collective-permute-start | bytes 3145736 | tf_op jit(solution)/shard_map/down_grad/ppermute | solution.py:570
  375.7 13.4 %collective-permute-start.48 = (bf16[1024,256]{1,0:T(8,128)(2,1)}, bf16[1024,256]{1,0:T(8,128)(2,1)}, u32[]{:S(2)}, u32[]{:S(2)}) collective-permute-start(bf16[1024,256]{1,0:T(8,128)(2,1)} %get-tuple-element.210), channel_id=1, source_target_pairs={{0,2},{1,3},{2,0},{3,1},{4,6},{5,7},{6,4},{7,5},{8,10},{9,11},{10,... | collective-permute-start | bytes 1572872 | tf_op jit(solution)/shard_map/gate_grad/ppermute | solution.py:570
  383.1 31.5 %collective-permute-start.44 = (bf16[512,1024]{1,0:T(8,128)(2,1)}, bf16[512,1024]{1,0:T(8,128)(2,1)}, u32[]{:S(2)}, u32[]{:S(2)}) collective-permute-start(bf16[512,1024]{1,0:T(8,128)(2,1)} %get-tuple-element.145), channel_id=1, source_target_pairs={{0,1},{1,0},{2,3},{3,2},{4,5},{5,4},{6,7},{7,6},{8,9},{9,8},{10,11... | collective-permute-start | bytes 3145736 | tf_op jit(solution)/shard_map/feed/ppermute | solution.py:567
  392.4 18.1 %collective-permute-start.51 = (bf16[1024,256]{1,0:T(8,128)(2,1)S(1)}, bf16[1024,256]{1,0:T(8,128)(2,1)S(1)}, u32[]{:S(2)}, u32[]{:S(2)}) collective-permute-start(bf16[1024,256]{1,0:T(8,128)(2,1)S(1)} %get-tuple-element.209), channel_id=1, source_target_pairs={{0,2},{1,3},{2,0},{3,1},{4,6},{5,7},{6,4},{7,5},{8,10},{9,11},{10,... | collective-permute-start | bytes 1572872 | tf_op jit(solution)/shard_map/up_grad/ppermute | solution.py:570
  394.5 18.7 %collective-permute-start.49 = (bf16[1024,256]{1,0:T(8,128)(2,1)}, bf16[1024,256]{1,0:T(8,128)(2,1)S(1)}, u32[]{:S(2)}, u32[]{:S(2)}) collective-permute-start(bf16[1024,256]{1,0:T(8,128)(2,1)} %get-tuple-element.208), channel_id=1, source_target_pairs={{0,4},{1,5},{2,6},{3,7},{4,0},{5,1},{6,2},{7,3},{8,12},{9,13},{10,... | collective-permute-start | bytes 1572872 | tf_op jit(solution)/shard_map/up_grad/ppermute | solution.py:570
  401.5 26.0 %collective-permute-start.29 = (bf16[512,1024]{1,0:T(8,128)(2,1)}, bf16[512,1024]{1,0:T(8,128)(2,1)}, u32[]{:S(2)}, u32[]{:S(2)}) collective-permute-start(bf16[512,1024]{1,0:T(8,128)(2,1)} %get-tuple-element.126), channel_id=1, source_target_pairs={{0,1},{1,0},{2,3},{3,2},{4,5},{5,4},{6,7},{7,6},{8,9},{9,8},{10,11... | collective-permute-start | bytes 3145736 | tf_op jit(solution)/shard_map/feed/ppermute | solution.py:567
  411.7 32.1 %collective-permute-start.52 = (bf16[2048,256]{1,0:T(8,128)(2,1)}, bf16[2048,256]{1,0:T(8,128)(2,1)}, u32[]{:S(2)}, u32[]{:S(2)}) collective-permute-start(bf16[2048,256]{1,0:T(8,128)(2,1)} %pad_maximum_fusion.9), channel_id=1, source_target_pairs={{0,4},{1,5},{2,6},{3,7},{4,0},{5,1},{6,2},{7,3},{8,12},{9,13},{10,... | collective-permute-start | bytes 3145736 | tf_op jit(solution)/shard_map/up_grad/ppermute | solution.py:570
  414.3 32.1 %collective-permute-start.50 = (bf16[2048,256]{1,0:T(8,128)(2,1)}, bf16[2048,256]{1,0:T(8,128)(2,1)}, u32[]{:S(2)}, u32[]{:S(2)}) collective-permute-start(bf16[2048,256]{1,0:T(8,128)(2,1)} %pad_maximum_fusion.8), channel_id=1, source_target_pairs={{0,2},{1,3},{2,0},{3,1},{4,6},{5,7},{6,4},{7,5},{8,10},{9,11},{10,... | collective-permute-start | bytes 3145736 | tf_op jit(solution)/shard_map/up_grad/ppermute | solution.py:570
  418.1 14.4 %collective-permute-start.45 = (bf16[256,1024]{1,0:T(8,128)(2,1)}, bf16[256,1024]{1,0:T(8,128)(2,1)}, u32[]{:S(2)}, u32[]{:S(2)}) collective-permute-start(bf16[256,1024]{1,0:T(8,128)(2,1)} %slice.245), channel_id=1, source_target_pairs={{0,8},{8,0},{16,24},{24,16},{1,9},{9,1},{17,25},{25,17},{2,10},{10... | collective-permute-start | bytes 1572872 | tf_op jit(solution)/shard_map/feed/ppermute | solution.py:584
  422.1 45.3 %all-to-all-start.3 = ((bf16[4,512,256]{2,1,0:T(8,128)(2,1)}), bf16[4,512,256]{2,1,0:T(8,128)(2,1)}, u32[]{:S(2)}, u32[]{:S(2)}) async-start(bf16[4,512,256]{2,1,0:T(8,128)(2,1)} %bitcast.82), calls=%async_computation.3 | async-start | bytes 2097152 | tf_op jit(solution)/shard_map/down_grad/all_to_all | solution.py:685
  427.2 89.7 %collective-permute-start.65 = (bf16[2048,256]{1,0:T(8,128)(2,1)}, bf16[2048,256]{1,0:T(8,128)(2,1)}, u32[]{:S(2)}, u32[]{:S(2)}) collective-permute-start(bf16[2048,256]{1,0:T(8,128)(2,1)} %pad_maximum_fusion.7), channel_id=1, source_target_pairs={{0,4},{1,5},{2,6},{3,7},{4,0},{5,1},{6,2},{7,3},{8,12},{9,13},{10,... | collective-permute-start | bytes 3145736 | tf_op jit(solution)/shard_map/gate_grad/ppermute | solution.py:570
  427.6 89.4 %collective-permute-start.64 = (bf16[2048,256]{1,0:T(8,128)(2,1)}, bf16[2048,256]{1,0:T(8,128)(2,1)}, u32[]{:S(2)}, u32[]{:S(2)}) collective-permute-start(bf16[2048,256]{1,0:T(8,128)(2,1)} %pad_maximum_fusion.6), channel_id=1, source_target_pairs={{0,2},{1,3},{2,0},{3,1},{4,6},{5,7},{6,4},{7,5},{8,10},{9,11},{10,... | collective-permute-start | bytes 3145736 | tf_op jit(solution)/shard_map/gate_grad/ppermute | solution.py:570
  432.4 69.3 %collective-permute-start.43 = (bf16[256,1024]{1,0:T(8,128)(2,1)}, bf16[256,1024]{1,0:T(8,128)(2,1)}, u32[]{:S(2)}, u32[]{:S(2)}) collective-permute-start(bf16[256,1024]{1,0:T(8,128)(2,1)} %slice.243), channel_id=1, source_target_pairs={{0,8},{8,0},{16,24},{24,16},{1,9},{9,1},{17,25},{25,17},{2,10},{10... | collective-permute-start | bytes 1572872 | tf_op jit(solution)/shard_map/feed/ppermute | solution.py:584
  443.8 58.0 %collective-permute-start.46 = (bf16[256,1024]{1,0:T(8,128)(2,1)}, bf16[256,1024]{1,0:T(8,128)(2,1)}, u32[]{:S(2)}, u32[]{:S(2)}) collective-permute-start(bf16[256,1024]{1,0:T(8,128)(2,1)} %fusion.33), channel_id=1, source_target_pairs={{0,16},{8,24},{16,0},{24,8},{1,17},{9,25},{17,1},{25,9},{2,18},{10... | collective-permute-start | bytes 1572872 | tf_op jit(solution)/shard_map/feed/ppermute | solution.py:584
  467.4 46.7 %all-to-all-start.5 = ((bf16[4,512,256]{2,1,0:T(8,128)(2,1)}), bf16[4,512,256]{2,1,0:T(8,128)(2,1)}, u32[]{:S(2)}, u32[]{:S(2)}) async-start(bf16[4,512,256]{2,1,0:T(8,128)(2,1)} %bitcast.81), calls=%async_computation.6 | async-start | bytes 2097152 | tf_op jit(solution)/shard_map/up_grad/all_to_all | solution.py:685
  471.6 134.4 %reduce-scatter.2.cloned.1.call-start = ((), (), s32[]{:S(2)}) async-start(), calls=%async_computation.10 | async-start | bytes 5242880 | tf_op jit(solution)/shard_map/heads_grad/reduce_scatter | solution.py:838
  509.9 16.4 %collective-permute-start.59 = (bf16[256,1024]{1,0:T(8,128)(2,1)}, bf16[256,1024]{1,0:T(8,128)(2,1)}, u32[]{:S(2)}, u32[]{:S(2)}) collective-permute-start(bf16[256,1024]{1,0:T(8,128)(2,1)} %get-tuple-element.203), channel_id=1, source_target_pairs={{0,6},{1,7},{2,4},{3,5},{4,2},{5,3},{6,0},{7,1},{8,14},{9,15},{10,... | collective-permute-start | bytes 1572872 | tf_op jit(solution)/shard_map/first_plane/ppermute | solution.py:570
  513.8 23.9 %collective-permute-start.58 = (bf16[256,1024]{1,0:T(8,128)(2,1)}, bf16[256,1024]{1,0:T(8,128)(2,1)}, u32[]{:S(2)}, u32[]{:S(2)}) collective-permute-start(bf16[256,1024]{1,0:T(8,128)(2,1)} %get-tuple-element.204), channel_id=1, source_target_pairs={{0,4},{1,5},{2,6},{3,7},{4,0},{5,1},{6,2},{7,3},{8,12},{9,13},{10,... | collective-permute-start | bytes 1572872 | tf_op jit(solution)/shard_map/first_plane/ppermute | solution.py:570
  513.8 23.9 %collective-permute-start.57 = (bf16[256,1024]{1,0:T(8,128)(2,1)}, bf16[256,1024]{1,0:T(8,128)(2,1)}, u32[]{:S(2)}, u32[]{:S(2)}) collective-permute-start(bf16[256,1024]{1,0:T(8,128)(2,1)} %get-tuple-element.202), channel_id=1, source_target_pairs={{0,2},{1,3},{2,0},{3,1},{4,6},{5,7},{6,4},{7,5},{8,10},{9,11},{10,... | collective-permute-start | bytes 1572872 | tf_op jit(solution)/shard_map/first_plane/ppermute | solution.py:570
  520.1 55.8 %all-to-all-start.4 = ((bf16[4,512,256]{2,1,0:T(8,128)(2,1)}), bf16[4,512,256]{2,1,0:T(8,128)(2,1)}, u32[]{:S(2)}, u32[]{:S(2)}) async-start(bf16[4,512,256]{2,1,0:T(8,128)(2,1)} %bitcast.80), calls=%async_computation.5 | async-start | bytes 2097152 | tf_op jit(solution)/shard_map/gate_grad/all_to_all | solution.py:685
  547.3 33.3 %collective-permute-start.54 = (bf16[256,256]{1,0:T(8,128)(2,1)S(1)}, bf16[256,256]{1,0:T(8,128)(2,1)S(1)}, u32[]{:S(2)}, u32[]{:S(2)}) collective-permute-start(bf16[256,256]{1,0:T(8,128)(2,1)S(1)} %get-tuple-element.238), channel_id=1, source_target_pairs={{0,2},{1,3},{2,0},{3,1},{4,6},{5,7},{6,4},{7,5},{8,10},{9,11},{10,... | collective-permute-start | bytes 393224 | tf_op jit(solution)/shard_map/block_out/ppermute | solution.py:570
  547.8 36.5 %collective-permute-start.55 = (bf16[256,256]{1,0:T(8,128)(2,1)S(1)}, bf16[256,256]{1,0:T(8,128)(2,1)S(1)}, u32[]{:S(2)}, u32[]{:S(2)}) collective-permute-start(bf16[256,256]{1,0:T(8,128)(2,1)S(1)} %get-tuple-element.237), channel_id=1, source_target_pairs={{0,4},{1,5},{2,6},{3,7},{4,0},{5,1},{6,2},{7,3},{8,12},{9,13},{10,... | collective-permute-start | bytes 393224 | tf_op jit(solution)/shard_map/block_out/ppermute | solution.py:570
  555.8 24.6 %collective-permute-start.66 = (f32[2,4,2,256]{3,2,1,0:T(2,128)S(1)}, f32[2,4,2,256]{3,2,1,0:T(2,128)S(1)}, u32[]{:S(2)}, u32[]{:S(2)}) collective-permute-start(f32[2,4,2,256]{3,2,1,0:T(2,128)S(1)} %bitcast.84), channel_id=1, source_target_pairs={{0,1},{1,0},{2,3},{3,2},{4,5},{5,4},{6,7},{7,6},{8,9},{9,8},{10,11... | collective-permute-start | bytes 49160 | tf_op jit(solution)/shard_map/gains/ppermute | solution.py:636
  578.7 14.5 %collective-permute-start.56 = (bf16[256,256]{1,0:T(8,128)(2,1)S(1)}, bf16[256,256]{1,0:T(8,128)(2,1)S(1)}, u32[]{:S(2)}, u32[]{:S(2)}) collective-permute-start(bf16[256,256]{1,0:T(8,128)(2,1)S(1)} %get-tuple-element.236), channel_id=1, source_target_pairs={{0,6},{1,7},{2,4},{3,5},{4,2},{5,3},{6,0},{7,1},{8,14},{9,15},{10,... | collective-permute-start | bytes 393224 | tf_op jit(solution)/shard_map/block_out/ppermute | solution.py:570
  (116 other events, 961.2 us)
Sparse Core Ops, SparseCore 0:
  14.3 102.7 all-gather.5
  118.8 45.3 all-gather.7
  171.2 43.6 all-gather.9
  384.6 46.1 all-gather.11
  504.4 101.6 reduce-scatter.1
